TPU v7x, 32 devices: a whole 2x2x4 slice. The times are simulated.
32 devices in a mesh: groups: 2 (over x), spec: 16 (over z, y, core).
Axes of the slice: x: 2, y: 2, z: 4, core: 2. Of those that a mesh axis runs over, the one named last changes fastest.
Arguments:
- flux: bfloat16 [4096, 3968], P(('groups', 'spec')), parts along dimension 0, may hold values from -6 to 6
- resolution: bfloat16 [4096, 11, 3968], P(('groups', 'spec')), parts along dimension 0, may hold values from 0.019897461 to 0.29882812
- destination: int32 [4096, 1], P(('groups', 'spec')), parts along dimension 0, may hold values from 0 to 15; in each aligned block of 128 rows (0 to 127, 128 to 255, ...) at most 20 rows name the same one
- resample_weight: bfloat16 [16, 2560, 128], P('spec'), may hold values from -0.5 to 0.5
- band_offset: int32 [16, 20], P('spec'), may hold values from 0 to 3840
Outputs:
- covariance: float32 [5120, 2560], P(('groups', 'spec')), parts along dimension 0
There are 2 independent parts, one for each index of `groups`. A program takes and returns all parts, laid end to end along the dimension named above; an argument that names none is the same for every part. Nothing has to cross between parts.
Inputs may be any that keep to these rules, and one draw needn't show every extreme that they name: `destination`: within the 128 spectra held by one device along `spec`, no redshift bin is named more than 20 times.
All inputs are finite; a program needn't handle non-finite values.
Results may differ from a plain program's by a relative error of at most 0.0039.
Values may be sent and summed in bfloat16 or wider, within the bound.
No kernel may reach another device: no remote copies, remote signals or barrier semaphores. Data moves between devices by JAX's collectives and lax.ppermute only.
A program may use at most 128 MiB of HBM per device.

v0:
```python
import jax
import jax.numpy as jnp
from jax import lax
from jax.sharding import PartitionSpec as P


def smooth(flux, resolution):
    nobs = flux.shape[1]
    taps = resolution.shape[1]
    half = (taps - 1) // 2
    padded = jnp.pad(flux.astype(jnp.float32), ((0, 0), (half, half)))
    total = jnp.zeros(flux.shape, jnp.float32)
    for tap in range(taps):
        total = total + resolution[:, tap, :].astype(jnp.float32) * padded[:, tap : tap + nobs]
    return total.astype(jnp.bfloat16)


def normalize(rest):
    scale = lax.rsqrt(jnp.mean(rest * rest, axis=-1, keepdims=True) + 1e-06)
    return (rest * scale).astype(jnp.bfloat16)


def local(flux, resolution, destination, resample_weight, band_offset):
    owners = lax.axis_size("spec")
    local_count = flux.shape[0]
    nobs = flux.shape[1]
    nrest = resample_weight.shape[1]
    band = resample_weight.shape[2]
    capacity = max(2, 2 * local_count // owners, 2 * nrest // (owners * owners))
    nblocks = band_offset.shape[1]
    blockr = nrest // nblocks
    total_spectra = local_count * owners
    smoothed = smooth(flux, resolution)
    targets = destination[:, 0]
    bins_row = jnp.arange(owners, dtype=jnp.int32)
    onehot = (targets[:, None] == bins_row[None, :]).astype(jnp.float32)
    row_ids = jnp.arange(local_count, dtype=jnp.int32)
    lower = (row_ids[:, None] > row_ids[None, :]).astype(jnp.float32)
    before = jnp.dot(lower, onehot, preferred_element_type=jnp.float32)
    rank = jnp.sum(before * onehot, axis=1).astype(jnp.int32)
    position = targets * capacity + rank
    slot_ids = jnp.arange(owners * capacity, dtype=jnp.int32)
    placing = (slot_ids[:, None] == position[None, :]).astype(jnp.bfloat16)
    outgoing = jnp.dot(placing, smoothed, preferred_element_type=jnp.float32).astype(jnp.bfloat16)
    outgoing = outgoing.reshape(owners, capacity, nobs)
    weights3 = resample_weight[0].reshape(nblocks, blockr, band)
    span = jnp.arange(band, dtype=jnp.int32)
    index = (band_offset[0][:, None] + span[None, :]).reshape(nblocks * band)
    arrived = lax.all_to_all(outgoing, "spec", split_axis=0, concat_axis=0, tiled=True)
    senders = arrived.shape[0]
    items = arrived.shape[1]
    rows = arrived.reshape(senders * items, nobs)
    window = jnp.take(rows, index, axis=1).reshape(senders * items, nblocks, band)
    rest = jnp.einsum("nbk,brk->nbr", window, weights3, preferred_element_type=jnp.float32)
    normed = normalize(rest.reshape(senders * items, nrest)).reshape(senders, items, nrest)
    normed = normed.reshape(owners * capacity, nrest)
    product = lax.dot_general(
        normed, normed, (((0,), (0,)), ((), ())), preferred_element_type=jnp.float32
    )
    covariance = lax.psum_scatter(product / total_spectra, "spec", scatter_dimension=0, tiled=True)
    return covariance


def solution(mesh):
    in_specs = (
        P(("groups", "spec"), None),
        P(("groups", "spec"), None, None),
        P(("groups", "spec"), None),
        P("spec", None, None),
        P("spec", None),
    )
    out_specs = P(("groups", "spec"), None)
    return jax.shard_map(local, mesh=mesh, in_specs=in_specs, out_specs=out_specs, check_vma=False)
```

profile of v0, /device:TPU:0, one launch (start us, length us, event | category | flops | bytes accessed | tf_op | source)
XLA Modules:
  0.0 388.3 jit_solution(5703239540531509298)
XLA Ops:
  6.5 0.0 copy-start
  6.5 0.9 fusion.17
  7.4 0.7 convert_add_fusion
  8.1 1.3 convert_element_type.100
  9.5 8.8 %convolution_convert_fusion = bf16[320,3968]{1,0:T(8,128)(2,1)S(1)} fusion(f32[128,3968]{1,0:T(8,128)S(1)} %convert_element_type.100, bf16[128,11,3968]{2,0,1:T(8,128)(2,1)} %param.6, s32[128]{0:T(128)S(1)} %convert_add_fusion), kind=kOutput, calls=%fused_computation.2 | convolution fusion | flops 343130112 | bytes 15745536 | tf_op jit(solution)/shard_map/dot_general | solution.py:44
  18.2 2.4 reshape.103
  20.6 0.0 copy-start.1
  20.6 7.6 %all-to-all-start = ((bf16[16,20,3968]{2,1,0:T(8,128)(2,1)}), bf16[16,20,3968]{2,1,0:T(8,128)(2,1)}, u32[]{:S(2)}, u32[]{:S(2)}) async-start(bf16[16,20,3968]{2,1,0:T(8,128)(2,1)} %reshape.103), calls=%async_computation | async-start | bytes 6094848 | tf_op jit(solution)/shard_map/all_to_all | solution.py:49
  28.2 0.0 reduce-scatter.2.cloned.1.call-start
  28.2 0.0 copy-done.1
  28.2 0.1 fusion.21
  28.4 0.1 fusion.24
  28.4 57.4 %all-to-all-done = bf16[16,20,3968]{2,1,0:T(8,128)(2,1)} async-done(((bf16[16,20,3968]{2,1,0:T(8,128)(2,1)}), bf16[16,20,3968]{2,1,0:T(8,128)(2,1)}, u32[]{:S(2)}, u32[]{:S(2)}) %all-to-all-start) | async-done | bytes 2539552 | tf_op jit(solution)/shard_map/all_to_all | solution.py:49
  85.9 2.8 reshape.104
  88.7 2.8 copy.11
  91.5 9.1 %gather_fusion = bf16[2560,320]{1,0:T(8,128)(2,1)S(1)} fusion(bf16[320,3968]{0,1:T(8,128)(2,1)} %copy.11, s32[3072]{0:T(1024)S(1)} %pad_clamp_fusion), kind=kCustom, calls=%fused_computation | custom fusion | bytes 3287040 | tf_op jit(solution)/shard_map/jit(_take)/gather | solution.py:53
  100.6 3.3 copy.12
  103.9 0.0 copy-done
  103.9 2.1 multiply_reduce_fusion
  106.0 12.6 %convolution_multiply_fusion = f32[2560,2560]{1,0:T(8,128)} fusion(f32[20,320,128]{2,1,0:T(8,128)S(1)} %get-tuple-element.6, f32[320]{0:T(512)S(1)} %add_rsqrt_fusion), kind=kOutput, calls=%fused_computation.1 | convolution fusion | flops 4202496000 | bytes 29492480 | tf_op jit(solution)/shard_map/dot_general | solution.py:57
  118.6 0.0 reduce-scatter.2.cloned.1.call-update
  118.7 262.8 %reduce-scatter.2.cloned.1.call-done = f32[160,2560]{1,0:T(8,128)} async-done(((f32[2560,2560]{1,0:T(8,128)}), f32[160,2560]{1,0:T(8,128)}) %reduce-scatter.2.cloned.1.call-update) | async-done | bytes 1638416 | tf_op jit(solution)/shard_map/reduce_scatter | solution.py:60
  (3 shorter events, 0.1 us)
Async XLA Ops:
  6.5 97.4 %copy-start = (bf16[1,2560,128]{2,1,0:T(8,128)(2,1)S(1)}, bf16[1,2560,128]{2,1,0:T(8,128)(2,1)}, u32[]{:S(2)}) copy-start(bf16[1,2560,128]{2,1,0:T(8,128)(2,1)} %param.8) | copy-start | bytes 1966084
  20.6 7.6 %copy-start.1 = (s32[1,20]{1,0:T(1,128)S(1)}, s32[1,20]{1,0:T(1,128)}, u32[]{:S(2)}) copy-start(s32[1,20]{1,0:T(1,128)} %param.9) | copy-start | bytes 244
  20.6 65.3 %all-to-all-start = ((bf16[16,20,3968]{2,1,0:T(8,128)(2,1)}), bf16[16,20,3968]{2,1,0:T(8,128)(2,1)}, u32[]{:S(2)}, u32[]{:S(2)}) async-start(bf16[16,20,3968]{2,1,0:T(8,128)(2,1)} %reshape.103), calls=%async_computation | async-start | bytes 6094848 | tf_op jit(solution)/shard_map/all_to_all | solution.py:49
  28.2 353.3 %reduce-scatter.2.cloned.1.call-start = ((), (), s32[]{:S(2)}) async-start(), calls=%async_computation.2 | async-start | bytes 27852800 | tf_op jit(solution)/shard_map/reduce_scatter | solution.py:60
Sparse Core Ops, SparseCore 0:
  118.8 262.6 reduce-scatter.1
where the time goes:
time: 389 us; the launch traced here: 388 us
  waiting for transfers between devices  320 us (82%)
  matrix products  24.4 us (6%)
  local copies, waits for them, and re-layouts  20.4 us (5%)
  between operations  13.5 us (3%)
  starting transfers between devices  7.61 us (2%)
    reduce_scatter x1, waiting for transfers between devices, local(): lax.psum_scatter(product / total_spectra, 'spec', scatter_dimension=0, ti...  263 us
    all_to_all x1, waiting for transfers between devices, local(): lax.all_to_all(outgoing, 'spec', split_axis=0, concat_axis=0, tiled=True)  57.4 us
    dot_general x1, matrix products, local(): lax.dot_general(normed, normed, (((0,), (0,)), ((), ())), preferred_eleme...  12.6 us
    gather x2, local copies, waits for them, and re-layouts, local(): jnp.take(rows, index, axis=1).reshape(senders * items, nblocks, band)  12.4 us
    dot_general x1, matrix products, local(): jnp.dot(placing, smoothed, preferred_element_type=jnp.float32)  8.78 us
  transfers between devices with their start and end apart: 2, of which 2 were waited for; matrix products, arithmetic and copies ran while one was open for 0% of the time, Pallas kernels for 0%

commit v1 on v0

v1 whole, which is shorter than its diff:
```python
import functools

import jax
import jax.numpy as jnp
from jax import lax
from jax.experimental import pallas as pl
from jax.experimental.pallas import tpu as pltpu
from jax.sharding import PartitionSpec as P

OUTER = 4
VMEM_LIMIT = 48 * 1024 * 1024


def smooth(flux, resolution):
    nobs = flux.shape[1]
    taps = resolution.shape[1]
    half = (taps - 1) // 2
    padded = jnp.pad(flux.astype(jnp.float32), ((0, 0), (half, half)))
    total = jnp.zeros(flux.shape, jnp.float32)
    for tap in range(taps):
        total = total + resolution[:, tap, :].astype(jnp.float32) * padded[:, tap : tap + nobs]
    return total.astype(jnp.bfloat16)


def cut_kernel(owners, slots, band, nblocks, outer_ref, starts_ref, smoothed_ref, placing_ref, back_ref, out_ref, placed, cut):
    nobs = smoothed_ref.shape[1]
    per = nblocks // OUTER
    last = nobs // band - 2
    mine = outer_ref[0]
    placed[...] = jnp.dot(placing_ref[...], smoothed_ref[...], preferred_element_type=jnp.float32)

    def one_bin(bin_id, carry):
        rows = pl.ds(pl.multiple_of(bin_id * slots, slots), slots)
        for away in range(OUTER):
            for j in range(per):
                start = starts_ref[bin_id, (mine ^ away) * per + j]
                chunk = jnp.minimum(start // band, last)
                shift = start - chunk * band
                wide = placed[rows, pl.ds(pl.multiple_of(chunk * band, band), 2 * band)]
                turned = pltpu.roll(wide, (2 * band - shift) & (2 * band - 1), 1)
                at = (away * per + j) * band
                cut[rows, at : at + band] = turned[:, :band]
        return carry

    lax.fori_loop(0, owners, one_bin, 0)
    width = per * band
    for away in range(OUTER):
        part = cut[:, away * width : (away + 1) * width].astype(jnp.bfloat16)
        out_ref[away] = jnp.dot(back_ref[...], part, preferred_element_type=jnp.float32).astype(jnp.bfloat16)


def cut_windows(outer, starts, smoothed, placing, slots, band):
    owners, nblocks = starts.shape
    rows, nobs = smoothed.shape
    vmem = pl.BlockSpec(memory_space=pltpu.VMEM)
    smem = pl.BlockSpec(memory_space=pltpu.SMEM)
    return pl.pallas_call(
        functools.partial(cut_kernel, owners, slots, band, nblocks),
        out_shape=jax.ShapeDtypeStruct((OUTER, rows, nblocks // OUTER * band), jnp.bfloat16),
        in_specs=[smem, smem, vmem, vmem, vmem],
        out_specs=vmem,
        scratch_shapes=[
            pltpu.VMEM((owners * slots, nobs), jnp.float32),
            pltpu.VMEM((owners * slots, nblocks * band), jnp.float32),
        ],
        compiler_params=pltpu.CompilerParams(vmem_limit_bytes=VMEM_LIMIT),
        cost_estimate=pl.CostEstimate(
            flops=4 * owners * slots * rows * nobs, bytes_accessed=4 * rows * nobs, transcendentals=0
        ),
    )(outer, starts, smoothed, placing, placing.T)


def rest_kernel(npieces, nbins, blocks, band, *refs):
    outer_ref, bins_ref, names_ref = refs[:3]
    windows = refs[3 : 3 + OUTER]
    weights = refs[3 + OUTER : 3 + OUTER + npieces]
    rest_ref, sent_ref, squares_ref = refs[3 + OUTER + npieces :]
    count = windows[0].shape[0]
    for away in range(OUTER):
        rows = pl.ds(pl.multiple_of((outer_ref[0] ^ away) * count, count), count)
        named = names_ref[rows, :]
        total = jnp.zeros((count, 1), jnp.float32)
        hit = [named == bins_ref[b] for b in range(npieces * nbins)]
        for block in range(blocks):
            lanes = slice(block * band, (block + 1) * band)
            window = windows[away][:, lanes]
            value = jnp.zeros((count, band), jnp.float32)
            for piece in range(npieces):
                masked = jnp.concatenate(
                    [
                        jnp.where(hit[piece * nbins + b], window, jnp.zeros_like(window))
                        for b in range(nbins)
                    ],
                    axis=1,
                )
                weight = jnp.concatenate([weights[piece][b, lanes, :] for b in range(nbins)], axis=1)
                value = value + lax.dot_general(
                    masked, weight, (((1,), (1,)), ((), ())), preferred_element_type=jnp.float32
                )
            rest_ref[rows, lanes] = value
            sent_ref[rows, lanes] = value.astype(jnp.bfloat16)
            total = total + jnp.sum(value * value, axis=1, keepdims=True)
        squares_ref[rows, :] = total


def resample(outer, bins, names, windows, weights, band):
    count, width = windows[0].shape
    rows = OUTER * count
    nbins = weights[0].shape[0]
    vmem = pl.BlockSpec(memory_space=pltpu.VMEM)
    smem = pl.BlockSpec(memory_space=pltpu.SMEM)
    return pl.pallas_call(
        functools.partial(rest_kernel, len(weights), nbins, width // band, band),
        out_shape=(
            jax.ShapeDtypeStruct((rows, width), jnp.float32),
            jax.ShapeDtypeStruct((rows, width), jnp.bfloat16),
            jax.ShapeDtypeStruct((rows, 1), jnp.float32),
        ),
        in_specs=[smem, smem, vmem] + [vmem] * (len(windows) + len(weights)),
        out_specs=(vmem, vmem, vmem),
        compiler_params=pltpu.CompilerParams(vmem_limit_bytes=VMEM_LIMIT),
        cost_estimate=pl.CostEstimate(
            flops=2 * rows * width * band * nbins * len(weights),
            bytes_accessed=rows * width * 8,
            transcendentals=0,
        ),
    )(outer, bins, names, *windows, *weights)


def local(flux, resolution, destination, resample_weight, band_offset):
    n = lax.axis_size("spec")
    inner = n // OUTER
    count = flux.shape[0]
    nrest, band = resample_weight.shape[1:]
    nblocks = band_offset.shape[1]
    capacity = max(2, 2 * count // n, 2 * nrest // (n * n))
    slots = -(-capacity // 8) * 8
    width = nrest // OUTER
    share = nrest // n
    me = lax.axis_index("spec")
    outer, q = me // inner, me % inner

    def swap(array, bit):
        return lax.ppermute(array, "spec", [(i, i ^ bit) for i in range(n)])

    def hop(array, pairs):
        return lax.ppermute(
            array, "spec", [(a * inner + i, b * inner + i) for a, b in pairs for i in range(inner)]
        )

    table = lax.all_gather(jnp.concatenate([band_offset[0], destination[:, 0]]), "spec")
    starts = table[:, :nblocks]
    names = table[:, nblocks:]

    by_outer = resample_weight[0].reshape(OUTER, width, band)
    pieces = [lax.dynamic_index_in_dim(by_outer, outer, 0, keepdims=False)]
    for away in range(1, OUTER):
        theirs = lax.dynamic_index_in_dim(by_outer, outer ^ away, 0, keepdims=False)
        pieces.append(swap(theirs, away * inner))
    weights = [jnp.stack(pieces)]
    ids = [jnp.stack([me ^ (away * inner) for away in range(OUTER)])]
    bit = inner // 2
    while bit:
        weights = weights + [swap(piece, bit) for piece in weights]
        ids = ids + [piece ^ bit for piece in ids]
        bit //= 2
    bins = jnp.concatenate(ids)

    smoothed = smooth(flux, resolution)
    targets = destination[:, 0]
    order = jnp.arange(count, dtype=jnp.int32)
    same = (targets[:, None] == targets[None, :]) & (order[:, None] > order[None, :])
    position = targets * slots + jnp.sum(same.astype(jnp.int32), axis=1)
    placing = (jnp.arange(n * slots, dtype=jnp.int32)[:, None] == position[None, :]).astype(jnp.bfloat16)
    windows = cut_windows(outer.reshape(1), starts, smoothed, placing, slots, band)
    arrived = [windows[0]] + [swap(windows[away], away * inner) for away in range(1, OUTER)]
    group = lax.dynamic_index_in_dim(names.reshape(OUTER, inner, count), q, 1, keepdims=False)
    rows = OUTER * count
    rest, sent, squares = resample(
        outer.reshape(1), bins, group.reshape(rows, 1), arrived, weights, band
    )

    squares = squares.reshape(rows)
    total = squares
    for away in range(1, OUTER):
        total = total + swap(squares, away * inner)
    scale = lax.rsqrt(total / nrest + 1e-06)
    left = (rest * (scale * scale / (count * n))[:, None]).astype(jnp.bfloat16)

    middle = (outer == 1) | (outer == 2)
    near = hop(sent, [(0, 1), (1, 0), (2, 3), (3, 2)])
    across = hop(sent, [(1, 2), (2, 1)])
    onward = hop(across, [(1, 0), (2, 3)])
    far = hop(near, [(1, 2), (2, 1)])
    end = hop(far, [(1, 0), (2, 3)])
    blocks = [
        (outer, sent),
        (outer ^ 1, near),
        (jnp.where(outer < 2, 2, 1), jnp.where(middle, across, onward)),
        (jnp.where(outer < 2, 3, 0), jnp.where(middle, far, end)),
    ]

    result = jnp.zeros((OUTER, share, width), jnp.float32)
    for column, block in blocks:
        product = lax.dot_general(
            left, block, (((0,), (0,)), ((), ())), preferred_element_type=jnp.float32
        ).reshape(inner, share, width)
        pieces = [lax.dynamic_index_in_dim(product, q ^ e, 0, keepdims=False) for e in range(inner)]
        held = jnp.stack(pieces)
        bit = 1
        while bit < inner:
            held = held.reshape(-1, 2, share, width)
            got = swap(held[:, 1].astype(jnp.bfloat16), bit)
            held = held[:, 0] + got.astype(jnp.float32)
            bit *= 2
        result = lax.dynamic_update_slice_in_dim(result, held.reshape(1, share, width), column, 0)
    return jnp.transpose(result, (1, 0, 2)).reshape(share, nrest)


def solution(mesh):
    in_specs = (
        P(("groups", "spec"), None),
        P(("groups", "spec"), None, None),
        P(("groups", "spec"), None),
        P("spec", None, None),
        P("spec", None),
    )
    out_specs = P(("groups", "spec"), None)
    return jax.shard_map(local, mesh=mesh, in_specs=in_specs, out_specs=out_specs, check_vma=False)
```

time: 389 us -> 241 us (0.62)
  waiting for transfers between devices: 320 us -> 66 us
  blocking collectives: 0 us -> 61 us
  local copies, waits for them, and re-layouts: 20.4 us -> 54.6 us
  matrix products: 24.4 us -> 2.81 us
  starting transfers between devices: 7.61 us -> 29.2 us
  between operations: 13.5 us -> 1.17 us
  other arithmetic: 2.22 us -> 13.5 us
  Pallas kernels: 0 us -> 10.9 us
    reduce_scatter x1 -> x0, waiting for transfers between devices: 263 us -> none  [local(): lax.psum_scatter(product / total_spectra, 'spec', scatter_dimension=0, ti...]
    ppermute x0 -> x25, waiting for transfers between devices: none -> 66 us  [the longest x5 37.3 us: hop(): lax.ppermute(array, 'spec', [(a * inner + i, b * inner + i) for a, b in p...]
    unnamed x0 -> x1, blocking collectives: none -> 61 us
    all_to_all x1 -> x0, waiting for transfers between devices: 57.4 us -> none  [local(): lax.all_to_all(outgoing, 'spec', split_axis=0, concat_axis=0, tiled=True)]
    dynamic_update_slice x0 -> x4, local copies, waits for them, and re-layouts: none -> 35.9 us  [local(): lax.dynamic_update_slice_in_dim(result, held.reshape(1, share, width), co...]
    ppermute x0 -> x25, starting transfers between devices: none -> 29.2 us  [the longest x20 21.2 us: swap(): return lax.ppermute(array, 'spec', [(i, i ^ bit) for i in range(n)])]
    dot_general x4, matrix products: 24.4 us -> 2.81 us  [local(): lax.dot_general(left, block, (((0,), (0,)), ((), ())), preferred_element_...]
    gather x2 -> x0, local copies, waits for them, and re-layouts: 12.4 us -> none  [local(): jnp.take(rows, index, axis=1).reshape(senders * items, nblocks, band)]
  transfers between devices with their start and end apart: 2 -> 25, of which waited for: 2 -> 9; matrix products, arithmetic and copies ran while one was open for 0% -> 18% of each run, Pallas kernels for 0% -> 3%
where the time goes in v1:
time: 241 us; the launch traced here: 239 us
  waiting for transfers between devices  66 us (27%)
  blocking collectives  61 us (25%)
  local copies, waits for them, and re-layouts  54.6 us (23%)
  starting transfers between devices  29.2 us (12%)
  other arithmetic  13.5 us (6%)
  Pallas kernels  10.9 us (5%)
  matrix products  2.81 us (1%)
    unnamed x1, blocking collectives  61 us
    ppermute x5, waiting for transfers between devices, hop(): lax.ppermute(array, 'spec', [(a * inner + i, b * inner + i) for a, b in p...  37.3 us
    dynamic_update_slice x4, local copies, waits for them, and re-layouts, local(): lax.dynamic_update_slice_in_dim(result, held.reshape(1, share, width), co...  35.9 us
    ppermute x20, waiting for transfers between devices, swap(): return lax.ppermute(array, 'spec', [(i, i ^ bit) for i in range(n)])  28.7 us
    ppermute x20, starting transfers between devices, swap(): return lax.ppermute(array, 'spec', [(i, i ^ bit) for i in range(n)])  21.2 us
    unnamed x35, local copies, waits for them, and re-layouts  10.2 us
    convert_element_type x1, other arithmetic, smooth(): return total.astype(jnp.bfloat16)  8.13 us
    ppermute x5, starting transfers between devices, hop(): lax.ppermute(array, 'spec', [(a * inner + i, b * inner + i) for a, b in p...  8.01 us
  transfers between devices with their start and end apart: 25, of which 9 were waited for; matrix products, arithmetic and copies ran while one was open for 18% of the time, Pallas kernels for 3%

profile of v1, /device:TPU:0, one launch (start us, length us, event | category | flops | bytes accessed | tf_op | source)
XLA Modules:
  0.0 239.2 jit_solution(10564005948372840290)
XLA Ops:
  0.0 1.3 constant_dynamic-slice_fusion.16
  1.3 3.1 %collective-permute-start.3 = (bf16[640,128]{1,0:T(8,128)(2,1)S(1)}, bf16[640,128]{1,0:T(8,128)(2,1)S(1)}, u32[]{:S(2)}, u32[]{:S(2)}) collective-permute-start(bf16[640,128]{1,0:T(8,128)(2,1)S(1)} %get-tuple-element.32), channel_id=1, source_target_pairs={{0,4},{1,5},{2,6},{3,7},{4,0},{5,1},{6,2},{7,3},{8,12},{9,13},{10,... | collective-permute-start | bytes 491528 | tf_op jit(solution)/shard_map/ppermute | solution.py:144
  4.4 2.6 %collective-permute-start.4 = (bf16[640,128]{1,0:T(8,128)(2,1)S(1)}, bf16[640,128]{1,0:T(8,128)(2,1)S(1)}, u32[]{:S(2)}, u32[]{:S(2)}) collective-permute-start(bf16[640,128]{1,0:T(8,128)(2,1)S(1)} %get-tuple-element.31), channel_id=1, source_target_pairs={{0,8},{1,9},{2,10},{3,11},{4,12},{5,13},{6,14},{7,15},{8,0},{9,1},... | collective-permute-start | bytes 491528 | tf_op jit(solution)/shard_map/ppermute | solution.py:144
  7.1 0.6 dynamic-slice
  8.4 8.1 %fusion.1.smoothed_ref = bf16[128,3968]{1,0:T(8,128)(2,1)S(1)} fusion(f32[128,3968]{1,0:T(8,128)S(1)} %convert_element_type.175, bf16[128,11,3968]{2,0,1:T(8,128)(2,1)} %param.6), kind=kLoop, calls=%fused_computation.2 | loop fusion | flops 16760832 | bytes 14221312 | tf_op jit(solution)/shard_map/convert_element_type | solution.py:22
  16.6 0.2 add_dynamic-update-slice_fusion
  16.8 61.0 %all-reduce.1 = s32[2368]{0:T(1024)S(1)} all-reduce(s32[2368]{0:T(1024)S(1)} %add_dynamic-update-slice_fusion), channel_id=2, replica_groups=mesh['groups'=2,'spec'=16] {'spec'}, use_global_device_ids=true, to_apply=%add.1 | all-reduce | flops 2368 | bytes 18944
  77.8 0.2 convert_reduce_fusion
  78.4 6.5 %shard_map.55 = bf16[4,128,640]{2,1,0:T(8,128)(2,1)S(1)} custom-call(s32[1]{0:T(128)} %bitcast.outer_ref.refs_0_, s32[16,20]{1,0:T(8,128)S(1)} %slice.182.starts_ref, bf16[128,3968]{1,0:T(8,128)(2,1)S(1)} %fusion.1.smoothed_ref, bf16[384,128]{1,0:T(8,128)(2,1)S(1)} %fusion.37.placing_ref, bf16[128,384]{1,0:T(8,128)(2,1)S(1)} %fusion.38.back_ref), custom_call_target="tpu_custom_call" | custom-call | flops 780140544 | bytes 2031616 | tf_op jit(solution)/shard_map/pallas_call | solution.py:57
  85.0 5.3 %collective-permute-done.6.refs_8_ = bf16[4,640,128]{2,1,0:T(8,128)(2,1)S(1)} collective-permute-done((bf16[4,640,128]{2,1,0:T(8,128)(2,1)S(1)}, bf16[4,640,128]{2,1,0:T(8,128)(2,1)S(1)}, u32[]{:S(2)}, u32[]{:S(2)}) %collective-permute-start.6) | collective-permute-done | bytes 655392 | tf_op jit(solution)/shard_map/ppermute | solution.py:144
  90.3 0.9 slice_bitcast_fusion.8
  91.1 1.4 collective-permute-start.1
  92.5 3.0 %collective-permute-start.2 = (bf16[128,640]{1,0:T(8,128)(2,1)}, bf16[128,640]{1,0:T(8,128)(2,1)}, u32[]{:S(2)}, u32[]{:S(2)}) collective-permute-start(bf16[128,640]{1,0:T(8,128)(2,1)} %get-tuple-element.33), channel_id=1, source_target_pairs={{0,12},{1,13},{2,14},{3,15},{4,8},{5,9},{6,10},{7,11},{8,4},{9,5},... | collective-permute-start | bytes 491528 | tf_op jit(solution)/shard_map/ppermute | solution.py:144
  95.9 3.3 %collective-permute-done.refs_4_ = bf16[128,640]{1,0:T(8,128)(2,1)S(1)} collective-permute-done((bf16[128,640]{1,0:T(8,128)(2,1)}, bf16[128,640]{1,0:T(8,128)(2,1)S(1)}, u32[]{:S(2)}, u32[]{:S(2)}) %collective-permute-start) | collective-permute-done | bytes 163872 | tf_op jit(solution)/shard_map/ppermute | solution.py:144
  99.3 7.1 %collective-permute-done.1.refs_5_ = bf16[128,640]{1,0:T(8,128)(2,1)S(1)} collective-permute-done((bf16[128,640]{1,0:T(8,128)(2,1)}, bf16[128,640]{1,0:T(8,128)(2,1)S(1)}, u32[]{:S(2)}, u32[]{:S(2)}) %collective-permute-start.1) | collective-permute-done | bytes 163872 | tf_op jit(solution)/shard_map/ppermute | solution.py:144
  106.3 0.7 copy-done.6
  107.0 0.9 copy-done.2
  107.9 0.9 copy-done.4
  108.7 1.1 copy-done.1
  109.8 1.1 copy-done.3
  110.9 1.1 copy-done.5
  112.0 0.9 copy-done.7
  112.9 4.4 %shard_map.56 = (f32[512,640]{1,0:T(8,128)S(1)}, bf16[512,640]{1,0:T(8,128)(2,1)S(1)}, f32[512,1]{1,0:T(8,128)S(1)}) custom-call(s32[1]{0:T(128)} %bitcast.outer_ref.refs_0_, s32[16]{0:T(128)S(1)} %concatenate.7.refs_1_, s32[512,1]{1,0:T(8,128)S(1)} %copy.36.refs_2_, bf16[128,640]{1,0:T(8,128)(2,1)S(1)} %get-tuple-element.36.refs_3_, ...), custom_call_target="tpu_custom_call" | custom-call | flops 1342177280 | bytes 2621440 | tf_op jit(solution)/shard_map/pallas_call | solution.py:112
  117.4 3.1 %collective-permute-start.10 = (f32[512]{0:T(512)S(1)}, f32[512]{0:T(512)S(1)}, u32[]{:S(2)}, u32[]{:S(2)}) collective-permute-start(f32[512]{0:T(512)S(1)} %reduce), channel_id=1, source_target_pairs={{0,8},{1,9},{2,10},{3,11},{4,12},{5,13},{6,14},{7,15},{8,0},{9,1},... | collective-permute-start | bytes 6152 | tf_op jit(solution)/shard_map/ppermute | solution.py:144
  120.6 2.4 collective-permute-start.11
  122.9 1.5 collective-permute-start.17
  124.4 3.2 %collective-permute-start.14 = (bf16[512,640]{1,0:T(8,128)(2,1)S(1)}, bf16[512,640]{1,0:T(8,128)(2,1)S(1)}, u32[]{:S(2)}, u32[]{:S(2)}) collective-permute-start(bf16[512,640]{1,0:T(8,128)(2,1)S(1)} %get-tuple-element.10), channel_id=1, source_target_pairs={{0,4},{1,5},{2,6},{3,7},{4,0},{5,1},{6,2},{7,3},{8,12},{9,13},{10,... | collective-permute-start | bytes 1966088 | tf_op jit(solution)/shard_map/ppermute | solution.py:147
  127.8 0.7 fusion.41
  128.5 12.6 %collective-permute-done.14 = bf16[512,640]{1,0:T(8,128)(2,1)S(1)} collective-permute-done((bf16[512,640]{1,0:T(8,128)(2,1)S(1)}, bf16[512,640]{1,0:T(8,128)(2,1)S(1)}, u32[]{:S(2)}, u32[]{:S(2)}) %collective-permute-start.14) | collective-permute-done | bytes 655392 | tf_op jit(solution)/shard_map/ppermute | solution.py:147
  141.1 0.7 fusion.42
  142.0 0.2 constant_dynamic-slice_fusion.11
  142.3 1.2 copy-done.8
  143.8 0.5 collective-permute-start.12
  144.3 0.4 copy-done.12
  144.7 0.7 collective-permute-start.21
  145.4 1.3 collective-permute-start.18
  146.7 1.1 fusion.16
  147.9 0.6 collective-permute-start.16
  148.6 1.3 collective-permute-start.22
  149.9 1.5 collective-permute-start.13
  151.5 4.3 %collective-permute-done.16 = bf16[1,160,640]{2,1,0:T(8,128)(2,1)S(1)} collective-permute-done((bf16[1,160,640]{2,1,0:T(8,128)(2,1)S(1)}, bf16[1,160,640]{2,1,0:T(8,128)(2,1)S(1)}, u32[]{:S(2)}, u32[]{:S(2)}) %collective-permute-start.16) | collective-permute-done | bytes 204832 | tf_op jit(solution)/shard_map/ppermute | solution.py:144
  155.8 10.5 %collective-permute-done.18 = bf16[512,640]{1,0:T(8,128)(2,1)S(1)} collective-permute-done((bf16[512,640]{1,0:T(8,128)(2,1)}, bf16[512,640]{1,0:T(8,128)(2,1)S(1)}, u32[]{:S(2)}, u32[]{:S(2)}) %collective-permute-start.18) | collective-permute-done | bytes 655392 | tf_op jit(solution)/shard_map/ppermute | solution.py:147
  166.4 0.7 fusion.21
  167.1 14.2 %collective-permute-done.22 = bf16[512,640]{1,0:T(8,128)(2,1)S(1)} collective-permute-done((bf16[512,640]{1,0:T(8,128)(2,1)S(1)}, bf16[512,640]{1,0:T(8,128)(2,1)S(1)}, u32[]{:S(2)}, u32[]{:S(2)}) %collective-permute-start.22) | collective-permute-done | bytes 655392 | tf_op jit(solution)/shard_map/ppermute | solution.py:147
  181.3 0.7 fusion.19
  182.0 1.3 constant_dynamic-slice_fusion.3
  183.4 0.8 fusion.28
  184.2 1.2 copy.40
  185.4 1.2 copy.38
  186.6 0.2 broadcast_in_dim.2
  186.8 9.5 %dynamic_update_slice.12 = f32[4,160,640]{2,0,1:T(4,128)S(1)} dynamic-update-slice(f32[4,160,640]{2,0,1:T(4,128)S(1)} %broadcast_in_dim.2, f32[1,160,640]{2,0,1:T(1,128)} %copy.38, s32[]{:T(128)S(6)} %select_n.77, s32[]{:T(128)} %constant.92.clone.1, s32[]{:T(128)} %constant.92.clone.1) | dynamic-update-slice | bytes 819204 | tf_op jit(solution)/shard_map/dynamic_update_slice | solution.py:216
  196.3 9.5 %dynamic_update_slice.13 = f32[4,160,640]{2,0,1:T(4,128)S(1)} dynamic-update-slice(f32[4,160,640]{2,0,1:T(4,128)S(1)} %dynamic_update_slice.12, f32[1,160,640]{2,0,1:T(1,128)} %copy.40, s32[]{:T(128)S(6)} %select_n.78, s32[]{:T(128)} %constant.92.clone.1, s32[]{:T(128)} %constant.92.clone.1) | dynamic-update-slice | bytes 819204 | tf_op jit(solution)/shard_map/dynamic_update_slice | solution.py:216
  205.8 1.5 pad_maximum_fusion.2
  207.3 0.6 collective-permute-start.19
  207.9 1.1 fusion.12
  209.0 0.6 collective-permute-start.24
  209.8 1.5 collective-permute-start.20
  211.3 5.7 %collective-permute-done.24 = bf16[1,160,640]{2,1,0:T(8,128)(2,1)S(1)} collective-permute-done((bf16[1,160,640]{2,1,0:T(8,128)(2,1)S(1)}, bf16[1,160,640]{2,1,0:T(8,128)(2,1)S(1)}, u32[]{:S(2)}, u32[]{:S(2)}) %collective-permute-start.24) | collective-permute-done | bytes 204832 | tf_op jit(solution)/shard_map/ppermute | solution.py:144
  217.1 0.4 copy.44
  217.5 3.0 %collective-permute-done.20 = bf16[1,160,640]{2,1,0:T(8,128)(2,1)S(1)} collective-permute-done((bf16[1,160,640]{2,1,0:T(8,128)(2,1)S(1)}, bf16[1,160,640]{2,1,0:T(8,128)(2,1)S(1)}, u32[]{:S(2)}, u32[]{:S(2)}) %collective-permute-start.20) | collective-permute-done | bytes 204832 | tf_op jit(solution)/shard_map/ppermute | solution.py:144
  220.5 0.4 copy.42
  221.0 8.5 %dynamic_update_slice.14 = f32[4,160,640]{2,0,1:T(4,128)S(1)} dynamic-update-slice(f32[4,160,640]{2,0,1:T(4,128)S(1)} %dynamic_update_slice.13, f32[1,160,640]{2,0,1:T(1,128)S(1)} %copy.42, s32[]{:T(128)S(6)} %select_n.86, s32[]{:T(128)} %constant.92.clone.1, s32[]{:T(128)} %constant.92.clone.1) | dynamic-update-slice | bytes 819204 | tf_op jit(solution)/shard_map/dynamic_update_slice | solution.py:216
  229.4 8.5 %dynamic_update_slice.15 = f32[4,160,640]{2,0,1:T(4,128)S(1)} dynamic-update-slice(f32[4,160,640]{2,0,1:T(4,128)S(1)} %dynamic_update_slice.14, f32[1,160,640]{2,0,1:T(1,128)S(1)} %copy.44, s32[]{:T(128)S(6)} %select_n.88, s32[]{:T(128)} %constant.92.clone.1, s32[]{:T(128)} %constant.92.clone.1) | dynamic-update-slice | bytes 819204 | tf_op jit(solution)/shard_map/dynamic_update_slice | solution.py:216
  237.9 1.3 copy.50
  (80 shorter events, 2.5 us)
Async XLA Ops:
  0.0 7.0 %copy-start.10 = (bf16[128,3968]{1,0:T(8,128)(2,1)S(1)}, bf16[128,3968]{1,0:T(8,128)(2,1)}, u32[]{:S(2)}) copy-start(bf16[128,3968]{1,0:T(8,128)(2,1)} %param.5) | copy-start | bytes 3047428
  1.3 5.8 %copy-start.15 = (u32[32]{0:T(128)S(1)}, u32[32]{0:T(128)}, u32[]{:S(2)}) copy-start(u32[32]{0:T(128)} %constant.109) | copy-start | bytes 388
  1.3 76.7 %collective-permute-start.3 = (bf16[640,128]{1,0:T(8,128)(2,1)S(1)}, bf16[640,128]{1,0:T(8,128)(2,1)S(1)}, u32[]{:S(2)}, u32[]{:S(2)}) collective-permute-start(bf16[640,128]{1,0:T(8,128)(2,1)S(1)} %get-tuple-element.32), channel_id=1, source_target_pairs={{0,4},{1,5},{2,6},{3,7},{4,0},{5,1},{6,2},{7,3},{8,12},{9,13},{10,... | collective-permute-start | bytes 491528 | tf_op jit(solution)/shard_map/ppermute | solution.py:144
  4.4 73.6 %collective-permute-start.4 = (bf16[640,128]{1,0:T(8,128)(2,1)S(1)}, bf16[640,128]{1,0:T(8,128)(2,1)S(1)}, u32[]{:S(2)}, u32[]{:S(2)}) collective-permute-start(bf16[640,128]{1,0:T(8,128)(2,1)S(1)} %get-tuple-element.31), channel_id=1, source_target_pairs={{0,8},{1,9},{2,10},{3,11},{4,12},{5,13},{6,14},{7,15},{8,0},{9,1},... | collective-permute-start | bytes 491528 | tf_op jit(solution)/shard_map/ppermute | solution.py:144
  7.0 71.1 %collective-permute-start.5 = (bf16[640,128]{1,0:T(8,128)(2,1)S(1)}, bf16[640,128]{1,0:T(8,128)(2,1)S(1)}, u32[]{:S(2)}, u32[]{:S(2)}) collective-permute-start(bf16[640,128]{1,0:T(8,128)(2,1)S(1)} %get-tuple-element.30), channel_id=1, source_target_pairs={{0,12},{1,13},{2,14},{3,15},{4,8},{5,9},{6,10},{7,11},{8,4},{9,5},... | collective-permute-start | bytes 491528 | tf_op jit(solution)/shard_map/ppermute | solution.py:144
  8.4 8.2 %copy-start.13 = (s32[1,20]{1,0:T(1,128)S(1)}, s32[1,20]{1,0:T(1,128)}, u32[]{:S(2)}) copy-start(s32[1,20]{1,0:T(1,128)} %param.9) | copy-start | bytes 244
  8.4 8.2 %copy-start.14 = (s32[128,1]{0,1:T(1,128)S(1)}, s32[128,1]{0,1:T(1,128)}, u32[]{:S(2)}) copy-start(s32[128,1]{0,1:T(1,128)} %param.7) | copy-start | bytes 1540
  78.1 12.1 %collective-permute-start.6 = (bf16[4,640,128]{2,1,0:T(8,128)(2,1)S(1)}, bf16[4,640,128]{2,1,0:T(8,128)(2,1)S(1)}, u32[]{:S(2)}, u32[]{:S(2)}) collective-permute-start(bf16[4,640,128]{2,1,0:T(8,128)(2,1)S(1)} %pad_maximum_fusion.4.refs_7_), channel_id=1, source_target_pairs={{0,2},{1,3},{2,0},{3,1},{4,6},{5,7},{6,4},{7,5},{8,10},{9,11},{10,... | collective-permute-start | bytes 1966088 | tf_op jit(solution)/shard_map/ppermute | solution.py:144
  84.9 22.1 %collective-permute-start.7 = (bf16[4,640,128]{2,1,0:T(8,128)(2,1)S(1)}, bf16[4,640,128]{2,1,0:T(8,128)(2,1)S(1)}, u32[]{:S(2)}, u32[]{:S(2)}) collective-permute-start(bf16[4,640,128]{2,1,0:T(8,128)(2,1)S(1)} %pad_maximum_fusion.4.refs_7_), channel_id=1, source_target_pairs={{0,1},{1,0},{2,3},{3,2},{4,5},{5,4},{6,7},{7,6},{8,9},{9,8},{10,11... | collective-permute-start | bytes 1966088 | tf_op jit(solution)/shard_map/ppermute | solution.py:144
  90.3 17.6 %copy-start = (bf16[4,640,128]{2,1,0:T(8,128)(2,1)}, bf16[4,640,128]{2,1,0:T(8,128)(2,1)S(1)}, u32[]{:S(2)}) copy-start(bf16[4,640,128]{2,1,0:T(8,128)(2,1)S(1)} %collective-permute-done.6.refs_8_) | copy-start | bytes 1966084
  90.3 17.6 %collective-permute-start.8 = (bf16[4,640,128]{2,1,0:T(8,128)(2,1)S(1)}, bf16[4,640,128]{2,1,0:T(8,128)(2,1)S(1)}, u32[]{:S(2)}, u32[]{:S(2)}) collective-permute-start(bf16[4,640,128]{2,1,0:T(8,128)(2,1)S(1)} %collective-permute-done.6.refs_8_), channel_id=1, source_target_pairs={{0,1},{1,0},{2,3},{3,2},{4,5},{5,4},{6,7},{7,6},{8,9},{9,8},{10,11... | collective-permute-start | bytes 1966088 | tf_op jit(solution)/shard_map/ppermute | solution.py:144
  91.1 8.1 %collective-permute-start = (bf16[128,640]{1,0:T(8,128)(2,1)}, bf16[128,640]{1,0:T(8,128)(2,1)S(1)}, u32[]{:S(2)}, u32[]{:S(2)}) collective-permute-start(bf16[128,640]{1,0:T(8,128)(2,1)} %get-tuple-element.35), channel_id=1, source_target_pairs={{0,4},{1,5},{2,6},{3,7},{4,0},{5,1},{6,2},{7,3},{8,12},{9,13},{10,... | collective-permute-start | bytes 491528 | tf_op jit(solution)/shard_map/ppermute | solution.py:144
  91.1 15.2 %collective-permute-start.1 = (bf16[128,640]{1,0:T(8,128)(2,1)}, bf16[128,640]{1,0:T(8,128)(2,1)S(1)}, u32[]{:S(2)}, u32[]{:S(2)}) collective-permute-start(bf16[128,640]{1,0:T(8,128)(2,1)} %get-tuple-element.34), channel_id=1, source_target_pairs={{0,8},{1,9},{2,10},{3,11},{4,12},{5,13},{6,14},{7,15},{8,0},{9,1},... | collective-permute-start | bytes 491528 | tf_op jit(solution)/shard_map/ppermute | solution.py:144
  92.5 14.5 %collective-permute-start.2 = (bf16[128,640]{1,0:T(8,128)(2,1)}, bf16[128,640]{1,0:T(8,128)(2,1)}, u32[]{:S(2)}, u32[]{:S(2)}) collective-permute-start(bf16[128,640]{1,0:T(8,128)(2,1)} %get-tuple-element.33), channel_id=1, source_target_pairs={{0,12},{1,13},{2,14},{3,15},{4,8},{5,9},{6,10},{7,11},{8,4},{9,5},... | collective-permute-start | bytes 491528 | tf_op jit(solution)/shard_map/ppermute | solution.py:144
  106.3 0.7 copy-start.6
  107.0 0.9 copy-start.2
  107.9 0.9 copy-start.4
  108.7 1.1 copy-start.1
  109.8 1.1 copy-start.3
  110.9 1.1 copy-start.5
  112.0 0.9 copy-start.7
  117.4 10.2 %collective-permute-start.10 = (f32[512]{0:T(512)S(1)}, f32[512]{0:T(512)S(1)}, u32[]{:S(2)}, u32[]{:S(2)}) collective-permute-start(f32[512]{0:T(512)S(1)} %reduce), channel_id=1, source_target_pairs={{0,8},{1,9},{2,10},{3,11},{4,12},{5,13},{6,14},{7,15},{8,0},{9,1},... | collective-permute-start | bytes 6152 | tf_op jit(solution)/shard_map/ppermute | solution.py:144
  120.6 7.1 %collective-permute-start.11 = (f32[512]{0:T(512)S(1)}, f32[512]{0:T(512)S(1)}, u32[]{:S(2)}, u32[]{:S(2)}) collective-permute-start(f32[512]{0:T(512)S(1)} %reduce), channel_id=1, source_target_pairs={{0,12},{1,13},{2,14},{3,15},{4,8},{5,9},{6,10},{7,11},{8,4},{9,5},... | collective-permute-start | bytes 6152 | tf_op jit(solution)/shard_map/ppermute | solution.py:144
  122.9 4.8 %collective-permute-start.9 = (f32[512]{0:T(512)S(1)}, f32[512]{0:T(512)S(1)}, u32[]{:S(2)}, u32[]{:S(2)}) collective-permute-start(f32[512]{0:T(512)S(1)} %reduce), channel_id=1, source_target_pairs={{0,4},{1,5},{2,6},{3,7},{4,0},{5,1},{6,2},{7,3},{8,12},{9,13},{10,... | collective-permute-start | bytes 6152 | tf_op jit(solution)/shard_map/ppermute | solution.py:144
  122.9 22.5 %collective-permute-start.17 = (bf16[512,640]{1,0:T(8,128)(2,1)S(1)}, bf16[512,640]{1,0:T(8,128)(2,1)}, u32[]{:S(2)}, u32[]{:S(2)}) collective-permute-start(bf16[512,640]{1,0:T(8,128)(2,1)S(1)} %get-tuple-element.10), channel_id=1, source_target_pairs={{4,8},{5,9},{6,10},{7,11},{8,4},{9,5},{10,6},{11,7},{20,24},{21,25... | collective-permute-start | bytes 1966088 | tf_op jit(solution)/shard_map/ppermute | solution.py:147
  124.4 16.7 %collective-permute-start.14 = (bf16[512,640]{1,0:T(8,128)(2,1)S(1)}, bf16[512,640]{1,0:T(8,128)(2,1)S(1)}, u32[]{:S(2)}, u32[]{:S(2)}) collective-permute-start(bf16[512,640]{1,0:T(8,128)(2,1)S(1)} %get-tuple-element.10), channel_id=1, source_target_pairs={{0,4},{1,5},{2,6},{3,7},{4,0},{5,1},{6,2},{7,3},{8,12},{9,13},{10,... | collective-permute-start | bytes 1966088 | tf_op jit(solution)/shard_map/ppermute | solution.py:147
  141.1 0.9 copy-start.11
  142.3 1.2 copy-start.8
  143.5 3.2 %collective-permute-start.15 = (bf16[2,160,640]{2,1,0:T(8,128)(2,1)S(1)}, bf16[2,160,640]{2,1,0:T(8,128)(2,1)}, u32[]{:S(2)}, u32[]{:S(2)}) collective-permute-start(bf16[2,160,640]{2,1,0:T(8,128)(2,1)S(1)} %fusion.26), channel_id=1, source_target_pairs={{0,1},{1,0},{2,3},{3,2},{4,5},{5,4},{6,7},{7,6},{8,9},{9,8},{10,11... | collective-permute-start | bytes 1228808 | tf_op jit(solution)/shard_map/ppermute | solution.py:144
  143.6 1.1 copy-start.12
  143.6 3.1 %copy-start.9 = (f32[4,160,640]{2,1,0:T(8,128)S(1)}, f32[4,160,640]{2,1,0:T(8,128)}, u32[]{:S(2)}) copy-start(f32[4,160,640]{2,1,0:T(8,128)} %copy-done.8) | copy-start | bytes 4915204
  143.8 4.7 %collective-permute-start.12 = (bf16[2,160,640]{2,1,0:T(8,128)(2,1)S(1)}, bf16[2,160,640]{2,1,0:T(8,128)(2,1)S(1)}, u32[]{:S(2)}, u32[]{:S(2)}) collective-permute-start(bf16[2,160,640]{2,1,0:T(8,128)(2,1)S(1)} %fusion.25), channel_id=1, source_target_pairs={{0,1},{1,0},{2,3},{3,2},{4,5},{5,4},{6,7},{7,6},{8,9},{9,8},{10,11... | collective-permute-start | bytes 1228808 | tf_op jit(solution)/shard_map/ppermute | solution.py:144
  144.7 3.9 %collective-permute-start.21 = (bf16[512,640]{1,0:T(8,128)(2,1)S(1)}, bf16[512,640]{1,0:T(8,128)(2,1)S(1)}, u32[]{:S(2)}, u32[]{:S(2)}) collective-permute-start(bf16[512,640]{1,0:T(8,128)(2,1)S(1)} %copy-done.12), channel_id=1, source_target_pairs={{4,8},{5,9},{6,10},{7,11},{8,4},{9,5},{10,6},{11,7},{20,24},{21,25... | collective-permute-start | bytes 1966088 | tf_op jit(solution)/shard_map/ppermute | solution.py:147
  145.4 21.0 %collective-permute-start.18 = (bf16[512,640]{1,0:T(8,128)(2,1)}, bf16[512,640]{1,0:T(8,128)(2,1)S(1)}, u32[]{:S(2)}, u32[]{:S(2)}) collective-permute-start(bf16[512,640]{1,0:T(8,128)(2,1)} %collective-permute-done.17), channel_id=1, source_target_pairs={{4,0},{5,1},{6,2},{7,3},{8,12},{9,13},{10,14},{11,15},{20,16},{21,... | collective-permute-start | bytes 1966088 | tf_op jit(solution)/shard_map/ppermute | solution.py:147
  147.9 7.9 %collective-permute-start.16 = (bf16[1,160,640]{2,1,0:T(8,128)(2,1)S(1)}, bf16[1,160,640]{2,1,0:T(8,128)(2,1)S(1)}, u32[]{:S(2)}, u32[]{:S(2)}) collective-permute-start(bf16[1,160,640]{2,1,0:T(8,128)(2,1)S(1)} %fusion.34), channel_id=1, source_target_pairs={{0,2},{1,3},{2,0},{3,1},{4,6},{5,7},{6,4},{7,5},{8,10},{9,11},{10,... | collective-permute-start | bytes 614408 | tf_op jit(solution)/shard_map/ppermute | solution.py:144
  148.6 32.7 %collective-permute-start.22 = (bf16[512,640]{1,0:T(8,128)(2,1)S(1)}, bf16[512,640]{1,0:T(8,128)(2,1)S(1)}, u32[]{:S(2)}, u32[]{:S(2)}) collective-permute-start(bf16[512,640]{1,0:T(8,128)(2,1)S(1)} %collective-permute-done.21), channel_id=1, source_target_pairs={{4,0},{5,1},{6,2},{7,3},{8,12},{9,13},{10,14},{11,15},{20,16},{21,... | collective-permute-start | bytes 1966088 | tf_op jit(solution)/shard_map/ppermute | solution.py:147
  149.9 34.2 %collective-permute-start.13 = (bf16[1,160,640]{2,1,0:T(8,128)(2,1)S(1)}, bf16[1,160,640]{2,1,0:T(8,128)(2,1)S(1)}, u32[]{:S(2)}, u32[]{:S(2)}) collective-permute-start(bf16[1,160,640]{2,1,0:T(8,128)(2,1)S(1)} %fusion.33), channel_id=1, source_target_pairs={{0,2},{1,3},{2,0},{3,1},{4,6},{5,7},{6,4},{7,5},{8,10},{9,11},{10,... | collective-permute-start | bytes 614408 | tf_op jit(solution)/shard_map/ppermute | solution.py:144
  184.2 23.8 %collective-permute-start.23 = (bf16[2,160,640]{2,1,0:T(8,128)(2,1)}, bf16[2,160,640]{2,1,0:T(8,128)(2,1)}, u32[]{:S(2)}, u32[]{:S(2)}) collective-permute-start(bf16[2,160,640]{2,1,0:T(8,128)(2,1)} %fusion.28), channel_id=1, source_target_pairs={{0,1},{1,0},{2,3},{3,2},{4,5},{5,4},{6,7},{7,6},{8,9},{9,8},{10,11... | collective-permute-start | bytes 1228808 | tf_op jit(solution)/shard_map/ppermute | solution.py:144
  207.3 2.3 collective-permute-start.19
  209.0 8.0 %collective-permute-start.24 = (bf16[1,160,640]{2,1,0:T(8,128)(2,1)S(1)}, bf16[1,160,640]{2,1,0:T(8,128)(2,1)S(1)}, u32[]{:S(2)}, u32[]{:S(2)}) collective-permute-start(bf16[1,160,640]{2,1,0:T(8,128)(2,1)S(1)} %fusion.36), channel_id=1, source_target_pairs={{0,2},{1,3},{2,0},{3,1},{4,6},{5,7},{6,4},{7,5},{8,10},{9,11},{10,... | collective-permute-start | bytes 614408 | tf_op jit(solution)/shard_map/ppermute | solution.py:144
  209.8 10.7 %collective-permute-start.20 = (bf16[1,160,640]{2,1,0:T(8,128)(2,1)S(1)}, bf16[1,160,640]{2,1,0:T(8,128)(2,1)S(1)}, u32[]{:S(2)}, u32[]{:S(2)}) collective-permute-start(bf16[1,160,640]{2,1,0:T(8,128)(2,1)S(1)} %fusion.35), channel_id=1, source_target_pairs={{0,2},{1,3},{2,0},{3,1},{4,6},{5,7},{6,4},{7,5},{8,10},{9,11},{10,... | collective-permute-start | bytes 614408 | tf_op jit(solution)/shard_map/ppermute | solution.py:144

commit v2 on v0

v2 whole, which is shorter than its diff:
```python
import functools

import jax
import jax.numpy as jnp
from jax import lax
from jax.experimental import pallas as pl
from jax.experimental.pallas import tpu as pltpu
from jax.sharding import PartitionSpec as P

OUTER = 4
GROUP = 8
VMEM_LIMIT = 56 * 1024 * 1024
VMEM = pl.BlockSpec(memory_space=pltpu.VMEM)
SMEM = pl.BlockSpec(memory_space=pltpu.SMEM)
ANY = pl.BlockSpec(memory_space=pl.ANY)
BF16, F32 = jnp.bfloat16, jnp.float32


def smooth(flux, resolution):
    nobs = flux.shape[1]
    taps = resolution.shape[1]
    half = (taps - 1) // 2
    padded = jnp.pad(flux.astype(jnp.float32), ((0, 0), (half, half)))
    total = jnp.zeros(flux.shape, jnp.float32)
    for tap in range(taps):
        total = total + resolution[:, tap, :].astype(jnp.float32) * padded[:, tap : tap + nobs]
    return total.astype(jnp.bfloat16)


def call(kernel, out_shape, in_specs, args, scratch=(), flops=0, moved=0):
    return pl.pallas_call(
        kernel,
        out_shape=out_shape,
        in_specs=in_specs,
        out_specs=jax.tree.map(lambda _: VMEM, out_shape),
        scratch_shapes=scratch,
        compiler_params=pltpu.CompilerParams(vmem_limit_bytes=VMEM_LIMIT),
        cost_estimate=pl.CostEstimate(flops=flops, bytes_accessed=moved, transcendentals=0),
    )(*args)


def cut_kernel(halves, per, low, high, band, *refs):
    outer_ref, bins_ref, starts_ref = refs[:3]
    smoothed = refs[3 : 3 + halves]
    placing = refs[3 + halves : 3 + 2 * halves]
    back_ref = refs[3 + 2 * halves]
    outs = refs[4 + 2 * halves : 4 + 2 * halves + OUTER]
    placed, cut = refs[4 + 2 * halves + OUTER :]
    last = placed.shape[1] // band - 2
    mine = outer_ref[0]
    placed[...] = sum(
        jnp.dot(a[...], b[...], preferred_element_type=F32) for a, b in zip(placing, smoothed)
    )

    def one_group(group, carry):
        rows = pl.ds(pl.multiple_of(group * GROUP, GROUP), GROUP)
        entry = bins_ref[group]
        for away in range(OUTER):
            for j in range(low, high):
                start = starts_ref[entry, (mine ^ away) * per + j]
                chunk = jnp.minimum(start // band, last)
                shift = start - chunk * band
                wide = placed[rows, pl.ds(pl.multiple_of(chunk * band, band), 2 * band)]
                turned = pltpu.roll(wide, (2 * band - shift) & (2 * band - 1), 1)
                at = (away * (high - low) + j - low) * band
                cut[rows, at : at + band] = turned[:, :band]
        return carry

    lax.fori_loop(0, placed.shape[0] // GROUP, one_group, 0)
    width = (high - low) * band
    for away in range(OUTER):
        part = cut[:, away * width : (away + 1) * width].astype(BF16)
        outs[away][...] = jnp.dot(back_ref[...], part, preferred_element_type=F32).astype(BF16)


def cut_windows(outer, bins, starts, smoothed, placing, back, low, high, band):
    per = starts.shape[1] // OUTER
    rows, places = back.shape
    nobs = smoothed[0].shape[1]
    width = (high - low) * band
    return call(
        functools.partial(cut_kernel, len(smoothed), per, low, high, band),
        (jax.ShapeDtypeStruct((rows, width), BF16),) * OUTER,
        [SMEM] * 3 + [VMEM] * (2 * len(smoothed) + 1),
        (outer, bins, starts, *smoothed, *placing, back),
        [pltpu.VMEM((places, nobs), F32), pltpu.VMEM((places, OUTER * width), F32)],
        flops=4 * places * rows * nobs,
        moved=4 * rows * nobs,
    )


def rest_kernel(npieces, nbins, low, high, band, *refs):
    outer_ref, bins_ref, names_ref = refs[:3]
    windows = refs[3 : 3 + OUTER]
    weights = refs[3 + OUTER : 3 + OUTER + npieces]
    rest_ref, sent_ref, squares_ref = refs[3 + OUTER + npieces : 6 + OUTER + npieces]
    window, weight, window_sem, weight_sem = refs[6 + OUTER + npieces :]
    count = windows[0].shape[0]
    copies = []
    for away in range(OUTER):
        rows = pl.ds(pl.multiple_of((outer_ref[0] ^ away) * count, count), count)
        copies.append(pltpu.make_async_copy(windows[away], window.at[rows], window_sem.at[away]))
    pieces = [
        pltpu.make_async_copy(
            weights[p].at[:, pl.ds(low * band, (high - low) * band)], weight.at[p], weight_sem.at[p]
        )
        for p in range(npieces)
    ]
    for copy in copies + pieces:
        copy.start()
    for copy in copies:
        copy.wait()
    named = names_ref[...]
    total = jnp.zeros((OUTER * count, 1), F32)
    for p in range(npieces):
        pieces[p].wait()
        hits = [
            jnp.broadcast_to((named == bins_ref[p * nbins + b]).astype(F32), (OUTER * count, band)).astype(BF16)
            for b in range(nbins)
        ]
        for block in range(high - low):
            lanes = slice(block * band, (block + 1) * band)
            masked = jnp.concatenate([window[:, lanes] * hit for hit in hits], axis=1)
            columns = jnp.concatenate([weight[p, b, lanes, :] for b in range(nbins)], axis=1)
            value = lax.dot_general(
                masked, columns, (((1,), (1,)), ((), ())), preferred_element_type=F32
            )
            if p:
                value = value + rest_ref[:, lanes]
            rest_ref[:, lanes] = value
            if p == npieces - 1:
                sent_ref[:, lanes] = value.astype(BF16)
                total = total + jnp.sum(value * value, axis=1, keepdims=True)
    squares_ref[...] = total


def resample(outer, bins, names, windows, weights, low, high, band):
    count, width = windows[0].shape
    rows = OUTER * count
    npieces, nbins = len(weights), weights[0].shape[0]
    return call(
        functools.partial(rest_kernel, npieces, nbins, low, high, band),
        (
            jax.ShapeDtypeStruct((rows, width), F32),
            jax.ShapeDtypeStruct((rows, width), BF16),
            jax.ShapeDtypeStruct((rows, 1), F32),
        ),
        [SMEM, SMEM, VMEM] + [ANY] * (OUTER + npieces),
        (outer, bins, names, *windows, *weights),
        [
            pltpu.VMEM((rows, width), BF16),
            pltpu.VMEM((npieces, nbins, width, band), BF16),
            pltpu.SemaphoreType.DMA((OUTER,)),
            pltpu.SemaphoreType.DMA((npieces,)),
        ],
        flops=2 * rows * width * band * nbins * npieces,
        moved=rows * width * 8,
    )


def product_kernel(nleft, widths, choices, inner, *refs):
    pick_ref = refs[0]
    left = refs[1 : 1 + nleft]
    at = 1 + nleft
    options = []
    for number in choices:
        options.append(refs[at : at + number])
        at += number
    send_ref, keep_ref, block, result, sem = refs[at:]
    share = send_ref.shape[1]
    offset = 0
    copies = []
    for c, (width, option) in enumerate(zip(widths, options)):
        target = block.at[:, pl.ds(offset, width)]
        if len(option) == 1:
            pltpu.make_async_copy(option[0], target, sem.at[c]).start()
        else:

            @pl.when(pick_ref[1] == 0)
            def _(option=option, target=target, c=c):
                pltpu.make_async_copy(option[0], target, sem.at[c]).start()

            @pl.when(pick_ref[1] != 0)
            def _(option=option, target=target, c=c):
                pltpu.make_async_copy(option[1], target, sem.at[c]).start()

        copies.append(pltpu.make_async_copy(option[0], target, sem.at[c]))
        offset += width
    for copy in copies:
        copy.wait()
    row = 0
    for part in left:
        tall = part.shape[1]
        result[row : row + tall, :] = lax.dot_general(
            part[...], block[...], (((0,), (0,)), ((), ())), preferred_element_type=F32
        )
        row += tall
    for e in range(inner):
        rows = pl.ds(pl.multiple_of((pick_ref[0] ^ e) * share, 8), share)
        if e % 2:
            send_ref[e // 2] = result[rows, :].astype(BF16)
        else:
            keep_ref[e // 2] = result[rows, :]


def product(pick, left, options, inner):
    rows = left[0].shape[0]
    tall = sum(part.shape[1] for part in left)
    widths = [option[0].shape[1] for option in options]
    wide = sum(widths)
    share = tall // inner
    return call(
        functools.partial(product_kernel, len(left), widths, [len(o) for o in options], inner),
        (
            jax.ShapeDtypeStruct((inner // 2, share, wide), BF16),
            jax.ShapeDtypeStruct((inner // 2, share, wide), F32),
        ),
        [SMEM] + [VMEM] * len(left) + [ANY] * sum(len(o) for o in options),
        (pick, *left, *[array for option in options for array in option]),
        [
            pltpu.VMEM((rows, wide), BF16),
            pltpu.VMEM((tall, wide), F32),
            pltpu.SemaphoreType.DMA((len(options),)),
        ],
        flops=2 * rows * tall * wide,
        moved=rows * (tall + wide) * 2 + tall * wide * 3,
    )


def place_kernel(columns, width, *refs):
    at_ref, out_ref = refs[0], refs[-1]
    for i, (slot, offset) in enumerate(columns):
        held, got = refs[1 + 2 * i], refs[2 + 2 * i]
        start = pl.multiple_of(at_ref[slot] * width + offset, 128)
        out_ref[:, pl.ds(start, held.shape[1])] = held[...] + got[...].astype(F32)


def place(at, columns, pairs, width):
    share = pairs[0][0].shape[0]
    return call(
        functools.partial(place_kernel, columns, width),
        jax.ShapeDtypeStruct((share, OUTER * width), F32),
        [SMEM] + [VMEM] * (2 * len(pairs)),
        (at, *[array for pair in pairs for array in pair]),
        moved=share * width * OUTER * 10,
    )


def local(flux, resolution, destination, resample_weight, band_offset):
    n = lax.axis_size("spec")
    inner = n // OUTER
    count = flux.shape[0]
    nrest, band = resample_weight.shape[1:]
    nblocks = band_offset.shape[1]
    per = nblocks // OUTER
    width = nrest // OUTER
    me = lax.axis_index("spec")
    outer, q = me // inner, me % inner
    outer1 = outer.reshape(1)

    def swap(array, bit):
        return lax.ppermute(array, "spec", [(i, i ^ bit) for i in range(n)])

    def hop(array, pairs):
        return lax.ppermute(
            array, "spec", [(a * inner + i, b * inner + i) for a, b in pairs for i in range(inner)]
        )

    targets = destination[:, 0]
    table = jnp.concatenate([band_offset[0], targets])
    tables = [table] + [swap(table, away * inner) for away in range(1, OUTER)]
    names = [piece[nblocks:] for piece in tables]
    names = jnp.stack(names)
    column = jnp.stack([piece[:nblocks] for piece in tables])
    starts = jnp.stack([column] + [swap(column, e) for e in range(1, inner)], axis=1)
    starts = starts.reshape(n, nblocks)

    by_outer = resample_weight[0].reshape(OUTER, width, band)
    pieces = [lax.dynamic_index_in_dim(by_outer, outer, 0, keepdims=False)]
    for away in range(1, OUTER):
        theirs = lax.dynamic_index_in_dim(by_outer, outer ^ away, 0, keepdims=False)
        pieces.append(swap(theirs, away * inner))
    weights = [jnp.stack(pieces)]
    ids = [jnp.stack([me ^ (away * inner) for away in range(OUTER)])]
    bit = inner // 2
    while bit:
        weights = weights + [swap(piece, bit) for piece in weights]
        ids = ids + [piece ^ bit for piece in ids]
        bit //= 2
    bins = jnp.concatenate(ids)

    order = jnp.arange(count, dtype=jnp.int32)
    which = jnp.arange(n, dtype=jnp.int32)
    same = (targets[:, None] == targets[None, :]) & (order[:, None] > order[None, :])
    rank = jnp.sum(same.astype(jnp.int32), axis=1)
    filled = jnp.sum((targets[:, None] == which[None, :]).astype(jnp.int32), axis=0)
    groups = (filled + GROUP - 1) // GROUP
    before = jnp.sum(jnp.where(which[None, :] < targets[:, None], groups[None, :], 0), axis=1)
    position = before * GROUP + rank
    places = -(-(count + n * (GROUP - 1)) // (2 * GROUP)) * 2 * GROUP
    slot = jnp.arange(places, dtype=jnp.int32)
    placing = (slot[:, None] == position[None, :]).astype(BF16)
    back = (position[:, None] == slot[None, :]).astype(BF16)
    ends = jnp.sum(jnp.where(which[:, None] <= which[None, :], groups[:, None], 0), axis=0)
    group_bin = jnp.sum((ends[None, :] <= slot[: places // GROUP, None]).astype(jnp.int32), axis=1)
    group_entry = jnp.minimum(group_bin, n - 1) ^ me

    half = count // 2
    smoothed = [smooth(flux[i : i + half], resolution[i : i + half]) for i in (0, half)]
    placings = [placing[:, i : i + half] for i in (0, half)]

    rows = OUTER * count
    order_of = jnp.arange(OUTER, dtype=jnp.int32) ^ outer
    named = jnp.sum(
        jnp.where(order_of[:, None, None] == jnp.arange(OUTER)[None, :, None], names[None], 0), axis=1
    ).reshape(rows, 1)
    middle = ((outer == 1) | (outer == 2)).astype(jnp.int32)
    pick = jnp.stack([q, middle])
    chunks = [(0, (per + 1) // 2), ((per + 1) // 2, per)]
    rests, sents, squares = [], [], jnp.zeros((rows,), F32)
    for low, high in chunks:
        windows = cut_windows(outer1, group_entry, starts, smoothed, placings, back, low, high, band)
        arrived = [windows[0]] + [swap(windows[away], away * inner) for away in range(1, OUTER)]
        rest, sent, square = resample(outer1, bins, named, arrived, weights, low, high, band)
        rests.append(rest)
        sents.append(sent)
        squares = squares + square.reshape(rows)
    near = [hop(sent, [(0, 1), (1, 0), (2, 3), (3, 2)]) for sent in sents]
    across = [hop(sent, [(1, 2), (2, 1)]) for sent in sents]
    total = squares
    for away in range(1, OUTER):
        total = total + swap(squares, away * inner)
    scale = lax.rsqrt(total / nrest + 1e-06)
    left = [(rest * (scale * scale / (count * n))[:, None]).astype(BF16) for rest in rests]
    far = [hop(block, [(1, 2), (2, 1)]) for block in near]
    onward = [hop(block, [(1, 0), (2, 3)]) for block in across]
    end = [hop(block, [(1, 0), (2, 3)]) for block in far]

    at = jnp.stack([outer, outer ^ 1, jnp.where(outer < 2, 2, 1), jnp.where(outer < 2, 3, 0)])
    work = [
        (0, 0, [(block,) for block in sents]),
        (1, 0, [(block,) for block in near]),
        (2, 0, list(zip(onward, across))),
    ]
    offset = 0
    for pair in zip(end, far):
        work.append((3, offset, [pair]))
        offset += pair[0].shape[1]
    columns, pairs = [], []
    for where, offset, options in work:
        send, held = product(pick, left, options, inner)
        got = swap(send, 1)
        bit = 2
        while bit < inner:
            held = held + got.astype(F32)
            got = swap(held[1::2].astype(BF16), bit)
            held = held[0::2]
            bit *= 2
        columns.append((where, offset))
        pairs.append((held[0], got[0]))
    return place(at, columns, pairs, width)


def solution(mesh):
    in_specs = (
        P(("groups", "spec"), None),
        P(("groups", "spec"), None, None),
        P(("groups", "spec"), None),
        P("spec", None, None),
        P("spec", None),
    )
    out_specs = P(("groups", "spec"), None)
    return jax.shard_map(local, mesh=mesh, in_specs=in_specs, out_specs=out_specs, check_vma=False)
```

time: 389 us -> 195 us (0.50)
  waiting for transfers between devices: 320 us -> 59.1 us
  Pallas kernels: 0 us -> 48.7 us
  starting transfers between devices: 7.61 us -> 43.3 us
  other arithmetic: 2.22 us -> 29.2 us
  matrix products: 24.4 us -> 0 us
  between operations: 13.5 us -> 0.64 us
  local copies, waits for them, and re-layouts: 20.4 us -> 13.4 us
    reduce_scatter x1 -> x0, waiting for transfers between devices: 263 us -> none  [local(): lax.psum_scatter(product / total_spectra, 'spec', scatter_dimension=0, ti...]
    ppermute x0 -> x41, waiting for transfers between devices: none -> 59.1 us  [the longest x10 38.6 us: hop(): lax.ppermute(array, 'spec', [(a * inner + i, b * inner + i) for a, b in p...]
    all_to_all x1 -> x0, waiting for transfers between devices: 57.4 us -> none  [local(): lax.all_to_all(outgoing, 'spec', split_axis=0, concat_axis=0, tiled=True)]
    pallas_call x0 -> x10, Pallas kernels: none -> 48.7 us  [call(): pl.pallas_call(kernel, out_shape=out_shape, in_specs=in_specs, out_specs=...]
    ppermute x0 -> x41, starting transfers between devices: none -> 43.3 us  [the longest x31 33.4 us: swap(): return lax.ppermute(array, 'spec', [(i, i ^ bit) for i in range(n)])]
    dot_general x4 -> x0, matrix products: 24.4 us -> none  [the longest x1 12.6 us: local(): lax.dot_general(normed, normed, (((0,), (0,)), ((), ())), preferred_eleme...]
    convert_element_type x0 -> x6, other arithmetic: none -> 15.4 us  [the longest x2 10.7 us: smooth(): return total.astype(jnp.bfloat16)]
    gather x2 -> x0, local copies, waits for them, and re-layouts: 12.4 us -> none  [local(): jnp.take(rows, index, axis=1).reshape(senders * items, nblocks, band)]
  transfers between devices with their start and end apart: 2 -> 41, of which waited for: 2 -> 7; matrix products, arithmetic and copies ran while one was open for 0% -> 18% of each run, Pallas kernels for 0% -> 20%
where the time goes in v2:
time: 195 us; the launch traced here: 194 us
  waiting for transfers between devices  59.1 us (30%)
  Pallas kernels  48.7 us (25%)
  starting transfers between devices  43.3 us (22%)
  other arithmetic  29.2 us (15%)
  local copies, waits for them, and re-layouts  13.4 us (7%)
    pallas_call x10, Pallas kernels, call(): pl.pallas_call(kernel, out_shape=out_shape, in_specs=in_specs, out_specs=...  48.7 us
    ppermute x10, waiting for transfers between devices, hop(): lax.ppermute(array, 'spec', [(a * inner + i, b * inner + i) for a, b in p...  38.6 us
    ppermute x31, starting transfers between devices, swap(): return lax.ppermute(array, 'spec', [(i, i ^ bit) for i in range(n)])  33.4 us
    ppermute x31, waiting for transfers between devices, swap(): return lax.ppermute(array, 'spec', [(i, i ^ bit) for i in range(n)])  20.5 us
    convert_element_type x2, other arithmetic, smooth(): return total.astype(jnp.bfloat16)  10.7 us
    ppermute x10, starting transfers between devices, hop(): lax.ppermute(array, 'spec', [(a * inner + i, b * inner + i) for a, b in p...  9.91 us
    add x5, other arithmetic, local(): held = held + got.astype(F32)  5.73 us
    unnamed x54, local copies, waits for them, and re-layouts  5.24 us
  transfers between devices with their start and end apart: 41, of which 7 were waited for; matrix products, arithmetic and copies ran while one was open for 18% of the time, Pallas kernels for 20%

profile of v2, /device:TPU:0, one launch (start us, length us, event | category | flops | bytes accessed | tf_op | source)
XLA Modules:
  0.0 194.4 jit_solution(11597514938284555194)
XLA Ops:
  0.0 0.8 pad_add_fusion.3
  0.8 5.0 %collective-permute-start.2 = (s32[148]{0:T(256)S(1)}, s32[148]{0:T(256)S(1)}, u32[]{:S(2)}, u32[]{:S(2)}) collective-permute-start(s32[148]{0:T(256)S(1)} %pad_add_fusion.3), channel_id=1, source_target_pairs={{0,12},{1,13},{2,14},{3,15},{4,8},{5,9},{6,10},{7,11},{8,4},{9,5},... | collective-permute-start | bytes 1784 | tf_op jit(solution)/shard_map/ppermute | solution.py:262
  6.5 1.2 constant_dynamic-slice_fusion
  7.7 3.8 %collective-permute-start.11 = (bf16[640,128]{1,0:T(8,128)(2,1)S(1)}, bf16[640,128]{1,0:T(8,128)(2,1)S(1)}, u32[]{:S(2)}, u32[]{:S(2)}) collective-permute-start(bf16[640,128]{1,0:T(8,128)(2,1)S(1)} %get-tuple-element.58), channel_id=1, source_target_pairs={{0,12},{1,13},{2,14},{3,15},{4,8},{5,9},{6,10},{7,11},{8,4},{9,5},... | collective-permute-start | bytes 491528 | tf_op jit(solution)/shard_map/ppermute | solution.py:262
  11.5 0.9 convert_reduce_fusion
  12.4 0.8 convert_reduce_fusion.2
  13.2 0.7 select_reduce_fusion
  14.1 0.7 fusion.22.refs_7_
  15.7 0.7 fusion.26
  16.4 1.3 slice_convert_fusion
  17.7 5.4 %fusion.1.refs_4_ = bf16[64,3968]{1,0:T(8,128)(2,1)} fusion(f32[64,3968]{1,0:T(8,128)S(1)} %get-tuple-element.55, bf16[128,11,3968]{2,0,1:T(8,128)(2,1)} %param.6), kind=kLoop, calls=%fused_computation.2 | loop fusion | flops 8380416 | bytes 7110656 | tf_op jit(solution)/shard_map/convert_element_type | solution.py:27
  23.1 5.4 %fusion.12.refs_3_ = bf16[64,3968]{1,0:T(8,128)(2,1)} fusion(f32[64,3968]{1,0:T(8,128)S(1)} %get-tuple-element.56, bf16[128,11,3968]{2,0,1:T(8,128)(2,1)} %param.6), kind=kLoop, calls=%fused_computation.24 | loop fusion | flops 8380416 | bytes 7110656 | tf_op jit(solution)/shard_map/convert_element_type | solution.py:27
  29.8 4.7 %collective-permute-done.9 = bf16[640,128]{1,0:T(8,128)(2,1)S(1)} collective-permute-done((bf16[640,128]{1,0:T(8,128)(2,1)S(1)}, bf16[640,128]{1,0:T(8,128)(2,1)S(1)}, u32[]{:S(2)}, u32[]{:S(2)}) %collective-permute-start.9) | collective-permute-done | bytes 163872 | tf_op jit(solution)/shard_map/ppermute | solution.py:262
  34.5 1.6 collective-permute-start.12
  36.7 1.6 collective-permute-start.5
  38.4 10.4 %collective-permute-done.12.refs_8_ = bf16[4,640,128]{2,1,0:T(8,128)(2,1)S(1)} collective-permute-done((bf16[4,640,128]{2,1,0:T(8,128)(2,1)S(1)}, bf16[4,640,128]{2,1,0:T(8,128)(2,1)S(1)}, u32[]{:S(2)}, u32[]{:S(2)}) %collective-permute-start.12) | collective-permute-done | bytes 655392 | tf_op jit(solution)/shard_map/ppermute | solution.py:262
  49.7 6.9 %shard_map.57 = (bf16[128,256]{1,0:T(8,128)(2,1)}, bf16[128,256]{1,0:T(8,128)(2,1)}, bf16[128,256]{1,0:T(8,128)(2,1)}, bf16[128,256]{1,0:T(8,128)(2,1)}) custom-call(s32[1]{0:T(128)} %bitcast.refs_0_, s32[30]{0:T(128)} %minimum_xor_fusion.refs_1_, s32[16,20]{1,0:T(8,128)} %bitcast.133, bf16[64,3968]{1,0:T(8,128)(2,1)} %fusion.12.refs_3_, ...), custom_call_target="tpu_custom_call" | custom-call | flops 487587840 | bytes 2031616 | tf_op jit(solution)/shard_map/pallas_call | solution.py:31
  57.3 2.3 %collective-permute-start.16 = (bf16[128,256]{1,0:T(8,128)(2,1)}, bf16[128,256]{1,0:T(8,128)(2,1)S(1)}, u32[]{:S(2)}, u32[]{:S(2)}) collective-permute-start(bf16[128,256]{1,0:T(8,128)(2,1)} %get-tuple-element.37), channel_id=1, source_target_pairs={{0,8},{1,9},{2,10},{3,11},{4,12},{5,13},{6,14},{7,15},{8,0},{9,1},... | collective-permute-start | bytes 196616 | tf_op jit(solution)/shard_map/ppermute | solution.py:262
  59.6 1.5 collective-permute-start.17
  61.0 8.4 %shard_map.55 = (bf16[128,384]{1,0:T(8,128)(2,1)}, bf16[128,384]{1,0:T(8,128)(2,1)}, bf16[128,384]{1,0:T(8,128)(2,1)}, bf16[128,384]{1,0:T(8,128)(2,1)}) custom-call(s32[1]{0:T(128)} %bitcast.refs_0_, s32[30]{0:T(128)} %minimum_xor_fusion.refs_1_, s32[16,20]{1,0:T(8,128)} %bitcast.134, bf16[64,3968]{1,0:T(8,128)(2,1)} %fusion.12.refs_3_, ...), custom_call_target="tpu_custom_call" | custom-call | flops 487587840 | bytes 2031616 | tf_op jit(solution)/shard_map/pallas_call | solution.py:31
  69.8 2.6 %collective-permute-start.7 = (bf16[128,384]{1,0:T(8,128)(2,1)}, bf16[128,384]{1,0:T(8,128)(2,1)S(1)}, u32[]{:S(2)}, u32[]{:S(2)}) collective-permute-start(bf16[128,384]{1,0:T(8,128)(2,1)} %get-tuple-element.31), channel_id=1, source_target_pairs={{0,8},{1,9},{2,10},{3,11},{4,12},{5,13},{6,14},{7,15},{8,0},{9,1},... | collective-permute-start | bytes 294920 | tf_op jit(solution)/shard_map/ppermute | solution.py:262
  72.5 1.5 collective-permute-start.8
  74.0 0.9 copy.11.refs_2_
  75.0 0.8 copy-done.2
  75.9 5.0 %shard_map.58 = (f32[512,256]{1,0:T(8,128)}, bf16[512,256]{1,0:T(8,128)(2,1)}, f32[512,1]{1,0:T(8,128)}) custom-call(s32[1]{0:T(128)} %bitcast.refs_0_, s32[16]{0:T(128)} %concatenate.7.refs_1_, s32[512,1]{1,0:T(8,128)} %copy.11.refs_2_, bf16[128,256]{1,0:T(8,128)(2,1)} %get-tuple-element.35.refs_3_, bf16[128,256]{1,0:T(8,128)(2,1)} %copy-done.20, ...), custom_call_target="tpu_custom_call" | custom-call | flops 536870912 | bytes 1048576 | tf_op jit(solution)/shard_map/pallas_call | solution.py:31
  81.7 6.8 %shard_map.56 = (f32[512,384]{1,0:T(8,128)}, bf16[512,384]{1,0:T(8,128)(2,1)}, f32[512,1]{1,0:T(8,128)}) custom-call(s32[1]{0:T(128)} %bitcast.refs_0_, s32[16]{0:T(128)} %concatenate.7.refs_1_, s32[512,1]{1,0:T(8,128)} %copy.11.refs_2_, bf16[128,384]{1,0:T(8,128)(2,1)} %get-tuple-element.29.refs_3_, bf16[128,384]{1,0:T(8,128)(2,1)} %copy-done.16, ...), custom_call_target="tpu_custom_call" | custom-call | flops 805306368 | bytes 1572864 | tf_op jit(solution)/shard_map/pallas_call | solution.py:31
  88.4 1.2 add_reduce_fusion
  89.6 2.4 %collective-permute-start.20 = (f32[512]{0:T(512)S(1)}, f32[512]{0:T(512)S(1)}, u32[]{:S(2)}, u32[]{:S(2)}) collective-permute-start(f32[512]{0:T(512)S(1)} %add_reduce_fusion), channel_id=1, source_target_pairs={{0,12},{1,13},{2,14},{3,15},{4,8},{5,9},{6,10},{7,11},{8,4},{9,5},... | collective-permute-start | bytes 6152 | tf_op jit(solution)/shard_map/ppermute | solution.py:262
  92.2 1.8 collective-permute-start.18
  94.9 1.8 collective-permute-start.23
  96.7 2.0 %multiply_convert_fusion.refs_1_ = bf16[512,384]{1,0:T(8,128)(2,1)} fusion(f32[512,384]{1,0:T(8,128)} %get-tuple-element.33, f32[512]{0:T(512)S(1)} %multiply_multiply_fusion), kind=kLoop, calls=%fused_computation.63 | loop fusion | flops 393216 | bytes 1181696 | tf_op jit(solution)/shard_map/convert_element_type | solution.py:334
  98.7 1.9 multiply_convert_fusion.1.refs_2_
  100.6 4.0 %shard_map.59 = (bf16[2,160,640]{2,1,0:T(8,128)(2,1)}, f32[2,160,640]{2,1,0:T(8,128)}) custom-call(s32[2]{0:T(128)} %pad_add_fusion.5.refs_0_, bf16[512,384]{1,0:T(8,128)(2,1)} %multiply_convert_fusion.refs_1_, bf16[512,256]{1,0:T(8,128)(2,1)} %multiply_convert_fusion.1.refs_2_, bf16[512,384]{1,0:T(8,128)(2,1)} %get-tuple-element.41.refs_3_, ...), custom_call_target="tpu_custom_call" | custom-call | flops 419430400 | bytes 2539520 | tf_op jit(solution)/shard_map/pallas_call | solution.py:31
  107.4 1.3 collective-permute-start.30
  108.7 0.8 collective-permute-done.23.refs_3_
  109.5 0.8 copy-done.25
  110.3 4.0 %shard_map.60 = (bf16[2,160,640]{2,1,0:T(8,128)(2,1)}, f32[2,160,640]{2,1,0:T(8,128)}) custom-call(s32[2]{0:T(128)} %pad_add_fusion.5.refs_0_, bf16[512,384]{1,0:T(8,128)(2,1)} %multiply_convert_fusion.refs_1_, bf16[512,256]{1,0:T(8,128)(2,1)} %multiply_convert_fusion.1.refs_2_, bf16[512,384]{1,0:T(8,128)(2,1)} %copy-done.25, bf16[512,256]{1,0:T(8,128)(2,1)} %copy-done.26), custom_call_target="tpu_custom_call" | custom-call | flops 419430400 | bytes 2539520 | tf_op jit(solution)/shard_map/pallas_call | solution.py:31
  115.1 1.3 collective-permute-start.28
  116.4 1.3 collective-permute-start.38
  117.7 1.2 convert_add_fusion.2
  118.9 0.8 slice_bitcast_fusion.2.refs_1_
  119.7 31.5 %collective-permute-done.38.refs_3_ = bf16[512,256]{1,0:T(8,128)(2,1)S(1)} collective-permute-done((bf16[512,256]{1,0:T(8,128)(2,1)S(1)}, bf16[512,256]{1,0:T(8,128)(2,1)S(1)}, u32[]{:S(2)}, u32[]{:S(2)}) %collective-permute-start.38) | collective-permute-done | bytes 262176 | tf_op jit(solution)/shard_map/ppermute | solution.py:265
  151.3 1.5 collective-permute-start.22
  152.8 3.2 %shard_map.63 = (bf16[2,160,256]{2,1,0:T(8,128)(2,1)}, f32[2,160,256]{2,1,0:T(8,128)}) custom-call(s32[2]{0:T(128)} %pad_add_fusion.5.refs_0_, bf16[512,384]{1,0:T(8,128)(2,1)} %multiply_convert_fusion.refs_1_, bf16[512,256]{1,0:T(8,128)(2,1)} %multiply_convert_fusion.1.refs_2_, bf16[512,256]{1,0:T(8,128)(2,1)} %copy-done.11, bf16[512,256]{1,0:T(8,128)(2,1)} %copy-done.10), custom_call_target="tpu_custom_call" | custom-call | flops 167772160 | bytes 1409024 | tf_op jit(solution)/shard_map/pallas_call | solution.py:31
  156.7 0.7 copy-done.6
  157.5 4.0 %shard_map.61 = (bf16[2,160,640]{2,1,0:T(8,128)(2,1)}, f32[2,160,640]{2,1,0:T(8,128)}) custom-call(s32[2]{0:T(128)} %pad_add_fusion.5.refs_0_, bf16[512,384]{1,0:T(8,128)(2,1)} %multiply_convert_fusion.refs_1_, bf16[512,256]{1,0:T(8,128)(2,1)} %multiply_convert_fusion.1.refs_2_, bf16[512,384]{1,0:T(8,128)(2,1)} %copy-done.6, bf16[512,384]{1,0:T(8,128)(2,1)} %copy-done.5, ...), custom_call_target="tpu_custom_call" | custom-call | flops 419430400 | bytes 2539520 | tf_op jit(solution)/shard_map/pallas_call | solution.py:31
  161.5 1.3 collective-permute-start.34
  162.8 1.2 convert_add_fusion.1
  164.1 0.8 collective-permute-start.26
  164.9 0.8 slice_bitcast_fusion.1.refs_3_
  165.6 1.0 convert_add_fusion.4
  166.7 1.4 collective-permute-start.40
  168.7 6.2 %collective-permute-done.34.refs_3_ = bf16[512,384]{1,0:T(8,128)(2,1)S(1)} collective-permute-done((bf16[512,384]{1,0:T(8,128)(2,1)S(1)}, bf16[512,384]{1,0:T(8,128)(2,1)S(1)}, u32[]{:S(2)}, u32[]{:S(2)}) %collective-permute-start.34) | collective-permute-done | bytes 393248 | tf_op jit(solution)/shard_map/ppermute | solution.py:265
  174.9 0.7 copy-done.7
  175.7 3.5 %shard_map.62 = (bf16[2,160,384]{2,1,0:T(8,128)(2,1)}, f32[2,160,384]{2,1,0:T(8,128)}) custom-call(s32[2]{0:T(128)} %pad_add_fusion.5.refs_0_, bf16[512,384]{1,0:T(8,128)(2,1)} %multiply_convert_fusion.refs_1_, bf16[512,256]{1,0:T(8,128)(2,1)} %multiply_convert_fusion.1.refs_2_, bf16[512,384]{1,0:T(8,128)(2,1)} %copy-done.7, bf16[512,384]{1,0:T(8,128)(2,1)} %copy-done.4), custom_call_target="tpu_custom_call" | custom-call | flops 251658240 | bytes 1785856 | tf_op jit(solution)/shard_map/pallas_call | solution.py:31
  179.3 1.2 convert_add_fusion
  180.5 0.8 collective-permute-start.32
  181.3 0.8 slice_bitcast_fusion.refs_5_
  182.1 1.1 convert_add_fusion.3
  183.2 1.4 collective-permute-start.36
  184.6 0.7 slice_bitcast_fusion.3.refs_7_
  185.4 3.1 %collective-permute-done.32 = bf16[1,160,640]{2,1,0:T(8,128)(2,1)S(1)} collective-permute-done((bf16[1,160,640]{2,1,0:T(8,128)(2,1)S(1)}, bf16[1,160,640]{2,1,0:T(8,128)(2,1)S(1)}, u32[]{:S(2)}, u32[]{:S(2)}) %collective-permute-start.32) | collective-permute-done | bytes 204832 | tf_op jit(solution)/shard_map/ppermute | solution.py:262
  188.5 2.2 %collective-permute-done.36 = bf16[1,160,384]{2,1,0:T(8,128)(2,1)S(1)} collective-permute-done((bf16[1,160,384]{2,1,0:T(8,128)(2,1)S(1)}, bf16[1,160,384]{2,1,0:T(8,128)(2,1)S(1)}, u32[]{:S(2)}, u32[]{:S(2)}) %collective-permute-start.36) | collective-permute-done | bytes 122912 | tf_op jit(solution)/shard_map/ppermute | solution.py:262
  191.4 3.0 %shard_map.64 = f32[160,2560]{1,0:T(8,128)} custom-call(s32[4]{0:T(128)} %pad_add_fusion.4.refs_0_, f32[160,640]{1,0:T(8,128)} %slice_bitcast_fusion.2.refs_1_, bf16[160,640]{1,0:T(8,128)(2,1)} %bitcast.124, f32[160,640]{1,0:T(8,128)} %slice_bitcast_fusion.1.refs_3_, bf16[160,640]{1,0:T(8,128)(2,1)} %bitcast.125, f32[160,640]{1,0:T(8,128)} %slice_bitcast_fusion.refs_5_, ...), custom_call_target="tpu_custom_call" | custom-call | bytes 4096000 | tf_op jit(solution)/shard_map/pallas_call | solution.py:31
  (139 shorter events, 13.4 us)
Async XLA Ops:
  0.0 61.0 %copy-start.24 = (s32[128,1]{0,1:T(1,128)S(1)}, s32[128,1]{0,1:T(1,128)}, u32[]{:S(2)}) copy-start(s32[128,1]{0,1:T(1,128)} %param.7) | copy-start | bytes 1540
  0.0 36.1 %copy-start.23 = (s32[1,20]{1,0:T(1,128)S(1)}, s32[1,20]{1,0:T(1,128)}, u32[]{:S(2)}) copy-start(s32[1,20]{1,0:T(1,128)} %param.9) | copy-start | bytes 244
  0.8 28.3 %collective-permute-start.2 = (s32[148]{0:T(256)S(1)}, s32[148]{0:T(256)S(1)}, u32[]{:S(2)}, u32[]{:S(2)}) collective-permute-start(s32[148]{0:T(256)S(1)} %pad_add_fusion.3), channel_id=1, source_target_pairs={{0,12},{1,13},{2,14},{3,15},{4,8},{5,9},{6,10},{7,11},{8,4},{9,5},... | collective-permute-start | bytes 1784 | tf_op jit(solution)/shard_map/ppermute | solution.py:262
  5.9 30.3 %collective-permute-start.1 = (s32[148]{0:T(256)S(1)}, s32[148]{0:T(256)S(1)}, u32[]{:S(2)}, u32[]{:S(2)}) collective-permute-start(s32[148]{0:T(256)S(1)} %pad_add_fusion.3), channel_id=1, source_target_pairs={{0,8},{1,9},{2,10},{3,11},{4,12},{5,13},{6,14},{7,15},{8,0},{9,1},... | collective-permute-start | bytes 1784 | tf_op jit(solution)/shard_map/ppermute | solution.py:262
  5.9 30.3 %collective-permute-start = (s32[148]{0:T(256)S(1)}, s32[148]{0:T(256)S(1)}, u32[]{:S(2)}, u32[]{:S(2)}) collective-permute-start(s32[148]{0:T(256)S(1)} %pad_add_fusion.3), channel_id=1, source_target_pairs={{0,4},{1,5},{2,6},{3,7},{4,0},{5,1},{6,2},{7,3},{8,12},{9,13},{10,... | collective-permute-start | bytes 1784 | tf_op jit(solution)/shard_map/ppermute | solution.py:262
  7.7 22.1 %collective-permute-start.11 = (bf16[640,128]{1,0:T(8,128)(2,1)S(1)}, bf16[640,128]{1,0:T(8,128)(2,1)S(1)}, u32[]{:S(2)}, u32[]{:S(2)}) collective-permute-start(bf16[640,128]{1,0:T(8,128)(2,1)S(1)} %get-tuple-element.58), channel_id=1, source_target_pairs={{0,12},{1,13},{2,14},{3,15},{4,8},{5,9},{6,10},{7,11},{8,4},{9,5},... | collective-permute-start | bytes 491528 | tf_op jit(solution)/shard_map/ppermute | solution.py:262
  11.5 18.2 %collective-permute-start.10 = (bf16[640,128]{1,0:T(8,128)(2,1)S(1)}, bf16[640,128]{1,0:T(8,128)(2,1)S(1)}, u32[]{:S(2)}, u32[]{:S(2)}) collective-permute-start(bf16[640,128]{1,0:T(8,128)(2,1)S(1)} %get-tuple-element.59), channel_id=1, source_target_pairs={{0,8},{1,9},{2,10},{3,11},{4,12},{5,13},{6,14},{7,15},{8,0},{9,1},... | collective-permute-start | bytes 491528 | tf_op jit(solution)/shard_map/ppermute | solution.py:262
  29.1 5.3 %collective-permute-start.9 = (bf16[640,128]{1,0:T(8,128)(2,1)S(1)}, bf16[640,128]{1,0:T(8,128)(2,1)S(1)}, u32[]{:S(2)}, u32[]{:S(2)}) collective-permute-start(bf16[640,128]{1,0:T(8,128)(2,1)S(1)} %get-tuple-element.60), channel_id=1, source_target_pairs={{0,4},{1,5},{2,6},{3,7},{4,0},{5,1},{6,2},{7,3},{8,12},{9,13},{10,... | collective-permute-start | bytes 491528 | tf_op jit(solution)/shard_map/ppermute | solution.py:262
  34.5 40.4 %copy-start = (bf16[4,640,128]{2,1,0:T(8,128)(2,1)}, bf16[4,640,128]{2,1,0:T(8,128)(2,1)S(1)}, u32[]{:S(2)}) copy-start(bf16[4,640,128]{2,1,0:T(8,128)(2,1)S(1)} %pad_maximum_fusion.refs_7_) | copy-start | bytes 1966084
  34.5 14.3 %collective-permute-start.12 = (bf16[4,640,128]{2,1,0:T(8,128)(2,1)S(1)}, bf16[4,640,128]{2,1,0:T(8,128)(2,1)S(1)}, u32[]{:S(2)}, u32[]{:S(2)}) collective-permute-start(bf16[4,640,128]{2,1,0:T(8,128)(2,1)S(1)} %pad_maximum_fusion.refs_7_), channel_id=1, source_target_pairs={{0,2},{1,3},{2,0},{3,1},{4,6},{5,7},{6,4},{7,5},{8,10},{9,11},{10,... | collective-permute-start | bytes 1966088 | tf_op jit(solution)/shard_map/ppermute | solution.py:262
  36.2 12.8 %collective-permute-start.4 = (s32[4,20]{1,0:T(4,128)S(1)}, s32[4,20]{1,0:T(4,128)S(1)}, u32[]{:S(2)}, u32[]{:S(2)}) collective-permute-start(s32[4,20]{1,0:T(4,128)S(1)} %get-tuple-element.64), channel_id=1, source_target_pairs={{0,2},{1,3},{2,0},{3,1},{4,6},{5,7},{6,4},{7,5},{8,10},{9,11},{10,... | collective-permute-start | bytes 968 | tf_op jit(solution)/shard_map/ppermute | solution.py:262
  36.7 12.3 %collective-permute-start.3 = (s32[4,20]{1,0:T(4,128)S(1)}, s32[4,20]{1,0:T(4,128)S(1)}, u32[]{:S(2)}, u32[]{:S(2)}) collective-permute-start(s32[4,20]{1,0:T(4,128)S(1)} %get-tuple-element.64), channel_id=1, source_target_pairs={{0,1},{1,0},{2,3},{3,2},{4,5},{5,4},{6,7},{7,6},{8,9},{9,8},{10,11... | collective-permute-start | bytes 968 | tf_op jit(solution)/shard_map/ppermute | solution.py:262
  36.7 12.3 %collective-permute-start.5 = (s32[4,20]{1,0:T(4,128)S(1)}, s32[4,20]{1,0:T(4,128)S(1)}, u32[]{:S(2)}, u32[]{:S(2)}) collective-permute-start(s32[4,20]{1,0:T(4,128)S(1)} %get-tuple-element.64), channel_id=1, source_target_pairs={{0,3},{1,2},{2,1},{3,0},{4,7},{5,6},{6,5},{7,4},{8,11},{9,10},{10,... | collective-permute-start | bytes 968 | tf_op jit(solution)/shard_map/ppermute | solution.py:262
  38.4 36.5 %collective-permute-start.13 = (bf16[4,640,128]{2,1,0:T(8,128)(2,1)S(1)}, bf16[4,640,128]{2,1,0:T(8,128)(2,1)S(1)}, u32[]{:S(2)}, u32[]{:S(2)}) collective-permute-start(bf16[4,640,128]{2,1,0:T(8,128)(2,1)S(1)} %pad_maximum_fusion.refs_7_), channel_id=1, source_target_pairs={{0,1},{1,0},{2,3},{3,2},{4,5},{5,4},{6,7},{7,6},{8,9},{9,8},{10,11... | collective-permute-start | bytes 1966088 | tf_op jit(solution)/shard_map/ppermute | solution.py:262
  48.8 26.1 %copy-start.1 = (bf16[4,640,128]{2,1,0:T(8,128)(2,1)}, bf16[4,640,128]{2,1,0:T(8,128)(2,1)S(1)}, u32[]{:S(2)}) copy-start(bf16[4,640,128]{2,1,0:T(8,128)(2,1)S(1)} %collective-permute-done.12.refs_8_) | copy-start | bytes 1966084
  48.8 26.1 %collective-permute-start.14 = (bf16[4,640,128]{2,1,0:T(8,128)(2,1)S(1)}, bf16[4,640,128]{2,1,0:T(8,128)(2,1)S(1)}, u32[]{:S(2)}, u32[]{:S(2)}) collective-permute-start(bf16[4,640,128]{2,1,0:T(8,128)(2,1)S(1)} %collective-permute-done.12.refs_8_), channel_id=1, source_target_pairs={{0,1},{1,0},{2,3},{3,2},{4,5},{5,4},{6,7},{7,6},{8,9},{9,8},{10,11... | collective-permute-start | bytes 1966088 | tf_op jit(solution)/shard_map/ppermute | solution.py:262
  56.6 12.8 %collective-permute-start.15 = (bf16[128,256]{1,0:T(8,128)(2,1)}, bf16[128,256]{1,0:T(8,128)(2,1)S(1)}, u32[]{:S(2)}, u32[]{:S(2)}) collective-permute-start(bf16[128,256]{1,0:T(8,128)(2,1)} %get-tuple-element.36), channel_id=1, source_target_pairs={{0,4},{1,5},{2,6},{3,7},{4,0},{5,1},{6,2},{7,3},{8,12},{9,13},{10,... | collective-permute-start | bytes 196616 | tf_op jit(solution)/shard_map/ppermute | solution.py:262
  57.3 12.5 %collective-permute-start.16 = (bf16[128,256]{1,0:T(8,128)(2,1)}, bf16[128,256]{1,0:T(8,128)(2,1)S(1)}, u32[]{:S(2)}, u32[]{:S(2)}) collective-permute-start(bf16[128,256]{1,0:T(8,128)(2,1)} %get-tuple-element.37), channel_id=1, source_target_pairs={{0,8},{1,9},{2,10},{3,11},{4,12},{5,13},{6,14},{7,15},{8,0},{9,1},... | collective-permute-start | bytes 196616 | tf_op jit(solution)/shard_map/ppermute | solution.py:262
  59.6 12.9 %collective-permute-start.17 = (bf16[128,256]{1,0:T(8,128)(2,1)}, bf16[128,256]{1,0:T(8,128)(2,1)S(1)}, u32[]{:S(2)}, u32[]{:S(2)}) collective-permute-start(bf16[128,256]{1,0:T(8,128)(2,1)} %get-tuple-element.38), channel_id=1, source_target_pairs={{0,12},{1,13},{2,14},{3,15},{4,8},{5,9},{6,10},{7,11},{8,4},{9,5},... | collective-permute-start | bytes 196616 | tf_op jit(solution)/shard_map/ppermute | solution.py:262
  69.4 5.5 %copy-start.20 = (bf16[128,256]{1,0:T(8,128)(2,1)}, bf16[128,256]{1,0:T(8,128)(2,1)S(1)}, u32[]{:S(2)}) copy-start(bf16[128,256]{1,0:T(8,128)(2,1)S(1)} %collective-permute-done.15.refs_4_) | copy-start | bytes 196612
  69.5 11.5 %collective-permute-start.6 = (bf16[128,384]{1,0:T(8,128)(2,1)}, bf16[128,384]{1,0:T(8,128)(2,1)S(1)}, u32[]{:S(2)}, u32[]{:S(2)}) collective-permute-start(bf16[128,384]{1,0:T(8,128)(2,1)} %get-tuple-element.30), channel_id=1, source_target_pairs={{0,4},{1,5},{2,6},{3,7},{4,0},{5,1},{6,2},{7,3},{8,12},{9,13},{10,... | collective-permute-start | bytes 294920 | tf_op jit(solution)/shard_map/ppermute | solution.py:262
  69.8 5.1 %copy-start.21 = (bf16[128,256]{1,0:T(8,128)(2,1)}, bf16[128,256]{1,0:T(8,128)(2,1)S(1)}, u32[]{:S(2)}) copy-start(bf16[128,256]{1,0:T(8,128)(2,1)S(1)} %collective-permute-done.16.refs_5_) | copy-start | bytes 196612
  69.8 11.1 %collective-permute-start.7 = (bf16[128,384]{1,0:T(8,128)(2,1)}, bf16[128,384]{1,0:T(8,128)(2,1)S(1)}, u32[]{:S(2)}, u32[]{:S(2)}) collective-permute-start(bf16[128,384]{1,0:T(8,128)(2,1)} %get-tuple-element.31), channel_id=1, source_target_pairs={{0,8},{1,9},{2,10},{3,11},{4,12},{5,13},{6,14},{7,15},{8,0},{9,1},... | collective-permute-start | bytes 294920 | tf_op jit(solution)/shard_map/ppermute | solution.py:262
  72.5 2.5 %copy-start.22 = (bf16[128,256]{1,0:T(8,128)(2,1)}, bf16[128,256]{1,0:T(8,128)(2,1)S(1)}, u32[]{:S(2)}) copy-start(bf16[128,256]{1,0:T(8,128)(2,1)S(1)} %collective-permute-done.17.refs_6_) | copy-start | bytes 196612
  72.5 8.5 %collective-permute-start.8 = (bf16[128,384]{1,0:T(8,128)(2,1)}, bf16[128,384]{1,0:T(8,128)(2,1)S(1)}, u32[]{:S(2)}, u32[]{:S(2)}) collective-permute-start(bf16[128,384]{1,0:T(8,128)(2,1)} %get-tuple-element.32), channel_id=1, source_target_pairs={{0,12},{1,13},{2,14},{3,15},{4,8},{5,9},{6,10},{7,11},{8,4},{9,5},... | collective-permute-start | bytes 294920 | tf_op jit(solution)/shard_map/ppermute | solution.py:262
  74.9 0.8 copy-start.2
  74.9 1.1 copy-start.3
  89.6 7.1 %collective-permute-start.20 = (f32[512]{0:T(512)S(1)}, f32[512]{0:T(512)S(1)}, u32[]{:S(2)}, u32[]{:S(2)}) collective-permute-start(f32[512]{0:T(512)S(1)} %add_reduce_fusion), channel_id=1, source_target_pairs={{0,12},{1,13},{2,14},{3,15},{4,8},{5,9},{6,10},{7,11},{8,4},{9,5},... | collective-permute-start | bytes 6152 | tf_op jit(solution)/shard_map/ppermute | solution.py:262
  92.0 4.7 %collective-permute-start.19 = (f32[512]{0:T(512)S(1)}, f32[512]{0:T(512)S(1)}, u32[]{:S(2)}, u32[]{:S(2)}) collective-permute-start(f32[512]{0:T(512)S(1)} %add_reduce_fusion), channel_id=1, source_target_pairs={{0,8},{1,9},{2,10},{3,11},{4,12},{5,13},{6,14},{7,15},{8,0},{9,1},... | collective-permute-start | bytes 6152 | tf_op jit(solution)/shard_map/ppermute | solution.py:262
  92.2 4.5 %collective-permute-start.18 = (f32[512]{0:T(512)S(1)}, f32[512]{0:T(512)S(1)}, u32[]{:S(2)}, u32[]{:S(2)}) collective-permute-start(f32[512]{0:T(512)S(1)} %add_reduce_fusion), channel_id=1, source_target_pairs={{0,4},{1,5},{2,6},{3,7},{4,0},{5,1},{6,2},{7,3},{8,12},{9,13},{10,... | collective-permute-start | bytes 6152 | tf_op jit(solution)/shard_map/ppermute | solution.py:262
  94.7 11.4 %collective-permute-start.24 = (bf16[512,256]{1,0:T(8,128)(2,1)}, bf16[512,256]{1,0:T(8,128)(2,1)S(1)}, u32[]{:S(2)}, u32[]{:S(2)}) collective-permute-start(bf16[512,256]{1,0:T(8,128)(2,1)} %get-tuple-element.42.refs_4_), channel_id=1, source_target_pairs={{0,4},{1,5},{2,6},{3,7},{4,0},{5,1},{6,2},{7,3},{8,12},{9,13},{10,... | collective-permute-start | bytes 786440 | tf_op jit(solution)/shard_map/ppermute | solution.py:265
  94.9 14.6 %collective-permute-start.23 = (bf16[512,384]{1,0:T(8,128)(2,1)}, bf16[512,384]{1,0:T(8,128)(2,1)S(1)}, u32[]{:S(2)}, u32[]{:S(2)}) collective-permute-start(bf16[512,384]{1,0:T(8,128)(2,1)} %get-tuple-element.41.refs_3_), channel_id=1, source_target_pairs={{0,4},{1,5},{2,6},{3,7},{4,0},{5,1},{6,2},{7,3},{8,12},{9,13},{10,... | collective-permute-start | bytes 1179656 | tf_op jit(solution)/shard_map/ppermute | solution.py:265
  104.6 10.4 %collective-permute-start.21 = (bf16[2,160,640]{2,1,0:T(8,128)(2,1)}, bf16[2,160,640]{2,1,0:T(8,128)(2,1)S(1)}, u32[]{:S(2)}, u32[]{:S(2)}) collective-permute-start(bf16[2,160,640]{2,1,0:T(8,128)(2,1)} %get-tuple-element.44), channel_id=1, source_target_pairs={{0,1},{1,0},{2,3},{3,2},{4,5},{5,4},{6,7},{7,6},{8,9},{9,8},{10,11... | collective-permute-start | bytes 1228808 | tf_op jit(solution)/shard_map/ppermute | solution.py:262
  104.7 9.6 %collective-permute-start.27 = (bf16[512,384]{1,0:T(8,128)(2,1)}, bf16[512,384]{1,0:T(8,128)(2,1)S(1)}, u32[]{:S(2)}, u32[]{:S(2)}) collective-permute-start(bf16[512,384]{1,0:T(8,128)(2,1)} %get-tuple-element.41.refs_3_), channel_id=1, source_target_pairs={{4,8},{5,9},{6,10},{7,11},{8,4},{9,5},{10,6},{11,7},{20,24},{21,25... | collective-permute-start | bytes 1179656 | tf_op jit(solution)/shard_map/ppermute | solution.py:265
  105.4 2.0 %collective-permute-start.29 = (bf16[512,256]{1,0:T(8,128)(2,1)}, bf16[512,256]{1,0:T(8,128)(2,1)S(1)}, u32[]{:S(2)}, u32[]{:S(2)}) collective-permute-start(bf16[512,256]{1,0:T(8,128)(2,1)} %get-tuple-element.42.refs_4_), channel_id=1, source_target_pairs={{4,8},{5,9},{6,10},{7,11},{8,4},{9,5},{10,6},{11,7},{20,24},{21,25... | collective-permute-start | bytes 786440 | tf_op jit(solution)/shard_map/ppermute | solution.py:265
  106.1 3.4 %copy-start.26 = (bf16[512,256]{1,0:T(8,128)(2,1)}, bf16[512,256]{1,0:T(8,128)(2,1)S(1)}, u32[]{:S(2)}) copy-start(bf16[512,256]{1,0:T(8,128)(2,1)S(1)} %collective-permute-done.24.refs_4_) | copy-start | bytes 786436
  106.1 10.3 %collective-permute-start.37 = (bf16[512,256]{1,0:T(8,128)(2,1)S(1)}, bf16[512,256]{1,0:T(8,128)(2,1)S(1)}, u32[]{:S(2)}, u32[]{:S(2)}) collective-permute-start(bf16[512,256]{1,0:T(8,128)(2,1)S(1)} %collective-permute-done.24.refs_4_), channel_id=1, source_target_pairs={{4,8},{5,9},{6,10},{7,11},{8,4},{9,5},{10,6},{11,7},{20,24},{21,25... | collective-permute-start | bytes 786440 | tf_op jit(solution)/shard_map/ppermute | solution.py:265
  107.4 48.7 %copy-start.8 = (bf16[512,256]{1,0:T(8,128)(2,1)}, bf16[512,256]{1,0:T(8,128)(2,1)S(1)}, u32[]{:S(2)}) copy-start(bf16[512,256]{1,0:T(8,128)(2,1)S(1)} %collective-permute-done.29.refs_6_) | copy-start | bytes 786436
  107.4 48.6 %collective-permute-start.30 = (bf16[512,256]{1,0:T(8,128)(2,1)S(1)}, bf16[512,256]{1,0:T(8,128)(2,1)S(1)}, u32[]{:S(2)}, u32[]{:S(2)}) collective-permute-start(bf16[512,256]{1,0:T(8,128)(2,1)S(1)} %collective-permute-done.29.refs_6_), channel_id=1, source_target_pairs={{4,0},{5,1},{6,2},{7,3},{8,12},{9,13},{10,14},{11,15},{20,16},{21,... | collective-permute-start | bytes 786440 | tf_op jit(solution)/shard_map/ppermute | solution.py:265
  109.5 0.8 copy-start.25
  114.2 48.6 %collective-permute-start.25 = (bf16[2,160,640]{2,1,0:T(8,128)(2,1)}, bf16[2,160,640]{2,1,0:T(8,128)(2,1)S(1)}, u32[]{:S(2)}, u32[]{:S(2)}) collective-permute-start(bf16[2,160,640]{2,1,0:T(8,128)(2,1)} %get-tuple-element.46), channel_id=1, source_target_pairs={{0,1},{1,0},{2,3},{3,2},{4,5},{5,4},{6,7},{7,6},{8,9},{9,8},{10,11... | collective-permute-start | bytes 1228808 | tf_op jit(solution)/shard_map/ppermute | solution.py:262
  114.3 41.8 %copy-start.5 = (bf16[512,384]{1,0:T(8,128)(2,1)}, bf16[512,384]{1,0:T(8,128)(2,1)S(1)}, u32[]{:S(2)}) copy-start(bf16[512,384]{1,0:T(8,128)(2,1)S(1)} %collective-permute-done.27.refs_4_) | copy-start | bytes 1179652
  114.3 47.2 %collective-permute-start.33 = (bf16[512,384]{1,0:T(8,128)(2,1)}, bf16[512,384]{1,0:T(8,128)(2,1)S(1)}, u32[]{:S(2)}, u32[]{:S(2)}) collective-permute-start(bf16[512,384]{1,0:T(8,128)(2,1)} %copy-done.25), channel_id=1, source_target_pairs={{4,8},{5,9},{6,10},{7,11},{8,4},{9,5},{10,6},{11,7},{20,24},{21,25... | collective-permute-start | bytes 1179656 | tf_op jit(solution)/shard_map/ppermute | solution.py:265
  115.1 41.0 %collective-permute-start.28 = (bf16[512,384]{1,0:T(8,128)(2,1)S(1)}, bf16[512,384]{1,0:T(8,128)(2,1)S(1)}, u32[]{:S(2)}, u32[]{:S(2)}) collective-permute-start(bf16[512,384]{1,0:T(8,128)(2,1)S(1)} %collective-permute-done.27.refs_4_), channel_id=1, source_target_pairs={{4,0},{5,1},{6,2},{7,3},{8,12},{9,13},{10,14},{11,15},{20,16},{21,... | collective-permute-start | bytes 1179656 | tf_op jit(solution)/shard_map/ppermute | solution.py:265
  116.4 36.4 %copy-start.10 = (bf16[512,256]{1,0:T(8,128)(2,1)}, bf16[512,256]{1,0:T(8,128)(2,1)S(1)}, u32[]{:S(2)}) copy-start(bf16[512,256]{1,0:T(8,128)(2,1)S(1)} %collective-permute-done.37.refs_4_) | copy-start | bytes 786436
  116.4 34.9 %collective-permute-start.38 = (bf16[512,256]{1,0:T(8,128)(2,1)S(1)}, bf16[512,256]{1,0:T(8,128)(2,1)S(1)}, u32[]{:S(2)}, u32[]{:S(2)}) collective-permute-start(bf16[512,256]{1,0:T(8,128)(2,1)S(1)} %collective-permute-done.37.refs_4_), channel_id=1, source_target_pairs={{4,0},{5,1},{6,2},{7,3},{8,12},{9,13},{10,14},{11,15},{20,16},{21,... | collective-permute-start | bytes 786440 | tf_op jit(solution)/shard_map/ppermute | solution.py:265
  151.3 1.5 copy-start.11
  151.3 34.1 %collective-permute-start.22 = (bf16[1,160,640]{2,1,0:T(8,128)(2,1)S(1)}, bf16[1,160,640]{2,1,0:T(8,128)(2,1)S(1)}, u32[]{:S(2)}, u32[]{:S(2)}) collective-permute-start(bf16[1,160,640]{2,1,0:T(8,128)(2,1)S(1)} %slice.399), channel_id=1, source_target_pairs={{0,2},{1,3},{2,0},{3,1},{4,6},{5,7},{6,4},{7,5},{8,10},{9,11},{10,... | collective-permute-start | bytes 614408 | tf_op jit(solution)/shard_map/ppermute | solution.py:262
  156.0 0.7 copy-start.9
  156.0 9.6 %collective-permute-start.39 = (bf16[2,160,256]{2,1,0:T(8,128)(2,1)}, bf16[2,160,256]{2,1,0:T(8,128)(2,1)S(1)}, u32[]{:S(2)}, u32[]{:S(2)}) collective-permute-start(bf16[2,160,256]{2,1,0:T(8,128)(2,1)} %get-tuple-element.52), channel_id=1, source_target_pairs={{0,1},{1,0},{2,3},{3,2},{4,5},{5,4},{6,7},{7,6},{8,9},{9,8},{10,11... | collective-permute-start | bytes 491528 | tf_op jit(solution)/shard_map/ppermute | solution.py:262
  156.7 0.7 copy-start.6
  161.4 17.8 %collective-permute-start.31 = (bf16[2,160,640]{2,1,0:T(8,128)(2,1)}, bf16[2,160,640]{2,1,0:T(8,128)(2,1)S(1)}, u32[]{:S(2)}, u32[]{:S(2)}) collective-permute-start(bf16[2,160,640]{2,1,0:T(8,128)(2,1)} %get-tuple-element.48), channel_id=1, source_target_pairs={{0,1},{1,0},{2,3},{3,2},{4,5},{5,4},{6,7},{7,6},{8,9},{9,8},{10,11... | collective-permute-start | bytes 1228808 | tf_op jit(solution)/shard_map/ppermute | solution.py:262
  161.5 13.4 %copy-start.4 = (bf16[512,384]{1,0:T(8,128)(2,1)}, bf16[512,384]{1,0:T(8,128)(2,1)S(1)}, u32[]{:S(2)}) copy-start(bf16[512,384]{1,0:T(8,128)(2,1)S(1)} %collective-permute-done.33.refs_4_) | copy-start | bytes 1179652
  161.5 13.4 %collective-permute-start.34 = (bf16[512,384]{1,0:T(8,128)(2,1)S(1)}, bf16[512,384]{1,0:T(8,128)(2,1)S(1)}, u32[]{:S(2)}, u32[]{:S(2)}) collective-permute-start(bf16[512,384]{1,0:T(8,128)(2,1)S(1)} %collective-permute-done.33.refs_4_), channel_id=1, source_target_pairs={{4,0},{5,1},{6,2},{7,3},{8,12},{9,13},{10,14},{11,15},{20,16},{21,... | collective-permute-start | bytes 1179656 | tf_op jit(solution)/shard_map/ppermute | solution.py:265
  164.1 21.2 %collective-permute-start.26 = (bf16[1,160,640]{2,1,0:T(8,128)(2,1)S(1)}, bf16[1,160,640]{2,1,0:T(8,128)(2,1)S(1)}, u32[]{:S(2)}, u32[]{:S(2)}) collective-permute-start(bf16[1,160,640]{2,1,0:T(8,128)(2,1)S(1)} %slice.398), channel_id=1, source_target_pairs={{0,2},{1,3},{2,0},{3,1},{4,6},{5,7},{6,4},{7,5},{8,10},{9,11},{10,... | collective-permute-start | bytes 614408 | tf_op jit(solution)/shard_map/ppermute | solution.py:262
  166.7 18.7 %collective-permute-start.40 = (bf16[1,160,256]{2,1,0:T(8,128)(2,1)S(1)}, bf16[1,160,256]{2,1,0:T(8,128)(2,1)S(1)}, u32[]{:S(2)}, u32[]{:S(2)}) collective-permute-start(bf16[1,160,256]{2,1,0:T(8,128)(2,1)S(1)} %slice.401), channel_id=1, source_target_pairs={{0,2},{1,3},{2,0},{3,1},{4,6},{5,7},{6,4},{7,5},{8,10},{9,11},{10,... | collective-permute-start | bytes 245768 | tf_op jit(solution)/shard_map/ppermute | solution.py:262
  174.9 0.7 copy-start.7
  179.2 2.9 %collective-permute-start.35 = (bf16[2,160,384]{2,1,0:T(8,128)(2,1)}, bf16[2,160,384]{2,1,0:T(8,128)(2,1)S(1)}, u32[]{:S(2)}, u32[]{:S(2)}) collective-permute-start(bf16[2,160,384]{2,1,0:T(8,128)(2,1)} %get-tuple-element.50), channel_id=1, source_target_pairs={{0,1},{1,0},{2,3},{3,2},{4,5},{5,4},{6,7},{7,6},{8,9},{9,8},{10,11... | collective-permute-start | bytes 737288 | tf_op jit(solution)/shard_map/ppermute | solution.py:262
  180.5 7.9 %collective-permute-start.32 = (bf16[1,160,640]{2,1,0:T(8,128)(2,1)S(1)}, bf16[1,160,640]{2,1,0:T(8,128)(2,1)S(1)}, u32[]{:S(2)}, u32[]{:S(2)}) collective-permute-start(bf16[1,160,640]{2,1,0:T(8,128)(2,1)S(1)} %slice.397), channel_id=1, source_target_pairs={{0,2},{1,3},{2,0},{3,1},{4,6},{5,7},{6,4},{7,5},{8,10},{9,11},{10,... | collective-permute-start | bytes 614408 | tf_op jit(solution)/shard_map/ppermute | solution.py:262
  183.2 7.5 %collective-permute-start.36 = (bf16[1,160,384]{2,1,0:T(8,128)(2,1)S(1)}, bf16[1,160,384]{2,1,0:T(8,128)(2,1)S(1)}, u32[]{:S(2)}, u32[]{:S(2)}) collective-permute-start(bf16[1,160,384]{2,1,0:T(8,128)(2,1)S(1)} %slice.400), channel_id=1, source_target_pairs={{0,2},{1,3},{2,0},{3,1},{4,6},{5,7},{6,4},{7,5},{8,10},{9,11},{10,... | collective-permute-start | bytes 368648 | tf_op jit(solution)/shard_map/ppermute | solution.py:262
  185.3 5.4 %copy-start.12 = (bf16[1,160,640]{2,1,0:T(8,128)(2,1)}, bf16[1,160,640]{2,1,0:T(8,128)(2,1)S(1)}, u32[]{:S(2)}) copy-start(bf16[1,160,640]{2,1,0:T(8,128)(2,1)S(1)} %collective-permute-done.22) | copy-start | bytes 614404
  185.3 5.4 %copy-start.13 = (bf16[1,160,640]{2,1,0:T(8,128)(2,1)}, bf16[1,160,640]{2,1,0:T(8,128)(2,1)S(1)}, u32[]{:S(2)}) copy-start(bf16[1,160,640]{2,1,0:T(8,128)(2,1)S(1)} %collective-permute-done.26) | copy-start | bytes 614404
  185.4 5.4 %copy-start.19 = (bf16[1,160,256]{2,1,0:T(8,128)(2,1)}, bf16[1,160,256]{2,1,0:T(8,128)(2,1)S(1)}, u32[]{:S(2)}) copy-start(bf16[1,160,256]{2,1,0:T(8,128)(2,1)S(1)} %collective-permute-done.40) | copy-start | bytes 245764
  188.5 2.2 %copy-start.14 = (bf16[1,160,640]{2,1,0:T(8,128)(2,1)}, bf16[1,160,640]{2,1,0:T(8,128)(2,1)S(1)}, u32[]{:S(2)}) copy-start(bf16[1,160,640]{2,1,0:T(8,128)(2,1)S(1)} %collective-permute-done.32) | copy-start | bytes 614404
  (4 other events, 2.6 us)

commit v3 on v2

v3 whole, which is shorter than its diff:
```python
import functools

import jax
import jax.numpy as jnp
from jax import lax
from jax.experimental import pallas as pl
from jax.experimental.pallas import tpu as pltpu
from jax.sharding import PartitionSpec as P

OUTER = 4
GROUP = 8
VMEM_LIMIT = 16 * 1024 * 1024
VMEM = pl.BlockSpec(memory_space=pltpu.VMEM)
SMEM = pl.BlockSpec(memory_space=pltpu.SMEM)
BF16, F32 = jnp.bfloat16, jnp.float32


def smooth_kernel(reach, flux_ref, resolution_ref, out_ref, padded):
    rows, nobs = flux_ref.shape
    taps = resolution_ref.shape[0]
    edge = jnp.zeros((rows, reach), F32)
    padded[:, :reach] = edge
    padded[:, reach + nobs :] = edge
    padded[:, reach : reach + nobs] = flux_ref[...].astype(F32)
    step = 256
    for start in range(0, nobs, step):
        stop = min(nobs, start + step)
        total = jnp.zeros((rows, stop - start), F32)
        for tap in range(taps):
            first = reach + start + tap - (taps - 1) // 2
            total = total + resolution_ref[tap, :, start:stop].astype(F32) * padded[:, first : first + stop - start]
        out_ref[:, start:stop] = total.astype(BF16)


def smooth(flux, resolution):
    rows, nobs = flux.shape
    taps = resolution.shape[0]
    tall, reach = 16, 128
    return pl.pallas_call(
        functools.partial(smooth_kernel, reach),
        grid=(rows // tall,),
        out_shape=jax.ShapeDtypeStruct((rows, nobs), BF16),
        in_specs=[
            pl.BlockSpec((tall, nobs), lambda i: (i, 0)),
            pl.BlockSpec((taps, tall, nobs), lambda i: (0, i, 0)),
        ],
        out_specs=pl.BlockSpec((tall, nobs), lambda i: (i, 0)),
        scratch_shapes=[pltpu.VMEM((tall, nobs + 2 * reach), F32)],
        compiler_params=pltpu.CompilerParams(vmem_limit_bytes=50 * 1024 * 1024),
        cost_estimate=pl.CostEstimate(
            flops=2 * rows * taps * nobs, bytes_accessed=2 * rows * nobs * (taps + 2), transcendentals=0
        ),
    )(flux, resolution)


def call(kernel, out_shape, in_specs, args, scratch=(), flops=0, moved=0, limit=VMEM_LIMIT):
    return pl.pallas_call(
        kernel,
        out_shape=out_shape,
        in_specs=in_specs,
        out_specs=jax.tree.map(lambda _: VMEM, out_shape),
        scratch_shapes=scratch,
        compiler_params=pltpu.CompilerParams(vmem_limit_bytes=limit),
        cost_estimate=pl.CostEstimate(flops=flops, bytes_accessed=moved, transcendentals=0),
    )(*args)


def cut_kernel(per, low, high, band, *refs):
    outer_ref, bins_ref, starts_ref, smoothed_ref, placing_ref, back_ref = refs[:6]
    outs = refs[6 : 6 + OUTER]
    placed, cut = refs[6 + OUTER :]
    last = placed.shape[1] // band - 2
    mine = outer_ref[0]
    placed[...] = jnp.dot(placing_ref[...], smoothed_ref[...], preferred_element_type=F32)

    def one_group(group, carry):
        rows = pl.ds(pl.multiple_of(group * GROUP, GROUP), GROUP)
        entry = bins_ref[group]
        for away in range(OUTER):
            for j in range(low, high):
                start = starts_ref[entry, (mine ^ away) * per + j]
                chunk = jnp.minimum(start // band, last)
                shift = start - chunk * band
                wide = placed[rows, pl.ds(pl.multiple_of(chunk * band, band), 2 * band)]
                turned = pltpu.roll(wide, (2 * band - shift) & (2 * band - 1), 1)
                at = (away * (high - low) + j - low) * band
                cut[rows, at : at + band] = turned[:, :band]
        return carry

    lax.fori_loop(0, placed.shape[0] // GROUP, one_group, 0)
    width = (high - low) * band
    for away in range(OUTER):
        part = cut[:, away * width : (away + 1) * width].astype(BF16)
        outs[away][...] = jnp.dot(back_ref[...], part, preferred_element_type=F32).astype(BF16)


def cut_windows(outer, bins, starts, smoothed, placing, back, low, high, band):
    per = starts.shape[1] // OUTER
    rows, places = back.shape
    nobs = smoothed.shape[1]
    width = (high - low) * band
    return call(
        functools.partial(cut_kernel, per, low, high, band),
        (jax.ShapeDtypeStruct((rows, width), BF16),) * OUTER,
        [SMEM] * 3 + [VMEM] * 3,
        (outer, bins, starts, smoothed, placing, back),
        [pltpu.VMEM((places, nobs), F32), pltpu.VMEM((places, OUTER * width), F32)],
        flops=4 * places * rows * nobs,
        moved=4 * rows * nobs,
    )


def rest_kernel(npieces, nbins, low, high, band, *refs):
    outer_ref, bins_ref, names_ref = refs[:3]
    windows = refs[3 : 3 + OUTER]
    weights = refs[3 + OUTER : 3 + OUTER + npieces]
    rest_ref, sent_ref, squares_ref = refs[3 + OUTER + npieces : 6 + OUTER + npieces]
    window = refs[6 + OUTER + npieces]
    count = windows[0].shape[0]
    for away in range(OUTER):
        rows = pl.ds(pl.multiple_of((outer_ref[0] ^ away) * count, count), count)
        window[rows, :] = windows[away][...]
    named = names_ref[...]
    total = jnp.zeros((OUTER * count, 1), F32)
    for p in range(npieces):
        hits = [
            jnp.broadcast_to((named == bins_ref[p * nbins + b]).astype(F32), (OUTER * count, band)).astype(BF16)
            for b in range(nbins)
        ]
        for block in range(high - low):
            lanes = slice(block * band, (block + 1) * band)
            masked = jnp.concatenate([window[:, lanes] * hit for hit in hits], axis=1)
            columns = jnp.concatenate(
                [weights[p][b, (low + block) * band : (low + block + 1) * band, :] for b in range(nbins)], axis=1
            )
            value = lax.dot_general(
                masked, columns, (((1,), (1,)), ((), ())), preferred_element_type=F32
            )
            if p:
                value = value + rest_ref[:, lanes]
            rest_ref[:, lanes] = value
            if p == npieces - 1:
                sent_ref[:, lanes] = value.astype(BF16)
                total = total + jnp.sum(value * value, axis=1, keepdims=True)
    squares_ref[...] = total


def resample(outer, bins, names, windows, weights, low, high, band):
    count, width = windows[0].shape
    rows = OUTER * count
    npieces, nbins = len(weights), weights[0].shape[0]
    return call(
        functools.partial(rest_kernel, npieces, nbins, low, high, band),
        (
            jax.ShapeDtypeStruct((rows, width), F32),
            jax.ShapeDtypeStruct((rows, width), BF16),
            jax.ShapeDtypeStruct((rows, 1), F32),
        ),
        [SMEM, SMEM] + [VMEM] * (1 + OUTER + npieces),
        (outer, bins, names, *windows, *weights),
        [pltpu.VMEM((rows, width), BF16)],
        flops=2 * rows * width * band * nbins * npieces,
        moved=rows * width * 8,
        limit=VMEM_LIMIT + npieces * nbins * weights[0].shape[1] * band * 2,
    )


def place_kernel(columns, width, *refs):
    at_ref, out_ref = refs[0], refs[-1]
    for i, (slot, offset) in enumerate(columns):
        held, got = refs[1 + 2 * i], refs[2 + 2 * i]
        start = pl.multiple_of(at_ref[slot] * width + offset, 128)
        out_ref[:, pl.ds(start, held.shape[1])] = held[...] + got[...].astype(F32)


def place(at, columns, pairs, width):
    share = pairs[0][0].shape[0]
    return call(
        functools.partial(place_kernel, columns, width),
        jax.ShapeDtypeStruct((share, OUTER * width), F32),
        [SMEM] + [VMEM] * (2 * len(pairs)),
        (at, *[array for pair in pairs for array in pair]),
        moved=share * width * OUTER * 10,
    )


def local(flux, resolution, destination, resample_weight, band_offset):
    n = lax.axis_size("spec")
    inner = n // OUTER
    count = flux.shape[0]
    nrest, band = resample_weight.shape[1:]
    nblocks = band_offset.shape[1]
    per = nblocks // OUTER
    width = nrest // OUTER
    share = nrest // n
    me = lax.axis_index("spec")
    outer, q = me // inner, me % inner
    outer1 = outer.reshape(1)

    def swap(array, bit):
        return lax.ppermute(array, "spec", [(i, i ^ bit) for i in range(n)])

    def hop(array, pairs):
        return lax.ppermute(
            array, "spec", [(a * inner + i, b * inner + i) for a, b in pairs for i in range(inner)]
        )

    targets = destination[:, 0]
    table = jnp.concatenate([band_offset[0], targets])
    tables = [table] + [swap(table, away * inner) for away in range(1, OUTER)]
    names = [piece[nblocks:] for piece in tables]
    names = jnp.stack(names)
    column = jnp.stack([piece[:nblocks] for piece in tables])
    column, names, by_outer = lax.optimization_barrier(
        (column, names, resample_weight[0].reshape(OUTER, width, band))
    )
    starts = column[:, None]
    bit = 1
    while bit < inner:
        if 2 * bit == inner:
            starts, resolution = lax.optimization_barrier((starts, resolution))
        starts = jnp.concatenate([starts, swap(starts, bit)], axis=1)
        bit *= 2
    starts = starts.reshape(n, nblocks)

    smoothed = smooth(flux, jnp.transpose(resolution, (1, 0, 2)))

    pieces = [lax.dynamic_index_in_dim(by_outer, outer, 0, keepdims=False)]
    for away in range(1, OUTER):
        theirs = lax.dynamic_index_in_dim(by_outer, outer ^ away, 0, keepdims=False)
        pieces.append(swap(theirs, away * inner))
    pieces, smoothed, starts = lax.optimization_barrier((pieces, smoothed, starts))
    weights = [jnp.stack(pieces)]
    ids = [jnp.stack([me ^ (away * inner) for away in range(OUTER)])]
    bit = inner // 2
    weights = weights + [swap(weights[0], bit)]
    ids = ids + [ids[0] ^ bit]

    order = jnp.arange(count, dtype=jnp.int32)
    which = jnp.arange(n, dtype=jnp.int32)
    same = (targets[:, None] == targets[None, :]) & (order[:, None] > order[None, :])
    rank = jnp.sum(same.astype(jnp.int32), axis=1)
    filled = jnp.sum((targets[:, None] == which[None, :]).astype(jnp.int32), axis=0)
    groups = (filled + GROUP - 1) // GROUP
    before = jnp.sum(jnp.where(which[None, :] < targets[:, None], groups[None, :], 0), axis=1)
    position = before * GROUP + rank
    places = -(-(count + n * (GROUP - 1)) // (2 * GROUP)) * 2 * GROUP
    slot = jnp.arange(places, dtype=jnp.int32)
    placing = (slot[:, None] == position[None, :]).astype(BF16)
    back = (position[:, None] == slot[None, :]).astype(BF16)
    ends = jnp.sum(jnp.where(which[:, None] <= which[None, :], groups[:, None], 0), axis=0)
    group_bin = jnp.sum((ends[None, :] <= slot[: places // GROUP, None]).astype(jnp.int32), axis=1)
    group_entry = jnp.minimum(group_bin, n - 1) ^ me

    rows = OUTER * count
    order_of = jnp.arange(OUTER, dtype=jnp.int32) ^ outer
    named = jnp.sum(
        jnp.where(order_of[:, None, None] == jnp.arange(OUTER)[None, :, None], names[None], 0), axis=1
    ).reshape(rows, 1)
    windows = cut_windows(outer1, group_entry, starts, smoothed, placing, back, 0, per, band)
    arrived = [windows[0]] + [swap(windows[away], away * inner) for away in range(1, OUTER)]
    weights, arrived[1] = lax.optimization_barrier((weights, arrived[1]))
    while bit > 1:
        bit //= 2
        weights = weights + [swap(piece, bit) for piece in weights]
        ids = ids + [piece ^ bit for piece in ids]
    bins = jnp.concatenate(ids)
    rest, sent, squares = resample(outer1, bins, named, arrived, weights, 0, per, band)
    rests, sents, squares = [rest], [sent], squares.reshape(rows)
    ring = [(o, (o + 1) % OUTER) for o in range(OUTER)]
    blocks = [sents]
    for _ in range(1, OUTER):
        blocks.append([hop(block, ring) for block in blocks[-1]])
    total = squares
    for away in range(1, OUTER):
        total = total + swap(squares, away * inner)
    scale = lax.rsqrt(total / nrest + 1e-06)
    factor = (scale * scale / (count * n))[:, None]
    left = jnp.concatenate([(rest * factor).astype(BF16).T for rest in rests])
    left = left.reshape(inner, share, rows)
    left = jnp.stack([lax.dynamic_index_in_dim(left, q ^ e, 0, keepdims=False) for e in range(inner)])
    left = left.reshape(width, rows)

    at = (outer - jnp.arange(OUTER, dtype=jnp.int32)) % OUTER
    columns, pairs = [], []
    for slot_of, parts in enumerate(blocks):
        offset = 0
        for part in parts:
            wide = part.shape[1]
            held = jnp.dot(left, part, preferred_element_type=F32).reshape(inner, share, wide)
            bit = 1
            while bit < inner:
                got = swap(held[1::2].astype(BF16), bit)
                held = held[0::2]
                bit *= 2
                if bit < inner:
                    held = held + got.astype(F32)
            columns.append((slot_of, offset))
            pairs.append((held[0], got[0]))
            offset += wide
    return place(at, columns, pairs, width)


def solution(mesh):
    in_specs = (
        P(("groups", "spec"), None),
        P(("groups", "spec"), None, None),
        P(("groups", "spec"), None),
        P("spec", None, None),
        P("spec", None),
    )
    out_specs = P(("groups", "spec"), None)
    return jax.shard_map(local, mesh=mesh, in_specs=in_specs, out_specs=out_specs, check_vma=False)
```

time: 195 us -> 145 us (0.74)
  Pallas kernels: 48.7 us -> 24 us
  other arithmetic: 29.2 us -> 5.83 us
  starting transfers between devices: 43.3 us -> 32.3 us
  waiting for transfers between devices: 59.1 us -> 68.4 us
  matrix products: 0 us -> 3.84 us
  local copies, waits for them, and re-layouts: 13.4 us -> 9.73 us
    pallas_call x10 -> x3, Pallas kernels: 48.7 us -> 15.3 us  [call(): pl.pallas_call(kernel, out_shape=out_shape, in_specs=in_specs, out_specs=...]
    convert_element_type x5 -> x0, other arithmetic: 16 us -> none  [the longest x2 10.7 us: smooth(): return total.astype(jnp.bfloat16)]
    ppermute x10 -> x3, starting transfers between devices: 9.91 us -> 1.05 us  [hop(): lax.ppermute(array, 'spec', [(a * inner + i, b * inner + i) for a, b in p...]
    pallas_call x0 -> x1, Pallas kernels: none -> 8.68 us  [smooth(): pl.pallas_call(functools.partial(smooth_kernel, reach), grid=(rows // tal...]
    ppermute x31 -> x25, waiting for transfers between devices: 20.5 us -> 28.8 us  [swap(): return lax.ppermute(array, 'spec', [(i, i ^ bit) for i in range(n)])]
    add x5 -> x4, other arithmetic: 5.73 us -> 0.3 us  [local(): held = held + got.astype(F32)]
    dot_general x0 -> x4, matrix products: none -> 3.84 us  [local(): jnp.dot(left, part, preferred_element_type=F32).reshape(inner, share, wide)]
    squeeze x5 -> x4, local copies, waits for them, and re-layouts: 3.73 us -> 0.11 us  [local(): pairs.append((held[0], got[0]))]
  transfers between devices with their start and end apart: 41 -> 28, of which waited for: 7 -> 12; matrix products, arithmetic and copies ran while one was open for 18% -> 7% of each run, Pallas kernels for 20% -> 12%
where the time goes in v3:
time: 145 us
  waiting for transfers between devices  68.4 us (47%)
  starting transfers between devices  32.3 us (22%)
  Pallas kernels  24 us (17%)
  local copies, waits for them, and re-layouts  9.73 us (7%)
  other arithmetic  5.83 us (4%)
  matrix products  3.84 us (3%)
    ppermute x3, waiting for transfers between devices, hop(): lax.ppermute(array, 'spec', [(a * inner + i, b * inner + i) for a, b in p...  39.7 us
    ppermute x25, starting transfers between devices, swap(): return lax.ppermute(array, 'spec', [(i, i ^ bit) for i in range(n)])  31.3 us
    ppermute x25, waiting for transfers between devices, swap(): return lax.ppermute(array, 'spec', [(i, i ^ bit) for i in range(n)])  28.8 us
    pallas_call x3, Pallas kernels, call(): pl.pallas_call(kernel, out_shape=out_shape, in_specs=in_specs, out_specs=...  15.3 us
    pallas_call x1, Pallas kernels, smooth(): pl.pallas_call(functools.partial(smooth_kernel, reach), grid=(rows // tal...  8.68 us
    unnamed x18, local copies, waits for them, and re-layouts  7.4 us
    dot_general x4, matrix products, local(): jnp.dot(left, part, preferred_element_type=F32).reshape(inner, share, wide)  3.84 us
  transfers between devices with their start and end apart: 28, of which 12 were waited for; matrix products, arithmetic and copies ran while one was open for 7% of the time, Pallas kernels for 12%

profile of v3, /device:TPU:0, one launch (start us, length us, event | category | flops | bytes accessed | tf_op | source)
XLA Modules:
  0.0 144.6 jit_solution(15880157172542655278)
XLA Ops:
  0.0 0.8 pad_add_fusion.4
  0.8 5.0 %collective-permute-start.2 = (s32[148]{0:T(256)S(1)}, s32[148]{0:T(256)S(1)}, u32[]{:S(2)}, u32[]{:S(2)}) collective-permute-start(s32[148]{0:T(256)S(1)} %pad_add_fusion.4), channel_id=1, source_target_pairs={{0,12},{1,13},{2,14},{3,15},{4,8},{5,9},{6,10},{7,11},{8,4},{9,5},... | collective-permute-start | bytes 1784 | tf_op jit(solution)/shard_map/ppermute | solution.py:201
  5.9 0.6 collective-permute-start
  6.5 0.8 convert_reduce_fusion.2
  7.3 0.1 select_reduce_fusion.1
  7.4 0.7 select_reduce_fusion
  8.1 0.9 convert_reduce_fusion
  9.1 0.1 convert_reduce_fusion.1
  9.2 1.1 collective-permute-done.1
  10.4 0.7 pad_add_fusion.2
  11.2 0.7 pad_add_fusion.3
  11.9 1.2 dynamic-slice_bitcast_fusion
  13.1 0.4 collective-permute-start.3
  13.5 2.9 %collective-permute-start.4 = (bf16[640,128]{1,0:T(8,128)(2,1)S(1)}, bf16[640,128]{1,0:T(8,128)(2,1)S(1)}, u32[]{:S(2)}, u32[]{:S(2)}) collective-permute-start(bf16[640,128]{1,0:T(8,128)(2,1)S(1)} %get-tuple-element.54), channel_id=1, source_target_pairs={{0,8},{1,9},{2,10},{3,11},{4,12},{5,13},{6,14},{7,15},{8,0},{9,1},... | collective-permute-start | bytes 491528 | tf_op jit(solution)/shard_map/ppermute | solution.py:201
  16.4 1.1 collective-permute-start.5
  17.6 1.5 %collective-permute-start.7 = (s32[4,2,20]{2,0,1:T(4,128)S(1)}, s32[4,2,20]{2,0,1:T(4,128)S(1)}, u32[]{:S(2)}, u32[]{:S(2)}) collective-permute-start(s32[4,2,20]{2,0,1:T(4,128)S(1)} %pad_add_fusion.1), channel_id=1, source_target_pairs={{0,2},{1,3},{2,0},{3,1},{4,6},{5,7},{6,4},{7,5},{8,10},{9,11},{10,... | collective-permute-start | bytes 1928 | tf_op jit(solution)/shard_map/ppermute | solution.py:201
  19.1 8.7 %shard_map.55.refs_3_ = bf16[128,3968]{1,0:T(8,128)(2,1)S(1)} custom-call(bf16[128,3968]{1,0:T(8,128)(2,1)S(1)} %copy-done, bf16[11,128,3968]{2,1,0:T(8,128)(2,1)} %bitcast.77), custom_call_target="tpu_custom_call" | custom-call | flops 11173888 | bytes 13205504 | tf_op jit(solution)/shard_map/pallas_call | solution.py:39
  27.8 0.6 collective-permute-done.4
  28.5 0.1 pad_maximum_fusion.refs_7_
  28.6 1.6 %collective-permute-start.8 = (bf16[4,640,128]{2,1,0:T(8,128)(2,1)S(1)}, bf16[4,640,128]{2,1,0:T(8,128)(2,1)S(1)}, u32[]{:S(2)}, u32[]{:S(2)}) collective-permute-start(bf16[4,640,128]{2,1,0:T(8,128)(2,1)S(1)} %pad_maximum_fusion.refs_7_), channel_id=1, source_target_pairs={{0,2},{1,3},{2,0},{3,1},{4,6},{5,7},{6,4},{7,5},{8,10},{9,11},{10,... | collective-permute-start | bytes 1966088 | tf_op jit(solution)/shard_map/ppermute | solution.py:201
  30.2 0.1 fusion.9.refs_5_
  30.2 9.1 %shard_map.56 = (bf16[128,640]{1,0:T(8,128)(2,1)S(1)}, bf16[128,640]{1,0:T(8,128)(2,1)S(1)}, bf16[128,640]{1,0:T(8,128)(2,1)S(1)}, bf16[128,640]{1,0:T(8,128)(2,1)S(1)}) custom-call(s32[1]{0:T(128)} %bitcast.refs_0_, s32[30]{0:T(128)S(1)} %minimum_xor_fusion.refs_1_, s32[16,20]{1,0:T(8,128)S(1)} %bitcast.76, bf16[128,3968]{1,0:T(8,128)(2,1)S(1)} %shard_map.55.refs_3_, ...), custom_call_target="tpu_custom_call" | custom-call | flops 487587840 | bytes 2031616 | tf_op jit(solution)/shard_map/pallas_call | solution.py:57
  39.4 0.7 copy-done.7
  40.0 3.7 %collective-permute-start.9 = (bf16[128,640]{1,0:T(8,128)(2,1)S(1)}, bf16[128,640]{1,0:T(8,128)(2,1)S(1)}, u32[]{:S(2)}, u32[]{:S(2)}) collective-permute-start(bf16[128,640]{1,0:T(8,128)(2,1)S(1)} %get-tuple-element.38), channel_id=1, source_target_pairs={{0,4},{1,5},{2,6},{3,7},{4,0},{5,1},{6,2},{7,3},{8,12},{9,13},{10,... | collective-permute-start | bytes 491528 | tf_op jit(solution)/shard_map/ppermute | solution.py:201
  43.8 3.7 %collective-permute-done.9.refs_4_ = bf16[128,640]{1,0:T(8,128)(2,1)S(1)} collective-permute-done((bf16[128,640]{1,0:T(8,128)(2,1)S(1)}, bf16[128,640]{1,0:T(8,128)(2,1)S(1)}, u32[]{:S(2)}, u32[]{:S(2)}) %collective-permute-start.9) | collective-permute-done | bytes 163872 | tf_op jit(solution)/shard_map/ppermute | solution.py:201
  47.5 0.5 collective-permute-start.13
  48.0 0.8 copy-done.1
  48.9 2.9 %collective-permute-start.10 = (bf16[128,640]{1,0:T(8,128)(2,1)S(1)}, bf16[128,640]{1,0:T(8,128)(2,1)}, u32[]{:S(2)}, u32[]{:S(2)}) collective-permute-start(bf16[128,640]{1,0:T(8,128)(2,1)S(1)} %get-tuple-element.40), channel_id=1, source_target_pairs={{0,8},{1,9},{2,10},{3,11},{4,12},{5,13},{6,14},{7,15},{8,0},{9,1},... | collective-permute-start | bytes 491528 | tf_op jit(solution)/shard_map/ppermute | solution.py:201
  51.8 1.2 collective-permute-start.11
  53.1 0.1 select_reduce_fusion.2
  53.2 0.2 copy.15.refs_2_
  53.4 10.6 %collective-permute-done.10.refs_5_ = bf16[128,640]{1,0:T(8,128)(2,1)} collective-permute-done((bf16[128,640]{1,0:T(8,128)(2,1)S(1)}, bf16[128,640]{1,0:T(8,128)(2,1)}, u32[]{:S(2)}, u32[]{:S(2)}) %collective-permute-start.10) | collective-permute-done | bytes 163872 | tf_op jit(solution)/shard_map/ppermute | solution.py:201
  63.9 0.9 copy-done.3
  64.8 0.9 copy-done.5
  65.7 1.1 copy-done.2
  66.8 1.1 copy-done.4
  67.9 1.1 copy-done.6
  68.9 0.9 copy-done.8
  69.9 4.3 %shard_map.57 = (f32[512,640]{1,0:T(8,128)S(1)}, bf16[512,640]{1,0:T(8,128)(2,1)S(1)}, f32[512,1]{1,0:T(8,128)S(1)}) custom-call(s32[1]{0:T(128)} %bitcast.refs_0_, s32[16]{0:T(128)S(1)} %concatenate.13.refs_1_, s32[512,1]{1,0:T(8,128)S(1)} %copy.15.refs_2_, bf16[128,640]{1,0:T(8,128)(2,1)S(1)} %copy-done.8, ...), custom_call_target="tpu_custom_call" | custom-call | flops 1342177280 | bytes 2621440 | tf_op jit(solution)/shard_map/pallas_call | solution.py:57
  74.2 0.1 reduce
  74.3 3.5 %collective-permute-start.14 = (f32[512]{0:T(512)S(1)}, f32[512]{0:T(512)S(1)}, u32[]{:S(2)}, u32[]{:S(2)}) collective-permute-start(f32[512]{0:T(512)S(1)} %reduce), channel_id=1, source_target_pairs={{0,4},{1,5},{2,6},{3,7},{4,0},{5,1},{6,2},{7,3},{8,12},{9,13},{10,... | collective-permute-start | bytes 6152 | tf_op jit(solution)/shard_map/ppermute | solution.py:201
  77.8 0.9 collective-permute-start.15
  78.7 1.6 %collective-permute-start.16 = (f32[512]{0:T(512)S(1)}, f32[512]{0:T(512)S(1)}, u32[]{:S(2)}, u32[]{:S(2)}) collective-permute-start(f32[512]{0:T(512)S(1)} %reduce), channel_id=1, source_target_pairs={{0,12},{1,13},{2,14},{3,15},{4,8},{5,9},{6,10},{7,11},{8,4},{9,5},... | collective-permute-start | bytes 6152 | tf_op jit(solution)/shard_map/ppermute | solution.py:201
  80.3 1.0 collective-permute-start.19
  81.3 1.0 collective-permute-done.15
  82.3 1.8 %collective-permute-done.16 = f32[512]{0:T(512)S(1)} collective-permute-done((f32[512]{0:T(512)S(1)}, f32[512]{0:T(512)S(1)}, u32[]{:S(2)}, u32[]{:S(2)}) %collective-permute-start.16) | collective-permute-done | bytes 2080 | tf_op jit(solution)/shard_map/ppermute | solution.py:201
  84.1 0.1 fusion
  84.3 0.3 copy.16
  84.6 0.7 fusion.13
  85.4 12.3 %collective-permute-done.19 = bf16[512,640]{1,0:T(8,128)(2,1)} collective-permute-done((bf16[512,640]{1,0:T(8,128)(2,1)S(1)}, bf16[512,640]{1,0:T(8,128)(2,1)}, u32[]{:S(2)}, u32[]{:S(2)}) %collective-permute-start.19) | collective-permute-done | bytes 655392 | tf_op jit(solution)/shard_map/ppermute | solution.py:204
  97.8 1.8 %fusion.14 = (bf16[4,160,640]{2,1,0:T(8,128)(2,1)S(1)}, f32[4,160,640]{2,1,0:T(8,128)S(1)}) fusion(bf16[512,640]{1,0:T(8,128)(2,1)} %collective-permute-done.19, bf16[1,160,512]{2,1,0:T(8,128)(2,1)S(1)} %get-tuple-element.50, bf16[1,160,512]{2,1,0:T(8,128)(2,1)S(1)} %get-tuple-element.51, bf16[1,160,512]{2,1,0:T(8,128)(2,1)S(1)} %get-tuple-element.52, ...), kind=kOutput, calls=%fused_computation.76 | convolution fusion | flops 420823040 | bytes 3768320 | tf_op jit(solution)/shard_map/dot_general | solution.py:290
  99.7 0.1 convert_add_fusion.3
  99.8 0.9 collective-permute-start.18
  100.7 13.7 %collective-permute-done.22 = bf16[512,640]{1,0:T(8,128)(2,1)S(1)} collective-permute-done((bf16[512,640]{1,0:T(8,128)(2,1)}, bf16[512,640]{1,0:T(8,128)(2,1)S(1)}, u32[]{:S(2)}, u32[]{:S(2)}) %collective-permute-start.22) | collective-permute-done | bytes 655392 | tf_op jit(solution)/shard_map/ppermute | solution.py:204
  114.5 0.7 fusion.15
  115.4 0.9 collective-permute-start.21
  116.3 13.7 %collective-permute-done.25 = bf16[512,640]{1,0:T(8,128)(2,1)S(1)} collective-permute-done((bf16[512,640]{1,0:T(8,128)(2,1)S(1)}, bf16[512,640]{1,0:T(8,128)(2,1)S(1)}, u32[]{:S(2)}, u32[]{:S(2)}) %collective-permute-start.25) | collective-permute-done | bytes 655392 | tf_op jit(solution)/shard_map/ppermute | solution.py:204
  129.9 0.7 fusion.16
  130.8 0.9 collective-permute-start.24
  131.8 0.7 collective-permute-done.26
  132.6 0.9 collective-permute-start.27
  133.5 5.3 %collective-permute-done.24 = bf16[1,160,640]{2,1,0:T(8,128)(2,1)S(1)} collective-permute-done((bf16[1,160,640]{2,1,0:T(8,128)(2,1)S(1)}, bf16[1,160,640]{2,1,0:T(8,128)(2,1)S(1)}, u32[]{:S(2)}, u32[]{:S(2)}) %collective-permute-start.24) | collective-permute-done | bytes 204832 | tf_op jit(solution)/shard_map/ppermute | solution.py:201
  138.8 4.0 %collective-permute-done.27 = bf16[1,160,640]{2,1,0:T(8,128)(2,1)S(1)} collective-permute-done((bf16[1,160,640]{2,1,0:T(8,128)(2,1)S(1)}, bf16[1,160,640]{2,1,0:T(8,128)(2,1)S(1)}, u32[]{:S(2)}, u32[]{:S(2)}) %collective-permute-start.27) | collective-permute-done | bytes 204832 | tf_op jit(solution)/shard_map/ppermute | solution.py:201
  142.8 1.9 %shard_map.58 = f32[160,2560]{1,0:T(8,128)} custom-call(s32[4]{0:T(128)S(1)} %and_select_fusion.1.refs_0_, f32[160,640]{1,0:T(8,128)S(1)} %slice_bitcast_fusion.3.refs_1_, bf16[160,640]{1,0:T(8,128)(2,1)S(1)} %bitcast.72, f32[160,640]{1,0:T(8,128)S(1)} %slice_bitcast_fusion.2.refs_3_, bf16[160,640]{1,0:T(8,128)(2,1)S(1)} %bitcast.73, ...), custom_call_target="tpu_custom_call" | custom-call | bytes 4096000 | tf_op jit(solution)/shard_map/pallas_call | solution.py:57
  (73 shorter events, 1.5 us)
Async XLA Ops:
  0.0 19.1 %copy-start = (bf16[128,3968]{1,0:T(8,128)(2,1)S(1)}, bf16[128,3968]{1,0:T(8,128)(2,1)}, u32[]{:S(2)}) copy-start(bf16[128,3968]{1,0:T(8,128)(2,1)} %flux_ref.1) | copy-start | bytes 3047428
  0.8 8.4 %collective-permute-start.2 = (s32[148]{0:T(256)S(1)}, s32[148]{0:T(256)S(1)}, u32[]{:S(2)}, u32[]{:S(2)}) collective-permute-start(s32[148]{0:T(256)S(1)} %pad_add_fusion.4), channel_id=1, source_target_pairs={{0,12},{1,13},{2,14},{3,15},{4,8},{5,9},{6,10},{7,11},{8,4},{9,5},... | collective-permute-start | bytes 1784 | tf_op jit(solution)/shard_map/ppermute | solution.py:201
  5.9 4.5 %collective-permute-start.1 = (s32[148]{0:T(256)S(1)}, s32[148]{0:T(256)S(1)}, u32[]{:S(2)}, u32[]{:S(2)}) collective-permute-start(s32[148]{0:T(256)S(1)} %pad_add_fusion.4), channel_id=1, source_target_pairs={{0,8},{1,9},{2,10},{3,11},{4,12},{5,13},{6,14},{7,15},{8,0},{9,1},... | collective-permute-start | bytes 1784 | tf_op jit(solution)/shard_map/ppermute | solution.py:201
  5.9 4.5 %collective-permute-start = (s32[148]{0:T(256)S(1)}, s32[148]{0:T(256)S(1)}, u32[]{:S(2)}, u32[]{:S(2)}) collective-permute-start(s32[148]{0:T(256)S(1)} %pad_add_fusion.4), channel_id=1, source_target_pairs={{0,4},{1,5},{2,6},{3,7},{4,0},{5,1},{6,2},{7,3},{8,12},{9,13},{10,... | collective-permute-start | bytes 1784 | tf_op jit(solution)/shard_map/ppermute | solution.py:201
  11.9 5.7 %collective-permute-start.6 = (s32[4,1,20]{2,0,1:T(4,128)S(1)}, s32[4,1,20]{2,0,1:T(4,128)S(1)}, u32[]{:S(2)}, u32[]{:S(2)}) collective-permute-start(s32[4,1,20]{2,0,1:T(4,128)S(1)} %bitcast.85), channel_id=1, source_target_pairs={{0,1},{1,0},{2,3},{3,2},{4,5},{5,4},{6,7},{7,6},{8,9},{9,8},{10,11... | collective-permute-start | bytes 968 | tf_op jit(solution)/shard_map/ppermute | solution.py:201
  13.1 14.7 %collective-permute-start.3 = (bf16[640,128]{1,0:T(8,128)(2,1)S(1)}, bf16[640,128]{1,0:T(8,128)(2,1)S(1)}, u32[]{:S(2)}, u32[]{:S(2)}) collective-permute-start(bf16[640,128]{1,0:T(8,128)(2,1)S(1)} %get-tuple-element.55), channel_id=1, source_target_pairs={{0,4},{1,5},{2,6},{3,7},{4,0},{5,1},{6,2},{7,3},{8,12},{9,13},{10,... | collective-permute-start | bytes 491528 | tf_op jit(solution)/shard_map/ppermute | solution.py:201
  13.5 15.0 %collective-permute-start.4 = (bf16[640,128]{1,0:T(8,128)(2,1)S(1)}, bf16[640,128]{1,0:T(8,128)(2,1)S(1)}, u32[]{:S(2)}, u32[]{:S(2)}) collective-permute-start(bf16[640,128]{1,0:T(8,128)(2,1)S(1)} %get-tuple-element.54), channel_id=1, source_target_pairs={{0,8},{1,9},{2,10},{3,11},{4,12},{5,13},{6,14},{7,15},{8,0},{9,1},... | collective-permute-start | bytes 491528 | tf_op jit(solution)/shard_map/ppermute | solution.py:201
  16.4 12.0 %collective-permute-start.5 = (bf16[640,128]{1,0:T(8,128)(2,1)S(1)}, bf16[640,128]{1,0:T(8,128)(2,1)S(1)}, u32[]{:S(2)}, u32[]{:S(2)}) collective-permute-start(bf16[640,128]{1,0:T(8,128)(2,1)S(1)} %get-tuple-element.53), channel_id=1, source_target_pairs={{0,12},{1,13},{2,14},{3,15},{4,8},{5,9},{6,10},{7,11},{8,4},{9,5},... | collective-permute-start | bytes 491528 | tf_op jit(solution)/shard_map/ppermute | solution.py:201
  17.6 10.2 %collective-permute-start.7 = (s32[4,2,20]{2,0,1:T(4,128)S(1)}, s32[4,2,20]{2,0,1:T(4,128)S(1)}, u32[]{:S(2)}, u32[]{:S(2)}) collective-permute-start(s32[4,2,20]{2,0,1:T(4,128)S(1)} %pad_add_fusion.1), channel_id=1, source_target_pairs={{0,2},{1,3},{2,0},{3,1},{4,6},{5,7},{6,4},{7,5},{8,10},{9,11},{10,... | collective-permute-start | bytes 1928 | tf_op jit(solution)/shard_map/ppermute | solution.py:201
  28.6 18.9 %collective-permute-start.8 = (bf16[4,640,128]{2,1,0:T(8,128)(2,1)S(1)}, bf16[4,640,128]{2,1,0:T(8,128)(2,1)S(1)}, u32[]{:S(2)}, u32[]{:S(2)}) collective-permute-start(bf16[4,640,128]{2,1,0:T(8,128)(2,1)S(1)} %pad_maximum_fusion.refs_7_), channel_id=1, source_target_pairs={{0,2},{1,3},{2,0},{3,1},{4,6},{5,7},{6,4},{7,5},{8,10},{9,11},{10,... | collective-permute-start | bytes 1966088 | tf_op jit(solution)/shard_map/ppermute | solution.py:201
  39.4 0.7 copy-start.7
  40.0 7.5 %collective-permute-start.9 = (bf16[128,640]{1,0:T(8,128)(2,1)S(1)}, bf16[128,640]{1,0:T(8,128)(2,1)S(1)}, u32[]{:S(2)}, u32[]{:S(2)}) collective-permute-start(bf16[128,640]{1,0:T(8,128)(2,1)S(1)} %get-tuple-element.38), channel_id=1, source_target_pairs={{0,4},{1,5},{2,6},{3,7},{4,0},{5,1},{6,2},{7,3},{8,12},{9,13},{10,... | collective-permute-start | bytes 491528 | tf_op jit(solution)/shard_map/ppermute | solution.py:201
  47.5 16.4 %collective-permute-start.12 = (bf16[4,640,128]{2,1,0:T(8,128)(2,1)S(1)}, bf16[4,640,128]{2,1,0:T(8,128)(2,1)S(1)}, u32[]{:S(2)}, u32[]{:S(2)}) collective-permute-start(bf16[4,640,128]{2,1,0:T(8,128)(2,1)S(1)} %pad_maximum_fusion.refs_7_), channel_id=1, source_target_pairs={{0,1},{1,0},{2,3},{3,2},{4,5},{5,4},{6,7},{7,6},{8,9},{9,8},{10,11... | collective-permute-start | bytes 1966088 | tf_op jit(solution)/shard_map/ppermute | solution.py:201
  47.5 17.3 %collective-permute-start.13 = (bf16[4,640,128]{2,1,0:T(8,128)(2,1)S(1)}, bf16[4,640,128]{2,1,0:T(8,128)(2,1)S(1)}, u32[]{:S(2)}, u32[]{:S(2)}) collective-permute-start(bf16[4,640,128]{2,1,0:T(8,128)(2,1)S(1)} %collective-permute-done.8.refs_8_), channel_id=1, source_target_pairs={{0,1},{1,0},{2,3},{3,2},{4,5},{5,4},{6,7},{7,6},{8,9},{9,8},{10,11... | collective-permute-start | bytes 1966088 | tf_op jit(solution)/shard_map/ppermute | solution.py:201
  48.0 0.8 copy-start.1
  48.9 15.1 %collective-permute-start.10 = (bf16[128,640]{1,0:T(8,128)(2,1)S(1)}, bf16[128,640]{1,0:T(8,128)(2,1)}, u32[]{:S(2)}, u32[]{:S(2)}) collective-permute-start(bf16[128,640]{1,0:T(8,128)(2,1)S(1)} %get-tuple-element.40), channel_id=1, source_target_pairs={{0,8},{1,9},{2,10},{3,11},{4,12},{5,13},{6,14},{7,15},{8,0},{9,1},... | collective-permute-start | bytes 491528 | tf_op jit(solution)/shard_map/ppermute | solution.py:201
  51.8 12.1 %collective-permute-start.11 = (bf16[128,640]{1,0:T(8,128)(2,1)S(1)}, bf16[128,640]{1,0:T(8,128)(2,1)}, u32[]{:S(2)}, u32[]{:S(2)}) collective-permute-start(bf16[128,640]{1,0:T(8,128)(2,1)S(1)} %get-tuple-element.41), channel_id=1, source_target_pairs={{0,12},{1,13},{2,14},{3,15},{4,8},{5,9},{6,10},{7,11},{8,4},{9,5},... | collective-permute-start | bytes 491528 | tf_op jit(solution)/shard_map/ppermute | solution.py:201
  63.9 0.9 copy-start.3
  64.8 0.9 copy-start.5
  65.7 1.1 copy-start.2
  66.8 1.1 copy-start.4
  67.9 1.1 copy-start.6
  68.9 0.9 copy-start.8
  74.3 7.0 %collective-permute-start.14 = (f32[512]{0:T(512)S(1)}, f32[512]{0:T(512)S(1)}, u32[]{:S(2)}, u32[]{:S(2)}) collective-permute-start(f32[512]{0:T(512)S(1)} %reduce), channel_id=1, source_target_pairs={{0,4},{1,5},{2,6},{3,7},{4,0},{5,1},{6,2},{7,3},{8,12},{9,13},{10,... | collective-permute-start | bytes 6152 | tf_op jit(solution)/shard_map/ppermute | solution.py:201
  77.8 4.5 %collective-permute-start.15 = (f32[512]{0:T(512)S(1)}, f32[512]{0:T(512)S(1)}, u32[]{:S(2)}, u32[]{:S(2)}) collective-permute-start(f32[512]{0:T(512)S(1)} %reduce), channel_id=1, source_target_pairs={{0,8},{1,9},{2,10},{3,11},{4,12},{5,13},{6,14},{7,15},{8,0},{9,1},... | collective-permute-start | bytes 6152 | tf_op jit(solution)/shard_map/ppermute | solution.py:201
  78.7 5.4 %collective-permute-start.16 = (f32[512]{0:T(512)S(1)}, f32[512]{0:T(512)S(1)}, u32[]{:S(2)}, u32[]{:S(2)}) collective-permute-start(f32[512]{0:T(512)S(1)} %reduce), channel_id=1, source_target_pairs={{0,12},{1,13},{2,14},{3,15},{4,8},{5,9},{6,10},{7,11},{8,4},{9,5},... | collective-permute-start | bytes 6152 | tf_op jit(solution)/shard_map/ppermute | solution.py:201
  80.3 17.5 %collective-permute-start.19 = (bf16[512,640]{1,0:T(8,128)(2,1)S(1)}, bf16[512,640]{1,0:T(8,128)(2,1)}, u32[]{:S(2)}, u32[]{:S(2)}) collective-permute-start(bf16[512,640]{1,0:T(8,128)(2,1)S(1)} %get-tuple-element.46), channel_id=1, source_target_pairs={{0,4},{1,5},{2,6},{3,7},{4,8},{5,9},{6,10},{7,11},{8,12},{9,13},{1... | collective-permute-start | bytes 1966088 | tf_op jit(solution)/shard_map/ppermute | solution.py:204
  85.3 14.4 %collective-permute-start.17 = (bf16[2,160,640]{2,1,0:T(8,128)(2,1)S(1)}, bf16[2,160,640]{2,1,0:T(8,128)(2,1)S(1)}, u32[]{:S(2)}, u32[]{:S(2)}) collective-permute-start(bf16[2,160,640]{2,1,0:T(8,128)(2,1)S(1)} %slice.93), channel_id=1, source_target_pairs={{0,1},{1,0},{2,3},{3,2},{4,5},{5,4},{6,7},{7,6},{8,9},{9,8},{10,11... | collective-permute-start | bytes 1228808 | tf_op jit(solution)/shard_map/ppermute | solution.py:201
  97.8 16.6 %collective-permute-start.22 = (bf16[512,640]{1,0:T(8,128)(2,1)}, bf16[512,640]{1,0:T(8,128)(2,1)S(1)}, u32[]{:S(2)}, u32[]{:S(2)}) collective-permute-start(bf16[512,640]{1,0:T(8,128)(2,1)} %collective-permute-done.19), channel_id=1, source_target_pairs={{0,4},{1,5},{2,6},{3,7},{4,8},{5,9},{6,10},{7,11},{8,12},{9,13},{1... | collective-permute-start | bytes 1966088 | tf_op jit(solution)/shard_map/ppermute | solution.py:204
  99.6 14.8 %collective-permute-start.20 = (bf16[2,160,640]{2,1,0:T(8,128)(2,1)S(1)}, bf16[2,160,640]{2,1,0:T(8,128)(2,1)S(1)}, u32[]{:S(2)}, u32[]{:S(2)}) collective-permute-start(bf16[2,160,640]{2,1,0:T(8,128)(2,1)S(1)} %slice.97), channel_id=1, source_target_pairs={{0,1},{1,0},{2,3},{3,2},{4,5},{5,4},{6,7},{7,6},{8,9},{9,8},{10,11... | collective-permute-start | bytes 1228808 | tf_op jit(solution)/shard_map/ppermute | solution.py:201
  99.8 33.7 %collective-permute-start.18 = (bf16[1,160,640]{2,1,0:T(8,128)(2,1)S(1)}, bf16[1,160,640]{2,1,0:T(8,128)(2,1)S(1)}, u32[]{:S(2)}, u32[]{:S(2)}) collective-permute-start(bf16[1,160,640]{2,1,0:T(8,128)(2,1)S(1)} %slice.137), channel_id=1, source_target_pairs={{0,2},{1,3},{2,0},{3,1},{4,6},{5,7},{6,4},{7,5},{8,10},{9,11},{10,... | collective-permute-start | bytes 614408 | tf_op jit(solution)/shard_map/ppermute | solution.py:201
  114.4 15.5 %collective-permute-start.25 = (bf16[512,640]{1,0:T(8,128)(2,1)S(1)}, bf16[512,640]{1,0:T(8,128)(2,1)S(1)}, u32[]{:S(2)}, u32[]{:S(2)}) collective-permute-start(bf16[512,640]{1,0:T(8,128)(2,1)S(1)} %collective-permute-done.22), channel_id=1, source_target_pairs={{0,4},{1,5},{2,6},{3,7},{4,8},{5,9},{6,10},{7,11},{8,12},{9,13},{1... | collective-permute-start | bytes 1966088 | tf_op jit(solution)/shard_map/ppermute | solution.py:204
  115.2 15.5 %collective-permute-start.23 = (bf16[2,160,640]{2,1,0:T(8,128)(2,1)S(1)}, bf16[2,160,640]{2,1,0:T(8,128)(2,1)S(1)}, u32[]{:S(2)}, u32[]{:S(2)}) collective-permute-start(bf16[2,160,640]{2,1,0:T(8,128)(2,1)S(1)} %slice.101), channel_id=1, source_target_pairs={{0,1},{1,0},{2,3},{3,2},{4,5},{5,4},{6,7},{7,6},{8,9},{9,8},{10,11... | collective-permute-start | bytes 1228808 | tf_op jit(solution)/shard_map/ppermute | solution.py:201
  115.4 18.1 %collective-permute-start.21 = (bf16[1,160,640]{2,1,0:T(8,128)(2,1)S(1)}, bf16[1,160,640]{2,1,0:T(8,128)(2,1)S(1)}, u32[]{:S(2)}, u32[]{:S(2)}) collective-permute-start(bf16[1,160,640]{2,1,0:T(8,128)(2,1)S(1)} %slice.136), channel_id=1, source_target_pairs={{0,2},{1,3},{2,0},{3,1},{4,6},{5,7},{6,4},{7,5},{8,10},{9,11},{10,... | collective-permute-start | bytes 614408 | tf_op jit(solution)/shard_map/ppermute | solution.py:201
  130.6 1.8 %collective-permute-start.26 = (bf16[2,160,640]{2,1,0:T(8,128)(2,1)S(1)}, bf16[2,160,640]{2,1,0:T(8,128)(2,1)S(1)}, u32[]{:S(2)}, u32[]{:S(2)}) collective-permute-start(bf16[2,160,640]{2,1,0:T(8,128)(2,1)S(1)} %slice.105), channel_id=1, source_target_pairs={{0,1},{1,0},{2,3},{3,2},{4,5},{5,4},{6,7},{7,6},{8,9},{9,8},{10,11... | collective-permute-start | bytes 1228808 | tf_op jit(solution)/shard_map/ppermute | solution.py:201
  130.8 7.9 %collective-permute-start.24 = (bf16[1,160,640]{2,1,0:T(8,128)(2,1)S(1)}, bf16[1,160,640]{2,1,0:T(8,128)(2,1)S(1)}, u32[]{:S(2)}, u32[]{:S(2)}) collective-permute-start(bf16[1,160,640]{2,1,0:T(8,128)(2,1)S(1)} %slice.135), channel_id=1, source_target_pairs={{0,2},{1,3},{2,0},{3,1},{4,6},{5,7},{6,4},{7,5},{8,10},{9,11},{10,... | collective-permute-start | bytes 614408 | tf_op jit(solution)/shard_map/ppermute | solution.py:201
  132.6 10.2 %collective-permute-start.27 = (bf16[1,160,640]{2,1,0:T(8,128)(2,1)S(1)}, bf16[1,160,640]{2,1,0:T(8,128)(2,1)S(1)}, u32[]{:S(2)}, u32[]{:S(2)}) collective-permute-start(bf16[1,160,640]{2,1,0:T(8,128)(2,1)S(1)} %slice.134), channel_id=1, source_target_pairs={{0,2},{1,3},{2,0},{3,1},{4,6},{5,7},{6,4},{7,5},{8,10},{9,11},{10,... | collective-permute-start | bytes 614408 | tf_op jit(solution)/shard_map/ppermute | solution.py:201

commit v4 on v0

v4 whole, which is shorter than its diff:
```python
import functools

import jax
import jax.numpy as jnp
from jax import lax
from jax.experimental import pallas as pl
from jax.experimental.pallas import tpu as pltpu
from jax.sharding import PartitionSpec as P

OUTER = 4
GROUP = 8
EXTRA = 16
VMEM = pl.BlockSpec(memory_space=pltpu.VMEM)
SMEM = pl.BlockSpec(memory_space=pltpu.SMEM)
BF16, F32, I32 = jnp.bfloat16, jnp.float32, jnp.int32


def call(kernel, out_shape, in_specs, args, scratch=(), flops=0, moved=0, aliases=None):
    return pl.pallas_call(
        kernel,
        out_shape=out_shape,
        in_specs=in_specs,
        out_specs=jax.tree.map(lambda _: VMEM, out_shape),
        scratch_shapes=scratch,
        input_output_aliases=aliases or {},
        compiler_params=pltpu.CompilerParams(vmem_limit_bytes=24 * 1024 * 1024),
        cost_estimate=pl.CostEstimate(flops=flops, bytes_accessed=moved, transcendentals=0),
    )(*args)


def smooth_kernel(reach, tall, flux_ref, resolution_ref, out_ref, padded):
    rows, nobs = flux_ref.shape
    taps = resolution_ref.shape[0]
    edge = jnp.zeros((tall, reach), F32)
    padded[:, :reach] = edge
    padded[:, reach + nobs :] = edge
    step = 256

    def one_tile(tile, carry):
        own = pl.ds(pl.multiple_of(tile * tall, tall), tall)
        padded[:, reach : reach + nobs] = flux_ref[own, :].astype(F32)
        for start in range(0, nobs, step):
            stop = min(nobs, start + step)
            total = jnp.zeros((tall, stop - start), F32)
            for tap in range(taps):
                first = reach + start + tap - (taps - 1) // 2
                total = total + resolution_ref[tap, own, start:stop].astype(F32) * padded[:, first : first + stop - start]
            out_ref[own, start:stop] = total.astype(BF16)
        return carry

    lax.fori_loop(0, rows // tall, one_tile, 0)


def smooth(flux, resolution):
    rows, nobs = flux.shape
    taps = resolution.shape[0]
    tall, reach = 16, 128
    return call(
        functools.partial(smooth_kernel, reach, tall),
        jax.ShapeDtypeStruct((rows, nobs), BF16),
        [VMEM, VMEM],
        (flux, resolution),
        [pltpu.VMEM((tall, nobs + 2 * reach), F32)],
        flops=2 * rows * taps * nobs,
        moved=4 * rows * nobs,
    )


def cut_kernel(per, low, high, band, unroll, bins_ref, starts_ref, turns_ref, smoothed_ref, placing_ref, back_ref, out_ref, placed, cut):
    placed[...] = jnp.dot(placing_ref[...], smoothed_ref[...], preferred_element_type=F32)

    def some_groups(step, carry):
        for i in range(unroll):
            group = step * unroll + i
            rows = pl.ds(pl.multiple_of(group * GROUP, GROUP), GROUP)
            entry = bins_ref[group]
            for outer in range(OUTER):
                for j in range(low, high):
                    start = pl.multiple_of(starts_ref[entry, outer * per + j], band)
                    wide = placed[rows, pl.ds(start, 2 * band)]
                    turned = pltpu.roll(wide, turns_ref[entry, outer * per + j], 1)
                    at = (outer * (high - low) + j - low) * band
                    cut[rows, at : at + band] = turned[:, :band]
        return carry

    lax.fori_loop(0, placed.shape[0] // GROUP // unroll, some_groups, 0)
    width = (high - low) * band
    for outer in range(OUTER):
        part = cut[:, outer * width : (outer + 1) * width].astype(BF16)
        out_ref[outer] = jnp.dot(back_ref[...], part, preferred_element_type=F32).astype(BF16)


def cut_windows(bins, starts, turns, smoothed, placing, back, low, high, band):
    per = starts.shape[1] // OUTER
    rows, places = back.shape
    nobs = smoothed.shape[1]
    width = (high - low) * band
    unroll = max(k for k in range(1, 7) if places // GROUP % k == 0)
    return call(
        functools.partial(cut_kernel, per, low, high, band, unroll),
        jax.ShapeDtypeStruct((OUTER, rows, width), BF16),
        [SMEM] * 3 + [VMEM] * 3,
        (bins, starts, turns, smoothed, placing, back),
        [pltpu.VMEM((places, nobs), F32), pltpu.VMEM((places, OUTER * width), F32)],
        flops=4 * places * rows * nobs,
        moved=4 * rows * nobs,
    )


def rest_kernel(npieces, low, high, band, begun, *refs):
    bins_ref, names_ref, window = refs[:3]
    weights = refs[3 : 3 + npieces]
    named = names_ref[...]
    rows = window.shape[0]
    total = jnp.zeros((rows, 1), F32)
    rest_ref = refs[3 + npieces + begun]
    for p in range(npieces):
        hits = [
            jnp.broadcast_to((named == bins_ref[p * OUTER + b]).astype(F32), (rows, band)).astype(BF16)
            for b in range(OUTER)
        ]
        for block in range(high - low):
            lanes = slice(block * band, (block + 1) * band)
            own = slice((low + block) * band, (low + block + 1) * band)
            masked = jnp.concatenate([window[:, lanes] * hit for hit in hits], axis=1)
            columns = jnp.concatenate([weights[p][b, own, :] for b in range(OUTER)], axis=1)
            value = lax.dot_general(masked, columns, (((1,), (1,)), ((), ())), preferred_element_type=F32)
            if p:
                value = value + rest_ref[:, lanes]
            elif begun:
                value = value + refs[3 + npieces][:, lanes]
            rest_ref[:, lanes] = value
            if begun and p == npieces - 1:
                sent_ref, squares_ref = refs[5 + npieces :]
                sent_ref[:, lanes] = value.astype(BF16)
                total = total + jnp.sum(value * value, axis=1, keepdims=True)
    if begun:
        squares_ref[...] = total


def resample(bins, names, window, weights, low, high, band, begun=None):
    rows, width = window.shape
    npieces = len(weights)
    rest = jax.ShapeDtypeStruct((rows, width), F32)
    last = begun is not None
    return call(
        functools.partial(rest_kernel, npieces, low, high, band, int(last)),
        (rest, jax.ShapeDtypeStruct((rows, width), BF16), jax.ShapeDtypeStruct((rows, 1), F32)) if last else rest,
        [SMEM] + [VMEM] * (2 + npieces + last),
        (bins, names, window, *weights) + ((begun,) if last else ()),
        flops=2 * rows * width * band * OUTER * npieces,
        moved=rows * width * 8,
        aliases={3 + npieces: 0} if last else None,
    )


def place_kernel(columns, width, *refs):
    at_ref, out_ref = refs[0], refs[-1]
    for i, (slot, offset) in enumerate(columns):
        held, got = refs[1 + 2 * i], refs[2 + 2 * i]
        start = pl.multiple_of(at_ref[slot] * width + offset, 128)
        out_ref[:, pl.ds(start, held.shape[1])] = held[...] + got[...].astype(F32)


def place(at, columns, pairs, width):
    share = pairs[0][0].shape[0]
    return call(
        functools.partial(place_kernel, columns, width),
        jax.ShapeDtypeStruct((share, OUTER * width), F32),
        [SMEM] + [VMEM] * (2 * len(pairs)),
        (at, *[array for pair in pairs for array in pair]),
        moved=share * width * OUTER * 10,
    )


def local(flux, resolution, destination, resample_weight, band_offset):
    n = lax.axis_size("spec")
    inner = n // OUTER
    count, nobs = flux.shape
    nrest, band = resample_weight.shape[1:]
    nblocks = band_offset.shape[1]
    per = nblocks // OUTER
    width = nrest // OUTER
    share = nrest // n
    rows = OUTER * count
    me = lax.axis_index("spec")
    outer, q = me // inner, me % inner
    groups = [[o * inner + i for o in range(OUTER)] for i in range(inner)]

    def swap(array, bit):
        return lax.ppermute(array, "spec", [(i, i ^ bit) for i in range(n)])

    def step_on(array):
        return lax.ppermute(array, "spec", [(i, (i + inner) % n) for i in range(n)])

    def to_outers(array):
        return lax.all_to_all(array, "spec", 0, 0, axis_index_groups=groups, tiled=True)

    targets = destination[:, 0]
    chunk = jnp.minimum(band_offset // band, nobs // band - 2)
    shift = band_offset - chunk * band
    small = jnp.pad(jnp.concatenate([chunk, shift]), ((0, 0), (0, band - nblocks)))
    small = jnp.concatenate([targets.reshape(count // band, band), small]).astype(BF16)
    small = jnp.pad(small, ((0, EXTRA - small.shape[0]), (0, 0)))
    small = jnp.broadcast_to(small[None], (OUTER, EXTRA, band))
    sent = jnp.concatenate([resample_weight[0].reshape(OUTER, width, band), small], axis=1)
    mixed = to_outers(sent)

    smoothed = smooth(flux, jnp.transpose(resolution, (1, 0, 2)))

    order = jnp.arange(count, dtype=I32)
    which = jnp.arange(n, dtype=I32)
    same = (targets[:, None] == targets[None, :]) & (order[:, None] > order[None, :])
    rank = jnp.sum(same.astype(I32), axis=1)
    filled = jnp.sum((targets[:, None] == which[None, :]).astype(I32), axis=0)
    amount = (filled + GROUP - 1) // GROUP
    before = jnp.sum(jnp.where(which[None, :] < targets[:, None], amount[None, :], 0), axis=1)
    position = before * GROUP + rank
    places = -(-(count + n * (GROUP - 1)) // (2 * GROUP)) * 2 * GROUP
    slot = jnp.arange(places, dtype=I32)
    placing = (slot[:, None] == position[None, :]).astype(BF16)
    back = (position[:, None] == slot[None, :]).astype(BF16)
    ends = jnp.sum(jnp.where(which[:, None] <= which[None, :], amount[:, None], 0), axis=0)
    group_bin = jnp.sum((ends[None, :] <= slot[: places // GROUP, None]).astype(I32), axis=1)
    entries = jnp.minimum(group_bin, n - 1) ^ q

    mixed, smoothed = lax.optimization_barrier((mixed, smoothed))
    lines = count // band
    names = mixed[:, width : width + lines].reshape(rows, 1).astype(I32)
    table = mixed[:, width + lines : width + lines + 2, :nblocks][:, None]
    bit = 1
    while bit < inner:
        table = jnp.concatenate([table, swap(table, bit)], axis=1)
        bit *= 2
    table = table.reshape(n, 2, nblocks).astype(I32)
    starts = table[:, 0] * band
    turns = (2 * band - table[:, 1]) & (2 * band - 1)

    mixed, starts = lax.optimization_barrier((mixed, starts))
    bit = inner // 2
    weights = [mixed, swap(mixed, bit)]
    mine = jnp.arange(OUTER, dtype=I32) * inner + q
    ids = [mine, mine ^ bit]

    chunks = [(0, (per + 1) // 2), ((per + 1) // 2, per)]
    windows = []
    for low, high in chunks:
        cut = cut_windows(entries, starts, turns, smoothed, placing, back, low, high, band)
        windows.append(to_outers(cut).reshape(rows, (high - low) * band))
    weights, windows[0] = lax.optimization_barrier((weights, windows[0]))
    while bit > 1:
        bit //= 2
        weights = weights + [swap(piece, bit) for piece in weights]
        ids = ids + [piece ^ bit for piece in ids]
    early, late = jnp.concatenate(ids[:2]), jnp.concatenate(ids[2:])
    rests, blocks, squares = [], [], jnp.zeros((rows,), F32)
    for (low, high), window in zip(chunks, windows):
        begun = resample(early, names, window, weights[:2], low, high, band)
        rest, block, square = resample(late, names, window, weights[2:], low, high, band, begun)
        rests.append(rest)
        blocks.append(block)
        squares = squares + square.reshape(rows)
    ring = [jnp.concatenate(blocks, axis=1)]
    for _ in range(1, OUTER):
        ring.append(step_on(ring[-1]))

    total = jnp.sum(to_outers(jnp.broadcast_to(squares[None], (OUTER, rows))), axis=0)
    scale = lax.rsqrt(total / nrest + 1e-06)
    factor = (scale * scale / (count * n))[:, None]
    left = jnp.concatenate([(rest * factor).astype(BF16).T for rest in rests])
    left = left.reshape(inner, share, rows)
    left = jnp.stack([lax.dynamic_index_in_dim(left, q ^ e, 0, keepdims=False) for e in range(inner)])
    left = left.reshape(width, rows)

    at = (outer - jnp.arange(OUTER, dtype=I32)) % OUTER
    pairs = []
    for slot_of, part in enumerate(ring):
        if slot_of == OUTER - 1:
            part, last = lax.optimization_barrier((part, pairs[-1][1]))
            pairs[-1] = (pairs[-1][0], last)
        held = jnp.dot(left, part, preferred_element_type=F32).reshape(inner, share, part.shape[1])
        bit = 1
        while bit < inner:
            got = swap(held[1::2].astype(BF16), bit)
            held = held[0::2]
            bit *= 2
            if bit < inner:
                held = held + got.astype(F32)
        pairs.append((held[0], got[0]))
    return place(at, [(slot_of, 0) for slot_of in range(OUTER)], pairs, width)


def solution(mesh):
    in_specs = (
        P(("groups", "spec"), None),
        P(("groups", "spec"), None, None),
        P(("groups", "spec"), None),
        P("spec", None, None),
        P("spec", None),
    )
    out_specs = P(("groups", "spec"), None)
    return jax.shard_map(local, mesh=mesh, in_specs=in_specs, out_specs=out_specs, check_vma=False)
```

time: 389 us -> 154 us (0.40)
  waiting for transfers between devices: 320 us -> 73.6 us
  Pallas kernels: 0 us -> 22.7 us
  matrix products: 24.4 us -> 4.89 us
  starting transfers between devices: 7.61 us -> 22.8 us
  blocking collectives: 0 us -> 13.2 us
  between operations: 13.5 us -> 0.49 us
  local copies, waits for them, and re-layouts: 20.4 us -> 9.51 us
    reduce_scatter x1 -> x0, waiting for transfers between devices: 263 us -> none  [local(): lax.psum_scatter(product / total_spectra, 'spec', scatter_dimension=0, ti...]
    ppermute x0 -> x16, waiting for transfers between devices: none -> 53 us  [the longest x3 32.2 us: step_on(): return lax.ppermute(array, 'spec', [(i, (i + inner) % n) for i in range(n)])]
    all_to_all x1 -> x3, waiting for transfers between devices: 57.4 us -> 20.6 us  [to_outers(): lax.all_to_all(array, 'spec', 0, 0, axis_index_groups=groups, tiled=True)]
    pallas_call x0 -> x8, Pallas kernels: none -> 22.7 us  [call(): pl.pallas_call(kernel, out_shape=out_shape, in_specs=in_specs, out_specs=...]
    dot_general x4, matrix products: 24.4 us -> 4.89 us  [local(): jnp.dot(left, part, preferred_element_type=F32)]
    all_to_all x0 -> x1, blocking collectives: none -> 13.2 us  [to_outers(): lax.all_to_all(array, 'spec', 0, 0, axis_index_groups=groups, tiled=True)]
    gather x2 -> x0, local copies, waits for them, and re-layouts: 12.4 us -> none  [local(): jnp.take(rows, index, axis=1).reshape(senders * items, nblocks, band)]
    ppermute x0 -> x16, starting transfers between devices: none -> 9.8 us  [the longest x13 7.76 us: swap(): return lax.ppermute(array, 'spec', [(i, i ^ bit) for i in range(n)])]
  transfers between devices with their start and end apart: 2 -> 19, of which waited for: 2 -> 11; matrix products, arithmetic and copies ran while one was open for 0% -> 4% of each run, Pallas kernels for 0% -> 10%
where the time goes in v4:
time: 154 us; the launch traced here: 153 us
  waiting for transfers between devices  73.6 us (48%)
  starting transfers between devices  22.8 us (15%)
  Pallas kernels  22.7 us (15%)
  blocking collectives  13.2 us (9%)
  local copies, waits for them, and re-layouts  9.51 us (6%)
  other arithmetic  5.82 us (4%)
  matrix products  4.89 us (3%)
    ppermute x3, waiting for transfers between devices, step_on(): return lax.ppermute(array, 'spec', [(i, (i + inner) % n) for i in range(n)])  32.2 us
    pallas_call x8, Pallas kernels, call(): pl.pallas_call(kernel, out_shape=out_shape, in_specs=in_specs, out_specs=...  22.7 us
    ppermute x13, waiting for transfers between devices, swap(): return lax.ppermute(array, 'spec', [(i, i ^ bit) for i in range(n)])  20.8 us
    all_to_all x3, waiting for transfers between devices, to_outers(): lax.all_to_all(array, 'spec', 0, 0, axis_index_groups=groups, tiled=True)  20.6 us
    all_to_all x1, blocking collectives, to_outers(): lax.all_to_all(array, 'spec', 0, 0, axis_index_groups=groups, tiled=True)  13.2 us
    all_to_all x3, starting transfers between devices, to_outers(): lax.all_to_all(array, 'spec', 0, 0, axis_index_groups=groups, tiled=True)  13 us
    unnamed x23, local copies, waits for them, and re-layouts  8.04 us
    ppermute x13, starting transfers between devices, swap(): return lax.ppermute(array, 'spec', [(i, i ^ bit) for i in range(n)])  7.76 us
  transfers between devices with their start and end apart: 19, of which 11 were waited for; matrix products, arithmetic and copies ran while one was open for 4% of the time, Pallas kernels for 10%

profile of v4, /device:TPU:0, one launch (start us, length us, event | category | flops | bytes accessed | tf_op | source)
XLA Modules:
  0.0 153.0 jit_solution(2880857847920341182)
XLA Ops:
  0.0 0.7 convert_bitcast_fusion
  0.8 0.7 fusion.24
  1.4 0.7 subtract_convert_fusion
  2.1 2.0 %pad_maximum_fusion = bf16[4,656,128]{2,1,0:T(8,128)(2,1)} fusion(bf16[4,16,128]{2,1,0:T(8,128)(2,1)S(1)} %broadcast_in_dim.26, bf16[4,640,128]{2,1,0:T(8,128)(2,1)} %bitcast.64), kind=kLoop, calls=%fused_computation.5 | loop fusion | flops 1343488 | bytes 1343488 | tf_op jit(solution)/shard_map/concatenate | solution.py:206
  4.1 6.3 %all-to-all-start = ((bf16[4,656,128]{2,1,0:T(8,128)(2,1)}), bf16[4,656,128]{2,1,0:T(8,128)(2,1)S(1)}, u32[]{:S(2)}, u32[]{:S(2)}) async-start(bf16[4,656,128]{2,1,0:T(8,128)(2,1)} %pad_maximum_fusion), calls=%async_computation | async-start | bytes 1343488 | tf_op jit(solution)/shard_map/all_to_all | solution.py:197
  10.4 0.1 convert_reduce_fusion.2
  10.6 4.2 %copy-done = bf16[128,11,3968]{2,0,1:T(8,128)(2,1)S(1)} copy-done((bf16[128,11,3968]{2,0,1:T(8,128)(2,1)S(1)}, bf16[128,11,3968]{2,0,1:T(8,128)(2,1)}, u32[]{:S(2)}) %copy-start) | copy-done | bytes 11173912
  14.7 4.8 %shard_map.55.smoothed_ref = bf16[128,3968]{1,0:T(8,128)(2,1)S(1)} custom-call(bf16[128,3968]{1,0:T(8,128)(2,1)S(1)} %copy-done.3, bf16[11,128,3968]{2,1,0:T(8,128)(2,1)S(1)} %bitcast.54), custom_call_target="tpu_custom_call" | custom-call | flops 11173888 | bytes 2031616 | tf_op jit(solution)/shard_map/pallas_call | solution.py:19
  19.5 0.1 select_reduce_fusion.1
  19.6 0.1 select_reduce_fusion
  19.7 0.2 convert_reduce_fusion
  19.9 0.1 fusion.10.back_ref
  20.0 8.1 %all-to-all-done.refs_3_ = bf16[4,656,128]{2,1,0:T(8,128)(2,1)S(1)} async-done(((bf16[4,656,128]{2,1,0:T(8,128)(2,1)}), bf16[4,656,128]{2,1,0:T(8,128)(2,1)S(1)}, u32[]{:S(2)}, u32[]{:S(2)}) %all-to-all-start) | async-done | bytes 671776 | tf_op jit(solution)/shard_map/all_to_all | solution.py:197
  28.1 0.1 convert_reduce_fusion.1
  28.2 1.1 collective-permute-done
  29.2 1.6 %collective-permute-start.1 = (bf16[4,2,2,20]{3,2,0,1:T(2,128)(2,1)S(1)}, bf16[4,2,2,20]{3,2,0,1:T(2,128)(2,1)S(1)}, u32[]{:S(2)}, u32[]{:S(2)}) collective-permute-start(bf16[4,2,2,20]{3,2,0,1:T(2,128)(2,1)S(1)} %pad_maximum_fusion.3), channel_id=1, source_target_pairs={{0,2},{1,3},{2,0},{3,1},{4,6},{5,7},{6,4},{7,5},{8,10},{9,11},{10,... | collective-permute-start | bytes 1928 | tf_op jit(solution)/shard_map/ppermute | solution.py:191
  30.8 2.1 %collective-permute-done.1 = bf16[4,2,2,20]{3,2,0,1:T(2,128)(2,1)S(1)} collective-permute-done((bf16[4,2,2,20]{3,2,0,1:T(2,128)(2,1)S(1)}, bf16[4,2,2,20]{3,2,0,1:T(2,128)(2,1)S(1)}, u32[]{:S(2)}, u32[]{:S(2)}) %collective-permute-start.1) | collective-permute-done | bytes 672 | tf_op jit(solution)/shard_map/ppermute | solution.py:191
  33.0 1.6 %collective-permute-start.2 = (bf16[4,656,128]{2,1,0:T(8,128)(2,1)S(1)}, bf16[4,656,128]{2,1,0:T(8,128)(2,1)}, u32[]{:S(2)}, u32[]{:S(2)}) collective-permute-start(bf16[4,656,128]{2,1,0:T(8,128)(2,1)S(1)} %all-to-all-done.refs_3_), channel_id=1, source_target_pairs={{0,2},{1,3},{2,0},{3,1},{4,6},{5,7},{6,4},{7,5},{8,10},{9,11},{10,... | collective-permute-start | bytes 2015240 | tf_op jit(solution)/shard_map/ppermute | solution.py:191
  34.6 3.5 %shard_map.56 = bf16[4,128,384]{2,1,0:T(8,128)(2,1)S(1)} custom-call(s32[30]{0:T(128)S(1)} %minimum_xor_fusion.bins_ref, s32[16,20]{1,0:T(8,128)S(1)} %get-tuple-element.22.starts_ref, s32[16,20]{1,0:T(8,128)S(1)} %get-tuple-element.41.turns_ref, bf16[128,3968]{1,0:T(8,128)(2,1)S(1)} %shard_map.55.smoothed_ref, bf16[240,128]{1,0:T(8,128)(2,1)S(1)} %fusion.11.placing_ref, ...), custom_call_target="tpu_custom_call" | custom-call | flops 487587840 | bytes 2031616 | tf_op jit(solution)/shard_map/pallas_call | solution.py:19
  38.0 0.9 copy-done.4
  39.0 13.2 %all_to_all.21 = bf16[4,128,384]{2,1,0:T(8,128)(2,1)S(1)} all-to-all(bf16[4,128,384]{2,1,0:T(8,128)(2,1)S(1)} %shard_map.56), channel_id=1, replica_groups={{0,4,8,12},{1,5,9,13},{2,6,10,14},{3,7,11,15},{16,20,24,28},{17,21,25,2..., dimensions={0} | all-to-all | bytes 786432 | tf_op jit(solution)/shard_map/all_to_all | solution.py:197
  52.2 0.5 collective-permute-start.4
  52.8 1.2 copy-done.5
  54.0 3.6 %shard_map.59 = bf16[4,128,256]{2,1,0:T(8,128)(2,1)} custom-call(s32[30]{0:T(128)S(1)} %minimum_xor_fusion.bins_ref, s32[16,20]{1,0:T(8,128)S(1)} %get-tuple-element.22.starts_ref, s32[16,20]{1,0:T(8,128)S(1)} %get-tuple-element.41.turns_ref, bf16[128,3968]{1,0:T(8,128)(2,1)S(1)} %copy-done.5, bf16[240,128]{1,0:T(8,128)(2,1)S(1)} %fusion.11.placing_ref, ...), custom_call_target="tpu_custom_call" | custom-call | flops 487587840 | bytes 2031616 | tf_op jit(solution)/shard_map/pallas_call | solution.py:19
  57.6 3.4 %all-to-all-start.2 = ((bf16[4,128,256]{2,1,0:T(8,128)(2,1)}), bf16[4,128,256]{2,1,0:T(8,128)(2,1)S(1)}, u32[]{:S(2)}, u32[]{:S(2)}) async-start(bf16[4,128,256]{2,1,0:T(8,128)(2,1)} %shard_map.59), calls=%async_computation.2 | async-start | bytes 524288 | tf_op jit(solution)/shard_map/all_to_all | solution.py:197
  61.0 0.1 pad_add_fusion.refs_0_
  61.1 0.1 pad_add_fusion.1.refs_0_
  61.2 0.1 copy.37.refs_1_
  61.3 9.0 %all-to-all-done.2 = bf16[4,128,256]{2,1,0:T(8,128)(2,1)S(1)} async-done(((bf16[4,128,256]{2,1,0:T(8,128)(2,1)}), bf16[4,128,256]{2,1,0:T(8,128)(2,1)S(1)}, u32[]{:S(2)}, u32[]{:S(2)}) %all-to-all-start.2) | async-done | bytes 262176 | tf_op jit(solution)/shard_map/all_to_all | solution.py:197
  70.3 1.9 %shard_map.60.refs_5_ = f32[512,256]{1,0:T(8,128)S(1)} custom-call(s32[8]{0:T(128)S(1)} %pad_add_fusion.1.refs_0_, s32[512,1]{1,0:T(8,128)S(1)} %copy.37.refs_1_, bf16[512,256]{1,0:T(8,128)(2,1)S(1)} %bitcast.57, bf16[4,656,128]{2,1,0:T(8,128)(2,1)S(1)} %all-to-all-done.refs_3_, bf16[4,656,128]{2,1,0:T(8,128)(2,1)} %collective-permute-done.2.refs_4_), custom_call_target="tpu_custom_call" | custom-call | flops 268435456 | bytes 1048576 | tf_op jit(solution)/shard_map/pallas_call | solution.py:19
  72.2 0.7 copy-done.1
  72.9 2.2 %shard_map.57.refs_5_ = f32[512,384]{1,0:T(8,128)S(1)} custom-call(s32[8]{0:T(128)S(1)} %pad_add_fusion.1.refs_0_, s32[512,1]{1,0:T(8,128)S(1)} %copy.37.refs_1_, bf16[512,384]{1,0:T(8,128)(2,1)S(1)} %bitcast.55, bf16[4,656,128]{2,1,0:T(8,128)(2,1)S(1)} %all-to-all-done.refs_3_, bf16[4,656,128]{2,1,0:T(8,128)(2,1)} %collective-permute-done.2.refs_4_), custom_call_target="tpu_custom_call" | custom-call | flops 402653184 | bytes 1572864 | tf_op jit(solution)/shard_map/pallas_call | solution.py:19
  75.2 0.9 copy-done.2
  76.2 2.2 %shard_map.61 = (f32[512,256]{1,0:T(8,128)S(1)}, bf16[512,256]{1,0:T(8,128)(2,1)S(1)}, f32[512,1]{1,0:T(8,128)S(1)}) custom-call(s32[8]{0:T(128)S(1)} %pad_add_fusion.refs_0_, s32[512,1]{1,0:T(8,128)S(1)} %copy.37.refs_1_, bf16[512,256]{1,0:T(8,128)(2,1)S(1)} %bitcast.58, ...), custom_call_target="tpu_custom_call", output_to_operand_aliasing={{0}: (5, {})} | custom-call | flops 268435456 | bytes 1048576 | tf_op jit(solution)/shard_map/pallas_call | solution.py:19
  78.4 2.6 %shard_map.58 = (f32[512,384]{1,0:T(8,128)S(1)}, bf16[512,384]{1,0:T(8,128)(2,1)S(1)}, f32[512,1]{1,0:T(8,128)S(1)}) custom-call(s32[8]{0:T(128)S(1)} %pad_add_fusion.refs_0_, s32[512,1]{1,0:T(8,128)S(1)} %copy.37.refs_1_, bf16[512,384]{1,0:T(8,128)(2,1)S(1)} %bitcast.56, ...), custom_call_target="tpu_custom_call", output_to_operand_aliasing={{0}: (5, {})} | custom-call | flops 402653184 | bytes 1572864 | tf_op jit(solution)/shard_map/pallas_call | solution.py:19
  81.0 0.2 add_reduce_fusion
  81.1 0.6 broadcast_in_dim.36
  81.8 3.2 %all-to-all-start.3 = ((f32[4,1,512]{2,1,0:T(1,128)}), f32[4,1,512]{2,1,0:T(1,128)S(1)}, u32[]{:S(2)}, u32[]{:S(2)}) async-start(f32[4,1,512]{2,1,0:T(1,128)} %broadcast_in_dim.36), calls=%async_computation.3 | async-start | bytes 16384 | tf_op jit(solution)/shard_map/all_to_all | solution.py:197
  85.1 2.0 %collective-permute-start.7 = (bf16[512,640]{1,0:T(8,128)(2,1)S(1)}, bf16[512,640]{1,0:T(8,128)(2,1)}, u32[]{:S(2)}, u32[]{:S(2)}) collective-permute-start(bf16[512,640]{1,0:T(8,128)(2,1)S(1)} %constant_dynamic-update-slice_fusion), channel_id=1, source_target_pairs={{0,4},{1,5},{2,6},{3,7},{4,8},{5,9},{6,10},{7,11},{8,12},{9,13},{1... | collective-permute-start | bytes 1966088 | tf_op jit(solution)/shard_map/ppermute | solution.py:194
  87.1 3.6 %all-to-all-done.3 = f32[4,1,512]{2,1,0:T(1,128)S(1)} async-done(((f32[4,1,512]{2,1,0:T(1,128)}), f32[4,1,512]{2,1,0:T(1,128)S(1)}, u32[]{:S(2)}, u32[]{:S(2)}) %all-to-all-start.3) | async-done | bytes 8224 | tf_op jit(solution)/shard_map/all_to_all | solution.py:197
  90.7 0.1 fusion.8
  90.9 0.1 fusion.9
  91.1 0.3 copy.41
  91.4 0.7 fusion.26
  92.2 0.1 collective-permute-start.5
  92.3 9.9 %collective-permute-done.7 = bf16[512,640]{1,0:T(8,128)(2,1)} collective-permute-done((bf16[512,640]{1,0:T(8,128)(2,1)S(1)}, bf16[512,640]{1,0:T(8,128)(2,1)}, u32[]{:S(2)}, u32[]{:S(2)}) %collective-permute-start.7) | collective-permute-done | bytes 655392 | tf_op jit(solution)/shard_map/ppermute | solution.py:194
  102.2 0.1 convert_add_fusion.3
  102.3 16.0 %collective-permute-done.10 = bf16[512,640]{1,0:T(8,128)(2,1)} collective-permute-done((bf16[512,640]{1,0:T(8,128)(2,1)}, bf16[512,640]{1,0:T(8,128)(2,1)}, u32[]{:S(2)}, u32[]{:S(2)}) %collective-permute-start.10) | collective-permute-done | bytes 655392 | tf_op jit(solution)/shard_map/ppermute | solution.py:194
  118.3 1.8 %fusion.28 = (bf16[4,160,640]{2,1,0:T(8,128)(2,1)S(1)}, f32[4,160,640]{2,1,0:T(8,128)S(1)}) fusion(bf16[512,640]{1,0:T(8,128)(2,1)} %collective-permute-done.10, bf16[1,160,512]{2,1,0:T(8,128)(2,1)S(1)} %get-tuple-element.38, bf16[1,160,512]{2,1,0:T(8,128)(2,1)S(1)} %copy-done.7, bf16[1,160,512]{2,1,0:T(8,128)(2,1)S(1)} %copy-done.9, ...), kind=kOutput, calls=%fused_computation.92 | convolution fusion | flops 420823040 | bytes 3768320 | tf_op jit(solution)/shard_map/dot_general | solution.py:281
  120.2 1.8 %fusion.27 = (bf16[4,160,640]{2,1,0:T(8,128)(2,1)S(1)}, f32[4,160,640]{2,1,0:T(8,128)S(1)}) fusion(bf16[512,640]{1,0:T(8,128)(2,1)} %collective-permute-done.7, bf16[1,160,512]{2,1,0:T(8,128)(2,1)S(1)} %get-tuple-element.38, bf16[1,160,512]{2,1,0:T(8,128)(2,1)S(1)} %copy-done.7, bf16[1,160,512]{2,1,0:T(8,128)(2,1)S(1)} %copy-done.9, ...), kind=kOutput, calls=%fused_computation.91 | convolution fusion | flops 420823040 | bytes 3768320 | tf_op jit(solution)/shard_map/dot_general | solution.py:281
  122.0 0.6 collective-permute-start.8
  122.7 0.6 collective-permute-start.6
  123.2 0.1 convert_add_fusion.1
  123.4 1.6 %collective-permute-start.13 = (bf16[1,160,640]{2,1,0:T(8,128)(2,1)S(1)}, bf16[1,160,640]{2,1,0:T(8,128)(2,1)S(1)}, u32[]{:S(2)}, u32[]{:S(2)}) collective-permute-start(bf16[1,160,640]{2,1,0:T(8,128)(2,1)S(1)} %slice.133), channel_id=1, source_target_pairs={{0,2},{1,3},{2,0},{3,1},{4,6},{5,7},{6,4},{7,5},{8,10},{9,11},{10,... | collective-permute-start | bytes 614408 | tf_op jit(solution)/shard_map/ppermute | solution.py:191
  124.9 0.1 convert_add_fusion.2
  125.1 0.6 collective-permute-start.9
  125.6 9.4 %collective-permute-done.13 = bf16[1,160,640]{2,1,0:T(8,128)(2,1)S(1)} collective-permute-done((bf16[1,160,640]{2,1,0:T(8,128)(2,1)S(1)}, bf16[1,160,640]{2,1,0:T(8,128)(2,1)S(1)}, u32[]{:S(2)}, u32[]{:S(2)}) %collective-permute-start.13) | collective-permute-done | bytes 204832 | tf_op jit(solution)/shard_map/ppermute | solution.py:191
  135.0 6.3 %collective-permute-done.12 = bf16[512,640]{1,0:T(8,128)(2,1)S(1)} collective-permute-done((bf16[512,640]{1,0:T(8,128)(2,1)}, bf16[512,640]{1,0:T(8,128)(2,1)S(1)}, u32[]{:S(2)}, u32[]{:S(2)}) %collective-permute-start.12) | collective-permute-done | bytes 655392 | tf_op jit(solution)/shard_map/ppermute | solution.py:194
  141.3 0.7 fusion.29
  142.0 0.1 collective-permute-start.14
  142.2 1.7 %collective-permute-done.14 = bf16[2,160,640]{2,1,0:T(8,128)(2,1)S(1)} collective-permute-done((bf16[2,160,640]{2,1,0:T(8,128)(2,1)S(1)}, bf16[2,160,640]{2,1,0:T(8,128)(2,1)S(1)}, u32[]{:S(2)}, u32[]{:S(2)}) %collective-permute-start.14) | collective-permute-done | bytes 409632 | tf_op jit(solution)/shard_map/ppermute | solution.py:191
  143.9 0.6 collective-permute-start.15
  144.6 6.6 %collective-permute-done.15 = bf16[1,160,640]{2,1,0:T(8,128)(2,1)S(1)} collective-permute-done((bf16[1,160,640]{2,1,0:T(8,128)(2,1)S(1)}, bf16[1,160,640]{2,1,0:T(8,128)(2,1)S(1)}, u32[]{:S(2)}, u32[]{:S(2)}) %collective-permute-start.15) | collective-permute-done | bytes 204832 | tf_op jit(solution)/shard_map/ppermute | solution.py:191
  151.1 1.9 %shard_map.62 = f32[160,2560]{1,0:T(8,128)} custom-call(s32[4]{0:T(128)S(1)} %and_select_fusion.2.refs_0_, f32[160,640]{1,0:T(8,128)S(1)} %slice_bitcast_fusion.3.refs_1_, bf16[160,640]{1,0:T(8,128)(2,1)S(1)} %bitcast.59, f32[160,640]{1,0:T(8,128)S(1)} %slice_bitcast_fusion.2.refs_3_, bf16[160,640]{1,0:T(8,128)(2,1)S(1)} %bitcast.61, ...), custom_call_target="tpu_custom_call" | custom-call | bytes 4096000 | tf_op jit(solution)/shard_map/pallas_call | solution.py:19
  (67 shorter events, 1.0 us)
Async XLA Ops:
  0.0 10.4 %copy-start.10 = (s32[128,1]{0,1:T(1,128)S(1)}, s32[128,1]{0,1:T(1,128)}, u32[]{:S(2)}) copy-start(s32[128,1]{0,1:T(1,128)} %param.7) | copy-start | bytes 1540
  0.0 10.6 %copy-start.3 = (bf16[128,3968]{1,0:T(8,128)(2,1)S(1)}, bf16[128,3968]{1,0:T(8,128)(2,1)}, u32[]{:S(2)}) copy-start(bf16[128,3968]{1,0:T(8,128)(2,1)} %flux_ref.1) | copy-start | bytes 3047428
  4.1 24.0 %all-to-all-start = ((bf16[4,656,128]{2,1,0:T(8,128)(2,1)}), bf16[4,656,128]{2,1,0:T(8,128)(2,1)S(1)}, u32[]{:S(2)}, u32[]{:S(2)}) async-start(bf16[4,656,128]{2,1,0:T(8,128)(2,1)} %pad_maximum_fusion), calls=%async_computation | async-start | bytes 1343488 | tf_op jit(solution)/shard_map/all_to_all | solution.py:197
  10.6 4.2 %copy-start = (bf16[128,11,3968]{2,0,1:T(8,128)(2,1)S(1)}, bf16[128,11,3968]{2,0,1:T(8,128)(2,1)}, u32[]{:S(2)}) copy-start(bf16[128,11,3968]{2,0,1:T(8,128)(2,1)} %param.6) | copy-start | bytes 33521668
  28.1 1.2 collective-permute-start
  29.2 3.7 %collective-permute-start.1 = (bf16[4,2,2,20]{3,2,0,1:T(2,128)(2,1)S(1)}, bf16[4,2,2,20]{3,2,0,1:T(2,128)(2,1)S(1)}, u32[]{:S(2)}, u32[]{:S(2)}) collective-permute-start(bf16[4,2,2,20]{3,2,0,1:T(2,128)(2,1)S(1)} %pad_maximum_fusion.3), channel_id=1, source_target_pairs={{0,2},{1,3},{2,0},{3,1},{4,6},{5,7},{6,4},{7,5},{8,10},{9,11},{10,... | collective-permute-start | bytes 1928 | tf_op jit(solution)/shard_map/ppermute | solution.py:191
  33.0 19.3 %collective-permute-start.2 = (bf16[4,656,128]{2,1,0:T(8,128)(2,1)S(1)}, bf16[4,656,128]{2,1,0:T(8,128)(2,1)}, u32[]{:S(2)}, u32[]{:S(2)}) collective-permute-start(bf16[4,656,128]{2,1,0:T(8,128)(2,1)S(1)} %all-to-all-done.refs_3_), channel_id=1, source_target_pairs={{0,2},{1,3},{2,0},{3,1},{4,6},{5,7},{6,4},{7,5},{8,10},{9,11},{10,... | collective-permute-start | bytes 2015240 | tf_op jit(solution)/shard_map/ppermute | solution.py:191
  38.0 1.0 copy-start.4
  52.2 23.0 %collective-permute-start.3 = (bf16[4,656,128]{2,1,0:T(8,128)(2,1)S(1)}, bf16[4,656,128]{2,1,0:T(8,128)(2,1)S(1)}, u32[]{:S(2)}, u32[]{:S(2)}) collective-permute-start(bf16[4,656,128]{2,1,0:T(8,128)(2,1)S(1)} %all-to-all-done.refs_3_), channel_id=1, source_target_pairs={{0,1},{1,0},{2,3},{3,2},{4,5},{5,4},{6,7},{7,6},{8,9},{9,8},{10,11... | collective-permute-start | bytes 2015240 | tf_op jit(solution)/shard_map/ppermute | solution.py:191
  52.2 23.0 %collective-permute-start.4 = (bf16[4,656,128]{2,1,0:T(8,128)(2,1)}, bf16[4,656,128]{2,1,0:T(8,128)(2,1)}, u32[]{:S(2)}, u32[]{:S(2)}) collective-permute-start(bf16[4,656,128]{2,1,0:T(8,128)(2,1)} %collective-permute-done.2.refs_4_), channel_id=1, source_target_pairs={{0,1},{1,0},{2,3},{3,2},{4,5},{5,4},{6,7},{7,6},{8,9},{9,8},{10,11... | collective-permute-start | bytes 2015240 | tf_op jit(solution)/shard_map/ppermute | solution.py:191
  52.8 1.2 copy-start.5
  57.6 12.7 %all-to-all-start.2 = ((bf16[4,128,256]{2,1,0:T(8,128)(2,1)}), bf16[4,128,256]{2,1,0:T(8,128)(2,1)S(1)}, u32[]{:S(2)}, u32[]{:S(2)}) async-start(bf16[4,128,256]{2,1,0:T(8,128)(2,1)} %shard_map.59), calls=%async_computation.2 | async-start | bytes 524288 | tf_op jit(solution)/shard_map/all_to_all | solution.py:197
  72.2 0.7 copy-start.1
  75.2 1.0 copy-start.2
  81.8 8.9 %all-to-all-start.3 = ((f32[4,1,512]{2,1,0:T(1,128)}), f32[4,1,512]{2,1,0:T(1,128)S(1)}, u32[]{:S(2)}, u32[]{:S(2)}) async-start(f32[4,1,512]{2,1,0:T(1,128)} %broadcast_in_dim.36), calls=%async_computation.3 | async-start | bytes 16384 | tf_op jit(solution)/shard_map/all_to_all | solution.py:197
  85.1 17.1 %collective-permute-start.7 = (bf16[512,640]{1,0:T(8,128)(2,1)S(1)}, bf16[512,640]{1,0:T(8,128)(2,1)}, u32[]{:S(2)}, u32[]{:S(2)}) collective-permute-start(bf16[512,640]{1,0:T(8,128)(2,1)S(1)} %constant_dynamic-update-slice_fusion), channel_id=1, source_target_pairs={{0,4},{1,5},{2,6},{3,7},{4,8},{5,9},{6,10},{7,11},{8,12},{9,13},{1... | collective-permute-start | bytes 1966088 | tf_op jit(solution)/shard_map/ppermute | solution.py:194
  91.4 0.7 copy-start.6
  91.4 0.7 copy-start.8
  92.2 10.0 %collective-permute-start.5 = (bf16[2,160,640]{2,1,0:T(8,128)(2,1)S(1)}, bf16[2,160,640]{2,1,0:T(8,128)(2,1)S(1)}, u32[]{:S(2)}, u32[]{:S(2)}) collective-permute-start(bf16[2,160,640]{2,1,0:T(8,128)(2,1)S(1)} %slice.85), channel_id=1, source_target_pairs={{0,1},{1,0},{2,3},{3,2},{4,5},{5,4},{6,7},{7,6},{8,9},{9,8},{10,11... | collective-permute-start | bytes 1228808 | tf_op jit(solution)/shard_map/ppermute | solution.py:191
  102.2 16.1 %copy-start.7 = (bf16[1,160,512]{2,1,0:T(8,128)(2,1)S(1)}, bf16[1,160,512]{2,1,0:T(8,128)(2,1)}, u32[]{:S(2)}) copy-start(bf16[1,160,512]{2,1,0:T(8,128)(2,1)} %copy-done.6) | copy-start | bytes 491524
  102.2 16.1 %copy-start.9 = (bf16[1,160,512]{2,1,0:T(8,128)(2,1)S(1)}, bf16[1,160,512]{2,1,0:T(8,128)(2,1)}, u32[]{:S(2)}) copy-start(bf16[1,160,512]{2,1,0:T(8,128)(2,1)} %copy-done.8) | copy-start | bytes 491524
  102.2 16.1 %collective-permute-start.10 = (bf16[512,640]{1,0:T(8,128)(2,1)}, bf16[512,640]{1,0:T(8,128)(2,1)}, u32[]{:S(2)}, u32[]{:S(2)}) collective-permute-start(bf16[512,640]{1,0:T(8,128)(2,1)} %collective-permute-done.7), channel_id=1, source_target_pairs={{0,4},{1,5},{2,6},{3,7},{4,8},{5,9},{6,10},{7,11},{8,12},{9,13},{1... | collective-permute-start | bytes 1966088 | tf_op jit(solution)/shard_map/ppermute | solution.py:194
  120.1 3.1 %collective-permute-start.11 = (bf16[2,160,640]{2,1,0:T(8,128)(2,1)S(1)}, bf16[2,160,640]{2,1,0:T(8,128)(2,1)S(1)}, u32[]{:S(2)}, u32[]{:S(2)}) collective-permute-start(bf16[2,160,640]{2,1,0:T(8,128)(2,1)S(1)} %slice.93), channel_id=1, source_target_pairs={{0,1},{1,0},{2,3},{3,2},{4,5},{5,4},{6,7},{7,6},{8,9},{9,8},{10,11... | collective-permute-start | bytes 1228808 | tf_op jit(solution)/shard_map/ppermute | solution.py:191
  122.0 2.9 %collective-permute-start.8 = (bf16[2,160,640]{2,1,0:T(8,128)(2,1)S(1)}, bf16[2,160,640]{2,1,0:T(8,128)(2,1)S(1)}, u32[]{:S(2)}, u32[]{:S(2)}) collective-permute-start(bf16[2,160,640]{2,1,0:T(8,128)(2,1)S(1)} %slice.89), channel_id=1, source_target_pairs={{0,1},{1,0},{2,3},{3,2},{4,5},{5,4},{6,7},{7,6},{8,9},{9,8},{10,11... | collective-permute-start | bytes 1228808 | tf_op jit(solution)/shard_map/ppermute | solution.py:191
  122.6 18.7 %collective-permute-start.12 = (bf16[512,640]{1,0:T(8,128)(2,1)}, bf16[512,640]{1,0:T(8,128)(2,1)S(1)}, u32[]{:S(2)}, u32[]{:S(2)}) collective-permute-start(bf16[512,640]{1,0:T(8,128)(2,1)} %collective-permute-done.10), channel_id=1, source_target_pairs={{0,4},{1,5},{2,6},{3,7},{4,8},{5,9},{6,10},{7,11},{8,12},{9,13},{1... | collective-permute-start | bytes 1966088 | tf_op jit(solution)/shard_map/ppermute | solution.py:194
  122.7 21.9 %collective-permute-start.6 = (bf16[1,160,640]{2,1,0:T(8,128)(2,1)S(1)}, bf16[1,160,640]{2,1,0:T(8,128)(2,1)S(1)}, u32[]{:S(2)}, u32[]{:S(2)}) collective-permute-start(bf16[1,160,640]{2,1,0:T(8,128)(2,1)S(1)} %slice.135), channel_id=1, source_target_pairs={{0,2},{1,3},{2,0},{3,1},{4,6},{5,7},{6,4},{7,5},{8,10},{9,11},{10,... | collective-permute-start | bytes 614408 | tf_op jit(solution)/shard_map/ppermute | solution.py:191
  123.4 11.7 %collective-permute-start.13 = (bf16[1,160,640]{2,1,0:T(8,128)(2,1)S(1)}, bf16[1,160,640]{2,1,0:T(8,128)(2,1)S(1)}, u32[]{:S(2)}, u32[]{:S(2)}) collective-permute-start(bf16[1,160,640]{2,1,0:T(8,128)(2,1)S(1)} %slice.133), channel_id=1, source_target_pairs={{0,2},{1,3},{2,0},{3,1},{4,6},{5,7},{6,4},{7,5},{8,10},{9,11},{10,... | collective-permute-start | bytes 614408 | tf_op jit(solution)/shard_map/ppermute | solution.py:191
  125.1 19.5 %collective-permute-start.9 = (bf16[1,160,640]{2,1,0:T(8,128)(2,1)S(1)}, bf16[1,160,640]{2,1,0:T(8,128)(2,1)S(1)}, u32[]{:S(2)}, u32[]{:S(2)}) collective-permute-start(bf16[1,160,640]{2,1,0:T(8,128)(2,1)S(1)} %slice.134), channel_id=1, source_target_pairs={{0,2},{1,3},{2,0},{3,1},{4,6},{5,7},{6,4},{7,5},{8,10},{9,11},{10,... | collective-permute-start | bytes 614408 | tf_op jit(solution)/shard_map/ppermute | solution.py:191
  142.0 1.8 %collective-permute-start.14 = (bf16[2,160,640]{2,1,0:T(8,128)(2,1)S(1)}, bf16[2,160,640]{2,1,0:T(8,128)(2,1)S(1)}, u32[]{:S(2)}, u32[]{:S(2)}) collective-permute-start(bf16[2,160,640]{2,1,0:T(8,128)(2,1)S(1)} %slice.97), channel_id=1, source_target_pairs={{0,1},{1,0},{2,3},{3,2},{4,5},{5,4},{6,7},{7,6},{8,9},{9,8},{10,11... | collective-permute-start | bytes 1228808 | tf_op jit(solution)/shard_map/ppermute | solution.py:191
  143.9 7.2 %collective-permute-start.15 = (bf16[1,160,640]{2,1,0:T(8,128)(2,1)S(1)}, bf16[1,160,640]{2,1,0:T(8,128)(2,1)S(1)}, u32[]{:S(2)}, u32[]{:S(2)}) collective-permute-start(bf16[1,160,640]{2,1,0:T(8,128)(2,1)S(1)} %slice.132), channel_id=1, source_target_pairs={{0,2},{1,3},{2,0},{3,1},{4,6},{5,7},{6,4},{7,5},{8,10},{9,11},{10,... | collective-permute-start | bytes 614408 | tf_op jit(solution)/shard_map/ppermute | solution.py:191

commit v5 on v4

v5 whole, which is shorter than its diff:
```python
import functools

import jax
import jax.numpy as jnp
from jax import lax
from jax.experimental import pallas as pl
from jax.experimental.pallas import tpu as pltpu
from jax.sharding import PartitionSpec as P

OUTER = 4
GROUP = 8
EXTRA = 16
VMEM = pl.BlockSpec(memory_space=pltpu.VMEM)
ANY = pl.BlockSpec(memory_space=pl.ANY)
SMEM = pl.BlockSpec(memory_space=pltpu.SMEM)
BF16, F32, I32 = jnp.bfloat16, jnp.float32, jnp.int32


def call(kernel, out_shape, in_specs, args, scratch=(), aliases=None, limit=24 * 1024 * 1024):
    return pl.pallas_call(
        kernel,
        out_shape=out_shape,
        in_specs=in_specs,
        out_specs=jax.tree.map(lambda _: VMEM, out_shape),
        scratch_shapes=scratch,
        input_output_aliases=aliases or {},
        compiler_params=pltpu.CompilerParams(vmem_limit_bytes=limit),
        cost_estimate=pl.CostEstimate(flops=1, bytes_accessed=1, transcendentals=0),
    )(*args)


def smooth_kernel(reach, tall, flux_ref, resolution_ref, out_ref, flux, resolution, padded, sem):
    rows, nobs = flux.shape
    taps = resolution.shape[0]
    tiles = rows // tall

    def copies(tile):
        own = pl.ds(pl.multiple_of(tile * tall, tall), tall)
        return (
            pltpu.make_async_copy(flux_ref.at[own], flux.at[own], sem.at[0, tile]),
            pltpu.make_async_copy(resolution_ref.at[:, own], resolution.at[:, own], sem.at[1, tile]),
        )

    for tile in range(tiles):
        for copy in copies(tile):
            copy.start()
    edge = jnp.zeros((tall, reach), F32)
    padded[:, :reach] = edge
    padded[:, reach + nobs :] = edge
    step = 256

    def one_tile(tile, carry):
        for copy in copies(tile):
            copy.wait()
        own = pl.ds(pl.multiple_of(tile * tall, tall), tall)
        padded[:, reach : reach + nobs] = flux[own, :].astype(F32)
        for start in range(0, nobs, step):
            stop = min(nobs, start + step)
            total = jnp.zeros((tall, stop - start), F32)
            for tap in range(taps):
                first = reach + start + tap - (taps - 1) // 2
                total = total + resolution[tap, own, start:stop].astype(F32) * padded[:, first : first + stop - start]
            out_ref[own, start:stop] = total.astype(BF16)
        return carry

    lax.fori_loop(0, tiles, one_tile, 0)


def smooth(flux, resolution):
    rows, nobs = flux.shape
    taps = resolution.shape[0]
    tall, reach = 16, 128
    return call(
        functools.partial(smooth_kernel, reach, tall),
        jax.ShapeDtypeStruct((rows, nobs), BF16),
        [ANY, ANY],
        (flux, resolution),
        [
            pltpu.VMEM((rows, nobs), BF16),
            pltpu.VMEM((taps, rows, nobs), BF16),
            pltpu.VMEM((tall, nobs + 2 * reach), F32),
            pltpu.SemaphoreType.DMA((2, rows // tall)),
        ],
        limit=50 * 1024 * 1024,
    )


def cut_kernel(per, band, unroll, outer_ref, bins_ref, starts_ref, turns_ref, smoothed_ref, placing_ref, back_ref, *refs):
    outs, (placed, cut) = refs[:OUTER], refs[OUTER:]
    placed[...] = jnp.dot(placing_ref[...], smoothed_ref[...], preferred_element_type=F32)

    def some_groups(step, carry):
        for i in range(unroll):
            group = step * unroll + i
            rows = pl.ds(pl.multiple_of(group * GROUP, GROUP), GROUP)
            entry = bins_ref[group]
            for away in range(OUTER):
                first = (outer_ref[0] ^ away) * per
                for j in range(per):
                    start = pl.multiple_of(starts_ref[entry, first + j], band)
                    wide = placed[rows, pl.ds(start, 2 * band)]
                    turned = pltpu.roll(wide, turns_ref[entry, first + j], 1)
                    at = (away * per + j) * band
                    cut[rows, at : at + band] = turned[:, :band]
        return carry

    lax.fori_loop(0, placed.shape[0] // GROUP // unroll, some_groups, 0)
    width = per * band
    for away in range(OUTER):
        part = cut[:, away * width : (away + 1) * width].astype(BF16)
        outs[away][...] = jnp.dot(back_ref[...], part, preferred_element_type=F32).astype(BF16)


def cut_windows(outer, bins, starts, turns, smoothed, placing, back, band):
    per = starts.shape[1] // OUTER
    rows, places = back.shape
    nobs = smoothed.shape[1]
    width = per * band
    unroll = max(k for k in range(1, 7) if places // GROUP % k == 0)
    return call(
        functools.partial(cut_kernel, per, band, unroll),
        (jax.ShapeDtypeStruct((rows, width), BF16),) * OUTER,
        [SMEM] * 4 + [VMEM] * 3,
        (outer, bins, starts, turns, smoothed, placing, back),
        [pltpu.VMEM((places, nobs), F32), pltpu.VMEM((places, OUTER * width), F32)],
    )


def rest_kernel(npieces, splits, band, begun, outer_ref, bins_ref, names_ref, *refs):
    windows, refs = refs[:OUTER], refs[OUTER:]
    weights, refs = refs[:npieces], refs[npieces:]
    if begun:
        before_ref, refs = refs[0], refs[1:]
        sents, squares_ref = refs[1 : 1 + len(splits)], refs[1 + len(splits)]
    rest_ref, window = refs[0], refs[-1]
    count = windows[0].shape[0]
    for away in range(OUTER):
        own = pl.ds(pl.multiple_of((outer_ref[0] ^ away) * count, count), count)
        window[own, :] = windows[away][...]
    rows, width = window.shape
    named = names_ref[...]
    total = jnp.zeros((rows, 1), F32)
    for p in range(npieces):
        hits = [
            jnp.broadcast_to((named == bins_ref[p * OUTER + b]).astype(F32), (rows, band)).astype(BF16)
            for b in range(OUTER)
        ]
        for at in range(0, width, band):
            lanes = slice(at, at + band)
            masked = jnp.concatenate([window[:, lanes] * hit for hit in hits], axis=1)
            columns = jnp.concatenate([weights[p][b, lanes, :] for b in range(OUTER)], axis=1)
            value = lax.dot_general(masked, columns, (((1,), (1,)), ((), ())), preferred_element_type=F32)
            if p:
                value = value + rest_ref[:, lanes]
            elif begun:
                value = value + before_ref[:, lanes]
            rest_ref[:, lanes] = value
            if begun and p == npieces - 1:
                for (low, high), sent_ref in zip(splits, sents):
                    if low <= at < high:
                        sent_ref[:, at - low : at - low + band] = value.astype(BF16)
                total = total + jnp.sum(value * value, axis=1, keepdims=True)
    if begun:
        squares_ref[...] = total


def resample(outer, bins, names, windows, weights, splits, band, begun=None):
    count, width = windows[0].shape
    rows = OUTER * count
    npieces = len(weights)
    rest = jax.ShapeDtypeStruct((rows, width), F32)
    last = begun is not None
    sents = tuple(jax.ShapeDtypeStruct((rows, high - low), BF16) for low, high in splits)
    return call(
        functools.partial(rest_kernel, npieces, splits, band, int(last)),
        (rest, *sents, jax.ShapeDtypeStruct((rows, 1), F32)) if last else rest,
        [SMEM, SMEM] + [VMEM] * (1 + OUTER + npieces + last),
        (outer, bins, names, *windows, *weights) + ((begun,) if last else ()),
        [pltpu.VMEM((rows, width), BF16)],
        aliases={3 + OUTER + npieces: 0} if last else None,
    )


def product_kernel(left_ref, block_ref, send_ref, keep_ref):
    pairs, share, wide = keep_ref.shape
    value = jnp.dot(left_ref[...], block_ref[...], preferred_element_type=F32)
    value = value.reshape(pairs, 2, share, wide)
    keep_ref[...] = value[:, 0]
    send_ref[...] = value[:, 1].astype(BF16)


def product(left, block, inner):
    wide = block.shape[1]
    shape = (inner // 2, left.shape[0] // inner, wide)
    return call(
        product_kernel,
        (jax.ShapeDtypeStruct(shape, BF16), jax.ShapeDtypeStruct(shape, F32)),
        [VMEM, VMEM],
        (left, block),
    )


def fold_kernel(held_ref, got_ref, send_ref, keep_ref):
    for i in range(keep_ref.shape[0]):
        keep_ref[i] = held_ref[2 * i] + got_ref[2 * i].astype(F32)
        send_ref[i] = (held_ref[2 * i + 1] + got_ref[2 * i + 1].astype(F32)).astype(BF16)


def fold(held, got):
    shape = (held.shape[0] // 2,) + held.shape[1:]
    return call(
        fold_kernel,
        (jax.ShapeDtypeStruct(shape, BF16), jax.ShapeDtypeStruct(shape, F32)),
        [VMEM, VMEM],
        (held, got),
    )


def mirror_kernel(q_ref, block_ref, scaled_ref, send_ref, keep_ref, value):
    pairs, share, wide = keep_ref.shape
    value[...] = lax.dot_general(
        block_ref[...], scaled_ref[...], (((0,), (0,)), ((), ())), preferred_element_type=F32
    )
    for e in range(2 * pairs):
        own = value[pl.ds(pl.multiple_of((q_ref[0] ^ e) * share, 8), share), :]
        if e % 2:
            send_ref[e // 2] = own.astype(BF16)
        else:
            keep_ref[e // 2] = own


def mirror(q, block, scaled, inner):
    tall, wide = block.shape[1], scaled.shape[1]
    shape = (inner // 2, tall // inner, wide)
    return call(
        mirror_kernel,
        (jax.ShapeDtypeStruct(shape, BF16), jax.ShapeDtypeStruct(shape, F32)),
        [SMEM, VMEM, VMEM],
        (q, block, scaled),
        [pltpu.VMEM((tall, wide), F32)],
    )


def place_kernel(width, *refs):
    at_ref, mirrored_ref, out_ref = refs[0], refs[1], refs[-1]
    for slot in range(OUTER):
        columns = pl.ds(pl.multiple_of(at_ref[slot] * width, 128), width)
        if slot == OUTER - 1:
            out_ref[:, columns] = mirrored_ref[...].astype(F32)
        else:
            held, got = refs[2 + 2 * slot], refs[3 + 2 * slot]
            out_ref[:, columns] = held[...] + got[...].astype(F32)


def place(at, mirrored, pairs):
    share, width = mirrored.shape
    return call(
        functools.partial(place_kernel, width),
        jax.ShapeDtypeStruct((share, OUTER * width), F32),
        [SMEM] + [VMEM] * (1 + 2 * len(pairs)),
        (at, mirrored, *[array for pair in pairs for array in pair]),
    )


def local(flux, resolution, destination, resample_weight, band_offset):
    n = lax.axis_size("spec")
    inner = n // OUTER
    count, nobs = flux.shape
    nrest, band = resample_weight.shape[1:]
    nblocks = band_offset.shape[1]
    per = nblocks // OUTER
    width = nrest // OUTER
    share = nrest // n
    rows = OUTER * count
    me = lax.axis_index("spec")
    outer, q = me // inner, me % inner

    def swap(array, bit):
        return lax.ppermute(array, "spec", [(i, i ^ bit) for i in range(n)])

    def step(array, outers):
        return lax.ppermute(array, "spec", [(i, (i + outers * inner) % n) for i in range(n)])

    targets = destination[:, 0]
    chunk = jnp.minimum(band_offset // band, nobs // band - 2)
    shift = band_offset - chunk * band
    small = jnp.pad(jnp.concatenate([chunk, shift]), ((0, 0), (0, band - nblocks)))
    small = jnp.concatenate([targets.reshape(count // band, band), small]).astype(BF16)
    small = jnp.pad(small, ((0, EXTRA - small.shape[0]), (0, 0)))
    table = lax.all_to_all(jnp.broadcast_to(small[None], (n, EXTRA, band)), "spec", 0, 0, tiled=True)
    by_outer = resample_weight[0].reshape(OUTER, width, band)
    pieces = [lax.dynamic_index_in_dim(by_outer, outer, 0, keepdims=False)]
    for away in range(1, OUTER):
        theirs = lax.dynamic_index_in_dim(by_outer, outer ^ away, 0, keepdims=False)
        pieces.append(swap(theirs, away * inner))

    smoothed = smooth(flux, jnp.transpose(resolution, (1, 0, 2)))

    order = jnp.arange(count, dtype=I32)
    which = jnp.arange(n, dtype=I32)
    same = (targets[:, None] == targets[None, :]) & (order[:, None] > order[None, :])
    rank = jnp.sum(same.astype(I32), axis=1)
    filled = jnp.sum((targets[:, None] == which[None, :]).astype(I32), axis=0)
    amount = (filled + GROUP - 1) // GROUP
    before = jnp.sum(jnp.where(which[None, :] < targets[:, None], amount[None, :], 0), axis=1)
    position = before * GROUP + rank
    places = -(-(count + n * (GROUP - 1)) // (2 * GROUP)) * 2 * GROUP
    slot = jnp.arange(places, dtype=I32)
    placing = (slot[:, None] == position[None, :]).astype(BF16)
    placed = (position[:, None] == slot[None, :]).astype(BF16)
    ends = jnp.sum(jnp.where(which[:, None] <= which[None, :], amount[:, None], 0), axis=0)
    group_bin = jnp.sum((ends[None, :] <= slot[: places // GROUP, None]).astype(I32), axis=1)
    entries = jnp.minimum(group_bin, n - 1)

    table, smoothed = lax.optimization_barrier((table, smoothed))
    lines = count // band
    names = lax.dynamic_index_in_dim(table[:, :lines].reshape(OUTER, inner, count), q, 1, keepdims=False)
    names = names.reshape(rows, 1).astype(I32)
    starts = table[:, lines, :nblocks].astype(I32) * band
    turns = (2 * band - table[:, lines + 1, :nblocks].astype(I32)) & (2 * band - 1)
    outer1 = outer.reshape(1)
    windows = cut_windows(outer1, entries, starts, turns, smoothed, placing, placed, band)

    pieces, windows = lax.optimization_barrier((pieces, windows))
    mixed = jnp.stack(pieces)
    bit = inner // 2
    weights = [mixed, swap(mixed, bit)]
    mine = me ^ (jnp.arange(OUTER, dtype=I32) * inner)
    ids = [mine, mine ^ bit]
    arrived = [windows[0]] + [swap(windows[away], away * inner) for away in range(1, OUTER)]
    weights, arrived = lax.optimization_barrier((weights, arrived))
    while bit > 1:
        bit //= 2
        weights = weights + [swap(piece, bit) for piece in weights]
        ids = ids + [piece ^ bit for piece in ids]
    early, late = jnp.concatenate(ids[:2]), jnp.concatenate(ids[2:])
    begun = resample(outer1, early, names, arrived, weights[:2], [(0, width)], band)
    rest, sent, squares = resample(outer1, late, names, arrived, weights[2:], [(0, width)], band, begun)
    squares = squares.reshape(rows)

    total = squares
    for away in range(1, OUTER):
        total = total + swap(squares, away * inner)
    scale = lax.rsqrt(total / nrest + 1e-06)
    factor = (scale * scale / (count * n))[:, None]
    scaled = (rest * factor).astype(BF16)
    left = scaled.T
    left = left.reshape(inner, share, rows)
    left = jnp.stack([lax.dynamic_index_in_dim(left, q ^ e, 0, keepdims=False) for e in range(inner)])
    left = left.reshape(width, rows)

    def reduce(send, held):
        bit = 1
        while 2 * bit < inner:
            send, held = fold(held, swap(send, bit))
            bit *= 2
        return send, held[0]

    def finish(send):
        return swap(send, inner // 2)[0]

    send0, held0 = reduce(*product(left, sent, inner))
    first = step(sent, 1)
    first, send0 = lax.optimization_barrier((first, send0))
    second = step(first, 1)
    got0 = finish(send0)
    sendm, heldm = reduce(*mirror(q.reshape(1), first, scaled, inner))
    gotm = finish(sendm)
    send1, held1 = reduce(*product(left, first, inner))
    got1 = finish(send1)
    second, got0, got1, gotm = lax.optimization_barrier((second, got0, got1, gotm))
    send2, held2 = reduce(*product(left, second, inner))
    got2 = finish(send2)
    back = step((heldm + gotm.astype(F32)).astype(BF16), -1)
    at = (outer - jnp.arange(OUTER, dtype=I32)) % OUTER
    return place(at, back, [(held0, got0), (held1, got1), (held2, got2)])


def solution(mesh):
    in_specs = (
        P(("groups", "spec"), None),
        P(("groups", "spec"), None, None),
        P(("groups", "spec"), None),
        P("spec", None, None),
        P("spec", None),
    )
    out_specs = P(("groups", "spec"), None)
    return jax.shard_map(local, mesh=mesh, in_specs=in_specs, out_specs=out_specs, check_vma=False)
```

time: 154 us -> 115 us (0.75)
  waiting for transfers between devices: 73.6 us -> 44.6 us
  blocking collectives: 13.2 us -> 0 us
  starting transfers between devices: 22.8 us -> 32.3 us
  matrix products: 4.89 us -> 0 us
  Pallas kernels: 22.7 us -> 26.2 us
  other arithmetic: 5.82 us -> 2.43 us
    all_to_all x3 -> x1, waiting for transfers between devices: 20.6 us -> 0.01 us  [local(): lax.all_to_all(jnp.broadcast_to(small[None], (n, EXTRA, band)), 'spec', 0...]
    ppermute x3, waiting for transfers between devices: 32.2 us -> 13.2 us  [step(): lax.ppermute(array, 'spec', [(i, (i + outers * inner) % n) for i in range...]
    ppermute x13 -> x20, starting transfers between devices: 7.76 us -> 21.2 us  [swap(): return lax.ppermute(array, 'spec', [(i, i ^ bit) for i in range(n)])]
    all_to_all x1 -> x0, blocking collectives: 13.2 us -> none  [to_outers(): lax.all_to_all(array, 'spec', 0, 0, axis_index_groups=groups, tiled=True)]
    ppermute x13 -> x20, waiting for transfers between devices: 20.8 us -> 31.4 us  [swap(): return lax.ppermute(array, 'spec', [(i, i ^ bit) for i in range(n)])]
    all_to_all x3 -> x1, starting transfers between devices: 13 us -> 6.16 us  [local(): lax.all_to_all(jnp.broadcast_to(small[None], (n, EXTRA, band)), 'spec', 0...]
    dot_general x4 -> x0, matrix products: 4.89 us -> none  [local(): jnp.dot(left, part, preferred_element_type=F32)]
    pallas_call x8 -> x13, Pallas kernels: 22.7 us -> 26.2 us  [call(): pl.pallas_call(kernel, out_shape=out_shape, in_specs=in_specs, out_specs=...]
  transfers between devices with their start and end apart: 19 -> 24, of which waited for: 11 -> 11; matrix products, arithmetic and copies ran while one was open for 4% -> 4% of each run, Pallas kernels for 10% -> 17%
where the time goes in v5:
time: 115 us
  waiting for transfers between devices  44.6 us (39%)
  starting transfers between devices  32.3 us (28%)
  Pallas kernels  26.2 us (23%)
  local copies, waits for them, and re-layouts  9.17 us (8%)
  other arithmetic  2.43 us (2%)
    ppermute x20, waiting for transfers between devices, swap(): return lax.ppermute(array, 'spec', [(i, i ^ bit) for i in range(n)])  31.4 us
    pallas_call x13, Pallas kernels, call(): pl.pallas_call(kernel, out_shape=out_shape, in_specs=in_specs, out_specs=...  26.2 us
    ppermute x20, starting transfers between devices, swap(): return lax.ppermute(array, 'spec', [(i, i ^ bit) for i in range(n)])  21.2 us
    ppermute x3, waiting for transfers between devices, step(): lax.ppermute(array, 'spec', [(i, (i + outers * inner) % n) for i in range...  13.2 us
    all_to_all x1, starting transfers between devices, local(): lax.all_to_all(jnp.broadcast_to(small[None], (n, EXTRA, band)), 'spec', 0...  6.16 us
    unnamed x22, local copies, waits for them, and re-layouts  5.69 us
    ppermute x3, starting transfers between devices, step(): lax.ppermute(array, 'spec', [(i, (i + outers * inner) % n) for i in range...  4.91 us
  transfers between devices with their start and end apart: 24, of which 11 were waited for; matrix products, arithmetic and copies ran while one was open for 4% of the time, Pallas kernels for 17%

profile of v5, /device:TPU:0, one launch (start us, length us, event | category | flops | bytes accessed | tf_op | source)
XLA Modules:
  0.0 115.0 jit_solution(1734526689368835963)
XLA Ops:
  0.0 1.3 %dynamic-slice_bitcast_fusion = (bf16[640,128]{1,0:T(8,128)(2,1)S(1)}, bf16[640,128]{1,0:T(8,128)(2,1)S(1)}, bf16[640,128]{1,0:T(8,128)(2,1)S(1)}, bf16[640,128]{1,0:T(8,128)(2,1)S(1)}) fusion(bf16[4,640,128]{2,1,0:T(8,128)(2,1)} %bitcast.56, s32[]{:T(128)S(6)} %select_n.79, s32[]{:T(128)S(6)} %select_n.78, s32[]{:T(128)S(6)} %select_n.77, s32[]{:T(128)S(6)} %select_n.76), kind=kLoop, calls=%fused_computation.5 | loop fusion | bytes 1310736 | tf_op jit(solution)/shard_map/jit(dynamic_index_in_dim)/squeeze | solution.py:294
  1.3 3.1 %collective-permute-start = (bf16[640,128]{1,0:T(8,128)(2,1)S(1)}, bf16[640,128]{1,0:T(8,128)(2,1)S(1)}, u32[]{:S(2)}, u32[]{:S(2)}) collective-permute-start(bf16[640,128]{1,0:T(8,128)(2,1)S(1)} %get-tuple-element.103), channel_id=1, source_target_pairs={{0,4},{1,5},{2,6},{3,7},{4,0},{5,1},{6,2},{7,3},{8,12},{9,13},{10,... | collective-permute-start | bytes 491528 | tf_op jit(solution)/shard_map/ppermute | solution.py:279
  4.4 2.6 %collective-permute-start.1 = (bf16[640,128]{1,0:T(8,128)(2,1)S(1)}, bf16[640,128]{1,0:T(8,128)(2,1)S(1)}, u32[]{:S(2)}, u32[]{:S(2)}) collective-permute-start(bf16[640,128]{1,0:T(8,128)(2,1)S(1)} %get-tuple-element.102), channel_id=1, source_target_pairs={{0,8},{1,9},{2,10},{3,11},{4,12},{5,13},{6,14},{7,15},{8,0},{9,1},... | collective-permute-start | bytes 491528 | tf_op jit(solution)/shard_map/ppermute | solution.py:279
  7.1 0.6 broadcast_in_dim.22
  7.7 6.2 %all-to-all-start = ((bf16[16,16,128]{2,1,0:T(8,128)(2,1)}), bf16[16,16,128]{2,1,0:T(8,128)(2,1)S(1)}, u32[]{:S(2)}, u32[]{:S(2)}) async-start(bf16[16,16,128]{2,1,0:T(8,128)(2,1)} %broadcast_in_dim.22), calls=%async_computation | async-start | bytes 131072 | tf_op jit(solution)/shard_map/all_to_all | solution.py:290
  13.9 0.1 convert_reduce_fusion.2
  14.0 0.2 convert_reduce_fusion
  14.2 0.1 select_reduce_fusion
  14.3 0.1 fusion.1.back_ref
  14.4 0.1 select_reduce_fusion.1
  14.5 10.3 %shard_map.55.smoothed_ref = bf16[128,3968]{1,0:T(8,128)(2,1)S(1)} custom-call(bf16[128,3968]{1,0:T(8,128)(2,1)S(1)} %copy-done, bf16[11,128,3968]{2,1,0:T(8,128)(2,1)} %bitcast.53), custom_call_target="tpu_custom_call" | custom-call | flops 1 | bytes 1 | tf_op jit(solution)/shard_map/pallas_call | solution.py:20
  24.8 0.1 convert_reduce_fusion.1
  25.0 5.4 %shard_map.56 = (bf16[128,640]{1,0:T(8,128)(2,1)S(1)}, bf16[128,640]{1,0:T(8,128)(2,1)S(1)}, bf16[128,640]{1,0:T(8,128)(2,1)S(1)}, bf16[128,640]{1,0:T(8,128)(2,1)S(1)}) custom-call(s32[1]{0:T(128)} %bitcast.1.outer_ref, s32[30]{0:T(128)S(1)} %broadcast_minimum_fusion.bins_ref, s32[16,20]{1,0:T(8,128)S(1)} %get-tuple-element.106.starts_ref, ...), custom_call_target="tpu_custom_call" | custom-call | flops 1 | bytes 1 | tf_op jit(solution)/shard_map/pallas_call | solution.py:20
  30.4 0.1 pad_maximum_fusion.refs_4_
  30.5 2.0 %collective-permute-start.3 = (bf16[4,640,128]{2,1,0:T(8,128)(2,1)S(1)}, bf16[4,640,128]{2,1,0:T(8,128)(2,1)S(1)}, u32[]{:S(2)}, u32[]{:S(2)}) collective-permute-start(bf16[4,640,128]{2,1,0:T(8,128)(2,1)S(1)} %pad_maximum_fusion.refs_4_), channel_id=1, source_target_pairs={{0,2},{1,3},{2,0},{3,1},{4,6},{5,7},{6,4},{7,5},{8,10},{9,11},{10,... | collective-permute-start | bytes 1966088 | tf_op jit(solution)/shard_map/ppermute | solution.py:279
  32.5 1.5 %collective-permute-start.4 = (bf16[128,640]{1,0:T(8,128)(2,1)S(1)}, bf16[128,640]{1,0:T(8,128)(2,1)S(1)}, u32[]{:S(2)}, u32[]{:S(2)}) collective-permute-start(bf16[128,640]{1,0:T(8,128)(2,1)S(1)} %get-tuple-element.61), channel_id=1, source_target_pairs={{0,4},{1,5},{2,6},{3,7},{4,0},{5,1},{6,2},{7,3},{8,12},{9,13},{10,... | collective-permute-start | bytes 491528 | tf_op jit(solution)/shard_map/ppermute | solution.py:279
  33.9 2.4 %collective-permute-start.5 = (bf16[128,640]{1,0:T(8,128)(2,1)S(1)}, bf16[128,640]{1,0:T(8,128)(2,1)S(1)}, u32[]{:S(2)}, u32[]{:S(2)}) collective-permute-start(bf16[128,640]{1,0:T(8,128)(2,1)S(1)} %get-tuple-element.62), channel_id=1, source_target_pairs={{0,8},{1,9},{2,10},{3,11},{4,12},{5,13},{6,14},{7,15},{8,0},{9,1},... | collective-permute-start | bytes 491528 | tf_op jit(solution)/shard_map/ppermute | solution.py:279
  36.3 0.6 collective-permute-start.6
  36.9 4.2 %collective-permute-done.4.refs_1_ = bf16[128,640]{1,0:T(8,128)(2,1)S(1)} collective-permute-done((bf16[128,640]{1,0:T(8,128)(2,1)S(1)}, bf16[128,640]{1,0:T(8,128)(2,1)S(1)}, u32[]{:S(2)}, u32[]{:S(2)}) %collective-permute-start.4) | collective-permute-done | bytes 163872 | tf_op jit(solution)/shard_map/ppermute | solution.py:279
  41.0 0.7 copy-done.3
  41.7 7.3 %collective-permute-done.5.refs_2_ = bf16[128,640]{1,0:T(8,128)(2,1)S(1)} collective-permute-done((bf16[128,640]{1,0:T(8,128)(2,1)S(1)}, bf16[128,640]{1,0:T(8,128)(2,1)S(1)}, u32[]{:S(2)}, u32[]{:S(2)}) %collective-permute-start.5) | collective-permute-done | bytes 163872 | tf_op jit(solution)/shard_map/ppermute | solution.py:279
  49.0 0.7 copy-done.5
  49.7 0.7 copy-done.7
  50.3 0.5 collective-permute-start.8
  50.8 0.1 pad_add_fusion.1.bins_ref
  50.9 0.1 pad_add_fusion.bins_ref
  51.0 0.1 copy.32.names_ref
  51.2 0.9 copy-done.2
  52.1 0.9 copy-done.4
  53.0 0.9 copy-done.6
  53.9 0.9 copy-done.8
  54.8 2.2 %shard_map.57.refs_6_ = f32[512,640]{1,0:T(8,128)S(1)} custom-call(s32[1]{0:T(128)} %bitcast.1.outer_ref, s32[8]{0:T(128)S(1)} %pad_add_fusion.1.bins_ref, s32[512,1]{1,0:T(8,128)S(1)} %copy.32.names_ref, bf16[128,640]{1,0:T(8,128)(2,1)S(1)} %copy-done.2, bf16[128,640]{1,0:T(8,128)(2,1)S(1)} %copy-done.4, bf16[128,640]{1,0:T(8,128)(2,1)S(1)} %copy-done.6, ...), custom_call_target="tpu_custom_call" | custom-call | flops 1 | bytes 1 | tf_op jit(solution)/shard_map/pallas_call | solution.py:20
  57.1 3.3 %shard_map.58 = (f32[512,640]{1,0:T(8,128)S(1)}, bf16[512,640]{1,0:T(8,128)(2,1)S(1)}, f32[512,1]{1,0:T(8,128)S(1)}) custom-call(s32[1]{0:T(128)} %bitcast.1.outer_ref, s32[8]{0:T(128)S(1)} %pad_add_fusion.bins_ref, s32[512,1]{1,0:T(8,128)S(1)} %copy.32.names_ref, bf16[128,640]{1,0:T(8,128)(2,1)S(1)} %copy-done.2, ...), custom_call_target="tpu_custom_call", output_to_operand_aliasing={{0}: (9, {})} | custom-call | flops 1 | bytes 1 | tf_op jit(solution)/shard_map/pallas_call | solution.py:20
  60.4 0.1 reduce
  60.6 2.1 %collective-permute-start.10 = (f32[512]{0:T(512)S(1)}, f32[512]{0:T(512)S(1)}, u32[]{:S(2)}, u32[]{:S(2)}) collective-permute-start(f32[512]{0:T(512)S(1)} %reduce), channel_id=1, source_target_pairs={{0,4},{1,5},{2,6},{3,7},{4,0},{5,1},{6,2},{7,3},{8,12},{9,13},{10,... | collective-permute-start | bytes 6152 | tf_op jit(solution)/shard_map/ppermute | solution.py:279
  62.6 1.0 collective-permute-start.11
  63.6 1.5 %collective-permute-start.12 = (f32[512]{0:T(512)S(1)}, f32[512]{0:T(512)S(1)}, u32[]{:S(2)}, u32[]{:S(2)}) collective-permute-start(f32[512]{0:T(512)S(1)} %reduce), channel_id=1, source_target_pairs={{0,12},{1,13},{2,14},{3,15},{4,8},{5,9},{6,10},{7,11},{8,4},{9,5},... | collective-permute-start | bytes 6152 | tf_op jit(solution)/shard_map/ppermute | solution.py:279
  65.1 1.0 collective-permute-start.9
  66.1 1.0 collective-permute-done.11
  67.1 1.9 %collective-permute-done.12 = f32[512]{0:T(512)S(1)} collective-permute-done((f32[512]{0:T(512)S(1)}, f32[512]{0:T(512)S(1)}, u32[]{:S(2)}, u32[]{:S(2)}) %collective-permute-start.12) | collective-permute-done | bytes 2080 | tf_op jit(solution)/shard_map/ppermute | solution.py:279
  69.0 1.0 fusion.16
  70.0 1.3 %copy.33 = bf16[640,512]{1,0:T(8,128)(2,1)S(1)} copy(bf16[640,512]{0,1:T(8,128)(2,1)} %fusion.16) | data formatting | bytes 1310720 | tf_op jit(solution)/shard_map/transpose | solution.py:347
  71.4 0.1 pad_maximum_fusion.1
  71.5 0.7 shard_map.59
  72.2 0.1 collective-permute-start.13
  72.3 1.7 %collective-permute-done.13.got_ref = bf16[2,160,640]{2,1,0:T(8,128)(2,1)S(1)} collective-permute-done((bf16[2,160,640]{2,1,0:T(8,128)(2,1)S(1)}, bf16[2,160,640]{2,1,0:T(8,128)(2,1)S(1)}, u32[]{:S(2)}, u32[]{:S(2)}) %collective-permute-start.13) | collective-permute-done | bytes 409632 | tf_op jit(solution)/shard_map/ppermute | solution.py:279
  74.1 9.0 %collective-permute-done.9.block_ref = bf16[512,640]{1,0:T(8,128)(2,1)S(1)} collective-permute-done((bf16[512,640]{1,0:T(8,128)(2,1)S(1)}, bf16[512,640]{1,0:T(8,128)(2,1)S(1)}, u32[]{:S(2)}, u32[]{:S(2)}) %collective-permute-start.9) | collective-permute-done | bytes 655392 | tf_op jit(solution)/shard_map/ppermute | solution.py:282
  83.0 0.7 shard_map.63
  83.9 0.1 multiply_convert_fusion.scaled_ref
  84.0 0.8 shard_map.61
  84.8 0.6 collective-permute-start.14
  85.4 0.6 collective-permute-start.16
  86.0 1.5 %collective-permute-start.18 = (bf16[1,160,640]{2,1,0:T(8,128)(2,1)S(1)}, bf16[1,160,640]{2,1,0:T(8,128)(2,1)S(1)}, u32[]{:S(2)}, u32[]{:S(2)}) collective-permute-start(bf16[1,160,640]{2,1,0:T(8,128)(2,1)S(1)} %get-tuple-element.83), channel_id=1, source_target_pairs={{0,2},{1,3},{2,0},{3,1},{4,6},{5,7},{6,4},{7,5},{8,10},{9,11},{10,... | collective-permute-start | bytes 614408 | tf_op jit(solution)/shard_map/ppermute | solution.py:279
  87.6 0.6 collective-permute-start.19
  88.3 5.1 %collective-permute-done.16 = bf16[1,160,640]{2,1,0:T(8,128)(2,1)S(1)} collective-permute-done((bf16[1,160,640]{2,1,0:T(8,128)(2,1)S(1)}, bf16[1,160,640]{2,1,0:T(8,128)(2,1)S(1)}, u32[]{:S(2)}, u32[]{:S(2)}) %collective-permute-start.16) | collective-permute-done | bytes 204832 | tf_op jit(solution)/shard_map/ppermute | solution.py:279
  93.3 4.4 %collective-permute-done.18 = bf16[1,160,640]{2,1,0:T(8,128)(2,1)S(1)} collective-permute-done((bf16[1,160,640]{2,1,0:T(8,128)(2,1)S(1)}, bf16[1,160,640]{2,1,0:T(8,128)(2,1)S(1)}, u32[]{:S(2)}, u32[]{:S(2)}) %collective-permute-start.18) | collective-permute-done | bytes 204832 | tf_op jit(solution)/shard_map/ppermute | solution.py:279
  97.7 3.5 %collective-permute-done.19 = bf16[1,160,640]{2,1,0:T(8,128)(2,1)S(1)} collective-permute-done((bf16[1,160,640]{2,1,0:T(8,128)(2,1)S(1)}, bf16[1,160,640]{2,1,0:T(8,128)(2,1)S(1)}, u32[]{:S(2)}, u32[]{:S(2)}) %collective-permute-start.19) | collective-permute-done | bytes 204832 | tf_op jit(solution)/shard_map/ppermute | solution.py:279
  101.2 0.7 shard_map.65
  102.0 3.8 %collective-permute-start.20 = (bf16[160,640]{1,0:T(8,128)(2,1)S(1)}, bf16[160,640]{1,0:T(8,128)(2,1)S(1)}, u32[]{:S(2)}, u32[]{:S(2)}) collective-permute-start(bf16[160,640]{1,0:T(8,128)(2,1)S(1)} %fusion), channel_id=1, source_target_pairs={{0,12},{1,13},{2,14},{3,15},{4,0},{5,1},{6,2},{7,3},{8,4},{9,5},{1... | collective-permute-start | bytes 614408 | tf_op jit(solution)/shard_map/ppermute | solution.py:282
  105.8 0.1 shard_map.66
  105.9 0.6 collective-permute-start.22
  106.6 4.2 %collective-permute-done.20.refs_1_ = bf16[160,640]{1,0:T(8,128)(2,1)S(1)} collective-permute-done((bf16[160,640]{1,0:T(8,128)(2,1)S(1)}, bf16[160,640]{1,0:T(8,128)(2,1)S(1)}, u32[]{:S(2)}, u32[]{:S(2)}) %collective-permute-start.20) | collective-permute-done | bytes 204832 | tf_op jit(solution)/shard_map/ppermute | solution.py:282
  110.8 2.4 %collective-permute-done.22 = bf16[1,160,640]{2,1,0:T(8,128)(2,1)S(1)} collective-permute-done((bf16[1,160,640]{2,1,0:T(8,128)(2,1)S(1)}, bf16[1,160,640]{2,1,0:T(8,128)(2,1)S(1)}, u32[]{:S(2)}, u32[]{:S(2)}) %collective-permute-start.22) | collective-permute-done | bytes 204832 | tf_op jit(solution)/shard_map/ppermute | solution.py:279
  113.2 1.8 %shard_map.67 = f32[160,2560]{1,0:T(8,128)} custom-call(s32[4]{0:T(128)S(1)} %and_select_fusion.2.refs_0_, bf16[160,640]{1,0:T(8,128)(2,1)S(1)} %collective-permute-done.20.refs_1_, f32[160,640]{1,0:T(8,128)S(1)} %bitcast.47, bf16[160,640]{1,0:T(8,128)(2,1)S(1)} %bitcast.50, f32[160,640]{1,0:T(8,128)S(1)} %bitcast.48, bf16[160,640]{1,0:T(8,128)(2,1)S(1)} %bitcast.51, ...), custom_call_target="tpu_custom_call" | custom-call | flops 1 | bytes 1 | tf_op jit(solution)/shard_map/pallas_call | solution.py:20
  (57 shorter events, 0.8 us)
Async XLA Ops:
  0.0 7.0 %copy-start.9 = (s32[1,20]{1,0:T(1,128)S(1)}, s32[1,20]{1,0:T(1,128)}, u32[]{:S(2)}) copy-start(s32[1,20]{1,0:T(1,128)} %param.9) | copy-start | bytes 244
  0.0 7.0 %copy-start.10 = (s32[128,1]{0,1:T(1,128)S(1)}, s32[128,1]{0,1:T(1,128)}, u32[]{:S(2)}) copy-start(s32[128,1]{0,1:T(1,128)} %param.7) | copy-start | bytes 1540
  0.0 14.5 %copy-start = (bf16[128,3968]{1,0:T(8,128)(2,1)S(1)}, bf16[128,3968]{1,0:T(8,128)(2,1)}, u32[]{:S(2)}) copy-start(bf16[128,3968]{1,0:T(8,128)(2,1)} %flux_ref.1) | copy-start | bytes 3047428
  1.3 29.1 %collective-permute-start = (bf16[640,128]{1,0:T(8,128)(2,1)S(1)}, bf16[640,128]{1,0:T(8,128)(2,1)S(1)}, u32[]{:S(2)}, u32[]{:S(2)}) collective-permute-start(bf16[640,128]{1,0:T(8,128)(2,1)S(1)} %get-tuple-element.103), channel_id=1, source_target_pairs={{0,4},{1,5},{2,6},{3,7},{4,0},{5,1},{6,2},{7,3},{8,12},{9,13},{10,... | collective-permute-start | bytes 491528 | tf_op jit(solution)/shard_map/ppermute | solution.py:279
  4.4 25.9 %collective-permute-start.1 = (bf16[640,128]{1,0:T(8,128)(2,1)S(1)}, bf16[640,128]{1,0:T(8,128)(2,1)S(1)}, u32[]{:S(2)}, u32[]{:S(2)}) collective-permute-start(bf16[640,128]{1,0:T(8,128)(2,1)S(1)} %get-tuple-element.102), channel_id=1, source_target_pairs={{0,8},{1,9},{2,10},{3,11},{4,12},{5,13},{6,14},{7,15},{8,0},{9,1},... | collective-permute-start | bytes 491528 | tf_op jit(solution)/shard_map/ppermute | solution.py:279
  7.0 23.4 %collective-permute-start.2 = (bf16[640,128]{1,0:T(8,128)(2,1)S(1)}, bf16[640,128]{1,0:T(8,128)(2,1)S(1)}, u32[]{:S(2)}, u32[]{:S(2)}) collective-permute-start(bf16[640,128]{1,0:T(8,128)(2,1)S(1)} %get-tuple-element.101), channel_id=1, source_target_pairs={{0,12},{1,13},{2,14},{3,15},{4,8},{5,9},{6,10},{7,11},{8,4},{9,5},... | collective-permute-start | bytes 491528 | tf_op jit(solution)/shard_map/ppermute | solution.py:279
  7.7 17.2 %all-to-all-start = ((bf16[16,16,128]{2,1,0:T(8,128)(2,1)}), bf16[16,16,128]{2,1,0:T(8,128)(2,1)S(1)}, u32[]{:S(2)}, u32[]{:S(2)}) async-start(bf16[16,16,128]{2,1,0:T(8,128)(2,1)} %broadcast_in_dim.22), calls=%async_computation | async-start | bytes 131072 | tf_op jit(solution)/shard_map/all_to_all | solution.py:290
  30.3 20.0 %copy-start.1 = (bf16[128,640]{1,0:T(8,128)(2,1)}, bf16[128,640]{1,0:T(8,128)(2,1)S(1)}, u32[]{:S(2)}) copy-start(bf16[128,640]{1,0:T(8,128)(2,1)S(1)} %get-tuple-element.64.refs_0_) | copy-start | bytes 491524
  30.5 19.8 %collective-permute-start.3 = (bf16[4,640,128]{2,1,0:T(8,128)(2,1)S(1)}, bf16[4,640,128]{2,1,0:T(8,128)(2,1)S(1)}, u32[]{:S(2)}, u32[]{:S(2)}) collective-permute-start(bf16[4,640,128]{2,1,0:T(8,128)(2,1)S(1)} %pad_maximum_fusion.refs_4_), channel_id=1, source_target_pairs={{0,2},{1,3},{2,0},{3,1},{4,6},{5,7},{6,4},{7,5},{8,10},{9,11},{10,... | collective-permute-start | bytes 1966088 | tf_op jit(solution)/shard_map/ppermute | solution.py:279
  32.5 8.5 %collective-permute-start.4 = (bf16[128,640]{1,0:T(8,128)(2,1)S(1)}, bf16[128,640]{1,0:T(8,128)(2,1)S(1)}, u32[]{:S(2)}, u32[]{:S(2)}) collective-permute-start(bf16[128,640]{1,0:T(8,128)(2,1)S(1)} %get-tuple-element.61), channel_id=1, source_target_pairs={{0,4},{1,5},{2,6},{3,7},{4,0},{5,1},{6,2},{7,3},{8,12},{9,13},{10,... | collective-permute-start | bytes 491528 | tf_op jit(solution)/shard_map/ppermute | solution.py:279
  33.9 15.0 %collective-permute-start.5 = (bf16[128,640]{1,0:T(8,128)(2,1)S(1)}, bf16[128,640]{1,0:T(8,128)(2,1)S(1)}, u32[]{:S(2)}, u32[]{:S(2)}) collective-permute-start(bf16[128,640]{1,0:T(8,128)(2,1)S(1)} %get-tuple-element.62), channel_id=1, source_target_pairs={{0,8},{1,9},{2,10},{3,11},{4,12},{5,13},{6,14},{7,15},{8,0},{9,1},... | collective-permute-start | bytes 491528 | tf_op jit(solution)/shard_map/ppermute | solution.py:279
  36.3 13.4 %collective-permute-start.6 = (bf16[128,640]{1,0:T(8,128)(2,1)S(1)}, bf16[128,640]{1,0:T(8,128)(2,1)S(1)}, u32[]{:S(2)}, u32[]{:S(2)}) collective-permute-start(bf16[128,640]{1,0:T(8,128)(2,1)S(1)} %get-tuple-element.63), channel_id=1, source_target_pairs={{0,12},{1,13},{2,14},{3,15},{4,8},{5,9},{6,10},{7,11},{8,4},{9,5},... | collective-permute-start | bytes 491528 | tf_op jit(solution)/shard_map/ppermute | solution.py:279
  41.0 0.7 copy-start.3
  49.0 0.7 copy-start.5
  49.7 0.7 copy-start.7
  50.3 6.8 %collective-permute-start.7 = (bf16[4,640,128]{2,1,0:T(8,128)(2,1)S(1)}, bf16[4,640,128]{2,1,0:T(8,128)(2,1)S(1)}, u32[]{:S(2)}, u32[]{:S(2)}) collective-permute-start(bf16[4,640,128]{2,1,0:T(8,128)(2,1)S(1)} %pad_maximum_fusion.refs_4_), channel_id=1, source_target_pairs={{0,1},{1,0},{2,3},{3,2},{4,5},{5,4},{6,7},{7,6},{8,9},{9,8},{10,11... | collective-permute-start | bytes 1966088 | tf_op jit(solution)/shard_map/ppermute | solution.py:279
  50.3 6.8 %collective-permute-start.8 = (bf16[4,640,128]{2,1,0:T(8,128)(2,1)S(1)}, bf16[4,640,128]{2,1,0:T(8,128)(2,1)}, u32[]{:S(2)}, u32[]{:S(2)}) collective-permute-start(bf16[4,640,128]{2,1,0:T(8,128)(2,1)S(1)} %collective-permute-done.3.refs_5_), channel_id=1, source_target_pairs={{0,1},{1,0},{2,3},{3,2},{4,5},{5,4},{6,7},{7,6},{8,9},{9,8},{10,11... | collective-permute-start | bytes 1966088 | tf_op jit(solution)/shard_map/ppermute | solution.py:279
  51.2 0.9 copy-start.2
  52.1 0.9 copy-start.4
  53.0 0.9 copy-start.6
  53.9 0.9 copy-start.8
  60.6 5.6 %collective-permute-start.10 = (f32[512]{0:T(512)S(1)}, f32[512]{0:T(512)S(1)}, u32[]{:S(2)}, u32[]{:S(2)}) collective-permute-start(f32[512]{0:T(512)S(1)} %reduce), channel_id=1, source_target_pairs={{0,4},{1,5},{2,6},{3,7},{4,0},{5,1},{6,2},{7,3},{8,12},{9,13},{10,... | collective-permute-start | bytes 6152 | tf_op jit(solution)/shard_map/ppermute | solution.py:279
  62.6 4.5 %collective-permute-start.11 = (f32[512]{0:T(512)S(1)}, f32[512]{0:T(512)S(1)}, u32[]{:S(2)}, u32[]{:S(2)}) collective-permute-start(f32[512]{0:T(512)S(1)} %reduce), channel_id=1, source_target_pairs={{0,8},{1,9},{2,10},{3,11},{4,12},{5,13},{6,14},{7,15},{8,0},{9,1},... | collective-permute-start | bytes 6152 | tf_op jit(solution)/shard_map/ppermute | solution.py:279
  63.6 5.4 %collective-permute-start.12 = (f32[512]{0:T(512)S(1)}, f32[512]{0:T(512)S(1)}, u32[]{:S(2)}, u32[]{:S(2)}) collective-permute-start(f32[512]{0:T(512)S(1)} %reduce), channel_id=1, source_target_pairs={{0,12},{1,13},{2,14},{3,15},{4,8},{5,9},{6,10},{7,11},{8,4},{9,5},... | collective-permute-start | bytes 6152 | tf_op jit(solution)/shard_map/ppermute | solution.py:279
  65.1 18.0 %collective-permute-start.9 = (bf16[512,640]{1,0:T(8,128)(2,1)S(1)}, bf16[512,640]{1,0:T(8,128)(2,1)S(1)}, u32[]{:S(2)}, u32[]{:S(2)}) collective-permute-start(bf16[512,640]{1,0:T(8,128)(2,1)S(1)} %get-tuple-element.70.block_ref), channel_id=1, source_target_pairs={{0,4},{1,5},{2,6},{3,7},{4,8},{5,9},{6,10},{7,11},{8,12},{9,13},{1... | collective-permute-start | bytes 1966088 | tf_op jit(solution)/shard_map/ppermute | solution.py:282
  72.2 1.8 %collective-permute-start.13 = (bf16[2,160,640]{2,1,0:T(8,128)(2,1)S(1)}, bf16[2,160,640]{2,1,0:T(8,128)(2,1)S(1)}, u32[]{:S(2)}, u32[]{:S(2)}) collective-permute-start(bf16[2,160,640]{2,1,0:T(8,128)(2,1)S(1)} %get-tuple-element.74), channel_id=1, source_target_pairs={{0,1},{1,0},{2,3},{3,2},{4,5},{5,4},{6,7},{7,6},{8,9},{9,8},{10,11... | collective-permute-start | bytes 1228808 | tf_op jit(solution)/shard_map/ppermute | solution.py:279
  83.7 17.5 %collective-permute-start.15 = (bf16[512,640]{1,0:T(8,128)(2,1)S(1)}, bf16[512,640]{1,0:T(8,128)(2,1)S(1)}, u32[]{:S(2)}, u32[]{:S(2)}) collective-permute-start(bf16[512,640]{1,0:T(8,128)(2,1)S(1)} %collective-permute-done.9.block_ref), channel_id=1, source_target_pairs={{0,4},{1,5},{2,6},{3,7},{4,8},{5,9},{6,10},{7,11},{8,12},{9,13},{1... | collective-permute-start | bytes 1966088 | tf_op jit(solution)/shard_map/ppermute | solution.py:282
  83.8 2.2 %collective-permute-start.17 = (bf16[2,160,640]{2,1,0:T(8,128)(2,1)S(1)}, bf16[2,160,640]{2,1,0:T(8,128)(2,1)S(1)}, u32[]{:S(2)}, u32[]{:S(2)}) collective-permute-start(bf16[2,160,640]{2,1,0:T(8,128)(2,1)S(1)} %get-tuple-element.82), channel_id=1, source_target_pairs={{0,1},{1,0},{2,3},{3,2},{4,5},{5,4},{6,7},{7,6},{8,9},{9,8},{10,11... | collective-permute-start | bytes 1228808 | tf_op jit(solution)/shard_map/ppermute | solution.py:279
  84.8 2.7 %collective-permute-start.14 = (bf16[2,160,640]{2,1,0:T(8,128)(2,1)S(1)}, bf16[2,160,640]{2,1,0:T(8,128)(2,1)S(1)}, u32[]{:S(2)}, u32[]{:S(2)}) collective-permute-start(bf16[2,160,640]{2,1,0:T(8,128)(2,1)S(1)} %get-tuple-element.78), channel_id=1, source_target_pairs={{0,1},{1,0},{2,3},{3,2},{4,5},{5,4},{6,7},{7,6},{8,9},{9,8},{10,11... | collective-permute-start | bytes 1228808 | tf_op jit(solution)/shard_map/ppermute | solution.py:279
  85.4 7.9 %collective-permute-start.16 = (bf16[1,160,640]{2,1,0:T(8,128)(2,1)S(1)}, bf16[1,160,640]{2,1,0:T(8,128)(2,1)S(1)}, u32[]{:S(2)}, u32[]{:S(2)}) collective-permute-start(bf16[1,160,640]{2,1,0:T(8,128)(2,1)S(1)} %get-tuple-element.80), channel_id=1, source_target_pairs={{0,2},{1,3},{2,0},{3,1},{4,6},{5,7},{6,4},{7,5},{8,10},{9,11},{10,... | collective-permute-start | bytes 614408 | tf_op jit(solution)/shard_map/ppermute | solution.py:279
  86.0 11.7 %collective-permute-start.18 = (bf16[1,160,640]{2,1,0:T(8,128)(2,1)S(1)}, bf16[1,160,640]{2,1,0:T(8,128)(2,1)S(1)}, u32[]{:S(2)}, u32[]{:S(2)}) collective-permute-start(bf16[1,160,640]{2,1,0:T(8,128)(2,1)S(1)} %get-tuple-element.83), channel_id=1, source_target_pairs={{0,2},{1,3},{2,0},{3,1},{4,6},{5,7},{6,4},{7,5},{8,10},{9,11},{10,... | collective-permute-start | bytes 614408 | tf_op jit(solution)/shard_map/ppermute | solution.py:279
  87.6 13.6 %collective-permute-start.19 = (bf16[1,160,640]{2,1,0:T(8,128)(2,1)S(1)}, bf16[1,160,640]{2,1,0:T(8,128)(2,1)S(1)}, u32[]{:S(2)}, u32[]{:S(2)}) collective-permute-start(bf16[1,160,640]{2,1,0:T(8,128)(2,1)S(1)} %get-tuple-element.84), channel_id=1, source_target_pairs={{0,2},{1,3},{2,0},{3,1},{4,6},{5,7},{6,4},{7,5},{8,10},{9,11},{10,... | collective-permute-start | bytes 614408 | tf_op jit(solution)/shard_map/ppermute | solution.py:279
  101.9 3.9 %collective-permute-start.21 = (bf16[2,160,640]{2,1,0:T(8,128)(2,1)S(1)}, bf16[2,160,640]{2,1,0:T(8,128)(2,1)S(1)}, u32[]{:S(2)}, u32[]{:S(2)}) collective-permute-start(bf16[2,160,640]{2,1,0:T(8,128)(2,1)S(1)} %get-tuple-element.92), channel_id=1, source_target_pairs={{0,1},{1,0},{2,3},{3,2},{4,5},{5,4},{6,7},{7,6},{8,9},{9,8},{10,11... | collective-permute-start | bytes 1228808 | tf_op jit(solution)/shard_map/ppermute | solution.py:279
  102.0 8.8 %collective-permute-start.20 = (bf16[160,640]{1,0:T(8,128)(2,1)S(1)}, bf16[160,640]{1,0:T(8,128)(2,1)S(1)}, u32[]{:S(2)}, u32[]{:S(2)}) collective-permute-start(bf16[160,640]{1,0:T(8,128)(2,1)S(1)} %fusion), channel_id=1, source_target_pairs={{0,12},{1,13},{2,14},{3,15},{4,0},{5,1},{6,2},{7,3},{8,4},{9,5},{1... | collective-permute-start | bytes 614408 | tf_op jit(solution)/shard_map/ppermute | solution.py:282
  105.9 7.3 %collective-permute-start.22 = (bf16[1,160,640]{2,1,0:T(8,128)(2,1)S(1)}, bf16[1,160,640]{2,1,0:T(8,128)(2,1)S(1)}, u32[]{:S(2)}, u32[]{:S(2)}) collective-permute-start(bf16[1,160,640]{2,1,0:T(8,128)(2,1)S(1)} %get-tuple-element.94), channel_id=1, source_target_pairs={{0,2},{1,3},{2,0},{3,1},{4,6},{5,7},{6,4},{7,5},{8,10},{9,11},{10,... | collective-permute-start | bytes 614408 | tf_op jit(solution)/shard_map/ppermute | solution.py:279

commit v6 on v5

--- a/solution.py
+++ b/solution.py
@@ -16,7 +16,7 @@
 BF16, F32, I32 = jnp.bfloat16, jnp.float32, jnp.int32
 
 
-def call(kernel, out_shape, in_specs, args, scratch=(), aliases=None, limit=24 * 1024 * 1024):
+def call(kernel, out_shape, in_specs, args, scratch=(), aliases=None, limit=12 * 1024 * 1024):
     return pl.pallas_call(
         kernel,
         out_shape=out_shape,
@@ -41,7 +41,8 @@
             pltpu.make_async_copy(resolution_ref.at[:, own], resolution.at[:, own], sem.at[1, tile]),
         )
 
-    for tile in range(tiles):
+    ahead = min(3, tiles)
+    for tile in range(ahead):
         for copy in copies(tile):
             copy.start()
     edge = jnp.zeros((tall, reach), F32)
@@ -52,6 +53,12 @@
     def one_tile(tile, carry):
         for copy in copies(tile):
             copy.wait()
+
+        @pl.when(tile + ahead < tiles)
+        def _():
+            for copy in copies(tile + ahead):
+                copy.start()
+
         own = pl.ds(pl.multiple_of(tile * tall, tall), tall)
         padded[:, reach : reach + nobs] = flux[own, :].astype(F32)
         for start in range(0, nobs, step):
@@ -123,6 +130,7 @@
         [SMEM] * 4 + [VMEM] * 3,
         (outer, bins, starts, turns, smoothed, placing, back),
         [pltpu.VMEM((places, nobs), F32), pltpu.VMEM((places, OUTER * width), F32)],
+        limit=max(12 * 1024 * 1024, places * (nobs + OUTER * width) * 6),
     )
 
 
@@ -181,45 +189,14 @@
     )
 
 
-def product_kernel(left_ref, block_ref, send_ref, keep_ref):
-    pairs, share, wide = keep_ref.shape
-    value = jnp.dot(left_ref[...], block_ref[...], preferred_element_type=F32)
-    value = value.reshape(pairs, 2, share, wide)
-    keep_ref[...] = value[:, 0]
-    send_ref[...] = value[:, 1].astype(BF16)
-
-
-def product(left, block, inner):
-    wide = block.shape[1]
-    shape = (inner // 2, left.shape[0] // inner, wide)
-    return call(
-        product_kernel,
-        (jax.ShapeDtypeStruct(shape, BF16), jax.ShapeDtypeStruct(shape, F32)),
-        [VMEM, VMEM],
-        (left, block),
-    )
-
-
-def fold_kernel(held_ref, got_ref, send_ref, keep_ref):
-    for i in range(keep_ref.shape[0]):
-        keep_ref[i] = held_ref[2 * i] + got_ref[2 * i].astype(F32)
-        send_ref[i] = (held_ref[2 * i + 1] + got_ref[2 * i + 1].astype(F32)).astype(BF16)
-
-
-def fold(held, got):
-    shape = (held.shape[0] // 2,) + held.shape[1:]
-    return call(
-        fold_kernel,
-        (jax.ShapeDtypeStruct(shape, BF16), jax.ShapeDtypeStruct(shape, F32)),
-        [VMEM, VMEM],
-        (held, got),
-    )
-
-
-def mirror_kernel(q_ref, block_ref, scaled_ref, send_ref, keep_ref, value):
-    pairs, share, wide = keep_ref.shape
+def scale_kernel(rest_ref, factor_ref, out_ref):
+    out_ref[...] = (rest_ref[...] * factor_ref[...]).astype(BF16)
+
+
+def product_kernel(q_ref, tall_ref, wide_ref, send_ref, keep_ref, value):
+    pairs, share, _ = keep_ref.shape
     value[...] = lax.dot_general(
-        block_ref[...], scaled_ref[...], (((0,), (0,)), ((), ())), preferred_element_type=F32
+        tall_ref[...], wide_ref[...], (((0,), (0,)), ((), ())), preferred_element_type=F32
     )
     for e in range(2 * pairs):
         own = value[pl.ds(pl.multiple_of((q_ref[0] ^ e) * share, 8), share), :]
@@ -229,15 +206,31 @@
             keep_ref[e // 2] = own
 
 
-def mirror(q, block, scaled, inner):
-    tall, wide = block.shape[1], scaled.shape[1]
-    shape = (inner // 2, tall // inner, wide)
-    return call(
-        mirror_kernel,
+def product(q, tall, wide, inner):
+    rows, columns = tall.shape[1], wide.shape[1]
+    shape = (inner // 2, rows // inner, columns)
+    return call(
+        product_kernel,
         (jax.ShapeDtypeStruct(shape, BF16), jax.ShapeDtypeStruct(shape, F32)),
         [SMEM, VMEM, VMEM],
-        (q, block, scaled),
-        [pltpu.VMEM((tall, wide), F32)],
+        (q, tall, wide),
+        [pltpu.VMEM((rows, columns), F32)],
+    )
+
+
+def fold_kernel(held_ref, got_ref, send_ref, keep_ref):
+    for i in range(keep_ref.shape[0]):
+        keep_ref[i] = held_ref[2 * i] + got_ref[2 * i].astype(F32)
+        send_ref[i] = (held_ref[2 * i + 1] + got_ref[2 * i + 1].astype(F32)).astype(BF16)
+
+
+def fold(held, got):
+    shape = (held.shape[0] // 2,) + held.shape[1:]
+    return call(
+        fold_kernel,
+        (jax.ShapeDtypeStruct(shape, BF16), jax.ShapeDtypeStruct(shape, F32)),
+        [VMEM, VMEM],
+        (held, got),
     )
 
 
@@ -282,13 +275,19 @@
         return lax.ppermute(array, "spec", [(i, (i + outers * inner) % n) for i in range(n)])
 
     targets = destination[:, 0]
-    chunk = jnp.minimum(band_offset // band, nobs // band - 2)
-    shift = band_offset - chunk * band
-    small = jnp.pad(jnp.concatenate([chunk, shift]), ((0, 0), (0, band - nblocks)))
-    small = jnp.concatenate([targets.reshape(count // band, band), small]).astype(BF16)
-    small = jnp.pad(small, ((0, EXTRA - small.shape[0]), (0, 0)))
-    table = lax.all_to_all(jnp.broadcast_to(small[None], (n, EXTRA, band)), "spec", 0, 0, tiled=True)
+    table = jnp.concatenate([band_offset[0], targets])
+    tables = jnp.stack([table] + [swap(table, away * inner) for away in range(1, OUTER)])
     by_outer = resample_weight[0].reshape(OUTER, width, band)
+    tables, by_outer = lax.optimization_barrier((tables, by_outer))
+    names, offsets = tables[:, nblocks:], tables[:, None, :nblocks]
+    bit = 1
+    while bit < inner:
+        if 2 * bit == inner:
+            offsets, flux = lax.optimization_barrier((offsets, flux))
+        offsets = jnp.concatenate([offsets, swap(offsets, bit)], axis=1)
+        bit *= 2
+    offsets = offsets.reshape(n, nblocks)
+
     pieces = [lax.dynamic_index_in_dim(by_outer, outer, 0, keepdims=False)]
     for away in range(1, OUTER):
         theirs = lax.dynamic_index_in_dim(by_outer, outer ^ away, 0, keepdims=False)
@@ -310,23 +309,19 @@
     placed = (position[:, None] == slot[None, :]).astype(BF16)
     ends = jnp.sum(jnp.where(which[:, None] <= which[None, :], amount[:, None], 0), axis=0)
     group_bin = jnp.sum((ends[None, :] <= slot[: places // GROUP, None]).astype(I32), axis=1)
-    entries = jnp.minimum(group_bin, n - 1)
-
-    table, smoothed = lax.optimization_barrier((table, smoothed))
-    lines = count // band
-    names = lax.dynamic_index_in_dim(table[:, :lines].reshape(OUTER, inner, count), q, 1, keepdims=False)
-    names = names.reshape(rows, 1).astype(I32)
-    starts = table[:, lines, :nblocks].astype(I32) * band
-    turns = (2 * band - table[:, lines + 1, :nblocks].astype(I32)) & (2 * band - 1)
-    outer1 = outer.reshape(1)
-    windows = cut_windows(outer1, entries, starts, turns, smoothed, placing, placed, band)
-
-    pieces, windows = lax.optimization_barrier((pieces, windows))
+    entries = jnp.minimum(group_bin, n - 1) ^ me
+
+    pieces, smoothed, offsets = lax.optimization_barrier((pieces, smoothed, offsets))
     mixed = jnp.stack(pieces)
     bit = inner // 2
     weights = [mixed, swap(mixed, bit)]
     mine = me ^ (jnp.arange(OUTER, dtype=I32) * inner)
     ids = [mine, mine ^ bit]
+
+    chunk = jnp.minimum(offsets // band, nobs // band - 2)
+    turns = (2 * band + chunk * band - offsets) & (2 * band - 1)
+    outer1 = outer.reshape(1)
+    windows = cut_windows(outer1, entries, chunk * band, turns, smoothed, placing, placed, band)
     arrived = [windows[0]] + [swap(windows[away], away * inner) for away in range(1, OUTER)]
     weights, arrived = lax.optimization_barrier((weights, arrived))
     while bit > 1:
@@ -334,20 +329,20 @@
         weights = weights + [swap(piece, bit) for piece in weights]
         ids = ids + [piece ^ bit for piece in ids]
     early, late = jnp.concatenate(ids[:2]), jnp.concatenate(ids[2:])
-    begun = resample(outer1, early, names, arrived, weights[:2], [(0, width)], band)
-    rest, sent, squares = resample(outer1, late, names, arrived, weights[2:], [(0, width)], band, begun)
+    order_of = jnp.arange(OUTER, dtype=I32) ^ outer
+    named = jnp.sum(
+        jnp.where(order_of[:, None, None] == jnp.arange(OUTER, dtype=I32)[None, :, None], names[None], 0), axis=1
+    ).reshape(rows, 1)
+    begun = resample(outer1, early, named, arrived, weights[:2], [(0, width)], band)
+    rest, sent, squares = resample(outer1, late, named, arrived, weights[2:], [(0, width)], band, begun)
     squares = squares.reshape(rows)
 
     total = squares
     for away in range(1, OUTER):
         total = total + swap(squares, away * inner)
     scale = lax.rsqrt(total / nrest + 1e-06)
-    factor = (scale * scale / (count * n))[:, None]
-    scaled = (rest * factor).astype(BF16)
-    left = scaled.T
-    left = left.reshape(inner, share, rows)
-    left = jnp.stack([lax.dynamic_index_in_dim(left, q ^ e, 0, keepdims=False) for e in range(inner)])
-    left = left.reshape(width, rows)
+    factor = (scale * scale / (count * n)).reshape(rows, 1)
+    scaled = call(scale_kernel, jax.ShapeDtypeStruct(rest.shape, BF16), [VMEM, VMEM], (rest, factor))
 
     def reduce(send, held):
         bit = 1
@@ -359,19 +354,21 @@
     def finish(send):
         return swap(send, inner // 2)[0]
 
-    send0, held0 = reduce(*product(left, sent, inner))
+    q1 = q.reshape(1)
+    send0, held0 = reduce(*product(q1, scaled, sent, inner))
+    got0 = finish(send0)
     first = step(sent, 1)
-    first, send0 = lax.optimization_barrier((first, send0))
+    first, got0 = lax.optimization_barrier((first, got0))
     second = step(first, 1)
-    got0 = finish(send0)
-    sendm, heldm = reduce(*mirror(q.reshape(1), first, scaled, inner))
+    sendm, heldm = reduce(*product(q1, first, scaled, inner))
+    sendm, first = lax.optimization_barrier((sendm, first))
     gotm = finish(sendm)
-    send1, held1 = reduce(*product(left, first, inner))
+    send1, held1 = reduce(*product(q1, scaled, first, inner))
     got1 = finish(send1)
-    second, got0, got1, gotm = lax.optimization_barrier((second, got0, got1, gotm))
-    send2, held2 = reduce(*product(left, second, inner))
+    second, got1, gotm = lax.optimization_barrier((second, got1, gotm))
+    back = step((heldm + gotm.astype(F32)).astype(BF16), -1)
+    send2, held2 = reduce(*product(q1, scaled, second, inner))
     got2 = finish(send2)
-    back = step((heldm + gotm.astype(F32)).astype(BF16), -1)
     at = (outer - jnp.arange(OUTER, dtype=I32)) % OUTER
     return place(at, back, [(held0, got0), (held1, got1), (held2, got2)])
 

time: 115 us -> 118 us (1.026)
  waiting for transfers between devices: 44.6 us -> 55.1 us
  starting transfers between devices: 32.3 us -> 26.3 us
  Pallas kernels: 26.2 us -> 23.7 us
  other arithmetic: 2.43 us -> 4.22 us
  local copies, waits for them, and re-layouts: 9.17 us -> 7.92 us
    all_to_all x1 -> x0, starting transfers between devices: 6.16 us -> none  [local(): lax.all_to_all(jnp.broadcast_to(small[None], (n, EXTRA, band)), 'spec', 0...]
    ppermute x20 -> x25, waiting for transfers between devices: 31.4 us -> 36.9 us  [swap(): return lax.ppermute(array, 'spec', [(i, i ^ bit) for i in range(n)])]
    ppermute x3, waiting for transfers between devices: 13.2 us -> 18.3 us  [step(): lax.ppermute(array, 'spec', [(i, (i + outers * inner) % n) for i in range...]
    ppermute x20 -> x25, starting transfers between devices: 21.2 us -> 25.3 us  [swap(): return lax.ppermute(array, 'spec', [(i, i ^ bit) for i in range(n)])]
    ppermute x3, starting transfers between devices: 4.91 us -> 1.05 us  [step(): lax.ppermute(array, 'spec', [(i, (i + outers * inner) % n) for i in range...]
    pallas_call x13 -> x14, Pallas kernels: 26.2 us -> 23.7 us  [call(): pl.pallas_call(kernel, out_shape=out_shape, in_specs=in_specs, out_specs=...]
    transpose x1 -> x0, local copies, waits for them, and re-layouts: 1.33 us -> none  [local(): left = scaled.T]
    unnamed x22 -> x18, local copies, waits for them, and re-layouts: 5.69 us -> 6.33 us
  transfers between devices with their start and end apart: 24 -> 28, of which waited for: 11 -> 17; matrix products, arithmetic and copies ran while one was open for 4% -> 4% of each run, Pallas kernels for 17% -> 14%
where the time goes in v6:
time: 118 us
  waiting for transfers between devices  55.1 us (47%)
  starting transfers between devices  26.3 us (22%)
  Pallas kernels  23.7 us (20%)
  local copies, waits for them, and re-layouts  7.92 us (7%)
  other arithmetic  4.22 us (4%)
    ppermute x25, waiting for transfers between devices, swap(): return lax.ppermute(array, 'spec', [(i, i ^ bit) for i in range(n)])  36.9 us
    ppermute x25, starting transfers between devices, swap(): return lax.ppermute(array, 'spec', [(i, i ^ bit) for i in range(n)])  25.3 us
    pallas_call x14, Pallas kernels, call(): pl.pallas_call(kernel, out_shape=out_shape, in_specs=in_specs, out_specs=...  23.7 us
    ppermute x3, waiting for transfers between devices, step(): lax.ppermute(array, 'spec', [(i, (i + outers * inner) % n) for i in range...  18.3 us
    unnamed x18, local copies, waits for them, and re-layouts  6.33 us
  transfers between devices with their start and end apart: 28, of which 17 were waited for; matrix products, arithmetic and copies ran while one was open for 4% of the time, Pallas kernels for 14%

profile of v6, /device:TPU:0, one launch (start us, length us, event | category | flops | bytes accessed | tf_op | source)
XLA Modules:
  0.0 117.7 jit_solution(13373598453440931402)
XLA Ops:
  0.0 0.8 pad_add_fusion.3
  0.8 5.0 %collective-permute-start.2 = (s32[148]{0:T(256)S(1)}, s32[148]{0:T(256)S(1)}, u32[]{:S(2)}, u32[]{:S(2)}) collective-permute-start(s32[148]{0:T(256)S(1)} %pad_add_fusion.3), channel_id=1, source_target_pairs={{0,12},{1,13},{2,14},{3,15},{4,8},{5,9},{6,10},{7,11},{8,4},{9,5},... | collective-permute-start | bytes 1784 | tf_op jit(solution)/shard_map/ppermute | solution.py:272
  5.9 0.6 collective-permute-start
  6.5 0.9 convert_reduce_fusion
  7.4 0.8 convert_reduce_fusion.2
  8.2 0.7 select_reduce_fusion
  9.2 1.1 collective-permute-done.1
  10.5 1.2 %dynamic-slice_bitcast_fusion = (bf16[640,128]{1,0:T(8,128)(2,1)S(1)}, bf16[640,128]{1,0:T(8,128)(2,1)S(1)}, bf16[640,128]{1,0:T(8,128)(2,1)S(1)}, bf16[640,128]{1,0:T(8,128)(2,1)S(1)}) fusion(bf16[4,640,128]{2,1,0:T(8,128)(2,1)} %bitcast.46, s32[]{:T(128)S(6)} %select_n.67, s32[]{:T(128)S(6)} %select_n.66, s32[]{:T(128)S(6)} %select_n.65, s32[]{:T(128)S(6)} %select_n.64), kind=kLoop, calls=%fused_computation.3 | loop fusion | bytes 1310736 | tf_op jit(solution)/shard_map/jit(dynamic_index_in_dim)/squeeze | solution.py:293
  11.7 2.7 %collective-permute-start.5 = (bf16[640,128]{1,0:T(8,128)(2,1)S(1)}, bf16[640,128]{1,0:T(8,128)(2,1)S(1)}, u32[]{:S(2)}, u32[]{:S(2)}) collective-permute-start(bf16[640,128]{1,0:T(8,128)(2,1)S(1)} %get-tuple-element.97), channel_id=1, source_target_pairs={{0,12},{1,13},{2,14},{3,15},{4,8},{5,9},{6,10},{7,11},{8,4},{9,5},... | collective-permute-start | bytes 491528 | tf_op jit(solution)/shard_map/ppermute | solution.py:272
  14.4 1.7 %collective-permute-start.3 = (bf16[640,128]{1,0:T(8,128)(2,1)S(1)}, bf16[640,128]{1,0:T(8,128)(2,1)S(1)}, u32[]{:S(2)}, u32[]{:S(2)}) collective-permute-start(bf16[640,128]{1,0:T(8,128)(2,1)S(1)} %get-tuple-element.99), channel_id=1, source_target_pairs={{0,4},{1,5},{2,6},{3,7},{4,0},{5,1},{6,2},{7,3},{8,12},{9,13},{10,... | collective-permute-start | bytes 491528 | tf_op jit(solution)/shard_map/ppermute | solution.py:272
  16.1 1.5 %collective-permute-start.7 = (s32[4,2,20]{2,0,1:T(4,128)S(1)}, s32[4,2,20]{2,0,1:T(4,128)S(1)}, u32[]{:S(2)}, u32[]{:S(2)}) collective-permute-start(s32[4,2,20]{2,0,1:T(4,128)S(1)} %pad_add_fusion.2), channel_id=1, source_target_pairs={{0,2},{1,3},{2,0},{3,1},{4,6},{5,7},{6,4},{7,5},{8,10},{9,11},{10,... | collective-permute-start | bytes 1928 | tf_op jit(solution)/shard_map/ppermute | solution.py:272
  17.7 0.1 convert_reduce_fusion.1
  17.7 7.2 %shard_map.55.smoothed_ref = bf16[128,3968]{1,0:T(8,128)(2,1)S(1)} custom-call(bf16[128,3968]{1,0:T(8,128)(2,1)S(1)} %copy-done, bf16[11,128,3968]{2,1,0:T(8,128)(2,1)} %bitcast.44), custom_call_target="tpu_custom_call" | custom-call | flops 1 | bytes 1 | tf_op jit(solution)/shard_map/pallas_call | solution.py:20
  25.0 4.1 %collective-permute-done.4 = bf16[640,128]{1,0:T(8,128)(2,1)S(1)} collective-permute-done((bf16[640,128]{1,0:T(8,128)(2,1)S(1)}, bf16[640,128]{1,0:T(8,128)(2,1)S(1)}, u32[]{:S(2)}, u32[]{:S(2)}) %collective-permute-start.4) | collective-permute-done | bytes 163872 | tf_op jit(solution)/shard_map/ppermute | solution.py:272
  29.2 1.6 %collective-permute-start.8 = (bf16[4,640,128]{2,1,0:T(8,128)(2,1)S(1)}, bf16[4,640,128]{2,1,0:T(8,128)(2,1)S(1)}, u32[]{:S(2)}, u32[]{:S(2)}) collective-permute-start(bf16[4,640,128]{2,1,0:T(8,128)(2,1)S(1)} %pad_maximum_fusion.refs_4_), channel_id=1, source_target_pairs={{0,2},{1,3},{2,0},{3,1},{4,6},{5,7},{6,4},{7,5},{8,10},{9,11},{10,... | collective-permute-start | bytes 1966088 | tf_op jit(solution)/shard_map/ppermute | solution.py:272
  30.8 5.4 %shard_map.56 = (bf16[128,640]{1,0:T(8,128)(2,1)S(1)}, bf16[128,640]{1,0:T(8,128)(2,1)S(1)}, bf16[128,640]{1,0:T(8,128)(2,1)S(1)}, bf16[128,640]{1,0:T(8,128)(2,1)S(1)}) custom-call(s32[1]{0:T(128)} %bitcast.1.outer_ref, s32[30]{0:T(128)S(1)} %minimum_xor_fusion.bins_ref, s32[16,20]{1,0:T(8,128)S(1)} %get-tuple-element.102.starts_ref, ...), custom_call_target="tpu_custom_call" | custom-call | flops 1 | bytes 1 | tf_op jit(solution)/shard_map/pallas_call | solution.py:20
  36.2 0.7 copy-done.1
  36.9 3.2 %collective-permute-start.10 = (bf16[128,640]{1,0:T(8,128)(2,1)S(1)}, bf16[128,640]{1,0:T(8,128)(2,1)S(1)}, u32[]{:S(2)}, u32[]{:S(2)}) collective-permute-start(bf16[128,640]{1,0:T(8,128)(2,1)S(1)} %get-tuple-element.63), channel_id=1, source_target_pairs={{0,8},{1,9},{2,10},{3,11},{4,12},{5,13},{6,14},{7,15},{8,0},{9,1},... | collective-permute-start | bytes 491528 | tf_op jit(solution)/shard_map/ppermute | solution.py:272
  40.1 1.2 %collective-permute-start.11 = (bf16[128,640]{1,0:T(8,128)(2,1)S(1)}, bf16[128,640]{1,0:T(8,128)(2,1)S(1)}, u32[]{:S(2)}, u32[]{:S(2)}) collective-permute-start(bf16[128,640]{1,0:T(8,128)(2,1)S(1)} %get-tuple-element.64), channel_id=1, source_target_pairs={{0,12},{1,13},{2,14},{3,15},{4,8},{5,9},{6,10},{7,11},{8,4},{9,5},... | collective-permute-start | bytes 491528 | tf_op jit(solution)/shard_map/ppermute | solution.py:272
  41.3 3.9 %collective-permute-done.9.refs_1_ = bf16[128,640]{1,0:T(8,128)(2,1)S(1)} collective-permute-done((bf16[128,640]{1,0:T(8,128)(2,1)S(1)}, bf16[128,640]{1,0:T(8,128)(2,1)S(1)}, u32[]{:S(2)}, u32[]{:S(2)}) %collective-permute-start.9) | collective-permute-done | bytes 163872 | tf_op jit(solution)/shard_map/ppermute | solution.py:272
  45.2 0.7 copy-done.3
  45.9 6.3 %collective-permute-done.10.refs_2_ = bf16[128,640]{1,0:T(8,128)(2,1)S(1)} collective-permute-done((bf16[128,640]{1,0:T(8,128)(2,1)S(1)}, bf16[128,640]{1,0:T(8,128)(2,1)S(1)}, u32[]{:S(2)}, u32[]{:S(2)}) %collective-permute-start.10) | collective-permute-done | bytes 163872 | tf_op jit(solution)/shard_map/ppermute | solution.py:272
  52.2 0.7 copy-done.5
  52.9 0.7 copy-done.7
  53.6 0.5 collective-permute-start.13
  54.4 0.1 select_reduce_fusion.2
  54.5 0.1 copy.14.names_ref
  54.6 0.9 copy-done.2
  55.6 0.9 copy-done.4
  56.5 0.9 copy-done.6
  57.4 0.9 copy-done.8
  58.3 2.2 %shard_map.57.refs_6_ = f32[512,640]{1,0:T(8,128)S(1)} custom-call(s32[1]{0:T(128)} %bitcast.1.outer_ref, s32[8]{0:T(128)S(1)} %pad_add_fusion.5.bins_ref, s32[512,1]{1,0:T(8,128)S(1)} %copy.14.names_ref, bf16[128,640]{1,0:T(8,128)(2,1)S(1)} %copy-done.2, bf16[128,640]{1,0:T(8,128)(2,1)S(1)} %copy-done.4, bf16[128,640]{1,0:T(8,128)(2,1)S(1)} %copy-done.6, ...), custom_call_target="tpu_custom_call" | custom-call | flops 1 | bytes 1 | tf_op jit(solution)/shard_map/pallas_call | solution.py:20
  60.5 3.3 %shard_map.58 = (f32[512,640]{1,0:T(8,128)S(1)}, bf16[512,640]{1,0:T(8,128)(2,1)S(1)}, f32[512,1]{1,0:T(8,128)S(1)}) custom-call(s32[1]{0:T(128)} %bitcast.1.outer_ref, s32[8]{0:T(128)S(1)} %pad_add_fusion.4.bins_ref, s32[512,1]{1,0:T(8,128)S(1)} %copy.14.names_ref, bf16[128,640]{1,0:T(8,128)(2,1)S(1)} %copy-done.2, ...), custom_call_target="tpu_custom_call", output_to_operand_aliasing={{0}: (9, {})} | custom-call | flops 1 | bytes 1 | tf_op jit(solution)/shard_map/pallas_call | solution.py:20
  63.9 0.1 reduce
  64.0 2.3 %collective-permute-start.17 = (f32[512]{0:T(512)S(1)}, f32[512]{0:T(512)S(1)}, u32[]{:S(2)}, u32[]{:S(2)}) collective-permute-start(f32[512]{0:T(512)S(1)} %reduce), channel_id=1, source_target_pairs={{0,12},{1,13},{2,14},{3,15},{4,8},{5,9},{6,10},{7,11},{8,4},{9,5},... | collective-permute-start | bytes 6152 | tf_op jit(solution)/shard_map/ppermute | solution.py:272
  66.3 1.1 collective-permute-start.16
  67.4 1.1 collective-permute-start.15
  68.5 0.9 collective-permute-start.14
  69.4 1.3 %collective-permute-done.16 = f32[512]{0:T(512)S(1)} collective-permute-done((f32[512]{0:T(512)S(1)}, f32[512]{0:T(512)S(1)}, u32[]{:S(2)}, u32[]{:S(2)}) %collective-permute-start.16) | collective-permute-done | bytes 2080 | tf_op jit(solution)/shard_map/ppermute | solution.py:272
  70.8 0.2 collective-permute-done.15
  71.0 0.2 copy.15.factor_ref
  71.1 0.1 shard_map.59.tall_ref.wide_ref
  71.3 0.8 shard_map.60
  72.2 1.7 %collective-permute-done.18.got_ref = bf16[2,160,640]{2,1,0:T(8,128)(2,1)S(1)} collective-permute-done((bf16[2,160,640]{2,1,0:T(8,128)(2,1)S(1)}, bf16[2,160,640]{2,1,0:T(8,128)(2,1)S(1)}, u32[]{:S(2)}, u32[]{:S(2)}) %collective-permute-start.18) | collective-permute-done | bytes 409632 | tf_op jit(solution)/shard_map/ppermute | solution.py:272
  73.9 0.1 shard_map.61
  74.0 0.6 collective-permute-start.19
  74.6 6.6 %collective-permute-done.19 = bf16[1,160,640]{2,1,0:T(8,128)(2,1)S(1)} collective-permute-done((bf16[1,160,640]{2,1,0:T(8,128)(2,1)S(1)}, bf16[1,160,640]{2,1,0:T(8,128)(2,1)S(1)}, u32[]{:S(2)}, u32[]{:S(2)}) %collective-permute-start.19) | collective-permute-done | bytes 204832 | tf_op jit(solution)/shard_map/ppermute | solution.py:272
  81.2 4.9 %collective-permute-done.14.tall_ref.wide_ref = bf16[512,640]{1,0:T(8,128)(2,1)S(1)} collective-permute-done((bf16[512,640]{1,0:T(8,128)(2,1)S(1)}, bf16[512,640]{1,0:T(8,128)(2,1)S(1)}, u32[]{:S(2)}, u32[]{:S(2)}) %collective-permute-start.14) | collective-permute-done | bytes 655392 | tf_op jit(solution)/shard_map/ppermute | solution.py:275
  86.1 0.8 shard_map.62
  87.0 1.7 %collective-permute-done.20.got_ref = bf16[2,160,640]{2,1,0:T(8,128)(2,1)S(1)} collective-permute-done((bf16[2,160,640]{2,1,0:T(8,128)(2,1)S(1)}, bf16[2,160,640]{2,1,0:T(8,128)(2,1)S(1)}, u32[]{:S(2)}, u32[]{:S(2)}) %collective-permute-start.20) | collective-permute-done | bytes 409632 | tf_op jit(solution)/shard_map/ppermute | solution.py:272
  88.7 0.1 shard_map.63
  88.8 0.8 shard_map.64
  89.6 0.2 collective-permute-start.22
  89.8 0.5 collective-permute-start.24
  90.3 1.1 collective-permute-done.22.got_ref
  91.5 0.6 collective-permute-start.23
  92.1 5.7 %collective-permute-done.24 = bf16[1,160,640]{2,1,0:T(8,128)(2,1)S(1)} collective-permute-done((bf16[1,160,640]{2,1,0:T(8,128)(2,1)S(1)}, bf16[1,160,640]{2,1,0:T(8,128)(2,1)S(1)}, u32[]{:S(2)}, u32[]{:S(2)}) %collective-permute-start.24) | collective-permute-done | bytes 204832 | tf_op jit(solution)/shard_map/ppermute | solution.py:272
  97.7 8.2 %collective-permute-done.21.wide_ref = bf16[512,640]{1,0:T(8,128)(2,1)S(1)} collective-permute-done((bf16[512,640]{1,0:T(8,128)(2,1)S(1)}, bf16[512,640]{1,0:T(8,128)(2,1)S(1)}, u32[]{:S(2)}, u32[]{:S(2)}) %collective-permute-start.21) | collective-permute-done | bytes 655392 | tf_op jit(solution)/shard_map/ppermute | solution.py:275
  105.9 0.8 shard_map.66
  106.9 1.6 %collective-permute-done.26.got_ref = bf16[2,160,640]{2,1,0:T(8,128)(2,1)S(1)} collective-permute-done((bf16[2,160,640]{2,1,0:T(8,128)(2,1)S(1)}, bf16[2,160,640]{2,1,0:T(8,128)(2,1)S(1)}, u32[]{:S(2)}, u32[]{:S(2)}) %collective-permute-start.26) | collective-permute-done | bytes 409632 | tf_op jit(solution)/shard_map/ppermute | solution.py:272
  108.6 0.6 collective-permute-start.27
  109.2 5.2 %collective-permute-done.25.refs_1_ = bf16[160,640]{1,0:T(8,128)(2,1)S(1)} collective-permute-done((bf16[160,640]{1,0:T(8,128)(2,1)S(1)}, bf16[160,640]{1,0:T(8,128)(2,1)S(1)}, u32[]{:S(2)}, u32[]{:S(2)}) %collective-permute-start.25) | collective-permute-done | bytes 204832 | tf_op jit(solution)/shard_map/ppermute | solution.py:275
  114.4 1.4 %collective-permute-done.27 = bf16[1,160,640]{2,1,0:T(8,128)(2,1)S(1)} collective-permute-done((bf16[1,160,640]{2,1,0:T(8,128)(2,1)S(1)}, bf16[1,160,640]{2,1,0:T(8,128)(2,1)S(1)}, u32[]{:S(2)}, u32[]{:S(2)}) %collective-permute-start.27) | collective-permute-done | bytes 204832 | tf_op jit(solution)/shard_map/ppermute | solution.py:272
  115.8 1.9 %shard_map.68 = f32[160,2560]{1,0:T(8,128)} custom-call(s32[4]{0:T(128)S(1)} %and_select_fusion.1.refs_0_, bf16[160,640]{1,0:T(8,128)(2,1)S(1)} %collective-permute-done.25.refs_1_, f32[160,640]{1,0:T(8,128)S(1)} %bitcast.38, bf16[160,640]{1,0:T(8,128)(2,1)S(1)} %bitcast.41, f32[160,640]{1,0:T(8,128)S(1)} %bitcast.39, bf16[160,640]{1,0:T(8,128)(2,1)S(1)} %bitcast.42, ...), custom_call_target="tpu_custom_call" | custom-call | flops 1 | bytes 1 | tf_op jit(solution)/shard_map/pallas_call | solution.py:20
  (59 shorter events, 1.4 us)
Async XLA Ops:
  0.0 17.7 %copy-start = (bf16[128,3968]{1,0:T(8,128)(2,1)S(1)}, bf16[128,3968]{1,0:T(8,128)(2,1)}, u32[]{:S(2)}) copy-start(bf16[128,3968]{1,0:T(8,128)(2,1)} %flux_ref) | copy-start | bytes 3047428
  0.8 8.4 %collective-permute-start.2 = (s32[148]{0:T(256)S(1)}, s32[148]{0:T(256)S(1)}, u32[]{:S(2)}, u32[]{:S(2)}) collective-permute-start(s32[148]{0:T(256)S(1)} %pad_add_fusion.3), channel_id=1, source_target_pairs={{0,12},{1,13},{2,14},{3,15},{4,8},{5,9},{6,10},{7,11},{8,4},{9,5},... | collective-permute-start | bytes 1784 | tf_op jit(solution)/shard_map/ppermute | solution.py:272
  5.9 4.5 %collective-permute-start.1 = (s32[148]{0:T(256)S(1)}, s32[148]{0:T(256)S(1)}, u32[]{:S(2)}, u32[]{:S(2)}) collective-permute-start(s32[148]{0:T(256)S(1)} %pad_add_fusion.3), channel_id=1, source_target_pairs={{0,8},{1,9},{2,10},{3,11},{4,12},{5,13},{6,14},{7,15},{8,0},{9,1},... | collective-permute-start | bytes 1784 | tf_op jit(solution)/shard_map/ppermute | solution.py:272
  5.9 4.5 %collective-permute-start = (s32[148]{0:T(256)S(1)}, s32[148]{0:T(256)S(1)}, u32[]{:S(2)}, u32[]{:S(2)}) collective-permute-start(s32[148]{0:T(256)S(1)} %pad_add_fusion.3), channel_id=1, source_target_pairs={{0,4},{1,5},{2,6},{3,7},{4,0},{5,1},{6,2},{7,3},{8,12},{9,13},{10,... | collective-permute-start | bytes 1784 | tf_op jit(solution)/shard_map/ppermute | solution.py:272
  10.4 5.8 %collective-permute-start.6 = (s32[4,1,20]{2,0,1:T(4,128)S(1)}, s32[4,1,20]{2,0,1:T(4,128)S(1)}, u32[]{:S(2)}, u32[]{:S(2)}) collective-permute-start(s32[4,1,20]{2,0,1:T(4,128)S(1)} %slice_bitcast_fusion), channel_id=1, source_target_pairs={{0,1},{1,0},{2,3},{3,2},{4,5},{5,4},{6,7},{7,6},{8,9},{9,8},{10,11... | collective-permute-start | bytes 968 | tf_op jit(solution)/shard_map/ppermute | solution.py:272
  11.7 13.4 %collective-permute-start.5 = (bf16[640,128]{1,0:T(8,128)(2,1)S(1)}, bf16[640,128]{1,0:T(8,128)(2,1)S(1)}, u32[]{:S(2)}, u32[]{:S(2)}) collective-permute-start(bf16[640,128]{1,0:T(8,128)(2,1)S(1)} %get-tuple-element.97), channel_id=1, source_target_pairs={{0,12},{1,13},{2,14},{3,15},{4,8},{5,9},{6,10},{7,11},{8,4},{9,5},... | collective-permute-start | bytes 491528 | tf_op jit(solution)/shard_map/ppermute | solution.py:272
  14.4 14.7 %collective-permute-start.4 = (bf16[640,128]{1,0:T(8,128)(2,1)S(1)}, bf16[640,128]{1,0:T(8,128)(2,1)S(1)}, u32[]{:S(2)}, u32[]{:S(2)}) collective-permute-start(bf16[640,128]{1,0:T(8,128)(2,1)S(1)} %get-tuple-element.98), channel_id=1, source_target_pairs={{0,8},{1,9},{2,10},{3,11},{4,12},{5,13},{6,14},{7,15},{8,0},{9,1},... | collective-permute-start | bytes 491528 | tf_op jit(solution)/shard_map/ppermute | solution.py:272
  14.4 14.7 %collective-permute-start.3 = (bf16[640,128]{1,0:T(8,128)(2,1)S(1)}, bf16[640,128]{1,0:T(8,128)(2,1)S(1)}, u32[]{:S(2)}, u32[]{:S(2)}) collective-permute-start(bf16[640,128]{1,0:T(8,128)(2,1)S(1)} %get-tuple-element.99), channel_id=1, source_target_pairs={{0,4},{1,5},{2,6},{3,7},{4,0},{5,1},{6,2},{7,3},{8,12},{9,13},{10,... | collective-permute-start | bytes 491528 | tf_op jit(solution)/shard_map/ppermute | solution.py:272
  16.1 8.9 %collective-permute-start.7 = (s32[4,2,20]{2,0,1:T(4,128)S(1)}, s32[4,2,20]{2,0,1:T(4,128)S(1)}, u32[]{:S(2)}, u32[]{:S(2)}) collective-permute-start(s32[4,2,20]{2,0,1:T(4,128)S(1)} %pad_add_fusion.2), channel_id=1, source_target_pairs={{0,2},{1,3},{2,0},{3,1},{4,6},{5,7},{6,4},{7,5},{8,10},{9,11},{10,... | collective-permute-start | bytes 1928 | tf_op jit(solution)/shard_map/ppermute | solution.py:272
  29.2 24.3 %collective-permute-start.8 = (bf16[4,640,128]{2,1,0:T(8,128)(2,1)S(1)}, bf16[4,640,128]{2,1,0:T(8,128)(2,1)S(1)}, u32[]{:S(2)}, u32[]{:S(2)}) collective-permute-start(bf16[4,640,128]{2,1,0:T(8,128)(2,1)S(1)} %pad_maximum_fusion.refs_4_), channel_id=1, source_target_pairs={{0,2},{1,3},{2,0},{3,1},{4,6},{5,7},{6,4},{7,5},{8,10},{9,11},{10,... | collective-permute-start | bytes 1966088 | tf_op jit(solution)/shard_map/ppermute | solution.py:272
  36.2 0.7 copy-start.1
  36.9 8.3 %collective-permute-start.9 = (bf16[128,640]{1,0:T(8,128)(2,1)S(1)}, bf16[128,640]{1,0:T(8,128)(2,1)S(1)}, u32[]{:S(2)}, u32[]{:S(2)}) collective-permute-start(bf16[128,640]{1,0:T(8,128)(2,1)S(1)} %get-tuple-element.62), channel_id=1, source_target_pairs={{0,4},{1,5},{2,6},{3,7},{4,0},{5,1},{6,2},{7,3},{8,12},{9,13},{10,... | collective-permute-start | bytes 491528 | tf_op jit(solution)/shard_map/ppermute | solution.py:272
  36.9 15.3 %collective-permute-start.10 = (bf16[128,640]{1,0:T(8,128)(2,1)S(1)}, bf16[128,640]{1,0:T(8,128)(2,1)S(1)}, u32[]{:S(2)}, u32[]{:S(2)}) collective-permute-start(bf16[128,640]{1,0:T(8,128)(2,1)S(1)} %get-tuple-element.63), channel_id=1, source_target_pairs={{0,8},{1,9},{2,10},{3,11},{4,12},{5,13},{6,14},{7,15},{8,0},{9,1},... | collective-permute-start | bytes 491528 | tf_op jit(solution)/shard_map/ppermute | solution.py:272
  40.1 12.8 %collective-permute-start.11 = (bf16[128,640]{1,0:T(8,128)(2,1)S(1)}, bf16[128,640]{1,0:T(8,128)(2,1)S(1)}, u32[]{:S(2)}, u32[]{:S(2)}) collective-permute-start(bf16[128,640]{1,0:T(8,128)(2,1)S(1)} %get-tuple-element.64), channel_id=1, source_target_pairs={{0,12},{1,13},{2,14},{3,15},{4,8},{5,9},{6,10},{7,11},{8,4},{9,5},... | collective-permute-start | bytes 491528 | tf_op jit(solution)/shard_map/ppermute | solution.py:272
  45.2 0.7 copy-start.3
  52.2 0.7 copy-start.5
  52.9 0.7 copy-start.7
  53.6 7.0 %collective-permute-start.12 = (bf16[4,640,128]{2,1,0:T(8,128)(2,1)S(1)}, bf16[4,640,128]{2,1,0:T(8,128)(2,1)S(1)}, u32[]{:S(2)}, u32[]{:S(2)}) collective-permute-start(bf16[4,640,128]{2,1,0:T(8,128)(2,1)S(1)} %pad_maximum_fusion.refs_4_), channel_id=1, source_target_pairs={{0,1},{1,0},{2,3},{3,2},{4,5},{5,4},{6,7},{7,6},{8,9},{9,8},{10,11... | collective-permute-start | bytes 1966088 | tf_op jit(solution)/shard_map/ppermute | solution.py:272
  53.6 7.0 %collective-permute-start.13 = (bf16[4,640,128]{2,1,0:T(8,128)(2,1)S(1)}, bf16[4,640,128]{2,1,0:T(8,128)(2,1)}, u32[]{:S(2)}, u32[]{:S(2)}) collective-permute-start(bf16[4,640,128]{2,1,0:T(8,128)(2,1)S(1)} %collective-permute-done.8.refs_5_), channel_id=1, source_target_pairs={{0,1},{1,0},{2,3},{3,2},{4,5},{5,4},{6,7},{7,6},{8,9},{9,8},{10,11... | collective-permute-start | bytes 1966088 | tf_op jit(solution)/shard_map/ppermute | solution.py:272
  54.6 0.9 copy-start.2
  55.5 0.9 copy-start.4
  56.5 0.9 copy-start.6
  57.4 0.9 copy-start.8
  64.0 5.4 %collective-permute-start.17 = (f32[512]{0:T(512)S(1)}, f32[512]{0:T(512)S(1)}, u32[]{:S(2)}, u32[]{:S(2)}) collective-permute-start(f32[512]{0:T(512)S(1)} %reduce), channel_id=1, source_target_pairs={{0,12},{1,13},{2,14},{3,15},{4,8},{5,9},{6,10},{7,11},{8,4},{9,5},... | collective-permute-start | bytes 6152 | tf_op jit(solution)/shard_map/ppermute | solution.py:272
  66.3 4.5 %collective-permute-start.16 = (f32[512]{0:T(512)S(1)}, f32[512]{0:T(512)S(1)}, u32[]{:S(2)}, u32[]{:S(2)}) collective-permute-start(f32[512]{0:T(512)S(1)} %reduce), channel_id=1, source_target_pairs={{0,8},{1,9},{2,10},{3,11},{4,12},{5,13},{6,14},{7,15},{8,0},{9,1},... | collective-permute-start | bytes 6152 | tf_op jit(solution)/shard_map/ppermute | solution.py:272
  67.4 3.6 %collective-permute-start.15 = (f32[512]{0:T(512)S(1)}, f32[512]{0:T(512)S(1)}, u32[]{:S(2)}, u32[]{:S(2)}) collective-permute-start(f32[512]{0:T(512)S(1)} %reduce), channel_id=1, source_target_pairs={{0,4},{1,5},{2,6},{3,7},{4,0},{5,1},{6,2},{7,3},{8,12},{9,13},{10,... | collective-permute-start | bytes 6152 | tf_op jit(solution)/shard_map/ppermute | solution.py:272
  68.5 17.6 %collective-permute-start.14 = (bf16[512,640]{1,0:T(8,128)(2,1)S(1)}, bf16[512,640]{1,0:T(8,128)(2,1)S(1)}, u32[]{:S(2)}, u32[]{:S(2)}) collective-permute-start(bf16[512,640]{1,0:T(8,128)(2,1)S(1)} %get-tuple-element.71.wide_ref), channel_id=1, source_target_pairs={{0,4},{1,5},{2,6},{3,7},{4,8},{5,9},{6,10},{7,11},{8,12},{9,13},{1... | collective-permute-start | bytes 1966088 | tf_op jit(solution)/shard_map/ppermute | solution.py:275
  72.1 1.8 %collective-permute-start.18 = (bf16[2,160,640]{2,1,0:T(8,128)(2,1)S(1)}, bf16[2,160,640]{2,1,0:T(8,128)(2,1)S(1)}, u32[]{:S(2)}, u32[]{:S(2)}) collective-permute-start(bf16[2,160,640]{2,1,0:T(8,128)(2,1)S(1)} %get-tuple-element.75), channel_id=1, source_target_pairs={{0,1},{1,0},{2,3},{3,2},{4,5},{5,4},{6,7},{7,6},{8,9},{9,8},{10,11... | collective-permute-start | bytes 1228808 | tf_op jit(solution)/shard_map/ppermute | solution.py:272
  74.0 7.2 %collective-permute-start.19 = (bf16[1,160,640]{2,1,0:T(8,128)(2,1)S(1)}, bf16[1,160,640]{2,1,0:T(8,128)(2,1)S(1)}, u32[]{:S(2)}, u32[]{:S(2)}) collective-permute-start(bf16[1,160,640]{2,1,0:T(8,128)(2,1)S(1)} %get-tuple-element.76), channel_id=1, source_target_pairs={{0,2},{1,3},{2,0},{3,1},{4,6},{5,7},{6,4},{7,5},{8,10},{9,11},{10,... | collective-permute-start | bytes 614408 | tf_op jit(solution)/shard_map/ppermute | solution.py:272
  86.9 1.8 %collective-permute-start.20 = (bf16[2,160,640]{2,1,0:T(8,128)(2,1)S(1)}, bf16[2,160,640]{2,1,0:T(8,128)(2,1)S(1)}, u32[]{:S(2)}, u32[]{:S(2)}) collective-permute-start(bf16[2,160,640]{2,1,0:T(8,128)(2,1)S(1)} %get-tuple-element.79), channel_id=1, source_target_pairs={{0,1},{1,0},{2,3},{3,2},{4,5},{5,4},{6,7},{7,6},{8,9},{9,8},{10,11... | collective-permute-start | bytes 1228808 | tf_op jit(solution)/shard_map/ppermute | solution.py:272
  87.0 18.9 %collective-permute-start.21 = (bf16[512,640]{1,0:T(8,128)(2,1)S(1)}, bf16[512,640]{1,0:T(8,128)(2,1)S(1)}, u32[]{:S(2)}, u32[]{:S(2)}) collective-permute-start(bf16[512,640]{1,0:T(8,128)(2,1)S(1)} %collective-permute-done.14.tall_ref.wide_ref), channel_id=1, source_target_pairs={{0,4},{1,5},{2,6},{3,7},{4,8},{5,9},{6,10},{7,11},{8,12},{9,13},{1... | collective-permute-start | bytes 1966088 | tf_op jit(solution)/shard_map/ppermute | solution.py:275
  89.6 1.8 %collective-permute-start.22 = (bf16[2,160,640]{2,1,0:T(8,128)(2,1)S(1)}, bf16[2,160,640]{2,1,0:T(8,128)(2,1)S(1)}, u32[]{:S(2)}, u32[]{:S(2)}) collective-permute-start(bf16[2,160,640]{2,1,0:T(8,128)(2,1)S(1)} %get-tuple-element.84), channel_id=1, source_target_pairs={{0,1},{1,0},{2,3},{3,2},{4,5},{5,4},{6,7},{7,6},{8,9},{9,8},{10,11... | collective-permute-start | bytes 1228808 | tf_op jit(solution)/shard_map/ppermute | solution.py:272
  89.8 7.9 %collective-permute-start.24 = (bf16[1,160,640]{2,1,0:T(8,128)(2,1)S(1)}, bf16[1,160,640]{2,1,0:T(8,128)(2,1)S(1)}, u32[]{:S(2)}, u32[]{:S(2)}) collective-permute-start(bf16[1,160,640]{2,1,0:T(8,128)(2,1)S(1)} %get-tuple-element.86), channel_id=1, source_target_pairs={{0,2},{1,3},{2,0},{3,1},{4,6},{5,7},{6,4},{7,5},{8,10},{9,11},{10,... | collective-permute-start | bytes 614408 | tf_op jit(solution)/shard_map/ppermute | solution.py:272
  91.5 14.4 %collective-permute-start.23 = (bf16[1,160,640]{2,1,0:T(8,128)(2,1)S(1)}, bf16[1,160,640]{2,1,0:T(8,128)(2,1)S(1)}, u32[]{:S(2)}, u32[]{:S(2)}) collective-permute-start(bf16[1,160,640]{2,1,0:T(8,128)(2,1)S(1)} %get-tuple-element.85), channel_id=1, source_target_pairs={{0,2},{1,3},{2,0},{3,1},{4,6},{5,7},{6,4},{7,5},{8,10},{9,11},{10,... | collective-permute-start | bytes 614408 | tf_op jit(solution)/shard_map/ppermute | solution.py:272
  106.7 1.8 %collective-permute-start.26 = (bf16[2,160,640]{2,1,0:T(8,128)(2,1)S(1)}, bf16[2,160,640]{2,1,0:T(8,128)(2,1)S(1)}, u32[]{:S(2)}, u32[]{:S(2)}) collective-permute-start(bf16[2,160,640]{2,1,0:T(8,128)(2,1)S(1)} %get-tuple-element.94), channel_id=1, source_target_pairs={{0,1},{1,0},{2,3},{3,2},{4,5},{5,4},{6,7},{7,6},{8,9},{9,8},{10,11... | collective-permute-start | bytes 1228808 | tf_op jit(solution)/shard_map/ppermute | solution.py:272
  106.9 7.5 %collective-permute-start.25 = (bf16[160,640]{1,0:T(8,128)(2,1)S(1)}, bf16[160,640]{1,0:T(8,128)(2,1)S(1)}, u32[]{:S(2)}, u32[]{:S(2)}) collective-permute-start(bf16[160,640]{1,0:T(8,128)(2,1)S(1)} %fusion), channel_id=1, source_target_pairs={{0,12},{1,13},{2,14},{3,15},{4,0},{5,1},{6,2},{7,3},{8,4},{9,5},{1... | collective-permute-start | bytes 614408 | tf_op jit(solution)/shard_map/ppermute | solution.py:275
  108.6 7.2 %collective-permute-start.27 = (bf16[1,160,640]{2,1,0:T(8,128)(2,1)S(1)}, bf16[1,160,640]{2,1,0:T(8,128)(2,1)S(1)}, u32[]{:S(2)}, u32[]{:S(2)}) collective-permute-start(bf16[1,160,640]{2,1,0:T(8,128)(2,1)S(1)} %get-tuple-element.96), channel_id=1, source_target_pairs={{0,2},{1,3},{2,0},{3,1},{4,6},{5,7},{6,4},{7,5},{8,10},{9,11},{10,... | collective-permute-start | bytes 614408 | tf_op jit(solution)/shard_map/ppermute | solution.py:272

commit v7 on v6

--- a/solution.py
+++ b/solution.py
@@ -140,17 +140,18 @@
     if begun:
         before_ref, refs = refs[0], refs[1:]
         sents, squares_ref = refs[1 : 1 + len(splits)], refs[1 + len(splits)]
-    rest_ref, window = refs[0], refs[-1]
+    rest_ref, window, named_ref = refs[0], refs[-2], refs[-1]
     count = windows[0].shape[0]
     for away in range(OUTER):
         own = pl.ds(pl.multiple_of((outer_ref[0] ^ away) * count, count), count)
         window[own, :] = windows[away][...]
+        named_ref[own, :] = jnp.broadcast_to(names_ref[away : away + 1, :].astype(F32), (band, count)).T
     rows, width = window.shape
-    named = names_ref[...]
-    total = jnp.zeros((rows, 1), F32)
+    named = named_ref[...]
+    total = jnp.zeros((rows, band), F32)
     for p in range(npieces):
         hits = [
-            jnp.broadcast_to((named == bins_ref[p * OUTER + b]).astype(F32), (rows, band)).astype(BF16)
+            (named == bins_ref[p * OUTER + b].astype(F32)).astype(F32).astype(BF16)
             for b in range(OUTER)
         ]
         for at in range(0, width, band):
@@ -167,9 +168,12 @@
                 for (low, high), sent_ref in zip(splits, sents):
                     if low <= at < high:
                         sent_ref[:, at - low : at - low + band] = value.astype(BF16)
-                total = total + jnp.sum(value * value, axis=1, keepdims=True)
+                total = total + value * value
     if begun:
-        squares_ref[...] = total
+        for outer in range(OUTER):
+            squares_ref[outer : outer + 1, :] = jnp.sum(
+                total[outer * count : (outer + 1) * count].T, axis=0, keepdims=True
+            )
 
 
 def resample(outer, bins, names, windows, weights, splits, band, begun=None):
@@ -181,16 +185,22 @@
     sents = tuple(jax.ShapeDtypeStruct((rows, high - low), BF16) for low, high in splits)
     return call(
         functools.partial(rest_kernel, npieces, splits, band, int(last)),
-        (rest, *sents, jax.ShapeDtypeStruct((rows, 1), F32)) if last else rest,
+        (rest, *sents, jax.ShapeDtypeStruct((OUTER, count), F32)) if last else rest,
         [SMEM, SMEM] + [VMEM] * (1 + OUTER + npieces + last),
         (outer, bins, names, *windows, *weights) + ((begun,) if last else ()),
-        [pltpu.VMEM((rows, width), BF16)],
+        [pltpu.VMEM((rows, width), BF16), pltpu.VMEM((rows, band), F32)],
         aliases={3 + OUTER + npieces: 0} if last else None,
     )
 
 
 def scale_kernel(rest_ref, factor_ref, out_ref):
-    out_ref[...] = (rest_ref[...] * factor_ref[...]).astype(BF16)
+    outers, count = factor_ref.shape
+    width = rest_ref.shape[1]
+    for outer in range(outers):
+        own = slice(outer * count, (outer + 1) * count)
+        factor = jnp.broadcast_to(factor_ref[outer : outer + 1, :], (128, count)).T
+        for at in range(0, width, 128):
+            out_ref[own, at : at + 128] = (rest_ref[own, at : at + 128] * factor).astype(BF16)
 
 
 def product_kernel(q_ref, tall_ref, wide_ref, send_ref, keep_ref, value):
@@ -277,8 +287,6 @@
     targets = destination[:, 0]
     table = jnp.concatenate([band_offset[0], targets])
     tables = jnp.stack([table] + [swap(table, away * inner) for away in range(1, OUTER)])
-    by_outer = resample_weight[0].reshape(OUTER, width, band)
-    tables, by_outer = lax.optimization_barrier((tables, by_outer))
     names, offsets = tables[:, nblocks:], tables[:, None, :nblocks]
     bit = 1
     while bit < inner:
@@ -288,6 +296,7 @@
         bit *= 2
     offsets = offsets.reshape(n, nblocks)
 
+    by_outer = resample_weight[0].reshape(OUTER, width, band)
     pieces = [lax.dynamic_index_in_dim(by_outer, outer, 0, keepdims=False)]
     for away in range(1, OUTER):
         theirs = lax.dynamic_index_in_dim(by_outer, outer ^ away, 0, keepdims=False)
@@ -311,37 +320,32 @@
     group_bin = jnp.sum((ends[None, :] <= slot[: places // GROUP, None]).astype(I32), axis=1)
     entries = jnp.minimum(group_bin, n - 1) ^ me
 
-    pieces, smoothed, offsets = lax.optimization_barrier((pieces, smoothed, offsets))
+    chunk = jnp.minimum(offsets // band, nobs // band - 2)
+    turns = (2 * band + chunk * band - offsets) & (2 * band - 1)
+    outer1 = outer.reshape(1)
+    windows = cut_windows(outer1, entries, chunk * band, turns, smoothed, placing, placed, band)
+
+    pieces, windows = lax.optimization_barrier((pieces, windows))
+    arrived = [windows[0]] + [swap(windows[away], away * inner) for away in range(1, OUTER)]
     mixed = jnp.stack(pieces)
     bit = inner // 2
     weights = [mixed, swap(mixed, bit)]
     mine = me ^ (jnp.arange(OUTER, dtype=I32) * inner)
     ids = [mine, mine ^ bit]
-
-    chunk = jnp.minimum(offsets // band, nobs // band - 2)
-    turns = (2 * band + chunk * band - offsets) & (2 * band - 1)
-    outer1 = outer.reshape(1)
-    windows = cut_windows(outer1, entries, chunk * band, turns, smoothed, placing, placed, band)
-    arrived = [windows[0]] + [swap(windows[away], away * inner) for away in range(1, OUTER)]
     weights, arrived = lax.optimization_barrier((weights, arrived))
     while bit > 1:
         bit //= 2
         weights = weights + [swap(piece, bit) for piece in weights]
         ids = ids + [piece ^ bit for piece in ids]
     early, late = jnp.concatenate(ids[:2]), jnp.concatenate(ids[2:])
-    order_of = jnp.arange(OUTER, dtype=I32) ^ outer
-    named = jnp.sum(
-        jnp.where(order_of[:, None, None] == jnp.arange(OUTER, dtype=I32)[None, :, None], names[None], 0), axis=1
-    ).reshape(rows, 1)
-    begun = resample(outer1, early, named, arrived, weights[:2], [(0, width)], band)
-    rest, sent, squares = resample(outer1, late, named, arrived, weights[2:], [(0, width)], band, begun)
-    squares = squares.reshape(rows)
+    begun = resample(outer1, early, names, arrived, weights[:2], [(0, width)], band)
+    rest, sent, squares = resample(outer1, late, names, arrived, weights[2:], [(0, width)], band, begun)
 
     total = squares
     for away in range(1, OUTER):
         total = total + swap(squares, away * inner)
     scale = lax.rsqrt(total / nrest + 1e-06)
-    factor = (scale * scale / (count * n)).reshape(rows, 1)
+    factor = scale * scale / (count * n)
     scaled = call(scale_kernel, jax.ShapeDtypeStruct(rest.shape, BF16), [VMEM, VMEM], (rest, factor))
 
     def reduce(send, held):

time: 118 us -> 107 us (0.907)
  waiting for transfers between devices: 55.1 us -> 48.2 us
  local copies, waits for them, and re-layouts: 7.92 us -> 1.28 us
  starting transfers between devices: 26.3 us -> 30.3 us
    unnamed x18 -> x2, local copies, waits for them, and re-layouts: 6.33 us -> 0.01 us
    ppermute x25, waiting for transfers between devices: 36.9 us -> 31.6 us  [swap(): return lax.ppermute(array, 'spec', [(i, i ^ bit) for i in range(n)])]
    ppermute x25, starting transfers between devices: 25.3 us -> 28.4 us  [swap(): return lax.ppermute(array, 'spec', [(i, i ^ bit) for i in range(n)])]
    ppermute x3, waiting for transfers between devices: 18.3 us -> 16.6 us  [step(): lax.ppermute(array, 'spec', [(i, (i + outers * inner) % n) for i in range...]
  transfers between devices with their start and end apart: 28 -> 28, of which waited for: 17 -> 14; matrix products, arithmetic and copies ran while one was open for 4% -> 4% of each run, Pallas kernels for 14% -> 16%
where the time goes in v7:
time: 107 us
  waiting for transfers between devices  48.2 us (45%)
  starting transfers between devices  30.3 us (28%)
  Pallas kernels  23 us (21%)
  other arithmetic  3.92 us (4%)
  local copies, waits for them, and re-layouts  1.28 us (1%)
    ppermute x25, waiting for transfers between devices, swap(): return lax.ppermute(array, 'spec', [(i, i ^ bit) for i in range(n)])  31.6 us
    ppermute x25, starting transfers between devices, swap(): return lax.ppermute(array, 'spec', [(i, i ^ bit) for i in range(n)])  28.4 us
    pallas_call x14, Pallas kernels, call(): pl.pallas_call(kernel, out_shape=out_shape, in_specs=in_specs, out_specs=...  23 us
    ppermute x3, waiting for transfers between devices, step(): lax.ppermute(array, 'spec', [(i, (i + outers * inner) % n) for i in range...  16.6 us
  transfers between devices with their start and end apart: 28, of which 14 were waited for; matrix products, arithmetic and copies ran while one was open for 4% of the time, Pallas kernels for 16%

profile of v7, /device:TPU:0, one launch (start us, length us, event | category | flops | bytes accessed | tf_op | source)
XLA Modules:
  0.0 107.0 jit_solution(14400796231196905375)
XLA Ops:
  0.0 0.8 pad_add_fusion.3
  0.8 5.0 %collective-permute-start.2 = (s32[148]{0:T(256)S(1)}, s32[148]{0:T(256)S(1)}, u32[]{:S(2)}, u32[]{:S(2)}) collective-permute-start(s32[148]{0:T(256)S(1)} %pad_add_fusion.3), channel_id=1, source_target_pairs={{0,12},{1,13},{2,14},{3,15},{4,8},{5,9},{6,10},{7,11},{8,4},{9,5},... | collective-permute-start | bytes 1784 | tf_op jit(solution)/shard_map/ppermute | solution.py:282
  5.9 0.6 collective-permute-start
  6.5 1.2 %dynamic-slice_bitcast_fusion = (bf16[640,128]{1,0:T(8,128)(2,1)S(1)}, bf16[640,128]{1,0:T(8,128)(2,1)S(1)}, bf16[640,128]{1,0:T(8,128)(2,1)S(1)}, bf16[640,128]{1,0:T(8,128)(2,1)S(1)}) fusion(bf16[4,640,128]{2,1,0:T(8,128)(2,1)} %bitcast.44, s32[]{:T(128)S(6)} %select_n.62, s32[]{:T(128)S(6)} %select_n.61, s32[]{:T(128)S(6)} %select_n.60, s32[]{:T(128)S(6)} %select_n.59), kind=kLoop, calls=%fused_computation.3 | loop fusion | bytes 1310736 | tf_op jit(solution)/shard_map/jit(dynamic_index_in_dim)/squeeze | solution.py:302
  7.7 3.8 %collective-permute-start.5 = (bf16[640,128]{1,0:T(8,128)(2,1)S(1)}, bf16[640,128]{1,0:T(8,128)(2,1)S(1)}, u32[]{:S(2)}, u32[]{:S(2)}) collective-permute-start(bf16[640,128]{1,0:T(8,128)(2,1)S(1)} %get-tuple-element.97), channel_id=1, source_target_pairs={{0,12},{1,13},{2,14},{3,15},{4,8},{5,9},{6,10},{7,11},{8,4},{9,5},... | collective-permute-start | bytes 491528 | tf_op jit(solution)/shard_map/ppermute | solution.py:282
  11.5 0.9 convert_reduce_fusion
  12.4 0.8 convert_reduce_fusion.2
  13.2 0.7 select_reduce_fusion
  14.0 0.1 fusion.1.back_ref
  14.1 0.1 select_reduce_fusion.1
  14.2 0.7 collective-permute-start.3
  14.9 0.1 collective-permute-start.6
  15.0 0.1 convert_reduce_fusion.1
  15.1 1.1 collective-permute-done.6
  16.2 1.7 %collective-permute-start.7 = (s32[4,2,20]{2,0,1:T(4,128)S(1)}, s32[4,2,20]{2,0,1:T(4,128)S(1)}, u32[]{:S(2)}, u32[]{:S(2)}) collective-permute-start(s32[4,2,20]{2,0,1:T(4,128)S(1)} %pad_add_fusion.2), channel_id=1, source_target_pairs={{0,2},{1,3},{2,0},{3,1},{4,6},{5,7},{6,4},{7,5},{8,10},{9,11},{10,... | collective-permute-start | bytes 1928 | tf_op jit(solution)/shard_map/ppermute | solution.py:282
  17.8 7.2 %shard_map.55.smoothed_ref = bf16[128,3968]{1,0:T(8,128)(2,1)S(1)} custom-call(bf16[128,3968]{1,0:T(8,128)(2,1)S(1)} %copy-done, bf16[11,128,3968]{2,1,0:T(8,128)(2,1)} %bitcast.42), custom_call_target="tpu_custom_call" | custom-call | flops 1 | bytes 1 | tf_op jit(solution)/shard_map/pallas_call | solution.py:20
  25.1 5.4 %shard_map.56 = (bf16[128,640]{1,0:T(8,128)(2,1)S(1)}, bf16[128,640]{1,0:T(8,128)(2,1)S(1)}, bf16[128,640]{1,0:T(8,128)(2,1)S(1)}, bf16[128,640]{1,0:T(8,128)(2,1)S(1)}) custom-call(s32[1]{0:T(128)} %bitcast.1.outer_ref, s32[30]{0:T(128)S(1)} %minimum_xor_fusion.bins_ref, s32[16,20]{1,0:T(8,128)S(1)} %get-tuple-element.102.starts_ref, ...), custom_call_target="tpu_custom_call" | custom-call | flops 1 | bytes 1 | tf_op jit(solution)/shard_map/pallas_call | solution.py:20
  30.5 0.1 pad_maximum_fusion.refs_4_
  30.6 0.4 collective-permute-start.8
  31.1 1.4 %collective-permute-start.9 = (bf16[128,640]{1,0:T(8,128)(2,1)S(1)}, bf16[128,640]{1,0:T(8,128)(2,1)S(1)}, u32[]{:S(2)}, u32[]{:S(2)}) collective-permute-start(bf16[128,640]{1,0:T(8,128)(2,1)S(1)} %get-tuple-element.62), channel_id=1, source_target_pairs={{0,4},{1,5},{2,6},{3,7},{4,0},{5,1},{6,2},{7,3},{8,12},{9,13},{10,... | collective-permute-start | bytes 491528 | tf_op jit(solution)/shard_map/ppermute | solution.py:282
  32.4 2.9 %collective-permute-start.10 = (bf16[128,640]{1,0:T(8,128)(2,1)S(1)}, bf16[128,640]{1,0:T(8,128)(2,1)S(1)}, u32[]{:S(2)}, u32[]{:S(2)}) collective-permute-start(bf16[128,640]{1,0:T(8,128)(2,1)S(1)} %get-tuple-element.63), channel_id=1, source_target_pairs={{0,8},{1,9},{2,10},{3,11},{4,12},{5,13},{6,14},{7,15},{8,0},{9,1},... | collective-permute-start | bytes 491528 | tf_op jit(solution)/shard_map/ppermute | solution.py:282
  35.4 0.1 collective-permute-start.11
  35.4 3.8 %collective-permute-done.9.refs_1_ = bf16[128,640]{1,0:T(8,128)(2,1)S(1)} collective-permute-done((bf16[128,640]{1,0:T(8,128)(2,1)S(1)}, bf16[128,640]{1,0:T(8,128)(2,1)S(1)}, u32[]{:S(2)}, u32[]{:S(2)}) %collective-permute-start.9) | collective-permute-done | bytes 163872 | tf_op jit(solution)/shard_map/ppermute | solution.py:282
  39.3 8.2 %collective-permute-done.10.refs_2_ = bf16[128,640]{1,0:T(8,128)(2,1)S(1)} collective-permute-done((bf16[128,640]{1,0:T(8,128)(2,1)S(1)}, bf16[128,640]{1,0:T(8,128)(2,1)S(1)}, u32[]{:S(2)}, u32[]{:S(2)}) %collective-permute-start.10) | collective-permute-done | bytes 163872 | tf_op jit(solution)/shard_map/ppermute | solution.py:282
  47.5 0.5 collective-permute-start.13
  48.0 0.1 pad_add_fusion.4.bins_ref
  48.1 0.1 pad_add_fusion.5.bins_ref
  48.2 0.1 slice.12.names_ref
  48.2 2.2 %shard_map.57.refs_6_ = f32[512,640]{1,0:T(8,128)S(1)} custom-call(s32[1]{0:T(128)} %bitcast.1.outer_ref, s32[8]{0:T(128)S(1)} %pad_add_fusion.5.bins_ref, s32[4,128]{1,0:T(4,128)S(1)} %slice.12.names_ref, bf16[128,640]{1,0:T(8,128)(2,1)S(1)} %get-tuple-element.65.refs_0_, bf16[128,640]{1,0:T(8,128)(2,1)S(1)} %collective-permute-done.9.refs_1_, ...), custom_call_target="tpu_custom_call" | custom-call | flops 1 | bytes 1 | tf_op jit(solution)/shard_map/pallas_call | solution.py:20
  50.5 2.6 %shard_map.58 = (f32[512,640]{1,0:T(8,128)S(1)}, bf16[512,640]{1,0:T(8,128)(2,1)S(1)}, f32[4,128]{1,0:T(4,128)S(1)}) custom-call(s32[1]{0:T(128)} %bitcast.1.outer_ref, s32[8]{0:T(128)S(1)} %pad_add_fusion.4.bins_ref, s32[4,128]{1,0:T(4,128)S(1)} %slice.12.names_ref, ...), custom_call_target="tpu_custom_call", output_to_operand_aliasing={{0}: (9, {})} | custom-call | flops 1 | bytes 1 | tf_op jit(solution)/shard_map/pallas_call | solution.py:20
  53.2 3.4 %collective-permute-start.17 = (f32[4,128]{1,0:T(4,128)S(1)}, f32[4,128]{1,0:T(4,128)S(1)}, u32[]{:S(2)}, u32[]{:S(2)}) collective-permute-start(f32[4,128]{1,0:T(4,128)S(1)} %get-tuple-element.73), channel_id=1, source_target_pairs={{0,12},{1,13},{2,14},{3,15},{4,8},{5,9},{6,10},{7,11},{8,4},{9,5},... | collective-permute-start | bytes 6152 | tf_op jit(solution)/shard_map/ppermute | solution.py:282
  56.6 0.8 collective-permute-start.16
  57.4 0.2 collective-permute-start.15
  57.6 1.8 %collective-permute-start.14 = (bf16[512,640]{1,0:T(8,128)(2,1)S(1)}, bf16[512,640]{1,0:T(8,128)(2,1)S(1)}, u32[]{:S(2)}, u32[]{:S(2)}) collective-permute-start(bf16[512,640]{1,0:T(8,128)(2,1)S(1)} %get-tuple-element.71.wide_ref), channel_id=1, source_target_pairs={{0,4},{1,5},{2,6},{3,7},{4,8},{5,9},{6,10},{7,11},{8,12},{9,13},{1... | collective-permute-start | bytes 1966088 | tf_op jit(solution)/shard_map/ppermute | solution.py:285
  59.5 1.6 %collective-permute-done.16 = f32[4,128]{1,0:T(4,128)S(1)} collective-permute-done((f32[4,128]{1,0:T(4,128)S(1)}, f32[4,128]{1,0:T(4,128)S(1)}, u32[]{:S(2)}, u32[]{:S(2)}) %collective-permute-start.16) | collective-permute-done | bytes 2080 | tf_op jit(solution)/shard_map/ppermute | solution.py:282
  61.1 0.2 shard_map.59.tall_ref.wide_ref
  61.3 0.8 shard_map.60
  62.1 0.1 collective-permute-start.18
  62.2 1.7 %collective-permute-done.18.got_ref = bf16[2,160,640]{2,1,0:T(8,128)(2,1)S(1)} collective-permute-done((bf16[2,160,640]{2,1,0:T(8,128)(2,1)S(1)}, bf16[2,160,640]{2,1,0:T(8,128)(2,1)S(1)}, u32[]{:S(2)}, u32[]{:S(2)}) %collective-permute-start.18) | collective-permute-done | bytes 409632 | tf_op jit(solution)/shard_map/ppermute | solution.py:282
  63.9 0.1 shard_map.61
  64.0 1.5 %collective-permute-start.19 = (bf16[1,160,640]{2,1,0:T(8,128)(2,1)S(1)}, bf16[1,160,640]{2,1,0:T(8,128)(2,1)S(1)}, u32[]{:S(2)}, u32[]{:S(2)}) collective-permute-start(bf16[1,160,640]{2,1,0:T(8,128)(2,1)S(1)} %get-tuple-element.76), channel_id=1, source_target_pairs={{0,2},{1,3},{2,0},{3,1},{4,6},{5,7},{6,4},{7,5},{8,10},{9,11},{10,... | collective-permute-start | bytes 614408 | tf_op jit(solution)/shard_map/ppermute | solution.py:282
  65.5 5.7 %collective-permute-done.19 = bf16[1,160,640]{2,1,0:T(8,128)(2,1)S(1)} collective-permute-done((bf16[1,160,640]{2,1,0:T(8,128)(2,1)S(1)}, bf16[1,160,640]{2,1,0:T(8,128)(2,1)S(1)}, u32[]{:S(2)}, u32[]{:S(2)}) %collective-permute-start.19) | collective-permute-done | bytes 204832 | tf_op jit(solution)/shard_map/ppermute | solution.py:282
  71.2 4.3 %collective-permute-done.14.tall_ref.wide_ref = bf16[512,640]{1,0:T(8,128)(2,1)S(1)} collective-permute-done((bf16[512,640]{1,0:T(8,128)(2,1)S(1)}, bf16[512,640]{1,0:T(8,128)(2,1)S(1)}, u32[]{:S(2)}, u32[]{:S(2)}) %collective-permute-start.14) | collective-permute-done | bytes 655392 | tf_op jit(solution)/shard_map/ppermute | solution.py:285
  75.5 0.8 shard_map.62
  76.3 0.1 collective-permute-start.20
  76.4 0.1 collective-permute-start.21
  76.4 1.7 %collective-permute-done.20.got_ref = bf16[2,160,640]{2,1,0:T(8,128)(2,1)S(1)} collective-permute-done((bf16[2,160,640]{2,1,0:T(8,128)(2,1)S(1)}, bf16[2,160,640]{2,1,0:T(8,128)(2,1)S(1)}, u32[]{:S(2)}, u32[]{:S(2)}) %collective-permute-start.20) | collective-permute-done | bytes 409632 | tf_op jit(solution)/shard_map/ppermute | solution.py:282
  78.1 0.1 shard_map.63
  78.2 0.8 shard_map.64
  79.0 0.2 collective-permute-start.22
  79.2 1.5 %collective-permute-start.24 = (bf16[1,160,640]{2,1,0:T(8,128)(2,1)S(1)}, bf16[1,160,640]{2,1,0:T(8,128)(2,1)S(1)}, u32[]{:S(2)}, u32[]{:S(2)}) collective-permute-start(bf16[1,160,640]{2,1,0:T(8,128)(2,1)S(1)} %get-tuple-element.86), channel_id=1, source_target_pairs={{0,2},{1,3},{2,0},{3,1},{4,6},{5,7},{6,4},{7,5},{8,10},{9,11},{10,... | collective-permute-start | bytes 614408 | tf_op jit(solution)/shard_map/ppermute | solution.py:282
  80.7 0.1 collective-permute-done.22.got_ref
  80.8 0.1 shard_map.65
  80.9 1.6 %collective-permute-start.23 = (bf16[1,160,640]{2,1,0:T(8,128)(2,1)S(1)}, bf16[1,160,640]{2,1,0:T(8,128)(2,1)S(1)}, u32[]{:S(2)}, u32[]{:S(2)}) collective-permute-start(bf16[1,160,640]{2,1,0:T(8,128)(2,1)S(1)} %get-tuple-element.85), channel_id=1, source_target_pairs={{0,2},{1,3},{2,0},{3,1},{4,6},{5,7},{6,4},{7,5},{8,10},{9,11},{10,... | collective-permute-start | bytes 614408 | tf_op jit(solution)/shard_map/ppermute | solution.py:282
  82.5 4.6 %collective-permute-done.24 = bf16[1,160,640]{2,1,0:T(8,128)(2,1)S(1)} collective-permute-done((bf16[1,160,640]{2,1,0:T(8,128)(2,1)S(1)}, bf16[1,160,640]{2,1,0:T(8,128)(2,1)S(1)}, u32[]{:S(2)}, u32[]{:S(2)}) %collective-permute-start.24) | collective-permute-done | bytes 204832 | tf_op jit(solution)/shard_map/ppermute | solution.py:282
  87.1 8.2 %collective-permute-done.21.wide_ref = bf16[512,640]{1,0:T(8,128)(2,1)S(1)} collective-permute-done((bf16[512,640]{1,0:T(8,128)(2,1)S(1)}, bf16[512,640]{1,0:T(8,128)(2,1)S(1)}, u32[]{:S(2)}, u32[]{:S(2)}) %collective-permute-start.21) | collective-permute-done | bytes 655392 | tf_op jit(solution)/shard_map/ppermute | solution.py:285
  95.3 0.8 shard_map.66
  96.1 0.1 collective-permute-start.26
  96.3 1.6 %collective-permute-done.26.got_ref = bf16[2,160,640]{2,1,0:T(8,128)(2,1)S(1)} collective-permute-done((bf16[2,160,640]{2,1,0:T(8,128)(2,1)S(1)}, bf16[2,160,640]{2,1,0:T(8,128)(2,1)S(1)}, u32[]{:S(2)}, u32[]{:S(2)}) %collective-permute-start.26) | collective-permute-done | bytes 409632 | tf_op jit(solution)/shard_map/ppermute | solution.py:282
  97.9 0.1 shard_map.67
  98.0 1.6 %collective-permute-start.27 = (bf16[1,160,640]{2,1,0:T(8,128)(2,1)S(1)}, bf16[1,160,640]{2,1,0:T(8,128)(2,1)S(1)}, u32[]{:S(2)}, u32[]{:S(2)}) collective-permute-start(bf16[1,160,640]{2,1,0:T(8,128)(2,1)S(1)} %get-tuple-element.96), channel_id=1, source_target_pairs={{0,2},{1,3},{2,0},{3,1},{4,6},{5,7},{6,4},{7,5},{8,10},{9,11},{10,... | collective-permute-start | bytes 614408 | tf_op jit(solution)/shard_map/ppermute | solution.py:282
  99.6 4.2 %collective-permute-done.25.refs_1_ = bf16[160,640]{1,0:T(8,128)(2,1)S(1)} collective-permute-done((bf16[160,640]{1,0:T(8,128)(2,1)S(1)}, bf16[160,640]{1,0:T(8,128)(2,1)S(1)}, u32[]{:S(2)}, u32[]{:S(2)}) %collective-permute-start.25) | collective-permute-done | bytes 204832 | tf_op jit(solution)/shard_map/ppermute | solution.py:285
  103.8 1.4 %collective-permute-done.27 = bf16[1,160,640]{2,1,0:T(8,128)(2,1)S(1)} collective-permute-done((bf16[1,160,640]{2,1,0:T(8,128)(2,1)S(1)}, bf16[1,160,640]{2,1,0:T(8,128)(2,1)S(1)}, u32[]{:S(2)}, u32[]{:S(2)}) %collective-permute-start.27) | collective-permute-done | bytes 204832 | tf_op jit(solution)/shard_map/ppermute | solution.py:282
  105.2 1.8 %shard_map.68 = f32[160,2560]{1,0:T(8,128)} custom-call(s32[4]{0:T(128)S(1)} %and_select_fusion.1.refs_0_, bf16[160,640]{1,0:T(8,128)(2,1)S(1)} %collective-permute-done.25.refs_1_, f32[160,640]{1,0:T(8,128)S(1)} %bitcast.36, bf16[160,640]{1,0:T(8,128)(2,1)S(1)} %bitcast.39, f32[160,640]{1,0:T(8,128)S(1)} %bitcast.37, bf16[160,640]{1,0:T(8,128)(2,1)S(1)} %bitcast.40, ...), custom_call_target="tpu_custom_call" | custom-call | flops 1 | bytes 1 | tf_op jit(solution)/shard_map/pallas_call | solution.py:20
  (37 shorter events, 0.3 us)
Async XLA Ops:
  0.0 17.8 %copy-start = (bf16[128,3968]{1,0:T(8,128)(2,1)S(1)}, bf16[128,3968]{1,0:T(8,128)(2,1)}, u32[]{:S(2)}) copy-start(bf16[128,3968]{1,0:T(8,128)(2,1)} %flux_ref) | copy-start | bytes 3047428
  0.8 13.4 %collective-permute-start.2 = (s32[148]{0:T(256)S(1)}, s32[148]{0:T(256)S(1)}, u32[]{:S(2)}, u32[]{:S(2)}) collective-permute-start(s32[148]{0:T(256)S(1)} %pad_add_fusion.3), channel_id=1, source_target_pairs={{0,12},{1,13},{2,14},{3,15},{4,8},{5,9},{6,10},{7,11},{8,4},{9,5},... | collective-permute-start | bytes 1784 | tf_op jit(solution)/shard_map/ppermute | solution.py:282
  5.9 9.0 %collective-permute-start.1 = (s32[148]{0:T(256)S(1)}, s32[148]{0:T(256)S(1)}, u32[]{:S(2)}, u32[]{:S(2)}) collective-permute-start(s32[148]{0:T(256)S(1)} %pad_add_fusion.3), channel_id=1, source_target_pairs={{0,8},{1,9},{2,10},{3,11},{4,12},{5,13},{6,14},{7,15},{8,0},{9,1},... | collective-permute-start | bytes 1784 | tf_op jit(solution)/shard_map/ppermute | solution.py:282
  5.9 9.0 %collective-permute-start = (s32[148]{0:T(256)S(1)}, s32[148]{0:T(256)S(1)}, u32[]{:S(2)}, u32[]{:S(2)}) collective-permute-start(s32[148]{0:T(256)S(1)} %pad_add_fusion.3), channel_id=1, source_target_pairs={{0,4},{1,5},{2,6},{3,7},{4,0},{5,1},{6,2},{7,3},{8,12},{9,13},{10,... | collective-permute-start | bytes 1784 | tf_op jit(solution)/shard_map/ppermute | solution.py:282
  7.7 22.8 %collective-permute-start.5 = (bf16[640,128]{1,0:T(8,128)(2,1)S(1)}, bf16[640,128]{1,0:T(8,128)(2,1)S(1)}, u32[]{:S(2)}, u32[]{:S(2)}) collective-permute-start(bf16[640,128]{1,0:T(8,128)(2,1)S(1)} %get-tuple-element.97), channel_id=1, source_target_pairs={{0,12},{1,13},{2,14},{3,15},{4,8},{5,9},{6,10},{7,11},{8,4},{9,5},... | collective-permute-start | bytes 491528 | tf_op jit(solution)/shard_map/ppermute | solution.py:282
  11.5 19.0 %collective-permute-start.4 = (bf16[640,128]{1,0:T(8,128)(2,1)S(1)}, bf16[640,128]{1,0:T(8,128)(2,1)S(1)}, u32[]{:S(2)}, u32[]{:S(2)}) collective-permute-start(bf16[640,128]{1,0:T(8,128)(2,1)S(1)} %get-tuple-element.98), channel_id=1, source_target_pairs={{0,8},{1,9},{2,10},{3,11},{4,12},{5,13},{6,14},{7,15},{8,0},{9,1},... | collective-permute-start | bytes 491528 | tf_op jit(solution)/shard_map/ppermute | solution.py:282
  14.2 16.3 %collective-permute-start.3 = (bf16[640,128]{1,0:T(8,128)(2,1)S(1)}, bf16[640,128]{1,0:T(8,128)(2,1)S(1)}, u32[]{:S(2)}, u32[]{:S(2)}) collective-permute-start(bf16[640,128]{1,0:T(8,128)(2,1)S(1)} %get-tuple-element.99), channel_id=1, source_target_pairs={{0,4},{1,5},{2,6},{3,7},{4,0},{5,1},{6,2},{7,3},{8,12},{9,13},{10,... | collective-permute-start | bytes 491528 | tf_op jit(solution)/shard_map/ppermute | solution.py:282
  14.9 1.2 %collective-permute-start.6 = (s32[4,1,20]{2,0,1:T(4,128)S(1)}, s32[4,1,20]{2,0,1:T(4,128)S(1)}, u32[]{:S(2)}, u32[]{:S(2)}) collective-permute-start(s32[4,1,20]{2,0,1:T(4,128)S(1)} %slice_bitcast_fusion), channel_id=1, source_target_pairs={{0,1},{1,0},{2,3},{3,2},{4,5},{5,4},{6,7},{7,6},{8,9},{9,8},{10,11... | collective-permute-start | bytes 968 | tf_op jit(solution)/shard_map/ppermute | solution.py:282
  16.2 8.9 %collective-permute-start.7 = (s32[4,2,20]{2,0,1:T(4,128)S(1)}, s32[4,2,20]{2,0,1:T(4,128)S(1)}, u32[]{:S(2)}, u32[]{:S(2)}) collective-permute-start(s32[4,2,20]{2,0,1:T(4,128)S(1)} %pad_add_fusion.2), channel_id=1, source_target_pairs={{0,2},{1,3},{2,0},{3,1},{4,6},{5,7},{6,4},{7,5},{8,10},{9,11},{10,... | collective-permute-start | bytes 1928 | tf_op jit(solution)/shard_map/ppermute | solution.py:282
  30.6 16.9 %collective-permute-start.8 = (bf16[4,640,128]{2,1,0:T(8,128)(2,1)S(1)}, bf16[4,640,128]{2,1,0:T(8,128)(2,1)S(1)}, u32[]{:S(2)}, u32[]{:S(2)}) collective-permute-start(bf16[4,640,128]{2,1,0:T(8,128)(2,1)S(1)} %pad_maximum_fusion.refs_4_), channel_id=1, source_target_pairs={{0,2},{1,3},{2,0},{3,1},{4,6},{5,7},{6,4},{7,5},{8,10},{9,11},{10,... | collective-permute-start | bytes 1966088 | tf_op jit(solution)/shard_map/ppermute | solution.py:282
  31.1 8.2 %collective-permute-start.9 = (bf16[128,640]{1,0:T(8,128)(2,1)S(1)}, bf16[128,640]{1,0:T(8,128)(2,1)S(1)}, u32[]{:S(2)}, u32[]{:S(2)}) collective-permute-start(bf16[128,640]{1,0:T(8,128)(2,1)S(1)} %get-tuple-element.62), channel_id=1, source_target_pairs={{0,4},{1,5},{2,6},{3,7},{4,0},{5,1},{6,2},{7,3},{8,12},{9,13},{10,... | collective-permute-start | bytes 491528 | tf_op jit(solution)/shard_map/ppermute | solution.py:282
  32.4 15.0 %collective-permute-start.10 = (bf16[128,640]{1,0:T(8,128)(2,1)S(1)}, bf16[128,640]{1,0:T(8,128)(2,1)S(1)}, u32[]{:S(2)}, u32[]{:S(2)}) collective-permute-start(bf16[128,640]{1,0:T(8,128)(2,1)S(1)} %get-tuple-element.63), channel_id=1, source_target_pairs={{0,8},{1,9},{2,10},{3,11},{4,12},{5,13},{6,14},{7,15},{8,0},{9,1},... | collective-permute-start | bytes 491528 | tf_op jit(solution)/shard_map/ppermute | solution.py:282
  35.4 12.1 %collective-permute-start.11 = (bf16[128,640]{1,0:T(8,128)(2,1)S(1)}, bf16[128,640]{1,0:T(8,128)(2,1)S(1)}, u32[]{:S(2)}, u32[]{:S(2)}) collective-permute-start(bf16[128,640]{1,0:T(8,128)(2,1)S(1)} %get-tuple-element.64), channel_id=1, source_target_pairs={{0,12},{1,13},{2,14},{3,15},{4,8},{5,9},{6,10},{7,11},{8,4},{9,5},... | collective-permute-start | bytes 491528 | tf_op jit(solution)/shard_map/ppermute | solution.py:282
  47.5 3.0 %collective-permute-start.12 = (bf16[4,640,128]{2,1,0:T(8,128)(2,1)S(1)}, bf16[4,640,128]{2,1,0:T(8,128)(2,1)S(1)}, u32[]{:S(2)}, u32[]{:S(2)}) collective-permute-start(bf16[4,640,128]{2,1,0:T(8,128)(2,1)S(1)} %pad_maximum_fusion.refs_4_), channel_id=1, source_target_pairs={{0,1},{1,0},{2,3},{3,2},{4,5},{5,4},{6,7},{7,6},{8,9},{9,8},{10,11... | collective-permute-start | bytes 1966088 | tf_op jit(solution)/shard_map/ppermute | solution.py:282
  47.5 3.0 %collective-permute-start.13 = (bf16[4,640,128]{2,1,0:T(8,128)(2,1)S(1)}, bf16[4,640,128]{2,1,0:T(8,128)(2,1)S(1)}, u32[]{:S(2)}, u32[]{:S(2)}) collective-permute-start(bf16[4,640,128]{2,1,0:T(8,128)(2,1)S(1)} %collective-permute-done.8.refs_5_), channel_id=1, source_target_pairs={{0,1},{1,0},{2,3},{3,2},{4,5},{5,4},{6,7},{7,6},{8,9},{9,8},{10,11... | collective-permute-start | bytes 1966088 | tf_op jit(solution)/shard_map/ppermute | solution.py:282
  53.2 6.3 %collective-permute-start.17 = (f32[4,128]{1,0:T(4,128)S(1)}, f32[4,128]{1,0:T(4,128)S(1)}, u32[]{:S(2)}, u32[]{:S(2)}) collective-permute-start(f32[4,128]{1,0:T(4,128)S(1)} %get-tuple-element.73), channel_id=1, source_target_pairs={{0,12},{1,13},{2,14},{3,15},{4,8},{5,9},{6,10},{7,11},{8,4},{9,5},... | collective-permute-start | bytes 6152 | tf_op jit(solution)/shard_map/ppermute | solution.py:282
  56.6 4.5 %collective-permute-start.16 = (f32[4,128]{1,0:T(4,128)S(1)}, f32[4,128]{1,0:T(4,128)S(1)}, u32[]{:S(2)}, u32[]{:S(2)}) collective-permute-start(f32[4,128]{1,0:T(4,128)S(1)} %get-tuple-element.73), channel_id=1, source_target_pairs={{0,8},{1,9},{2,10},{3,11},{4,12},{5,13},{6,14},{7,15},{8,0},{9,1},... | collective-permute-start | bytes 6152 | tf_op jit(solution)/shard_map/ppermute | solution.py:282
  57.4 3.7 %collective-permute-start.15 = (f32[4,128]{1,0:T(4,128)S(1)}, f32[4,128]{1,0:T(4,128)S(1)}, u32[]{:S(2)}, u32[]{:S(2)}) collective-permute-start(f32[4,128]{1,0:T(4,128)S(1)} %get-tuple-element.73), channel_id=1, source_target_pairs={{0,4},{1,5},{2,6},{3,7},{4,0},{5,1},{6,2},{7,3},{8,12},{9,13},{10,... | collective-permute-start | bytes 6152 | tf_op jit(solution)/shard_map/ppermute | solution.py:282
  57.6 17.8 %collective-permute-start.14 = (bf16[512,640]{1,0:T(8,128)(2,1)S(1)}, bf16[512,640]{1,0:T(8,128)(2,1)S(1)}, u32[]{:S(2)}, u32[]{:S(2)}) collective-permute-start(bf16[512,640]{1,0:T(8,128)(2,1)S(1)} %get-tuple-element.71.wide_ref), channel_id=1, source_target_pairs={{0,4},{1,5},{2,6},{3,7},{4,8},{5,9},{6,10},{7,11},{8,12},{9,13},{1... | collective-permute-start | bytes 1966088 | tf_op jit(solution)/shard_map/ppermute | solution.py:285
  62.1 1.8 %collective-permute-start.18 = (bf16[2,160,640]{2,1,0:T(8,128)(2,1)S(1)}, bf16[2,160,640]{2,1,0:T(8,128)(2,1)S(1)}, u32[]{:S(2)}, u32[]{:S(2)}) collective-permute-start(bf16[2,160,640]{2,1,0:T(8,128)(2,1)S(1)} %get-tuple-element.75), channel_id=1, source_target_pairs={{0,1},{1,0},{2,3},{3,2},{4,5},{5,4},{6,7},{7,6},{8,9},{9,8},{10,11... | collective-permute-start | bytes 1228808 | tf_op jit(solution)/shard_map/ppermute | solution.py:282
  64.0 7.2 %collective-permute-start.19 = (bf16[1,160,640]{2,1,0:T(8,128)(2,1)S(1)}, bf16[1,160,640]{2,1,0:T(8,128)(2,1)S(1)}, u32[]{:S(2)}, u32[]{:S(2)}) collective-permute-start(bf16[1,160,640]{2,1,0:T(8,128)(2,1)S(1)} %get-tuple-element.76), channel_id=1, source_target_pairs={{0,2},{1,3},{2,0},{3,1},{4,6},{5,7},{6,4},{7,5},{8,10},{9,11},{10,... | collective-permute-start | bytes 614408 | tf_op jit(solution)/shard_map/ppermute | solution.py:282
  76.3 1.8 %collective-permute-start.20 = (bf16[2,160,640]{2,1,0:T(8,128)(2,1)S(1)}, bf16[2,160,640]{2,1,0:T(8,128)(2,1)S(1)}, u32[]{:S(2)}, u32[]{:S(2)}) collective-permute-start(bf16[2,160,640]{2,1,0:T(8,128)(2,1)S(1)} %get-tuple-element.79), channel_id=1, source_target_pairs={{0,1},{1,0},{2,3},{3,2},{4,5},{5,4},{6,7},{7,6},{8,9},{9,8},{10,11... | collective-permute-start | bytes 1228808 | tf_op jit(solution)/shard_map/ppermute | solution.py:282
  76.4 18.9 %collective-permute-start.21 = (bf16[512,640]{1,0:T(8,128)(2,1)S(1)}, bf16[512,640]{1,0:T(8,128)(2,1)S(1)}, u32[]{:S(2)}, u32[]{:S(2)}) collective-permute-start(bf16[512,640]{1,0:T(8,128)(2,1)S(1)} %collective-permute-done.14.tall_ref.wide_ref), channel_id=1, source_target_pairs={{0,4},{1,5},{2,6},{3,7},{4,8},{5,9},{6,10},{7,11},{8,12},{9,13},{1... | collective-permute-start | bytes 1966088 | tf_op jit(solution)/shard_map/ppermute | solution.py:285
  79.0 1.8 %collective-permute-start.22 = (bf16[2,160,640]{2,1,0:T(8,128)(2,1)S(1)}, bf16[2,160,640]{2,1,0:T(8,128)(2,1)S(1)}, u32[]{:S(2)}, u32[]{:S(2)}) collective-permute-start(bf16[2,160,640]{2,1,0:T(8,128)(2,1)S(1)} %get-tuple-element.84), channel_id=1, source_target_pairs={{0,1},{1,0},{2,3},{3,2},{4,5},{5,4},{6,7},{7,6},{8,9},{9,8},{10,11... | collective-permute-start | bytes 1228808 | tf_op jit(solution)/shard_map/ppermute | solution.py:282
  79.2 7.9 %collective-permute-start.24 = (bf16[1,160,640]{2,1,0:T(8,128)(2,1)S(1)}, bf16[1,160,640]{2,1,0:T(8,128)(2,1)S(1)}, u32[]{:S(2)}, u32[]{:S(2)}) collective-permute-start(bf16[1,160,640]{2,1,0:T(8,128)(2,1)S(1)} %get-tuple-element.86), channel_id=1, source_target_pairs={{0,2},{1,3},{2,0},{3,1},{4,6},{5,7},{6,4},{7,5},{8,10},{9,11},{10,... | collective-permute-start | bytes 614408 | tf_op jit(solution)/shard_map/ppermute | solution.py:282
  80.9 14.4 %collective-permute-start.23 = (bf16[1,160,640]{2,1,0:T(8,128)(2,1)S(1)}, bf16[1,160,640]{2,1,0:T(8,128)(2,1)S(1)}, u32[]{:S(2)}, u32[]{:S(2)}) collective-permute-start(bf16[1,160,640]{2,1,0:T(8,128)(2,1)S(1)} %get-tuple-element.85), channel_id=1, source_target_pairs={{0,2},{1,3},{2,0},{3,1},{4,6},{5,7},{6,4},{7,5},{8,10},{9,11},{10,... | collective-permute-start | bytes 614408 | tf_op jit(solution)/shard_map/ppermute | solution.py:282
  96.1 1.8 %collective-permute-start.26 = (bf16[2,160,640]{2,1,0:T(8,128)(2,1)S(1)}, bf16[2,160,640]{2,1,0:T(8,128)(2,1)S(1)}, u32[]{:S(2)}, u32[]{:S(2)}) collective-permute-start(bf16[2,160,640]{2,1,0:T(8,128)(2,1)S(1)} %get-tuple-element.94), channel_id=1, source_target_pairs={{0,1},{1,0},{2,3},{3,2},{4,5},{5,4},{6,7},{7,6},{8,9},{9,8},{10,11... | collective-permute-start | bytes 1228808 | tf_op jit(solution)/shard_map/ppermute | solution.py:282
  96.3 7.5 %collective-permute-start.25 = (bf16[160,640]{1,0:T(8,128)(2,1)S(1)}, bf16[160,640]{1,0:T(8,128)(2,1)S(1)}, u32[]{:S(2)}, u32[]{:S(2)}) collective-permute-start(bf16[160,640]{1,0:T(8,128)(2,1)S(1)} %fusion), channel_id=1, source_target_pairs={{0,12},{1,13},{2,14},{3,15},{4,0},{5,1},{6,2},{7,3},{8,4},{9,5},{1... | collective-permute-start | bytes 614408 | tf_op jit(solution)/shard_map/ppermute | solution.py:285
  98.0 7.2 %collective-permute-start.27 = (bf16[1,160,640]{2,1,0:T(8,128)(2,1)S(1)}, bf16[1,160,640]{2,1,0:T(8,128)(2,1)S(1)}, u32[]{:S(2)}, u32[]{:S(2)}) collective-permute-start(bf16[1,160,640]{2,1,0:T(8,128)(2,1)S(1)} %get-tuple-element.96), channel_id=1, source_target_pairs={{0,2},{1,3},{2,0},{3,1},{4,6},{5,7},{6,4},{7,5},{8,10},{9,11},{10,... | collective-permute-start | bytes 614408 | tf_op jit(solution)/shard_map/ppermute | solution.py:282

commit v8 on v7

--- a/solution.py
+++ b/solution.py
@@ -16,7 +16,7 @@
 BF16, F32, I32 = jnp.bfloat16, jnp.float32, jnp.int32
 
 
-def call(kernel, out_shape, in_specs, args, scratch=(), aliases=None, limit=12 * 1024 * 1024):
+def call(kernel, out_shape, in_specs, args, scratch=(), aliases=None, limit=12 * 1024 * 1024, moved=1):
     return pl.pallas_call(
         kernel,
         out_shape=out_shape,
@@ -25,7 +25,7 @@
         scratch_shapes=scratch,
         input_output_aliases=aliases or {},
         compiler_params=pltpu.CompilerParams(vmem_limit_bytes=limit),
-        cost_estimate=pl.CostEstimate(flops=1, bytes_accessed=1, transcendentals=0),
+        cost_estimate=pl.CostEstimate(flops=1, bytes_accessed=moved, transcendentals=0),
     )(*args)
 
 
@@ -33,33 +33,33 @@
     rows, nobs = flux.shape
     taps = resolution.shape[0]
     tiles = rows // tall
-
-    def copies(tile):
-        own = pl.ds(pl.multiple_of(tile * tall, tall), tall)
-        return (
-            pltpu.make_async_copy(flux_ref.at[own], flux.at[own], sem.at[0, tile]),
-            pltpu.make_async_copy(resolution_ref.at[:, own], resolution.at[:, own], sem.at[1, tile]),
-        )
-
-    ahead = min(3, tiles)
+    ahead = min(2, tiles)
+
+    def own_rows(tile):
+        return pl.ds(pl.multiple_of(tile * tall, tall), tall)
+
+    def fetch(tile):
+        own = own_rows(tile)
+        pltpu.make_async_copy(flux_ref.at[own], flux.at[own], sem.at[0, tile]).start()
+        for tap in range(taps):
+            pltpu.make_async_copy(resolution_ref.at[tap, own], resolution.at[tap, own], sem.at[1, tile]).start()
+
     for tile in range(ahead):
-        for copy in copies(tile):
-            copy.start()
+        fetch(tile)
     edge = jnp.zeros((tall, reach), F32)
     padded[:, :reach] = edge
     padded[:, reach + nobs :] = edge
     step = 256
 
     def one_tile(tile, carry):
-        for copy in copies(tile):
-            copy.wait()
+        own = own_rows(tile)
+        pltpu.make_async_copy(flux_ref.at[own], flux.at[own], sem.at[0, tile]).wait()
+        pltpu.make_async_copy(resolution_ref.at[:, own], resolution.at[:, own], sem.at[1, tile]).wait()
 
         @pl.when(tile + ahead < tiles)
         def _():
-            for copy in copies(tile + ahead):
-                copy.start()
-
-        own = pl.ds(pl.multiple_of(tile * tall, tall), tall)
+            fetch(tile + ahead)
+
         padded[:, reach : reach + nobs] = flux[own, :].astype(F32)
         for start in range(0, nobs, step):
             stop = min(nobs, start + step)
@@ -92,7 +92,40 @@
     )
 
 
-def cut_kernel(per, band, unroll, outer_ref, bins_ref, starts_ref, turns_ref, smoothed_ref, placing_ref, back_ref, *refs):
+def plan_kernel(owners, targets_ref, placing_ref, groups_ref):
+    count = targets_ref.shape[1]
+    across = targets_ref[...].astype(F32)
+    square = (count, count)
+    row = lax.broadcasted_iota(I32, square, 0).astype(F32)
+    lane = lax.broadcasted_iota(I32, square, 1).astype(F32)
+    target = jnp.broadcast_to(across, square)
+    down = target.T
+    rank = jnp.sum(jnp.where((down == target) & (row < lane), 1.0, 0.0), axis=0, keepdims=True)
+    filled = jnp.sum(jnp.where(down == lane, 1.0, 0.0), axis=0, keepdims=True)
+    amount = jnp.floor((filled + (GROUP - 1)) * (1.0 / GROUP))
+    amounts = jnp.broadcast_to(amount, square)
+    before = jnp.sum(jnp.where(row < target, amounts.T, 0.0), axis=0, keepdims=True)
+    position = before * GROUP + rank
+    slot = lax.broadcasted_iota(I32, placing_ref.shape, 0).astype(F32)
+    placing_ref[...] = jnp.where(slot == position, 1.0, 0.0).astype(BF16)
+    ends = jnp.sum(jnp.where(lane <= row, amounts, 0.0), axis=1, keepdims=True)
+    owner = jnp.sum(jnp.where((ends <= lane) & (row < owners - 1), 1.0, 0.0), axis=0, keepdims=True)
+    used = jnp.sum(amount, axis=1, keepdims=True)
+    groups_ref[...] = jnp.concatenate([owner, jnp.broadcast_to(used, owner.shape)], axis=0).astype(I32)
+
+
+def plan(targets, owners, places):
+    count = targets.shape[1]
+    return call(
+        functools.partial(plan_kernel, owners),
+        (jax.ShapeDtypeStruct((places, count), BF16), jax.ShapeDtypeStruct((2, count), I32)),
+        [VMEM],
+        (targets,),
+        moved=24 * 1024 * 1024,
+    )
+
+
+def cut_kernel(per, band, unroll, me_ref, groups_ref, starts_ref, turns_ref, smoothed_ref, placing_ref, *refs):
     outs, (placed, cut) = refs[:OUTER], refs[OUTER:]
     placed[...] = jnp.dot(placing_ref[...], smoothed_ref[...], preferred_element_type=F32)
 
@@ -100,9 +133,9 @@
         for i in range(unroll):
             group = step * unroll + i
             rows = pl.ds(pl.multiple_of(group * GROUP, GROUP), GROUP)
-            entry = bins_ref[group]
+            entry = groups_ref[0, group] ^ me_ref[0]
             for away in range(OUTER):
-                first = (outer_ref[0] ^ away) * per
+                first = (me_ref[1] ^ away) * per
                 for j in range(per):
                     start = pl.multiple_of(starts_ref[entry, first + j], band)
                     wide = placed[rows, pl.ds(start, 2 * band)]
@@ -111,24 +144,34 @@
                     cut[rows, at : at + band] = turned[:, :band]
         return carry
 
-    lax.fori_loop(0, placed.shape[0] // GROUP // unroll, some_groups, 0)
+    def clear_groups(step, carry):
+        rows = pl.ds(pl.multiple_of(step * unroll * GROUP, unroll * GROUP), unroll * GROUP)
+        cut[rows, :] = jnp.zeros((unroll * GROUP, cut.shape[1]), F32)
+        return carry
+
+    steps = placed.shape[0] // GROUP // unroll
+    done = jnp.minimum((groups_ref[1, 0] + unroll - 1) // unroll, steps)
+    lax.fori_loop(0, done, some_groups, 0)
+    lax.fori_loop(done, steps, clear_groups, 0)
     width = per * band
     for away in range(OUTER):
         part = cut[:, away * width : (away + 1) * width].astype(BF16)
-        outs[away][...] = jnp.dot(back_ref[...], part, preferred_element_type=F32).astype(BF16)
-
-
-def cut_windows(outer, bins, starts, turns, smoothed, placing, back, band):
+        outs[away][...] = lax.dot_general(
+            placing_ref[...], part, (((0,), (0,)), ((), ())), preferred_element_type=F32
+        ).astype(BF16)
+
+
+def cut_windows(me, groups, starts, turns, smoothed, placing, band):
     per = starts.shape[1] // OUTER
-    rows, places = back.shape
+    places, rows = placing.shape
     nobs = smoothed.shape[1]
     width = per * band
     unroll = max(k for k in range(1, 7) if places // GROUP % k == 0)
     return call(
         functools.partial(cut_kernel, per, band, unroll),
         (jax.ShapeDtypeStruct((rows, width), BF16),) * OUTER,
-        [SMEM] * 4 + [VMEM] * 3,
-        (outer, bins, starts, turns, smoothed, placing, back),
+        [SMEM] * 4 + [VMEM] * 2,
+        (me, groups, starts, turns, smoothed, placing),
         [pltpu.VMEM((places, nobs), F32), pltpu.VMEM((places, OUTER * width), F32)],
         limit=max(12 * 1024 * 1024, places * (nobs + OUTER * width) * 6),
     )
@@ -244,25 +287,34 @@
     )
 
 
-def place_kernel(width, *refs):
-    at_ref, mirrored_ref, out_ref = refs[0], refs[1], refs[-1]
-    for slot in range(OUTER):
+def place_kernel(slots, begun, at_ref, *refs):
+    parts = refs[: 2 * len(slots)]
+    out_ref, staged, sem = refs[-3:]
+    width = staged.shape[2]
+    copies = []
+    for i, slot in enumerate(slots):
+        held, got = parts[2 * i], parts[2 * i + 1]
+        staged[i] = held[...].astype(F32) + got[...].astype(F32)
         columns = pl.ds(pl.multiple_of(at_ref[slot] * width, 128), width)
-        if slot == OUTER - 1:
-            out_ref[:, columns] = mirrored_ref[...].astype(F32)
-        else:
-            held, got = refs[2 + 2 * slot], refs[3 + 2 * slot]
-            out_ref[:, columns] = held[...] + got[...].astype(F32)
-
-
-def place(at, mirrored, pairs):
-    share, width = mirrored.shape
-    return call(
-        functools.partial(place_kernel, width),
-        jax.ShapeDtypeStruct((share, OUTER * width), F32),
-        [SMEM] + [VMEM] * (1 + 2 * len(pairs)),
-        (at, mirrored, *[array for pair in pairs for array in pair]),
-    )
+        copies.append(pltpu.make_async_copy(staged.at[i], out_ref.at[:, columns], sem.at[i]))
+        copies[-1].start()
+    for copy in copies:
+        copy.wait()
+
+
+def place(at, slots, pairs, begun=None):
+    share, width = pairs[0][0].shape
+    last = begun is not None
+    return pl.pallas_call(
+        functools.partial(place_kernel, slots, last),
+        out_shape=jax.ShapeDtypeStruct((share, OUTER * width), F32),
+        in_specs=[SMEM] + [VMEM] * (2 * len(pairs)) + [ANY] * last,
+        out_specs=ANY,
+        scratch_shapes=[pltpu.VMEM((len(pairs), share, width), F32), pltpu.SemaphoreType.DMA((len(pairs),))],
+        input_output_aliases={1 + 2 * len(pairs): 0} if last else {},
+        compiler_params=pltpu.CompilerParams(vmem_limit_bytes=12 * 1024 * 1024),
+        cost_estimate=pl.CostEstimate(flops=1, bytes_accessed=1, transcendentals=0),
+    )(at, *[array for pair in pairs for array in pair], *([begun] if last else []))
 
 
 def local(flux, resolution, destination, resample_weight, band_offset):
@@ -304,26 +356,13 @@
 
     smoothed = smooth(flux, jnp.transpose(resolution, (1, 0, 2)))
 
-    order = jnp.arange(count, dtype=I32)
-    which = jnp.arange(n, dtype=I32)
-    same = (targets[:, None] == targets[None, :]) & (order[:, None] > order[None, :])
-    rank = jnp.sum(same.astype(I32), axis=1)
-    filled = jnp.sum((targets[:, None] == which[None, :]).astype(I32), axis=0)
-    amount = (filled + GROUP - 1) // GROUP
-    before = jnp.sum(jnp.where(which[None, :] < targets[:, None], amount[None, :], 0), axis=1)
-    position = before * GROUP + rank
     places = -(-(count + n * (GROUP - 1)) // (2 * GROUP)) * 2 * GROUP
-    slot = jnp.arange(places, dtype=I32)
-    placing = (slot[:, None] == position[None, :]).astype(BF16)
-    placed = (position[:, None] == slot[None, :]).astype(BF16)
-    ends = jnp.sum(jnp.where(which[:, None] <= which[None, :], amount[:, None], 0), axis=0)
-    group_bin = jnp.sum((ends[None, :] <= slot[: places // GROUP, None]).astype(I32), axis=1)
-    entries = jnp.minimum(group_bin, n - 1) ^ me
+    placing, group_bins = plan(targets.reshape(1, count), n, places)
 
     chunk = jnp.minimum(offsets // band, nobs // band - 2)
     turns = (2 * band + chunk * band - offsets) & (2 * band - 1)
     outer1 = outer.reshape(1)
-    windows = cut_windows(outer1, entries, chunk * band, turns, smoothed, placing, placed, band)
+    windows = cut_windows(jnp.stack([me, outer]), group_bins, chunk * band, turns, smoothed, placing, band)
 
     pieces, windows = lax.optimization_barrier((pieces, windows))
     arrived = [windows[0]] + [swap(windows[away], away * inner) for away in range(1, OUTER)]
@@ -342,8 +381,10 @@
     rest, sent, squares = resample(outer1, late, names, arrived, weights[2:], [(0, width)], band, begun)
 
     total = squares
-    for away in range(1, OUTER):
-        total = total + swap(squares, away * inner)
+    bit = inner
+    while bit < n:
+        total = total + swap(total, bit)
+        bit *= 2
     scale = lax.rsqrt(total / nrest + 1e-06)
     factor = scale * scale / (count * n)
     scaled = call(scale_kernel, jax.ShapeDtypeStruct(rest.shape, BF16), [VMEM, VMEM], (rest, factor))
@@ -374,7 +415,8 @@
     send2, held2 = reduce(*product(q1, scaled, second, inner))
     got2 = finish(send2)
     at = (outer - jnp.arange(OUTER, dtype=I32)) % OUTER
-    return place(at, back, [(held0, got0), (held1, got1), (held2, got2)])
+    begun = place(at, [0, 1], [(held0, got0), (held1, got1)])
+    return place(at, [2, 3], [(held2, got2), (back, jnp.zeros_like(back))], begun)
 
 
 def solution(mesh):

time: 107 us -> 106 us (level)
  starting transfers between devices: 30.3 us -> 25 us
  waiting for transfers between devices: 48.2 us -> 53.2 us
  other arithmetic: 3.92 us -> 1.27 us
  Pallas kernels: 23 us -> 24.3 us
    ppermute x25 -> x24, waiting for transfers between devices: 31.6 us -> 39.3 us  [swap(): return lax.ppermute(array, 'spec', [(i, i ^ bit) for i in range(n)])]
    ppermute x25 -> x24, starting transfers between devices: 28.4 us -> 23.9 us  [swap(): return lax.ppermute(array, 'spec', [(i, i ^ bit) for i in range(n)])]
    pallas_call x0 -> x2, Pallas kernels: none -> 2.96 us  [place(): pl.pallas_call(functools.partial(place_kernel, slots, last), out_shape=ja...]
    ppermute x3, waiting for transfers between devices: 16.6 us -> 13.9 us  [step(): lax.ppermute(array, 'spec', [(i, (i + outers * inner) % n) for i in range...]
    reduce_sum x5 -> x0, other arithmetic: 2.59 us -> none  [the longest x1 0.9 us: local(): rank = jnp.sum(same.astype(I32), axis=1)]
    pallas_call x14, Pallas kernels: 23 us -> 21.3 us  [call(): pl.pallas_call(kernel, out_shape=out_shape, in_specs=in_specs, out_specs=...]
  transfers between devices with their start and end apart: 28 -> 27, of which waited for: 14 -> 17; matrix products, arithmetic and copies ran while one was open for 4% -> 2% of each run, Pallas kernels for 16% -> 17%
where the time goes in v8:
time: 106 us
  waiting for transfers between devices  53.2 us (50%)
  starting transfers between devices  25 us (24%)
  Pallas kernels  24.3 us (23%)
  local copies, waits for them, and re-layouts  1.95 us (2%)
  other arithmetic  1.27 us (1%)
    ppermute x24, waiting for transfers between devices, swap(): return lax.ppermute(array, 'spec', [(i, i ^ bit) for i in range(n)])  39.3 us
    ppermute x24, starting transfers between devices, swap(): return lax.ppermute(array, 'spec', [(i, i ^ bit) for i in range(n)])  23.9 us
    pallas_call x14, Pallas kernels, call(): pl.pallas_call(kernel, out_shape=out_shape, in_specs=in_specs, out_specs=...  21.3 us
    ppermute x3, waiting for transfers between devices, step(): lax.ppermute(array, 'spec', [(i, (i + outers * inner) % n) for i in range...  13.9 us
    pallas_call x2, Pallas kernels, place(): pl.pallas_call(functools.partial(place_kernel, slots, last), out_shape=ja...  2.96 us
  transfers between devices with their start and end apart: 27, of which 17 were waited for; matrix products, arithmetic and copies ran while one was open for 2% of the time, Pallas kernels for 17%

profile of v8, /device:TPU:0, one launch (start us, length us, event | category | flops | bytes accessed | tf_op | source)
XLA Modules:
  0.0 105.9 jit_solution(2089777431256540866)
XLA Ops:
  0.0 0.8 pad_add_fusion.3
  0.8 3.0 %collective-permute-start = (s32[148]{0:T(256)S(1)}, s32[148]{0:T(256)S(1)}, u32[]{:S(2)}, u32[]{:S(2)}) collective-permute-start(s32[148]{0:T(256)S(1)} %pad_add_fusion.3), channel_id=1, source_target_pairs={{0,4},{1,5},{2,6},{3,7},{4,0},{5,1},{6,2},{7,3},{8,12},{9,13},{10,... | collective-permute-start | bytes 1784 | tf_op jit(solution)/shard_map/ppermute | solution.py:334
  3.9 2.6 %collective-permute-start.1 = (s32[148]{0:T(256)S(1)}, s32[148]{0:T(256)S(1)}, u32[]{:S(2)}, u32[]{:S(2)}) collective-permute-start(s32[148]{0:T(256)S(1)} %pad_add_fusion.3), channel_id=1, source_target_pairs={{0,8},{1,9},{2,10},{3,11},{4,12},{5,13},{6,14},{7,15},{8,0},{9,1},... | collective-permute-start | bytes 1784 | tf_op jit(solution)/shard_map/ppermute | solution.py:334
  6.5 1.2 %dynamic-slice_bitcast_fusion = (bf16[640,128]{1,0:T(8,128)(2,1)S(1)}, bf16[640,128]{1,0:T(8,128)(2,1)S(1)}, bf16[640,128]{1,0:T(8,128)(2,1)S(1)}, bf16[640,128]{1,0:T(8,128)(2,1)S(1)}) fusion(bf16[4,640,128]{2,1,0:T(8,128)(2,1)} %bitcast.48, s32[]{:T(128)S(6)} %select_n.41, s32[]{:T(128)S(6)} %select_n.40, s32[]{:T(128)S(6)} %select_n.39, s32[]{:T(128)S(6)} %select_n.38), kind=kLoop, calls=%fused_computation.3 | loop fusion | bytes 1310736 | tf_op jit(solution)/shard_map/jit(dynamic_index_in_dim)/squeeze | solution.py:354
  7.7 0.7 collective-permute-done.1
  8.3 3.5 %collective-permute-done.2 = s32[148]{0:T(256)S(1)} collective-permute-done((s32[148]{0:T(256)S(1)}, s32[148]{0:T(256)S(1)}, u32[]{:S(2)}, u32[]{:S(2)}) %collective-permute-start.2) | collective-permute-done | bytes 624 | tf_op jit(solution)/shard_map/ppermute | solution.py:334
  11.8 0.1 collective-permute-start.6
  11.9 0.1 collective-permute-start.3
  12.0 0.6 collective-permute-start.4
  12.6 3.8 %collective-permute-start.5 = (bf16[640,128]{1,0:T(8,128)(2,1)S(1)}, bf16[640,128]{1,0:T(8,128)(2,1)S(1)}, u32[]{:S(2)}, u32[]{:S(2)}) collective-permute-start(bf16[640,128]{1,0:T(8,128)(2,1)S(1)} %get-tuple-element.101), channel_id=1, source_target_pairs={{0,12},{1,13},{2,14},{3,15},{4,8},{5,9},{6,10},{7,11},{8,4},{9,5},... | collective-permute-start | bytes 491528 | tf_op jit(solution)/shard_map/ppermute | solution.py:334
  16.4 1.5 %collective-permute-start.7 = (s32[4,2,20]{2,0,1:T(4,128)S(1)}, s32[4,2,20]{2,0,1:T(4,128)S(1)}, u32[]{:S(2)}, u32[]{:S(2)}) collective-permute-start(s32[4,2,20]{2,0,1:T(4,128)S(1)} %pad_add_fusion.2), channel_id=1, source_target_pairs={{0,2},{1,3},{2,0},{3,1},{4,6},{5,7},{6,4},{7,5},{8,10},{9,11},{10,... | collective-permute-start | bytes 1928 | tf_op jit(solution)/shard_map/ppermute | solution.py:334
  17.9 0.1 pad_add_fusion.5.me_ref
  18.0 0.7 copy-done.1
  18.6 0.2 shard_map.55
  18.9 7.7 %shard_map.56.smoothed_ref = bf16[128,3968]{1,0:T(8,128)(2,1)S(1)} custom-call(bf16[128,3968]{1,0:T(8,128)(2,1)S(1)} %copy-done, bf16[11,128,3968]{2,1,0:T(8,128)(2,1)} %bitcast.46), custom_call_target="tpu_custom_call" | custom-call | flops 1 | bytes 1 | tf_op jit(solution)/shard_map/pallas_call | solution.py:20
  26.6 4.7 %shard_map.57 = (bf16[128,640]{1,0:T(8,128)(2,1)S(1)}, bf16[128,640]{1,0:T(8,128)(2,1)S(1)}, bf16[128,640]{1,0:T(8,128)(2,1)S(1)}, bf16[128,640]{1,0:T(8,128)(2,1)S(1)}) custom-call(s32[2]{0:T(128)S(1)} %pad_add_fusion.5.me_ref, s32[2,128]{1,0:T(2,128)S(1)} %get-tuple-element.53.groups_ref, s32[16,20]{1,0:T(8,128)S(1)} %get-tuple-element.106.starts_ref, ...), custom_call_target="tpu_custom_call" | custom-call | flops 1 | bytes 1 | tf_op jit(solution)/shard_map/pallas_call | solution.py:20
  31.4 0.1 pad_maximum_fusion.refs_4_
  31.5 0.6 collective-permute-start.8
  32.1 0.2 collective-permute-start.10
  32.3 2.3 %collective-permute-start.11 = (bf16[128,640]{1,0:T(8,128)(2,1)S(1)}, bf16[128,640]{1,0:T(8,128)(2,1)S(1)}, u32[]{:S(2)}, u32[]{:S(2)}) collective-permute-start(bf16[128,640]{1,0:T(8,128)(2,1)S(1)} %get-tuple-element.68), channel_id=1, source_target_pairs={{0,12},{1,13},{2,14},{3,15},{4,8},{5,9},{6,10},{7,11},{8,4},{9,5},... | collective-permute-start | bytes 491528 | tf_op jit(solution)/shard_map/ppermute | solution.py:334
  34.6 0.9 collective-permute-start.9
  35.5 9.6 %collective-permute-done.10.refs_2_ = bf16[128,640]{1,0:T(8,128)(2,1)S(1)} collective-permute-done((bf16[128,640]{1,0:T(8,128)(2,1)S(1)}, bf16[128,640]{1,0:T(8,128)(2,1)S(1)}, u32[]{:S(2)}, u32[]{:S(2)}) %collective-permute-start.10) | collective-permute-done | bytes 163872 | tf_op jit(solution)/shard_map/ppermute | solution.py:334
  45.1 1.2 %collective-permute-done.9.refs_1_ = bf16[128,640]{1,0:T(8,128)(2,1)S(1)} collective-permute-done((bf16[128,640]{1,0:T(8,128)(2,1)S(1)}, bf16[128,640]{1,0:T(8,128)(2,1)S(1)}, u32[]{:S(2)}, u32[]{:S(2)}) %collective-permute-start.9) | collective-permute-done | bytes 163872 | tf_op jit(solution)/shard_map/ppermute | solution.py:334
  46.3 1.2 %collective-permute-done.8.refs_5_ = bf16[4,640,128]{2,1,0:T(8,128)(2,1)S(1)} collective-permute-done((bf16[4,640,128]{2,1,0:T(8,128)(2,1)S(1)}, bf16[4,640,128]{2,1,0:T(8,128)(2,1)S(1)}, u32[]{:S(2)}, u32[]{:S(2)}) %collective-permute-start.8) | collective-permute-done | bytes 655392 | tf_op jit(solution)/shard_map/ppermute | solution.py:334
  47.5 0.5 collective-permute-start.13
  48.0 0.1 pad_add_fusion.6.bins_ref
  48.1 0.1 pad_add_fusion.4.bins_ref
  48.2 0.1 slice.8.names_ref
  48.3 2.2 %shard_map.58.refs_6_ = f32[512,640]{1,0:T(8,128)S(1)} custom-call(s32[1]{0:T(128)} %bitcast.1.outer_ref, s32[8]{0:T(128)S(1)} %pad_add_fusion.6.bins_ref, s32[4,128]{1,0:T(4,128)S(1)} %slice.8.names_ref, bf16[128,640]{1,0:T(8,128)(2,1)S(1)} %get-tuple-element.69.refs_0_, bf16[128,640]{1,0:T(8,128)(2,1)S(1)} %collective-permute-done.9.refs_1_, ...), custom_call_target="tpu_custom_call" | custom-call | flops 1 | bytes 1 | tf_op jit(solution)/shard_map/pallas_call | solution.py:20
  50.5 2.7 %shard_map.59 = (f32[512,640]{1,0:T(8,128)S(1)}, bf16[512,640]{1,0:T(8,128)(2,1)S(1)}, f32[4,128]{1,0:T(4,128)S(1)}) custom-call(s32[1]{0:T(128)} %bitcast.1.outer_ref, s32[8]{0:T(128)S(1)} %pad_add_fusion.4.bins_ref, s32[4,128]{1,0:T(4,128)S(1)} %slice.8.names_ref, bf16[128,640]{1,0:T(8,128)(2,1)S(1)} %get-tuple-element.69.refs_0_, ...), custom_call_target="tpu_custom_call", output_to_operand_aliasing={{0}: (9, {})} | custom-call | flops 1 | bytes 1 | tf_op jit(solution)/shard_map/pallas_call | solution.py:20
  53.2 1.7 %collective-permute-start.14 = (f32[4,128]{1,0:T(4,128)S(1)}, f32[4,128]{1,0:T(4,128)S(1)}, u32[]{:S(2)}, u32[]{:S(2)}) collective-permute-start(f32[4,128]{1,0:T(4,128)S(1)} %get-tuple-element.76), channel_id=1, source_target_pairs={{0,4},{1,5},{2,6},{3,7},{4,0},{5,1},{6,2},{7,3},{8,12},{9,13},{10,... | collective-permute-start | bytes 6152 | tf_op jit(solution)/shard_map/ppermute | solution.py:334
  54.9 2.0 %collective-permute-done.14 = f32[4,128]{1,0:T(4,128)S(1)} collective-permute-done((f32[4,128]{1,0:T(4,128)S(1)}, f32[4,128]{1,0:T(4,128)S(1)}, u32[]{:S(2)}, u32[]{:S(2)}) %collective-permute-start.14) | collective-permute-done | bytes 2080 | tf_op jit(solution)/shard_map/ppermute | solution.py:334
  56.9 0.6 collective-permute-start.15
  57.5 1.0 collective-permute-start.16
  58.5 3.1 %collective-permute-done.15 = f32[4,128]{1,0:T(4,128)S(1)} collective-permute-done((f32[4,128]{1,0:T(4,128)S(1)}, f32[4,128]{1,0:T(4,128)S(1)}, u32[]{:S(2)}, u32[]{:S(2)}) %collective-permute-start.15) | collective-permute-done | bytes 2080 | tf_op jit(solution)/shard_map/ppermute | solution.py:334
  61.6 0.2 shard_map.60.tall_ref.wide_ref
  61.7 0.8 shard_map.61
  62.6 0.1 collective-permute-start.17
  62.6 1.7 %collective-permute-done.17.got_ref = bf16[2,160,640]{2,1,0:T(8,128)(2,1)S(1)} collective-permute-done((bf16[2,160,640]{2,1,0:T(8,128)(2,1)S(1)}, bf16[2,160,640]{2,1,0:T(8,128)(2,1)S(1)}, u32[]{:S(2)}, u32[]{:S(2)}) %collective-permute-start.17) | collective-permute-done | bytes 409632 | tf_op jit(solution)/shard_map/ppermute | solution.py:334
  64.4 0.1 shard_map.62
  64.5 0.4 collective-permute-start.18
  64.8 6.8 %collective-permute-done.18 = bf16[1,160,640]{2,1,0:T(8,128)(2,1)S(1)} collective-permute-done((bf16[1,160,640]{2,1,0:T(8,128)(2,1)S(1)}, bf16[1,160,640]{2,1,0:T(8,128)(2,1)S(1)}, u32[]{:S(2)}, u32[]{:S(2)}) %collective-permute-start.18) | collective-permute-done | bytes 204832 | tf_op jit(solution)/shard_map/ppermute | solution.py:334
  71.7 3.0 %collective-permute-done.16.tall_ref.wide_ref = bf16[512,640]{1,0:T(8,128)(2,1)S(1)} collective-permute-done((bf16[512,640]{1,0:T(8,128)(2,1)S(1)}, bf16[512,640]{1,0:T(8,128)(2,1)S(1)}, u32[]{:S(2)}, u32[]{:S(2)}) %collective-permute-start.16) | collective-permute-done | bytes 655392 | tf_op jit(solution)/shard_map/ppermute | solution.py:337
  74.7 0.8 shard_map.63
  75.5 0.1 collective-permute-start.20
  75.6 1.7 %collective-permute-done.20.got_ref = bf16[2,160,640]{2,1,0:T(8,128)(2,1)S(1)} collective-permute-done((bf16[2,160,640]{2,1,0:T(8,128)(2,1)S(1)}, bf16[2,160,640]{2,1,0:T(8,128)(2,1)S(1)}, u32[]{:S(2)}, u32[]{:S(2)}) %collective-permute-start.20) | collective-permute-done | bytes 409632 | tf_op jit(solution)/shard_map/ppermute | solution.py:334
  77.3 0.1 shard_map.64
  77.4 0.8 shard_map.65
  78.2 0.2 collective-permute-start.21
  78.4 1.5 %collective-permute-start.23 = (bf16[1,160,640]{2,1,0:T(8,128)(2,1)S(1)}, bf16[1,160,640]{2,1,0:T(8,128)(2,1)S(1)}, u32[]{:S(2)}, u32[]{:S(2)}) collective-permute-start(bf16[1,160,640]{2,1,0:T(8,128)(2,1)S(1)} %get-tuple-element.89), channel_id=1, source_target_pairs={{0,2},{1,3},{2,0},{3,1},{4,6},{5,7},{6,4},{7,5},{8,10},{9,11},{10,... | collective-permute-start | bytes 614408 | tf_op jit(solution)/shard_map/ppermute | solution.py:334
  79.9 0.1 collective-permute-done.21.got_ref
  80.0 0.1 shard_map.66
  80.1 1.6 %collective-permute-start.22 = (bf16[1,160,640]{2,1,0:T(8,128)(2,1)S(1)}, bf16[1,160,640]{2,1,0:T(8,128)(2,1)S(1)}, u32[]{:S(2)}, u32[]{:S(2)}) collective-permute-start(bf16[1,160,640]{2,1,0:T(8,128)(2,1)S(1)} %get-tuple-element.88), channel_id=1, source_target_pairs={{0,2},{1,3},{2,0},{3,1},{4,6},{5,7},{6,4},{7,5},{8,10},{9,11},{10,... | collective-permute-start | bytes 614408 | tf_op jit(solution)/shard_map/ppermute | solution.py:334
  81.7 4.6 %collective-permute-done.23 = bf16[1,160,640]{2,1,0:T(8,128)(2,1)S(1)} collective-permute-done((bf16[1,160,640]{2,1,0:T(8,128)(2,1)S(1)}, bf16[1,160,640]{2,1,0:T(8,128)(2,1)S(1)}, u32[]{:S(2)}, u32[]{:S(2)}) %collective-permute-start.23) | collective-permute-done | bytes 204832 | tf_op jit(solution)/shard_map/ppermute | solution.py:334
  86.3 8.2 %collective-permute-done.19.wide_ref = bf16[512,640]{1,0:T(8,128)(2,1)S(1)} collective-permute-done((bf16[512,640]{1,0:T(8,128)(2,1)S(1)}, bf16[512,640]{1,0:T(8,128)(2,1)S(1)}, u32[]{:S(2)}, u32[]{:S(2)}) %collective-permute-start.19) | collective-permute-done | bytes 655392 | tf_op jit(solution)/shard_map/ppermute | solution.py:337
  94.5 0.8 shard_map.67
  95.3 0.1 collective-permute-start.24
  95.5 1.6 %collective-permute-done.24.got_ref = bf16[2,160,640]{2,1,0:T(8,128)(2,1)S(1)} collective-permute-done((bf16[2,160,640]{2,1,0:T(8,128)(2,1)S(1)}, bf16[2,160,640]{2,1,0:T(8,128)(2,1)S(1)}, u32[]{:S(2)}, u32[]{:S(2)}) %collective-permute-start.24) | collective-permute-done | bytes 409632 | tf_op jit(solution)/shard_map/ppermute | solution.py:334
  97.1 0.1 shard_map.68
  97.2 1.6 %collective-permute-start.25 = (bf16[1,160,640]{2,1,0:T(8,128)(2,1)S(1)}, bf16[1,160,640]{2,1,0:T(8,128)(2,1)S(1)}, u32[]{:S(2)}, u32[]{:S(2)}) collective-permute-start(bf16[1,160,640]{2,1,0:T(8,128)(2,1)S(1)} %get-tuple-element.94), channel_id=1, source_target_pairs={{0,2},{1,3},{2,0},{3,1},{4,6},{5,7},{6,4},{7,5},{8,10},{9,11},{10,... | collective-permute-start | bytes 614408 | tf_op jit(solution)/shard_map/ppermute | solution.py:334
  98.8 1.5 %shard_map.69.refs_4_ = f32[160,2560]{1,0:T(8,128)} custom-call(s32[4]{0:T(128)S(1)} %and_select_fusion.at_ref, f32[160,640]{1,0:T(8,128)S(1)} %bitcast.38, bf16[160,640]{1,0:T(8,128)(2,1)S(1)} %bitcast.41, f32[160,640]{1,0:T(8,128)S(1)} %bitcast.39, bf16[160,640]{1,0:T(8,128)(2,1)S(1)} %bitcast.42), custom_call_target="tpu_custom_call" | custom-call | flops 1 | bytes 1 | tf_op jit(solution)/shard_map/pallas_call | solution.py:308
  100.3 2.7 %collective-permute-done.26.refs_2_ = bf16[160,640]{1,0:T(8,128)(2,1)S(1)} collective-permute-done((bf16[160,640]{1,0:T(8,128)(2,1)S(1)}, bf16[160,640]{1,0:T(8,128)(2,1)S(1)}, u32[]{:S(2)}, u32[]{:S(2)}) %collective-permute-start.26) | collective-permute-done | bytes 204832 | tf_op jit(solution)/shard_map/ppermute | solution.py:337
  103.0 1.4 %collective-permute-done.25 = bf16[1,160,640]{2,1,0:T(8,128)(2,1)S(1)} collective-permute-done((bf16[1,160,640]{2,1,0:T(8,128)(2,1)S(1)}, bf16[1,160,640]{2,1,0:T(8,128)(2,1)S(1)}, u32[]{:S(2)}, u32[]{:S(2)}) %collective-permute-start.25) | collective-permute-done | bytes 204832 | tf_op jit(solution)/shard_map/ppermute | solution.py:334
  104.5 1.5 %shard_map.70 = f32[160,2560]{1,0:T(8,128)} custom-call(s32[4]{0:T(128)S(1)} %and_select_fusion.at_ref, f32[160,640]{1,0:T(8,128)S(1)} %bitcast.40, bf16[160,640]{1,0:T(8,128)(2,1)S(1)} %bitcast.43, bf16[160,640]{1,0:T(8,128)(2,1)S(1)} %collective-permute-done.26.refs_2_, ...), custom_call_target="tpu_custom_call", output_to_operand_aliasing={{}: (5, {})} | custom-call | flops 1 | bytes 1 | tf_op jit(solution)/shard_map/pallas_call | solution.py:308
  (30 shorter events, 0.3 us)
Async XLA Ops:
  0.0 18.9 %copy-start = (bf16[128,3968]{1,0:T(8,128)(2,1)S(1)}, bf16[128,3968]{1,0:T(8,128)(2,1)}, u32[]{:S(2)}) copy-start(bf16[128,3968]{1,0:T(8,128)(2,1)} %flux_ref) | copy-start | bytes 3047428
  0.8 6.8 %collective-permute-start = (s32[148]{0:T(256)S(1)}, s32[148]{0:T(256)S(1)}, u32[]{:S(2)}, u32[]{:S(2)}) collective-permute-start(s32[148]{0:T(256)S(1)} %pad_add_fusion.3), channel_id=1, source_target_pairs={{0,4},{1,5},{2,6},{3,7},{4,0},{5,1},{6,2},{7,3},{8,12},{9,13},{10,... | collective-permute-start | bytes 1784 | tf_op jit(solution)/shard_map/ppermute | solution.py:334
  3.9 4.5 %collective-permute-start.1 = (s32[148]{0:T(256)S(1)}, s32[148]{0:T(256)S(1)}, u32[]{:S(2)}, u32[]{:S(2)}) collective-permute-start(s32[148]{0:T(256)S(1)} %pad_add_fusion.3), channel_id=1, source_target_pairs={{0,8},{1,9},{2,10},{3,11},{4,12},{5,13},{6,14},{7,15},{8,0},{9,1},... | collective-permute-start | bytes 1784 | tf_op jit(solution)/shard_map/ppermute | solution.py:334
  6.4 5.4 %collective-permute-start.2 = (s32[148]{0:T(256)S(1)}, s32[148]{0:T(256)S(1)}, u32[]{:S(2)}, u32[]{:S(2)}) collective-permute-start(s32[148]{0:T(256)S(1)} %pad_add_fusion.3), channel_id=1, source_target_pairs={{0,12},{1,13},{2,14},{3,15},{4,8},{5,9},{6,10},{7,11},{8,4},{9,5},... | collective-permute-start | bytes 1784 | tf_op jit(solution)/shard_map/ppermute | solution.py:334
  11.8 4.5 %collective-permute-start.6 = (s32[4,1,20]{2,0,1:T(4,128)S(1)}, s32[4,1,20]{2,0,1:T(4,128)S(1)}, u32[]{:S(2)}, u32[]{:S(2)}) collective-permute-start(s32[4,1,20]{2,0,1:T(4,128)S(1)} %slice_bitcast_fusion), channel_id=1, source_target_pairs={{0,1},{1,0},{2,3},{3,2},{4,5},{5,4},{6,7},{7,6},{8,9},{9,8},{10,11... | collective-permute-start | bytes 968 | tf_op jit(solution)/shard_map/ppermute | solution.py:334
  11.9 19.4 %collective-permute-start.3 = (bf16[640,128]{1,0:T(8,128)(2,1)S(1)}, bf16[640,128]{1,0:T(8,128)(2,1)S(1)}, u32[]{:S(2)}, u32[]{:S(2)}) collective-permute-start(bf16[640,128]{1,0:T(8,128)(2,1)S(1)} %get-tuple-element.103), channel_id=1, source_target_pairs={{0,4},{1,5},{2,6},{3,7},{4,0},{5,1},{6,2},{7,3},{8,12},{9,13},{10,... | collective-permute-start | bytes 491528 | tf_op jit(solution)/shard_map/ppermute | solution.py:334
  12.0 19.4 %collective-permute-start.4 = (bf16[640,128]{1,0:T(8,128)(2,1)S(1)}, bf16[640,128]{1,0:T(8,128)(2,1)S(1)}, u32[]{:S(2)}, u32[]{:S(2)}) collective-permute-start(bf16[640,128]{1,0:T(8,128)(2,1)S(1)} %get-tuple-element.102), channel_id=1, source_target_pairs={{0,8},{1,9},{2,10},{3,11},{4,12},{5,13},{6,14},{7,15},{8,0},{9,1},... | collective-permute-start | bytes 491528 | tf_op jit(solution)/shard_map/ppermute | solution.py:334
  12.6 18.8 %collective-permute-start.5 = (bf16[640,128]{1,0:T(8,128)(2,1)S(1)}, bf16[640,128]{1,0:T(8,128)(2,1)S(1)}, u32[]{:S(2)}, u32[]{:S(2)}) collective-permute-start(bf16[640,128]{1,0:T(8,128)(2,1)S(1)} %get-tuple-element.101), channel_id=1, source_target_pairs={{0,12},{1,13},{2,14},{3,15},{4,8},{5,9},{6,10},{7,11},{8,4},{9,5},... | collective-permute-start | bytes 491528 | tf_op jit(solution)/shard_map/ppermute | solution.py:334
  16.4 10.2 %collective-permute-start.7 = (s32[4,2,20]{2,0,1:T(4,128)S(1)}, s32[4,2,20]{2,0,1:T(4,128)S(1)}, u32[]{:S(2)}, u32[]{:S(2)}) collective-permute-start(s32[4,2,20]{2,0,1:T(4,128)S(1)} %pad_add_fusion.2), channel_id=1, source_target_pairs={{0,2},{1,3},{2,0},{3,1},{4,6},{5,7},{6,4},{7,5},{8,10},{9,11},{10,... | collective-permute-start | bytes 1928 | tf_op jit(solution)/shard_map/ppermute | solution.py:334
  18.0 0.7 copy-start.1
  31.5 16.0 %collective-permute-start.8 = (bf16[4,640,128]{2,1,0:T(8,128)(2,1)S(1)}, bf16[4,640,128]{2,1,0:T(8,128)(2,1)S(1)}, u32[]{:S(2)}, u32[]{:S(2)}) collective-permute-start(bf16[4,640,128]{2,1,0:T(8,128)(2,1)S(1)} %pad_maximum_fusion.refs_4_), channel_id=1, source_target_pairs={{0,2},{1,3},{2,0},{3,1},{4,6},{5,7},{6,4},{7,5},{8,10},{9,11},{10,... | collective-permute-start | bytes 1966088 | tf_op jit(solution)/shard_map/ppermute | solution.py:334
  32.1 13.1 %collective-permute-start.10 = (bf16[128,640]{1,0:T(8,128)(2,1)S(1)}, bf16[128,640]{1,0:T(8,128)(2,1)S(1)}, u32[]{:S(2)}, u32[]{:S(2)}) collective-permute-start(bf16[128,640]{1,0:T(8,128)(2,1)S(1)} %get-tuple-element.67), channel_id=1, source_target_pairs={{0,8},{1,9},{2,10},{3,11},{4,12},{5,13},{6,14},{7,15},{8,0},{9,1},... | collective-permute-start | bytes 491528 | tf_op jit(solution)/shard_map/ppermute | solution.py:334
  32.3 12.9 %collective-permute-start.11 = (bf16[128,640]{1,0:T(8,128)(2,1)S(1)}, bf16[128,640]{1,0:T(8,128)(2,1)S(1)}, u32[]{:S(2)}, u32[]{:S(2)}) collective-permute-start(bf16[128,640]{1,0:T(8,128)(2,1)S(1)} %get-tuple-element.68), channel_id=1, source_target_pairs={{0,12},{1,13},{2,14},{3,15},{4,8},{5,9},{6,10},{7,11},{8,4},{9,5},... | collective-permute-start | bytes 491528 | tf_op jit(solution)/shard_map/ppermute | solution.py:334
  34.6 11.7 %collective-permute-start.9 = (bf16[128,640]{1,0:T(8,128)(2,1)S(1)}, bf16[128,640]{1,0:T(8,128)(2,1)S(1)}, u32[]{:S(2)}, u32[]{:S(2)}) collective-permute-start(bf16[128,640]{1,0:T(8,128)(2,1)S(1)} %get-tuple-element.66), channel_id=1, source_target_pairs={{0,4},{1,5},{2,6},{3,7},{4,0},{5,1},{6,2},{7,3},{8,12},{9,13},{10,... | collective-permute-start | bytes 491528 | tf_op jit(solution)/shard_map/ppermute | solution.py:334
  47.5 3.0 %collective-permute-start.12 = (bf16[4,640,128]{2,1,0:T(8,128)(2,1)S(1)}, bf16[4,640,128]{2,1,0:T(8,128)(2,1)S(1)}, u32[]{:S(2)}, u32[]{:S(2)}) collective-permute-start(bf16[4,640,128]{2,1,0:T(8,128)(2,1)S(1)} %pad_maximum_fusion.refs_4_), channel_id=1, source_target_pairs={{0,1},{1,0},{2,3},{3,2},{4,5},{5,4},{6,7},{7,6},{8,9},{9,8},{10,11... | collective-permute-start | bytes 1966088 | tf_op jit(solution)/shard_map/ppermute | solution.py:334
  47.5 3.0 %collective-permute-start.13 = (bf16[4,640,128]{2,1,0:T(8,128)(2,1)S(1)}, bf16[4,640,128]{2,1,0:T(8,128)(2,1)S(1)}, u32[]{:S(2)}, u32[]{:S(2)}) collective-permute-start(bf16[4,640,128]{2,1,0:T(8,128)(2,1)S(1)} %collective-permute-done.8.refs_5_), channel_id=1, source_target_pairs={{0,1},{1,0},{2,3},{3,2},{4,5},{5,4},{6,7},{7,6},{8,9},{9,8},{10,11... | collective-permute-start | bytes 1966088 | tf_op jit(solution)/shard_map/ppermute | solution.py:334
  53.2 3.7 %collective-permute-start.14 = (f32[4,128]{1,0:T(4,128)S(1)}, f32[4,128]{1,0:T(4,128)S(1)}, u32[]{:S(2)}, u32[]{:S(2)}) collective-permute-start(f32[4,128]{1,0:T(4,128)S(1)} %get-tuple-element.76), channel_id=1, source_target_pairs={{0,4},{1,5},{2,6},{3,7},{4,0},{5,1},{6,2},{7,3},{8,12},{9,13},{10,... | collective-permute-start | bytes 6152 | tf_op jit(solution)/shard_map/ppermute | solution.py:334
  56.9 4.7 %collective-permute-start.15 = (f32[4,128]{1,0:T(4,128)S(1)}, f32[4,128]{1,0:T(4,128)S(1)}, u32[]{:S(2)}, u32[]{:S(2)}) collective-permute-start(f32[4,128]{1,0:T(4,128)S(1)} %add.54), channel_id=1, source_target_pairs={{0,8},{1,9},{2,10},{3,11},{4,12},{5,13},{6,14},{7,15},{8,0},{9,1},... | collective-permute-start | bytes 6152 | tf_op jit(solution)/shard_map/ppermute | solution.py:334
  57.5 17.2 %collective-permute-start.16 = (bf16[512,640]{1,0:T(8,128)(2,1)S(1)}, bf16[512,640]{1,0:T(8,128)(2,1)S(1)}, u32[]{:S(2)}, u32[]{:S(2)}) collective-permute-start(bf16[512,640]{1,0:T(8,128)(2,1)S(1)} %get-tuple-element.77.wide_ref), channel_id=1, source_target_pairs={{0,4},{1,5},{2,6},{3,7},{4,8},{5,9},{6,10},{7,11},{8,12},{9,13},{1... | collective-permute-start | bytes 1966088 | tf_op jit(solution)/shard_map/ppermute | solution.py:337
  62.6 1.8 %collective-permute-start.17 = (bf16[2,160,640]{2,1,0:T(8,128)(2,1)S(1)}, bf16[2,160,640]{2,1,0:T(8,128)(2,1)S(1)}, u32[]{:S(2)}, u32[]{:S(2)}) collective-permute-start(bf16[2,160,640]{2,1,0:T(8,128)(2,1)S(1)} %get-tuple-element.79), channel_id=1, source_target_pairs={{0,1},{1,0},{2,3},{3,2},{4,5},{5,4},{6,7},{7,6},{8,9},{9,8},{10,11... | collective-permute-start | bytes 1228808 | tf_op jit(solution)/shard_map/ppermute | solution.py:334
  64.5 7.2 %collective-permute-start.18 = (bf16[1,160,640]{2,1,0:T(8,128)(2,1)S(1)}, bf16[1,160,640]{2,1,0:T(8,128)(2,1)S(1)}, u32[]{:S(2)}, u32[]{:S(2)}) collective-permute-start(bf16[1,160,640]{2,1,0:T(8,128)(2,1)S(1)} %get-tuple-element.80), channel_id=1, source_target_pairs={{0,2},{1,3},{2,0},{3,1},{4,6},{5,7},{6,4},{7,5},{8,10},{9,11},{10,... | collective-permute-start | bytes 614408 | tf_op jit(solution)/shard_map/ppermute | solution.py:334
  75.5 1.8 %collective-permute-start.20 = (bf16[2,160,640]{2,1,0:T(8,128)(2,1)S(1)}, bf16[2,160,640]{2,1,0:T(8,128)(2,1)S(1)}, u32[]{:S(2)}, u32[]{:S(2)}) collective-permute-start(bf16[2,160,640]{2,1,0:T(8,128)(2,1)S(1)} %get-tuple-element.83), channel_id=1, source_target_pairs={{0,1},{1,0},{2,3},{3,2},{4,5},{5,4},{6,7},{7,6},{8,9},{9,8},{10,11... | collective-permute-start | bytes 1228808 | tf_op jit(solution)/shard_map/ppermute | solution.py:334
  75.6 18.9 %collective-permute-start.19 = (bf16[512,640]{1,0:T(8,128)(2,1)S(1)}, bf16[512,640]{1,0:T(8,128)(2,1)S(1)}, u32[]{:S(2)}, u32[]{:S(2)}) collective-permute-start(bf16[512,640]{1,0:T(8,128)(2,1)S(1)} %collective-permute-done.16.tall_ref.wide_ref), channel_id=1, source_target_pairs={{0,4},{1,5},{2,6},{3,7},{4,8},{5,9},{6,10},{7,11},{8,12},{9,13},{1... | collective-permute-start | bytes 1966088 | tf_op jit(solution)/shard_map/ppermute | solution.py:337
  78.2 1.8 %collective-permute-start.21 = (bf16[2,160,640]{2,1,0:T(8,128)(2,1)S(1)}, bf16[2,160,640]{2,1,0:T(8,128)(2,1)S(1)}, u32[]{:S(2)}, u32[]{:S(2)}) collective-permute-start(bf16[2,160,640]{2,1,0:T(8,128)(2,1)S(1)} %get-tuple-element.87), channel_id=1, source_target_pairs={{0,1},{1,0},{2,3},{3,2},{4,5},{5,4},{6,7},{7,6},{8,9},{9,8},{10,11... | collective-permute-start | bytes 1228808 | tf_op jit(solution)/shard_map/ppermute | solution.py:334
  78.4 7.9 %collective-permute-start.23 = (bf16[1,160,640]{2,1,0:T(8,128)(2,1)S(1)}, bf16[1,160,640]{2,1,0:T(8,128)(2,1)S(1)}, u32[]{:S(2)}, u32[]{:S(2)}) collective-permute-start(bf16[1,160,640]{2,1,0:T(8,128)(2,1)S(1)} %get-tuple-element.89), channel_id=1, source_target_pairs={{0,2},{1,3},{2,0},{3,1},{4,6},{5,7},{6,4},{7,5},{8,10},{9,11},{10,... | collective-permute-start | bytes 614408 | tf_op jit(solution)/shard_map/ppermute | solution.py:334
  80.1 14.4 %collective-permute-start.22 = (bf16[1,160,640]{2,1,0:T(8,128)(2,1)S(1)}, bf16[1,160,640]{2,1,0:T(8,128)(2,1)S(1)}, u32[]{:S(2)}, u32[]{:S(2)}) collective-permute-start(bf16[1,160,640]{2,1,0:T(8,128)(2,1)S(1)} %get-tuple-element.88), channel_id=1, source_target_pairs={{0,2},{1,3},{2,0},{3,1},{4,6},{5,7},{6,4},{7,5},{8,10},{9,11},{10,... | collective-permute-start | bytes 614408 | tf_op jit(solution)/shard_map/ppermute | solution.py:334
  95.3 1.8 %collective-permute-start.24 = (bf16[2,160,640]{2,1,0:T(8,128)(2,1)S(1)}, bf16[2,160,640]{2,1,0:T(8,128)(2,1)S(1)}, u32[]{:S(2)}, u32[]{:S(2)}) collective-permute-start(bf16[2,160,640]{2,1,0:T(8,128)(2,1)S(1)} %get-tuple-element.92), channel_id=1, source_target_pairs={{0,1},{1,0},{2,3},{3,2},{4,5},{5,4},{6,7},{7,6},{8,9},{9,8},{10,11... | collective-permute-start | bytes 1228808 | tf_op jit(solution)/shard_map/ppermute | solution.py:334
  95.5 7.5 %collective-permute-start.26 = (bf16[160,640]{1,0:T(8,128)(2,1)S(1)}, bf16[160,640]{1,0:T(8,128)(2,1)S(1)}, u32[]{:S(2)}, u32[]{:S(2)}) collective-permute-start(bf16[160,640]{1,0:T(8,128)(2,1)S(1)} %fusion), channel_id=1, source_target_pairs={{0,12},{1,13},{2,14},{3,15},{4,0},{5,1},{6,2},{7,3},{8,4},{9,5},{1... | collective-permute-start | bytes 614408 | tf_op jit(solution)/shard_map/ppermute | solution.py:337
  97.2 7.2 %collective-permute-start.25 = (bf16[1,160,640]{2,1,0:T(8,128)(2,1)S(1)}, bf16[1,160,640]{2,1,0:T(8,128)(2,1)S(1)}, u32[]{:S(2)}, u32[]{:S(2)}) collective-permute-start(bf16[1,160,640]{2,1,0:T(8,128)(2,1)S(1)} %get-tuple-element.94), channel_id=1, source_target_pairs={{0,2},{1,3},{2,0},{3,1},{4,6},{5,7},{6,4},{7,5},{8,10},{9,11},{10,... | collective-permute-start | bytes 614408 | tf_op jit(solution)/shard_map/ppermute | solution.py:334

commit v9 on v8

--- a/solution.py
+++ b/solution.py
@@ -33,16 +33,21 @@
     rows, nobs = flux.shape
     taps = resolution.shape[0]
     tiles = rows // tall
-    ahead = min(2, tiles)
+    ahead = min(3, tiles)
 
     def own_rows(tile):
         return pl.ds(pl.multiple_of(tile * tall, tall), tall)
 
+    def copies(tile):
+        own = own_rows(tile)
+        return (
+            pltpu.make_async_copy(flux_ref.at[own], flux.at[own], sem.at[0, tile]),
+            pltpu.make_async_copy(resolution_ref.at[:, own], resolution.at[:, own], sem.at[1, tile]),
+        )
+
     def fetch(tile):
-        own = own_rows(tile)
-        pltpu.make_async_copy(flux_ref.at[own], flux.at[own], sem.at[0, tile]).start()
-        for tap in range(taps):
-            pltpu.make_async_copy(resolution_ref.at[tap, own], resolution.at[tap, own], sem.at[1, tile]).start()
+        for copy in copies(tile):
+            copy.start()
 
     for tile in range(ahead):
         fetch(tile)
@@ -53,8 +58,8 @@
 
     def one_tile(tile, carry):
         own = own_rows(tile)
-        pltpu.make_async_copy(flux_ref.at[own], flux.at[own], sem.at[0, tile]).wait()
-        pltpu.make_async_copy(resolution_ref.at[:, own], resolution.at[:, own], sem.at[1, tile]).wait()
+        for copy in copies(tile):
+            copy.wait()
 
         @pl.when(tile + ahead < tiles)
         def _():
@@ -177,62 +182,83 @@
     )
 
 
-def rest_kernel(npieces, splits, band, begun, outer_ref, bins_ref, names_ref, *refs):
-    windows, refs = refs[:OUTER], refs[OUTER:]
-    weights, refs = refs[:npieces], refs[npieces:]
-    if begun:
-        before_ref, refs = refs[0], refs[1:]
-        sents, squares_ref = refs[1 : 1 + len(splits)], refs[1 + len(splits)]
-    rest_ref, window, named_ref = refs[0], refs[-2], refs[-1]
+def masked_rest(windows, names, bins_ref, weights, band, window, named_ref, value_ref, begun):
     count = windows[0].shape[0]
-    for away in range(OUTER):
-        own = pl.ds(pl.multiple_of((outer_ref[0] ^ away) * count, count), count)
-        window[own, :] = windows[away][...]
-        named_ref[own, :] = jnp.broadcast_to(names_ref[away : away + 1, :].astype(F32), (band, count)).T
-    rows, width = window.shape
+    for i in range(len(windows)):
+        own = slice(i * count, (i + 1) * count)
+        window[own, :] = windows[i][...]
+        named_ref[own, :] = jnp.broadcast_to(names[i], (band, count)).T
     named = named_ref[...]
-    total = jnp.zeros((rows, band), F32)
-    for p in range(npieces):
+    for p in range(len(weights)):
         hits = [
             (named == bins_ref[p * OUTER + b].astype(F32)).astype(F32).astype(BF16)
             for b in range(OUTER)
         ]
-        for at in range(0, width, band):
+        for at in range(0, window.shape[1], band):
             lanes = slice(at, at + band)
             masked = jnp.concatenate([window[:, lanes] * hit for hit in hits], axis=1)
             columns = jnp.concatenate([weights[p][b, lanes, :] for b in range(OUTER)], axis=1)
             value = lax.dot_general(masked, columns, (((1,), (1,)), ((), ())), preferred_element_type=F32)
-            if p:
-                value = value + rest_ref[:, lanes]
-            elif begun:
-                value = value + before_ref[:, lanes]
-            rest_ref[:, lanes] = value
-            if begun and p == npieces - 1:
-                for (low, high), sent_ref in zip(splits, sents):
-                    if low <= at < high:
-                        sent_ref[:, at - low : at - low + band] = value.astype(BF16)
-                total = total + value * value
-    if begun:
-        for outer in range(OUTER):
-            squares_ref[outer : outer + 1, :] = jnp.sum(
-                total[outer * count : (outer + 1) * count].T, axis=0, keepdims=True
-            )
-
-
-def resample(outer, bins, names, windows, weights, splits, band, begun=None):
+            if p or begun:
+                value = value + value_ref[:, lanes]
+            value_ref[:, lanes] = value
+
+
+def begin_kernel(aways, npieces, band, bins_ref, names_ref, *refs):
+    windows, weights = refs[: len(aways)], refs[len(aways) : len(aways) + npieces]
+    value_ref, window, named_ref = refs[len(aways) + npieces :]
+    names = [names_ref[away : away + 1, :].astype(F32) for away in aways]
+    masked_rest(windows, names, bins_ref, weights, band, window, named_ref, value_ref, False)
+
+
+def begin_rest(bins, names, aways, windows, weights, band):
+    count, width = windows[0].shape
+    rows = len(aways) * count
+    return call(
+        functools.partial(begin_kernel, aways, len(weights), band),
+        jax.ShapeDtypeStruct((rows, width), F32),
+        [SMEM] + [VMEM] * (1 + len(aways) + len(weights)),
+        (bins, names, *windows, *weights),
+        [pltpu.VMEM((rows, width), BF16), pltpu.VMEM((rows, band), F32)],
+    )
+
+
+def end_kernel(nbegun, npieces, band, outer_ref, bins_ref, names_ref, *refs):
+    windows, begun, weights = refs[:OUTER], refs[OUTER : OUTER + nbegun], refs[OUTER + nbegun : OUTER + nbegun + npieces]
+    rest_ref, sent_ref, squares_ref, window, named_ref, value_ref = refs[OUTER + nbegun + npieces :]
+    count, width = windows[0].shape
+    row = 0
+    for part in begun:
+        value_ref[row : row + part.shape[0], :] = part[...]
+        row += part.shape[0]
+    names = [names_ref[away : away + 1, :].astype(F32) for away in range(OUTER)]
+    masked_rest(windows, names, bins_ref, weights, band, window, named_ref, value_ref, True)
+    for away in range(OUTER):
+        own = slice(away * count, (away + 1) * count)
+        place = outer_ref[0] ^ away
+        rows = pl.ds(pl.multiple_of(place * count, count), count)
+        total = jnp.zeros((count, band), F32)
+        for at in range(0, width, band):
+            value = value_ref[own, at : at + band]
+            rest_ref[rows, at : at + band] = value
+            sent_ref[rows, at : at + band] = value.astype(BF16)
+            total = total + value * value
+        squares_ref[pl.ds(place, 1), :] = jnp.sum(total.T, axis=0, keepdims=True)
+
+
+def end_rest(outer, bins, names, windows, begun, weights, band):
     count, width = windows[0].shape
     rows = OUTER * count
-    npieces = len(weights)
-    rest = jax.ShapeDtypeStruct((rows, width), F32)
-    last = begun is not None
-    sents = tuple(jax.ShapeDtypeStruct((rows, high - low), BF16) for low, high in splits)
-    return call(
-        functools.partial(rest_kernel, npieces, splits, band, int(last)),
-        (rest, *sents, jax.ShapeDtypeStruct((OUTER, count), F32)) if last else rest,
-        [SMEM, SMEM] + [VMEM] * (1 + OUTER + npieces + last),
-        (outer, bins, names, *windows, *weights) + ((begun,) if last else ()),
-        [pltpu.VMEM((rows, width), BF16), pltpu.VMEM((rows, band), F32)],
-        aliases={3 + OUTER + npieces: 0} if last else None,
+    return call(
+        functools.partial(end_kernel, len(begun), len(weights), band),
+        (
+            jax.ShapeDtypeStruct((rows, width), F32),
+            jax.ShapeDtypeStruct((rows, width), BF16),
+            jax.ShapeDtypeStruct((OUTER, count), F32),
+        ),
+        [SMEM, SMEM] + [VMEM] * (1 + OUTER + len(begun) + len(weights)),
+        (outer, bins, names, *windows, *begun, *weights),
+        [pltpu.VMEM((rows, width), BF16), pltpu.VMEM((rows, band), F32), pltpu.VMEM((rows, width), F32)],
     )
 
 
@@ -370,21 +396,27 @@
     bit = inner // 2
     weights = [mixed, swap(mixed, bit)]
     mine = me ^ (jnp.arange(OUTER, dtype=I32) * inner)
-    ids = [mine, mine ^ bit]
-    weights, arrived = lax.optimization_barrier((weights, arrived))
+    near, bits = [mixed], []
     while bit > 1:
         bit //= 2
-        weights = weights + [swap(piece, bit) for piece in weights]
-        ids = ids + [piece ^ bit for piece in ids]
-    early, late = jnp.concatenate(ids[:2]), jnp.concatenate(ids[2:])
-    begun = resample(outer1, early, names, arrived, weights[:2], [(0, width)], band)
-    rest, sent, squares = resample(outer1, late, names, arrived, weights[2:], [(0, width)], band, begun)
+        bits.append(bit)
+        near = near + [swap(piece, bit) for piece in near]
+    near_bins = [mine]
+    for bit in bits:
+        near_bins = near_bins + [piece ^ bit for piece in near_bins]
+    far_bins = jnp.concatenate([piece ^ (inner // 2) for piece in near_bins])
+    near_bins = jnp.concatenate(near_bins)
+    begun = [begin_rest(near_bins, names, (0, 1), arrived[:2], near, band)]
+    across, begun[0], *arrived = lax.optimization_barrier((weights[1], begun[0], *arrived))
+    begun.append(begin_rest(near_bins, names, (2, 3), arrived[2:], near, band))
+    far = [across]
+    for bit in bits:
+        far = far + [swap(piece, bit) for piece in far]
+    rest, sent, squares = end_rest(outer1, far_bins, names, arrived, begun, far, band)
 
     total = squares
-    bit = inner
-    while bit < n:
-        total = total + swap(total, bit)
-        bit *= 2
+    for away in range(1, OUTER):
+        total = total + swap(squares, away * inner)
     scale = lax.rsqrt(total / nrest + 1e-06)
     factor = scale * scale / (count * n)
     scaled = call(scale_kernel, jax.ShapeDtypeStruct(rest.shape, BF16), [VMEM, VMEM], (rest, factor))
@@ -401,16 +433,16 @@
 
     q1 = q.reshape(1)
     send0, held0 = reduce(*product(q1, scaled, sent, inner))
+    first = step(sent, 1)
+    first, send0 = lax.optimization_barrier((first, send0))
     got0 = finish(send0)
-    first = step(sent, 1)
-    first, got0 = lax.optimization_barrier((first, got0))
     second = step(first, 1)
     sendm, heldm = reduce(*product(q1, first, scaled, inner))
     sendm, first = lax.optimization_barrier((sendm, first))
     gotm = finish(sendm)
     send1, held1 = reduce(*product(q1, scaled, first, inner))
     got1 = finish(send1)
-    second, got1, gotm = lax.optimization_barrier((second, got1, gotm))
+    second, got0, got1, gotm = lax.optimization_barrier((second, got0, got1, gotm))
     back = step((heldm + gotm.astype(F32)).astype(BF16), -1)
     send2, held2 = reduce(*product(q1, scaled, second, inner))
     got2 = finish(send2)

time: 106 us -> 107 us (level)
  starting transfers between devices: 25 us -> 30.3 us
  waiting for transfers between devices: 53.2 us -> 48.3 us
    ppermute x3, waiting for transfers between devices: 13.9 us -> 6.38 us  [step(): lax.ppermute(array, 'spec', [(i, (i + outers * inner) % n) for i in range...]
    ppermute x3, starting transfers between devices: 1.08 us -> 4.99 us  [step(): lax.ppermute(array, 'spec', [(i, (i + outers * inner) % n) for i in range...]
    ppermute x24 -> x25, waiting for transfers between devices: 39.3 us -> 42 us  [swap(): return lax.ppermute(array, 'spec', [(i, i ^ bit) for i in range(n)])]
    ppermute x24 -> x25, starting transfers between devices: 23.9 us -> 25.3 us  [swap(): return lax.ppermute(array, 'spec', [(i, i ^ bit) for i in range(n)])]
    pallas_call x14 -> x15, Pallas kernels: 21.3 us -> 21.4 us  [call(): pl.pallas_call(kernel, out_shape=out_shape, in_specs=in_specs, out_specs=...]
  transfers between devices with their start and end apart: 27 -> 28, of which waited for: 17 -> 16; matrix products, arithmetic and copies ran while one was open for 2% -> 1% of each run, Pallas kernels for 17% -> 18%
where the time goes in v9:
time: 107 us; the launch traced here: 106 us
  waiting for transfers between devices  48.3 us (45%)
  starting transfers between devices  30.3 us (28%)
  Pallas kernels  24.3 us (23%)
  local copies, waits for them, and re-layouts  1.95 us (2%)
  other arithmetic  1.26 us (1%)
    ppermute x25, waiting for transfers between devices, swap(): return lax.ppermute(array, 'spec', [(i, i ^ bit) for i in range(n)])  42 us
    ppermute x25, starting transfers between devices, swap(): return lax.ppermute(array, 'spec', [(i, i ^ bit) for i in range(n)])  25.3 us
    pallas_call x15, Pallas kernels, call(): pl.pallas_call(kernel, out_shape=out_shape, in_specs=in_specs, out_specs=...  21.4 us
    ppermute x3, waiting for transfers between devices, step(): lax.ppermute(array, 'spec', [(i, (i + outers * inner) % n) for i in range...  6.38 us
    ppermute x3, starting transfers between devices, step(): lax.ppermute(array, 'spec', [(i, (i + outers * inner) % n) for i in range...  4.99 us
    pallas_call x2, Pallas kernels, place(): pl.pallas_call(functools.partial(place_kernel, slots, last), out_shape=ja...  2.96 us
  transfers between devices with their start and end apart: 28, of which 16 were waited for; matrix products, arithmetic and copies ran while one was open for 1% of the time, Pallas kernels for 18%

profile of v9, /device:TPU:0, one launch (start us, length us, event | category | flops | bytes accessed | tf_op | source)
XLA Modules:
  0.0 106.4 jit_solution(2125215474848474056)
XLA Ops:
  0.0 0.8 pad_add_fusion.3
  0.8 3.0 %collective-permute-start = (s32[148]{0:T(256)S(1)}, s32[148]{0:T(256)S(1)}, u32[]{:S(2)}, u32[]{:S(2)}) collective-permute-start(s32[148]{0:T(256)S(1)} %pad_add_fusion.3), channel_id=1, source_target_pairs={{0,4},{1,5},{2,6},{3,7},{4,0},{5,1},{6,2},{7,3},{8,12},{9,13},{10,... | collective-permute-start | bytes 1784 | tf_op jit(solution)/shard_map/ppermute | solution.py:360
  3.9 2.6 %collective-permute-start.1 = (s32[148]{0:T(256)S(1)}, s32[148]{0:T(256)S(1)}, u32[]{:S(2)}, u32[]{:S(2)}) collective-permute-start(s32[148]{0:T(256)S(1)} %pad_add_fusion.3), channel_id=1, source_target_pairs={{0,8},{1,9},{2,10},{3,11},{4,12},{5,13},{6,14},{7,15},{8,0},{9,1},... | collective-permute-start | bytes 1784 | tf_op jit(solution)/shard_map/ppermute | solution.py:360
  6.5 1.2 %dynamic-slice_bitcast_fusion = (bf16[640,128]{1,0:T(8,128)(2,1)S(1)}, bf16[640,128]{1,0:T(8,128)(2,1)S(1)}, bf16[640,128]{1,0:T(8,128)(2,1)S(1)}, bf16[640,128]{1,0:T(8,128)(2,1)S(1)}) fusion(bf16[4,640,128]{2,1,0:T(8,128)(2,1)} %bitcast.48, s32[]{:T(128)S(6)} %select_n.41, s32[]{:T(128)S(6)} %select_n.40, s32[]{:T(128)S(6)} %select_n.39, s32[]{:T(128)S(6)} %select_n.38), kind=kLoop, calls=%fused_computation.3 | loop fusion | bytes 1310736 | tf_op jit(solution)/shard_map/jit(dynamic_index_in_dim)/squeeze | solution.py:380
  7.7 0.7 collective-permute-done.1
  8.3 3.5 %collective-permute-done.2 = s32[148]{0:T(256)S(1)} collective-permute-done((s32[148]{0:T(256)S(1)}, s32[148]{0:T(256)S(1)}, u32[]{:S(2)}, u32[]{:S(2)}) %collective-permute-start.2) | collective-permute-done | bytes 624 | tf_op jit(solution)/shard_map/ppermute | solution.py:360
  11.8 0.1 collective-permute-start.6
  11.9 0.1 collective-permute-start.3
  12.0 0.6 collective-permute-start.4
  12.6 3.8 %collective-permute-start.5 = (bf16[640,128]{1,0:T(8,128)(2,1)S(1)}, bf16[640,128]{1,0:T(8,128)(2,1)S(1)}, u32[]{:S(2)}, u32[]{:S(2)}) collective-permute-start(bf16[640,128]{1,0:T(8,128)(2,1)S(1)} %get-tuple-element.103), channel_id=1, source_target_pairs={{0,12},{1,13},{2,14},{3,15},{4,8},{5,9},{6,10},{7,11},{8,4},{9,5},... | collective-permute-start | bytes 491528 | tf_op jit(solution)/shard_map/ppermute | solution.py:360
  16.4 1.5 %collective-permute-start.7 = (s32[4,2,20]{2,0,1:T(4,128)S(1)}, s32[4,2,20]{2,0,1:T(4,128)S(1)}, u32[]{:S(2)}, u32[]{:S(2)}) collective-permute-start(s32[4,2,20]{2,0,1:T(4,128)S(1)} %pad_add_fusion.2), channel_id=1, source_target_pairs={{0,2},{1,3},{2,0},{3,1},{4,6},{5,7},{6,4},{7,5},{8,10},{9,11},{10,... | collective-permute-start | bytes 1928 | tf_op jit(solution)/shard_map/ppermute | solution.py:360
  17.9 0.1 pad_add_fusion.5.me_ref
  18.0 0.7 copy-done.1
  18.6 0.2 shard_map.55
  18.9 7.2 %shard_map.56.smoothed_ref = bf16[128,3968]{1,0:T(8,128)(2,1)S(1)} custom-call(bf16[128,3968]{1,0:T(8,128)(2,1)S(1)} %copy-done, bf16[11,128,3968]{2,1,0:T(8,128)(2,1)} %bitcast.46), custom_call_target="tpu_custom_call" | custom-call | flops 1 | bytes 1 | tf_op jit(solution)/shard_map/pallas_call | solution.py:20
  26.2 4.7 %shard_map.57 = (bf16[128,640]{1,0:T(8,128)(2,1)S(1)}, bf16[128,640]{1,0:T(8,128)(2,1)S(1)}, bf16[128,640]{1,0:T(8,128)(2,1)S(1)}, bf16[128,640]{1,0:T(8,128)(2,1)S(1)}) custom-call(s32[2]{0:T(128)S(1)} %pad_add_fusion.5.me_ref, s32[2,128]{1,0:T(2,128)S(1)} %get-tuple-element.54.groups_ref, s32[16,20]{1,0:T(8,128)S(1)} %get-tuple-element.108.starts_ref, ...), custom_call_target="tpu_custom_call" | custom-call | flops 1 | bytes 1 | tf_op jit(solution)/shard_map/pallas_call | solution.py:20
  30.9 0.1 pad_maximum_fusion.refs_2_
  31.0 0.1 collective-permute-start.10
  31.1 0.6 collective-permute-start.8
  31.7 0.6 collective-permute-start.9
  32.3 3.7 %collective-permute-start.12 = (bf16[128,640]{1,0:T(8,128)(2,1)S(1)}, bf16[128,640]{1,0:T(8,128)(2,1)S(1)}, u32[]{:S(2)}, u32[]{:S(2)}) collective-permute-start(bf16[128,640]{1,0:T(8,128)(2,1)S(1)} %get-tuple-element.69), channel_id=1, source_target_pairs={{0,12},{1,13},{2,14},{3,15},{4,8},{5,9},{6,10},{7,11},{8,4},{9,5},... | collective-permute-start | bytes 491528 | tf_op jit(solution)/shard_map/ppermute | solution.py:360
  36.1 0.1 pad_add_fusion.6.bins_ref
  36.2 0.1 slice.8.names_ref
  36.2 4.1 %collective-permute-done.9.refs_1_ = bf16[128,640]{1,0:T(8,128)(2,1)S(1)} collective-permute-done((bf16[128,640]{1,0:T(8,128)(2,1)S(1)}, bf16[128,640]{1,0:T(8,128)(2,1)S(1)}, u32[]{:S(2)}, u32[]{:S(2)}) %collective-permute-start.9) | collective-permute-done | bytes 163872 | tf_op jit(solution)/shard_map/ppermute | solution.py:360
  40.4 1.5 %shard_map.58.refs_4_ = f32[256,640]{1,0:T(8,128)S(1)} custom-call(s32[8]{0:T(128)S(1)} %pad_add_fusion.6.bins_ref, s32[4,128]{1,0:T(4,128)S(1)} %slice.8.names_ref, bf16[128,640]{1,0:T(8,128)(2,1)S(1)} %get-tuple-element.70.refs_0_, bf16[128,640]{1,0:T(8,128)(2,1)S(1)} %collective-permute-done.9.refs_1_, bf16[4,640,128]{2,1,0:T(8,128)(2,1)S(1)} %pad_maximum_fusion.refs_2_, ...), custom_call_target="tpu_custom_call" | custom-call | flops 1 | bytes 1 | tf_op jit(solution)/shard_map/pallas_call | solution.py:20
  41.9 5.4 %collective-permute-done.11.refs_0_.refs_2_ = bf16[128,640]{1,0:T(8,128)(2,1)S(1)} collective-permute-done((bf16[128,640]{1,0:T(8,128)(2,1)S(1)}, bf16[128,640]{1,0:T(8,128)(2,1)S(1)}, u32[]{:S(2)}, u32[]{:S(2)}) %collective-permute-start.11) | collective-permute-done | bytes 163872 | tf_op jit(solution)/shard_map/ppermute | solution.py:360
  47.3 0.9 collective-permute-done.8.refs_6_
  48.3 0.1 pad_add_fusion.4.bins_ref
  48.4 1.5 %shard_map.59.refs_5_ = f32[256,640]{1,0:T(8,128)S(1)} custom-call(s32[8]{0:T(128)S(1)} %pad_add_fusion.6.bins_ref, s32[4,128]{1,0:T(4,128)S(1)} %slice.8.names_ref, bf16[128,640]{1,0:T(8,128)(2,1)S(1)} %collective-permute-done.11.refs_0_.refs_2_, bf16[128,640]{1,0:T(8,128)(2,1)S(1)} %collective-permute-done.12.refs_1_.refs_3_, ...), custom_call_target="tpu_custom_call" | custom-call | flops 1 | bytes 1 | tf_op jit(solution)/shard_map/pallas_call | solution.py:20
  49.9 0.5 collective-permute-done.13.refs_7_
  50.4 2.3 %shard_map.60 = (f32[512,640]{1,0:T(8,128)S(1)}, bf16[512,640]{1,0:T(8,128)(2,1)S(1)}, f32[4,128]{1,0:T(4,128)S(1)}) custom-call(s32[1]{0:T(128)} %bitcast.1.outer_ref, s32[8]{0:T(128)S(1)} %pad_add_fusion.4.bins_ref, s32[4,128]{1,0:T(4,128)S(1)} %slice.8.names_ref, bf16[128,640]{1,0:T(8,128)(2,1)S(1)} %get-tuple-element.70.refs_0_, ...), custom_call_target="tpu_custom_call" | custom-call | flops 1 | bytes 1 | tf_op jit(solution)/shard_map/pallas_call | solution.py:20
  52.7 2.1 %collective-permute-start.17 = (bf16[512,640]{1,0:T(8,128)(2,1)S(1)}, bf16[512,640]{1,0:T(8,128)(2,1)S(1)}, u32[]{:S(2)}, u32[]{:S(2)}) collective-permute-start(bf16[512,640]{1,0:T(8,128)(2,1)S(1)} %get-tuple-element.78.wide_ref), channel_id=1, source_target_pairs={{0,4},{1,5},{2,6},{3,7},{4,8},{5,9},{6,10},{7,11},{8,12},{9,13},{1... | collective-permute-start | bytes 1966088 | tf_op jit(solution)/shard_map/ppermute | solution.py:363
  54.8 0.6 collective-permute-start.14
  55.4 1.7 %collective-permute-start.15 = (f32[4,128]{1,0:T(4,128)S(1)}, f32[4,128]{1,0:T(4,128)S(1)}, u32[]{:S(2)}, u32[]{:S(2)}) collective-permute-start(f32[4,128]{1,0:T(4,128)S(1)} %get-tuple-element.77), channel_id=1, source_target_pairs={{0,8},{1,9},{2,10},{3,11},{4,12},{5,13},{6,14},{7,15},{8,0},{9,1},... | collective-permute-start | bytes 6152 | tf_op jit(solution)/shard_map/ppermute | solution.py:360
  57.1 2.1 %collective-permute-start.16 = (f32[4,128]{1,0:T(4,128)S(1)}, f32[4,128]{1,0:T(4,128)S(1)}, u32[]{:S(2)}, u32[]{:S(2)}) collective-permute-start(f32[4,128]{1,0:T(4,128)S(1)} %get-tuple-element.77), channel_id=1, source_target_pairs={{0,12},{1,13},{2,14},{3,15},{4,8},{5,9},{6,10},{7,11},{8,4},{9,5},... | collective-permute-start | bytes 6152 | tf_op jit(solution)/shard_map/ppermute | solution.py:360
  59.2 10.0 %collective-permute-done.14 = f32[4,128]{1,0:T(4,128)S(1)} collective-permute-done((f32[4,128]{1,0:T(4,128)S(1)}, f32[4,128]{1,0:T(4,128)S(1)}, u32[]{:S(2)}, u32[]{:S(2)}) %collective-permute-start.14) | collective-permute-done | bytes 2080 | tf_op jit(solution)/shard_map/ppermute | solution.py:360
  69.2 2.3 %collective-permute-done.16 = f32[4,128]{1,0:T(4,128)S(1)} collective-permute-done((f32[4,128]{1,0:T(4,128)S(1)}, f32[4,128]{1,0:T(4,128)S(1)}, u32[]{:S(2)}, u32[]{:S(2)}) %collective-permute-start.16) | collective-permute-done | bytes 2080 | tf_op jit(solution)/shard_map/ppermute | solution.py:360
  71.5 0.2 shard_map.61.tall_ref.wide_ref
  71.7 0.8 shard_map.62
  72.6 1.7 %collective-permute-done.18.got_ref = bf16[2,160,640]{2,1,0:T(8,128)(2,1)S(1)} collective-permute-done((bf16[2,160,640]{2,1,0:T(8,128)(2,1)S(1)}, bf16[2,160,640]{2,1,0:T(8,128)(2,1)S(1)}, u32[]{:S(2)}, u32[]{:S(2)}) %collective-permute-start.18) | collective-permute-done | bytes 409632 | tf_op jit(solution)/shard_map/ppermute | solution.py:360
  74.3 0.1 shard_map.63
  74.4 0.8 shard_map.64
  75.2 0.2 collective-permute-start.21
  75.4 0.6 collective-permute-start.19
  76.0 1.1 collective-permute-done.21.got_ref
  77.0 0.1 shard_map.65
  77.1 0.8 shard_map.66
  78.0 0.2 collective-permute-start.22
  78.2 0.5 collective-permute-start.20
  78.7 1.5 %collective-permute-start.24 = (bf16[1,160,640]{2,1,0:T(8,128)(2,1)S(1)}, bf16[1,160,640]{2,1,0:T(8,128)(2,1)S(1)}, u32[]{:S(2)}, u32[]{:S(2)}) collective-permute-start(bf16[1,160,640]{2,1,0:T(8,128)(2,1)S(1)} %get-tuple-element.91), channel_id=1, source_target_pairs={{0,2},{1,3},{2,0},{3,1},{4,6},{5,7},{6,4},{7,5},{8,10},{9,11},{10,... | collective-permute-start | bytes 614408 | tf_op jit(solution)/shard_map/ppermute | solution.py:360
  80.2 0.1 shard_map.67
  80.3 0.6 collective-permute-start.23
  80.9 5.2 %collective-permute-done.20 = bf16[1,160,640]{2,1,0:T(8,128)(2,1)S(1)} collective-permute-done((bf16[1,160,640]{2,1,0:T(8,128)(2,1)S(1)}, bf16[1,160,640]{2,1,0:T(8,128)(2,1)S(1)}, u32[]{:S(2)}, u32[]{:S(2)}) %collective-permute-start.20) | collective-permute-done | bytes 204832 | tf_op jit(solution)/shard_map/ppermute | solution.py:360
  86.1 4.4 %collective-permute-done.24 = bf16[1,160,640]{2,1,0:T(8,128)(2,1)S(1)} collective-permute-done((bf16[1,160,640]{2,1,0:T(8,128)(2,1)S(1)}, bf16[1,160,640]{2,1,0:T(8,128)(2,1)S(1)}, u32[]{:S(2)}, u32[]{:S(2)}) %collective-permute-start.24) | collective-permute-done | bytes 204832 | tf_op jit(solution)/shard_map/ppermute | solution.py:360
  90.5 3.8 %collective-permute-done.19.wide_ref = bf16[512,640]{1,0:T(8,128)(2,1)S(1)} collective-permute-done((bf16[512,640]{1,0:T(8,128)(2,1)S(1)}, bf16[512,640]{1,0:T(8,128)(2,1)S(1)}, u32[]{:S(2)}, u32[]{:S(2)}) %collective-permute-start.19) | collective-permute-done | bytes 655392 | tf_op jit(solution)/shard_map/ppermute | solution.py:363
  94.3 0.8 shard_map.68
  95.1 0.1 collective-permute-start.25
  95.2 2.3 %collective-permute-start.27 = (bf16[160,640]{1,0:T(8,128)(2,1)S(1)}, bf16[160,640]{1,0:T(8,128)(2,1)S(1)}, u32[]{:S(2)}, u32[]{:S(2)}) collective-permute-start(bf16[160,640]{1,0:T(8,128)(2,1)S(1)} %fusion), channel_id=1, source_target_pairs={{0,12},{1,13},{2,14},{3,15},{4,0},{5,1},{6,2},{7,3},{8,4},{9,5},{1... | collective-permute-start | bytes 614408 | tf_op jit(solution)/shard_map/ppermute | solution.py:363
  97.5 0.1 shard_map.69
  97.6 1.0 collective-permute-start.26
  98.7 1.5 %shard_map.70.refs_4_ = f32[160,2560]{1,0:T(8,128)} custom-call(s32[4]{0:T(128)S(1)} %and_select_fusion.at_ref, f32[160,640]{1,0:T(8,128)S(1)} %bitcast.38, bf16[160,640]{1,0:T(8,128)(2,1)S(1)} %bitcast.41, f32[160,640]{1,0:T(8,128)S(1)} %bitcast.39, bf16[160,640]{1,0:T(8,128)(2,1)S(1)} %bitcast.42), custom_call_target="tpu_custom_call" | custom-call | flops 1 | bytes 1 | tf_op jit(solution)/shard_map/pallas_call | solution.py:334
  100.2 2.6 %collective-permute-done.27.refs_2_ = bf16[160,640]{1,0:T(8,128)(2,1)S(1)} collective-permute-done((bf16[160,640]{1,0:T(8,128)(2,1)S(1)}, bf16[160,640]{1,0:T(8,128)(2,1)S(1)}, u32[]{:S(2)}, u32[]{:S(2)}) %collective-permute-start.27) | collective-permute-done | bytes 204832 | tf_op jit(solution)/shard_map/ppermute | solution.py:363
  102.8 2.1 %collective-permute-done.26 = bf16[1,160,640]{2,1,0:T(8,128)(2,1)S(1)} collective-permute-done((bf16[1,160,640]{2,1,0:T(8,128)(2,1)S(1)}, bf16[1,160,640]{2,1,0:T(8,128)(2,1)S(1)}, u32[]{:S(2)}, u32[]{:S(2)}) %collective-permute-start.26) | collective-permute-done | bytes 204832 | tf_op jit(solution)/shard_map/ppermute | solution.py:360
  104.9 1.5 %shard_map.71 = f32[160,2560]{1,0:T(8,128)} custom-call(s32[4]{0:T(128)S(1)} %and_select_fusion.at_ref, f32[160,640]{1,0:T(8,128)S(1)} %bitcast.40, bf16[160,640]{1,0:T(8,128)(2,1)S(1)} %bitcast.43, bf16[160,640]{1,0:T(8,128)(2,1)S(1)} %collective-permute-done.27.refs_2_, ...), custom_call_target="tpu_custom_call", output_to_operand_aliasing={{}: (5, {})} | custom-call | flops 1 | bytes 1 | tf_op jit(solution)/shard_map/pallas_call | solution.py:334
  (32 shorter events, 0.3 us)
Async XLA Ops:
  0.0 18.9 %copy-start = (bf16[128,3968]{1,0:T(8,128)(2,1)S(1)}, bf16[128,3968]{1,0:T(8,128)(2,1)}, u32[]{:S(2)}) copy-start(bf16[128,3968]{1,0:T(8,128)(2,1)} %flux_ref) | copy-start | bytes 3047428
  0.8 6.8 %collective-permute-start = (s32[148]{0:T(256)S(1)}, s32[148]{0:T(256)S(1)}, u32[]{:S(2)}, u32[]{:S(2)}) collective-permute-start(s32[148]{0:T(256)S(1)} %pad_add_fusion.3), channel_id=1, source_target_pairs={{0,4},{1,5},{2,6},{3,7},{4,0},{5,1},{6,2},{7,3},{8,12},{9,13},{10,... | collective-permute-start | bytes 1784 | tf_op jit(solution)/shard_map/ppermute | solution.py:360
  3.9 4.5 %collective-permute-start.1 = (s32[148]{0:T(256)S(1)}, s32[148]{0:T(256)S(1)}, u32[]{:S(2)}, u32[]{:S(2)}) collective-permute-start(s32[148]{0:T(256)S(1)} %pad_add_fusion.3), channel_id=1, source_target_pairs={{0,8},{1,9},{2,10},{3,11},{4,12},{5,13},{6,14},{7,15},{8,0},{9,1},... | collective-permute-start | bytes 1784 | tf_op jit(solution)/shard_map/ppermute | solution.py:360
  6.4 5.4 %collective-permute-start.2 = (s32[148]{0:T(256)S(1)}, s32[148]{0:T(256)S(1)}, u32[]{:S(2)}, u32[]{:S(2)}) collective-permute-start(s32[148]{0:T(256)S(1)} %pad_add_fusion.3), channel_id=1, source_target_pairs={{0,12},{1,13},{2,14},{3,15},{4,8},{5,9},{6,10},{7,11},{8,4},{9,5},... | collective-permute-start | bytes 1784 | tf_op jit(solution)/shard_map/ppermute | solution.py:360
  11.8 4.5 %collective-permute-start.6 = (s32[4,1,20]{2,0,1:T(4,128)S(1)}, s32[4,1,20]{2,0,1:T(4,128)S(1)}, u32[]{:S(2)}, u32[]{:S(2)}) collective-permute-start(s32[4,1,20]{2,0,1:T(4,128)S(1)} %slice_bitcast_fusion), channel_id=1, source_target_pairs={{0,1},{1,0},{2,3},{3,2},{4,5},{5,4},{6,7},{7,6},{8,9},{9,8},{10,11... | collective-permute-start | bytes 968 | tf_op jit(solution)/shard_map/ppermute | solution.py:360
  11.9 19.0 %collective-permute-start.3 = (bf16[640,128]{1,0:T(8,128)(2,1)S(1)}, bf16[640,128]{1,0:T(8,128)(2,1)S(1)}, u32[]{:S(2)}, u32[]{:S(2)}) collective-permute-start(bf16[640,128]{1,0:T(8,128)(2,1)S(1)} %get-tuple-element.105), channel_id=1, source_target_pairs={{0,4},{1,5},{2,6},{3,7},{4,0},{5,1},{6,2},{7,3},{8,12},{9,13},{10,... | collective-permute-start | bytes 491528 | tf_op jit(solution)/shard_map/ppermute | solution.py:360
  12.0 18.9 %collective-permute-start.4 = (bf16[640,128]{1,0:T(8,128)(2,1)S(1)}, bf16[640,128]{1,0:T(8,128)(2,1)S(1)}, u32[]{:S(2)}, u32[]{:S(2)}) collective-permute-start(bf16[640,128]{1,0:T(8,128)(2,1)S(1)} %get-tuple-element.104), channel_id=1, source_target_pairs={{0,8},{1,9},{2,10},{3,11},{4,12},{5,13},{6,14},{7,15},{8,0},{9,1},... | collective-permute-start | bytes 491528 | tf_op jit(solution)/shard_map/ppermute | solution.py:360
  12.6 18.4 %collective-permute-start.5 = (bf16[640,128]{1,0:T(8,128)(2,1)S(1)}, bf16[640,128]{1,0:T(8,128)(2,1)S(1)}, u32[]{:S(2)}, u32[]{:S(2)}) collective-permute-start(bf16[640,128]{1,0:T(8,128)(2,1)S(1)} %get-tuple-element.103), channel_id=1, source_target_pairs={{0,12},{1,13},{2,14},{3,15},{4,8},{5,9},{6,10},{7,11},{8,4},{9,5},... | collective-permute-start | bytes 491528 | tf_op jit(solution)/shard_map/ppermute | solution.py:360
  16.4 9.8 %collective-permute-start.7 = (s32[4,2,20]{2,0,1:T(4,128)S(1)}, s32[4,2,20]{2,0,1:T(4,128)S(1)}, u32[]{:S(2)}, u32[]{:S(2)}) collective-permute-start(s32[4,2,20]{2,0,1:T(4,128)S(1)} %pad_add_fusion.2), channel_id=1, source_target_pairs={{0,2},{1,3},{2,0},{3,1},{4,6},{5,7},{6,4},{7,5},{8,10},{9,11},{10,... | collective-permute-start | bytes 1928 | tf_op jit(solution)/shard_map/ppermute | solution.py:360
  18.0 0.7 copy-start.1
  31.0 9.3 %collective-permute-start.10 = (bf16[4,640,128]{2,1,0:T(8,128)(2,1)S(1)}, bf16[4,640,128]{2,1,0:T(8,128)(2,1)S(1)}, u32[]{:S(2)}, u32[]{:S(2)}) collective-permute-start(bf16[4,640,128]{2,1,0:T(8,128)(2,1)S(1)} %pad_maximum_fusion.refs_2_), channel_id=1, source_target_pairs={{0,1},{1,0},{2,3},{3,2},{4,5},{5,4},{6,7},{7,6},{8,9},{9,8},{10,11... | collective-permute-start | bytes 1966088 | tf_op jit(solution)/shard_map/ppermute | solution.py:360
  31.1 17.1 %collective-permute-start.8 = (bf16[4,640,128]{2,1,0:T(8,128)(2,1)S(1)}, bf16[4,640,128]{2,1,0:T(8,128)(2,1)S(1)}, u32[]{:S(2)}, u32[]{:S(2)}) collective-permute-start(bf16[4,640,128]{2,1,0:T(8,128)(2,1)S(1)} %pad_maximum_fusion.refs_2_), channel_id=1, source_target_pairs={{0,2},{1,3},{2,0},{3,1},{4,6},{5,7},{6,4},{7,5},{8,10},{9,11},{10,... | collective-permute-start | bytes 1966088 | tf_op jit(solution)/shard_map/ppermute | solution.py:360
  31.7 8.7 %collective-permute-start.9 = (bf16[128,640]{1,0:T(8,128)(2,1)S(1)}, bf16[128,640]{1,0:T(8,128)(2,1)S(1)}, u32[]{:S(2)}, u32[]{:S(2)}) collective-permute-start(bf16[128,640]{1,0:T(8,128)(2,1)S(1)} %get-tuple-element.67), channel_id=1, source_target_pairs={{0,4},{1,5},{2,6},{3,7},{4,0},{5,1},{6,2},{7,3},{8,12},{9,13},{10,... | collective-permute-start | bytes 491528 | tf_op jit(solution)/shard_map/ppermute | solution.py:360
  32.3 15.0 %collective-permute-start.11 = (bf16[128,640]{1,0:T(8,128)(2,1)S(1)}, bf16[128,640]{1,0:T(8,128)(2,1)S(1)}, u32[]{:S(2)}, u32[]{:S(2)}) collective-permute-start(bf16[128,640]{1,0:T(8,128)(2,1)S(1)} %get-tuple-element.68), channel_id=1, source_target_pairs={{0,8},{1,9},{2,10},{3,11},{4,12},{5,13},{6,14},{7,15},{8,0},{9,1},... | collective-permute-start | bytes 491528 | tf_op jit(solution)/shard_map/ppermute | solution.py:360
  32.3 15.0 %collective-permute-start.12 = (bf16[128,640]{1,0:T(8,128)(2,1)S(1)}, bf16[128,640]{1,0:T(8,128)(2,1)S(1)}, u32[]{:S(2)}, u32[]{:S(2)}) collective-permute-start(bf16[128,640]{1,0:T(8,128)(2,1)S(1)} %get-tuple-element.69), channel_id=1, source_target_pairs={{0,12},{1,13},{2,14},{3,15},{4,8},{5,9},{6,10},{7,11},{8,4},{9,5},... | collective-permute-start | bytes 491528 | tf_op jit(solution)/shard_map/ppermute | solution.py:360
  48.3 2.1 %collective-permute-start.13 = (bf16[4,640,128]{2,1,0:T(8,128)(2,1)S(1)}, bf16[4,640,128]{2,1,0:T(8,128)(2,1)S(1)}, u32[]{:S(2)}, u32[]{:S(2)}) collective-permute-start(bf16[4,640,128]{2,1,0:T(8,128)(2,1)S(1)} %collective-permute-done.8.refs_6_), channel_id=1, source_target_pairs={{0,1},{1,0},{2,3},{3,2},{4,5},{5,4},{6,7},{7,6},{8,9},{9,8},{10,11... | collective-permute-start | bytes 1966088 | tf_op jit(solution)/shard_map/ppermute | solution.py:360
  52.7 21.7 %collective-permute-start.17 = (bf16[512,640]{1,0:T(8,128)(2,1)S(1)}, bf16[512,640]{1,0:T(8,128)(2,1)S(1)}, u32[]{:S(2)}, u32[]{:S(2)}) collective-permute-start(bf16[512,640]{1,0:T(8,128)(2,1)S(1)} %get-tuple-element.78.wide_ref), channel_id=1, source_target_pairs={{0,4},{1,5},{2,6},{3,7},{4,8},{5,9},{6,10},{7,11},{8,12},{9,13},{1... | collective-permute-start | bytes 1966088 | tf_op jit(solution)/shard_map/ppermute | solution.py:363
  54.8 14.4 %collective-permute-start.14 = (f32[4,128]{1,0:T(4,128)S(1)}, f32[4,128]{1,0:T(4,128)S(1)}, u32[]{:S(2)}, u32[]{:S(2)}) collective-permute-start(f32[4,128]{1,0:T(4,128)S(1)} %get-tuple-element.77), channel_id=1, source_target_pairs={{0,4},{1,5},{2,6},{3,7},{4,0},{5,1},{6,2},{7,3},{8,12},{9,13},{10,... | collective-permute-start | bytes 6152 | tf_op jit(solution)/shard_map/ppermute | solution.py:360
  55.4 13.8 %collective-permute-start.15 = (f32[4,128]{1,0:T(4,128)S(1)}, f32[4,128]{1,0:T(4,128)S(1)}, u32[]{:S(2)}, u32[]{:S(2)}) collective-permute-start(f32[4,128]{1,0:T(4,128)S(1)} %get-tuple-element.77), channel_id=1, source_target_pairs={{0,8},{1,9},{2,10},{3,11},{4,12},{5,13},{6,14},{7,15},{8,0},{9,1},... | collective-permute-start | bytes 6152 | tf_op jit(solution)/shard_map/ppermute | solution.py:360
  57.1 14.4 %collective-permute-start.16 = (f32[4,128]{1,0:T(4,128)S(1)}, f32[4,128]{1,0:T(4,128)S(1)}, u32[]{:S(2)}, u32[]{:S(2)}) collective-permute-start(f32[4,128]{1,0:T(4,128)S(1)} %get-tuple-element.77), channel_id=1, source_target_pairs={{0,12},{1,13},{2,14},{3,15},{4,8},{5,9},{6,10},{7,11},{8,4},{9,5},... | collective-permute-start | bytes 6152 | tf_op jit(solution)/shard_map/ppermute | solution.py:360
  72.5 1.8 %collective-permute-start.18 = (bf16[2,160,640]{2,1,0:T(8,128)(2,1)S(1)}, bf16[2,160,640]{2,1,0:T(8,128)(2,1)S(1)}, u32[]{:S(2)}, u32[]{:S(2)}) collective-permute-start(bf16[2,160,640]{2,1,0:T(8,128)(2,1)S(1)} %get-tuple-element.80), channel_id=1, source_target_pairs={{0,1},{1,0},{2,3},{3,2},{4,5},{5,4},{6,7},{7,6},{8,9},{9,8},{10,11... | collective-permute-start | bytes 1228808 | tf_op jit(solution)/shard_map/ppermute | solution.py:360
  75.2 1.8 %collective-permute-start.21 = (bf16[2,160,640]{2,1,0:T(8,128)(2,1)S(1)}, bf16[2,160,640]{2,1,0:T(8,128)(2,1)S(1)}, u32[]{:S(2)}, u32[]{:S(2)}) collective-permute-start(bf16[2,160,640]{2,1,0:T(8,128)(2,1)S(1)} %get-tuple-element.85), channel_id=1, source_target_pairs={{0,1},{1,0},{2,3},{3,2},{4,5},{5,4},{6,7},{7,6},{8,9},{9,8},{10,11... | collective-permute-start | bytes 1228808 | tf_op jit(solution)/shard_map/ppermute | solution.py:360
  75.4 18.8 %collective-permute-start.19 = (bf16[512,640]{1,0:T(8,128)(2,1)S(1)}, bf16[512,640]{1,0:T(8,128)(2,1)S(1)}, u32[]{:S(2)}, u32[]{:S(2)}) collective-permute-start(bf16[512,640]{1,0:T(8,128)(2,1)S(1)} %collective-permute-done.17.tall_ref.wide_ref), channel_id=1, source_target_pairs={{0,4},{1,5},{2,6},{3,7},{4,8},{5,9},{6,10},{7,11},{8,12},{9,13},{1... | collective-permute-start | bytes 1966088 | tf_op jit(solution)/shard_map/ppermute | solution.py:363
  78.0 2.2 %collective-permute-start.22 = (bf16[2,160,640]{2,1,0:T(8,128)(2,1)S(1)}, bf16[2,160,640]{2,1,0:T(8,128)(2,1)S(1)}, u32[]{:S(2)}, u32[]{:S(2)}) collective-permute-start(bf16[2,160,640]{2,1,0:T(8,128)(2,1)S(1)} %get-tuple-element.89), channel_id=1, source_target_pairs={{0,1},{1,0},{2,3},{3,2},{4,5},{5,4},{6,7},{7,6},{8,9},{9,8},{10,11... | collective-permute-start | bytes 1228808 | tf_op jit(solution)/shard_map/ppermute | solution.py:360
  78.2 7.9 %collective-permute-start.20 = (bf16[1,160,640]{2,1,0:T(8,128)(2,1)S(1)}, bf16[1,160,640]{2,1,0:T(8,128)(2,1)S(1)}, u32[]{:S(2)}, u32[]{:S(2)}) collective-permute-start(bf16[1,160,640]{2,1,0:T(8,128)(2,1)S(1)} %get-tuple-element.83), channel_id=1, source_target_pairs={{0,2},{1,3},{2,0},{3,1},{4,6},{5,7},{6,4},{7,5},{8,10},{9,11},{10,... | collective-permute-start | bytes 614408 | tf_op jit(solution)/shard_map/ppermute | solution.py:360
  78.7 11.8 %collective-permute-start.24 = (bf16[1,160,640]{2,1,0:T(8,128)(2,1)S(1)}, bf16[1,160,640]{2,1,0:T(8,128)(2,1)S(1)}, u32[]{:S(2)}, u32[]{:S(2)}) collective-permute-start(bf16[1,160,640]{2,1,0:T(8,128)(2,1)S(1)} %get-tuple-element.91), channel_id=1, source_target_pairs={{0,2},{1,3},{2,0},{3,1},{4,6},{5,7},{6,4},{7,5},{8,10},{9,11},{10,... | collective-permute-start | bytes 614408 | tf_op jit(solution)/shard_map/ppermute | solution.py:360
  80.3 14.0 %collective-permute-start.23 = (bf16[1,160,640]{2,1,0:T(8,128)(2,1)S(1)}, bf16[1,160,640]{2,1,0:T(8,128)(2,1)S(1)}, u32[]{:S(2)}, u32[]{:S(2)}) collective-permute-start(bf16[1,160,640]{2,1,0:T(8,128)(2,1)S(1)} %get-tuple-element.90), channel_id=1, source_target_pairs={{0,2},{1,3},{2,0},{3,1},{4,6},{5,7},{6,4},{7,5},{8,10},{9,11},{10,... | collective-permute-start | bytes 614408 | tf_op jit(solution)/shard_map/ppermute | solution.py:360
  95.1 2.4 %collective-permute-start.25 = (bf16[2,160,640]{2,1,0:T(8,128)(2,1)S(1)}, bf16[2,160,640]{2,1,0:T(8,128)(2,1)S(1)}, u32[]{:S(2)}, u32[]{:S(2)}) collective-permute-start(bf16[2,160,640]{2,1,0:T(8,128)(2,1)S(1)} %get-tuple-element.94), channel_id=1, source_target_pairs={{0,1},{1,0},{2,3},{3,2},{4,5},{5,4},{6,7},{7,6},{8,9},{9,8},{10,11... | collective-permute-start | bytes 1228808 | tf_op jit(solution)/shard_map/ppermute | solution.py:360
  95.2 7.5 %collective-permute-start.27 = (bf16[160,640]{1,0:T(8,128)(2,1)S(1)}, bf16[160,640]{1,0:T(8,128)(2,1)S(1)}, u32[]{:S(2)}, u32[]{:S(2)}) collective-permute-start(bf16[160,640]{1,0:T(8,128)(2,1)S(1)} %fusion), channel_id=1, source_target_pairs={{0,12},{1,13},{2,14},{3,15},{4,0},{5,1},{6,2},{7,3},{8,4},{9,5},{1... | collective-permute-start | bytes 614408 | tf_op jit(solution)/shard_map/ppermute | solution.py:363
  97.6 7.3 %collective-permute-start.26 = (bf16[1,160,640]{2,1,0:T(8,128)(2,1)S(1)}, bf16[1,160,640]{2,1,0:T(8,128)(2,1)S(1)}, u32[]{:S(2)}, u32[]{:S(2)}) collective-permute-start(bf16[1,160,640]{2,1,0:T(8,128)(2,1)S(1)} %get-tuple-element.96), channel_id=1, source_target_pairs={{0,2},{1,3},{2,0},{3,1},{4,6},{5,7},{6,4},{7,5},{8,10},{9,11},{10,... | collective-permute-start | bytes 614408 | tf_op jit(solution)/shard_map/ppermute | solution.py:360

commit v10 on v9

--- a/solution.py
+++ b/solution.py
@@ -433,16 +433,16 @@
 
     q1 = q.reshape(1)
     send0, held0 = reduce(*product(q1, scaled, sent, inner))
+    got0 = finish(send0)
     first = step(sent, 1)
-    first, send0 = lax.optimization_barrier((first, send0))
-    got0 = finish(send0)
+    first, got0 = lax.optimization_barrier((first, got0))
     second = step(first, 1)
     sendm, heldm = reduce(*product(q1, first, scaled, inner))
     sendm, first = lax.optimization_barrier((sendm, first))
     gotm = finish(sendm)
     send1, held1 = reduce(*product(q1, scaled, first, inner))
     got1 = finish(send1)
-    second, got0, got1, gotm = lax.optimization_barrier((second, got0, got1, gotm))
+    second, got1, gotm = lax.optimization_barrier((second, got1, gotm))
     back = step((heldm + gotm.astype(F32)).astype(BF16), -1)
     send2, held2 = reduce(*product(q1, scaled, second, inner))
     got2 = finish(send2)

time: 107 us -> 107 us (level)
  waiting for transfers between devices: 48.3 us -> 51 us
  starting transfers between devices: 30.3 us -> 27.7 us
    ppermute x3, waiting for transfers between devices: 6.38 us -> 16.1 us  [step(): lax.ppermute(array, 'spec', [(i, (i + outers * inner) % n) for i in range...]
    ppermute x25, waiting for transfers between devices: 42 us -> 34.9 us  [swap(): return lax.ppermute(array, 'spec', [(i, i ^ bit) for i in range(n)])]
    ppermute x3, starting transfers between devices: 4.99 us -> 1.17 us  [step(): lax.ppermute(array, 'spec', [(i, (i + outers * inner) % n) for i in range...]
    ppermute x25, starting transfers between devices: 25.3 us -> 26.6 us  [swap(): return lax.ppermute(array, 'spec', [(i, i ^ bit) for i in range(n)])]
  transfers between devices with their start and end apart: 28 -> 28, of which waited for: 16 -> 18; matrix products, arithmetic and copies ran while one was open for 1% -> 2% of each run, Pallas kernels for 18% -> 18%
where the time goes in v10:
time: 107 us
  waiting for transfers between devices  51 us (48%)
  starting transfers between devices  27.7 us (26%)
  Pallas kernels  24.3 us (23%)
  local copies, waits for them, and re-layouts  1.95 us (2%)
  other arithmetic  1.27 us (1%)
    ppermute x25, waiting for transfers between devices, swap(): return lax.ppermute(array, 'spec', [(i, i ^ bit) for i in range(n)])  34.9 us
    ppermute x25, starting transfers between devices, swap(): return lax.ppermute(array, 'spec', [(i, i ^ bit) for i in range(n)])  26.6 us
    pallas_call x15, Pallas kernels, call(): pl.pallas_call(kernel, out_shape=out_shape, in_specs=in_specs, out_specs=...  21.3 us
    ppermute x3, waiting for transfers between devices, step(): lax.ppermute(array, 'spec', [(i, (i + outers * inner) % n) for i in range...  16.1 us
    pallas_call x2, Pallas kernels, place(): pl.pallas_call(functools.partial(place_kernel, slots, last), out_shape=ja...  2.96 us
  transfers between devices with their start and end apart: 28, of which 18 were waited for; matrix products, arithmetic and copies ran while one was open for 2% of the time, Pallas kernels for 18%

profile of v10, /device:TPU:0, one launch (start us, length us, event | category | flops | bytes accessed | tf_op | source)
XLA Modules:
  0.0 106.5 jit_solution(12709947110312131173)
XLA Ops:
  0.0 0.8 pad_add_fusion.3
  0.8 3.0 %collective-permute-start = (s32[148]{0:T(256)S(1)}, s32[148]{0:T(256)S(1)}, u32[]{:S(2)}, u32[]{:S(2)}) collective-permute-start(s32[148]{0:T(256)S(1)} %pad_add_fusion.3), channel_id=1, source_target_pairs={{0,4},{1,5},{2,6},{3,7},{4,0},{5,1},{6,2},{7,3},{8,12},{9,13},{10,... | collective-permute-start | bytes 1784 | tf_op jit(solution)/shard_map/ppermute | solution.py:360
  3.9 2.6 %collective-permute-start.1 = (s32[148]{0:T(256)S(1)}, s32[148]{0:T(256)S(1)}, u32[]{:S(2)}, u32[]{:S(2)}) collective-permute-start(s32[148]{0:T(256)S(1)} %pad_add_fusion.3), channel_id=1, source_target_pairs={{0,8},{1,9},{2,10},{3,11},{4,12},{5,13},{6,14},{7,15},{8,0},{9,1},... | collective-permute-start | bytes 1784 | tf_op jit(solution)/shard_map/ppermute | solution.py:360
  6.5 1.2 %dynamic-slice_bitcast_fusion = (bf16[640,128]{1,0:T(8,128)(2,1)S(1)}, bf16[640,128]{1,0:T(8,128)(2,1)S(1)}, bf16[640,128]{1,0:T(8,128)(2,1)S(1)}, bf16[640,128]{1,0:T(8,128)(2,1)S(1)}) fusion(bf16[4,640,128]{2,1,0:T(8,128)(2,1)} %bitcast.48, s32[]{:T(128)S(6)} %select_n.41, s32[]{:T(128)S(6)} %select_n.40, s32[]{:T(128)S(6)} %select_n.39, s32[]{:T(128)S(6)} %select_n.38), kind=kLoop, calls=%fused_computation.3 | loop fusion | bytes 1310736 | tf_op jit(solution)/shard_map/jit(dynamic_index_in_dim)/squeeze | solution.py:380
  7.7 0.7 collective-permute-done.1
  8.3 3.5 %collective-permute-done.2 = s32[148]{0:T(256)S(1)} collective-permute-done((s32[148]{0:T(256)S(1)}, s32[148]{0:T(256)S(1)}, u32[]{:S(2)}, u32[]{:S(2)}) %collective-permute-start.2) | collective-permute-done | bytes 624 | tf_op jit(solution)/shard_map/ppermute | solution.py:360
  11.9 0.1 collective-permute-start.3
  12.0 0.6 collective-permute-start.4
  12.6 3.8 %collective-permute-start.5 = (bf16[640,128]{1,0:T(8,128)(2,1)S(1)}, bf16[640,128]{1,0:T(8,128)(2,1)S(1)}, u32[]{:S(2)}, u32[]{:S(2)}) collective-permute-start(bf16[640,128]{1,0:T(8,128)(2,1)S(1)} %get-tuple-element.101), channel_id=1, source_target_pairs={{0,12},{1,13},{2,14},{3,15},{4,8},{5,9},{6,10},{7,11},{8,4},{9,5},... | collective-permute-start | bytes 491528 | tf_op jit(solution)/shard_map/ppermute | solution.py:360
  16.4 1.5 %collective-permute-start.7 = (s32[4,2,20]{2,0,1:T(4,128)S(1)}, s32[4,2,20]{2,0,1:T(4,128)S(1)}, u32[]{:S(2)}, u32[]{:S(2)}) collective-permute-start(s32[4,2,20]{2,0,1:T(4,128)S(1)} %pad_add_fusion.2), channel_id=1, source_target_pairs={{0,2},{1,3},{2,0},{3,1},{4,6},{5,7},{6,4},{7,5},{8,10},{9,11},{10,... | collective-permute-start | bytes 1928 | tf_op jit(solution)/shard_map/ppermute | solution.py:360
  17.9 0.1 pad_add_fusion.5.me_ref
  18.0 0.7 copy-done.1
  18.6 0.2 shard_map.55
  18.9 7.2 %shard_map.56.smoothed_ref = bf16[128,3968]{1,0:T(8,128)(2,1)S(1)} custom-call(bf16[128,3968]{1,0:T(8,128)(2,1)S(1)} %copy-done, bf16[11,128,3968]{2,1,0:T(8,128)(2,1)} %bitcast.46), custom_call_target="tpu_custom_call" | custom-call | flops 1 | bytes 1 | tf_op jit(solution)/shard_map/pallas_call | solution.py:20
  26.2 4.7 %shard_map.57 = (bf16[128,640]{1,0:T(8,128)(2,1)S(1)}, bf16[128,640]{1,0:T(8,128)(2,1)S(1)}, bf16[128,640]{1,0:T(8,128)(2,1)S(1)}, bf16[128,640]{1,0:T(8,128)(2,1)S(1)}) custom-call(s32[2]{0:T(128)S(1)} %pad_add_fusion.5.me_ref, s32[2,128]{1,0:T(2,128)S(1)} %get-tuple-element.53.groups_ref, s32[16,20]{1,0:T(8,128)S(1)} %get-tuple-element.106.starts_ref, ...), custom_call_target="tpu_custom_call" | custom-call | flops 1 | bytes 1 | tf_op jit(solution)/shard_map/pallas_call | solution.py:20
  30.9 0.1 pad_maximum_fusion.refs_2_
  31.0 0.1 collective-permute-start.10
  31.1 0.6 collective-permute-start.8
  31.7 0.6 collective-permute-start.9
  32.3 3.7 %collective-permute-start.12 = (bf16[128,640]{1,0:T(8,128)(2,1)S(1)}, bf16[128,640]{1,0:T(8,128)(2,1)S(1)}, u32[]{:S(2)}, u32[]{:S(2)}) collective-permute-start(bf16[128,640]{1,0:T(8,128)(2,1)S(1)} %get-tuple-element.68), channel_id=1, source_target_pairs={{0,12},{1,13},{2,14},{3,15},{4,8},{5,9},{6,10},{7,11},{8,4},{9,5},... | collective-permute-start | bytes 491528 | tf_op jit(solution)/shard_map/ppermute | solution.py:360
  36.1 0.1 pad_add_fusion.6.bins_ref
  36.2 0.1 slice.8.names_ref
  36.2 4.1 %collective-permute-done.9.refs_1_ = bf16[128,640]{1,0:T(8,128)(2,1)S(1)} collective-permute-done((bf16[128,640]{1,0:T(8,128)(2,1)S(1)}, bf16[128,640]{1,0:T(8,128)(2,1)S(1)}, u32[]{:S(2)}, u32[]{:S(2)}) %collective-permute-start.9) | collective-permute-done | bytes 163872 | tf_op jit(solution)/shard_map/ppermute | solution.py:360
  40.4 1.5 %shard_map.58.refs_4_ = f32[256,640]{1,0:T(8,128)S(1)} custom-call(s32[8]{0:T(128)S(1)} %pad_add_fusion.6.bins_ref, s32[4,128]{1,0:T(4,128)S(1)} %slice.8.names_ref, bf16[128,640]{1,0:T(8,128)(2,1)S(1)} %get-tuple-element.69.refs_0_, bf16[128,640]{1,0:T(8,128)(2,1)S(1)} %collective-permute-done.9.refs_1_, bf16[4,640,128]{2,1,0:T(8,128)(2,1)S(1)} %pad_maximum_fusion.refs_2_, ...), custom_call_target="tpu_custom_call" | custom-call | flops 1 | bytes 1 | tf_op jit(solution)/shard_map/pallas_call | solution.py:20
  41.9 5.4 %collective-permute-done.11.refs_0_.refs_2_ = bf16[128,640]{1,0:T(8,128)(2,1)S(1)} collective-permute-done((bf16[128,640]{1,0:T(8,128)(2,1)S(1)}, bf16[128,640]{1,0:T(8,128)(2,1)S(1)}, u32[]{:S(2)}, u32[]{:S(2)}) %collective-permute-start.11) | collective-permute-done | bytes 163872 | tf_op jit(solution)/shard_map/ppermute | solution.py:360
  47.3 0.9 collective-permute-done.8.refs_6_
  48.3 0.1 pad_add_fusion.4.bins_ref
  48.4 1.5 %shard_map.59.refs_5_ = f32[256,640]{1,0:T(8,128)S(1)} custom-call(s32[8]{0:T(128)S(1)} %pad_add_fusion.6.bins_ref, s32[4,128]{1,0:T(4,128)S(1)} %slice.8.names_ref, bf16[128,640]{1,0:T(8,128)(2,1)S(1)} %collective-permute-done.11.refs_0_.refs_2_, bf16[128,640]{1,0:T(8,128)(2,1)S(1)} %collective-permute-done.12.refs_1_.refs_3_, ...), custom_call_target="tpu_custom_call" | custom-call | flops 1 | bytes 1 | tf_op jit(solution)/shard_map/pallas_call | solution.py:20
  49.9 0.5 collective-permute-done.13.refs_7_
  50.4 2.3 %shard_map.60 = (f32[512,640]{1,0:T(8,128)S(1)}, bf16[512,640]{1,0:T(8,128)(2,1)S(1)}, f32[4,128]{1,0:T(4,128)S(1)}) custom-call(s32[1]{0:T(128)} %bitcast.1.outer_ref, s32[8]{0:T(128)S(1)} %pad_add_fusion.4.bins_ref, s32[4,128]{1,0:T(4,128)S(1)} %slice.8.names_ref, bf16[128,640]{1,0:T(8,128)(2,1)S(1)} %get-tuple-element.69.refs_0_, ...), custom_call_target="tpu_custom_call" | custom-call | flops 1 | bytes 1 | tf_op jit(solution)/shard_map/pallas_call | solution.py:20
  52.7 2.1 %collective-permute-start.14 = (f32[4,128]{1,0:T(4,128)S(1)}, f32[4,128]{1,0:T(4,128)S(1)}, u32[]{:S(2)}, u32[]{:S(2)}) collective-permute-start(f32[4,128]{1,0:T(4,128)S(1)} %get-tuple-element.76), channel_id=1, source_target_pairs={{0,4},{1,5},{2,6},{3,7},{4,0},{5,1},{6,2},{7,3},{8,12},{9,13},{10,... | collective-permute-start | bytes 6152 | tf_op jit(solution)/shard_map/ppermute | solution.py:360
  54.8 0.1 collective-permute-start.15
  54.9 2.3 %collective-permute-start.16 = (f32[4,128]{1,0:T(4,128)S(1)}, f32[4,128]{1,0:T(4,128)S(1)}, u32[]{:S(2)}, u32[]{:S(2)}) collective-permute-start(f32[4,128]{1,0:T(4,128)S(1)} %get-tuple-element.76), channel_id=1, source_target_pairs={{0,12},{1,13},{2,14},{3,15},{4,8},{5,9},{6,10},{7,11},{8,4},{9,5},... | collective-permute-start | bytes 6152 | tf_op jit(solution)/shard_map/ppermute | solution.py:360
  57.3 1.0 collective-permute-start.17
  58.3 1.0 collective-permute-done.15
  59.3 1.0 collective-permute-done.16
  60.3 0.2 shard_map.61.tall_ref.wide_ref
  60.5 0.8 shard_map.62
  61.3 0.1 collective-permute-start.18
  61.4 1.7 %collective-permute-done.18.got_ref = bf16[2,160,640]{2,1,0:T(8,128)(2,1)S(1)} collective-permute-done((bf16[2,160,640]{2,1,0:T(8,128)(2,1)S(1)}, bf16[2,160,640]{2,1,0:T(8,128)(2,1)S(1)}, u32[]{:S(2)}, u32[]{:S(2)}) %collective-permute-start.18) | collective-permute-done | bytes 409632 | tf_op jit(solution)/shard_map/ppermute | solution.py:360
  63.1 0.1 shard_map.63
  63.2 1.2 %collective-permute-start.19 = (bf16[1,160,640]{2,1,0:T(8,128)(2,1)S(1)}, bf16[1,160,640]{2,1,0:T(8,128)(2,1)S(1)}, u32[]{:S(2)}, u32[]{:S(2)}) collective-permute-start(bf16[1,160,640]{2,1,0:T(8,128)(2,1)S(1)} %get-tuple-element.80), channel_id=1, source_target_pairs={{0,2},{1,3},{2,0},{3,1},{4,6},{5,7},{6,4},{7,5},{8,10},{9,11},{10,... | collective-permute-start | bytes 614408 | tf_op jit(solution)/shard_map/ppermute | solution.py:360
  64.5 6.0 %collective-permute-done.19 = bf16[1,160,640]{2,1,0:T(8,128)(2,1)S(1)} collective-permute-done((bf16[1,160,640]{2,1,0:T(8,128)(2,1)S(1)}, bf16[1,160,640]{2,1,0:T(8,128)(2,1)S(1)}, u32[]{:S(2)}, u32[]{:S(2)}) %collective-permute-start.19) | collective-permute-done | bytes 204832 | tf_op jit(solution)/shard_map/ppermute | solution.py:360
  70.4 4.9 %collective-permute-done.17.tall_ref.wide_ref = bf16[512,640]{1,0:T(8,128)(2,1)S(1)} collective-permute-done((bf16[512,640]{1,0:T(8,128)(2,1)S(1)}, bf16[512,640]{1,0:T(8,128)(2,1)S(1)}, u32[]{:S(2)}, u32[]{:S(2)}) %collective-permute-start.17) | collective-permute-done | bytes 655392 | tf_op jit(solution)/shard_map/ppermute | solution.py:363
  75.3 0.8 shard_map.64
  76.2 1.7 %collective-permute-done.21.got_ref = bf16[2,160,640]{2,1,0:T(8,128)(2,1)S(1)} collective-permute-done((bf16[2,160,640]{2,1,0:T(8,128)(2,1)S(1)}, bf16[2,160,640]{2,1,0:T(8,128)(2,1)S(1)}, u32[]{:S(2)}, u32[]{:S(2)}) %collective-permute-start.21) | collective-permute-done | bytes 409632 | tf_op jit(solution)/shard_map/ppermute | solution.py:360
  77.9 0.1 shard_map.65
  78.0 0.8 shard_map.66
  78.8 0.2 collective-permute-start.22
  79.0 1.2 %collective-permute-start.24 = (bf16[1,160,640]{2,1,0:T(8,128)(2,1)S(1)}, bf16[1,160,640]{2,1,0:T(8,128)(2,1)S(1)}, u32[]{:S(2)}, u32[]{:S(2)}) collective-permute-start(bf16[1,160,640]{2,1,0:T(8,128)(2,1)S(1)} %get-tuple-element.89), channel_id=1, source_target_pairs={{0,2},{1,3},{2,0},{3,1},{4,6},{5,7},{6,4},{7,5},{8,10},{9,11},{10,... | collective-permute-start | bytes 614408 | tf_op jit(solution)/shard_map/ppermute | solution.py:360
  80.2 0.4 collective-permute-done.22.got_ref
  80.6 0.1 shard_map.67
  80.7 1.2 %collective-permute-start.23 = (bf16[1,160,640]{2,1,0:T(8,128)(2,1)S(1)}, bf16[1,160,640]{2,1,0:T(8,128)(2,1)S(1)}, u32[]{:S(2)}, u32[]{:S(2)}) collective-permute-start(bf16[1,160,640]{2,1,0:T(8,128)(2,1)S(1)} %get-tuple-element.88), channel_id=1, source_target_pairs={{0,2},{1,3},{2,0},{3,1},{4,6},{5,7},{6,4},{7,5},{8,10},{9,11},{10,... | collective-permute-start | bytes 614408 | tf_op jit(solution)/shard_map/ppermute | solution.py:360
  82.0 5.0 %collective-permute-done.24 = bf16[1,160,640]{2,1,0:T(8,128)(2,1)S(1)} collective-permute-done((bf16[1,160,640]{2,1,0:T(8,128)(2,1)S(1)}, bf16[1,160,640]{2,1,0:T(8,128)(2,1)S(1)}, u32[]{:S(2)}, u32[]{:S(2)}) %collective-permute-start.24) | collective-permute-done | bytes 204832 | tf_op jit(solution)/shard_map/ppermute | solution.py:360
  86.9 8.2 %collective-permute-done.20.wide_ref = bf16[512,640]{1,0:T(8,128)(2,1)S(1)} collective-permute-done((bf16[512,640]{1,0:T(8,128)(2,1)S(1)}, bf16[512,640]{1,0:T(8,128)(2,1)S(1)}, u32[]{:S(2)}, u32[]{:S(2)}) %collective-permute-start.20) | collective-permute-done | bytes 655392 | tf_op jit(solution)/shard_map/ppermute | solution.py:363
  95.1 0.8 shard_map.68
  95.9 0.1 collective-permute-start.25
  96.1 1.6 %collective-permute-done.25.got_ref = bf16[2,160,640]{2,1,0:T(8,128)(2,1)S(1)} collective-permute-done((bf16[2,160,640]{2,1,0:T(8,128)(2,1)S(1)}, bf16[2,160,640]{2,1,0:T(8,128)(2,1)S(1)}, u32[]{:S(2)}, u32[]{:S(2)}) %collective-permute-start.25) | collective-permute-done | bytes 409632 | tf_op jit(solution)/shard_map/ppermute | solution.py:360
  97.7 0.1 shard_map.69
  97.8 1.2 %collective-permute-start.26 = (bf16[1,160,640]{2,1,0:T(8,128)(2,1)S(1)}, bf16[1,160,640]{2,1,0:T(8,128)(2,1)S(1)}, u32[]{:S(2)}, u32[]{:S(2)}) collective-permute-start(bf16[1,160,640]{2,1,0:T(8,128)(2,1)S(1)} %get-tuple-element.94), channel_id=1, source_target_pairs={{0,2},{1,3},{2,0},{3,1},{4,6},{5,7},{6,4},{7,5},{8,10},{9,11},{10,... | collective-permute-start | bytes 614408 | tf_op jit(solution)/shard_map/ppermute | solution.py:360
  99.1 1.5 %shard_map.70.refs_4_ = f32[160,2560]{1,0:T(8,128)} custom-call(s32[4]{0:T(128)S(1)} %and_select_fusion.at_ref, f32[160,640]{1,0:T(8,128)S(1)} %bitcast.38, bf16[160,640]{1,0:T(8,128)(2,1)S(1)} %bitcast.41, f32[160,640]{1,0:T(8,128)S(1)} %bitcast.39, bf16[160,640]{1,0:T(8,128)(2,1)S(1)} %bitcast.42), custom_call_target="tpu_custom_call" | custom-call | flops 1 | bytes 1 | tf_op jit(solution)/shard_map/pallas_call | solution.py:334
  100.6 3.0 %collective-permute-done.27.refs_2_ = bf16[160,640]{1,0:T(8,128)(2,1)S(1)} collective-permute-done((bf16[160,640]{1,0:T(8,128)(2,1)S(1)}, bf16[160,640]{1,0:T(8,128)(2,1)S(1)}, u32[]{:S(2)}, u32[]{:S(2)}) %collective-permute-start.27) | collective-permute-done | bytes 204832 | tf_op jit(solution)/shard_map/ppermute | solution.py:363
  103.6 1.4 %collective-permute-done.26 = bf16[1,160,640]{2,1,0:T(8,128)(2,1)S(1)} collective-permute-done((bf16[1,160,640]{2,1,0:T(8,128)(2,1)S(1)}, bf16[1,160,640]{2,1,0:T(8,128)(2,1)S(1)}, u32[]{:S(2)}, u32[]{:S(2)}) %collective-permute-start.26) | collective-permute-done | bytes 204832 | tf_op jit(solution)/shard_map/ppermute | solution.py:360
  105.0 1.5 %shard_map.71 = f32[160,2560]{1,0:T(8,128)} custom-call(s32[4]{0:T(128)S(1)} %and_select_fusion.at_ref, f32[160,640]{1,0:T(8,128)S(1)} %bitcast.40, bf16[160,640]{1,0:T(8,128)(2,1)S(1)} %bitcast.43, bf16[160,640]{1,0:T(8,128)(2,1)S(1)} %collective-permute-done.27.refs_2_, ...), custom_call_target="tpu_custom_call", output_to_operand_aliasing={{}: (5, {})} | custom-call | flops 1 | bytes 1 | tf_op jit(solution)/shard_map/pallas_call | solution.py:334
  (32 shorter events, 0.5 us)
Async XLA Ops:
  0.0 18.9 %copy-start = (bf16[128,3968]{1,0:T(8,128)(2,1)S(1)}, bf16[128,3968]{1,0:T(8,128)(2,1)}, u32[]{:S(2)}) copy-start(bf16[128,3968]{1,0:T(8,128)(2,1)} %flux_ref) | copy-start | bytes 3047428
  0.8 6.8 %collective-permute-start = (s32[148]{0:T(256)S(1)}, s32[148]{0:T(256)S(1)}, u32[]{:S(2)}, u32[]{:S(2)}) collective-permute-start(s32[148]{0:T(256)S(1)} %pad_add_fusion.3), channel_id=1, source_target_pairs={{0,4},{1,5},{2,6},{3,7},{4,0},{5,1},{6,2},{7,3},{8,12},{9,13},{10,... | collective-permute-start | bytes 1784 | tf_op jit(solution)/shard_map/ppermute | solution.py:360
  3.9 4.5 %collective-permute-start.1 = (s32[148]{0:T(256)S(1)}, s32[148]{0:T(256)S(1)}, u32[]{:S(2)}, u32[]{:S(2)}) collective-permute-start(s32[148]{0:T(256)S(1)} %pad_add_fusion.3), channel_id=1, source_target_pairs={{0,8},{1,9},{2,10},{3,11},{4,12},{5,13},{6,14},{7,15},{8,0},{9,1},... | collective-permute-start | bytes 1784 | tf_op jit(solution)/shard_map/ppermute | solution.py:360
  6.4 5.4 %collective-permute-start.2 = (s32[148]{0:T(256)S(1)}, s32[148]{0:T(256)S(1)}, u32[]{:S(2)}, u32[]{:S(2)}) collective-permute-start(s32[148]{0:T(256)S(1)} %pad_add_fusion.3), channel_id=1, source_target_pairs={{0,12},{1,13},{2,14},{3,15},{4,8},{5,9},{6,10},{7,11},{8,4},{9,5},... | collective-permute-start | bytes 1784 | tf_op jit(solution)/shard_map/ppermute | solution.py:360
  11.8 4.5 %collective-permute-start.6 = (s32[4,1,20]{2,0,1:T(4,128)S(1)}, s32[4,1,20]{2,0,1:T(4,128)S(1)}, u32[]{:S(2)}, u32[]{:S(2)}) collective-permute-start(s32[4,1,20]{2,0,1:T(4,128)S(1)} %slice_bitcast_fusion), channel_id=1, source_target_pairs={{0,1},{1,0},{2,3},{3,2},{4,5},{5,4},{6,7},{7,6},{8,9},{9,8},{10,11... | collective-permute-start | bytes 968 | tf_op jit(solution)/shard_map/ppermute | solution.py:360
  11.9 19.0 %collective-permute-start.3 = (bf16[640,128]{1,0:T(8,128)(2,1)S(1)}, bf16[640,128]{1,0:T(8,128)(2,1)S(1)}, u32[]{:S(2)}, u32[]{:S(2)}) collective-permute-start(bf16[640,128]{1,0:T(8,128)(2,1)S(1)} %get-tuple-element.103), channel_id=1, source_target_pairs={{0,4},{1,5},{2,6},{3,7},{4,0},{5,1},{6,2},{7,3},{8,12},{9,13},{10,... | collective-permute-start | bytes 491528 | tf_op jit(solution)/shard_map/ppermute | solution.py:360
  12.0 18.9 %collective-permute-start.4 = (bf16[640,128]{1,0:T(8,128)(2,1)S(1)}, bf16[640,128]{1,0:T(8,128)(2,1)S(1)}, u32[]{:S(2)}, u32[]{:S(2)}) collective-permute-start(bf16[640,128]{1,0:T(8,128)(2,1)S(1)} %get-tuple-element.102), channel_id=1, source_target_pairs={{0,8},{1,9},{2,10},{3,11},{4,12},{5,13},{6,14},{7,15},{8,0},{9,1},... | collective-permute-start | bytes 491528 | tf_op jit(solution)/shard_map/ppermute | solution.py:360
  12.6 18.4 %collective-permute-start.5 = (bf16[640,128]{1,0:T(8,128)(2,1)S(1)}, bf16[640,128]{1,0:T(8,128)(2,1)S(1)}, u32[]{:S(2)}, u32[]{:S(2)}) collective-permute-start(bf16[640,128]{1,0:T(8,128)(2,1)S(1)} %get-tuple-element.101), channel_id=1, source_target_pairs={{0,12},{1,13},{2,14},{3,15},{4,8},{5,9},{6,10},{7,11},{8,4},{9,5},... | collective-permute-start | bytes 491528 | tf_op jit(solution)/shard_map/ppermute | solution.py:360
  16.4 9.8 %collective-permute-start.7 = (s32[4,2,20]{2,0,1:T(4,128)S(1)}, s32[4,2,20]{2,0,1:T(4,128)S(1)}, u32[]{:S(2)}, u32[]{:S(2)}) collective-permute-start(s32[4,2,20]{2,0,1:T(4,128)S(1)} %pad_add_fusion.2), channel_id=1, source_target_pairs={{0,2},{1,3},{2,0},{3,1},{4,6},{5,7},{6,4},{7,5},{8,10},{9,11},{10,... | collective-permute-start | bytes 1928 | tf_op jit(solution)/shard_map/ppermute | solution.py:360
  18.0 0.7 copy-start.1
  31.0 9.3 %collective-permute-start.10 = (bf16[4,640,128]{2,1,0:T(8,128)(2,1)S(1)}, bf16[4,640,128]{2,1,0:T(8,128)(2,1)S(1)}, u32[]{:S(2)}, u32[]{:S(2)}) collective-permute-start(bf16[4,640,128]{2,1,0:T(8,128)(2,1)S(1)} %pad_maximum_fusion.refs_2_), channel_id=1, source_target_pairs={{0,1},{1,0},{2,3},{3,2},{4,5},{5,4},{6,7},{7,6},{8,9},{9,8},{10,11... | collective-permute-start | bytes 1966088 | tf_op jit(solution)/shard_map/ppermute | solution.py:360
  31.1 17.1 %collective-permute-start.8 = (bf16[4,640,128]{2,1,0:T(8,128)(2,1)S(1)}, bf16[4,640,128]{2,1,0:T(8,128)(2,1)S(1)}, u32[]{:S(2)}, u32[]{:S(2)}) collective-permute-start(bf16[4,640,128]{2,1,0:T(8,128)(2,1)S(1)} %pad_maximum_fusion.refs_2_), channel_id=1, source_target_pairs={{0,2},{1,3},{2,0},{3,1},{4,6},{5,7},{6,4},{7,5},{8,10},{9,11},{10,... | collective-permute-start | bytes 1966088 | tf_op jit(solution)/shard_map/ppermute | solution.py:360
  31.7 8.7 %collective-permute-start.9 = (bf16[128,640]{1,0:T(8,128)(2,1)S(1)}, bf16[128,640]{1,0:T(8,128)(2,1)S(1)}, u32[]{:S(2)}, u32[]{:S(2)}) collective-permute-start(bf16[128,640]{1,0:T(8,128)(2,1)S(1)} %get-tuple-element.66), channel_id=1, source_target_pairs={{0,4},{1,5},{2,6},{3,7},{4,0},{5,1},{6,2},{7,3},{8,12},{9,13},{10,... | collective-permute-start | bytes 491528 | tf_op jit(solution)/shard_map/ppermute | solution.py:360
  32.3 15.0 %collective-permute-start.11 = (bf16[128,640]{1,0:T(8,128)(2,1)S(1)}, bf16[128,640]{1,0:T(8,128)(2,1)S(1)}, u32[]{:S(2)}, u32[]{:S(2)}) collective-permute-start(bf16[128,640]{1,0:T(8,128)(2,1)S(1)} %get-tuple-element.67), channel_id=1, source_target_pairs={{0,8},{1,9},{2,10},{3,11},{4,12},{5,13},{6,14},{7,15},{8,0},{9,1},... | collective-permute-start | bytes 491528 | tf_op jit(solution)/shard_map/ppermute | solution.py:360
  32.3 15.0 %collective-permute-start.12 = (bf16[128,640]{1,0:T(8,128)(2,1)S(1)}, bf16[128,640]{1,0:T(8,128)(2,1)S(1)}, u32[]{:S(2)}, u32[]{:S(2)}) collective-permute-start(bf16[128,640]{1,0:T(8,128)(2,1)S(1)} %get-tuple-element.68), channel_id=1, source_target_pairs={{0,12},{1,13},{2,14},{3,15},{4,8},{5,9},{6,10},{7,11},{8,4},{9,5},... | collective-permute-start | bytes 491528 | tf_op jit(solution)/shard_map/ppermute | solution.py:360
  48.3 2.1 %collective-permute-start.13 = (bf16[4,640,128]{2,1,0:T(8,128)(2,1)S(1)}, bf16[4,640,128]{2,1,0:T(8,128)(2,1)S(1)}, u32[]{:S(2)}, u32[]{:S(2)}) collective-permute-start(bf16[4,640,128]{2,1,0:T(8,128)(2,1)S(1)} %collective-permute-done.8.refs_6_), channel_id=1, source_target_pairs={{0,1},{1,0},{2,3},{3,2},{4,5},{5,4},{6,7},{7,6},{8,9},{9,8},{10,11... | collective-permute-start | bytes 1966088 | tf_op jit(solution)/shard_map/ppermute | solution.py:360
  52.7 5.6 %collective-permute-start.14 = (f32[4,128]{1,0:T(4,128)S(1)}, f32[4,128]{1,0:T(4,128)S(1)}, u32[]{:S(2)}, u32[]{:S(2)}) collective-permute-start(f32[4,128]{1,0:T(4,128)S(1)} %get-tuple-element.76), channel_id=1, source_target_pairs={{0,4},{1,5},{2,6},{3,7},{4,0},{5,1},{6,2},{7,3},{8,12},{9,13},{10,... | collective-permute-start | bytes 6152 | tf_op jit(solution)/shard_map/ppermute | solution.py:360
  54.8 4.5 %collective-permute-start.15 = (f32[4,128]{1,0:T(4,128)S(1)}, f32[4,128]{1,0:T(4,128)S(1)}, u32[]{:S(2)}, u32[]{:S(2)}) collective-permute-start(f32[4,128]{1,0:T(4,128)S(1)} %get-tuple-element.76), channel_id=1, source_target_pairs={{0,8},{1,9},{2,10},{3,11},{4,12},{5,13},{6,14},{7,15},{8,0},{9,1},... | collective-permute-start | bytes 6152 | tf_op jit(solution)/shard_map/ppermute | solution.py:360
  54.9 5.4 %collective-permute-start.16 = (f32[4,128]{1,0:T(4,128)S(1)}, f32[4,128]{1,0:T(4,128)S(1)}, u32[]{:S(2)}, u32[]{:S(2)}) collective-permute-start(f32[4,128]{1,0:T(4,128)S(1)} %get-tuple-element.76), channel_id=1, source_target_pairs={{0,12},{1,13},{2,14},{3,15},{4,8},{5,9},{6,10},{7,11},{8,4},{9,5},... | collective-permute-start | bytes 6152 | tf_op jit(solution)/shard_map/ppermute | solution.py:360
  57.3 18.0 %collective-permute-start.17 = (bf16[512,640]{1,0:T(8,128)(2,1)S(1)}, bf16[512,640]{1,0:T(8,128)(2,1)S(1)}, u32[]{:S(2)}, u32[]{:S(2)}) collective-permute-start(bf16[512,640]{1,0:T(8,128)(2,1)S(1)} %get-tuple-element.77.wide_ref), channel_id=1, source_target_pairs={{0,4},{1,5},{2,6},{3,7},{4,8},{5,9},{6,10},{7,11},{8,12},{9,13},{1... | collective-permute-start | bytes 1966088 | tf_op jit(solution)/shard_map/ppermute | solution.py:363
  61.3 1.8 %collective-permute-start.18 = (bf16[2,160,640]{2,1,0:T(8,128)(2,1)S(1)}, bf16[2,160,640]{2,1,0:T(8,128)(2,1)S(1)}, u32[]{:S(2)}, u32[]{:S(2)}) collective-permute-start(bf16[2,160,640]{2,1,0:T(8,128)(2,1)S(1)} %get-tuple-element.79), channel_id=1, source_target_pairs={{0,1},{1,0},{2,3},{3,2},{4,5},{5,4},{6,7},{7,6},{8,9},{9,8},{10,11... | collective-permute-start | bytes 1228808 | tf_op jit(solution)/shard_map/ppermute | solution.py:360
  63.2 7.2 %collective-permute-start.19 = (bf16[1,160,640]{2,1,0:T(8,128)(2,1)S(1)}, bf16[1,160,640]{2,1,0:T(8,128)(2,1)S(1)}, u32[]{:S(2)}, u32[]{:S(2)}) collective-permute-start(bf16[1,160,640]{2,1,0:T(8,128)(2,1)S(1)} %get-tuple-element.80), channel_id=1, source_target_pairs={{0,2},{1,3},{2,0},{3,1},{4,6},{5,7},{6,4},{7,5},{8,10},{9,11},{10,... | collective-permute-start | bytes 614408 | tf_op jit(solution)/shard_map/ppermute | solution.py:360
  76.1 1.8 %collective-permute-start.21 = (bf16[2,160,640]{2,1,0:T(8,128)(2,1)S(1)}, bf16[2,160,640]{2,1,0:T(8,128)(2,1)S(1)}, u32[]{:S(2)}, u32[]{:S(2)}) collective-permute-start(bf16[2,160,640]{2,1,0:T(8,128)(2,1)S(1)} %get-tuple-element.83), channel_id=1, source_target_pairs={{0,1},{1,0},{2,3},{3,2},{4,5},{5,4},{6,7},{7,6},{8,9},{9,8},{10,11... | collective-permute-start | bytes 1228808 | tf_op jit(solution)/shard_map/ppermute | solution.py:360
  76.2 18.9 %collective-permute-start.20 = (bf16[512,640]{1,0:T(8,128)(2,1)S(1)}, bf16[512,640]{1,0:T(8,128)(2,1)S(1)}, u32[]{:S(2)}, u32[]{:S(2)}) collective-permute-start(bf16[512,640]{1,0:T(8,128)(2,1)S(1)} %collective-permute-done.17.tall_ref.wide_ref), channel_id=1, source_target_pairs={{0,4},{1,5},{2,6},{3,7},{4,8},{5,9},{6,10},{7,11},{8,12},{9,13},{1... | collective-permute-start | bytes 1966088 | tf_op jit(solution)/shard_map/ppermute | solution.py:363
  78.8 1.8 %collective-permute-start.22 = (bf16[2,160,640]{2,1,0:T(8,128)(2,1)S(1)}, bf16[2,160,640]{2,1,0:T(8,128)(2,1)S(1)}, u32[]{:S(2)}, u32[]{:S(2)}) collective-permute-start(bf16[2,160,640]{2,1,0:T(8,128)(2,1)S(1)} %get-tuple-element.87), channel_id=1, source_target_pairs={{0,1},{1,0},{2,3},{3,2},{4,5},{5,4},{6,7},{7,6},{8,9},{9,8},{10,11... | collective-permute-start | bytes 1228808 | tf_op jit(solution)/shard_map/ppermute | solution.py:360
  79.0 7.9 %collective-permute-start.24 = (bf16[1,160,640]{2,1,0:T(8,128)(2,1)S(1)}, bf16[1,160,640]{2,1,0:T(8,128)(2,1)S(1)}, u32[]{:S(2)}, u32[]{:S(2)}) collective-permute-start(bf16[1,160,640]{2,1,0:T(8,128)(2,1)S(1)} %get-tuple-element.89), channel_id=1, source_target_pairs={{0,2},{1,3},{2,0},{3,1},{4,6},{5,7},{6,4},{7,5},{8,10},{9,11},{10,... | collective-permute-start | bytes 614408 | tf_op jit(solution)/shard_map/ppermute | solution.py:360
  80.7 14.4 %collective-permute-start.23 = (bf16[1,160,640]{2,1,0:T(8,128)(2,1)S(1)}, bf16[1,160,640]{2,1,0:T(8,128)(2,1)S(1)}, u32[]{:S(2)}, u32[]{:S(2)}) collective-permute-start(bf16[1,160,640]{2,1,0:T(8,128)(2,1)S(1)} %get-tuple-element.88), channel_id=1, source_target_pairs={{0,2},{1,3},{2,0},{3,1},{4,6},{5,7},{6,4},{7,5},{8,10},{9,11},{10,... | collective-permute-start | bytes 614408 | tf_op jit(solution)/shard_map/ppermute | solution.py:360
  95.9 1.8 %collective-permute-start.25 = (bf16[2,160,640]{2,1,0:T(8,128)(2,1)S(1)}, bf16[2,160,640]{2,1,0:T(8,128)(2,1)S(1)}, u32[]{:S(2)}, u32[]{:S(2)}) collective-permute-start(bf16[2,160,640]{2,1,0:T(8,128)(2,1)S(1)} %get-tuple-element.92), channel_id=1, source_target_pairs={{0,1},{1,0},{2,3},{3,2},{4,5},{5,4},{6,7},{7,6},{8,9},{9,8},{10,11... | collective-permute-start | bytes 1228808 | tf_op jit(solution)/shard_map/ppermute | solution.py:360
  96.1 7.5 %collective-permute-start.27 = (bf16[160,640]{1,0:T(8,128)(2,1)S(1)}, bf16[160,640]{1,0:T(8,128)(2,1)S(1)}, u32[]{:S(2)}, u32[]{:S(2)}) collective-permute-start(bf16[160,640]{1,0:T(8,128)(2,1)S(1)} %fusion), channel_id=1, source_target_pairs={{0,12},{1,13},{2,14},{3,15},{4,0},{5,1},{6,2},{7,3},{8,4},{9,5},{1... | collective-permute-start | bytes 614408 | tf_op jit(solution)/shard_map/ppermute | solution.py:363
  97.8 7.2 %collective-permute-start.26 = (bf16[1,160,640]{2,1,0:T(8,128)(2,1)S(1)}, bf16[1,160,640]{2,1,0:T(8,128)(2,1)S(1)}, u32[]{:S(2)}, u32[]{:S(2)}) collective-permute-start(bf16[1,160,640]{2,1,0:T(8,128)(2,1)S(1)} %get-tuple-element.94), channel_id=1, source_target_pairs={{0,2},{1,3},{2,0},{3,1},{4,6},{5,7},{6,4},{7,5},{8,10},{9,11},{10,... | collective-permute-start | bytes 614408 | tf_op jit(solution)/shard_map/ppermute | solution.py:360

commit v11 on v10

--- a/solution.py
+++ b/solution.py
@@ -225,7 +225,8 @@
 
 def end_kernel(nbegun, npieces, band, outer_ref, bins_ref, names_ref, *refs):
     windows, begun, weights = refs[:OUTER], refs[OUTER : OUTER + nbegun], refs[OUTER + nbegun : OUTER + nbegun + npieces]
-    rest_ref, sent_ref, squares_ref, window, named_ref, value_ref = refs[OUTER + nbegun + npieces :]
+    rest_ref, *sents, squares_ref, window, named_ref, value_ref = refs[OUTER + nbegun + npieces :]
+    splits = [sent.shape[1] for sent in sents]
     count, width = windows[0].shape
     row = 0
     for part in begun:
@@ -241,7 +242,8 @@
         for at in range(0, width, band):
             value = value_ref[own, at : at + band]
             rest_ref[rows, at : at + band] = value
-            sent_ref[rows, at : at + band] = value.astype(BF16)
+            part = int(at >= splits[0])
+            sents[part][rows, at - part * splits[0] : at - part * splits[0] + band] = value.astype(BF16)
             total = total + value * value
         squares_ref[pl.ds(place, 1), :] = jnp.sum(total.T, axis=0, keepdims=True)
 
@@ -249,11 +251,13 @@
 def end_rest(outer, bins, names, windows, begun, weights, band):
     count, width = windows[0].shape
     rows = OUTER * count
+    split = (width // band + 1) // 2 * band
     return call(
         functools.partial(end_kernel, len(begun), len(weights), band),
         (
             jax.ShapeDtypeStruct((rows, width), F32),
-            jax.ShapeDtypeStruct((rows, width), BF16),
+            jax.ShapeDtypeStruct((rows, split), BF16),
+            jax.ShapeDtypeStruct((rows, width - split), BF16),
             jax.ShapeDtypeStruct((OUTER, count), F32),
         ),
         [SMEM, SMEM] + [VMEM] * (1 + OUTER + len(begun) + len(weights)),
@@ -272,11 +276,18 @@
             out_ref[own, at : at + 128] = (rest_ref[own, at : at + 128] * factor).astype(BF16)
 
 
-def product_kernel(q_ref, tall_ref, wide_ref, send_ref, keep_ref, value):
+def product_kernel(ntall, nwide, q_ref, *refs):
+    talls, wides, (send_ref, keep_ref, value) = refs[:ntall], refs[ntall : ntall + nwide], refs[ntall + nwide :]
     pairs, share, _ = keep_ref.shape
-    value[...] = lax.dot_general(
-        tall_ref[...], wide_ref[...], (((0,), (0,)), ((), ())), preferred_element_type=F32
-    )
+    row = 0
+    for tall in talls:
+        column = 0
+        for wide in wides:
+            value[row : row + tall.shape[1], column : column + wide.shape[1]] = lax.dot_general(
+                tall[...], wide[...], (((0,), (0,)), ((), ())), preferred_element_type=F32
+            )
+            column += wide.shape[1]
+        row += tall.shape[1]
     for e in range(2 * pairs):
         own = value[pl.ds(pl.multiple_of((q_ref[0] ^ e) * share, 8), share), :]
         if e % 2:
@@ -285,14 +296,15 @@
             keep_ref[e // 2] = own
 
 
-def product(q, tall, wide, inner):
-    rows, columns = tall.shape[1], wide.shape[1]
+def product(q, talls, wides, inner):
+    rows = sum(tall.shape[1] for tall in talls)
+    columns = sum(wide.shape[1] for wide in wides)
     shape = (inner // 2, rows // inner, columns)
     return call(
-        product_kernel,
+        functools.partial(product_kernel, len(talls), len(wides)),
         (jax.ShapeDtypeStruct(shape, BF16), jax.ShapeDtypeStruct(shape, F32)),
-        [SMEM, VMEM, VMEM],
-        (q, tall, wide),
+        [SMEM] + [VMEM] * (len(talls) + len(wides)),
+        (q, *talls, *wides),
         [pltpu.VMEM((rows, columns), F32)],
     )
 
@@ -412,7 +424,7 @@
     far = [across]
     for bit in bits:
         far = far + [swap(piece, bit) for piece in far]
-    rest, sent, squares = end_rest(outer1, far_bins, names, arrived, begun, far, band)
+    rest, *sent, squares = end_rest(outer1, far_bins, names, arrived, begun, far, band)
 
     total = squares
     for away in range(1, OUTER):
@@ -432,19 +444,19 @@
         return swap(send, inner // 2)[0]
 
     q1 = q.reshape(1)
-    send0, held0 = reduce(*product(q1, scaled, sent, inner))
+    send0, held0 = reduce(*product(q1, [scaled], sent, inner))
     got0 = finish(send0)
-    first = step(sent, 1)
+    first = [step(part, 1) for part in sent]
     first, got0 = lax.optimization_barrier((first, got0))
-    second = step(first, 1)
-    sendm, heldm = reduce(*product(q1, first, scaled, inner))
+    second = [step(part, 1) for part in first]
+    sendm, heldm = reduce(*product(q1, first, [scaled], inner))
     sendm, first = lax.optimization_barrier((sendm, first))
     gotm = finish(sendm)
-    send1, held1 = reduce(*product(q1, scaled, first, inner))
+    send1, held1 = reduce(*product(q1, [scaled], first, inner))
     got1 = finish(send1)
     second, got1, gotm = lax.optimization_barrier((second, got1, gotm))
     back = step((heldm + gotm.astype(F32)).astype(BF16), -1)
-    send2, held2 = reduce(*product(q1, scaled, second, inner))
+    send2, held2 = reduce(*product(q1, [scaled], second, inner))
     got2 = finish(send2)
     at = (outer - jnp.arange(OUTER, dtype=I32)) % OUTER
     begun = place(at, [0, 1], [(held0, got0), (held1, got1)])

time: 107 us -> 114 us (1.065)
  waiting for transfers between devices: 51 us -> 58.2 us
    ppermute x3 -> x5, waiting for transfers between devices: 16.1 us -> 34.8 us  [step(): lax.ppermute(array, 'spec', [(i, (i + outers * inner) % n) for i in range...]
    ppermute x25, waiting for transfers between devices: 34.9 us -> 23.4 us  [swap(): return lax.ppermute(array, 'spec', [(i, i ^ bit) for i in range(n)])]
  transfers between devices with their start and end apart: 28 -> 30, of which waited for: 18 -> 16; matrix products, arithmetic and copies ran while one was open for 2% -> 1% of each run, Pallas kernels for 18% -> 15%
where the time goes in v11:
time: 114 us
  waiting for transfers between devices  58.2 us (51%)
  starting transfers between devices  28.3 us (25%)
  Pallas kernels  24.3 us (21%)
  local copies, waits for them, and re-layouts  1.95 us (2%)
  other arithmetic  1.26 us (1%)
    ppermute x5, waiting for transfers between devices, step(): lax.ppermute(array, 'spec', [(i, (i + outers * inner) % n) for i in range...  34.8 us
    ppermute x25, starting transfers between devices, swap(): return lax.ppermute(array, 'spec', [(i, i ^ bit) for i in range(n)])  26.6 us
    ppermute x25, waiting for transfers between devices, swap(): return lax.ppermute(array, 'spec', [(i, i ^ bit) for i in range(n)])  23.4 us
    pallas_call x15, Pallas kernels, call(): pl.pallas_call(kernel, out_shape=out_shape, in_specs=in_specs, out_specs=...  21.3 us
    pallas_call x2, Pallas kernels, place(): pl.pallas_call(functools.partial(place_kernel, slots, last), out_shape=ja...  2.98 us
  transfers between devices with their start and end apart: 30, of which 16 were waited for; matrix products, arithmetic and copies ran while one was open for 1% of the time, Pallas kernels for 15%

profile of v11, /device:TPU:0, one launch (start us, length us, event | category | flops | bytes accessed | tf_op | source)
XLA Modules:
  0.0 114.3 jit_solution(7796088603090758372)
XLA Ops:
  0.0 0.8 pad_add_fusion.3
  0.8 3.0 %collective-permute-start = (s32[148]{0:T(256)S(1)}, s32[148]{0:T(256)S(1)}, u32[]{:S(2)}, u32[]{:S(2)}) collective-permute-start(s32[148]{0:T(256)S(1)} %pad_add_fusion.3), channel_id=1, source_target_pairs={{0,4},{1,5},{2,6},{3,7},{4,0},{5,1},{6,2},{7,3},{8,12},{9,13},{10,... | collective-permute-start | bytes 1784 | tf_op jit(solution)/shard_map/ppermute | solution.py:372
  3.9 2.6 %collective-permute-start.1 = (s32[148]{0:T(256)S(1)}, s32[148]{0:T(256)S(1)}, u32[]{:S(2)}, u32[]{:S(2)}) collective-permute-start(s32[148]{0:T(256)S(1)} %pad_add_fusion.3), channel_id=1, source_target_pairs={{0,8},{1,9},{2,10},{3,11},{4,12},{5,13},{6,14},{7,15},{8,0},{9,1},... | collective-permute-start | bytes 1784 | tf_op jit(solution)/shard_map/ppermute | solution.py:372
  6.5 1.2 %dynamic-slice_bitcast_fusion = (bf16[640,128]{1,0:T(8,128)(2,1)S(1)}, bf16[640,128]{1,0:T(8,128)(2,1)S(1)}, bf16[640,128]{1,0:T(8,128)(2,1)S(1)}, bf16[640,128]{1,0:T(8,128)(2,1)S(1)}) fusion(bf16[4,640,128]{2,1,0:T(8,128)(2,1)} %bitcast.48, s32[]{:T(128)S(6)} %select_n.41, s32[]{:T(128)S(6)} %select_n.40, s32[]{:T(128)S(6)} %select_n.39, s32[]{:T(128)S(6)} %select_n.38), kind=kLoop, calls=%fused_computation.3 | loop fusion | bytes 1310736 | tf_op jit(solution)/shard_map/jit(dynamic_index_in_dim)/squeeze | solution.py:392
  7.7 0.7 collective-permute-done.1
  8.3 3.5 %collective-permute-done.2 = s32[148]{0:T(256)S(1)} collective-permute-done((s32[148]{0:T(256)S(1)}, s32[148]{0:T(256)S(1)}, u32[]{:S(2)}, u32[]{:S(2)}) %collective-permute-start.2) | collective-permute-done | bytes 624 | tf_op jit(solution)/shard_map/ppermute | solution.py:372
  11.8 0.1 collective-permute-start.6
  11.9 0.1 collective-permute-start.3
  12.0 0.6 collective-permute-start.4
  12.6 3.8 %collective-permute-start.5 = (bf16[640,128]{1,0:T(8,128)(2,1)S(1)}, bf16[640,128]{1,0:T(8,128)(2,1)S(1)}, u32[]{:S(2)}, u32[]{:S(2)}) collective-permute-start(bf16[640,128]{1,0:T(8,128)(2,1)S(1)} %get-tuple-element.109), channel_id=1, source_target_pairs={{0,12},{1,13},{2,14},{3,15},{4,8},{5,9},{6,10},{7,11},{8,4},{9,5},... | collective-permute-start | bytes 491528 | tf_op jit(solution)/shard_map/ppermute | solution.py:372
  16.4 1.5 %collective-permute-start.7 = (s32[4,2,20]{2,0,1:T(4,128)S(1)}, s32[4,2,20]{2,0,1:T(4,128)S(1)}, u32[]{:S(2)}, u32[]{:S(2)}) collective-permute-start(s32[4,2,20]{2,0,1:T(4,128)S(1)} %pad_add_fusion.2), channel_id=1, source_target_pairs={{0,2},{1,3},{2,0},{3,1},{4,6},{5,7},{6,4},{7,5},{8,10},{9,11},{10,... | collective-permute-start | bytes 1928 | tf_op jit(solution)/shard_map/ppermute | solution.py:372
  17.9 0.1 pad_add_fusion.5.me_ref
  18.0 0.7 copy-done.1
  18.6 0.2 shard_map.55
  18.9 7.2 %shard_map.56.smoothed_ref = bf16[128,3968]{1,0:T(8,128)(2,1)S(1)} custom-call(bf16[128,3968]{1,0:T(8,128)(2,1)S(1)} %copy-done, bf16[11,128,3968]{2,1,0:T(8,128)(2,1)} %bitcast.46), custom_call_target="tpu_custom_call" | custom-call | flops 1 | bytes 1 | tf_op jit(solution)/shard_map/pallas_call | solution.py:20
  26.2 4.7 %shard_map.57 = (bf16[128,640]{1,0:T(8,128)(2,1)S(1)}, bf16[128,640]{1,0:T(8,128)(2,1)S(1)}, bf16[128,640]{1,0:T(8,128)(2,1)S(1)}, bf16[128,640]{1,0:T(8,128)(2,1)S(1)}) custom-call(s32[2]{0:T(128)S(1)} %pad_add_fusion.5.me_ref, s32[2,128]{1,0:T(2,128)S(1)} %get-tuple-element.57.groups_ref, s32[16,20]{1,0:T(8,128)S(1)} %get-tuple-element.114.starts_ref, ...), custom_call_target="tpu_custom_call" | custom-call | flops 1 | bytes 1 | tf_op jit(solution)/shard_map/pallas_call | solution.py:20
  30.9 0.1 pad_maximum_fusion.refs_2_
  31.0 0.1 collective-permute-start.10
  31.1 0.6 collective-permute-start.8
  31.7 0.6 collective-permute-start.9
  32.3 3.7 %collective-permute-start.12 = (bf16[128,640]{1,0:T(8,128)(2,1)S(1)}, bf16[128,640]{1,0:T(8,128)(2,1)S(1)}, u32[]{:S(2)}, u32[]{:S(2)}) collective-permute-start(bf16[128,640]{1,0:T(8,128)(2,1)S(1)} %get-tuple-element.72), channel_id=1, source_target_pairs={{0,12},{1,13},{2,14},{3,15},{4,8},{5,9},{6,10},{7,11},{8,4},{9,5},... | collective-permute-start | bytes 491528 | tf_op jit(solution)/shard_map/ppermute | solution.py:372
  36.1 0.1 pad_add_fusion.6.bins_ref
  36.2 0.1 slice.8.names_ref
  36.2 4.1 %collective-permute-done.9.refs_1_ = bf16[128,640]{1,0:T(8,128)(2,1)S(1)} collective-permute-done((bf16[128,640]{1,0:T(8,128)(2,1)S(1)}, bf16[128,640]{1,0:T(8,128)(2,1)S(1)}, u32[]{:S(2)}, u32[]{:S(2)}) %collective-permute-start.9) | collective-permute-done | bytes 163872 | tf_op jit(solution)/shard_map/ppermute | solution.py:372
  40.4 1.5 %shard_map.58.refs_4_ = f32[256,640]{1,0:T(8,128)S(1)} custom-call(s32[8]{0:T(128)S(1)} %pad_add_fusion.6.bins_ref, s32[4,128]{1,0:T(4,128)S(1)} %slice.8.names_ref, bf16[128,640]{1,0:T(8,128)(2,1)S(1)} %get-tuple-element.73.refs_0_, bf16[128,640]{1,0:T(8,128)(2,1)S(1)} %collective-permute-done.9.refs_1_, bf16[4,640,128]{2,1,0:T(8,128)(2,1)S(1)} %pad_maximum_fusion.refs_2_, ...), custom_call_target="tpu_custom_call" | custom-call | flops 1 | bytes 1 | tf_op jit(solution)/shard_map/pallas_call | solution.py:20
  41.9 5.4 %collective-permute-done.11.refs_0_.refs_2_ = bf16[128,640]{1,0:T(8,128)(2,1)S(1)} collective-permute-done((bf16[128,640]{1,0:T(8,128)(2,1)S(1)}, bf16[128,640]{1,0:T(8,128)(2,1)S(1)}, u32[]{:S(2)}, u32[]{:S(2)}) %collective-permute-start.11) | collective-permute-done | bytes 163872 | tf_op jit(solution)/shard_map/ppermute | solution.py:372
  47.3 0.9 collective-permute-done.8.refs_6_
  48.3 0.1 pad_add_fusion.4.bins_ref
  48.4 1.5 %shard_map.59.refs_5_ = f32[256,640]{1,0:T(8,128)S(1)} custom-call(s32[8]{0:T(128)S(1)} %pad_add_fusion.6.bins_ref, s32[4,128]{1,0:T(4,128)S(1)} %slice.8.names_ref, bf16[128,640]{1,0:T(8,128)(2,1)S(1)} %collective-permute-done.11.refs_0_.refs_2_, bf16[128,640]{1,0:T(8,128)(2,1)S(1)} %collective-permute-done.12.refs_1_.refs_3_, ...), custom_call_target="tpu_custom_call" | custom-call | flops 1 | bytes 1 | tf_op jit(solution)/shard_map/pallas_call | solution.py:20
  49.9 0.5 collective-permute-done.13.refs_7_
  50.4 2.3 %shard_map.60 = (f32[512,640]{1,0:T(8,128)S(1)}, bf16[512,384]{1,0:T(8,128)(2,1)S(1)}, bf16[512,256]{1,0:T(8,128)(2,1)S(1)}, f32[4,128]{1,0:T(4,128)S(1)}) custom-call(s32[1]{0:T(128)} %bitcast.1.outer_ref, s32[8]{0:T(128)S(1)} %pad_add_fusion.4.bins_ref, s32[4,128]{1,0:T(4,128)S(1)} %slice.8.names_ref, bf16[128,640]{1,0:T(8,128)(2,1)S(1)} %get-tuple-element.73.refs_0_, ...), custom_call_target="tpu_custom_call" | custom-call | flops 1 | bytes 1 | tf_op jit(solution)/shard_map/pallas_call | solution.py:20
  52.6 2.2 %collective-permute-start.14 = (f32[4,128]{1,0:T(4,128)S(1)}, f32[4,128]{1,0:T(4,128)S(1)}, u32[]{:S(2)}, u32[]{:S(2)}) collective-permute-start(f32[4,128]{1,0:T(4,128)S(1)} %get-tuple-element.80), channel_id=1, source_target_pairs={{0,4},{1,5},{2,6},{3,7},{4,0},{5,1},{6,2},{7,3},{8,12},{9,13},{10,... | collective-permute-start | bytes 6152 | tf_op jit(solution)/shard_map/ppermute | solution.py:372
  54.8 0.1 collective-permute-start.15
  54.9 2.3 %collective-permute-start.16 = (f32[4,128]{1,0:T(4,128)S(1)}, f32[4,128]{1,0:T(4,128)S(1)}, u32[]{:S(2)}, u32[]{:S(2)}) collective-permute-start(f32[4,128]{1,0:T(4,128)S(1)} %get-tuple-element.80), channel_id=1, source_target_pairs={{0,12},{1,13},{2,14},{3,15},{4,8},{5,9},{6,10},{7,11},{8,4},{9,5},... | collective-permute-start | bytes 6152 | tf_op jit(solution)/shard_map/ppermute | solution.py:372
  57.2 2.0 %collective-permute-done.15 = f32[4,128]{1,0:T(4,128)S(1)} collective-permute-done((f32[4,128]{1,0:T(4,128)S(1)}, f32[4,128]{1,0:T(4,128)S(1)}, u32[]{:S(2)}, u32[]{:S(2)}) %collective-permute-start.15) | collective-permute-done | bytes 2080 | tf_op jit(solution)/shard_map/ppermute | solution.py:372
  59.3 1.0 collective-permute-done.16
  60.3 0.2 shard_map.61.refs_0_.refs_2_
  60.5 0.8 shard_map.62
  61.3 0.1 collective-permute-start.19
  61.4 0.2 collective-permute-start.17
  61.6 1.5 %collective-permute-start.18 = (bf16[512,256]{1,0:T(8,128)(2,1)S(1)}, bf16[512,256]{1,0:T(8,128)(2,1)S(1)}, u32[]{:S(2)}, u32[]{:S(2)}) collective-permute-start(bf16[512,256]{1,0:T(8,128)(2,1)S(1)} %get-tuple-element.82.refs_2_), channel_id=1, source_target_pairs={{0,4},{1,5},{2,6},{3,7},{4,8},{5,9},{6,10},{7,11},{8,12},{9,13},{1... | collective-permute-start | bytes 786440 | tf_op jit(solution)/shard_map/ppermute | solution.py:375
  63.0 0.1 collective-permute-done.19.got_ref
  63.1 0.1 shard_map.63
  63.2 1.2 %collective-permute-start.20 = (bf16[1,160,640]{2,1,0:T(8,128)(2,1)S(1)}, bf16[1,160,640]{2,1,0:T(8,128)(2,1)S(1)}, u32[]{:S(2)}, u32[]{:S(2)}) collective-permute-start(bf16[1,160,640]{2,1,0:T(8,128)(2,1)S(1)} %get-tuple-element.85), channel_id=1, source_target_pairs={{0,2},{1,3},{2,0},{3,1},{4,6},{5,7},{6,4},{7,5},{8,10},{9,11},{10,... | collective-permute-start | bytes 614408 | tf_op jit(solution)/shard_map/ppermute | solution.py:372
  64.4 15.9 %collective-permute-done.18.refs_1_.refs_2_ = bf16[512,256]{1,0:T(8,128)(2,1)S(1)} collective-permute-done((bf16[512,256]{1,0:T(8,128)(2,1)S(1)}, bf16[512,256]{1,0:T(8,128)(2,1)S(1)}, u32[]{:S(2)}, u32[]{:S(2)}) %collective-permute-start.18) | collective-permute-done | bytes 262176 | tf_op jit(solution)/shard_map/ppermute | solution.py:375
  80.3 0.8 shard_map.64
  81.2 0.1 collective-permute-start.23
  81.2 1.7 %collective-permute-done.23.got_ref = bf16[2,160,640]{2,1,0:T(8,128)(2,1)S(1)} collective-permute-done((bf16[2,160,640]{2,1,0:T(8,128)(2,1)S(1)}, bf16[2,160,640]{2,1,0:T(8,128)(2,1)S(1)}, u32[]{:S(2)}, u32[]{:S(2)}) %collective-permute-start.23) | collective-permute-done | bytes 409632 | tf_op jit(solution)/shard_map/ppermute | solution.py:372
  83.0 0.1 shard_map.65
  83.1 0.8 shard_map.66
  83.9 0.2 collective-permute-start.24
  84.1 1.2 %collective-permute-start.26 = (bf16[1,160,640]{2,1,0:T(8,128)(2,1)S(1)}, bf16[1,160,640]{2,1,0:T(8,128)(2,1)S(1)}, u32[]{:S(2)}, u32[]{:S(2)}) collective-permute-start(bf16[1,160,640]{2,1,0:T(8,128)(2,1)S(1)} %get-tuple-element.96), channel_id=1, source_target_pairs={{0,2},{1,3},{2,0},{3,1},{4,6},{5,7},{6,4},{7,5},{8,10},{9,11},{10,... | collective-permute-start | bytes 614408 | tf_op jit(solution)/shard_map/ppermute | solution.py:372
  85.3 0.4 collective-permute-done.24.got_ref
  85.7 0.1 shard_map.67
  85.8 1.2 %collective-permute-start.25 = (bf16[1,160,640]{2,1,0:T(8,128)(2,1)S(1)}, bf16[1,160,640]{2,1,0:T(8,128)(2,1)S(1)}, u32[]{:S(2)}, u32[]{:S(2)}) collective-permute-start(bf16[1,160,640]{2,1,0:T(8,128)(2,1)S(1)} %get-tuple-element.95), channel_id=1, source_target_pairs={{0,2},{1,3},{2,0},{3,1},{4,6},{5,7},{6,4},{7,5},{8,10},{9,11},{10,... | collective-permute-start | bytes 614408 | tf_op jit(solution)/shard_map/ppermute | solution.py:372
  87.0 15.9 %collective-permute-done.22.refs_2_ = bf16[512,256]{1,0:T(8,128)(2,1)S(1)} collective-permute-done((bf16[512,256]{1,0:T(8,128)(2,1)S(1)}, bf16[512,256]{1,0:T(8,128)(2,1)S(1)}, u32[]{:S(2)}, u32[]{:S(2)}) %collective-permute-start.22) | collective-permute-done | bytes 262176 | tf_op jit(solution)/shard_map/ppermute | solution.py:375
  102.9 0.8 shard_map.68
  103.7 0.1 collective-permute-start.27
  103.9 1.6 %collective-permute-done.27.got_ref = bf16[2,160,640]{2,1,0:T(8,128)(2,1)S(1)} collective-permute-done((bf16[2,160,640]{2,1,0:T(8,128)(2,1)S(1)}, bf16[2,160,640]{2,1,0:T(8,128)(2,1)S(1)}, u32[]{:S(2)}, u32[]{:S(2)}) %collective-permute-start.27) | collective-permute-done | bytes 409632 | tf_op jit(solution)/shard_map/ppermute | solution.py:372
  105.6 1.2 %collective-permute-start.28 = (bf16[1,160,640]{2,1,0:T(8,128)(2,1)S(1)}, bf16[1,160,640]{2,1,0:T(8,128)(2,1)S(1)}, u32[]{:S(2)}, u32[]{:S(2)}) collective-permute-start(bf16[1,160,640]{2,1,0:T(8,128)(2,1)S(1)} %get-tuple-element.102), channel_id=1, source_target_pairs={{0,2},{1,3},{2,0},{3,1},{4,6},{5,7},{6,4},{7,5},{8,10},{9,11},{10,... | collective-permute-start | bytes 614408 | tf_op jit(solution)/shard_map/ppermute | solution.py:372
  106.9 1.5 %shard_map.70.refs_4_ = f32[160,2560]{1,0:T(8,128)} custom-call(s32[4]{0:T(128)S(1)} %and_select_fusion.at_ref, f32[160,640]{1,0:T(8,128)S(1)} %bitcast.38, bf16[160,640]{1,0:T(8,128)(2,1)S(1)} %bitcast.41, f32[160,640]{1,0:T(8,128)S(1)} %bitcast.39, bf16[160,640]{1,0:T(8,128)(2,1)S(1)} %bitcast.42), custom_call_target="tpu_custom_call" | custom-call | flops 1 | bytes 1 | tf_op jit(solution)/shard_map/pallas_call | solution.py:346
  108.4 3.0 %collective-permute-done.29.refs_2_ = bf16[160,640]{1,0:T(8,128)(2,1)S(1)} collective-permute-done((bf16[160,640]{1,0:T(8,128)(2,1)S(1)}, bf16[160,640]{1,0:T(8,128)(2,1)S(1)}, u32[]{:S(2)}, u32[]{:S(2)}) %collective-permute-start.29) | collective-permute-done | bytes 204832 | tf_op jit(solution)/shard_map/ppermute | solution.py:375
  111.4 1.4 %collective-permute-done.28 = bf16[1,160,640]{2,1,0:T(8,128)(2,1)S(1)} collective-permute-done((bf16[1,160,640]{2,1,0:T(8,128)(2,1)S(1)}, bf16[1,160,640]{2,1,0:T(8,128)(2,1)S(1)}, u32[]{:S(2)}, u32[]{:S(2)}) %collective-permute-start.28) | collective-permute-done | bytes 204832 | tf_op jit(solution)/shard_map/ppermute | solution.py:372
  112.8 1.5 %shard_map.71 = f32[160,2560]{1,0:T(8,128)} custom-call(s32[4]{0:T(128)S(1)} %and_select_fusion.at_ref, f32[160,640]{1,0:T(8,128)S(1)} %bitcast.40, bf16[160,640]{1,0:T(8,128)(2,1)S(1)} %bitcast.43, bf16[160,640]{1,0:T(8,128)(2,1)S(1)} %collective-permute-done.29.refs_2_, ...), custom_call_target="tpu_custom_call", output_to_operand_aliasing={{}: (5, {})} | custom-call | flops 1 | bytes 1 | tf_op jit(solution)/shard_map/pallas_call | solution.py:346
  (36 shorter events, 0.3 us)
Async XLA Ops:
  0.0 18.9 %copy-start = (bf16[128,3968]{1,0:T(8,128)(2,1)S(1)}, bf16[128,3968]{1,0:T(8,128)(2,1)}, u32[]{:S(2)}) copy-start(bf16[128,3968]{1,0:T(8,128)(2,1)} %flux_ref) | copy-start | bytes 3047428
  0.8 6.8 %collective-permute-start = (s32[148]{0:T(256)S(1)}, s32[148]{0:T(256)S(1)}, u32[]{:S(2)}, u32[]{:S(2)}) collective-permute-start(s32[148]{0:T(256)S(1)} %pad_add_fusion.3), channel_id=1, source_target_pairs={{0,4},{1,5},{2,6},{3,7},{4,0},{5,1},{6,2},{7,3},{8,12},{9,13},{10,... | collective-permute-start | bytes 1784 | tf_op jit(solution)/shard_map/ppermute | solution.py:372
  3.9 4.5 %collective-permute-start.1 = (s32[148]{0:T(256)S(1)}, s32[148]{0:T(256)S(1)}, u32[]{:S(2)}, u32[]{:S(2)}) collective-permute-start(s32[148]{0:T(256)S(1)} %pad_add_fusion.3), channel_id=1, source_target_pairs={{0,8},{1,9},{2,10},{3,11},{4,12},{5,13},{6,14},{7,15},{8,0},{9,1},... | collective-permute-start | bytes 1784 | tf_op jit(solution)/shard_map/ppermute | solution.py:372
  6.4 5.4 %collective-permute-start.2 = (s32[148]{0:T(256)S(1)}, s32[148]{0:T(256)S(1)}, u32[]{:S(2)}, u32[]{:S(2)}) collective-permute-start(s32[148]{0:T(256)S(1)} %pad_add_fusion.3), channel_id=1, source_target_pairs={{0,12},{1,13},{2,14},{3,15},{4,8},{5,9},{6,10},{7,11},{8,4},{9,5},... | collective-permute-start | bytes 1784 | tf_op jit(solution)/shard_map/ppermute | solution.py:372
  11.8 4.5 %collective-permute-start.6 = (s32[4,1,20]{2,0,1:T(4,128)S(1)}, s32[4,1,20]{2,0,1:T(4,128)S(1)}, u32[]{:S(2)}, u32[]{:S(2)}) collective-permute-start(s32[4,1,20]{2,0,1:T(4,128)S(1)} %slice_bitcast_fusion), channel_id=1, source_target_pairs={{0,1},{1,0},{2,3},{3,2},{4,5},{5,4},{6,7},{7,6},{8,9},{9,8},{10,11... | collective-permute-start | bytes 968 | tf_op jit(solution)/shard_map/ppermute | solution.py:372
  11.9 19.0 %collective-permute-start.3 = (bf16[640,128]{1,0:T(8,128)(2,1)S(1)}, bf16[640,128]{1,0:T(8,128)(2,1)S(1)}, u32[]{:S(2)}, u32[]{:S(2)}) collective-permute-start(bf16[640,128]{1,0:T(8,128)(2,1)S(1)} %get-tuple-element.111), channel_id=1, source_target_pairs={{0,4},{1,5},{2,6},{3,7},{4,0},{5,1},{6,2},{7,3},{8,12},{9,13},{10,... | collective-permute-start | bytes 491528 | tf_op jit(solution)/shard_map/ppermute | solution.py:372
  12.0 18.9 %collective-permute-start.4 = (bf16[640,128]{1,0:T(8,128)(2,1)S(1)}, bf16[640,128]{1,0:T(8,128)(2,1)S(1)}, u32[]{:S(2)}, u32[]{:S(2)}) collective-permute-start(bf16[640,128]{1,0:T(8,128)(2,1)S(1)} %get-tuple-element.110), channel_id=1, source_target_pairs={{0,8},{1,9},{2,10},{3,11},{4,12},{5,13},{6,14},{7,15},{8,0},{9,1},... | collective-permute-start | bytes 491528 | tf_op jit(solution)/shard_map/ppermute | solution.py:372
  12.6 18.4 %collective-permute-start.5 = (bf16[640,128]{1,0:T(8,128)(2,1)S(1)}, bf16[640,128]{1,0:T(8,128)(2,1)S(1)}, u32[]{:S(2)}, u32[]{:S(2)}) collective-permute-start(bf16[640,128]{1,0:T(8,128)(2,1)S(1)} %get-tuple-element.109), channel_id=1, source_target_pairs={{0,12},{1,13},{2,14},{3,15},{4,8},{5,9},{6,10},{7,11},{8,4},{9,5},... | collective-permute-start | bytes 491528 | tf_op jit(solution)/shard_map/ppermute | solution.py:372
  16.4 9.8 %collective-permute-start.7 = (s32[4,2,20]{2,0,1:T(4,128)S(1)}, s32[4,2,20]{2,0,1:T(4,128)S(1)}, u32[]{:S(2)}, u32[]{:S(2)}) collective-permute-start(s32[4,2,20]{2,0,1:T(4,128)S(1)} %pad_add_fusion.2), channel_id=1, source_target_pairs={{0,2},{1,3},{2,0},{3,1},{4,6},{5,7},{6,4},{7,5},{8,10},{9,11},{10,... | collective-permute-start | bytes 1928 | tf_op jit(solution)/shard_map/ppermute | solution.py:372
  18.0 0.7 copy-start.1
  31.0 9.3 %collective-permute-start.10 = (bf16[4,640,128]{2,1,0:T(8,128)(2,1)S(1)}, bf16[4,640,128]{2,1,0:T(8,128)(2,1)S(1)}, u32[]{:S(2)}, u32[]{:S(2)}) collective-permute-start(bf16[4,640,128]{2,1,0:T(8,128)(2,1)S(1)} %pad_maximum_fusion.refs_2_), channel_id=1, source_target_pairs={{0,1},{1,0},{2,3},{3,2},{4,5},{5,4},{6,7},{7,6},{8,9},{9,8},{10,11... | collective-permute-start | bytes 1966088 | tf_op jit(solution)/shard_map/ppermute | solution.py:372
  31.1 17.1 %collective-permute-start.8 = (bf16[4,640,128]{2,1,0:T(8,128)(2,1)S(1)}, bf16[4,640,128]{2,1,0:T(8,128)(2,1)S(1)}, u32[]{:S(2)}, u32[]{:S(2)}) collective-permute-start(bf16[4,640,128]{2,1,0:T(8,128)(2,1)S(1)} %pad_maximum_fusion.refs_2_), channel_id=1, source_target_pairs={{0,2},{1,3},{2,0},{3,1},{4,6},{5,7},{6,4},{7,5},{8,10},{9,11},{10,... | collective-permute-start | bytes 1966088 | tf_op jit(solution)/shard_map/ppermute | solution.py:372
  31.7 8.7 %collective-permute-start.9 = (bf16[128,640]{1,0:T(8,128)(2,1)S(1)}, bf16[128,640]{1,0:T(8,128)(2,1)S(1)}, u32[]{:S(2)}, u32[]{:S(2)}) collective-permute-start(bf16[128,640]{1,0:T(8,128)(2,1)S(1)} %get-tuple-element.70), channel_id=1, source_target_pairs={{0,4},{1,5},{2,6},{3,7},{4,0},{5,1},{6,2},{7,3},{8,12},{9,13},{10,... | collective-permute-start | bytes 491528 | tf_op jit(solution)/shard_map/ppermute | solution.py:372
  32.3 15.0 %collective-permute-start.11 = (bf16[128,640]{1,0:T(8,128)(2,1)S(1)}, bf16[128,640]{1,0:T(8,128)(2,1)S(1)}, u32[]{:S(2)}, u32[]{:S(2)}) collective-permute-start(bf16[128,640]{1,0:T(8,128)(2,1)S(1)} %get-tuple-element.71), channel_id=1, source_target_pairs={{0,8},{1,9},{2,10},{3,11},{4,12},{5,13},{6,14},{7,15},{8,0},{9,1},... | collective-permute-start | bytes 491528 | tf_op jit(solution)/shard_map/ppermute | solution.py:372
  32.3 15.0 %collective-permute-start.12 = (bf16[128,640]{1,0:T(8,128)(2,1)S(1)}, bf16[128,640]{1,0:T(8,128)(2,1)S(1)}, u32[]{:S(2)}, u32[]{:S(2)}) collective-permute-start(bf16[128,640]{1,0:T(8,128)(2,1)S(1)} %get-tuple-element.72), channel_id=1, source_target_pairs={{0,12},{1,13},{2,14},{3,15},{4,8},{5,9},{6,10},{7,11},{8,4},{9,5},... | collective-permute-start | bytes 491528 | tf_op jit(solution)/shard_map/ppermute | solution.py:372
  48.3 2.1 %collective-permute-start.13 = (bf16[4,640,128]{2,1,0:T(8,128)(2,1)S(1)}, bf16[4,640,128]{2,1,0:T(8,128)(2,1)S(1)}, u32[]{:S(2)}, u32[]{:S(2)}) collective-permute-start(bf16[4,640,128]{2,1,0:T(8,128)(2,1)S(1)} %collective-permute-done.8.refs_6_), channel_id=1, source_target_pairs={{0,1},{1,0},{2,3},{3,2},{4,5},{5,4},{6,7},{7,6},{8,9},{9,8},{10,11... | collective-permute-start | bytes 1966088 | tf_op jit(solution)/shard_map/ppermute | solution.py:372
  52.6 4.6 %collective-permute-start.14 = (f32[4,128]{1,0:T(4,128)S(1)}, f32[4,128]{1,0:T(4,128)S(1)}, u32[]{:S(2)}, u32[]{:S(2)}) collective-permute-start(f32[4,128]{1,0:T(4,128)S(1)} %get-tuple-element.80), channel_id=1, source_target_pairs={{0,4},{1,5},{2,6},{3,7},{4,0},{5,1},{6,2},{7,3},{8,12},{9,13},{10,... | collective-permute-start | bytes 6152 | tf_op jit(solution)/shard_map/ppermute | solution.py:372
  54.8 4.5 %collective-permute-start.15 = (f32[4,128]{1,0:T(4,128)S(1)}, f32[4,128]{1,0:T(4,128)S(1)}, u32[]{:S(2)}, u32[]{:S(2)}) collective-permute-start(f32[4,128]{1,0:T(4,128)S(1)} %get-tuple-element.80), channel_id=1, source_target_pairs={{0,8},{1,9},{2,10},{3,11},{4,12},{5,13},{6,14},{7,15},{8,0},{9,1},... | collective-permute-start | bytes 6152 | tf_op jit(solution)/shard_map/ppermute | solution.py:372
  54.9 5.4 %collective-permute-start.16 = (f32[4,128]{1,0:T(4,128)S(1)}, f32[4,128]{1,0:T(4,128)S(1)}, u32[]{:S(2)}, u32[]{:S(2)}) collective-permute-start(f32[4,128]{1,0:T(4,128)S(1)} %get-tuple-element.80), channel_id=1, source_target_pairs={{0,12},{1,13},{2,14},{3,15},{4,8},{5,9},{6,10},{7,11},{8,4},{9,5},... | collective-permute-start | bytes 6152 | tf_op jit(solution)/shard_map/ppermute | solution.py:372
  61.3 1.8 %collective-permute-start.19 = (bf16[2,160,640]{2,1,0:T(8,128)(2,1)S(1)}, bf16[2,160,640]{2,1,0:T(8,128)(2,1)S(1)}, u32[]{:S(2)}, u32[]{:S(2)}) collective-permute-start(bf16[2,160,640]{2,1,0:T(8,128)(2,1)S(1)} %get-tuple-element.84), channel_id=1, source_target_pairs={{0,1},{1,0},{2,3},{3,2},{4,5},{5,4},{6,7},{7,6},{8,9},{9,8},{10,11... | collective-permute-start | bytes 1228808 | tf_op jit(solution)/shard_map/ppermute | solution.py:372
  61.4 18.9 %collective-permute-start.17 = (bf16[512,384]{1,0:T(8,128)(2,1)S(1)}, bf16[512,384]{1,0:T(8,128)(2,1)S(1)}, u32[]{:S(2)}, u32[]{:S(2)}) collective-permute-start(bf16[512,384]{1,0:T(8,128)(2,1)S(1)} %get-tuple-element.81.refs_1_), channel_id=1, source_target_pairs={{0,4},{1,5},{2,6},{3,7},{4,8},{5,9},{6,10},{7,11},{8,12},{9,13},{1... | collective-permute-start | bytes 1179656 | tf_op jit(solution)/shard_map/ppermute | solution.py:375
  61.6 18.7 %collective-permute-start.18 = (bf16[512,256]{1,0:T(8,128)(2,1)S(1)}, bf16[512,256]{1,0:T(8,128)(2,1)S(1)}, u32[]{:S(2)}, u32[]{:S(2)}) collective-permute-start(bf16[512,256]{1,0:T(8,128)(2,1)S(1)} %get-tuple-element.82.refs_2_), channel_id=1, source_target_pairs={{0,4},{1,5},{2,6},{3,7},{4,8},{5,9},{6,10},{7,11},{8,12},{9,13},{1... | collective-permute-start | bytes 786440 | tf_op jit(solution)/shard_map/ppermute | solution.py:375
  63.2 17.1 %collective-permute-start.20 = (bf16[1,160,640]{2,1,0:T(8,128)(2,1)S(1)}, bf16[1,160,640]{2,1,0:T(8,128)(2,1)S(1)}, u32[]{:S(2)}, u32[]{:S(2)}) collective-permute-start(bf16[1,160,640]{2,1,0:T(8,128)(2,1)S(1)} %get-tuple-element.85), channel_id=1, source_target_pairs={{0,2},{1,3},{2,0},{3,1},{4,6},{5,7},{6,4},{7,5},{8,10},{9,11},{10,... | collective-permute-start | bytes 614408 | tf_op jit(solution)/shard_map/ppermute | solution.py:372
  81.2 1.8 %collective-permute-start.23 = (bf16[2,160,640]{2,1,0:T(8,128)(2,1)S(1)}, bf16[2,160,640]{2,1,0:T(8,128)(2,1)S(1)}, u32[]{:S(2)}, u32[]{:S(2)}) collective-permute-start(bf16[2,160,640]{2,1,0:T(8,128)(2,1)S(1)} %get-tuple-element.89), channel_id=1, source_target_pairs={{0,1},{1,0},{2,3},{3,2},{4,5},{5,4},{6,7},{7,6},{8,9},{9,8},{10,11... | collective-permute-start | bytes 1228808 | tf_op jit(solution)/shard_map/ppermute | solution.py:372
  83.9 1.8 %collective-permute-start.24 = (bf16[2,160,640]{2,1,0:T(8,128)(2,1)S(1)}, bf16[2,160,640]{2,1,0:T(8,128)(2,1)S(1)}, u32[]{:S(2)}, u32[]{:S(2)}) collective-permute-start(bf16[2,160,640]{2,1,0:T(8,128)(2,1)S(1)} %get-tuple-element.94), channel_id=1, source_target_pairs={{0,1},{1,0},{2,3},{3,2},{4,5},{5,4},{6,7},{7,6},{8,9},{9,8},{10,11... | collective-permute-start | bytes 1228808 | tf_op jit(solution)/shard_map/ppermute | solution.py:372
  84.1 18.8 %collective-permute-start.21 = (bf16[512,384]{1,0:T(8,128)(2,1)S(1)}, bf16[512,384]{1,0:T(8,128)(2,1)S(1)}, u32[]{:S(2)}, u32[]{:S(2)}) collective-permute-start(bf16[512,384]{1,0:T(8,128)(2,1)S(1)} %collective-permute-done.17.refs_0_.refs_1_), channel_id=1, source_target_pairs={{0,4},{1,5},{2,6},{3,7},{4,8},{5,9},{6,10},{7,11},{8,12},{9,13},{1... | collective-permute-start | bytes 1179656 | tf_op jit(solution)/shard_map/ppermute | solution.py:375
  84.1 18.8 %collective-permute-start.22 = (bf16[512,256]{1,0:T(8,128)(2,1)S(1)}, bf16[512,256]{1,0:T(8,128)(2,1)S(1)}, u32[]{:S(2)}, u32[]{:S(2)}) collective-permute-start(bf16[512,256]{1,0:T(8,128)(2,1)S(1)} %collective-permute-done.18.refs_1_.refs_2_), channel_id=1, source_target_pairs={{0,4},{1,5},{2,6},{3,7},{4,8},{5,9},{6,10},{7,11},{8,12},{9,13},{1... | collective-permute-start | bytes 786440 | tf_op jit(solution)/shard_map/ppermute | solution.py:375
  84.1 18.8 %collective-permute-start.26 = (bf16[1,160,640]{2,1,0:T(8,128)(2,1)S(1)}, bf16[1,160,640]{2,1,0:T(8,128)(2,1)S(1)}, u32[]{:S(2)}, u32[]{:S(2)}) collective-permute-start(bf16[1,160,640]{2,1,0:T(8,128)(2,1)S(1)} %get-tuple-element.96), channel_id=1, source_target_pairs={{0,2},{1,3},{2,0},{3,1},{4,6},{5,7},{6,4},{7,5},{8,10},{9,11},{10,... | collective-permute-start | bytes 614408 | tf_op jit(solution)/shard_map/ppermute | solution.py:372
  85.8 17.1 %collective-permute-start.25 = (bf16[1,160,640]{2,1,0:T(8,128)(2,1)S(1)}, bf16[1,160,640]{2,1,0:T(8,128)(2,1)S(1)}, u32[]{:S(2)}, u32[]{:S(2)}) collective-permute-start(bf16[1,160,640]{2,1,0:T(8,128)(2,1)S(1)} %get-tuple-element.95), channel_id=1, source_target_pairs={{0,2},{1,3},{2,0},{3,1},{4,6},{5,7},{6,4},{7,5},{8,10},{9,11},{10,... | collective-permute-start | bytes 614408 | tf_op jit(solution)/shard_map/ppermute | solution.py:372
  103.7 1.8 %collective-permute-start.27 = (bf16[2,160,640]{2,1,0:T(8,128)(2,1)S(1)}, bf16[2,160,640]{2,1,0:T(8,128)(2,1)S(1)}, u32[]{:S(2)}, u32[]{:S(2)}) collective-permute-start(bf16[2,160,640]{2,1,0:T(8,128)(2,1)S(1)} %get-tuple-element.100), channel_id=1, source_target_pairs={{0,1},{1,0},{2,3},{3,2},{4,5},{5,4},{6,7},{7,6},{8,9},{9,8},{10,11... | collective-permute-start | bytes 1228808 | tf_op jit(solution)/shard_map/ppermute | solution.py:372
  103.9 7.5 %collective-permute-start.29 = (bf16[160,640]{1,0:T(8,128)(2,1)S(1)}, bf16[160,640]{1,0:T(8,128)(2,1)S(1)}, u32[]{:S(2)}, u32[]{:S(2)}) collective-permute-start(bf16[160,640]{1,0:T(8,128)(2,1)S(1)} %fusion), channel_id=1, source_target_pairs={{0,12},{1,13},{2,14},{3,15},{4,0},{5,1},{6,2},{7,3},{8,4},{9,5},{1... | collective-permute-start | bytes 614408 | tf_op jit(solution)/shard_map/ppermute | solution.py:375
  105.6 7.2 %collective-permute-start.28 = (bf16[1,160,640]{2,1,0:T(8,128)(2,1)S(1)}, bf16[1,160,640]{2,1,0:T(8,128)(2,1)S(1)}, u32[]{:S(2)}, u32[]{:S(2)}) collective-permute-start(bf16[1,160,640]{2,1,0:T(8,128)(2,1)S(1)} %get-tuple-element.102), channel_id=1, source_target_pairs={{0,2},{1,3},{2,0},{3,1},{4,6},{5,7},{6,4},{7,5},{8,10},{9,11},{10,... | collective-permute-start | bytes 614408 | tf_op jit(solution)/shard_map/ppermute | solution.py:372

commit v12 on v10

--- a/solution.py
+++ b/solution.py
@@ -359,8 +359,14 @@
     def swap(array, bit):
         return lax.ppermute(array, "spec", [(i, i ^ bit) for i in range(n)])
 
-    def step(array, outers):
-        return lax.ppermute(array, "spec", [(i, (i + outers * inner) % n) for i in range(n)])
+    def fold_at(place):
+        return place ^ (place >> 1)
+
+    def step(array, places):
+        to = [fold_at((fold_at(o) + places) % OUTER) for o in range(OUTER)]
+        return lax.ppermute(
+            array, "spec", [(o * inner + i, to[o] * inner + i) for o in range(OUTER) for i in range(inner)]
+        )
 
     targets = destination[:, 0]
     table = jnp.concatenate([band_offset[0], targets])
@@ -446,7 +452,7 @@
     back = step((heldm + gotm.astype(F32)).astype(BF16), -1)
     send2, held2 = reduce(*product(q1, scaled, second, inner))
     got2 = finish(send2)
-    at = (outer - jnp.arange(OUTER, dtype=I32)) % OUTER
+    at = fold_at((fold_at(outer) - jnp.arange(OUTER, dtype=I32)) % OUTER)
     begun = place(at, [0, 1], [(held0, got0), (held1, got1)])
     return place(at, [2, 3], [(held2, got2), (back, jnp.zeros_like(back))], begun)
 

time: 107 us -> 105 us (0.981)
  waiting for transfers between devices: 51 us -> 49.2 us
    ppermute x3, waiting for transfers between devices: 16.1 us -> 14.3 us  [step(): lax.ppermute(array, 'spec', [(o * inner + i, to[o] * inner + i) for o in...]
where the time goes in v12:
time: 105 us
  waiting for transfers between devices  49.2 us (47%)
  starting transfers between devices  27.7 us (26%)
  Pallas kernels  24.2 us (23%)
  local copies, waits for them, and re-layouts  1.95 us (2%)
  other arithmetic  1.27 us (1%)
    ppermute x25, waiting for transfers between devices, swap(): return lax.ppermute(array, 'spec', [(i, i ^ bit) for i in range(n)])  34.9 us
    ppermute x25, starting transfers between devices, swap(): return lax.ppermute(array, 'spec', [(i, i ^ bit) for i in range(n)])  26.6 us
    pallas_call x15, Pallas kernels, call(): pl.pallas_call(kernel, out_shape=out_shape, in_specs=in_specs, out_specs=...  21.3 us
    ppermute x3, waiting for transfers between devices, step(): lax.ppermute(array, 'spec', [(o * inner + i, to[o] * inner + i) for o in...  14.3 us
    pallas_call x2, Pallas kernels, place(): pl.pallas_call(functools.partial(place_kernel, slots, last), out_shape=ja...  2.96 us
  transfers between devices with their start and end apart: 28, of which 18 were waited for; matrix products, arithmetic and copies ran while one was open for 2% of the time, Pallas kernels for 18%

profile of v12, /device:TPU:0, one launch (start us, length us, event | category | flops | bytes accessed | tf_op | source)
XLA Modules:
  0.0 104.7 jit_solution(2890842869318360178)
XLA Ops:
  0.0 0.8 pad_add_fusion.3
  0.8 3.0 %collective-permute-start = (s32[148]{0:T(256)S(1)}, s32[148]{0:T(256)S(1)}, u32[]{:S(2)}, u32[]{:S(2)}) collective-permute-start(s32[148]{0:T(256)S(1)} %pad_add_fusion.3), channel_id=1, source_target_pairs={{0,4},{1,5},{2,6},{3,7},{4,0},{5,1},{6,2},{7,3},{8,12},{9,13},{10,... | collective-permute-start | bytes 1784 | tf_op jit(solution)/shard_map/ppermute | solution.py:360
  3.9 2.6 %collective-permute-start.1 = (s32[148]{0:T(256)S(1)}, s32[148]{0:T(256)S(1)}, u32[]{:S(2)}, u32[]{:S(2)}) collective-permute-start(s32[148]{0:T(256)S(1)} %pad_add_fusion.3), channel_id=1, source_target_pairs={{0,8},{1,9},{2,10},{3,11},{4,12},{5,13},{6,14},{7,15},{8,0},{9,1},... | collective-permute-start | bytes 1784 | tf_op jit(solution)/shard_map/ppermute | solution.py:360
  6.5 1.2 %dynamic-slice_bitcast_fusion = (bf16[640,128]{1,0:T(8,128)(2,1)S(1)}, bf16[640,128]{1,0:T(8,128)(2,1)S(1)}, bf16[640,128]{1,0:T(8,128)(2,1)S(1)}, bf16[640,128]{1,0:T(8,128)(2,1)S(1)}) fusion(bf16[4,640,128]{2,1,0:T(8,128)(2,1)} %bitcast.48, s32[]{:T(128)S(6)} %select_n.41, s32[]{:T(128)S(6)} %select_n.40, s32[]{:T(128)S(6)} %select_n.39, s32[]{:T(128)S(6)} %select_n.38), kind=kLoop, calls=%fused_computation.3 | loop fusion | bytes 1310736 | tf_op jit(solution)/shard_map/jit(dynamic_index_in_dim)/squeeze | solution.py:386
  7.7 0.7 collective-permute-done.1
  8.3 3.5 %collective-permute-done.2 = s32[148]{0:T(256)S(1)} collective-permute-done((s32[148]{0:T(256)S(1)}, s32[148]{0:T(256)S(1)}, u32[]{:S(2)}, u32[]{:S(2)}) %collective-permute-start.2) | collective-permute-done | bytes 624 | tf_op jit(solution)/shard_map/ppermute | solution.py:360
  11.8 0.1 collective-permute-start.6
  11.9 0.1 collective-permute-start.3
  12.0 0.6 collective-permute-start.4
  12.6 3.8 %collective-permute-start.5 = (bf16[640,128]{1,0:T(8,128)(2,1)S(1)}, bf16[640,128]{1,0:T(8,128)(2,1)S(1)}, u32[]{:S(2)}, u32[]{:S(2)}) collective-permute-start(bf16[640,128]{1,0:T(8,128)(2,1)S(1)} %get-tuple-element.101), channel_id=1, source_target_pairs={{0,12},{1,13},{2,14},{3,15},{4,8},{5,9},{6,10},{7,11},{8,4},{9,5},... | collective-permute-start | bytes 491528 | tf_op jit(solution)/shard_map/ppermute | solution.py:360
  16.4 1.5 %collective-permute-start.7 = (s32[4,2,20]{2,0,1:T(4,128)S(1)}, s32[4,2,20]{2,0,1:T(4,128)S(1)}, u32[]{:S(2)}, u32[]{:S(2)}) collective-permute-start(s32[4,2,20]{2,0,1:T(4,128)S(1)} %pad_add_fusion.2), channel_id=1, source_target_pairs={{0,2},{1,3},{2,0},{3,1},{4,6},{5,7},{6,4},{7,5},{8,10},{9,11},{10,... | collective-permute-start | bytes 1928 | tf_op jit(solution)/shard_map/ppermute | solution.py:360
  17.9 0.1 pad_add_fusion.5.me_ref
  18.0 0.7 copy-done.1
  18.6 0.2 shard_map.55
  18.9 7.2 %shard_map.56.smoothed_ref = bf16[128,3968]{1,0:T(8,128)(2,1)S(1)} custom-call(bf16[128,3968]{1,0:T(8,128)(2,1)S(1)} %copy-done, bf16[11,128,3968]{2,1,0:T(8,128)(2,1)} %bitcast.46), custom_call_target="tpu_custom_call" | custom-call | flops 1 | bytes 1 | tf_op jit(solution)/shard_map/pallas_call | solution.py:20
  26.2 4.7 %shard_map.57 = (bf16[128,640]{1,0:T(8,128)(2,1)S(1)}, bf16[128,640]{1,0:T(8,128)(2,1)S(1)}, bf16[128,640]{1,0:T(8,128)(2,1)S(1)}, bf16[128,640]{1,0:T(8,128)(2,1)S(1)}) custom-call(s32[2]{0:T(128)S(1)} %pad_add_fusion.5.me_ref, s32[2,128]{1,0:T(2,128)S(1)} %get-tuple-element.53.groups_ref, s32[16,20]{1,0:T(8,128)S(1)} %get-tuple-element.106.starts_ref, ...), custom_call_target="tpu_custom_call" | custom-call | flops 1 | bytes 1 | tf_op jit(solution)/shard_map/pallas_call | solution.py:20
  30.9 0.1 pad_maximum_fusion.refs_2_
  31.0 0.1 collective-permute-start.10
  31.1 0.6 collective-permute-start.8
  31.7 0.6 collective-permute-start.9
  32.3 3.7 %collective-permute-start.12 = (bf16[128,640]{1,0:T(8,128)(2,1)S(1)}, bf16[128,640]{1,0:T(8,128)(2,1)S(1)}, u32[]{:S(2)}, u32[]{:S(2)}) collective-permute-start(bf16[128,640]{1,0:T(8,128)(2,1)S(1)} %get-tuple-element.68), channel_id=1, source_target_pairs={{0,12},{1,13},{2,14},{3,15},{4,8},{5,9},{6,10},{7,11},{8,4},{9,5},... | collective-permute-start | bytes 491528 | tf_op jit(solution)/shard_map/ppermute | solution.py:360
  36.1 0.1 pad_add_fusion.6.bins_ref
  36.2 0.1 slice.8.names_ref
  36.2 4.1 %collective-permute-done.9.refs_1_ = bf16[128,640]{1,0:T(8,128)(2,1)S(1)} collective-permute-done((bf16[128,640]{1,0:T(8,128)(2,1)S(1)}, bf16[128,640]{1,0:T(8,128)(2,1)S(1)}, u32[]{:S(2)}, u32[]{:S(2)}) %collective-permute-start.9) | collective-permute-done | bytes 163872 | tf_op jit(solution)/shard_map/ppermute | solution.py:360
  40.4 1.5 %shard_map.58.refs_4_ = f32[256,640]{1,0:T(8,128)S(1)} custom-call(s32[8]{0:T(128)S(1)} %pad_add_fusion.6.bins_ref, s32[4,128]{1,0:T(4,128)S(1)} %slice.8.names_ref, bf16[128,640]{1,0:T(8,128)(2,1)S(1)} %get-tuple-element.69.refs_0_, bf16[128,640]{1,0:T(8,128)(2,1)S(1)} %collective-permute-done.9.refs_1_, bf16[4,640,128]{2,1,0:T(8,128)(2,1)S(1)} %pad_maximum_fusion.refs_2_, ...), custom_call_target="tpu_custom_call" | custom-call | flops 1 | bytes 1 | tf_op jit(solution)/shard_map/pallas_call | solution.py:20
  41.9 5.4 %collective-permute-done.11.refs_0_.refs_2_ = bf16[128,640]{1,0:T(8,128)(2,1)S(1)} collective-permute-done((bf16[128,640]{1,0:T(8,128)(2,1)S(1)}, bf16[128,640]{1,0:T(8,128)(2,1)S(1)}, u32[]{:S(2)}, u32[]{:S(2)}) %collective-permute-start.11) | collective-permute-done | bytes 163872 | tf_op jit(solution)/shard_map/ppermute | solution.py:360
  47.3 0.9 collective-permute-done.8.refs_6_
  48.3 0.1 pad_add_fusion.4.bins_ref
  48.4 1.5 %shard_map.59.refs_5_ = f32[256,640]{1,0:T(8,128)S(1)} custom-call(s32[8]{0:T(128)S(1)} %pad_add_fusion.6.bins_ref, s32[4,128]{1,0:T(4,128)S(1)} %slice.8.names_ref, bf16[128,640]{1,0:T(8,128)(2,1)S(1)} %collective-permute-done.11.refs_0_.refs_2_, bf16[128,640]{1,0:T(8,128)(2,1)S(1)} %collective-permute-done.12.refs_1_.refs_3_, ...), custom_call_target="tpu_custom_call" | custom-call | flops 1 | bytes 1 | tf_op jit(solution)/shard_map/pallas_call | solution.py:20
  49.9 0.5 collective-permute-done.13.refs_7_
  50.4 2.3 %shard_map.60 = (f32[512,640]{1,0:T(8,128)S(1)}, bf16[512,640]{1,0:T(8,128)(2,1)S(1)}, f32[4,128]{1,0:T(4,128)S(1)}) custom-call(s32[1]{0:T(128)} %bitcast.1.outer_ref, s32[8]{0:T(128)S(1)} %pad_add_fusion.4.bins_ref, s32[4,128]{1,0:T(4,128)S(1)} %slice.8.names_ref, bf16[128,640]{1,0:T(8,128)(2,1)S(1)} %get-tuple-element.69.refs_0_, ...), custom_call_target="tpu_custom_call" | custom-call | flops 1 | bytes 1 | tf_op jit(solution)/shard_map/pallas_call | solution.py:20
  52.7 2.1 %collective-permute-start.14 = (f32[4,128]{1,0:T(4,128)S(1)}, f32[4,128]{1,0:T(4,128)S(1)}, u32[]{:S(2)}, u32[]{:S(2)}) collective-permute-start(f32[4,128]{1,0:T(4,128)S(1)} %get-tuple-element.76), channel_id=1, source_target_pairs={{0,4},{1,5},{2,6},{3,7},{4,0},{5,1},{6,2},{7,3},{8,12},{9,13},{10,... | collective-permute-start | bytes 6152 | tf_op jit(solution)/shard_map/ppermute | solution.py:360
  54.8 0.1 collective-permute-start.15
  54.9 2.3 %collective-permute-start.16 = (f32[4,128]{1,0:T(4,128)S(1)}, f32[4,128]{1,0:T(4,128)S(1)}, u32[]{:S(2)}, u32[]{:S(2)}) collective-permute-start(f32[4,128]{1,0:T(4,128)S(1)} %get-tuple-element.76), channel_id=1, source_target_pairs={{0,12},{1,13},{2,14},{3,15},{4,8},{5,9},{6,10},{7,11},{8,4},{9,5},... | collective-permute-start | bytes 6152 | tf_op jit(solution)/shard_map/ppermute | solution.py:360
  57.3 1.0 %collective-permute-start.17 = (bf16[512,640]{1,0:T(8,128)(2,1)S(1)}, bf16[512,640]{1,0:T(8,128)(2,1)S(1)}, u32[]{:S(2)}, u32[]{:S(2)}) collective-permute-start(bf16[512,640]{1,0:T(8,128)(2,1)S(1)} %get-tuple-element.77.wide_ref), channel_id=1, source_target_pairs={{0,4},{1,5},{2,6},{3,7},{4,12},{5,13},{6,14},{7,15},{8,0},{9,1},{1... | collective-permute-start | bytes 1966088 | tf_op jit(solution)/shard_map/ppermute | solution.py:367
  58.3 1.0 collective-permute-done.15
  59.3 1.0 collective-permute-done.16
  60.3 0.2 shard_map.61.tall_ref.wide_ref
  60.5 0.8 shard_map.62
  61.3 0.1 collective-permute-start.18
  61.4 1.7 %collective-permute-done.18.got_ref = bf16[2,160,640]{2,1,0:T(8,128)(2,1)S(1)} collective-permute-done((bf16[2,160,640]{2,1,0:T(8,128)(2,1)S(1)}, bf16[2,160,640]{2,1,0:T(8,128)(2,1)S(1)}, u32[]{:S(2)}, u32[]{:S(2)}) %collective-permute-start.18) | collective-permute-done | bytes 409632 | tf_op jit(solution)/shard_map/ppermute | solution.py:360
  63.1 0.1 shard_map.63
  63.2 1.2 %collective-permute-start.19 = (bf16[1,160,640]{2,1,0:T(8,128)(2,1)S(1)}, bf16[1,160,640]{2,1,0:T(8,128)(2,1)S(1)}, u32[]{:S(2)}, u32[]{:S(2)}) collective-permute-start(bf16[1,160,640]{2,1,0:T(8,128)(2,1)S(1)} %get-tuple-element.80), channel_id=1, source_target_pairs={{0,2},{1,3},{2,0},{3,1},{4,6},{5,7},{6,4},{7,5},{8,10},{9,11},{10,... | collective-permute-start | bytes 614408 | tf_op jit(solution)/shard_map/ppermute | solution.py:360
  64.5 6.0 %collective-permute-done.19 = bf16[1,160,640]{2,1,0:T(8,128)(2,1)S(1)} collective-permute-done((bf16[1,160,640]{2,1,0:T(8,128)(2,1)S(1)}, bf16[1,160,640]{2,1,0:T(8,128)(2,1)S(1)}, u32[]{:S(2)}, u32[]{:S(2)}) %collective-permute-start.19) | collective-permute-done | bytes 204832 | tf_op jit(solution)/shard_map/ppermute | solution.py:360
  70.4 4.0 %collective-permute-done.17.tall_ref.wide_ref = bf16[512,640]{1,0:T(8,128)(2,1)S(1)} collective-permute-done((bf16[512,640]{1,0:T(8,128)(2,1)S(1)}, bf16[512,640]{1,0:T(8,128)(2,1)S(1)}, u32[]{:S(2)}, u32[]{:S(2)}) %collective-permute-start.17) | collective-permute-done | bytes 655392 | tf_op jit(solution)/shard_map/ppermute | solution.py:367
  74.4 0.8 shard_map.64
  75.2 0.1 collective-permute-start.21
  75.3 1.7 %collective-permute-done.21.got_ref = bf16[2,160,640]{2,1,0:T(8,128)(2,1)S(1)} collective-permute-done((bf16[2,160,640]{2,1,0:T(8,128)(2,1)S(1)}, bf16[2,160,640]{2,1,0:T(8,128)(2,1)S(1)}, u32[]{:S(2)}, u32[]{:S(2)}) %collective-permute-start.21) | collective-permute-done | bytes 409632 | tf_op jit(solution)/shard_map/ppermute | solution.py:360
  77.0 0.1 shard_map.65
  77.1 0.8 shard_map.66
  77.9 0.2 collective-permute-start.22
  78.1 1.2 %collective-permute-start.24 = (bf16[1,160,640]{2,1,0:T(8,128)(2,1)S(1)}, bf16[1,160,640]{2,1,0:T(8,128)(2,1)S(1)}, u32[]{:S(2)}, u32[]{:S(2)}) collective-permute-start(bf16[1,160,640]{2,1,0:T(8,128)(2,1)S(1)} %get-tuple-element.89), channel_id=1, source_target_pairs={{0,2},{1,3},{2,0},{3,1},{4,6},{5,7},{6,4},{7,5},{8,10},{9,11},{10,... | collective-permute-start | bytes 614408 | tf_op jit(solution)/shard_map/ppermute | solution.py:360
  79.3 0.4 collective-permute-done.22.got_ref
  79.7 0.1 shard_map.67
  79.8 1.2 %collective-permute-start.23 = (bf16[1,160,640]{2,1,0:T(8,128)(2,1)S(1)}, bf16[1,160,640]{2,1,0:T(8,128)(2,1)S(1)}, u32[]{:S(2)}, u32[]{:S(2)}) collective-permute-start(bf16[1,160,640]{2,1,0:T(8,128)(2,1)S(1)} %get-tuple-element.88), channel_id=1, source_target_pairs={{0,2},{1,3},{2,0},{3,1},{4,6},{5,7},{6,4},{7,5},{8,10},{9,11},{10,... | collective-permute-start | bytes 614408 | tf_op jit(solution)/shard_map/ppermute | solution.py:360
  81.0 5.0 %collective-permute-done.24 = bf16[1,160,640]{2,1,0:T(8,128)(2,1)S(1)} collective-permute-done((bf16[1,160,640]{2,1,0:T(8,128)(2,1)S(1)}, bf16[1,160,640]{2,1,0:T(8,128)(2,1)S(1)}, u32[]{:S(2)}, u32[]{:S(2)}) %collective-permute-start.24) | collective-permute-done | bytes 204832 | tf_op jit(solution)/shard_map/ppermute | solution.py:360
  86.0 7.3 %collective-permute-done.20.wide_ref = bf16[512,640]{1,0:T(8,128)(2,1)S(1)} collective-permute-done((bf16[512,640]{1,0:T(8,128)(2,1)S(1)}, bf16[512,640]{1,0:T(8,128)(2,1)S(1)}, u32[]{:S(2)}, u32[]{:S(2)}) %collective-permute-start.20) | collective-permute-done | bytes 655392 | tf_op jit(solution)/shard_map/ppermute | solution.py:367
  93.3 0.8 shard_map.68
  94.3 1.6 %collective-permute-done.25.got_ref = bf16[2,160,640]{2,1,0:T(8,128)(2,1)S(1)} collective-permute-done((bf16[2,160,640]{2,1,0:T(8,128)(2,1)S(1)}, bf16[2,160,640]{2,1,0:T(8,128)(2,1)S(1)}, u32[]{:S(2)}, u32[]{:S(2)}) %collective-permute-start.25) | collective-permute-done | bytes 409632 | tf_op jit(solution)/shard_map/ppermute | solution.py:360
  96.0 1.2 %collective-permute-start.26 = (bf16[1,160,640]{2,1,0:T(8,128)(2,1)S(1)}, bf16[1,160,640]{2,1,0:T(8,128)(2,1)S(1)}, u32[]{:S(2)}, u32[]{:S(2)}) collective-permute-start(bf16[1,160,640]{2,1,0:T(8,128)(2,1)S(1)} %get-tuple-element.94), channel_id=1, source_target_pairs={{0,2},{1,3},{2,0},{3,1},{4,6},{5,7},{6,4},{7,5},{8,10},{9,11},{10,... | collective-permute-start | bytes 614408 | tf_op jit(solution)/shard_map/ppermute | solution.py:360
  97.3 1.5 %shard_map.70.refs_4_ = f32[160,2560]{1,0:T(8,128)} custom-call(s32[4]{0:T(128)S(1)} %shift-right-arithmetic_xor_fusion.at_ref, f32[160,640]{1,0:T(8,128)S(1)} %bitcast.38, bf16[160,640]{1,0:T(8,128)(2,1)S(1)} %bitcast.41, f32[160,640]{1,0:T(8,128)S(1)} %bitcast.39, bf16[160,640]{1,0:T(8,128)(2,1)S(1)} %bitcast.42), custom_call_target="tpu_custom_call" | custom-call | flops 1 | bytes 1 | tf_op jit(solution)/shard_map/pallas_call | solution.py:334
  98.8 3.0 %collective-permute-done.27.refs_2_ = bf16[160,640]{1,0:T(8,128)(2,1)S(1)} collective-permute-done((bf16[160,640]{1,0:T(8,128)(2,1)S(1)}, bf16[160,640]{1,0:T(8,128)(2,1)S(1)}, u32[]{:S(2)}, u32[]{:S(2)}) %collective-permute-start.27) | collective-permute-done | bytes 204832 | tf_op jit(solution)/shard_map/ppermute | solution.py:367
  101.8 1.4 %collective-permute-done.26 = bf16[1,160,640]{2,1,0:T(8,128)(2,1)S(1)} collective-permute-done((bf16[1,160,640]{2,1,0:T(8,128)(2,1)S(1)}, bf16[1,160,640]{2,1,0:T(8,128)(2,1)S(1)}, u32[]{:S(2)}, u32[]{:S(2)}) %collective-permute-start.26) | collective-permute-done | bytes 204832 | tf_op jit(solution)/shard_map/ppermute | solution.py:360
  103.2 1.5 %shard_map.71 = f32[160,2560]{1,0:T(8,128)} custom-call(s32[4]{0:T(128)S(1)} %shift-right-arithmetic_xor_fusion.at_ref, f32[160,640]{1,0:T(8,128)S(1)} %bitcast.40, bf16[160,640]{1,0:T(8,128)(2,1)S(1)} %bitcast.43, bf16[160,640]{1,0:T(8,128)(2,1)S(1)} %collective-permute-done.27.refs_2_, ...), custom_call_target="tpu_custom_call", output_to_operand_aliasing={{}: (5, {})} | custom-call | flops 1 | bytes 1 | tf_op jit(solution)/shard_map/pallas_call | solution.py:334
  (32 shorter events, 0.5 us)
Async XLA Ops:
  0.0 18.9 %copy-start = (bf16[128,3968]{1,0:T(8,128)(2,1)S(1)}, bf16[128,3968]{1,0:T(8,128)(2,1)}, u32[]{:S(2)}) copy-start(bf16[128,3968]{1,0:T(8,128)(2,1)} %flux_ref) | copy-start | bytes 3047428
  0.8 6.8 %collective-permute-start = (s32[148]{0:T(256)S(1)}, s32[148]{0:T(256)S(1)}, u32[]{:S(2)}, u32[]{:S(2)}) collective-permute-start(s32[148]{0:T(256)S(1)} %pad_add_fusion.3), channel_id=1, source_target_pairs={{0,4},{1,5},{2,6},{3,7},{4,0},{5,1},{6,2},{7,3},{8,12},{9,13},{10,... | collective-permute-start | bytes 1784 | tf_op jit(solution)/shard_map/ppermute | solution.py:360
  3.9 4.5 %collective-permute-start.1 = (s32[148]{0:T(256)S(1)}, s32[148]{0:T(256)S(1)}, u32[]{:S(2)}, u32[]{:S(2)}) collective-permute-start(s32[148]{0:T(256)S(1)} %pad_add_fusion.3), channel_id=1, source_target_pairs={{0,8},{1,9},{2,10},{3,11},{4,12},{5,13},{6,14},{7,15},{8,0},{9,1},... | collective-permute-start | bytes 1784 | tf_op jit(solution)/shard_map/ppermute | solution.py:360
  6.4 5.4 %collective-permute-start.2 = (s32[148]{0:T(256)S(1)}, s32[148]{0:T(256)S(1)}, u32[]{:S(2)}, u32[]{:S(2)}) collective-permute-start(s32[148]{0:T(256)S(1)} %pad_add_fusion.3), channel_id=1, source_target_pairs={{0,12},{1,13},{2,14},{3,15},{4,8},{5,9},{6,10},{7,11},{8,4},{9,5},... | collective-permute-start | bytes 1784 | tf_op jit(solution)/shard_map/ppermute | solution.py:360
  11.8 4.5 %collective-permute-start.6 = (s32[4,1,20]{2,0,1:T(4,128)S(1)}, s32[4,1,20]{2,0,1:T(4,128)S(1)}, u32[]{:S(2)}, u32[]{:S(2)}) collective-permute-start(s32[4,1,20]{2,0,1:T(4,128)S(1)} %slice_bitcast_fusion), channel_id=1, source_target_pairs={{0,1},{1,0},{2,3},{3,2},{4,5},{5,4},{6,7},{7,6},{8,9},{9,8},{10,11... | collective-permute-start | bytes 968 | tf_op jit(solution)/shard_map/ppermute | solution.py:360
  11.9 19.0 %collective-permute-start.3 = (bf16[640,128]{1,0:T(8,128)(2,1)S(1)}, bf16[640,128]{1,0:T(8,128)(2,1)S(1)}, u32[]{:S(2)}, u32[]{:S(2)}) collective-permute-start(bf16[640,128]{1,0:T(8,128)(2,1)S(1)} %get-tuple-element.103), channel_id=1, source_target_pairs={{0,4},{1,5},{2,6},{3,7},{4,0},{5,1},{6,2},{7,3},{8,12},{9,13},{10,... | collective-permute-start | bytes 491528 | tf_op jit(solution)/shard_map/ppermute | solution.py:360
  12.0 18.9 %collective-permute-start.4 = (bf16[640,128]{1,0:T(8,128)(2,1)S(1)}, bf16[640,128]{1,0:T(8,128)(2,1)S(1)}, u32[]{:S(2)}, u32[]{:S(2)}) collective-permute-start(bf16[640,128]{1,0:T(8,128)(2,1)S(1)} %get-tuple-element.102), channel_id=1, source_target_pairs={{0,8},{1,9},{2,10},{3,11},{4,12},{5,13},{6,14},{7,15},{8,0},{9,1},... | collective-permute-start | bytes 491528 | tf_op jit(solution)/shard_map/ppermute | solution.py:360
  12.6 18.4 %collective-permute-start.5 = (bf16[640,128]{1,0:T(8,128)(2,1)S(1)}, bf16[640,128]{1,0:T(8,128)(2,1)S(1)}, u32[]{:S(2)}, u32[]{:S(2)}) collective-permute-start(bf16[640,128]{1,0:T(8,128)(2,1)S(1)} %get-tuple-element.101), channel_id=1, source_target_pairs={{0,12},{1,13},{2,14},{3,15},{4,8},{5,9},{6,10},{7,11},{8,4},{9,5},... | collective-permute-start | bytes 491528 | tf_op jit(solution)/shard_map/ppermute | solution.py:360
  16.4 9.8 %collective-permute-start.7 = (s32[4,2,20]{2,0,1:T(4,128)S(1)}, s32[4,2,20]{2,0,1:T(4,128)S(1)}, u32[]{:S(2)}, u32[]{:S(2)}) collective-permute-start(s32[4,2,20]{2,0,1:T(4,128)S(1)} %pad_add_fusion.2), channel_id=1, source_target_pairs={{0,2},{1,3},{2,0},{3,1},{4,6},{5,7},{6,4},{7,5},{8,10},{9,11},{10,... | collective-permute-start | bytes 1928 | tf_op jit(solution)/shard_map/ppermute | solution.py:360
  18.0 0.7 copy-start.1
  31.0 9.3 %collective-permute-start.10 = (bf16[4,640,128]{2,1,0:T(8,128)(2,1)S(1)}, bf16[4,640,128]{2,1,0:T(8,128)(2,1)S(1)}, u32[]{:S(2)}, u32[]{:S(2)}) collective-permute-start(bf16[4,640,128]{2,1,0:T(8,128)(2,1)S(1)} %pad_maximum_fusion.refs_2_), channel_id=1, source_target_pairs={{0,1},{1,0},{2,3},{3,2},{4,5},{5,4},{6,7},{7,6},{8,9},{9,8},{10,11... | collective-permute-start | bytes 1966088 | tf_op jit(solution)/shard_map/ppermute | solution.py:360
  31.1 17.1 %collective-permute-start.8 = (bf16[4,640,128]{2,1,0:T(8,128)(2,1)S(1)}, bf16[4,640,128]{2,1,0:T(8,128)(2,1)S(1)}, u32[]{:S(2)}, u32[]{:S(2)}) collective-permute-start(bf16[4,640,128]{2,1,0:T(8,128)(2,1)S(1)} %pad_maximum_fusion.refs_2_), channel_id=1, source_target_pairs={{0,2},{1,3},{2,0},{3,1},{4,6},{5,7},{6,4},{7,5},{8,10},{9,11},{10,... | collective-permute-start | bytes 1966088 | tf_op jit(solution)/shard_map/ppermute | solution.py:360
  31.7 8.7 %collective-permute-start.9 = (bf16[128,640]{1,0:T(8,128)(2,1)S(1)}, bf16[128,640]{1,0:T(8,128)(2,1)S(1)}, u32[]{:S(2)}, u32[]{:S(2)}) collective-permute-start(bf16[128,640]{1,0:T(8,128)(2,1)S(1)} %get-tuple-element.66), channel_id=1, source_target_pairs={{0,4},{1,5},{2,6},{3,7},{4,0},{5,1},{6,2},{7,3},{8,12},{9,13},{10,... | collective-permute-start | bytes 491528 | tf_op jit(solution)/shard_map/ppermute | solution.py:360
  32.3 15.0 %collective-permute-start.11 = (bf16[128,640]{1,0:T(8,128)(2,1)S(1)}, bf16[128,640]{1,0:T(8,128)(2,1)S(1)}, u32[]{:S(2)}, u32[]{:S(2)}) collective-permute-start(bf16[128,640]{1,0:T(8,128)(2,1)S(1)} %get-tuple-element.67), channel_id=1, source_target_pairs={{0,8},{1,9},{2,10},{3,11},{4,12},{5,13},{6,14},{7,15},{8,0},{9,1},... | collective-permute-start | bytes 491528 | tf_op jit(solution)/shard_map/ppermute | solution.py:360
  32.3 15.0 %collective-permute-start.12 = (bf16[128,640]{1,0:T(8,128)(2,1)S(1)}, bf16[128,640]{1,0:T(8,128)(2,1)S(1)}, u32[]{:S(2)}, u32[]{:S(2)}) collective-permute-start(bf16[128,640]{1,0:T(8,128)(2,1)S(1)} %get-tuple-element.68), channel_id=1, source_target_pairs={{0,12},{1,13},{2,14},{3,15},{4,8},{5,9},{6,10},{7,11},{8,4},{9,5},... | collective-permute-start | bytes 491528 | tf_op jit(solution)/shard_map/ppermute | solution.py:360
  48.3 2.1 %collective-permute-start.13 = (bf16[4,640,128]{2,1,0:T(8,128)(2,1)S(1)}, bf16[4,640,128]{2,1,0:T(8,128)(2,1)S(1)}, u32[]{:S(2)}, u32[]{:S(2)}) collective-permute-start(bf16[4,640,128]{2,1,0:T(8,128)(2,1)S(1)} %collective-permute-done.8.refs_6_), channel_id=1, source_target_pairs={{0,1},{1,0},{2,3},{3,2},{4,5},{5,4},{6,7},{7,6},{8,9},{9,8},{10,11... | collective-permute-start | bytes 1966088 | tf_op jit(solution)/shard_map/ppermute | solution.py:360
  52.7 5.6 %collective-permute-start.14 = (f32[4,128]{1,0:T(4,128)S(1)}, f32[4,128]{1,0:T(4,128)S(1)}, u32[]{:S(2)}, u32[]{:S(2)}) collective-permute-start(f32[4,128]{1,0:T(4,128)S(1)} %get-tuple-element.76), channel_id=1, source_target_pairs={{0,4},{1,5},{2,6},{3,7},{4,0},{5,1},{6,2},{7,3},{8,12},{9,13},{10,... | collective-permute-start | bytes 6152 | tf_op jit(solution)/shard_map/ppermute | solution.py:360
  54.8 4.5 %collective-permute-start.15 = (f32[4,128]{1,0:T(4,128)S(1)}, f32[4,128]{1,0:T(4,128)S(1)}, u32[]{:S(2)}, u32[]{:S(2)}) collective-permute-start(f32[4,128]{1,0:T(4,128)S(1)} %get-tuple-element.76), channel_id=1, source_target_pairs={{0,8},{1,9},{2,10},{3,11},{4,12},{5,13},{6,14},{7,15},{8,0},{9,1},... | collective-permute-start | bytes 6152 | tf_op jit(solution)/shard_map/ppermute | solution.py:360
  54.9 5.4 %collective-permute-start.16 = (f32[4,128]{1,0:T(4,128)S(1)}, f32[4,128]{1,0:T(4,128)S(1)}, u32[]{:S(2)}, u32[]{:S(2)}) collective-permute-start(f32[4,128]{1,0:T(4,128)S(1)} %get-tuple-element.76), channel_id=1, source_target_pairs={{0,12},{1,13},{2,14},{3,15},{4,8},{5,9},{6,10},{7,11},{8,4},{9,5},... | collective-permute-start | bytes 6152 | tf_op jit(solution)/shard_map/ppermute | solution.py:360
  57.3 17.1 %collective-permute-start.17 = (bf16[512,640]{1,0:T(8,128)(2,1)S(1)}, bf16[512,640]{1,0:T(8,128)(2,1)S(1)}, u32[]{:S(2)}, u32[]{:S(2)}) collective-permute-start(bf16[512,640]{1,0:T(8,128)(2,1)S(1)} %get-tuple-element.77.wide_ref), channel_id=1, source_target_pairs={{0,4},{1,5},{2,6},{3,7},{4,12},{5,13},{6,14},{7,15},{8,0},{9,1},{1... | collective-permute-start | bytes 1966088 | tf_op jit(solution)/shard_map/ppermute | solution.py:367
  61.3 1.8 %collective-permute-start.18 = (bf16[2,160,640]{2,1,0:T(8,128)(2,1)S(1)}, bf16[2,160,640]{2,1,0:T(8,128)(2,1)S(1)}, u32[]{:S(2)}, u32[]{:S(2)}) collective-permute-start(bf16[2,160,640]{2,1,0:T(8,128)(2,1)S(1)} %get-tuple-element.79), channel_id=1, source_target_pairs={{0,1},{1,0},{2,3},{3,2},{4,5},{5,4},{6,7},{7,6},{8,9},{9,8},{10,11... | collective-permute-start | bytes 1228808 | tf_op jit(solution)/shard_map/ppermute | solution.py:360
  63.2 7.2 %collective-permute-start.19 = (bf16[1,160,640]{2,1,0:T(8,128)(2,1)S(1)}, bf16[1,160,640]{2,1,0:T(8,128)(2,1)S(1)}, u32[]{:S(2)}, u32[]{:S(2)}) collective-permute-start(bf16[1,160,640]{2,1,0:T(8,128)(2,1)S(1)} %get-tuple-element.80), channel_id=1, source_target_pairs={{0,2},{1,3},{2,0},{3,1},{4,6},{5,7},{6,4},{7,5},{8,10},{9,11},{10,... | collective-permute-start | bytes 614408 | tf_op jit(solution)/shard_map/ppermute | solution.py:360
  75.2 1.8 %collective-permute-start.21 = (bf16[2,160,640]{2,1,0:T(8,128)(2,1)S(1)}, bf16[2,160,640]{2,1,0:T(8,128)(2,1)S(1)}, u32[]{:S(2)}, u32[]{:S(2)}) collective-permute-start(bf16[2,160,640]{2,1,0:T(8,128)(2,1)S(1)} %get-tuple-element.83), channel_id=1, source_target_pairs={{0,1},{1,0},{2,3},{3,2},{4,5},{5,4},{6,7},{7,6},{8,9},{9,8},{10,11... | collective-permute-start | bytes 1228808 | tf_op jit(solution)/shard_map/ppermute | solution.py:360
  75.3 18.0 %collective-permute-start.20 = (bf16[512,640]{1,0:T(8,128)(2,1)S(1)}, bf16[512,640]{1,0:T(8,128)(2,1)S(1)}, u32[]{:S(2)}, u32[]{:S(2)}) collective-permute-start(bf16[512,640]{1,0:T(8,128)(2,1)S(1)} %collective-permute-done.17.tall_ref.wide_ref), channel_id=1, source_target_pairs={{0,4},{1,5},{2,6},{3,7},{4,12},{5,13},{6,14},{7,15},{8,0},{9,1},{1... | collective-permute-start | bytes 1966088 | tf_op jit(solution)/shard_map/ppermute | solution.py:367
  77.9 1.8 %collective-permute-start.22 = (bf16[2,160,640]{2,1,0:T(8,128)(2,1)S(1)}, bf16[2,160,640]{2,1,0:T(8,128)(2,1)S(1)}, u32[]{:S(2)}, u32[]{:S(2)}) collective-permute-start(bf16[2,160,640]{2,1,0:T(8,128)(2,1)S(1)} %get-tuple-element.87), channel_id=1, source_target_pairs={{0,1},{1,0},{2,3},{3,2},{4,5},{5,4},{6,7},{7,6},{8,9},{9,8},{10,11... | collective-permute-start | bytes 1228808 | tf_op jit(solution)/shard_map/ppermute | solution.py:360
  78.1 7.9 %collective-permute-start.24 = (bf16[1,160,640]{2,1,0:T(8,128)(2,1)S(1)}, bf16[1,160,640]{2,1,0:T(8,128)(2,1)S(1)}, u32[]{:S(2)}, u32[]{:S(2)}) collective-permute-start(bf16[1,160,640]{2,1,0:T(8,128)(2,1)S(1)} %get-tuple-element.89), channel_id=1, source_target_pairs={{0,2},{1,3},{2,0},{3,1},{4,6},{5,7},{6,4},{7,5},{8,10},{9,11},{10,... | collective-permute-start | bytes 614408 | tf_op jit(solution)/shard_map/ppermute | solution.py:360
  79.8 13.5 %collective-permute-start.23 = (bf16[1,160,640]{2,1,0:T(8,128)(2,1)S(1)}, bf16[1,160,640]{2,1,0:T(8,128)(2,1)S(1)}, u32[]{:S(2)}, u32[]{:S(2)}) collective-permute-start(bf16[1,160,640]{2,1,0:T(8,128)(2,1)S(1)} %get-tuple-element.88), channel_id=1, source_target_pairs={{0,2},{1,3},{2,0},{3,1},{4,6},{5,7},{6,4},{7,5},{8,10},{9,11},{10,... | collective-permute-start | bytes 614408 | tf_op jit(solution)/shard_map/ppermute | solution.py:360
  94.1 1.8 %collective-permute-start.25 = (bf16[2,160,640]{2,1,0:T(8,128)(2,1)S(1)}, bf16[2,160,640]{2,1,0:T(8,128)(2,1)S(1)}, u32[]{:S(2)}, u32[]{:S(2)}) collective-permute-start(bf16[2,160,640]{2,1,0:T(8,128)(2,1)S(1)} %get-tuple-element.92), channel_id=1, source_target_pairs={{0,1},{1,0},{2,3},{3,2},{4,5},{5,4},{6,7},{7,6},{8,9},{9,8},{10,11... | collective-permute-start | bytes 1228808 | tf_op jit(solution)/shard_map/ppermute | solution.py:360
  94.3 7.5 %collective-permute-start.27 = (bf16[160,640]{1,0:T(8,128)(2,1)S(1)}, bf16[160,640]{1,0:T(8,128)(2,1)S(1)}, u32[]{:S(2)}, u32[]{:S(2)}) collective-permute-start(bf16[160,640]{1,0:T(8,128)(2,1)S(1)} %fusion), channel_id=1, source_target_pairs={{0,8},{1,9},{2,10},{3,11},{4,0},{5,1},{6,2},{7,3},{8,12},{9,13},{1... | collective-permute-start | bytes 614408 | tf_op jit(solution)/shard_map/ppermute | solution.py:367
  96.0 7.2 %collective-permute-start.26 = (bf16[1,160,640]{2,1,0:T(8,128)(2,1)S(1)}, bf16[1,160,640]{2,1,0:T(8,128)(2,1)S(1)}, u32[]{:S(2)}, u32[]{:S(2)}) collective-permute-start(bf16[1,160,640]{2,1,0:T(8,128)(2,1)S(1)} %get-tuple-element.94), channel_id=1, source_target_pairs={{0,2},{1,3},{2,0},{3,1},{4,6},{5,7},{6,4},{7,5},{8,10},{9,11},{10,... | collective-permute-start | bytes 614408 | tf_op jit(solution)/shard_map/ppermute | solution.py:360

commit v13 on v12

--- a/solution.py
+++ b/solution.py
@@ -225,7 +225,8 @@
 
 def end_kernel(nbegun, npieces, band, outer_ref, bins_ref, names_ref, *refs):
     windows, begun, weights = refs[:OUTER], refs[OUTER : OUTER + nbegun], refs[OUTER + nbegun : OUTER + nbegun + npieces]
-    rest_ref, sent_ref, squares_ref, window, named_ref, value_ref = refs[OUTER + nbegun + npieces :]
+    rest_ref, sent_ref, *sents, squares_ref, window, named_ref, value_ref = refs[OUTER + nbegun + npieces :]
+    split = sents[0].shape[1]
     count, width = windows[0].shape
     row = 0
     for part in begun:
@@ -242,6 +243,8 @@
             value = value_ref[own, at : at + band]
             rest_ref[rows, at : at + band] = value
             sent_ref[rows, at : at + band] = value.astype(BF16)
+            part = int(at >= split)
+            sents[part][rows, at - part * split : at - part * split + band] = value.astype(BF16)
             total = total + value * value
         squares_ref[pl.ds(place, 1), :] = jnp.sum(total.T, axis=0, keepdims=True)
 
@@ -249,11 +252,14 @@
 def end_rest(outer, bins, names, windows, begun, weights, band):
     count, width = windows[0].shape
     rows = OUTER * count
+    split = (width // band + 1) // 2 * band
     return call(
         functools.partial(end_kernel, len(begun), len(weights), band),
         (
             jax.ShapeDtypeStruct((rows, width), F32),
             jax.ShapeDtypeStruct((rows, width), BF16),
+            jax.ShapeDtypeStruct((rows, split), BF16),
+            jax.ShapeDtypeStruct((rows, width - split), BF16),
             jax.ShapeDtypeStruct((OUTER, count), F32),
         ),
         [SMEM, SMEM] + [VMEM] * (1 + OUTER + len(begun) + len(weights)),
@@ -272,11 +278,18 @@
             out_ref[own, at : at + 128] = (rest_ref[own, at : at + 128] * factor).astype(BF16)
 
 
-def product_kernel(q_ref, tall_ref, wide_ref, send_ref, keep_ref, value):
+def product_kernel(ntall, q_ref, *refs):
+    talls, wide_ref, (send_ref, keep_ref, *joined_ref, value) = refs[:ntall], refs[ntall], refs[ntall + 1 :]
     pairs, share, _ = keep_ref.shape
-    value[...] = lax.dot_general(
-        tall_ref[...], wide_ref[...], (((0,), (0,)), ((), ())), preferred_element_type=F32
-    )
+    row = 0
+    for tall in talls:
+        rows = slice(row, row + tall.shape[1])
+        value[rows, :] = lax.dot_general(
+            tall[...], wide_ref[...], (((0,), (0,)), ((), ())), preferred_element_type=F32
+        )
+        if joined_ref:
+            joined_ref[0][:, rows] = tall[...]
+        row += tall.shape[1]
     for e in range(2 * pairs):
         own = value[pl.ds(pl.multiple_of((q_ref[0] ^ e) * share, 8), share), :]
         if e % 2:
@@ -285,14 +298,16 @@
             keep_ref[e // 2] = own
 
 
-def product(q, tall, wide, inner):
-    rows, columns = tall.shape[1], wide.shape[1]
+def product(q, talls, wide, inner, join=False):
+    rows = sum(tall.shape[1] for tall in talls)
+    columns = wide.shape[1]
     shape = (inner // 2, rows // inner, columns)
-    return call(
-        product_kernel,
-        (jax.ShapeDtypeStruct(shape, BF16), jax.ShapeDtypeStruct(shape, F32)),
-        [SMEM, VMEM, VMEM],
-        (q, tall, wide),
+    joined = (jax.ShapeDtypeStruct((wide.shape[0], rows), BF16),) if join else ()
+    return call(
+        functools.partial(product_kernel, len(talls)),
+        (jax.ShapeDtypeStruct(shape, BF16), jax.ShapeDtypeStruct(shape, F32), *joined),
+        [SMEM] + [VMEM] * (len(talls) + 1),
+        (q, *talls, wide),
         [pltpu.VMEM((rows, columns), F32)],
     )
 
@@ -418,11 +433,13 @@
     far = [across]
     for bit in bits:
         far = far + [swap(piece, bit) for piece in far]
-    rest, sent, squares = end_rest(outer1, far_bins, names, arrived, begun, far, band)
-
+    rest, sent, *sents, squares = end_rest(outer1, far_bins, names, arrived, begun, far, band)
+
+    firsts = [step(part, 1) for part in sents]
     total = squares
     for away in range(1, OUTER):
         total = total + swap(squares, away * inner)
+    total, firsts[0] = lax.optimization_barrier((total, firsts[0]))
     scale = lax.rsqrt(total / nrest + 1e-06)
     factor = scale * scale / (count * n)
     scaled = call(scale_kernel, jax.ShapeDtypeStruct(rest.shape, BF16), [VMEM, VMEM], (rest, factor))
@@ -438,19 +455,20 @@
         return swap(send, inner // 2)[0]
 
     q1 = q.reshape(1)
-    send0, held0 = reduce(*product(q1, scaled, sent, inner))
+    send0, held0 = product(q1, [scaled], sent, inner)
+    firsts[1], send0 = lax.optimization_barrier((firsts[1], send0))
+    send0, held0 = reduce(send0, held0)
     got0 = finish(send0)
-    first = step(sent, 1)
-    first, got0 = lax.optimization_barrier((first, got0))
+    sendm, heldm, first = product(q1, firsts, scaled, inner, join=True)
     second = step(first, 1)
-    sendm, heldm = reduce(*product(q1, first, scaled, inner))
+    sendm, heldm = reduce(sendm, heldm)
     sendm, first = lax.optimization_barrier((sendm, first))
     gotm = finish(sendm)
-    send1, held1 = reduce(*product(q1, scaled, first, inner))
+    send1, held1 = reduce(*product(q1, [scaled], first, inner))
     got1 = finish(send1)
-    second, got1, gotm = lax.optimization_barrier((second, got1, gotm))
+    second, got0, got1, gotm = lax.optimization_barrier((second, got0, got1, gotm))
     back = step((heldm + gotm.astype(F32)).astype(BF16), -1)
-    send2, held2 = reduce(*product(q1, scaled, second, inner))
+    send2, held2 = reduce(*product(q1, [scaled], second, inner))
     got2 = finish(send2)
     at = fold_at((fold_at(outer) - jnp.arange(OUTER, dtype=I32)) % OUTER)
     begun = place(at, [0, 1], [(held0, got0), (held1, got1)])

time: 105 us -> 102 us (0.971)
  waiting for transfers between devices: 49.2 us -> 43.7 us
  starting transfers between devices: 27.7 us -> 30.4 us
    ppermute x3 -> x4, waiting for transfers between devices: 14.3 us -> 9.47 us  [step(): lax.ppermute(array, 'spec', [(o * inner + i, to[o] * inner + i) for o in...]
    ppermute x3 -> x4, starting transfers between devices: 1.17 us -> 4.8 us  [step(): lax.ppermute(array, 'spec', [(o * inner + i, to[o] * inner + i) for o in...]
  transfers between devices with their start and end apart: 28 -> 29, of which waited for: 18 -> 18; matrix products, arithmetic and copies ran while one was open for 2% -> 2% of each run, Pallas kernels for 18% -> 18%
where the time goes in v13:
time: 102 us
  waiting for transfers between devices  43.7 us (43%)
  starting transfers between devices  30.4 us (30%)
  Pallas kernels  24.4 us (24%)
  local copies, waits for them, and re-layouts  1.95 us (2%)
  other arithmetic  1.27 us (1%)
    ppermute x25, waiting for transfers between devices, swap(): return lax.ppermute(array, 'spec', [(i, i ^ bit) for i in range(n)])  34.2 us
    ppermute x25, starting transfers between devices, swap(): return lax.ppermute(array, 'spec', [(i, i ^ bit) for i in range(n)])  25.6 us
    pallas_call x15, Pallas kernels, call(): pl.pallas_call(kernel, out_shape=out_shape, in_specs=in_specs, out_specs=...  21.4 us
    ppermute x4, waiting for transfers between devices, step(): lax.ppermute(array, 'spec', [(o * inner + i, to[o] * inner + i) for o in...  9.47 us
    ppermute x4, starting transfers between devices, step(): lax.ppermute(array, 'spec', [(o * inner + i, to[o] * inner + i) for o in...  4.8 us
    pallas_call x2, Pallas kernels, place(): pl.pallas_call(functools.partial(place_kernel, slots, last), out_shape=ja...  2.98 us
  transfers between devices with their start and end apart: 29, of which 18 were waited for; matrix products, arithmetic and copies ran while one was open for 2% of the time, Pallas kernels for 18%

profile of v13, /device:TPU:0, one launch (start us, length us, event | category | flops | bytes accessed | tf_op | source)
XLA Modules:
  0.0 102.0 jit_solution(2115354095122627741)
XLA Ops:
  0.0 0.8 pad_add_fusion.3
  0.8 3.0 %collective-permute-start = (s32[148]{0:T(256)S(1)}, s32[148]{0:T(256)S(1)}, u32[]{:S(2)}, u32[]{:S(2)}) collective-permute-start(s32[148]{0:T(256)S(1)} %pad_add_fusion.3), channel_id=1, source_target_pairs={{0,4},{1,5},{2,6},{3,7},{4,0},{5,1},{6,2},{7,3},{8,12},{9,13},{10,... | collective-permute-start | bytes 1784 | tf_op jit(solution)/shard_map/ppermute | solution.py:375
  3.9 2.6 %collective-permute-start.1 = (s32[148]{0:T(256)S(1)}, s32[148]{0:T(256)S(1)}, u32[]{:S(2)}, u32[]{:S(2)}) collective-permute-start(s32[148]{0:T(256)S(1)} %pad_add_fusion.3), channel_id=1, source_target_pairs={{0,8},{1,9},{2,10},{3,11},{4,12},{5,13},{6,14},{7,15},{8,0},{9,1},... | collective-permute-start | bytes 1784 | tf_op jit(solution)/shard_map/ppermute | solution.py:375
  6.5 1.2 %dynamic-slice_bitcast_fusion = (bf16[640,128]{1,0:T(8,128)(2,1)S(1)}, bf16[640,128]{1,0:T(8,128)(2,1)S(1)}, bf16[640,128]{1,0:T(8,128)(2,1)S(1)}, bf16[640,128]{1,0:T(8,128)(2,1)S(1)}) fusion(bf16[4,640,128]{2,1,0:T(8,128)(2,1)} %bitcast.48, s32[]{:T(128)S(6)} %select_n.41, s32[]{:T(128)S(6)} %select_n.40, s32[]{:T(128)S(6)} %select_n.39, s32[]{:T(128)S(6)} %select_n.38), kind=kLoop, calls=%fused_computation.3 | loop fusion | bytes 1310736 | tf_op jit(solution)/shard_map/jit(dynamic_index_in_dim)/squeeze | solution.py:401
  7.7 0.7 collective-permute-done.1
  8.3 3.5 %collective-permute-done.2 = s32[148]{0:T(256)S(1)} collective-permute-done((s32[148]{0:T(256)S(1)}, s32[148]{0:T(256)S(1)}, u32[]{:S(2)}, u32[]{:S(2)}) %collective-permute-start.2) | collective-permute-done | bytes 624 | tf_op jit(solution)/shard_map/ppermute | solution.py:375
  11.9 0.1 collective-permute-start.3
  12.0 0.6 collective-permute-start.4
  12.6 3.8 %collective-permute-start.5 = (bf16[640,128]{1,0:T(8,128)(2,1)S(1)}, bf16[640,128]{1,0:T(8,128)(2,1)S(1)}, u32[]{:S(2)}, u32[]{:S(2)}) collective-permute-start(bf16[640,128]{1,0:T(8,128)(2,1)S(1)} %get-tuple-element.113), channel_id=1, source_target_pairs={{0,12},{1,13},{2,14},{3,15},{4,8},{5,9},{6,10},{7,11},{8,4},{9,5},... | collective-permute-start | bytes 491528 | tf_op jit(solution)/shard_map/ppermute | solution.py:375
  16.4 1.5 %collective-permute-start.7 = (s32[4,2,20]{2,0,1:T(4,128)S(1)}, s32[4,2,20]{2,0,1:T(4,128)S(1)}, u32[]{:S(2)}, u32[]{:S(2)}) collective-permute-start(s32[4,2,20]{2,0,1:T(4,128)S(1)} %pad_add_fusion.2), channel_id=1, source_target_pairs={{0,2},{1,3},{2,0},{3,1},{4,6},{5,7},{6,4},{7,5},{8,10},{9,11},{10,... | collective-permute-start | bytes 1928 | tf_op jit(solution)/shard_map/ppermute | solution.py:375
  17.9 0.1 pad_add_fusion.5.me_ref
  18.0 0.7 copy-done.1
  18.6 0.2 shard_map.55
  18.9 7.2 %shard_map.56.smoothed_ref = bf16[128,3968]{1,0:T(8,128)(2,1)S(1)} custom-call(bf16[128,3968]{1,0:T(8,128)(2,1)S(1)} %copy-done, bf16[11,128,3968]{2,1,0:T(8,128)(2,1)} %bitcast.46), custom_call_target="tpu_custom_call" | custom-call | flops 1 | bytes 1 | tf_op jit(solution)/shard_map/pallas_call | solution.py:20
  26.2 4.7 %shard_map.57 = (bf16[128,640]{1,0:T(8,128)(2,1)S(1)}, bf16[128,640]{1,0:T(8,128)(2,1)S(1)}, bf16[128,640]{1,0:T(8,128)(2,1)S(1)}, bf16[128,640]{1,0:T(8,128)(2,1)S(1)}) custom-call(s32[2]{0:T(128)S(1)} %pad_add_fusion.5.me_ref, s32[2,128]{1,0:T(2,128)S(1)} %get-tuple-element.59.groups_ref, s32[16,20]{1,0:T(8,128)S(1)} %get-tuple-element.118.starts_ref, ...), custom_call_target="tpu_custom_call" | custom-call | flops 1 | bytes 1 | tf_op jit(solution)/shard_map/pallas_call | solution.py:20
  30.9 0.1 pad_maximum_fusion.refs_2_
  31.1 0.6 collective-permute-start.8
  31.7 0.6 collective-permute-start.9
  32.3 0.2 collective-permute-start.11
  32.5 3.6 %collective-permute-start.12 = (bf16[128,640]{1,0:T(8,128)(2,1)S(1)}, bf16[128,640]{1,0:T(8,128)(2,1)S(1)}, u32[]{:S(2)}, u32[]{:S(2)}) collective-permute-start(bf16[128,640]{1,0:T(8,128)(2,1)S(1)} %get-tuple-element.74), channel_id=1, source_target_pairs={{0,12},{1,13},{2,14},{3,15},{4,8},{5,9},{6,10},{7,11},{8,4},{9,5},... | collective-permute-start | bytes 491528 | tf_op jit(solution)/shard_map/ppermute | solution.py:375
  36.1 0.1 pad_add_fusion.6.bins_ref
  36.2 0.1 slice.8.names_ref
  36.2 4.1 %collective-permute-done.9.refs_1_ = bf16[128,640]{1,0:T(8,128)(2,1)S(1)} collective-permute-done((bf16[128,640]{1,0:T(8,128)(2,1)S(1)}, bf16[128,640]{1,0:T(8,128)(2,1)S(1)}, u32[]{:S(2)}, u32[]{:S(2)}) %collective-permute-start.9) | collective-permute-done | bytes 163872 | tf_op jit(solution)/shard_map/ppermute | solution.py:375
  40.4 1.5 %shard_map.58.refs_4_ = f32[256,640]{1,0:T(8,128)S(1)} custom-call(s32[8]{0:T(128)S(1)} %pad_add_fusion.6.bins_ref, s32[4,128]{1,0:T(4,128)S(1)} %slice.8.names_ref, bf16[128,640]{1,0:T(8,128)(2,1)S(1)} %get-tuple-element.75.refs_0_, bf16[128,640]{1,0:T(8,128)(2,1)S(1)} %collective-permute-done.9.refs_1_, bf16[4,640,128]{2,1,0:T(8,128)(2,1)S(1)} %pad_maximum_fusion.refs_2_, ...), custom_call_target="tpu_custom_call" | custom-call | flops 1 | bytes 1 | tf_op jit(solution)/shard_map/pallas_call | solution.py:20
  41.9 5.4 %collective-permute-done.11.refs_0_.refs_2_ = bf16[128,640]{1,0:T(8,128)(2,1)S(1)} collective-permute-done((bf16[128,640]{1,0:T(8,128)(2,1)S(1)}, bf16[128,640]{1,0:T(8,128)(2,1)S(1)}, u32[]{:S(2)}, u32[]{:S(2)}) %collective-permute-start.11) | collective-permute-done | bytes 163872 | tf_op jit(solution)/shard_map/ppermute | solution.py:375
  47.3 0.9 collective-permute-done.8.refs_6_
  48.3 0.1 pad_add_fusion.4.bins_ref
  48.4 1.5 %shard_map.59.refs_5_ = f32[256,640]{1,0:T(8,128)S(1)} custom-call(s32[8]{0:T(128)S(1)} %pad_add_fusion.6.bins_ref, s32[4,128]{1,0:T(4,128)S(1)} %slice.8.names_ref, bf16[128,640]{1,0:T(8,128)(2,1)S(1)} %collective-permute-done.11.refs_0_.refs_2_, bf16[128,640]{1,0:T(8,128)(2,1)S(1)} %collective-permute-done.12.refs_1_.refs_3_, ...), custom_call_target="tpu_custom_call" | custom-call | flops 1 | bytes 1 | tf_op jit(solution)/shard_map/pallas_call | solution.py:20
  49.9 0.5 collective-permute-done.13.refs_7_
  50.4 2.4 %shard_map.60 = (f32[512,640]{1,0:T(8,128)S(1)}, bf16[512,640]{1,0:T(8,128)(2,1)S(1)}, bf16[512,384]{1,0:T(8,128)(2,1)S(1)}, bf16[512,256]{1,0:T(8,128)(2,1)S(1)}, f32[4,128]{1,0:T(4,128)S(1)}) custom-call(s32[1]{0:T(128)} %bitcast.1.outer_ref, s32[8]{0:T(128)S(1)} %pad_add_fusion.4.bins_ref, s32[4,128]{1,0:T(4,128)S(1)} %slice.8.names_ref, ...), custom_call_target="tpu_custom_call" | custom-call | flops 1 | bytes 1 | tf_op jit(solution)/shard_map/pallas_call | solution.py:20
  52.8 2.1 %collective-permute-start.17 = (bf16[512,384]{1,0:T(8,128)(2,1)S(1)}, bf16[512,384]{1,0:T(8,128)(2,1)S(1)}, u32[]{:S(2)}, u32[]{:S(2)}) collective-permute-start(bf16[512,384]{1,0:T(8,128)(2,1)S(1)} %get-tuple-element.83), channel_id=1, source_target_pairs={{0,4},{1,5},{2,6},{3,7},{4,12},{5,13},{6,14},{7,15},{8,0},{9,1},{1... | collective-permute-start | bytes 1179656 | tf_op jit(solution)/shard_map/ppermute | solution.py:382
  54.9 0.1 collective-permute-start.14
  55.0 2.0 %collective-permute-start.15 = (f32[4,128]{1,0:T(4,128)S(1)}, f32[4,128]{1,0:T(4,128)S(1)}, u32[]{:S(2)}, u32[]{:S(2)}) collective-permute-start(f32[4,128]{1,0:T(4,128)S(1)} %get-tuple-element.82), channel_id=1, source_target_pairs={{0,8},{1,9},{2,10},{3,11},{4,12},{5,13},{6,14},{7,15},{8,0},{9,1},... | collective-permute-start | bytes 6152 | tf_op jit(solution)/shard_map/ppermute | solution.py:375
  57.0 2.3 %collective-permute-start.16 = (f32[4,128]{1,0:T(4,128)S(1)}, f32[4,128]{1,0:T(4,128)S(1)}, u32[]{:S(2)}, u32[]{:S(2)}) collective-permute-start(f32[4,128]{1,0:T(4,128)S(1)} %get-tuple-element.82), channel_id=1, source_target_pairs={{0,12},{1,13},{2,14},{3,15},{4,8},{5,9},{6,10},{7,11},{8,4},{9,5},... | collective-permute-start | bytes 6152 | tf_op jit(solution)/shard_map/ppermute | solution.py:375
  59.3 5.1 %collective-permute-done.14 = f32[4,128]{1,0:T(4,128)S(1)} collective-permute-done((f32[4,128]{1,0:T(4,128)S(1)}, f32[4,128]{1,0:T(4,128)S(1)}, u32[]{:S(2)}, u32[]{:S(2)}) %collective-permute-start.14) | collective-permute-done | bytes 2080 | tf_op jit(solution)/shard_map/ppermute | solution.py:375
  64.4 1.3 %collective-permute-done.15 = f32[4,128]{1,0:T(4,128)S(1)} collective-permute-done((f32[4,128]{1,0:T(4,128)S(1)}, f32[4,128]{1,0:T(4,128)S(1)}, u32[]{:S(2)}, u32[]{:S(2)}) %collective-permute-start.15) | collective-permute-done | bytes 2080 | tf_op jit(solution)/shard_map/ppermute | solution.py:375
  65.8 0.7 collective-permute-done.16
  66.5 0.2 shard_map.61.refs_0_.refs_2_
  66.7 0.8 shard_map.62
  67.5 3.2 %collective-permute-done.18.refs_1_ = bf16[512,256]{1,0:T(8,128)(2,1)S(1)} collective-permute-done((bf16[512,256]{1,0:T(8,128)(2,1)S(1)}, bf16[512,256]{1,0:T(8,128)(2,1)S(1)}, u32[]{:S(2)}, u32[]{:S(2)}) %collective-permute-start.18) | collective-permute-done | bytes 262176 | tf_op jit(solution)/shard_map/ppermute | solution.py:382
  70.7 0.9 shard_map.63
  71.5 0.1 collective-permute-start.22
  71.6 1.2 %collective-permute-start.19 = (bf16[512,640]{1,0:T(8,128)(2,1)S(1)}, bf16[512,640]{1,0:T(8,128)(2,1)S(1)}, u32[]{:S(2)}, u32[]{:S(2)}) collective-permute-start(bf16[512,640]{1,0:T(8,128)(2,1)S(1)} %get-tuple-element.97.refs_1_), channel_id=1, source_target_pairs={{0,4},{1,5},{2,6},{3,7},{4,12},{5,13},{6,14},{7,15},{8,0},{9,1},{1... | collective-permute-start | bytes 1966088 | tf_op jit(solution)/shard_map/ppermute | solution.py:382
  72.8 0.2 collective-permute-start.20
  73.0 0.4 collective-permute-done.22.got_ref
  73.4 0.1 shard_map.65
  73.5 0.8 shard_map.66
  74.3 0.2 collective-permute-start.23
  74.5 1.0 collective-permute-start.25
  75.5 0.1 shard_map.64
  75.6 1.1 %collective-permute-start.21 = (bf16[1,160,640]{2,1,0:T(8,128)(2,1)S(1)}, bf16[1,160,640]{2,1,0:T(8,128)(2,1)S(1)}, u32[]{:S(2)}, u32[]{:S(2)}) collective-permute-start(bf16[1,160,640]{2,1,0:T(8,128)(2,1)S(1)} %get-tuple-element.93), channel_id=1, source_target_pairs={{0,2},{1,3},{2,0},{3,1},{4,6},{5,7},{6,4},{7,5},{8,10},{9,11},{10,... | collective-permute-start | bytes 614408 | tf_op jit(solution)/shard_map/ppermute | solution.py:375
  76.7 1.1 %collective-permute-start.24 = (bf16[1,160,640]{2,1,0:T(8,128)(2,1)S(1)}, bf16[1,160,640]{2,1,0:T(8,128)(2,1)S(1)}, u32[]{:S(2)}, u32[]{:S(2)}) collective-permute-start(bf16[1,160,640]{2,1,0:T(8,128)(2,1)S(1)} %get-tuple-element.100), channel_id=1, source_target_pairs={{0,2},{1,3},{2,0},{3,1},{4,6},{5,7},{6,4},{7,5},{8,10},{9,11},{10,... | collective-permute-start | bytes 614408 | tf_op jit(solution)/shard_map/ppermute | solution.py:375
  77.8 4.6 %collective-permute-done.25 = bf16[1,160,640]{2,1,0:T(8,128)(2,1)S(1)} collective-permute-done((bf16[1,160,640]{2,1,0:T(8,128)(2,1)S(1)}, bf16[1,160,640]{2,1,0:T(8,128)(2,1)S(1)}, u32[]{:S(2)}, u32[]{:S(2)}) %collective-permute-start.25) | collective-permute-done | bytes 204832 | tf_op jit(solution)/shard_map/ppermute | solution.py:375
  82.4 4.4 %collective-permute-done.21 = bf16[1,160,640]{2,1,0:T(8,128)(2,1)S(1)} collective-permute-done((bf16[1,160,640]{2,1,0:T(8,128)(2,1)S(1)}, bf16[1,160,640]{2,1,0:T(8,128)(2,1)S(1)}, u32[]{:S(2)}, u32[]{:S(2)}) %collective-permute-start.21) | collective-permute-done | bytes 204832 | tf_op jit(solution)/shard_map/ppermute | solution.py:375
  86.8 2.9 %collective-permute-done.19.refs_1_ = bf16[512,640]{1,0:T(8,128)(2,1)S(1)} collective-permute-done((bf16[512,640]{1,0:T(8,128)(2,1)S(1)}, bf16[512,640]{1,0:T(8,128)(2,1)S(1)}, u32[]{:S(2)}, u32[]{:S(2)}) %collective-permute-start.19) | collective-permute-done | bytes 655392 | tf_op jit(solution)/shard_map/ppermute | solution.py:382
  89.7 0.9 collective-permute-done.24
  90.6 0.8 shard_map.68
  91.6 1.5 %collective-permute-start.28 = (bf16[160,640]{1,0:T(8,128)(2,1)S(1)}, bf16[160,640]{1,0:T(8,128)(2,1)S(1)}, u32[]{:S(2)}, u32[]{:S(2)}) collective-permute-start(bf16[160,640]{1,0:T(8,128)(2,1)S(1)} %fusion), channel_id=1, source_target_pairs={{0,8},{1,9},{2,10},{3,11},{4,0},{5,1},{6,2},{7,3},{8,12},{9,13},{1... | collective-permute-start | bytes 614408 | tf_op jit(solution)/shard_map/ppermute | solution.py:382
  93.0 0.2 collective-permute-done.26.got_ref
  93.3 0.9 collective-permute-start.27
  94.2 1.5 %shard_map.70.refs_4_ = f32[160,2560]{1,0:T(8,128)} custom-call(s32[4]{0:T(128)S(1)} %shift-right-arithmetic_xor_fusion.at_ref, f32[160,640]{1,0:T(8,128)S(1)} %bitcast.38, bf16[160,640]{1,0:T(8,128)(2,1)S(1)} %bitcast.41, f32[160,640]{1,0:T(8,128)S(1)} %bitcast.39, bf16[160,640]{1,0:T(8,128)(2,1)S(1)} %bitcast.42), custom_call_target="tpu_custom_call" | custom-call | flops 1 | bytes 1 | tf_op jit(solution)/shard_map/pallas_call | solution.py:349
  95.7 3.4 %collective-permute-done.28.refs_2_ = bf16[160,640]{1,0:T(8,128)(2,1)S(1)} collective-permute-done((bf16[160,640]{1,0:T(8,128)(2,1)S(1)}, bf16[160,640]{1,0:T(8,128)(2,1)S(1)}, u32[]{:S(2)}, u32[]{:S(2)}) %collective-permute-start.28) | collective-permute-done | bytes 204832 | tf_op jit(solution)/shard_map/ppermute | solution.py:382
  99.1 1.4 %collective-permute-done.27 = bf16[1,160,640]{2,1,0:T(8,128)(2,1)S(1)} collective-permute-done((bf16[1,160,640]{2,1,0:T(8,128)(2,1)S(1)}, bf16[1,160,640]{2,1,0:T(8,128)(2,1)S(1)}, u32[]{:S(2)}, u32[]{:S(2)}) %collective-permute-start.27) | collective-permute-done | bytes 204832 | tf_op jit(solution)/shard_map/ppermute | solution.py:375
  100.5 1.5 %shard_map.71 = f32[160,2560]{1,0:T(8,128)} custom-call(s32[4]{0:T(128)S(1)} %shift-right-arithmetic_xor_fusion.at_ref, f32[160,640]{1,0:T(8,128)S(1)} %bitcast.40, bf16[160,640]{1,0:T(8,128)(2,1)S(1)} %bitcast.43, bf16[160,640]{1,0:T(8,128)(2,1)S(1)} %collective-permute-done.28.refs_2_, ...), custom_call_target="tpu_custom_call", output_to_operand_aliasing={{}: (5, {})} | custom-call | flops 1 | bytes 1 | tf_op jit(solution)/shard_map/pallas_call | solution.py:349
  (35 shorter events, 0.5 us)
Async XLA Ops:
  0.0 18.9 %copy-start = (bf16[128,3968]{1,0:T(8,128)(2,1)S(1)}, bf16[128,3968]{1,0:T(8,128)(2,1)}, u32[]{:S(2)}) copy-start(bf16[128,3968]{1,0:T(8,128)(2,1)} %flux_ref) | copy-start | bytes 3047428
  0.8 6.8 %collective-permute-start = (s32[148]{0:T(256)S(1)}, s32[148]{0:T(256)S(1)}, u32[]{:S(2)}, u32[]{:S(2)}) collective-permute-start(s32[148]{0:T(256)S(1)} %pad_add_fusion.3), channel_id=1, source_target_pairs={{0,4},{1,5},{2,6},{3,7},{4,0},{5,1},{6,2},{7,3},{8,12},{9,13},{10,... | collective-permute-start | bytes 1784 | tf_op jit(solution)/shard_map/ppermute | solution.py:375
  3.9 4.5 %collective-permute-start.1 = (s32[148]{0:T(256)S(1)}, s32[148]{0:T(256)S(1)}, u32[]{:S(2)}, u32[]{:S(2)}) collective-permute-start(s32[148]{0:T(256)S(1)} %pad_add_fusion.3), channel_id=1, source_target_pairs={{0,8},{1,9},{2,10},{3,11},{4,12},{5,13},{6,14},{7,15},{8,0},{9,1},... | collective-permute-start | bytes 1784 | tf_op jit(solution)/shard_map/ppermute | solution.py:375
  6.4 5.4 %collective-permute-start.2 = (s32[148]{0:T(256)S(1)}, s32[148]{0:T(256)S(1)}, u32[]{:S(2)}, u32[]{:S(2)}) collective-permute-start(s32[148]{0:T(256)S(1)} %pad_add_fusion.3), channel_id=1, source_target_pairs={{0,12},{1,13},{2,14},{3,15},{4,8},{5,9},{6,10},{7,11},{8,4},{9,5},... | collective-permute-start | bytes 1784 | tf_op jit(solution)/shard_map/ppermute | solution.py:375
  11.8 4.5 %collective-permute-start.6 = (s32[4,1,20]{2,0,1:T(4,128)S(1)}, s32[4,1,20]{2,0,1:T(4,128)S(1)}, u32[]{:S(2)}, u32[]{:S(2)}) collective-permute-start(s32[4,1,20]{2,0,1:T(4,128)S(1)} %slice_bitcast_fusion), channel_id=1, source_target_pairs={{0,1},{1,0},{2,3},{3,2},{4,5},{5,4},{6,7},{7,6},{8,9},{9,8},{10,11... | collective-permute-start | bytes 968 | tf_op jit(solution)/shard_map/ppermute | solution.py:375
  11.9 19.0 %collective-permute-start.3 = (bf16[640,128]{1,0:T(8,128)(2,1)S(1)}, bf16[640,128]{1,0:T(8,128)(2,1)S(1)}, u32[]{:S(2)}, u32[]{:S(2)}) collective-permute-start(bf16[640,128]{1,0:T(8,128)(2,1)S(1)} %get-tuple-element.115), channel_id=1, source_target_pairs={{0,4},{1,5},{2,6},{3,7},{4,0},{5,1},{6,2},{7,3},{8,12},{9,13},{10,... | collective-permute-start | bytes 491528 | tf_op jit(solution)/shard_map/ppermute | solution.py:375
  12.0 18.9 %collective-permute-start.4 = (bf16[640,128]{1,0:T(8,128)(2,1)S(1)}, bf16[640,128]{1,0:T(8,128)(2,1)S(1)}, u32[]{:S(2)}, u32[]{:S(2)}) collective-permute-start(bf16[640,128]{1,0:T(8,128)(2,1)S(1)} %get-tuple-element.114), channel_id=1, source_target_pairs={{0,8},{1,9},{2,10},{3,11},{4,12},{5,13},{6,14},{7,15},{8,0},{9,1},... | collective-permute-start | bytes 491528 | tf_op jit(solution)/shard_map/ppermute | solution.py:375
  12.6 18.4 %collective-permute-start.5 = (bf16[640,128]{1,0:T(8,128)(2,1)S(1)}, bf16[640,128]{1,0:T(8,128)(2,1)S(1)}, u32[]{:S(2)}, u32[]{:S(2)}) collective-permute-start(bf16[640,128]{1,0:T(8,128)(2,1)S(1)} %get-tuple-element.113), channel_id=1, source_target_pairs={{0,12},{1,13},{2,14},{3,15},{4,8},{5,9},{6,10},{7,11},{8,4},{9,5},... | collective-permute-start | bytes 491528 | tf_op jit(solution)/shard_map/ppermute | solution.py:375
  16.4 9.8 %collective-permute-start.7 = (s32[4,2,20]{2,0,1:T(4,128)S(1)}, s32[4,2,20]{2,0,1:T(4,128)S(1)}, u32[]{:S(2)}, u32[]{:S(2)}) collective-permute-start(s32[4,2,20]{2,0,1:T(4,128)S(1)} %pad_add_fusion.2), channel_id=1, source_target_pairs={{0,2},{1,3},{2,0},{3,1},{4,6},{5,7},{6,4},{7,5},{8,10},{9,11},{10,... | collective-permute-start | bytes 1928 | tf_op jit(solution)/shard_map/ppermute | solution.py:375
  18.0 0.7 copy-start.1
  31.0 9.3 %collective-permute-start.10 = (bf16[4,640,128]{2,1,0:T(8,128)(2,1)S(1)}, bf16[4,640,128]{2,1,0:T(8,128)(2,1)S(1)}, u32[]{:S(2)}, u32[]{:S(2)}) collective-permute-start(bf16[4,640,128]{2,1,0:T(8,128)(2,1)S(1)} %pad_maximum_fusion.refs_2_), channel_id=1, source_target_pairs={{0,1},{1,0},{2,3},{3,2},{4,5},{5,4},{6,7},{7,6},{8,9},{9,8},{10,11... | collective-permute-start | bytes 1966088 | tf_op jit(solution)/shard_map/ppermute | solution.py:375
  31.1 17.1 %collective-permute-start.8 = (bf16[4,640,128]{2,1,0:T(8,128)(2,1)S(1)}, bf16[4,640,128]{2,1,0:T(8,128)(2,1)S(1)}, u32[]{:S(2)}, u32[]{:S(2)}) collective-permute-start(bf16[4,640,128]{2,1,0:T(8,128)(2,1)S(1)} %pad_maximum_fusion.refs_2_), channel_id=1, source_target_pairs={{0,2},{1,3},{2,0},{3,1},{4,6},{5,7},{6,4},{7,5},{8,10},{9,11},{10,... | collective-permute-start | bytes 1966088 | tf_op jit(solution)/shard_map/ppermute | solution.py:375
  31.7 8.7 %collective-permute-start.9 = (bf16[128,640]{1,0:T(8,128)(2,1)S(1)}, bf16[128,640]{1,0:T(8,128)(2,1)S(1)}, u32[]{:S(2)}, u32[]{:S(2)}) collective-permute-start(bf16[128,640]{1,0:T(8,128)(2,1)S(1)} %get-tuple-element.72), channel_id=1, source_target_pairs={{0,4},{1,5},{2,6},{3,7},{4,0},{5,1},{6,2},{7,3},{8,12},{9,13},{10,... | collective-permute-start | bytes 491528 | tf_op jit(solution)/shard_map/ppermute | solution.py:375
  32.3 15.0 %collective-permute-start.11 = (bf16[128,640]{1,0:T(8,128)(2,1)S(1)}, bf16[128,640]{1,0:T(8,128)(2,1)S(1)}, u32[]{:S(2)}, u32[]{:S(2)}) collective-permute-start(bf16[128,640]{1,0:T(8,128)(2,1)S(1)} %get-tuple-element.73), channel_id=1, source_target_pairs={{0,8},{1,9},{2,10},{3,11},{4,12},{5,13},{6,14},{7,15},{8,0},{9,1},... | collective-permute-start | bytes 491528 | tf_op jit(solution)/shard_map/ppermute | solution.py:375
  32.5 14.8 %collective-permute-start.12 = (bf16[128,640]{1,0:T(8,128)(2,1)S(1)}, bf16[128,640]{1,0:T(8,128)(2,1)S(1)}, u32[]{:S(2)}, u32[]{:S(2)}) collective-permute-start(bf16[128,640]{1,0:T(8,128)(2,1)S(1)} %get-tuple-element.74), channel_id=1, source_target_pairs={{0,12},{1,13},{2,14},{3,15},{4,8},{5,9},{6,10},{7,11},{8,4},{9,5},... | collective-permute-start | bytes 491528 | tf_op jit(solution)/shard_map/ppermute | solution.py:375
  48.3 2.1 %collective-permute-start.13 = (bf16[4,640,128]{2,1,0:T(8,128)(2,1)S(1)}, bf16[4,640,128]{2,1,0:T(8,128)(2,1)S(1)}, u32[]{:S(2)}, u32[]{:S(2)}) collective-permute-start(bf16[4,640,128]{2,1,0:T(8,128)(2,1)S(1)} %collective-permute-done.8.refs_6_), channel_id=1, source_target_pairs={{0,1},{1,0},{2,3},{3,2},{4,5},{5,4},{6,7},{7,6},{8,9},{9,8},{10,11... | collective-permute-start | bytes 1966088 | tf_op jit(solution)/shard_map/ppermute | solution.py:375
  52.8 13.7 %collective-permute-start.17 = (bf16[512,384]{1,0:T(8,128)(2,1)S(1)}, bf16[512,384]{1,0:T(8,128)(2,1)S(1)}, u32[]{:S(2)}, u32[]{:S(2)}) collective-permute-start(bf16[512,384]{1,0:T(8,128)(2,1)S(1)} %get-tuple-element.83), channel_id=1, source_target_pairs={{0,4},{1,5},{2,6},{3,7},{4,12},{5,13},{6,14},{7,15},{8,0},{9,1},{1... | collective-permute-start | bytes 1179656 | tf_op jit(solution)/shard_map/ppermute | solution.py:382
  54.9 9.5 %collective-permute-start.14 = (f32[4,128]{1,0:T(4,128)S(1)}, f32[4,128]{1,0:T(4,128)S(1)}, u32[]{:S(2)}, u32[]{:S(2)}) collective-permute-start(f32[4,128]{1,0:T(4,128)S(1)} %get-tuple-element.82), channel_id=1, source_target_pairs={{0,4},{1,5},{2,6},{3,7},{4,0},{5,1},{6,2},{7,3},{8,12},{9,13},{10,... | collective-permute-start | bytes 6152 | tf_op jit(solution)/shard_map/ppermute | solution.py:375
  55.0 10.8 %collective-permute-start.15 = (f32[4,128]{1,0:T(4,128)S(1)}, f32[4,128]{1,0:T(4,128)S(1)}, u32[]{:S(2)}, u32[]{:S(2)}) collective-permute-start(f32[4,128]{1,0:T(4,128)S(1)} %get-tuple-element.82), channel_id=1, source_target_pairs={{0,8},{1,9},{2,10},{3,11},{4,12},{5,13},{6,14},{7,15},{8,0},{9,1},... | collective-permute-start | bytes 6152 | tf_op jit(solution)/shard_map/ppermute | solution.py:375
  57.0 9.5 %collective-permute-start.16 = (f32[4,128]{1,0:T(4,128)S(1)}, f32[4,128]{1,0:T(4,128)S(1)}, u32[]{:S(2)}, u32[]{:S(2)}) collective-permute-start(f32[4,128]{1,0:T(4,128)S(1)} %get-tuple-element.82), channel_id=1, source_target_pairs={{0,12},{1,13},{2,14},{3,15},{4,8},{5,9},{6,10},{7,11},{8,4},{9,5},... | collective-permute-start | bytes 6152 | tf_op jit(solution)/shard_map/ppermute | solution.py:375
  59.3 11.4 %collective-permute-start.18 = (bf16[512,256]{1,0:T(8,128)(2,1)S(1)}, bf16[512,256]{1,0:T(8,128)(2,1)S(1)}, u32[]{:S(2)}, u32[]{:S(2)}) collective-permute-start(bf16[512,256]{1,0:T(8,128)(2,1)S(1)} %get-tuple-element.86), channel_id=1, source_target_pairs={{0,4},{1,5},{2,6},{3,7},{4,12},{5,13},{6,14},{7,15},{8,0},{9,1},{1... | collective-permute-start | bytes 786440 | tf_op jit(solution)/shard_map/ppermute | solution.py:382
  71.5 1.8 %collective-permute-start.22 = (bf16[2,160,640]{2,1,0:T(8,128)(2,1)S(1)}, bf16[2,160,640]{2,1,0:T(8,128)(2,1)S(1)}, u32[]{:S(2)}, u32[]{:S(2)}) collective-permute-start(bf16[2,160,640]{2,1,0:T(8,128)(2,1)S(1)} %get-tuple-element.95), channel_id=1, source_target_pairs={{0,1},{1,0},{2,3},{3,2},{4,5},{5,4},{6,7},{7,6},{8,9},{9,8},{10,11... | collective-permute-start | bytes 1228808 | tf_op jit(solution)/shard_map/ppermute | solution.py:375
  71.6 18.0 %collective-permute-start.19 = (bf16[512,640]{1,0:T(8,128)(2,1)S(1)}, bf16[512,640]{1,0:T(8,128)(2,1)S(1)}, u32[]{:S(2)}, u32[]{:S(2)}) collective-permute-start(bf16[512,640]{1,0:T(8,128)(2,1)S(1)} %get-tuple-element.97.refs_1_), channel_id=1, source_target_pairs={{0,4},{1,5},{2,6},{3,7},{4,12},{5,13},{6,14},{7,15},{8,0},{9,1},{1... | collective-permute-start | bytes 1966088 | tf_op jit(solution)/shard_map/ppermute | solution.py:382
  72.8 2.7 %collective-permute-start.20 = (bf16[2,160,640]{2,1,0:T(8,128)(2,1)S(1)}, bf16[2,160,640]{2,1,0:T(8,128)(2,1)S(1)}, u32[]{:S(2)}, u32[]{:S(2)}) collective-permute-start(bf16[2,160,640]{2,1,0:T(8,128)(2,1)S(1)} %get-tuple-element.92), channel_id=1, source_target_pairs={{0,1},{1,0},{2,3},{3,2},{4,5},{5,4},{6,7},{7,6},{8,9},{9,8},{10,11... | collective-permute-start | bytes 1228808 | tf_op jit(solution)/shard_map/ppermute | solution.py:375
  74.3 2.4 %collective-permute-start.23 = (bf16[2,160,640]{2,1,0:T(8,128)(2,1)S(1)}, bf16[2,160,640]{2,1,0:T(8,128)(2,1)S(1)}, u32[]{:S(2)}, u32[]{:S(2)}) collective-permute-start(bf16[2,160,640]{2,1,0:T(8,128)(2,1)S(1)} %get-tuple-element.99), channel_id=1, source_target_pairs={{0,1},{1,0},{2,3},{3,2},{4,5},{5,4},{6,7},{7,6},{8,9},{9,8},{10,11... | collective-permute-start | bytes 1228808 | tf_op jit(solution)/shard_map/ppermute | solution.py:375
  74.5 7.9 %collective-permute-start.25 = (bf16[1,160,640]{2,1,0:T(8,128)(2,1)S(1)}, bf16[1,160,640]{2,1,0:T(8,128)(2,1)S(1)}, u32[]{:S(2)}, u32[]{:S(2)}) collective-permute-start(bf16[1,160,640]{2,1,0:T(8,128)(2,1)S(1)} %get-tuple-element.101), channel_id=1, source_target_pairs={{0,2},{1,3},{2,0},{3,1},{4,6},{5,7},{6,4},{7,5},{8,10},{9,11},{10,... | collective-permute-start | bytes 614408 | tf_op jit(solution)/shard_map/ppermute | solution.py:375
  75.6 11.2 %collective-permute-start.21 = (bf16[1,160,640]{2,1,0:T(8,128)(2,1)S(1)}, bf16[1,160,640]{2,1,0:T(8,128)(2,1)S(1)}, u32[]{:S(2)}, u32[]{:S(2)}) collective-permute-start(bf16[1,160,640]{2,1,0:T(8,128)(2,1)S(1)} %get-tuple-element.93), channel_id=1, source_target_pairs={{0,2},{1,3},{2,0},{3,1},{4,6},{5,7},{6,4},{7,5},{8,10},{9,11},{10,... | collective-permute-start | bytes 614408 | tf_op jit(solution)/shard_map/ppermute | solution.py:375
  76.7 13.9 %collective-permute-start.24 = (bf16[1,160,640]{2,1,0:T(8,128)(2,1)S(1)}, bf16[1,160,640]{2,1,0:T(8,128)(2,1)S(1)}, u32[]{:S(2)}, u32[]{:S(2)}) collective-permute-start(bf16[1,160,640]{2,1,0:T(8,128)(2,1)S(1)} %get-tuple-element.100), channel_id=1, source_target_pairs={{0,2},{1,3},{2,0},{3,1},{4,6},{5,7},{6,4},{7,5},{8,10},{9,11},{10,... | collective-permute-start | bytes 614408 | tf_op jit(solution)/shard_map/ppermute | solution.py:375
  91.4 1.8 %collective-permute-start.26 = (bf16[2,160,640]{2,1,0:T(8,128)(2,1)S(1)}, bf16[2,160,640]{2,1,0:T(8,128)(2,1)S(1)}, u32[]{:S(2)}, u32[]{:S(2)}) collective-permute-start(bf16[2,160,640]{2,1,0:T(8,128)(2,1)S(1)} %get-tuple-element.104), channel_id=1, source_target_pairs={{0,1},{1,0},{2,3},{3,2},{4,5},{5,4},{6,7},{7,6},{8,9},{9,8},{10,11... | collective-permute-start | bytes 1228808 | tf_op jit(solution)/shard_map/ppermute | solution.py:375
  91.6 7.5 %collective-permute-start.28 = (bf16[160,640]{1,0:T(8,128)(2,1)S(1)}, bf16[160,640]{1,0:T(8,128)(2,1)S(1)}, u32[]{:S(2)}, u32[]{:S(2)}) collective-permute-start(bf16[160,640]{1,0:T(8,128)(2,1)S(1)} %fusion), channel_id=1, source_target_pairs={{0,8},{1,9},{2,10},{3,11},{4,0},{5,1},{6,2},{7,3},{8,12},{9,13},{1... | collective-permute-start | bytes 614408 | tf_op jit(solution)/shard_map/ppermute | solution.py:382
  93.3 7.2 %collective-permute-start.27 = (bf16[1,160,640]{2,1,0:T(8,128)(2,1)S(1)}, bf16[1,160,640]{2,1,0:T(8,128)(2,1)S(1)}, u32[]{:S(2)}, u32[]{:S(2)}) collective-permute-start(bf16[1,160,640]{2,1,0:T(8,128)(2,1)S(1)} %get-tuple-element.106), channel_id=1, source_target_pairs={{0,2},{1,3},{2,0},{3,1},{4,6},{5,7},{6,4},{7,5},{8,10},{9,11},{10,... | collective-permute-start | bytes 614408 | tf_op jit(solution)/shard_map/ppermute | solution.py:375

commit v14 on v13

--- a/solution.py
+++ b/solution.py
@@ -159,11 +159,11 @@
     lax.fori_loop(0, done, some_groups, 0)
     lax.fori_loop(done, steps, clear_groups, 0)
     width = per * band
+    back = lax.dot_general(
+        placing_ref[...], cut[...].astype(BF16), (((0,), (0,)), ((), ())), preferred_element_type=F32
+    ).astype(BF16)
     for away in range(OUTER):
-        part = cut[:, away * width : (away + 1) * width].astype(BF16)
-        outs[away][...] = lax.dot_general(
-            placing_ref[...], part, (((0,), (0,)), ((), ())), preferred_element_type=F32
-        ).astype(BF16)
+        outs[away][...] = back[:, away * width : (away + 1) * width]
 
 
 def cut_windows(me, groups, starts, turns, smoothed, placing, band):
@@ -411,8 +411,7 @@
     outer1 = outer.reshape(1)
     windows = cut_windows(jnp.stack([me, outer]), group_bins, chunk * band, turns, smoothed, placing, band)
 
-    pieces, windows = lax.optimization_barrier((pieces, windows))
-    arrived = [windows[0]] + [swap(windows[away], away * inner) for away in range(1, OUTER)]
+    pieces, *windows = lax.optimization_barrier((pieces, *windows))
     mixed = jnp.stack(pieces)
     bit = inner // 2
     weights = [mixed, swap(mixed, bit)]
@@ -422,6 +421,8 @@
         bit //= 2
         bits.append(bit)
         near = near + [swap(piece, bit) for piece in near]
+    windows[1], near[-1] = lax.optimization_barrier((windows[1], near[-1]))
+    arrived = [windows[0]] + [swap(windows[away], away * inner) for away in range(1, OUTER)]
     near_bins = [mine]
     for bit in bits:
         near_bins = near_bins + [piece ^ bit for piece in near_bins]
@@ -472,7 +473,8 @@
     got2 = finish(send2)
     at = fold_at((fold_at(outer) - jnp.arange(OUTER, dtype=I32)) % OUTER)
     begun = place(at, [0, 1], [(held0, got0), (held1, got1)])
-    return place(at, [2, 3], [(held2, got2), (back, jnp.zeros_like(back))], begun)
+    begun = place(at, [3], [(back, jnp.zeros_like(back))], begun)
+    return place(at, [2], [(held2, got2)], begun)
 
 
 def solution(mesh):

time: 102 us -> 103 us (level)
  starting transfers between devices: 30.4 us -> 27.2 us
  waiting for transfers between devices: 43.7 us -> 46.1 us
  Pallas kernels: 24.4 us -> 25.6 us
    ppermute x4, starting transfers between devices: 4.8 us -> 2.86 us  [step(): lax.ppermute(array, 'spec', [(o * inner + i, to[o] * inner + i) for o in...]
    ppermute x25, waiting for transfers between devices: 34.2 us -> 35.8 us  [swap(): return lax.ppermute(array, 'spec', [(i, i ^ bit) for i in range(n)])]
    ppermute x25, starting transfers between devices: 25.6 us -> 24.3 us  [swap(): return lax.ppermute(array, 'spec', [(i, i ^ bit) for i in range(n)])]
    pallas_call x2 -> x3, Pallas kernels: 2.98 us -> 4.18 us  [place(): pl.pallas_call(functools.partial(place_kernel, slots, last), out_shape=ja...]
  transfers between devices with their start and end apart: 29 -> 29, of which waited for: 18 -> 15; matrix products, arithmetic and copies ran while one was open for 2% -> 2% of each run, Pallas kernels for 18% -> 20%
where the time goes in v14:
time: 103 us; the launch traced here: 102 us
  waiting for transfers between devices  46.1 us (45%)
  starting transfers between devices  27.2 us (26%)
  Pallas kernels  25.6 us (25%)
  local copies, waits for them, and re-layouts  1.95 us (2%)
  other arithmetic  1.27 us (1%)
    ppermute x25, waiting for transfers between devices, swap(): return lax.ppermute(array, 'spec', [(i, i ^ bit) for i in range(n)])  35.8 us
    ppermute x25, starting transfers between devices, swap(): return lax.ppermute(array, 'spec', [(i, i ^ bit) for i in range(n)])  24.3 us
    pallas_call x15, Pallas kernels, call(): pl.pallas_call(kernel, out_shape=out_shape, in_specs=in_specs, out_specs=...  21.4 us
    ppermute x4, waiting for transfers between devices, step(): lax.ppermute(array, 'spec', [(o * inner + i, to[o] * inner + i) for o in...  10.3 us
    pallas_call x3, Pallas kernels, place(): pl.pallas_call(functools.partial(place_kernel, slots, last), out_shape=ja...  4.18 us
    ppermute x4, starting transfers between devices, step(): lax.ppermute(array, 'spec', [(o * inner + i, to[o] * inner + i) for o in...  2.86 us
  transfers between devices with their start and end apart: 29, of which 15 were waited for; matrix products, arithmetic and copies ran while one was open for 2% of the time, Pallas kernels for 20%

profile of v14, /device:TPU:0, one launch (start us, length us, event | category | flops | bytes accessed | tf_op | source)
XLA Modules:
  0.0 102.5 jit_solution(18422603326845522167)
XLA Ops:
  0.0 0.8 pad_add_fusion.3
  0.8 3.0 %collective-permute-start = (s32[148]{0:T(256)S(1)}, s32[148]{0:T(256)S(1)}, u32[]{:S(2)}, u32[]{:S(2)}) collective-permute-start(s32[148]{0:T(256)S(1)} %pad_add_fusion.3), channel_id=1, source_target_pairs={{0,4},{1,5},{2,6},{3,7},{4,0},{5,1},{6,2},{7,3},{8,12},{9,13},{10,... | collective-permute-start | bytes 1784 | tf_op jit(solution)/shard_map/ppermute | solution.py:375
  3.9 2.6 %collective-permute-start.1 = (s32[148]{0:T(256)S(1)}, s32[148]{0:T(256)S(1)}, u32[]{:S(2)}, u32[]{:S(2)}) collective-permute-start(s32[148]{0:T(256)S(1)} %pad_add_fusion.3), channel_id=1, source_target_pairs={{0,8},{1,9},{2,10},{3,11},{4,12},{5,13},{6,14},{7,15},{8,0},{9,1},... | collective-permute-start | bytes 1784 | tf_op jit(solution)/shard_map/ppermute | solution.py:375
  6.5 1.2 %dynamic-slice_bitcast_fusion = (bf16[640,128]{1,0:T(8,128)(2,1)S(1)}, bf16[640,128]{1,0:T(8,128)(2,1)S(1)}, bf16[640,128]{1,0:T(8,128)(2,1)S(1)}, bf16[640,128]{1,0:T(8,128)(2,1)S(1)}) fusion(bf16[4,640,128]{2,1,0:T(8,128)(2,1)} %bitcast.48, s32[]{:T(128)S(6)} %select_n.41, s32[]{:T(128)S(6)} %select_n.40, s32[]{:T(128)S(6)} %select_n.39, s32[]{:T(128)S(6)} %select_n.38), kind=kLoop, calls=%fused_computation.3 | loop fusion | bytes 1310736 | tf_op jit(solution)/shard_map/jit(dynamic_index_in_dim)/squeeze | solution.py:401
  7.7 0.7 collective-permute-done.1
  8.3 3.5 %collective-permute-done.2 = s32[148]{0:T(256)S(1)} collective-permute-done((s32[148]{0:T(256)S(1)}, s32[148]{0:T(256)S(1)}, u32[]{:S(2)}, u32[]{:S(2)}) %collective-permute-start.2) | collective-permute-done | bytes 624 | tf_op jit(solution)/shard_map/ppermute | solution.py:375
  11.8 0.1 collective-permute-start.6
  11.9 0.1 collective-permute-start.3
  12.0 0.6 collective-permute-start.4
  12.6 3.8 %collective-permute-start.5 = (bf16[640,128]{1,0:T(8,128)(2,1)S(1)}, bf16[640,128]{1,0:T(8,128)(2,1)S(1)}, u32[]{:S(2)}, u32[]{:S(2)}) collective-permute-start(bf16[640,128]{1,0:T(8,128)(2,1)S(1)} %get-tuple-element.117), channel_id=1, source_target_pairs={{0,12},{1,13},{2,14},{3,15},{4,8},{5,9},{6,10},{7,11},{8,4},{9,5},... | collective-permute-start | bytes 491528 | tf_op jit(solution)/shard_map/ppermute | solution.py:375
  16.4 1.5 %collective-permute-start.7 = (s32[4,2,20]{2,0,1:T(4,128)S(1)}, s32[4,2,20]{2,0,1:T(4,128)S(1)}, u32[]{:S(2)}, u32[]{:S(2)}) collective-permute-start(s32[4,2,20]{2,0,1:T(4,128)S(1)} %pad_add_fusion.2), channel_id=1, source_target_pairs={{0,2},{1,3},{2,0},{3,1},{4,6},{5,7},{6,4},{7,5},{8,10},{9,11},{10,... | collective-permute-start | bytes 1928 | tf_op jit(solution)/shard_map/ppermute | solution.py:375
  17.9 0.1 pad_add_fusion.5.me_ref
  18.0 0.7 copy-done.1
  18.6 0.2 shard_map.55
  18.9 7.2 %shard_map.56.smoothed_ref = bf16[128,3968]{1,0:T(8,128)(2,1)S(1)} custom-call(bf16[128,3968]{1,0:T(8,128)(2,1)S(1)} %copy-done, bf16[11,128,3968]{2,1,0:T(8,128)(2,1)} %bitcast.46), custom_call_target="tpu_custom_call" | custom-call | flops 1 | bytes 1 | tf_op jit(solution)/shard_map/pallas_call | solution.py:20
  26.2 4.7 %shard_map.57 = (bf16[128,640]{1,0:T(8,128)(2,1)S(1)}, bf16[128,640]{1,0:T(8,128)(2,1)S(1)}, bf16[128,640]{1,0:T(8,128)(2,1)S(1)}, bf16[128,640]{1,0:T(8,128)(2,1)S(1)}) custom-call(s32[2]{0:T(128)S(1)} %pad_add_fusion.5.me_ref, s32[2,128]{1,0:T(2,128)S(1)} %get-tuple-element.61.groups_ref, s32[16,20]{1,0:T(8,128)S(1)} %get-tuple-element.122.starts_ref, ...), custom_call_target="tpu_custom_call" | custom-call | flops 1 | bytes 1 | tf_op jit(solution)/shard_map/pallas_call | solution.py:20
  30.9 0.1 pad_maximum_fusion.refs_2_
  31.0 0.1 collective-permute-start.9
  31.1 0.6 collective-permute-start.8
  31.7 0.7 collective-permute-start.11
  32.3 2.3 %collective-permute-start.12 = (bf16[128,640]{1,0:T(8,128)(2,1)S(1)}, bf16[128,640]{1,0:T(8,128)(2,1)S(1)}, u32[]{:S(2)}, u32[]{:S(2)}) collective-permute-start(bf16[128,640]{1,0:T(8,128)(2,1)S(1)} %get-tuple-element.78), channel_id=1, source_target_pairs={{0,12},{1,13},{2,14},{3,15},{4,8},{5,9},{6,10},{7,11},{8,4},{9,5},... | collective-permute-start | bytes 491528 | tf_op jit(solution)/shard_map/ppermute | solution.py:375
  34.7 0.5 collective-permute-start.10
  35.2 0.1 pad_add_fusion.6.bins_ref
  35.2 0.1 slice.8.names_ref
  35.3 11.9 %collective-permute-done.10.refs_1_ = bf16[128,640]{1,0:T(8,128)(2,1)S(1)} collective-permute-done((bf16[128,640]{1,0:T(8,128)(2,1)S(1)}, bf16[128,640]{1,0:T(8,128)(2,1)S(1)}, u32[]{:S(2)}, u32[]{:S(2)}) %collective-permute-start.10) | collective-permute-done | bytes 163872 | tf_op jit(solution)/shard_map/ppermute | solution.py:375
  47.2 1.5 %shard_map.58.refs_4_ = f32[256,640]{1,0:T(8,128)S(1)} custom-call(s32[8]{0:T(128)S(1)} %pad_add_fusion.6.bins_ref, s32[4,128]{1,0:T(4,128)S(1)} %slice.8.names_ref, bf16[128,640]{1,0:T(8,128)(2,1)S(1)} %get-tuple-element.79.refs_0_, bf16[128,640]{1,0:T(8,128)(2,1)S(1)} %collective-permute-done.10.refs_1_, bf16[4,640,128]{2,1,0:T(8,128)(2,1)S(1)} %pad_maximum_fusion.refs_2_, ...), custom_call_target="tpu_custom_call" | custom-call | flops 1 | bytes 1 | tf_op jit(solution)/shard_map/pallas_call | solution.py:20
  48.8 0.1 collective-permute-start.13
  48.9 0.1 pad_add_fusion.4.bins_ref
  49.0 1.5 %shard_map.59.refs_5_ = f32[256,640]{1,0:T(8,128)S(1)} custom-call(s32[8]{0:T(128)S(1)} %pad_add_fusion.6.bins_ref, s32[4,128]{1,0:T(4,128)S(1)} %slice.8.names_ref, bf16[128,640]{1,0:T(8,128)(2,1)S(1)} %collective-permute-done.11.refs_0_.refs_2_, bf16[128,640]{1,0:T(8,128)(2,1)S(1)} %collective-permute-done.12.refs_1_.refs_3_, ...), custom_call_target="tpu_custom_call" | custom-call | flops 1 | bytes 1 | tf_op jit(solution)/shard_map/pallas_call | solution.py:20
  50.5 0.5 collective-permute-done.13.refs_7_
  51.0 2.4 %shard_map.60 = (f32[512,640]{1,0:T(8,128)S(1)}, bf16[512,640]{1,0:T(8,128)(2,1)S(1)}, bf16[512,384]{1,0:T(8,128)(2,1)S(1)}, bf16[512,256]{1,0:T(8,128)(2,1)S(1)}, f32[4,128]{1,0:T(4,128)S(1)}) custom-call(s32[1]{0:T(128)} %bitcast.1.outer_ref, s32[8]{0:T(128)S(1)} %pad_add_fusion.4.bins_ref, s32[4,128]{1,0:T(4,128)S(1)} %slice.8.names_ref, ...), custom_call_target="tpu_custom_call" | custom-call | flops 1 | bytes 1 | tf_op jit(solution)/shard_map/pallas_call | solution.py:20
  53.4 1.2 %collective-permute-start.17 = (bf16[512,384]{1,0:T(8,128)(2,1)S(1)}, bf16[512,384]{1,0:T(8,128)(2,1)S(1)}, u32[]{:S(2)}, u32[]{:S(2)}) collective-permute-start(bf16[512,384]{1,0:T(8,128)(2,1)S(1)} %get-tuple-element.87), channel_id=1, source_target_pairs={{0,4},{1,5},{2,6},{3,7},{4,12},{5,13},{6,14},{7,15},{8,0},{9,1},{1... | collective-permute-start | bytes 1179656 | tf_op jit(solution)/shard_map/ppermute | solution.py:382
  54.6 0.1 collective-permute-start.14
  54.6 1.7 %collective-permute-start.15 = (f32[4,128]{1,0:T(4,128)S(1)}, f32[4,128]{1,0:T(4,128)S(1)}, u32[]{:S(2)}, u32[]{:S(2)}) collective-permute-start(f32[4,128]{1,0:T(4,128)S(1)} %get-tuple-element.86), channel_id=1, source_target_pairs={{0,8},{1,9},{2,10},{3,11},{4,12},{5,13},{6,14},{7,15},{8,0},{9,1},... | collective-permute-start | bytes 6152 | tf_op jit(solution)/shard_map/ppermute | solution.py:375
  56.4 2.6 %collective-permute-start.16 = (f32[4,128]{1,0:T(4,128)S(1)}, f32[4,128]{1,0:T(4,128)S(1)}, u32[]{:S(2)}, u32[]{:S(2)}) collective-permute-start(f32[4,128]{1,0:T(4,128)S(1)} %get-tuple-element.86), channel_id=1, source_target_pairs={{0,12},{1,13},{2,14},{3,15},{4,8},{5,9},{6,10},{7,11},{8,4},{9,5},... | collective-permute-start | bytes 6152 | tf_op jit(solution)/shard_map/ppermute | solution.py:375
  58.9 5.1 %collective-permute-done.14 = f32[4,128]{1,0:T(4,128)S(1)} collective-permute-done((f32[4,128]{1,0:T(4,128)S(1)}, f32[4,128]{1,0:T(4,128)S(1)}, u32[]{:S(2)}, u32[]{:S(2)}) %collective-permute-start.14) | collective-permute-done | bytes 2080 | tf_op jit(solution)/shard_map/ppermute | solution.py:375
  64.1 2.4 %collective-permute-done.15 = f32[4,128]{1,0:T(4,128)S(1)} collective-permute-done((f32[4,128]{1,0:T(4,128)S(1)}, f32[4,128]{1,0:T(4,128)S(1)}, u32[]{:S(2)}, u32[]{:S(2)}) %collective-permute-start.15) | collective-permute-done | bytes 2080 | tf_op jit(solution)/shard_map/ppermute | solution.py:375
  66.5 0.2 shard_map.61.refs_0_.refs_2_
  66.6 0.8 shard_map.62
  67.5 3.8 %collective-permute-done.18.refs_1_ = bf16[512,256]{1,0:T(8,128)(2,1)S(1)} collective-permute-done((bf16[512,256]{1,0:T(8,128)(2,1)S(1)}, bf16[512,256]{1,0:T(8,128)(2,1)S(1)}, u32[]{:S(2)}, u32[]{:S(2)}) %collective-permute-start.18) | collective-permute-done | bytes 262176 | tf_op jit(solution)/shard_map/ppermute | solution.py:382
  71.3 0.9 shard_map.63
  72.2 0.2 collective-permute-start.19
  72.5 0.3 collective-permute-start.20
  72.7 1.2 %collective-permute-done.22.got_ref = bf16[2,160,640]{2,1,0:T(8,128)(2,1)S(1)} collective-permute-done((bf16[2,160,640]{2,1,0:T(8,128)(2,1)S(1)}, bf16[2,160,640]{2,1,0:T(8,128)(2,1)S(1)}, u32[]{:S(2)}, u32[]{:S(2)}) %collective-permute-start.22) | collective-permute-done | bytes 409632 | tf_op jit(solution)/shard_map/ppermute | solution.py:375
  74.0 0.1 shard_map.65
  74.1 0.8 shard_map.66
  74.9 0.2 collective-permute-start.23
  75.1 0.6 collective-permute-start.25
  75.8 1.5 %collective-permute-start.21 = (bf16[1,160,640]{2,1,0:T(8,128)(2,1)S(1)}, bf16[1,160,640]{2,1,0:T(8,128)(2,1)S(1)}, u32[]{:S(2)}, u32[]{:S(2)}) collective-permute-start(bf16[1,160,640]{2,1,0:T(8,128)(2,1)S(1)} %get-tuple-element.97), channel_id=1, source_target_pairs={{0,2},{1,3},{2,0},{3,1},{4,6},{5,7},{6,4},{7,5},{8,10},{9,11},{10,... | collective-permute-start | bytes 614408 | tf_op jit(solution)/shard_map/ppermute | solution.py:375
  77.3 0.1 shard_map.67
  77.3 0.7 collective-permute-start.24
  78.0 5.0 %collective-permute-done.25 = bf16[1,160,640]{2,1,0:T(8,128)(2,1)S(1)} collective-permute-done((bf16[1,160,640]{2,1,0:T(8,128)(2,1)S(1)}, bf16[1,160,640]{2,1,0:T(8,128)(2,1)S(1)}, u32[]{:S(2)}, u32[]{:S(2)}) %collective-permute-start.25) | collective-permute-done | bytes 204832 | tf_op jit(solution)/shard_map/ppermute | solution.py:375
  83.0 4.4 %collective-permute-done.21 = bf16[1,160,640]{2,1,0:T(8,128)(2,1)S(1)} collective-permute-done((bf16[1,160,640]{2,1,0:T(8,128)(2,1)S(1)}, bf16[1,160,640]{2,1,0:T(8,128)(2,1)S(1)}, u32[]{:S(2)}, u32[]{:S(2)}) %collective-permute-start.21) | collective-permute-done | bytes 204832 | tf_op jit(solution)/shard_map/ppermute | solution.py:375
  87.4 2.9 %collective-permute-done.19.refs_1_ = bf16[512,640]{1,0:T(8,128)(2,1)S(1)} collective-permute-done((bf16[512,640]{1,0:T(8,128)(2,1)S(1)}, bf16[512,640]{1,0:T(8,128)(2,1)S(1)}, u32[]{:S(2)}, u32[]{:S(2)}) %collective-permute-start.19) | collective-permute-done | bytes 655392 | tf_op jit(solution)/shard_map/ppermute | solution.py:382
  90.3 0.9 collective-permute-done.24
  91.2 0.8 shard_map.68
  92.2 1.5 %collective-permute-start.28 = (bf16[160,640]{1,0:T(8,128)(2,1)S(1)}, bf16[160,640]{1,0:T(8,128)(2,1)S(1)}, u32[]{:S(2)}, u32[]{:S(2)}) collective-permute-start(bf16[160,640]{1,0:T(8,128)(2,1)S(1)} %fusion), channel_id=1, source_target_pairs={{0,8},{1,9},{2,10},{3,11},{4,0},{5,1},{6,2},{7,3},{8,12},{9,13},{1... | collective-permute-start | bytes 614408 | tf_op jit(solution)/shard_map/ppermute | solution.py:382
  93.6 0.2 collective-permute-done.26.got_ref
  93.8 0.1 shard_map.69
  93.9 0.7 collective-permute-start.27
  94.6 1.5 %shard_map.70.refs_2_ = f32[160,2560]{1,0:T(8,128)} custom-call(s32[4]{0:T(128)S(1)} %shift-right-arithmetic_xor_fusion.at_ref, f32[160,640]{1,0:T(8,128)S(1)} %bitcast.38, bf16[160,640]{1,0:T(8,128)(2,1)S(1)} %bitcast.41, f32[160,640]{1,0:T(8,128)S(1)} %bitcast.39, bf16[160,640]{1,0:T(8,128)(2,1)S(1)} %bitcast.42), custom_call_target="tpu_custom_call" | custom-call | flops 1 | bytes 1 | tf_op jit(solution)/shard_map/pallas_call | solution.py:349
  96.1 3.6 %collective-permute-done.28.refs_0_ = bf16[160,640]{1,0:T(8,128)(2,1)S(1)} collective-permute-done((bf16[160,640]{1,0:T(8,128)(2,1)S(1)}, bf16[160,640]{1,0:T(8,128)(2,1)S(1)}, u32[]{:S(2)}, u32[]{:S(2)}) %collective-permute-start.28) | collective-permute-done | bytes 204832 | tf_op jit(solution)/shard_map/ppermute | solution.py:382
  99.7 1.3 %shard_map.71.refs_2_ = f32[160,2560]{1,0:T(8,128)} custom-call(s32[4]{0:T(128)S(1)} %shift-right-arithmetic_xor_fusion.at_ref, bf16[160,640]{1,0:T(8,128)(2,1)S(1)} %collective-permute-done.28.refs_0_, bf16[160,640]{1,0:T(8,128)(2,1)S(1)} %broadcast_in_dim.7.refs_1_, f32[160,2560]{1,0:T(8,128)} %shard_map.70.refs_2_), custom_call_target="tpu_custom_call", output_to_operand_aliasing={{}: (3, {})} | custom-call | flops 1 | bytes 1 | tf_op jit(solution)/shard_map/pallas_call | solution.py:349
  101.1 1.3 %shard_map.72 = f32[160,2560]{1,0:T(8,128)} custom-call(s32[4]{0:T(128)S(1)} %shift-right-arithmetic_xor_fusion.at_ref, f32[160,640]{1,0:T(8,128)S(1)} %bitcast.40, bf16[160,640]{1,0:T(8,128)(2,1)S(1)} %bitcast.43, f32[160,2560]{1,0:T(8,128)} %shard_map.71.refs_2_), custom_call_target="tpu_custom_call", output_to_operand_aliasing={{}: (3, {})} | custom-call | flops 1 | bytes 1 | tf_op jit(solution)/shard_map/pallas_call | solution.py:349
  (36 shorter events, 0.5 us)
Async XLA Ops:
  0.0 18.9 %copy-start = (bf16[128,3968]{1,0:T(8,128)(2,1)S(1)}, bf16[128,3968]{1,0:T(8,128)(2,1)}, u32[]{:S(2)}) copy-start(bf16[128,3968]{1,0:T(8,128)(2,1)} %flux_ref) | copy-start | bytes 3047428
  0.8 6.8 %collective-permute-start = (s32[148]{0:T(256)S(1)}, s32[148]{0:T(256)S(1)}, u32[]{:S(2)}, u32[]{:S(2)}) collective-permute-start(s32[148]{0:T(256)S(1)} %pad_add_fusion.3), channel_id=1, source_target_pairs={{0,4},{1,5},{2,6},{3,7},{4,0},{5,1},{6,2},{7,3},{8,12},{9,13},{10,... | collective-permute-start | bytes 1784 | tf_op jit(solution)/shard_map/ppermute | solution.py:375
  3.9 4.5 %collective-permute-start.1 = (s32[148]{0:T(256)S(1)}, s32[148]{0:T(256)S(1)}, u32[]{:S(2)}, u32[]{:S(2)}) collective-permute-start(s32[148]{0:T(256)S(1)} %pad_add_fusion.3), channel_id=1, source_target_pairs={{0,8},{1,9},{2,10},{3,11},{4,12},{5,13},{6,14},{7,15},{8,0},{9,1},... | collective-permute-start | bytes 1784 | tf_op jit(solution)/shard_map/ppermute | solution.py:375
  6.4 5.4 %collective-permute-start.2 = (s32[148]{0:T(256)S(1)}, s32[148]{0:T(256)S(1)}, u32[]{:S(2)}, u32[]{:S(2)}) collective-permute-start(s32[148]{0:T(256)S(1)} %pad_add_fusion.3), channel_id=1, source_target_pairs={{0,12},{1,13},{2,14},{3,15},{4,8},{5,9},{6,10},{7,11},{8,4},{9,5},... | collective-permute-start | bytes 1784 | tf_op jit(solution)/shard_map/ppermute | solution.py:375
  11.8 4.5 %collective-permute-start.6 = (s32[4,1,20]{2,0,1:T(4,128)S(1)}, s32[4,1,20]{2,0,1:T(4,128)S(1)}, u32[]{:S(2)}, u32[]{:S(2)}) collective-permute-start(s32[4,1,20]{2,0,1:T(4,128)S(1)} %slice_bitcast_fusion), channel_id=1, source_target_pairs={{0,1},{1,0},{2,3},{3,2},{4,5},{5,4},{6,7},{7,6},{8,9},{9,8},{10,11... | collective-permute-start | bytes 968 | tf_op jit(solution)/shard_map/ppermute | solution.py:375
  11.9 19.0 %collective-permute-start.3 = (bf16[640,128]{1,0:T(8,128)(2,1)S(1)}, bf16[640,128]{1,0:T(8,128)(2,1)S(1)}, u32[]{:S(2)}, u32[]{:S(2)}) collective-permute-start(bf16[640,128]{1,0:T(8,128)(2,1)S(1)} %get-tuple-element.119), channel_id=1, source_target_pairs={{0,4},{1,5},{2,6},{3,7},{4,0},{5,1},{6,2},{7,3},{8,12},{9,13},{10,... | collective-permute-start | bytes 491528 | tf_op jit(solution)/shard_map/ppermute | solution.py:375
  12.0 18.9 %collective-permute-start.4 = (bf16[640,128]{1,0:T(8,128)(2,1)S(1)}, bf16[640,128]{1,0:T(8,128)(2,1)S(1)}, u32[]{:S(2)}, u32[]{:S(2)}) collective-permute-start(bf16[640,128]{1,0:T(8,128)(2,1)S(1)} %get-tuple-element.118), channel_id=1, source_target_pairs={{0,8},{1,9},{2,10},{3,11},{4,12},{5,13},{6,14},{7,15},{8,0},{9,1},... | collective-permute-start | bytes 491528 | tf_op jit(solution)/shard_map/ppermute | solution.py:375
  12.6 18.3 %collective-permute-start.5 = (bf16[640,128]{1,0:T(8,128)(2,1)S(1)}, bf16[640,128]{1,0:T(8,128)(2,1)S(1)}, u32[]{:S(2)}, u32[]{:S(2)}) collective-permute-start(bf16[640,128]{1,0:T(8,128)(2,1)S(1)} %get-tuple-element.117), channel_id=1, source_target_pairs={{0,12},{1,13},{2,14},{3,15},{4,8},{5,9},{6,10},{7,11},{8,4},{9,5},... | collective-permute-start | bytes 491528 | tf_op jit(solution)/shard_map/ppermute | solution.py:375
  16.4 9.8 %collective-permute-start.7 = (s32[4,2,20]{2,0,1:T(4,128)S(1)}, s32[4,2,20]{2,0,1:T(4,128)S(1)}, u32[]{:S(2)}, u32[]{:S(2)}) collective-permute-start(s32[4,2,20]{2,0,1:T(4,128)S(1)} %pad_add_fusion.2), channel_id=1, source_target_pairs={{0,2},{1,3},{2,0},{3,1},{4,6},{5,7},{6,4},{7,5},{8,10},{9,11},{10,... | collective-permute-start | bytes 1928 | tf_op jit(solution)/shard_map/ppermute | solution.py:375
  18.0 0.7 copy-start.1
  31.0 3.7 %collective-permute-start.9 = (bf16[4,640,128]{2,1,0:T(8,128)(2,1)S(1)}, bf16[4,640,128]{2,1,0:T(8,128)(2,1)S(1)}, u32[]{:S(2)}, u32[]{:S(2)}) collective-permute-start(bf16[4,640,128]{2,1,0:T(8,128)(2,1)S(1)} %pad_maximum_fusion.refs_2_), channel_id=1, source_target_pairs={{0,1},{1,0},{2,3},{3,2},{4,5},{5,4},{6,7},{7,6},{8,9},{9,8},{10,11... | collective-permute-start | bytes 1966088 | tf_op jit(solution)/shard_map/ppermute | solution.py:375
  31.1 17.7 %collective-permute-start.8 = (bf16[4,640,128]{2,1,0:T(8,128)(2,1)S(1)}, bf16[4,640,128]{2,1,0:T(8,128)(2,1)S(1)}, u32[]{:S(2)}, u32[]{:S(2)}) collective-permute-start(bf16[4,640,128]{2,1,0:T(8,128)(2,1)S(1)} %pad_maximum_fusion.refs_2_), channel_id=1, source_target_pairs={{0,2},{1,3},{2,0},{3,1},{4,6},{5,7},{6,4},{7,5},{8,10},{9,11},{10,... | collective-permute-start | bytes 1966088 | tf_op jit(solution)/shard_map/ppermute | solution.py:375
  31.7 17.1 %collective-permute-start.11 = (bf16[128,640]{1,0:T(8,128)(2,1)S(1)}, bf16[128,640]{1,0:T(8,128)(2,1)S(1)}, u32[]{:S(2)}, u32[]{:S(2)}) collective-permute-start(bf16[128,640]{1,0:T(8,128)(2,1)S(1)} %get-tuple-element.77), channel_id=1, source_target_pairs={{0,8},{1,9},{2,10},{3,11},{4,12},{5,13},{6,14},{7,15},{8,0},{9,1},... | collective-permute-start | bytes 491528 | tf_op jit(solution)/shard_map/ppermute | solution.py:375
  32.3 16.5 %collective-permute-start.12 = (bf16[128,640]{1,0:T(8,128)(2,1)S(1)}, bf16[128,640]{1,0:T(8,128)(2,1)S(1)}, u32[]{:S(2)}, u32[]{:S(2)}) collective-permute-start(bf16[128,640]{1,0:T(8,128)(2,1)S(1)} %get-tuple-element.78), channel_id=1, source_target_pairs={{0,12},{1,13},{2,14},{3,15},{4,8},{5,9},{6,10},{7,11},{8,4},{9,5},... | collective-permute-start | bytes 491528 | tf_op jit(solution)/shard_map/ppermute | solution.py:375
  34.7 12.5 %collective-permute-start.10 = (bf16[128,640]{1,0:T(8,128)(2,1)S(1)}, bf16[128,640]{1,0:T(8,128)(2,1)S(1)}, u32[]{:S(2)}, u32[]{:S(2)}) collective-permute-start(bf16[128,640]{1,0:T(8,128)(2,1)S(1)} %get-tuple-element.75), channel_id=1, source_target_pairs={{0,4},{1,5},{2,6},{3,7},{4,0},{5,1},{6,2},{7,3},{8,12},{9,13},{10,... | collective-permute-start | bytes 491528 | tf_op jit(solution)/shard_map/ppermute | solution.py:375
  48.8 2.2 %collective-permute-start.13 = (bf16[4,640,128]{2,1,0:T(8,128)(2,1)S(1)}, bf16[4,640,128]{2,1,0:T(8,128)(2,1)S(1)}, u32[]{:S(2)}, u32[]{:S(2)}) collective-permute-start(bf16[4,640,128]{2,1,0:T(8,128)(2,1)S(1)} %collective-permute-done.8.refs_6_), channel_id=1, source_target_pairs={{0,1},{1,0},{2,3},{3,2},{4,5},{5,4},{6,7},{7,6},{8,9},{9,8},{10,11... | collective-permute-start | bytes 1966088 | tf_op jit(solution)/shard_map/ppermute | solution.py:375
  53.4 13.1 %collective-permute-start.17 = (bf16[512,384]{1,0:T(8,128)(2,1)S(1)}, bf16[512,384]{1,0:T(8,128)(2,1)S(1)}, u32[]{:S(2)}, u32[]{:S(2)}) collective-permute-start(bf16[512,384]{1,0:T(8,128)(2,1)S(1)} %get-tuple-element.87), channel_id=1, source_target_pairs={{0,4},{1,5},{2,6},{3,7},{4,12},{5,13},{6,14},{7,15},{8,0},{9,1},{1... | collective-permute-start | bytes 1179656 | tf_op jit(solution)/shard_map/ppermute | solution.py:382
  54.6 9.5 %collective-permute-start.14 = (f32[4,128]{1,0:T(4,128)S(1)}, f32[4,128]{1,0:T(4,128)S(1)}, u32[]{:S(2)}, u32[]{:S(2)}) collective-permute-start(f32[4,128]{1,0:T(4,128)S(1)} %get-tuple-element.86), channel_id=1, source_target_pairs={{0,4},{1,5},{2,6},{3,7},{4,0},{5,1},{6,2},{7,3},{8,12},{9,13},{10,... | collective-permute-start | bytes 6152 | tf_op jit(solution)/shard_map/ppermute | solution.py:375
  54.6 11.8 %collective-permute-start.15 = (f32[4,128]{1,0:T(4,128)S(1)}, f32[4,128]{1,0:T(4,128)S(1)}, u32[]{:S(2)}, u32[]{:S(2)}) collective-permute-start(f32[4,128]{1,0:T(4,128)S(1)} %get-tuple-element.86), channel_id=1, source_target_pairs={{0,8},{1,9},{2,10},{3,11},{4,12},{5,13},{6,14},{7,15},{8,0},{9,1},... | collective-permute-start | bytes 6152 | tf_op jit(solution)/shard_map/ppermute | solution.py:375
  56.4 10.1 %collective-permute-start.16 = (f32[4,128]{1,0:T(4,128)S(1)}, f32[4,128]{1,0:T(4,128)S(1)}, u32[]{:S(2)}, u32[]{:S(2)}) collective-permute-start(f32[4,128]{1,0:T(4,128)S(1)} %get-tuple-element.86), channel_id=1, source_target_pairs={{0,12},{1,13},{2,14},{3,15},{4,8},{5,9},{6,10},{7,11},{8,4},{9,5},... | collective-permute-start | bytes 6152 | tf_op jit(solution)/shard_map/ppermute | solution.py:375
  58.9 12.3 %collective-permute-start.18 = (bf16[512,256]{1,0:T(8,128)(2,1)S(1)}, bf16[512,256]{1,0:T(8,128)(2,1)S(1)}, u32[]{:S(2)}, u32[]{:S(2)}) collective-permute-start(bf16[512,256]{1,0:T(8,128)(2,1)S(1)} %get-tuple-element.90), channel_id=1, source_target_pairs={{0,4},{1,5},{2,6},{3,7},{4,12},{5,13},{6,14},{7,15},{8,0},{9,1},{1... | collective-permute-start | bytes 786440 | tf_op jit(solution)/shard_map/ppermute | solution.py:382
  72.2 1.8 %collective-permute-start.22 = (bf16[2,160,640]{2,1,0:T(8,128)(2,1)S(1)}, bf16[2,160,640]{2,1,0:T(8,128)(2,1)S(1)}, u32[]{:S(2)}, u32[]{:S(2)}) collective-permute-start(bf16[2,160,640]{2,1,0:T(8,128)(2,1)S(1)} %get-tuple-element.99), channel_id=1, source_target_pairs={{0,1},{1,0},{2,3},{3,2},{4,5},{5,4},{6,7},{7,6},{8,9},{9,8},{10,11... | collective-permute-start | bytes 1228808 | tf_op jit(solution)/shard_map/ppermute | solution.py:375
  72.2 18.0 %collective-permute-start.19 = (bf16[512,640]{1,0:T(8,128)(2,1)S(1)}, bf16[512,640]{1,0:T(8,128)(2,1)S(1)}, u32[]{:S(2)}, u32[]{:S(2)}) collective-permute-start(bf16[512,640]{1,0:T(8,128)(2,1)S(1)} %get-tuple-element.101.refs_1_), channel_id=1, source_target_pairs={{0,4},{1,5},{2,6},{3,7},{4,12},{5,13},{6,14},{7,15},{8,0},{9,1},{1... | collective-permute-start | bytes 1966088 | tf_op jit(solution)/shard_map/ppermute | solution.py:382
  72.5 3.3 %collective-permute-start.20 = (bf16[2,160,640]{2,1,0:T(8,128)(2,1)S(1)}, bf16[2,160,640]{2,1,0:T(8,128)(2,1)S(1)}, u32[]{:S(2)}, u32[]{:S(2)}) collective-permute-start(bf16[2,160,640]{2,1,0:T(8,128)(2,1)S(1)} %get-tuple-element.96), channel_id=1, source_target_pairs={{0,1},{1,0},{2,3},{3,2},{4,5},{5,4},{6,7},{7,6},{8,9},{9,8},{10,11... | collective-permute-start | bytes 1228808 | tf_op jit(solution)/shard_map/ppermute | solution.py:375
  74.9 2.4 %collective-permute-start.23 = (bf16[2,160,640]{2,1,0:T(8,128)(2,1)S(1)}, bf16[2,160,640]{2,1,0:T(8,128)(2,1)S(1)}, u32[]{:S(2)}, u32[]{:S(2)}) collective-permute-start(bf16[2,160,640]{2,1,0:T(8,128)(2,1)S(1)} %get-tuple-element.103), channel_id=1, source_target_pairs={{0,1},{1,0},{2,3},{3,2},{4,5},{5,4},{6,7},{7,6},{8,9},{9,8},{10,11... | collective-permute-start | bytes 1228808 | tf_op jit(solution)/shard_map/ppermute | solution.py:375
  75.1 7.9 %collective-permute-start.25 = (bf16[1,160,640]{2,1,0:T(8,128)(2,1)S(1)}, bf16[1,160,640]{2,1,0:T(8,128)(2,1)S(1)}, u32[]{:S(2)}, u32[]{:S(2)}) collective-permute-start(bf16[1,160,640]{2,1,0:T(8,128)(2,1)S(1)} %get-tuple-element.105), channel_id=1, source_target_pairs={{0,2},{1,3},{2,0},{3,1},{4,6},{5,7},{6,4},{7,5},{8,10},{9,11},{10,... | collective-permute-start | bytes 614408 | tf_op jit(solution)/shard_map/ppermute | solution.py:375
  75.8 11.6 %collective-permute-start.21 = (bf16[1,160,640]{2,1,0:T(8,128)(2,1)S(1)}, bf16[1,160,640]{2,1,0:T(8,128)(2,1)S(1)}, u32[]{:S(2)}, u32[]{:S(2)}) collective-permute-start(bf16[1,160,640]{2,1,0:T(8,128)(2,1)S(1)} %get-tuple-element.97), channel_id=1, source_target_pairs={{0,2},{1,3},{2,0},{3,1},{4,6},{5,7},{6,4},{7,5},{8,10},{9,11},{10,... | collective-permute-start | bytes 614408 | tf_op jit(solution)/shard_map/ppermute | solution.py:375
  77.3 13.9 %collective-permute-start.24 = (bf16[1,160,640]{2,1,0:T(8,128)(2,1)S(1)}, bf16[1,160,640]{2,1,0:T(8,128)(2,1)S(1)}, u32[]{:S(2)}, u32[]{:S(2)}) collective-permute-start(bf16[1,160,640]{2,1,0:T(8,128)(2,1)S(1)} %get-tuple-element.104), channel_id=1, source_target_pairs={{0,2},{1,3},{2,0},{3,1},{4,6},{5,7},{6,4},{7,5},{8,10},{9,11},{10,... | collective-permute-start | bytes 614408 | tf_op jit(solution)/shard_map/ppermute | solution.py:375
  92.0 1.8 %collective-permute-start.26 = (bf16[2,160,640]{2,1,0:T(8,128)(2,1)S(1)}, bf16[2,160,640]{2,1,0:T(8,128)(2,1)S(1)}, u32[]{:S(2)}, u32[]{:S(2)}) collective-permute-start(bf16[2,160,640]{2,1,0:T(8,128)(2,1)S(1)} %get-tuple-element.108), channel_id=1, source_target_pairs={{0,1},{1,0},{2,3},{3,2},{4,5},{5,4},{6,7},{7,6},{8,9},{9,8},{10,11... | collective-permute-start | bytes 1228808 | tf_op jit(solution)/shard_map/ppermute | solution.py:375
  92.2 7.5 %collective-permute-start.28 = (bf16[160,640]{1,0:T(8,128)(2,1)S(1)}, bf16[160,640]{1,0:T(8,128)(2,1)S(1)}, u32[]{:S(2)}, u32[]{:S(2)}) collective-permute-start(bf16[160,640]{1,0:T(8,128)(2,1)S(1)} %fusion), channel_id=1, source_target_pairs={{0,8},{1,9},{2,10},{3,11},{4,0},{5,1},{6,2},{7,3},{8,12},{9,13},{1... | collective-permute-start | bytes 614408 | tf_op jit(solution)/shard_map/ppermute | solution.py:382
  93.9 7.2 %collective-permute-start.27 = (bf16[1,160,640]{2,1,0:T(8,128)(2,1)S(1)}, bf16[1,160,640]{2,1,0:T(8,128)(2,1)S(1)}, u32[]{:S(2)}, u32[]{:S(2)}) collective-permute-start(bf16[1,160,640]{2,1,0:T(8,128)(2,1)S(1)} %get-tuple-element.110), channel_id=1, source_target_pairs={{0,2},{1,3},{2,0},{3,1},{4,6},{5,7},{6,4},{7,5},{8,10},{9,11},{10,... | collective-permute-start | bytes 614408 | tf_op jit(solution)/shard_map/ppermute | solution.py:375

commit v15 on v14

--- a/solution.py
+++ b/solution.py
@@ -54,7 +54,7 @@
     edge = jnp.zeros((tall, reach), F32)
     padded[:, :reach] = edge
     padded[:, reach + nobs :] = edge
-    step = 256
+    step = 512
 
     def one_tile(tile, carry):
         own = own_rows(tile)
@@ -383,8 +383,8 @@
             array, "spec", [(o * inner + i, to[o] * inner + i) for o in range(OUTER) for i in range(inner)]
         )
 
-    targets = destination[:, 0]
-    table = jnp.concatenate([band_offset[0], targets])
+    table = lax.optimization_barrier(jnp.concatenate([band_offset[0], destination[:, 0]]))
+    targets = table[nblocks:]
     tables = jnp.stack([table] + [swap(table, away * inner) for away in range(1, OUTER)])
     names, offsets = tables[:, nblocks:], tables[:, None, :nblocks]
     bit = 1
@@ -428,9 +428,9 @@
         near_bins = near_bins + [piece ^ bit for piece in near_bins]
     far_bins = jnp.concatenate([piece ^ (inner // 2) for piece in near_bins])
     near_bins = jnp.concatenate(near_bins)
-    begun = [begin_rest(near_bins, names, (0, 1), arrived[:2], near, band)]
+    begun = [begin_rest(near_bins, names, (0,), arrived[:1], near, band)]
     across, begun[0], *arrived = lax.optimization_barrier((weights[1], begun[0], *arrived))
-    begun.append(begin_rest(near_bins, names, (2, 3), arrived[2:], near, band))
+    begun.append(begin_rest(near_bins, names, (1, 2, 3), arrived[1:], near, band))
     far = [across]
     for bit in bits:
         far = far + [swap(piece, bit) for piece in far]
@@ -473,8 +473,7 @@
     got2 = finish(send2)
     at = fold_at((fold_at(outer) - jnp.arange(OUTER, dtype=I32)) % OUTER)
     begun = place(at, [0, 1], [(held0, got0), (held1, got1)])
-    begun = place(at, [3], [(back, jnp.zeros_like(back))], begun)
-    return place(at, [2], [(held2, got2)], begun)
+    return place(at, [2, 3], [(held2, got2), (back, jnp.zeros_like(back))], begun)
 
 
 def solution(mesh):

time: 103 us -> 98.4 us (0.955)
  waiting for transfers between devices: 46.1 us -> 39.1 us
  starting transfers between devices: 27.2 us -> 32.4 us
  Pallas kernels: 25.6 us -> 23.8 us
    ppermute x25, waiting for transfers between devices: 35.8 us -> 29.6 us  [swap(): return lax.ppermute(array, 'spec', [(i, i ^ bit) for i in range(n)])]
    ppermute x25, starting transfers between devices: 24.3 us -> 27.3 us  [swap(): return lax.ppermute(array, 'spec', [(i, i ^ bit) for i in range(n)])]
    ppermute x4, starting transfers between devices: 2.86 us -> 5.17 us  [step(): lax.ppermute(array, 'spec', [(o * inner + i, to[o] * inner + i) for o in...]
    pallas_call x3 -> x2, Pallas kernels: 4.18 us -> 2.98 us  [place(): pl.pallas_call(functools.partial(place_kernel, slots, last), out_shape=ja...]
  transfers between devices with their start and end apart: 29 -> 29, of which waited for: 15 -> 15; matrix products, arithmetic and copies ran while one was open for 2% -> 2% of each run, Pallas kernels for 20% -> 19%
where the time goes in v15:
time: 98.4 us; the launch traced here: 98.2 us
  waiting for transfers between devices  39.1 us (40%)
  starting transfers between devices  32.4 us (33%)
  Pallas kernels  23.8 us (24%)
  local copies, waits for them, and re-layouts  1.37 us (1%)
  other arithmetic  1.27 us (1%)
    ppermute x25, waiting for transfers between devices, swap(): return lax.ppermute(array, 'spec', [(i, i ^ bit) for i in range(n)])  29.6 us
    ppermute x25, starting transfers between devices, swap(): return lax.ppermute(array, 'spec', [(i, i ^ bit) for i in range(n)])  27.3 us
    pallas_call x15, Pallas kernels, call(): pl.pallas_call(kernel, out_shape=out_shape, in_specs=in_specs, out_specs=...  20.8 us
    ppermute x4, waiting for transfers between devices, step(): lax.ppermute(array, 'spec', [(o * inner + i, to[o] * inner + i) for o in...  9.53 us
    ppermute x4, starting transfers between devices, step(): lax.ppermute(array, 'spec', [(o * inner + i, to[o] * inner + i) for o in...  5.17 us
    pallas_call x2, Pallas kernels, place(): pl.pallas_call(functools.partial(place_kernel, slots, last), out_shape=ja...  2.98 us
  transfers between devices with their start and end apart: 29, of which 15 were waited for; matrix products, arithmetic and copies ran while one was open for 2% of the time, Pallas kernels for 19%

profile of v15, /device:TPU:0, one launch (start us, length us, event | category | flops | bytes accessed | tf_op | source)
XLA Modules:
  0.0 98.2 jit_solution(6836751327506077005)
XLA Ops:
  0.0 0.8 pad_add_fusion.3
  0.8 3.0 %collective-permute-start = (s32[148]{0:T(256)S(1)}, s32[148]{0:T(256)S(1)}, u32[]{:S(2)}, u32[]{:S(2)}) collective-permute-start(s32[148]{0:T(256)S(1)} %pad_add_fusion.3), channel_id=1, source_target_pairs={{0,4},{1,5},{2,6},{3,7},{4,0},{5,1},{6,2},{7,3},{8,12},{9,13},{10,... | collective-permute-start | bytes 1784 | tf_op jit(solution)/shard_map/ppermute | solution.py:375
  3.9 2.6 %collective-permute-start.1 = (s32[148]{0:T(256)S(1)}, s32[148]{0:T(256)S(1)}, u32[]{:S(2)}, u32[]{:S(2)}) collective-permute-start(s32[148]{0:T(256)S(1)} %pad_add_fusion.3), channel_id=1, source_target_pairs={{0,8},{1,9},{2,10},{3,11},{4,12},{5,13},{6,14},{7,15},{8,0},{9,1},... | collective-permute-start | bytes 1784 | tf_op jit(solution)/shard_map/ppermute | solution.py:375
  6.5 1.2 %dynamic-slice_bitcast_fusion = (bf16[640,128]{1,0:T(8,128)(2,1)S(1)}, bf16[640,128]{1,0:T(8,128)(2,1)S(1)}, bf16[640,128]{1,0:T(8,128)(2,1)S(1)}, bf16[640,128]{1,0:T(8,128)(2,1)S(1)}) fusion(bf16[4,640,128]{2,1,0:T(8,128)(2,1)} %bitcast.47, s32[]{:T(128)S(6)} %select_n.41, s32[]{:T(128)S(6)} %select_n.40, s32[]{:T(128)S(6)} %select_n.39, s32[]{:T(128)S(6)} %select_n.38), kind=kLoop, calls=%fused_computation.3 | loop fusion | bytes 1310736 | tf_op jit(solution)/shard_map/jit(dynamic_index_in_dim)/squeeze | solution.py:401
  7.7 1.0 collective-permute-start.3
  8.6 3.5 %collective-permute-start.4 = (bf16[640,128]{1,0:T(8,128)(2,1)S(1)}, bf16[640,128]{1,0:T(8,128)(2,1)S(1)}, u32[]{:S(2)}, u32[]{:S(2)}) collective-permute-start(bf16[640,128]{1,0:T(8,128)(2,1)S(1)} %get-tuple-element.118), channel_id=1, source_target_pairs={{0,8},{1,9},{2,10},{3,11},{4,12},{5,13},{6,14},{7,15},{8,0},{9,1},... | collective-permute-start | bytes 491528 | tf_op jit(solution)/shard_map/ppermute | solution.py:375
  12.2 0.1 slice_bitcast_fusion.1.targets_ref
  12.3 1.1 %collective-permute-done.6 = s32[4,1,20]{2,0,1:T(4,128)S(1)} collective-permute-done((s32[4,1,20]{2,0,1:T(4,128)S(1)}, s32[4,1,20]{2,0,1:T(4,128)S(1)}, u32[]{:S(2)}, u32[]{:S(2)}) %collective-permute-start.6) | collective-permute-done | bytes 352 | tf_op jit(solution)/shard_map/ppermute | solution.py:375
  13.4 1.7 %collective-permute-start.7 = (s32[4,2,20]{2,0,1:T(4,128)S(1)}, s32[4,2,20]{2,0,1:T(4,128)S(1)}, u32[]{:S(2)}, u32[]{:S(2)}) collective-permute-start(s32[4,2,20]{2,0,1:T(4,128)S(1)} %pad_add_fusion.2), channel_id=1, source_target_pairs={{0,2},{1,3},{2,0},{3,1},{4,6},{5,7},{6,4},{7,5},{8,10},{9,11},{10,... | collective-permute-start | bytes 1928 | tf_op jit(solution)/shard_map/ppermute | solution.py:375
  15.1 0.1 pad_add_fusion.5.me_ref
  15.2 0.2 shard_map.55
  15.4 6.7 %shard_map.56.smoothed_ref = bf16[128,3968]{1,0:T(8,128)(2,1)S(1)} custom-call(bf16[128,3968]{1,0:T(8,128)(2,1)S(1)} %copy-done, bf16[11,128,3968]{2,1,0:T(8,128)(2,1)} %bitcast.45), custom_call_target="tpu_custom_call" | custom-call | flops 1 | bytes 1 | tf_op jit(solution)/shard_map/pallas_call | solution.py:20
  22.2 4.7 %shard_map.57 = (bf16[128,640]{1,0:T(8,128)(2,1)S(1)}, bf16[128,640]{1,0:T(8,128)(2,1)S(1)}, bf16[128,640]{1,0:T(8,128)(2,1)S(1)}, bf16[128,640]{1,0:T(8,128)(2,1)S(1)}) custom-call(s32[2]{0:T(128)S(1)} %pad_add_fusion.5.me_ref, s32[2,128]{1,0:T(2,128)S(1)} %get-tuple-element.61.groups_ref, s32[16,20]{1,0:T(8,128)S(1)} %get-tuple-element.122.starts_ref, ...), custom_call_target="tpu_custom_call" | custom-call | flops 1 | bytes 1 | tf_op jit(solution)/shard_map/pallas_call | solution.py:20
  27.0 0.1 pad_maximum_fusion.refs_1_.refs_3_
  27.1 0.1 collective-permute-start.9
  27.1 0.4 collective-permute-start.8
  27.5 1.5 %collective-permute-start.11 = (bf16[128,640]{1,0:T(8,128)(2,1)S(1)}, bf16[128,640]{1,0:T(8,128)(2,1)S(1)}, u32[]{:S(2)}, u32[]{:S(2)}) collective-permute-start(bf16[128,640]{1,0:T(8,128)(2,1)S(1)} %get-tuple-element.77), channel_id=1, source_target_pairs={{0,8},{1,9},{2,10},{3,11},{4,12},{5,13},{6,14},{7,15},{8,0},{9,1},... | collective-permute-start | bytes 491528 | tf_op jit(solution)/shard_map/ppermute | solution.py:375
  29.0 2.3 %collective-permute-start.12 = (bf16[128,640]{1,0:T(8,128)(2,1)S(1)}, bf16[128,640]{1,0:T(8,128)(2,1)S(1)}, u32[]{:S(2)}, u32[]{:S(2)}) collective-permute-start(bf16[128,640]{1,0:T(8,128)(2,1)S(1)} %get-tuple-element.78), channel_id=1, source_target_pairs={{0,12},{1,13},{2,14},{3,15},{4,8},{5,9},{6,10},{7,11},{8,4},{9,5},... | collective-permute-start | bytes 491528 | tf_op jit(solution)/shard_map/ppermute | solution.py:375
  31.3 0.6 collective-permute-start.10
  31.9 0.1 pad_add_fusion.6.bins_ref
  32.0 0.1 slice.12.names_ref
  32.0 1.2 %shard_map.58.refs_4_ = f32[128,640]{1,0:T(8,128)S(1)} custom-call(s32[8]{0:T(128)S(1)} %pad_add_fusion.6.bins_ref, s32[4,128]{1,0:T(4,128)S(1)} %slice.12.names_ref, bf16[128,640]{1,0:T(8,128)(2,1)S(1)} %get-tuple-element.79.refs_0_, bf16[4,640,128]{2,1,0:T(8,128)(2,1)S(1)} %pad_maximum_fusion.refs_1_.refs_3_, ...), custom_call_target="tpu_custom_call" | custom-call | flops 1 | bytes 1 | tf_op jit(solution)/shard_map/pallas_call | solution.py:20
  33.2 9.3 %collective-permute-done.11.refs_1_.refs_2_ = bf16[128,640]{1,0:T(8,128)(2,1)S(1)} collective-permute-done((bf16[128,640]{1,0:T(8,128)(2,1)S(1)}, bf16[128,640]{1,0:T(8,128)(2,1)S(1)}, u32[]{:S(2)}, u32[]{:S(2)}) %collective-permute-start.11) | collective-permute-done | bytes 163872 | tf_op jit(solution)/shard_map/ppermute | solution.py:375
  42.5 1.8 %collective-permute-done.8.refs_6_ = bf16[4,640,128]{2,1,0:T(8,128)(2,1)S(1)} collective-permute-done((bf16[4,640,128]{2,1,0:T(8,128)(2,1)S(1)}, bf16[4,640,128]{2,1,0:T(8,128)(2,1)S(1)}, u32[]{:S(2)}, u32[]{:S(2)}) %collective-permute-start.8) | collective-permute-done | bytes 655392 | tf_op jit(solution)/shard_map/ppermute | solution.py:375
  44.3 0.1 pad_add_fusion.4.bins_ref
  44.4 1.8 %shard_map.59.refs_5_ = f32[384,640]{1,0:T(8,128)S(1)} custom-call(s32[8]{0:T(128)S(1)} %pad_add_fusion.6.bins_ref, s32[4,128]{1,0:T(4,128)S(1)} %slice.12.names_ref, bf16[128,640]{1,0:T(8,128)(2,1)S(1)} %collective-permute-done.10.refs_0_.refs_1_, bf16[128,640]{1,0:T(8,128)(2,1)S(1)} %collective-permute-done.11.refs_1_.refs_2_, ...), custom_call_target="tpu_custom_call" | custom-call | flops 1 | bytes 1 | tf_op jit(solution)/shard_map/pallas_call | solution.py:20
  46.2 0.2 collective-permute-done.13.refs_7_
  46.4 2.4 %shard_map.60 = (f32[512,640]{1,0:T(8,128)S(1)}, bf16[512,640]{1,0:T(8,128)(2,1)S(1)}, bf16[512,384]{1,0:T(8,128)(2,1)S(1)}, bf16[512,256]{1,0:T(8,128)(2,1)S(1)}, f32[4,128]{1,0:T(4,128)S(1)}) custom-call(s32[1]{0:T(128)} %bitcast.1.outer_ref, s32[8]{0:T(128)S(1)} %pad_add_fusion.4.bins_ref, s32[4,128]{1,0:T(4,128)S(1)} %slice.12.names_ref, ...), custom_call_target="tpu_custom_call" | custom-call | flops 1 | bytes 1 | tf_op jit(solution)/shard_map/pallas_call | solution.py:20
  48.8 1.6 %collective-permute-start.17 = (bf16[512,384]{1,0:T(8,128)(2,1)S(1)}, bf16[512,384]{1,0:T(8,128)(2,1)S(1)}, u32[]{:S(2)}, u32[]{:S(2)}) collective-permute-start(bf16[512,384]{1,0:T(8,128)(2,1)S(1)} %get-tuple-element.87), channel_id=1, source_target_pairs={{0,4},{1,5},{2,6},{3,7},{4,12},{5,13},{6,14},{7,15},{8,0},{9,1},{1... | collective-permute-start | bytes 1179656 | tf_op jit(solution)/shard_map/ppermute | solution.py:382
  50.4 2.6 %collective-permute-start.14 = (f32[4,128]{1,0:T(4,128)S(1)}, f32[4,128]{1,0:T(4,128)S(1)}, u32[]{:S(2)}, u32[]{:S(2)}) collective-permute-start(f32[4,128]{1,0:T(4,128)S(1)} %get-tuple-element.86), channel_id=1, source_target_pairs={{0,4},{1,5},{2,6},{3,7},{4,0},{5,1},{6,2},{7,3},{8,12},{9,13},{10,... | collective-permute-start | bytes 6152 | tf_op jit(solution)/shard_map/ppermute | solution.py:375
  53.0 0.4 collective-permute-start.15
  53.4 2.0 %collective-permute-start.16 = (f32[4,128]{1,0:T(4,128)S(1)}, f32[4,128]{1,0:T(4,128)S(1)}, u32[]{:S(2)}, u32[]{:S(2)}) collective-permute-start(f32[4,128]{1,0:T(4,128)S(1)} %get-tuple-element.86), channel_id=1, source_target_pairs={{0,12},{1,13},{2,14},{3,15},{4,8},{5,9},{6,10},{7,11},{8,4},{9,5},... | collective-permute-start | bytes 6152 | tf_op jit(solution)/shard_map/ppermute | solution.py:375
  55.4 1.1 %collective-permute-start.18 = (bf16[512,256]{1,0:T(8,128)(2,1)S(1)}, bf16[512,256]{1,0:T(8,128)(2,1)S(1)}, u32[]{:S(2)}, u32[]{:S(2)}) collective-permute-start(bf16[512,256]{1,0:T(8,128)(2,1)S(1)} %get-tuple-element.90), channel_id=1, source_target_pairs={{0,4},{1,5},{2,6},{3,7},{4,12},{5,13},{6,14},{7,15},{8,0},{9,1},{1... | collective-permute-start | bytes 786440 | tf_op jit(solution)/shard_map/ppermute | solution.py:382
  56.5 3.4 %collective-permute-done.14 = f32[4,128]{1,0:T(4,128)S(1)} collective-permute-done((f32[4,128]{1,0:T(4,128)S(1)}, f32[4,128]{1,0:T(4,128)S(1)}, u32[]{:S(2)}, u32[]{:S(2)}) %collective-permute-start.14) | collective-permute-done | bytes 2080 | tf_op jit(solution)/shard_map/ppermute | solution.py:375
  59.9 1.9 %collective-permute-done.15 = f32[4,128]{1,0:T(4,128)S(1)} collective-permute-done((f32[4,128]{1,0:T(4,128)S(1)}, f32[4,128]{1,0:T(4,128)S(1)}, u32[]{:S(2)}, u32[]{:S(2)}) %collective-permute-start.15) | collective-permute-done | bytes 2080 | tf_op jit(solution)/shard_map/ppermute | solution.py:375
  61.8 1.1 %collective-permute-done.16 = f32[4,128]{1,0:T(4,128)S(1)} collective-permute-done((f32[4,128]{1,0:T(4,128)S(1)}, f32[4,128]{1,0:T(4,128)S(1)}, u32[]{:S(2)}, u32[]{:S(2)}) %collective-permute-start.16) | collective-permute-done | bytes 2080 | tf_op jit(solution)/shard_map/ppermute | solution.py:375
  62.9 0.2 shard_map.61.refs_0_.refs_2_
  63.1 0.8 shard_map.62
  63.9 3.0 %collective-permute-done.18.refs_1_ = bf16[512,256]{1,0:T(8,128)(2,1)S(1)} collective-permute-done((bf16[512,256]{1,0:T(8,128)(2,1)S(1)}, bf16[512,256]{1,0:T(8,128)(2,1)S(1)}, u32[]{:S(2)}, u32[]{:S(2)}) %collective-permute-start.18) | collective-permute-done | bytes 262176 | tf_op jit(solution)/shard_map/ppermute | solution.py:382
  66.9 0.8 shard_map.63
  67.7 0.1 collective-permute-start.22
  67.8 0.8 collective-permute-start.19
  68.6 0.2 collective-permute-start.20
  68.8 0.7 collective-permute-done.22.got_ref
  69.5 0.1 shard_map.65
  69.6 0.8 shard_map.66
  70.5 0.2 collective-permute-start.23
  70.7 1.4 %collective-permute-start.25 = (bf16[1,160,640]{2,1,0:T(8,128)(2,1)S(1)}, bf16[1,160,640]{2,1,0:T(8,128)(2,1)S(1)}, u32[]{:S(2)}, u32[]{:S(2)}) collective-permute-start(bf16[1,160,640]{2,1,0:T(8,128)(2,1)S(1)} %get-tuple-element.105), channel_id=1, source_target_pairs={{0,2},{1,3},{2,0},{3,1},{4,6},{5,7},{6,4},{7,5},{8,10},{9,11},{10,... | collective-permute-start | bytes 614408 | tf_op jit(solution)/shard_map/ppermute | solution.py:375
  72.1 0.1 shard_map.64
  72.1 0.7 collective-permute-start.21
  72.8 0.1 shard_map.67
  72.9 1.5 %collective-permute-start.24 = (bf16[1,160,640]{2,1,0:T(8,128)(2,1)S(1)}, bf16[1,160,640]{2,1,0:T(8,128)(2,1)S(1)}, u32[]{:S(2)}, u32[]{:S(2)}) collective-permute-start(bf16[1,160,640]{2,1,0:T(8,128)(2,1)S(1)} %get-tuple-element.104), channel_id=1, source_target_pairs={{0,2},{1,3},{2,0},{3,1},{4,6},{5,7},{6,4},{7,5},{8,10},{9,11},{10,... | collective-permute-start | bytes 614408 | tf_op jit(solution)/shard_map/ppermute | solution.py:375
  74.4 4.2 %collective-permute-done.25 = bf16[1,160,640]{2,1,0:T(8,128)(2,1)S(1)} collective-permute-done((bf16[1,160,640]{2,1,0:T(8,128)(2,1)S(1)}, bf16[1,160,640]{2,1,0:T(8,128)(2,1)S(1)}, u32[]{:S(2)}, u32[]{:S(2)}) %collective-permute-start.25) | collective-permute-done | bytes 204832 | tf_op jit(solution)/shard_map/ppermute | solution.py:375
  78.6 4.4 %collective-permute-done.21 = bf16[1,160,640]{2,1,0:T(8,128)(2,1)S(1)} collective-permute-done((bf16[1,160,640]{2,1,0:T(8,128)(2,1)S(1)}, bf16[1,160,640]{2,1,0:T(8,128)(2,1)S(1)}, u32[]{:S(2)}, u32[]{:S(2)}) %collective-permute-start.21) | collective-permute-done | bytes 204832 | tf_op jit(solution)/shard_map/ppermute | solution.py:375
  83.0 2.9 %collective-permute-done.19.refs_1_ = bf16[512,640]{1,0:T(8,128)(2,1)S(1)} collective-permute-done((bf16[512,640]{1,0:T(8,128)(2,1)S(1)}, bf16[512,640]{1,0:T(8,128)(2,1)S(1)}, u32[]{:S(2)}, u32[]{:S(2)}) %collective-permute-start.19) | collective-permute-done | bytes 655392 | tf_op jit(solution)/shard_map/ppermute | solution.py:382
  85.8 0.9 collective-permute-done.24
  86.8 0.8 shard_map.68
  87.7 1.6 %collective-permute-start.28 = (bf16[160,640]{1,0:T(8,128)(2,1)S(1)}, bf16[160,640]{1,0:T(8,128)(2,1)S(1)}, u32[]{:S(2)}, u32[]{:S(2)}) collective-permute-start(bf16[160,640]{1,0:T(8,128)(2,1)S(1)} %fusion), channel_id=1, source_target_pairs={{0,8},{1,9},{2,10},{3,11},{4,0},{5,1},{6,2},{7,3},{8,12},{9,13},{1... | collective-permute-start | bytes 614408 | tf_op jit(solution)/shard_map/ppermute | solution.py:382
  89.4 0.1 shard_map.69
  89.5 1.5 %collective-permute-start.27 = (bf16[1,160,640]{2,1,0:T(8,128)(2,1)S(1)}, bf16[1,160,640]{2,1,0:T(8,128)(2,1)S(1)}, u32[]{:S(2)}, u32[]{:S(2)}) collective-permute-start(bf16[1,160,640]{2,1,0:T(8,128)(2,1)S(1)} %get-tuple-element.110), channel_id=1, source_target_pairs={{0,2},{1,3},{2,0},{3,1},{4,6},{5,7},{6,4},{7,5},{8,10},{9,11},{10,... | collective-permute-start | bytes 614408 | tf_op jit(solution)/shard_map/ppermute | solution.py:375
  91.0 1.5 %shard_map.70.refs_4_ = f32[160,2560]{1,0:T(8,128)} custom-call(s32[4]{0:T(128)S(1)} %shift-right-arithmetic_xor_fusion.at_ref, f32[160,640]{1,0:T(8,128)S(1)} %bitcast.39, bf16[160,640]{1,0:T(8,128)(2,1)S(1)} %bitcast.42, f32[160,640]{1,0:T(8,128)S(1)} %bitcast.40, bf16[160,640]{1,0:T(8,128)(2,1)S(1)} %bitcast.43), custom_call_target="tpu_custom_call" | custom-call | flops 1 | bytes 1 | tf_op jit(solution)/shard_map/pallas_call | solution.py:349
  92.5 3.7 %collective-permute-done.28.refs_2_ = bf16[160,640]{1,0:T(8,128)(2,1)S(1)} collective-permute-done((bf16[160,640]{1,0:T(8,128)(2,1)S(1)}, bf16[160,640]{1,0:T(8,128)(2,1)S(1)}, u32[]{:S(2)}, u32[]{:S(2)}) %collective-permute-start.28) | collective-permute-done | bytes 204832 | tf_op jit(solution)/shard_map/ppermute | solution.py:382
  96.2 0.5 collective-permute-done.27
  96.7 1.5 %shard_map.71 = f32[160,2560]{1,0:T(8,128)} custom-call(s32[4]{0:T(128)S(1)} %shift-right-arithmetic_xor_fusion.at_ref, f32[160,640]{1,0:T(8,128)S(1)} %bitcast.41, bf16[160,640]{1,0:T(8,128)(2,1)S(1)} %bitcast.44, bf16[160,640]{1,0:T(8,128)(2,1)S(1)} %collective-permute-done.28.refs_2_, ...), custom_call_target="tpu_custom_call", output_to_operand_aliasing={{}: (5, {})} | custom-call | flops 1 | bytes 1 | tf_op jit(solution)/shard_map/pallas_call | solution.py:349
  (34 shorter events, 0.4 us)
Async XLA Ops:
  0.0 15.4 %copy-start = (bf16[128,3968]{1,0:T(8,128)(2,1)S(1)}, bf16[128,3968]{1,0:T(8,128)(2,1)}, u32[]{:S(2)}) copy-start(bf16[128,3968]{1,0:T(8,128)(2,1)} %flux_ref) | copy-start | bytes 3047428
  0.8 11.3 %collective-permute-start = (s32[148]{0:T(256)S(1)}, s32[148]{0:T(256)S(1)}, u32[]{:S(2)}, u32[]{:S(2)}) collective-permute-start(s32[148]{0:T(256)S(1)} %pad_add_fusion.3), channel_id=1, source_target_pairs={{0,4},{1,5},{2,6},{3,7},{4,0},{5,1},{6,2},{7,3},{8,12},{9,13},{10,... | collective-permute-start | bytes 1784 | tf_op jit(solution)/shard_map/ppermute | solution.py:375
  3.9 8.3 %collective-permute-start.1 = (s32[148]{0:T(256)S(1)}, s32[148]{0:T(256)S(1)}, u32[]{:S(2)}, u32[]{:S(2)}) collective-permute-start(s32[148]{0:T(256)S(1)} %pad_add_fusion.3), channel_id=1, source_target_pairs={{0,8},{1,9},{2,10},{3,11},{4,12},{5,13},{6,14},{7,15},{8,0},{9,1},... | collective-permute-start | bytes 1784 | tf_op jit(solution)/shard_map/ppermute | solution.py:375
  6.4 5.7 %collective-permute-start.2 = (s32[148]{0:T(256)S(1)}, s32[148]{0:T(256)S(1)}, u32[]{:S(2)}, u32[]{:S(2)}) collective-permute-start(s32[148]{0:T(256)S(1)} %pad_add_fusion.3), channel_id=1, source_target_pairs={{0,12},{1,13},{2,14},{3,15},{4,8},{5,9},{6,10},{7,11},{8,4},{9,5},... | collective-permute-start | bytes 1784 | tf_op jit(solution)/shard_map/ppermute | solution.py:375
  7.7 19.3 %collective-permute-start.3 = (bf16[640,128]{1,0:T(8,128)(2,1)S(1)}, bf16[640,128]{1,0:T(8,128)(2,1)S(1)}, u32[]{:S(2)}, u32[]{:S(2)}) collective-permute-start(bf16[640,128]{1,0:T(8,128)(2,1)S(1)} %get-tuple-element.119), channel_id=1, source_target_pairs={{0,4},{1,5},{2,6},{3,7},{4,0},{5,1},{6,2},{7,3},{8,12},{9,13},{10,... | collective-permute-start | bytes 491528 | tf_op jit(solution)/shard_map/ppermute | solution.py:375
  8.6 18.3 %collective-permute-start.4 = (bf16[640,128]{1,0:T(8,128)(2,1)S(1)}, bf16[640,128]{1,0:T(8,128)(2,1)S(1)}, u32[]{:S(2)}, u32[]{:S(2)}) collective-permute-start(bf16[640,128]{1,0:T(8,128)(2,1)S(1)} %get-tuple-element.118), channel_id=1, source_target_pairs={{0,8},{1,9},{2,10},{3,11},{4,12},{5,13},{6,14},{7,15},{8,0},{9,1},... | collective-permute-start | bytes 491528 | tf_op jit(solution)/shard_map/ppermute | solution.py:375
  12.1 14.9 %collective-permute-start.5 = (bf16[640,128]{1,0:T(8,128)(2,1)S(1)}, bf16[640,128]{1,0:T(8,128)(2,1)S(1)}, u32[]{:S(2)}, u32[]{:S(2)}) collective-permute-start(bf16[640,128]{1,0:T(8,128)(2,1)S(1)} %get-tuple-element.117), channel_id=1, source_target_pairs={{0,12},{1,13},{2,14},{3,15},{4,8},{5,9},{6,10},{7,11},{8,4},{9,5},... | collective-permute-start | bytes 491528 | tf_op jit(solution)/shard_map/ppermute | solution.py:375
  12.2 1.2 %collective-permute-start.6 = (s32[4,1,20]{2,0,1:T(4,128)S(1)}, s32[4,1,20]{2,0,1:T(4,128)S(1)}, u32[]{:S(2)}, u32[]{:S(2)}) collective-permute-start(s32[4,1,20]{2,0,1:T(4,128)S(1)} %slice_bitcast_fusion), channel_id=1, source_target_pairs={{0,1},{1,0},{2,3},{3,2},{4,5},{5,4},{6,7},{7,6},{8,9},{9,8},{10,11... | collective-permute-start | bytes 968 | tf_op jit(solution)/shard_map/ppermute | solution.py:375
  13.4 8.8 %collective-permute-start.7 = (s32[4,2,20]{2,0,1:T(4,128)S(1)}, s32[4,2,20]{2,0,1:T(4,128)S(1)}, u32[]{:S(2)}, u32[]{:S(2)}) collective-permute-start(s32[4,2,20]{2,0,1:T(4,128)S(1)} %pad_add_fusion.2), channel_id=1, source_target_pairs={{0,2},{1,3},{2,0},{3,1},{4,6},{5,7},{6,4},{7,5},{8,10},{9,11},{10,... | collective-permute-start | bytes 1928 | tf_op jit(solution)/shard_map/ppermute | solution.py:375
  27.1 4.3 %collective-permute-start.9 = (bf16[4,640,128]{2,1,0:T(8,128)(2,1)S(1)}, bf16[4,640,128]{2,1,0:T(8,128)(2,1)S(1)}, u32[]{:S(2)}, u32[]{:S(2)}) collective-permute-start(bf16[4,640,128]{2,1,0:T(8,128)(2,1)S(1)} %pad_maximum_fusion.refs_1_.refs_3_), channel_id=1, source_target_pairs={{0,1},{1,0},{2,3},{3,2},{4,5},{5,4},{6,7},{7,6},{8,9},{9,8},{10,11... | collective-permute-start | bytes 1966088 | tf_op jit(solution)/shard_map/ppermute | solution.py:375
  27.1 17.1 %collective-permute-start.8 = (bf16[4,640,128]{2,1,0:T(8,128)(2,1)S(1)}, bf16[4,640,128]{2,1,0:T(8,128)(2,1)S(1)}, u32[]{:S(2)}, u32[]{:S(2)}) collective-permute-start(bf16[4,640,128]{2,1,0:T(8,128)(2,1)S(1)} %pad_maximum_fusion.refs_1_.refs_3_), channel_id=1, source_target_pairs={{0,2},{1,3},{2,0},{3,1},{4,6},{5,7},{6,4},{7,5},{8,10},{9,11},{10,... | collective-permute-start | bytes 1966088 | tf_op jit(solution)/shard_map/ppermute | solution.py:375
  27.5 15.0 %collective-permute-start.11 = (bf16[128,640]{1,0:T(8,128)(2,1)S(1)}, bf16[128,640]{1,0:T(8,128)(2,1)S(1)}, u32[]{:S(2)}, u32[]{:S(2)}) collective-permute-start(bf16[128,640]{1,0:T(8,128)(2,1)S(1)} %get-tuple-element.77), channel_id=1, source_target_pairs={{0,8},{1,9},{2,10},{3,11},{4,12},{5,13},{6,14},{7,15},{8,0},{9,1},... | collective-permute-start | bytes 491528 | tf_op jit(solution)/shard_map/ppermute | solution.py:375
  29.0 13.5 %collective-permute-start.12 = (bf16[128,640]{1,0:T(8,128)(2,1)S(1)}, bf16[128,640]{1,0:T(8,128)(2,1)S(1)}, u32[]{:S(2)}, u32[]{:S(2)}) collective-permute-start(bf16[128,640]{1,0:T(8,128)(2,1)S(1)} %get-tuple-element.78), channel_id=1, source_target_pairs={{0,12},{1,13},{2,14},{3,15},{4,8},{5,9},{6,10},{7,11},{8,4},{9,5},... | collective-permute-start | bytes 491528 | tf_op jit(solution)/shard_map/ppermute | solution.py:375
  31.3 13.0 %collective-permute-start.10 = (bf16[128,640]{1,0:T(8,128)(2,1)S(1)}, bf16[128,640]{1,0:T(8,128)(2,1)S(1)}, u32[]{:S(2)}, u32[]{:S(2)}) collective-permute-start(bf16[128,640]{1,0:T(8,128)(2,1)S(1)} %get-tuple-element.76), channel_id=1, source_target_pairs={{0,4},{1,5},{2,6},{3,7},{4,0},{5,1},{6,2},{7,3},{8,12},{9,13},{10,... | collective-permute-start | bytes 491528 | tf_op jit(solution)/shard_map/ppermute | solution.py:375
  44.3 2.1 %collective-permute-start.13 = (bf16[4,640,128]{2,1,0:T(8,128)(2,1)S(1)}, bf16[4,640,128]{2,1,0:T(8,128)(2,1)S(1)}, u32[]{:S(2)}, u32[]{:S(2)}) collective-permute-start(bf16[4,640,128]{2,1,0:T(8,128)(2,1)S(1)} %collective-permute-done.8.refs_6_), channel_id=1, source_target_pairs={{0,1},{1,0},{2,3},{3,2},{4,5},{5,4},{6,7},{7,6},{8,9},{9,8},{10,11... | collective-permute-start | bytes 1966088 | tf_op jit(solution)/shard_map/ppermute | solution.py:375
  48.8 14.1 %collective-permute-start.17 = (bf16[512,384]{1,0:T(8,128)(2,1)S(1)}, bf16[512,384]{1,0:T(8,128)(2,1)S(1)}, u32[]{:S(2)}, u32[]{:S(2)}) collective-permute-start(bf16[512,384]{1,0:T(8,128)(2,1)S(1)} %get-tuple-element.87), channel_id=1, source_target_pairs={{0,4},{1,5},{2,6},{3,7},{4,12},{5,13},{6,14},{7,15},{8,0},{9,1},{1... | collective-permute-start | bytes 1179656 | tf_op jit(solution)/shard_map/ppermute | solution.py:382
  50.4 9.5 %collective-permute-start.14 = (f32[4,128]{1,0:T(4,128)S(1)}, f32[4,128]{1,0:T(4,128)S(1)}, u32[]{:S(2)}, u32[]{:S(2)}) collective-permute-start(f32[4,128]{1,0:T(4,128)S(1)} %get-tuple-element.86), channel_id=1, source_target_pairs={{0,4},{1,5},{2,6},{3,7},{4,0},{5,1},{6,2},{7,3},{8,12},{9,13},{10,... | collective-permute-start | bytes 6152 | tf_op jit(solution)/shard_map/ppermute | solution.py:375
  53.0 8.8 %collective-permute-start.15 = (f32[4,128]{1,0:T(4,128)S(1)}, f32[4,128]{1,0:T(4,128)S(1)}, u32[]{:S(2)}, u32[]{:S(2)}) collective-permute-start(f32[4,128]{1,0:T(4,128)S(1)} %get-tuple-element.86), channel_id=1, source_target_pairs={{0,8},{1,9},{2,10},{3,11},{4,12},{5,13},{6,14},{7,15},{8,0},{9,1},... | collective-permute-start | bytes 6152 | tf_op jit(solution)/shard_map/ppermute | solution.py:375
  53.4 9.5 %collective-permute-start.16 = (f32[4,128]{1,0:T(4,128)S(1)}, f32[4,128]{1,0:T(4,128)S(1)}, u32[]{:S(2)}, u32[]{:S(2)}) collective-permute-start(f32[4,128]{1,0:T(4,128)S(1)} %get-tuple-element.86), channel_id=1, source_target_pairs={{0,12},{1,13},{2,14},{3,15},{4,8},{5,9},{6,10},{7,11},{8,4},{9,5},... | collective-permute-start | bytes 6152 | tf_op jit(solution)/shard_map/ppermute | solution.py:375
  55.4 11.5 %collective-permute-start.18 = (bf16[512,256]{1,0:T(8,128)(2,1)S(1)}, bf16[512,256]{1,0:T(8,128)(2,1)S(1)}, u32[]{:S(2)}, u32[]{:S(2)}) collective-permute-start(bf16[512,256]{1,0:T(8,128)(2,1)S(1)} %get-tuple-element.90), channel_id=1, source_target_pairs={{0,4},{1,5},{2,6},{3,7},{4,12},{5,13},{6,14},{7,15},{8,0},{9,1},{1... | collective-permute-start | bytes 786440 | tf_op jit(solution)/shard_map/ppermute | solution.py:382
  67.7 1.8 %collective-permute-start.22 = (bf16[2,160,640]{2,1,0:T(8,128)(2,1)S(1)}, bf16[2,160,640]{2,1,0:T(8,128)(2,1)S(1)}, u32[]{:S(2)}, u32[]{:S(2)}) collective-permute-start(bf16[2,160,640]{2,1,0:T(8,128)(2,1)S(1)} %get-tuple-element.99), channel_id=1, source_target_pairs={{0,1},{1,0},{2,3},{3,2},{4,5},{5,4},{6,7},{7,6},{8,9},{9,8},{10,11... | collective-permute-start | bytes 1228808 | tf_op jit(solution)/shard_map/ppermute | solution.py:375
  67.8 18.0 %collective-permute-start.19 = (bf16[512,640]{1,0:T(8,128)(2,1)S(1)}, bf16[512,640]{1,0:T(8,128)(2,1)S(1)}, u32[]{:S(2)}, u32[]{:S(2)}) collective-permute-start(bf16[512,640]{1,0:T(8,128)(2,1)S(1)} %get-tuple-element.101.refs_1_), channel_id=1, source_target_pairs={{0,4},{1,5},{2,6},{3,7},{4,12},{5,13},{6,14},{7,15},{8,0},{9,1},{1... | collective-permute-start | bytes 1966088 | tf_op jit(solution)/shard_map/ppermute | solution.py:382
  68.6 3.4 %collective-permute-start.20 = (bf16[2,160,640]{2,1,0:T(8,128)(2,1)S(1)}, bf16[2,160,640]{2,1,0:T(8,128)(2,1)S(1)}, u32[]{:S(2)}, u32[]{:S(2)}) collective-permute-start(bf16[2,160,640]{2,1,0:T(8,128)(2,1)S(1)} %get-tuple-element.96), channel_id=1, source_target_pairs={{0,1},{1,0},{2,3},{3,2},{4,5},{5,4},{6,7},{7,6},{8,9},{9,8},{10,11... | collective-permute-start | bytes 1228808 | tf_op jit(solution)/shard_map/ppermute | solution.py:375
  70.5 2.4 %collective-permute-start.23 = (bf16[2,160,640]{2,1,0:T(8,128)(2,1)S(1)}, bf16[2,160,640]{2,1,0:T(8,128)(2,1)S(1)}, u32[]{:S(2)}, u32[]{:S(2)}) collective-permute-start(bf16[2,160,640]{2,1,0:T(8,128)(2,1)S(1)} %get-tuple-element.103), channel_id=1, source_target_pairs={{0,1},{1,0},{2,3},{3,2},{4,5},{5,4},{6,7},{7,6},{8,9},{9,8},{10,11... | collective-permute-start | bytes 1228808 | tf_op jit(solution)/shard_map/ppermute | solution.py:375
  70.7 7.9 %collective-permute-start.25 = (bf16[1,160,640]{2,1,0:T(8,128)(2,1)S(1)}, bf16[1,160,640]{2,1,0:T(8,128)(2,1)S(1)}, u32[]{:S(2)}, u32[]{:S(2)}) collective-permute-start(bf16[1,160,640]{2,1,0:T(8,128)(2,1)S(1)} %get-tuple-element.105), channel_id=1, source_target_pairs={{0,2},{1,3},{2,0},{3,1},{4,6},{5,7},{6,4},{7,5},{8,10},{9,11},{10,... | collective-permute-start | bytes 614408 | tf_op jit(solution)/shard_map/ppermute | solution.py:375
  72.1 10.8 %collective-permute-start.21 = (bf16[1,160,640]{2,1,0:T(8,128)(2,1)S(1)}, bf16[1,160,640]{2,1,0:T(8,128)(2,1)S(1)}, u32[]{:S(2)}, u32[]{:S(2)}) collective-permute-start(bf16[1,160,640]{2,1,0:T(8,128)(2,1)S(1)} %get-tuple-element.97), channel_id=1, source_target_pairs={{0,2},{1,3},{2,0},{3,1},{4,6},{5,7},{6,4},{7,5},{8,10},{9,11},{10,... | collective-permute-start | bytes 614408 | tf_op jit(solution)/shard_map/ppermute | solution.py:375
  72.9 13.9 %collective-permute-start.24 = (bf16[1,160,640]{2,1,0:T(8,128)(2,1)S(1)}, bf16[1,160,640]{2,1,0:T(8,128)(2,1)S(1)}, u32[]{:S(2)}, u32[]{:S(2)}) collective-permute-start(bf16[1,160,640]{2,1,0:T(8,128)(2,1)S(1)} %get-tuple-element.104), channel_id=1, source_target_pairs={{0,2},{1,3},{2,0},{3,1},{4,6},{5,7},{6,4},{7,5},{8,10},{9,11},{10,... | collective-permute-start | bytes 614408 | tf_op jit(solution)/shard_map/ppermute | solution.py:375
  87.6 1.8 %collective-permute-start.26 = (bf16[2,160,640]{2,1,0:T(8,128)(2,1)S(1)}, bf16[2,160,640]{2,1,0:T(8,128)(2,1)S(1)}, u32[]{:S(2)}, u32[]{:S(2)}) collective-permute-start(bf16[2,160,640]{2,1,0:T(8,128)(2,1)S(1)} %get-tuple-element.108), channel_id=1, source_target_pairs={{0,1},{1,0},{2,3},{3,2},{4,5},{5,4},{6,7},{7,6},{8,9},{9,8},{10,11... | collective-permute-start | bytes 1228808 | tf_op jit(solution)/shard_map/ppermute | solution.py:375
  87.7 8.4 %collective-permute-start.28 = (bf16[160,640]{1,0:T(8,128)(2,1)S(1)}, bf16[160,640]{1,0:T(8,128)(2,1)S(1)}, u32[]{:S(2)}, u32[]{:S(2)}) collective-permute-start(bf16[160,640]{1,0:T(8,128)(2,1)S(1)} %fusion), channel_id=1, source_target_pairs={{0,8},{1,9},{2,10},{3,11},{4,0},{5,1},{6,2},{7,3},{8,12},{9,13},{1... | collective-permute-start | bytes 614408 | tf_op jit(solution)/shard_map/ppermute | solution.py:382
  89.5 7.2 %collective-permute-start.27 = (bf16[1,160,640]{2,1,0:T(8,128)(2,1)S(1)}, bf16[1,160,640]{2,1,0:T(8,128)(2,1)S(1)}, u32[]{:S(2)}, u32[]{:S(2)}) collective-permute-start(bf16[1,160,640]{2,1,0:T(8,128)(2,1)S(1)} %get-tuple-element.110), channel_id=1, source_target_pairs={{0,2},{1,3},{2,0},{3,1},{4,6},{5,7},{6,4},{7,5},{8,10},{9,11},{10,... | collective-permute-start | bytes 614408 | tf_op jit(solution)/shard_map/ppermute | solution.py:375

commit v16 on v15

--- a/solution.py
+++ b/solution.py
@@ -54,7 +54,7 @@
     edge = jnp.zeros((tall, reach), F32)
     padded[:, :reach] = edge
     padded[:, reach + nobs :] = edge
-    step = 512
+    step = 1024
 
     def one_tile(tile, carry):
         own = own_rows(tile)
@@ -279,23 +279,29 @@
 
 
 def product_kernel(ntall, q_ref, *refs):
-    talls, wide_ref, (send_ref, keep_ref, *joined_ref, value) = refs[:ntall], refs[ntall], refs[ntall + 1 :]
+    talls, wide_ref, (send_ref, keep_ref, *joined_ref) = refs[:ntall], refs[ntall], refs[ntall + 1 :]
     pairs, share, _ = keep_ref.shape
-    row = 0
+    column = 0
+    parts = []
     for tall in talls:
-        rows = slice(row, row + tall.shape[1])
-        value[rows, :] = lax.dot_general(
-            tall[...], wide_ref[...], (((0,), (0,)), ((), ())), preferred_element_type=F32
+        parts.append(
+            lax.dot_general(tall[...], wide_ref[...], (((0,), (0,)), ((), ())), preferred_element_type=F32)
         )
         if joined_ref:
-            joined_ref[0][:, rows] = tall[...]
-        row += tall.shape[1]
-    for e in range(2 * pairs):
-        own = value[pl.ds(pl.multiple_of((q_ref[0] ^ e) * share, 8), share), :]
-        if e % 2:
-            send_ref[e // 2] = own.astype(BF16)
-        else:
-            keep_ref[e // 2] = own
+            joined_ref[0][:, column : column + tall.shape[1]] = tall[...]
+        column += tall.shape[1]
+    value = jnp.concatenate(parts, axis=0) if ntall > 1 else parts[0]
+    for i in range(2 * pairs):
+        rows = value[i * share : (i + 1) * share, :]
+        e = q_ref[0] ^ i
+
+        @pl.when(e % 2 == 1)
+        def _(rows=rows, e=e):
+            send_ref[e // 2] = rows.astype(BF16)
+
+        @pl.when(e % 2 == 0)
+        def _(rows=rows, e=e):
+            keep_ref[e // 2] = rows
 
 
 def product(q, talls, wide, inner, join=False):
@@ -308,7 +314,6 @@
         (jax.ShapeDtypeStruct(shape, BF16), jax.ShapeDtypeStruct(shape, F32), *joined),
         [SMEM] + [VMEM] * (len(talls) + 1),
         (q, *talls, wide),
-        [pltpu.VMEM((rows, columns), F32)],
     )
 
 
@@ -383,11 +388,12 @@
             array, "spec", [(o * inner + i, to[o] * inner + i) for o in range(OUTER) for i in range(inner)]
         )
 
-    table = lax.optimization_barrier(jnp.concatenate([band_offset[0], destination[:, 0]]))
-    targets = table[nblocks:]
+    own = lax.optimization_barrier(jnp.concatenate([band_offset[0], destination[:, 0]]))
+    targets = own[nblocks:]
+    table = jnp.concatenate([own[:nblocks], swap(own[:nblocks], 1), targets])
     tables = jnp.stack([table] + [swap(table, away * inner) for away in range(1, OUTER)])
-    names, offsets = tables[:, nblocks:], tables[:, None, :nblocks]
-    bit = 1
+    names, offsets = tables[:, 2 * nblocks :], tables[:, : 2 * nblocks].reshape(OUTER, 2, nblocks)
+    bit = 2
     while bit < inner:
         if 2 * bit == inner:
             offsets, flux = lax.optimization_barrier((offsets, flux))

time: 98.4 us -> 99.9 us (1.015)
  waiting for transfers between devices: 39.1 us -> 41.5 us
  starting transfers between devices: 32.4 us -> 31.2 us
    ppermute x25, waiting for transfers between devices: 29.6 us -> 32.6 us  [swap(): return lax.ppermute(array, 'spec', [(i, i ^ bit) for i in range(n)])]
    ppermute x25, starting transfers between devices: 27.3 us -> 26.2 us  [swap(): return lax.ppermute(array, 'spec', [(i, i ^ bit) for i in range(n)])]
  transfers between devices with their start and end apart: 29 -> 29, of which waited for: 15 -> 15; matrix products, arithmetic and copies ran while one was open for 2% -> 2% of each run, Pallas kernels for 19% -> 18%
where the time goes in v16:
time: 99.9 us; the launch traced here: 99.7 us
  waiting for transfers between devices  41.5 us (42%)
  starting transfers between devices  31.2 us (31%)
  Pallas kernels  23.9 us (24%)
  local copies, waits for them, and re-layouts  1.45 us (1%)
  other arithmetic  1.34 us (1%)
    ppermute x25, waiting for transfers between devices, swap(): return lax.ppermute(array, 'spec', [(i, i ^ bit) for i in range(n)])  32.6 us
    ppermute x25, starting transfers between devices, swap(): return lax.ppermute(array, 'spec', [(i, i ^ bit) for i in range(n)])  26.2 us
    pallas_call x15, Pallas kernels, call(): pl.pallas_call(kernel, out_shape=out_shape, in_specs=in_specs, out_specs=...  20.9 us
    ppermute x4, waiting for transfers between devices, step(): lax.ppermute(array, 'spec', [(o * inner + i, to[o] * inner + i) for o in...  8.89 us
    ppermute x4, starting transfers between devices, step(): lax.ppermute(array, 'spec', [(o * inner + i, to[o] * inner + i) for o in...  5.07 us
    pallas_call x2, Pallas kernels, place(): pl.pallas_call(functools.partial(place_kernel, slots, last), out_shape=ja...  2.98 us
  transfers between devices with their start and end apart: 29, of which 15 were waited for; matrix products, arithmetic and copies ran while one was open for 2% of the time, Pallas kernels for 18%

profile of v16, /device:TPU:0, one launch (start us, length us, event | category | flops | bytes accessed | tf_op | source)
XLA Modules:
  0.0 99.7 jit_solution(7160977875061976200)
XLA Ops:
  0.0 0.8 pad_add_fusion.2
  0.8 0.5 collective-permute-start
  1.3 0.1 slice_bitcast_fusion
  1.4 0.7 collective-permute-done
  2.1 0.1 pad_add_fusion.3
  2.2 2.9 %collective-permute-start.1 = (s32[168]{0:T(256)S(1)}, s32[168]{0:T(256)S(1)}, u32[]{:S(2)}, u32[]{:S(2)}) collective-permute-start(s32[168]{0:T(256)S(1)} %pad_add_fusion.3), channel_id=1, source_target_pairs={{0,4},{1,5},{2,6},{3,7},{4,0},{5,1},{6,2},{7,3},{8,12},{9,13},{10,... | collective-permute-start | bytes 2024 | tf_op jit(solution)/shard_map/ppermute | solution.py:380
  5.1 2.6 %collective-permute-start.2 = (s32[168]{0:T(256)S(1)}, s32[168]{0:T(256)S(1)}, u32[]{:S(2)}, u32[]{:S(2)}) collective-permute-start(s32[168]{0:T(256)S(1)} %pad_add_fusion.3), channel_id=1, source_target_pairs={{0,8},{1,9},{2,10},{3,11},{4,12},{5,13},{6,14},{7,15},{8,0},{9,1},... | collective-permute-start | bytes 2024 | tf_op jit(solution)/shard_map/ppermute | solution.py:380
  7.7 1.2 %dynamic-slice_bitcast_fusion = (bf16[640,128]{1,0:T(8,128)(2,1)S(1)}, bf16[640,128]{1,0:T(8,128)(2,1)S(1)}, bf16[640,128]{1,0:T(8,128)(2,1)S(1)}, bf16[640,128]{1,0:T(8,128)(2,1)S(1)}) fusion(bf16[4,640,128]{2,1,0:T(8,128)(2,1)} %bitcast.45, s32[]{:T(128)S(6)} %select_n.41, s32[]{:T(128)S(6)} %select_n.40, s32[]{:T(128)S(6)} %select_n.39, s32[]{:T(128)S(6)} %select_n.38), kind=kLoop, calls=%fused_computation.3 | loop fusion | bytes 1310736 | tf_op jit(solution)/shard_map/jit(dynamic_index_in_dim)/squeeze | solution.py:407
  8.9 1.0 collective-permute-start.4
  9.8 3.5 %collective-permute-start.5 = (bf16[640,128]{1,0:T(8,128)(2,1)S(1)}, bf16[640,128]{1,0:T(8,128)(2,1)S(1)}, u32[]{:S(2)}, u32[]{:S(2)}) collective-permute-start(bf16[640,128]{1,0:T(8,128)(2,1)S(1)} %get-tuple-element.118), channel_id=1, source_target_pairs={{0,8},{1,9},{2,10},{3,11},{4,12},{5,13},{6,14},{7,15},{8,0},{9,1},... | collective-permute-start | bytes 491528 | tf_op jit(solution)/shard_map/ppermute | solution.py:380
  13.4 0.1 reshape.18
  13.4 1.7 %collective-permute-start.7 = (s32[4,2,20]{2,1,0:T(2,128)S(1)}, s32[4,2,20]{2,1,0:T(2,128)S(1)}, u32[]{:S(2)}, u32[]{:S(2)}) collective-permute-start(s32[4,2,20]{2,1,0:T(2,128)S(1)} %reshape.18), channel_id=1, source_target_pairs={{0,2},{1,3},{2,0},{3,1},{4,6},{5,7},{6,4},{7,5},{8,10},{9,11},{10,... | collective-permute-start | bytes 1928 | tf_op jit(solution)/shard_map/ppermute | solution.py:380
  15.2 0.1 pad_add_fusion.5.me_ref
  15.2 0.2 shard_map.55
  15.5 6.6 %shard_map.56.smoothed_ref = bf16[128,3968]{1,0:T(8,128)(2,1)S(1)} custom-call(bf16[128,3968]{1,0:T(8,128)(2,1)S(1)} %copy-done, bf16[11,128,3968]{2,1,0:T(8,128)(2,1)} %bitcast.43), custom_call_target="tpu_custom_call" | custom-call | flops 1 | bytes 1 | tf_op jit(solution)/shard_map/pallas_call | solution.py:20
  22.2 4.7 %shard_map.57 = (bf16[128,640]{1,0:T(8,128)(2,1)S(1)}, bf16[128,640]{1,0:T(8,128)(2,1)S(1)}, bf16[128,640]{1,0:T(8,128)(2,1)S(1)}, bf16[128,640]{1,0:T(8,128)(2,1)S(1)}) custom-call(s32[2]{0:T(128)S(1)} %pad_add_fusion.5.me_ref, s32[2,128]{1,0:T(2,128)S(1)} %get-tuple-element.61.groups_ref, s32[16,20]{1,0:T(8,128)S(1)} %get-tuple-element.122.starts_ref, ...), custom_call_target="tpu_custom_call" | custom-call | flops 1 | bytes 1 | tf_op jit(solution)/shard_map/pallas_call | solution.py:20
  26.9 0.1 pad_maximum_fusion.refs_1_.refs_3_
  27.0 0.1 collective-permute-start.9
  27.1 0.4 collective-permute-start.8
  27.4 3.2 %collective-permute-start.11 = (bf16[128,640]{1,0:T(8,128)(2,1)S(1)}, bf16[128,640]{1,0:T(8,128)(2,1)S(1)}, u32[]{:S(2)}, u32[]{:S(2)}) collective-permute-start(bf16[128,640]{1,0:T(8,128)(2,1)S(1)} %get-tuple-element.77), channel_id=1, source_target_pairs={{0,8},{1,9},{2,10},{3,11},{4,12},{5,13},{6,14},{7,15},{8,0},{9,1},... | collective-permute-start | bytes 491528 | tf_op jit(solution)/shard_map/ppermute | solution.py:380
  30.6 1.4 %collective-permute-start.12 = (bf16[128,640]{1,0:T(8,128)(2,1)S(1)}, bf16[128,640]{1,0:T(8,128)(2,1)S(1)}, u32[]{:S(2)}, u32[]{:S(2)}) collective-permute-start(bf16[128,640]{1,0:T(8,128)(2,1)S(1)} %get-tuple-element.78), channel_id=1, source_target_pairs={{0,12},{1,13},{2,14},{3,15},{4,8},{5,9},{6,10},{7,11},{8,4},{9,5},... | collective-permute-start | bytes 491528 | tf_op jit(solution)/shard_map/ppermute | solution.py:380
  32.0 0.1 pad_add_fusion.6.bins_ref
  32.1 0.1 slice.17.names_ref
  32.2 1.2 %shard_map.58.refs_4_ = f32[128,640]{1,0:T(8,128)S(1)} custom-call(s32[8]{0:T(128)S(1)} %pad_add_fusion.6.bins_ref, s32[4,128]{1,0:T(4,128)S(1)} %slice.17.names_ref, bf16[128,640]{1,0:T(8,128)(2,1)S(1)} %get-tuple-element.79.refs_0_, bf16[4,640,128]{2,1,0:T(8,128)(2,1)S(1)} %pad_maximum_fusion.refs_1_.refs_3_, ...), custom_call_target="tpu_custom_call" | custom-call | flops 1 | bytes 1 | tf_op jit(solution)/shard_map/pallas_call | solution.py:20
  33.3 9.3 %collective-permute-done.11.refs_1_.refs_2_ = bf16[128,640]{1,0:T(8,128)(2,1)S(1)} collective-permute-done((bf16[128,640]{1,0:T(8,128)(2,1)S(1)}, bf16[128,640]{1,0:T(8,128)(2,1)S(1)}, u32[]{:S(2)}, u32[]{:S(2)}) %collective-permute-start.11) | collective-permute-done | bytes 163872 | tf_op jit(solution)/shard_map/ppermute | solution.py:380
  42.7 1.5 %collective-permute-done.8.refs_6_ = bf16[4,640,128]{2,1,0:T(8,128)(2,1)S(1)} collective-permute-done((bf16[4,640,128]{2,1,0:T(8,128)(2,1)S(1)}, bf16[4,640,128]{2,1,0:T(8,128)(2,1)S(1)}, u32[]{:S(2)}, u32[]{:S(2)}) %collective-permute-start.8) | collective-permute-done | bytes 655392 | tf_op jit(solution)/shard_map/ppermute | solution.py:380
  44.2 0.1 pad_add_fusion.4.bins_ref
  44.3 1.8 %shard_map.59.refs_5_ = f32[384,640]{1,0:T(8,128)S(1)} custom-call(s32[8]{0:T(128)S(1)} %pad_add_fusion.6.bins_ref, s32[4,128]{1,0:T(4,128)S(1)} %slice.17.names_ref, bf16[128,640]{1,0:T(8,128)(2,1)S(1)} %collective-permute-done.10.refs_0_.refs_1_, bf16[128,640]{1,0:T(8,128)(2,1)S(1)} %collective-permute-done.11.refs_1_.refs_2_, ...), custom_call_target="tpu_custom_call" | custom-call | flops 1 | bytes 1 | tf_op jit(solution)/shard_map/pallas_call | solution.py:20
  46.1 0.2 collective-permute-done.13.refs_7_
  46.3 2.4 %shard_map.60 = (f32[512,640]{1,0:T(8,128)S(1)}, bf16[512,640]{1,0:T(8,128)(2,1)S(1)}, bf16[512,384]{1,0:T(8,128)(2,1)S(1)}, bf16[512,256]{1,0:T(8,128)(2,1)S(1)}, f32[4,128]{1,0:T(4,128)S(1)}) custom-call(s32[1]{0:T(128)} %bitcast.1.outer_ref, s32[8]{0:T(128)S(1)} %pad_add_fusion.4.bins_ref, s32[4,128]{1,0:T(4,128)S(1)} %slice.17.names_ref, ...), custom_call_target="tpu_custom_call" | custom-call | flops 1 | bytes 1 | tf_op jit(solution)/shard_map/pallas_call | solution.py:20
  48.7 2.1 %collective-permute-start.17 = (bf16[512,384]{1,0:T(8,128)(2,1)S(1)}, bf16[512,384]{1,0:T(8,128)(2,1)S(1)}, u32[]{:S(2)}, u32[]{:S(2)}) collective-permute-start(bf16[512,384]{1,0:T(8,128)(2,1)S(1)} %get-tuple-element.87), channel_id=1, source_target_pairs={{0,4},{1,5},{2,6},{3,7},{4,12},{5,13},{6,14},{7,15},{8,0},{9,1},{1... | collective-permute-start | bytes 1179656 | tf_op jit(solution)/shard_map/ppermute | solution.py:387
  50.9 2.1 %collective-permute-start.14 = (f32[4,128]{1,0:T(4,128)S(1)}, f32[4,128]{1,0:T(4,128)S(1)}, u32[]{:S(2)}, u32[]{:S(2)}) collective-permute-start(f32[4,128]{1,0:T(4,128)S(1)} %get-tuple-element.86), channel_id=1, source_target_pairs={{0,4},{1,5},{2,6},{3,7},{4,0},{5,1},{6,2},{7,3},{8,12},{9,13},{10,... | collective-permute-start | bytes 6152 | tf_op jit(solution)/shard_map/ppermute | solution.py:380
  52.9 1.8 %collective-permute-start.15 = (f32[4,128]{1,0:T(4,128)S(1)}, f32[4,128]{1,0:T(4,128)S(1)}, u32[]{:S(2)}, u32[]{:S(2)}) collective-permute-start(f32[4,128]{1,0:T(4,128)S(1)} %get-tuple-element.86), channel_id=1, source_target_pairs={{0,8},{1,9},{2,10},{3,11},{4,12},{5,13},{6,14},{7,15},{8,0},{9,1},... | collective-permute-start | bytes 6152 | tf_op jit(solution)/shard_map/ppermute | solution.py:380
  54.7 0.6 collective-permute-start.16
  55.3 1.1 %collective-permute-start.18 = (bf16[512,256]{1,0:T(8,128)(2,1)S(1)}, bf16[512,256]{1,0:T(8,128)(2,1)S(1)}, u32[]{:S(2)}, u32[]{:S(2)}) collective-permute-start(bf16[512,256]{1,0:T(8,128)(2,1)S(1)} %get-tuple-element.90), channel_id=1, source_target_pairs={{0,4},{1,5},{2,6},{3,7},{4,12},{5,13},{6,14},{7,15},{8,0},{9,1},{1... | collective-permute-start | bytes 786440 | tf_op jit(solution)/shard_map/ppermute | solution.py:387
  56.4 3.9 %collective-permute-done.14 = f32[4,128]{1,0:T(4,128)S(1)} collective-permute-done((f32[4,128]{1,0:T(4,128)S(1)}, f32[4,128]{1,0:T(4,128)S(1)}, u32[]{:S(2)}, u32[]{:S(2)}) %collective-permute-start.14) | collective-permute-done | bytes 2080 | tf_op jit(solution)/shard_map/ppermute | solution.py:380
  60.4 2.2 %collective-permute-done.15 = f32[4,128]{1,0:T(4,128)S(1)} collective-permute-done((f32[4,128]{1,0:T(4,128)S(1)}, f32[4,128]{1,0:T(4,128)S(1)}, u32[]{:S(2)}, u32[]{:S(2)}) %collective-permute-start.15) | collective-permute-done | bytes 2080 | tf_op jit(solution)/shard_map/ppermute | solution.py:380
  62.6 1.6 %collective-permute-done.16 = f32[4,128]{1,0:T(4,128)S(1)} collective-permute-done((f32[4,128]{1,0:T(4,128)S(1)}, f32[4,128]{1,0:T(4,128)S(1)}, u32[]{:S(2)}, u32[]{:S(2)}) %collective-permute-start.16) | collective-permute-done | bytes 2080 | tf_op jit(solution)/shard_map/ppermute | solution.py:380
  64.2 0.2 shard_map.61.refs_0_.refs_2_
  64.4 0.9 shard_map.62
  65.3 2.7 %collective-permute-done.18.refs_1_ = bf16[512,256]{1,0:T(8,128)(2,1)S(1)} collective-permute-done((bf16[512,256]{1,0:T(8,128)(2,1)S(1)}, bf16[512,256]{1,0:T(8,128)(2,1)S(1)}, u32[]{:S(2)}, u32[]{:S(2)}) %collective-permute-start.18) | collective-permute-done | bytes 262176 | tf_op jit(solution)/shard_map/ppermute | solution.py:387
  68.0 0.9 shard_map.63
  68.9 0.1 collective-permute-start.22
  69.1 0.4 collective-permute-start.20
  69.5 1.2 %collective-permute-done.22.got_ref = bf16[2,160,640]{2,1,0:T(8,128)(2,1)S(1)} collective-permute-done((bf16[2,160,640]{2,1,0:T(8,128)(2,1)S(1)}, bf16[2,160,640]{2,1,0:T(8,128)(2,1)S(1)}, u32[]{:S(2)}, u32[]{:S(2)}) %collective-permute-start.22) | collective-permute-done | bytes 409632 | tf_op jit(solution)/shard_map/ppermute | solution.py:380
  70.8 0.1 shard_map.65
  70.9 0.9 shard_map.66
  71.7 0.2 collective-permute-start.23
  71.9 0.8 collective-permute-start.25
  72.8 0.1 shard_map.64
  72.8 1.3 %collective-permute-start.21 = (bf16[1,160,640]{2,1,0:T(8,128)(2,1)S(1)}, bf16[1,160,640]{2,1,0:T(8,128)(2,1)S(1)}, u32[]{:S(2)}, u32[]{:S(2)}) collective-permute-start(bf16[1,160,640]{2,1,0:T(8,128)(2,1)S(1)} %get-tuple-element.97), channel_id=1, source_target_pairs={{0,2},{1,3},{2,0},{3,1},{4,6},{5,7},{6,4},{7,5},{8,10},{9,11},{10,... | collective-permute-start | bytes 614408 | tf_op jit(solution)/shard_map/ppermute | solution.py:380
  74.1 0.1 shard_map.67
  74.2 0.9 collective-permute-start.24
  75.1 4.8 %collective-permute-done.25 = bf16[1,160,640]{2,1,0:T(8,128)(2,1)S(1)} collective-permute-done((bf16[1,160,640]{2,1,0:T(8,128)(2,1)S(1)}, bf16[1,160,640]{2,1,0:T(8,128)(2,1)S(1)}, u32[]{:S(2)}, u32[]{:S(2)}) %collective-permute-start.25) | collective-permute-done | bytes 204832 | tf_op jit(solution)/shard_map/ppermute | solution.py:380
  79.9 4.4 %collective-permute-done.21 = bf16[1,160,640]{2,1,0:T(8,128)(2,1)S(1)} collective-permute-done((bf16[1,160,640]{2,1,0:T(8,128)(2,1)S(1)}, bf16[1,160,640]{2,1,0:T(8,128)(2,1)S(1)}, u32[]{:S(2)}, u32[]{:S(2)}) %collective-permute-start.21) | collective-permute-done | bytes 204832 | tf_op jit(solution)/shard_map/ppermute | solution.py:380
  84.2 2.8 %collective-permute-done.19.refs_1_ = bf16[512,640]{1,0:T(8,128)(2,1)S(1)} collective-permute-done((bf16[512,640]{1,0:T(8,128)(2,1)S(1)}, bf16[512,640]{1,0:T(8,128)(2,1)S(1)}, u32[]{:S(2)}, u32[]{:S(2)}) %collective-permute-start.19) | collective-permute-done | bytes 655392 | tf_op jit(solution)/shard_map/ppermute | solution.py:387
  87.1 1.0 %collective-permute-done.24 = bf16[1,160,640]{2,1,0:T(8,128)(2,1)S(1)} collective-permute-done((bf16[1,160,640]{2,1,0:T(8,128)(2,1)S(1)}, bf16[1,160,640]{2,1,0:T(8,128)(2,1)S(1)}, u32[]{:S(2)}, u32[]{:S(2)}) %collective-permute-start.24) | collective-permute-done | bytes 204832 | tf_op jit(solution)/shard_map/ppermute | solution.py:380
  88.1 0.9 shard_map.68
  89.1 1.8 %collective-permute-start.28 = (bf16[160,640]{1,0:T(8,128)(2,1)S(1)}, bf16[160,640]{1,0:T(8,128)(2,1)S(1)}, u32[]{:S(2)}, u32[]{:S(2)}) collective-permute-start(bf16[160,640]{1,0:T(8,128)(2,1)S(1)} %fusion), channel_id=1, source_target_pairs={{0,8},{1,9},{2,10},{3,11},{4,0},{5,1},{6,2},{7,3},{8,12},{9,13},{1... | collective-permute-start | bytes 614408 | tf_op jit(solution)/shard_map/ppermute | solution.py:387
  90.9 0.8 collective-permute-start.27
  91.8 1.5 %shard_map.70.refs_4_ = f32[160,2560]{1,0:T(8,128)} custom-call(s32[4]{0:T(128)S(1)} %shift-right-arithmetic_xor_fusion.at_ref, f32[160,640]{1,0:T(8,128)S(1)} %bitcast.37, bf16[160,640]{1,0:T(8,128)(2,1)S(1)} %bitcast.40, f32[160,640]{1,0:T(8,128)S(1)} %bitcast.38, bf16[160,640]{1,0:T(8,128)(2,1)S(1)} %bitcast.41), custom_call_target="tpu_custom_call" | custom-call | flops 1 | bytes 1 | tf_op jit(solution)/shard_map/pallas_call | solution.py:354
  93.3 3.3 %collective-permute-done.28.refs_2_ = bf16[160,640]{1,0:T(8,128)(2,1)S(1)} collective-permute-done((bf16[160,640]{1,0:T(8,128)(2,1)S(1)}, bf16[160,640]{1,0:T(8,128)(2,1)S(1)}, u32[]{:S(2)}, u32[]{:S(2)}) %collective-permute-start.28) | collective-permute-done | bytes 204832 | tf_op jit(solution)/shard_map/ppermute | solution.py:387
  96.6 1.6 %collective-permute-done.27 = bf16[1,160,640]{2,1,0:T(8,128)(2,1)S(1)} collective-permute-done((bf16[1,160,640]{2,1,0:T(8,128)(2,1)S(1)}, bf16[1,160,640]{2,1,0:T(8,128)(2,1)S(1)}, u32[]{:S(2)}, u32[]{:S(2)}) %collective-permute-start.27) | collective-permute-done | bytes 204832 | tf_op jit(solution)/shard_map/ppermute | solution.py:380
  98.2 1.5 %shard_map.71 = f32[160,2560]{1,0:T(8,128)} custom-call(s32[4]{0:T(128)S(1)} %shift-right-arithmetic_xor_fusion.at_ref, f32[160,640]{1,0:T(8,128)S(1)} %bitcast.39, bf16[160,640]{1,0:T(8,128)(2,1)S(1)} %bitcast.42, bf16[160,640]{1,0:T(8,128)(2,1)S(1)} %collective-permute-done.28.refs_2_, ...), custom_call_target="tpu_custom_call", output_to_operand_aliasing={{}: (5, {})} | custom-call | flops 1 | bytes 1 | tf_op jit(solution)/shard_map/pallas_call | solution.py:354
  (35 shorter events, 0.4 us)
Async XLA Ops:
  0.0 15.5 %copy-start = (bf16[128,3968]{1,0:T(8,128)(2,1)S(1)}, bf16[128,3968]{1,0:T(8,128)(2,1)}, u32[]{:S(2)}) copy-start(bf16[128,3968]{1,0:T(8,128)(2,1)} %flux_ref) | copy-start | bytes 3047428
  0.8 1.3 %collective-permute-start = (s32[20]{0:T(128)S(1)}, s32[20]{0:T(128)S(1)}, u32[]{:S(2)}, u32[]{:S(2)}) collective-permute-start(s32[20]{0:T(128)S(1)} %slice.13), channel_id=1, source_target_pairs={{0,1},{1,0},{2,3},{3,2},{4,5},{5,4},{6,7},{7,6},{8,9},{9,8},{10,11... | collective-permute-start | bytes 248 | tf_op jit(solution)/shard_map/ppermute | solution.py:380
  2.2 11.1 %collective-permute-start.1 = (s32[168]{0:T(256)S(1)}, s32[168]{0:T(256)S(1)}, u32[]{:S(2)}, u32[]{:S(2)}) collective-permute-start(s32[168]{0:T(256)S(1)} %pad_add_fusion.3), channel_id=1, source_target_pairs={{0,4},{1,5},{2,6},{3,7},{4,0},{5,1},{6,2},{7,3},{8,12},{9,13},{10,... | collective-permute-start | bytes 2024 | tf_op jit(solution)/shard_map/ppermute | solution.py:380
  5.1 8.3 %collective-permute-start.2 = (s32[168]{0:T(256)S(1)}, s32[168]{0:T(256)S(1)}, u32[]{:S(2)}, u32[]{:S(2)}) collective-permute-start(s32[168]{0:T(256)S(1)} %pad_add_fusion.3), channel_id=1, source_target_pairs={{0,8},{1,9},{2,10},{3,11},{4,12},{5,13},{6,14},{7,15},{8,0},{9,1},... | collective-permute-start | bytes 2024 | tf_op jit(solution)/shard_map/ppermute | solution.py:380
  7.7 5.7 %collective-permute-start.3 = (s32[168]{0:T(256)S(1)}, s32[168]{0:T(256)S(1)}, u32[]{:S(2)}, u32[]{:S(2)}) collective-permute-start(s32[168]{0:T(256)S(1)} %pad_add_fusion.3), channel_id=1, source_target_pairs={{0,12},{1,13},{2,14},{3,15},{4,8},{5,9},{6,10},{7,11},{8,4},{9,5},... | collective-permute-start | bytes 2024 | tf_op jit(solution)/shard_map/ppermute | solution.py:380
  8.9 18.0 %collective-permute-start.4 = (bf16[640,128]{1,0:T(8,128)(2,1)S(1)}, bf16[640,128]{1,0:T(8,128)(2,1)S(1)}, u32[]{:S(2)}, u32[]{:S(2)}) collective-permute-start(bf16[640,128]{1,0:T(8,128)(2,1)S(1)} %get-tuple-element.119), channel_id=1, source_target_pairs={{0,4},{1,5},{2,6},{3,7},{4,0},{5,1},{6,2},{7,3},{8,12},{9,13},{10,... | collective-permute-start | bytes 491528 | tf_op jit(solution)/shard_map/ppermute | solution.py:380
  9.8 17.1 %collective-permute-start.5 = (bf16[640,128]{1,0:T(8,128)(2,1)S(1)}, bf16[640,128]{1,0:T(8,128)(2,1)S(1)}, u32[]{:S(2)}, u32[]{:S(2)}) collective-permute-start(bf16[640,128]{1,0:T(8,128)(2,1)S(1)} %get-tuple-element.118), channel_id=1, source_target_pairs={{0,8},{1,9},{2,10},{3,11},{4,12},{5,13},{6,14},{7,15},{8,0},{9,1},... | collective-permute-start | bytes 491528 | tf_op jit(solution)/shard_map/ppermute | solution.py:380
  13.3 13.6 %collective-permute-start.6 = (bf16[640,128]{1,0:T(8,128)(2,1)S(1)}, bf16[640,128]{1,0:T(8,128)(2,1)S(1)}, u32[]{:S(2)}, u32[]{:S(2)}) collective-permute-start(bf16[640,128]{1,0:T(8,128)(2,1)S(1)} %get-tuple-element.117), channel_id=1, source_target_pairs={{0,12},{1,13},{2,14},{3,15},{4,8},{5,9},{6,10},{7,11},{8,4},{9,5},... | collective-permute-start | bytes 491528 | tf_op jit(solution)/shard_map/ppermute | solution.py:380
  13.4 8.7 %collective-permute-start.7 = (s32[4,2,20]{2,1,0:T(2,128)S(1)}, s32[4,2,20]{2,1,0:T(2,128)S(1)}, u32[]{:S(2)}, u32[]{:S(2)}) collective-permute-start(s32[4,2,20]{2,1,0:T(2,128)S(1)} %reshape.18), channel_id=1, source_target_pairs={{0,2},{1,3},{2,0},{3,1},{4,6},{5,7},{6,4},{7,5},{8,10},{9,11},{10,... | collective-permute-start | bytes 1928 | tf_op jit(solution)/shard_map/ppermute | solution.py:380
  27.0 5.0 %collective-permute-start.9 = (bf16[4,640,128]{2,1,0:T(8,128)(2,1)S(1)}, bf16[4,640,128]{2,1,0:T(8,128)(2,1)S(1)}, u32[]{:S(2)}, u32[]{:S(2)}) collective-permute-start(bf16[4,640,128]{2,1,0:T(8,128)(2,1)S(1)} %pad_maximum_fusion.refs_1_.refs_3_), channel_id=1, source_target_pairs={{0,1},{1,0},{2,3},{3,2},{4,5},{5,4},{6,7},{7,6},{8,9},{9,8},{10,11... | collective-permute-start | bytes 1966088 | tf_op jit(solution)/shard_map/ppermute | solution.py:380
  27.1 17.1 %collective-permute-start.8 = (bf16[4,640,128]{2,1,0:T(8,128)(2,1)S(1)}, bf16[4,640,128]{2,1,0:T(8,128)(2,1)S(1)}, u32[]{:S(2)}, u32[]{:S(2)}) collective-permute-start(bf16[4,640,128]{2,1,0:T(8,128)(2,1)S(1)} %pad_maximum_fusion.refs_1_.refs_3_), channel_id=1, source_target_pairs={{0,2},{1,3},{2,0},{3,1},{4,6},{5,7},{6,4},{7,5},{8,10},{9,11},{10,... | collective-permute-start | bytes 1966088 | tf_op jit(solution)/shard_map/ppermute | solution.py:380
  27.4 15.2 %collective-permute-start.11 = (bf16[128,640]{1,0:T(8,128)(2,1)S(1)}, bf16[128,640]{1,0:T(8,128)(2,1)S(1)}, u32[]{:S(2)}, u32[]{:S(2)}) collective-permute-start(bf16[128,640]{1,0:T(8,128)(2,1)S(1)} %get-tuple-element.77), channel_id=1, source_target_pairs={{0,8},{1,9},{2,10},{3,11},{4,12},{5,13},{6,14},{7,15},{8,0},{9,1},... | collective-permute-start | bytes 491528 | tf_op jit(solution)/shard_map/ppermute | solution.py:380
  30.6 12.0 %collective-permute-start.12 = (bf16[128,640]{1,0:T(8,128)(2,1)S(1)}, bf16[128,640]{1,0:T(8,128)(2,1)S(1)}, u32[]{:S(2)}, u32[]{:S(2)}) collective-permute-start(bf16[128,640]{1,0:T(8,128)(2,1)S(1)} %get-tuple-element.78), channel_id=1, source_target_pairs={{0,12},{1,13},{2,14},{3,15},{4,8},{5,9},{6,10},{7,11},{8,4},{9,5},... | collective-permute-start | bytes 491528 | tf_op jit(solution)/shard_map/ppermute | solution.py:380
  32.0 12.2 %collective-permute-start.10 = (bf16[128,640]{1,0:T(8,128)(2,1)S(1)}, bf16[128,640]{1,0:T(8,128)(2,1)S(1)}, u32[]{:S(2)}, u32[]{:S(2)}) collective-permute-start(bf16[128,640]{1,0:T(8,128)(2,1)S(1)} %get-tuple-element.76), channel_id=1, source_target_pairs={{0,4},{1,5},{2,6},{3,7},{4,0},{5,1},{6,2},{7,3},{8,12},{9,13},{10,... | collective-permute-start | bytes 491528 | tf_op jit(solution)/shard_map/ppermute | solution.py:380
  44.2 2.1 %collective-permute-start.13 = (bf16[4,640,128]{2,1,0:T(8,128)(2,1)S(1)}, bf16[4,640,128]{2,1,0:T(8,128)(2,1)S(1)}, u32[]{:S(2)}, u32[]{:S(2)}) collective-permute-start(bf16[4,640,128]{2,1,0:T(8,128)(2,1)S(1)} %collective-permute-done.8.refs_6_), channel_id=1, source_target_pairs={{0,1},{1,0},{2,3},{3,2},{4,5},{5,4},{6,7},{7,6},{8,9},{9,8},{10,11... | collective-permute-start | bytes 1966088 | tf_op jit(solution)/shard_map/ppermute | solution.py:380
  48.7 15.5 %collective-permute-start.17 = (bf16[512,384]{1,0:T(8,128)(2,1)S(1)}, bf16[512,384]{1,0:T(8,128)(2,1)S(1)}, u32[]{:S(2)}, u32[]{:S(2)}) collective-permute-start(bf16[512,384]{1,0:T(8,128)(2,1)S(1)} %get-tuple-element.87), channel_id=1, source_target_pairs={{0,4},{1,5},{2,6},{3,7},{4,12},{5,13},{6,14},{7,15},{8,0},{9,1},{1... | collective-permute-start | bytes 1179656 | tf_op jit(solution)/shard_map/ppermute | solution.py:387
  50.9 9.5 %collective-permute-start.14 = (f32[4,128]{1,0:T(4,128)S(1)}, f32[4,128]{1,0:T(4,128)S(1)}, u32[]{:S(2)}, u32[]{:S(2)}) collective-permute-start(f32[4,128]{1,0:T(4,128)S(1)} %get-tuple-element.86), channel_id=1, source_target_pairs={{0,4},{1,5},{2,6},{3,7},{4,0},{5,1},{6,2},{7,3},{8,12},{9,13},{10,... | collective-permute-start | bytes 6152 | tf_op jit(solution)/shard_map/ppermute | solution.py:380
  52.9 9.7 %collective-permute-start.15 = (f32[4,128]{1,0:T(4,128)S(1)}, f32[4,128]{1,0:T(4,128)S(1)}, u32[]{:S(2)}, u32[]{:S(2)}) collective-permute-start(f32[4,128]{1,0:T(4,128)S(1)} %get-tuple-element.86), channel_id=1, source_target_pairs={{0,8},{1,9},{2,10},{3,11},{4,12},{5,13},{6,14},{7,15},{8,0},{9,1},... | collective-permute-start | bytes 6152 | tf_op jit(solution)/shard_map/ppermute | solution.py:380
  54.7 9.5 %collective-permute-start.16 = (f32[4,128]{1,0:T(4,128)S(1)}, f32[4,128]{1,0:T(4,128)S(1)}, u32[]{:S(2)}, u32[]{:S(2)}) collective-permute-start(f32[4,128]{1,0:T(4,128)S(1)} %get-tuple-element.86), channel_id=1, source_target_pairs={{0,12},{1,13},{2,14},{3,15},{4,8},{5,9},{6,10},{7,11},{8,4},{9,5},... | collective-permute-start | bytes 6152 | tf_op jit(solution)/shard_map/ppermute | solution.py:380
  55.3 12.7 %collective-permute-start.18 = (bf16[512,256]{1,0:T(8,128)(2,1)S(1)}, bf16[512,256]{1,0:T(8,128)(2,1)S(1)}, u32[]{:S(2)}, u32[]{:S(2)}) collective-permute-start(bf16[512,256]{1,0:T(8,128)(2,1)S(1)} %get-tuple-element.90), channel_id=1, source_target_pairs={{0,4},{1,5},{2,6},{3,7},{4,12},{5,13},{6,14},{7,15},{8,0},{9,1},{1... | collective-permute-start | bytes 786440 | tf_op jit(solution)/shard_map/ppermute | solution.py:387
  68.9 1.8 %collective-permute-start.22 = (bf16[2,160,640]{2,1,0:T(8,128)(2,1)S(1)}, bf16[2,160,640]{2,1,0:T(8,128)(2,1)S(1)}, u32[]{:S(2)}, u32[]{:S(2)}) collective-permute-start(bf16[2,160,640]{2,1,0:T(8,128)(2,1)S(1)} %get-tuple-element.99), channel_id=1, source_target_pairs={{0,1},{1,0},{2,3},{3,2},{4,5},{5,4},{6,7},{7,6},{8,9},{9,8},{10,11... | collective-permute-start | bytes 1228808 | tf_op jit(solution)/shard_map/ppermute | solution.py:380
  69.0 18.0 %collective-permute-start.19 = (bf16[512,640]{1,0:T(8,128)(2,1)S(1)}, bf16[512,640]{1,0:T(8,128)(2,1)S(1)}, u32[]{:S(2)}, u32[]{:S(2)}) collective-permute-start(bf16[512,640]{1,0:T(8,128)(2,1)S(1)} %get-tuple-element.101.refs_1_), channel_id=1, source_target_pairs={{0,4},{1,5},{2,6},{3,7},{4,12},{5,13},{6,14},{7,15},{8,0},{9,1},{1... | collective-permute-start | bytes 1966088 | tf_op jit(solution)/shard_map/ppermute | solution.py:387
  69.1 3.7 %collective-permute-start.20 = (bf16[2,160,640]{2,1,0:T(8,128)(2,1)S(1)}, bf16[2,160,640]{2,1,0:T(8,128)(2,1)S(1)}, u32[]{:S(2)}, u32[]{:S(2)}) collective-permute-start(bf16[2,160,640]{2,1,0:T(8,128)(2,1)S(1)} %get-tuple-element.96), channel_id=1, source_target_pairs={{0,1},{1,0},{2,3},{3,2},{4,5},{5,4},{6,7},{7,6},{8,9},{9,8},{10,11... | collective-permute-start | bytes 1228808 | tf_op jit(solution)/shard_map/ppermute | solution.py:380
  71.7 2.4 %collective-permute-start.23 = (bf16[2,160,640]{2,1,0:T(8,128)(2,1)S(1)}, bf16[2,160,640]{2,1,0:T(8,128)(2,1)S(1)}, u32[]{:S(2)}, u32[]{:S(2)}) collective-permute-start(bf16[2,160,640]{2,1,0:T(8,128)(2,1)S(1)} %get-tuple-element.103), channel_id=1, source_target_pairs={{0,1},{1,0},{2,3},{3,2},{4,5},{5,4},{6,7},{7,6},{8,9},{9,8},{10,11... | collective-permute-start | bytes 1228808 | tf_op jit(solution)/shard_map/ppermute | solution.py:380
  71.9 7.9 %collective-permute-start.25 = (bf16[1,160,640]{2,1,0:T(8,128)(2,1)S(1)}, bf16[1,160,640]{2,1,0:T(8,128)(2,1)S(1)}, u32[]{:S(2)}, u32[]{:S(2)}) collective-permute-start(bf16[1,160,640]{2,1,0:T(8,128)(2,1)S(1)} %get-tuple-element.105), channel_id=1, source_target_pairs={{0,2},{1,3},{2,0},{3,1},{4,6},{5,7},{6,4},{7,5},{8,10},{9,11},{10,... | collective-permute-start | bytes 614408 | tf_op jit(solution)/shard_map/ppermute | solution.py:380
  72.8 11.4 %collective-permute-start.21 = (bf16[1,160,640]{2,1,0:T(8,128)(2,1)S(1)}, bf16[1,160,640]{2,1,0:T(8,128)(2,1)S(1)}, u32[]{:S(2)}, u32[]{:S(2)}) collective-permute-start(bf16[1,160,640]{2,1,0:T(8,128)(2,1)S(1)} %get-tuple-element.97), channel_id=1, source_target_pairs={{0,2},{1,3},{2,0},{3,1},{4,6},{5,7},{6,4},{7,5},{8,10},{9,11},{10,... | collective-permute-start | bytes 614408 | tf_op jit(solution)/shard_map/ppermute | solution.py:380
  74.2 13.9 %collective-permute-start.24 = (bf16[1,160,640]{2,1,0:T(8,128)(2,1)S(1)}, bf16[1,160,640]{2,1,0:T(8,128)(2,1)S(1)}, u32[]{:S(2)}, u32[]{:S(2)}) collective-permute-start(bf16[1,160,640]{2,1,0:T(8,128)(2,1)S(1)} %get-tuple-element.104), channel_id=1, source_target_pairs={{0,2},{1,3},{2,0},{3,1},{4,6},{5,7},{6,4},{7,5},{8,10},{9,11},{10,... | collective-permute-start | bytes 614408 | tf_op jit(solution)/shard_map/ppermute | solution.py:380
  89.0 1.9 %collective-permute-start.26 = (bf16[2,160,640]{2,1,0:T(8,128)(2,1)S(1)}, bf16[2,160,640]{2,1,0:T(8,128)(2,1)S(1)}, u32[]{:S(2)}, u32[]{:S(2)}) collective-permute-start(bf16[2,160,640]{2,1,0:T(8,128)(2,1)S(1)} %get-tuple-element.108), channel_id=1, source_target_pairs={{0,1},{1,0},{2,3},{3,2},{4,5},{5,4},{6,7},{7,6},{8,9},{9,8},{10,11... | collective-permute-start | bytes 1228808 | tf_op jit(solution)/shard_map/ppermute | solution.py:380
  89.1 7.5 %collective-permute-start.28 = (bf16[160,640]{1,0:T(8,128)(2,1)S(1)}, bf16[160,640]{1,0:T(8,128)(2,1)S(1)}, u32[]{:S(2)}, u32[]{:S(2)}) collective-permute-start(bf16[160,640]{1,0:T(8,128)(2,1)S(1)} %fusion), channel_id=1, source_target_pairs={{0,8},{1,9},{2,10},{3,11},{4,0},{5,1},{6,2},{7,3},{8,12},{9,13},{1... | collective-permute-start | bytes 614408 | tf_op jit(solution)/shard_map/ppermute | solution.py:387
  90.9 7.3 %collective-permute-start.27 = (bf16[1,160,640]{2,1,0:T(8,128)(2,1)S(1)}, bf16[1,160,640]{2,1,0:T(8,128)(2,1)S(1)}, u32[]{:S(2)}, u32[]{:S(2)}) collective-permute-start(bf16[1,160,640]{2,1,0:T(8,128)(2,1)S(1)} %get-tuple-element.110), channel_id=1, source_target_pairs={{0,2},{1,3},{2,0},{3,1},{4,6},{5,7},{6,4},{7,5},{8,10},{9,11},{10,... | collective-permute-start | bytes 614408 | tf_op jit(solution)/shard_map/ppermute | solution.py:380

commit v17 on v15

--- a/solution.py
+++ b/solution.py
@@ -130,22 +130,24 @@
     )
 
 
-def cut_kernel(per, band, unroll, me_ref, groups_ref, starts_ref, turns_ref, smoothed_ref, placing_ref, *refs):
-    outs, (placed, cut) = refs[:OUTER], refs[OUTER:]
-    placed[...] = jnp.dot(placing_ref[...], smoothed_ref[...], preferred_element_type=F32)
+def cut_kernel(aways, per, band, unroll, placed_here, me_ref, groups_ref, starts_ref, turns_ref, placing_ref, source_ref, *refs):
+    outs, refs = refs[: len(aways)], refs[len(aways) :]
+    placed, cut = refs if placed_here else (source_ref, refs[0])
+    if placed_here:
+        placed[...] = jnp.dot(placing_ref[...], source_ref[...], preferred_element_type=F32)
 
     def some_groups(step, carry):
         for i in range(unroll):
             group = step * unroll + i
             rows = pl.ds(pl.multiple_of(group * GROUP, GROUP), GROUP)
             entry = groups_ref[0, group] ^ me_ref[0]
-            for away in range(OUTER):
+            for k, away in enumerate(aways):
                 first = (me_ref[1] ^ away) * per
                 for j in range(per):
                     start = pl.multiple_of(starts_ref[entry, first + j], band)
                     wide = placed[rows, pl.ds(start, 2 * band)]
                     turned = pltpu.roll(wide, turns_ref[entry, first + j], 1)
-                    at = (away * per + j) * band
+                    at = (k * per + j) * band
                     cut[rows, at : at + band] = turned[:, :band]
         return carry
 
@@ -154,7 +156,7 @@
         cut[rows, :] = jnp.zeros((unroll * GROUP, cut.shape[1]), F32)
         return carry
 
-    steps = placed.shape[0] // GROUP // unroll
+    steps = cut.shape[0] // GROUP // unroll
     done = jnp.minimum((groups_ref[1, 0] + unroll - 1) // unroll, steps)
     lax.fori_loop(0, done, some_groups, 0)
     lax.fori_loop(done, steps, clear_groups, 0)
@@ -162,22 +164,24 @@
     back = lax.dot_general(
         placing_ref[...], cut[...].astype(BF16), (((0,), (0,)), ((), ())), preferred_element_type=F32
     ).astype(BF16)
-    for away in range(OUTER):
-        outs[away][...] = back[:, away * width : (away + 1) * width]
-
-
-def cut_windows(me, groups, starts, turns, smoothed, placing, band):
+    for k in range(len(aways)):
+        outs[k][...] = back[:, k * width : (k + 1) * width]
+
+
+def cut_windows(aways, me, groups, starts, turns, placing, source, band):
     per = starts.shape[1] // OUTER
     places, rows = placing.shape
-    nobs = smoothed.shape[1]
+    nobs = source.shape[1]
     width = per * band
+    placed_here = source.dtype == BF16
     unroll = max(k for k in range(1, 7) if places // GROUP % k == 0)
-    return call(
-        functools.partial(cut_kernel, per, band, unroll),
-        (jax.ShapeDtypeStruct((rows, width), BF16),) * OUTER,
+    placed = (jax.ShapeDtypeStruct((places, nobs), F32),) if placed_here else ()
+    return call(
+        functools.partial(cut_kernel, aways, per, band, unroll, placed_here),
+        (jax.ShapeDtypeStruct((rows, width), BF16),) * len(aways) + placed,
         [SMEM] * 4 + [VMEM] * 2,
-        (me, groups, starts, turns, smoothed, placing),
-        [pltpu.VMEM((places, nobs), F32), pltpu.VMEM((places, OUTER * width), F32)],
+        (me, groups, starts, turns, placing, source),
+        [pltpu.VMEM((places, len(aways) * width), F32)],
         limit=max(12 * 1024 * 1024, places * (nobs + OUTER * width) * 6),
     )
 
@@ -409,9 +413,10 @@
     chunk = jnp.minimum(offsets // band, nobs // band - 2)
     turns = (2 * band + chunk * band - offsets) & (2 * band - 1)
     outer1 = outer.reshape(1)
-    windows = cut_windows(jnp.stack([me, outer]), group_bins, chunk * band, turns, smoothed, placing, band)
-
-    pieces, *windows = lax.optimization_barrier((pieces, *windows))
+    tables = (jnp.stack([me, outer]), group_bins, chunk * band, turns, placing)
+    *distant, placed = cut_windows((2, 3), *tables, smoothed, band)
+
+    pieces, *distant = lax.optimization_barrier((pieces, *distant))
     mixed = jnp.stack(pieces)
     bit = inner // 2
     weights = [mixed, swap(mixed, bit)]
@@ -421,7 +426,8 @@
         bit //= 2
         bits.append(bit)
         near = near + [swap(piece, bit) for piece in near]
-    windows[1], near[-1] = lax.optimization_barrier((windows[1], near[-1]))
+    placed, near[-1] = lax.optimization_barrier((placed, near[-1]))
+    windows = cut_windows((0, 1), *tables, placed, band) + tuple(distant)
     arrived = [windows[0]] + [swap(windows[away], away * inner) for away in range(1, OUTER)]
     near_bins = [mine]
     for bit in bits:

time: 98.4 us -> 98.4 us (level)
  Pallas kernels: 23.8 us -> 25.1 us
  waiting for transfers between devices: 39.1 us -> 38.1 us
    pallas_call x15 -> x16, Pallas kernels: 20.8 us -> 22.1 us  [call(): pl.pallas_call(kernel, out_shape=out_shape, in_specs=in_specs, out_specs=...]
  transfers between devices with their start and end apart: 29 -> 29, of which waited for: 15 -> 16; matrix products, arithmetic and copies ran while one was open for 2% -> 2% of each run, Pallas kernels for 19% -> 20%
where the time goes in v17:
time: 98.4 us; the launch traced here: 98.2 us
  waiting for transfers between devices  38.1 us (39%)
  starting transfers between devices  32.2 us (33%)
  Pallas kernels  25.1 us (26%)
  local copies, waits for them, and re-layouts  1.37 us (1%)
  other arithmetic  1.27 us (1%)
    ppermute x25, waiting for transfers between devices, swap(): return lax.ppermute(array, 'spec', [(i, i ^ bit) for i in range(n)])  28.8 us
    ppermute x25, starting transfers between devices, swap(): return lax.ppermute(array, 'spec', [(i, i ^ bit) for i in range(n)])  27.8 us
    pallas_call x16, Pallas kernels, call(): pl.pallas_call(kernel, out_shape=out_shape, in_specs=in_specs, out_specs=...  22.1 us
    ppermute x4, waiting for transfers between devices, step(): lax.ppermute(array, 'spec', [(o * inner + i, to[o] * inner + i) for o in...  9.25 us
    ppermute x4, starting transfers between devices, step(): lax.ppermute(array, 'spec', [(o * inner + i, to[o] * inner + i) for o in...  4.32 us
    pallas_call x2, Pallas kernels, place(): pl.pallas_call(functools.partial(place_kernel, slots, last), out_shape=ja...  2.98 us
  transfers between devices with their start and end apart: 29, of which 16 were waited for; matrix products, arithmetic and copies ran while one was open for 2% of the time, Pallas kernels for 20%

profile of v17, /device:TPU:0, one launch (start us, length us, event | category | flops | bytes accessed | tf_op | source)
XLA Modules:
  0.0 98.2 jit_solution(11489527685258849734)
XLA Ops:
  0.0 0.8 pad_add_fusion.3
  0.8 3.0 %collective-permute-start = (s32[148]{0:T(256)S(1)}, s32[148]{0:T(256)S(1)}, u32[]{:S(2)}, u32[]{:S(2)}) collective-permute-start(s32[148]{0:T(256)S(1)} %pad_add_fusion.3), channel_id=1, source_target_pairs={{0,4},{1,5},{2,6},{3,7},{4,0},{5,1},{6,2},{7,3},{8,12},{9,13},{10,... | collective-permute-start | bytes 1784 | tf_op jit(solution)/shard_map/ppermute | solution.py:379
  3.9 2.6 %collective-permute-start.1 = (s32[148]{0:T(256)S(1)}, s32[148]{0:T(256)S(1)}, u32[]{:S(2)}, u32[]{:S(2)}) collective-permute-start(s32[148]{0:T(256)S(1)} %pad_add_fusion.3), channel_id=1, source_target_pairs={{0,8},{1,9},{2,10},{3,11},{4,12},{5,13},{6,14},{7,15},{8,0},{9,1},... | collective-permute-start | bytes 1784 | tf_op jit(solution)/shard_map/ppermute | solution.py:379
  6.5 1.2 %dynamic-slice_bitcast_fusion = (bf16[640,128]{1,0:T(8,128)(2,1)S(1)}, bf16[640,128]{1,0:T(8,128)(2,1)S(1)}, bf16[640,128]{1,0:T(8,128)(2,1)S(1)}, bf16[640,128]{1,0:T(8,128)(2,1)S(1)}) fusion(bf16[4,640,128]{2,1,0:T(8,128)(2,1)} %bitcast.47, s32[]{:T(128)S(6)} %select_n.41, s32[]{:T(128)S(6)} %select_n.40, s32[]{:T(128)S(6)} %select_n.39, s32[]{:T(128)S(6)} %select_n.38), kind=kLoop, calls=%fused_computation.3 | loop fusion | bytes 1310736 | tf_op jit(solution)/shard_map/jit(dynamic_index_in_dim)/squeeze | solution.py:405
  7.7 1.0 collective-permute-start.3
  8.6 3.5 %collective-permute-start.4 = (bf16[640,128]{1,0:T(8,128)(2,1)S(1)}, bf16[640,128]{1,0:T(8,128)(2,1)S(1)}, u32[]{:S(2)}, u32[]{:S(2)}) collective-permute-start(bf16[640,128]{1,0:T(8,128)(2,1)S(1)} %get-tuple-element.116), channel_id=1, source_target_pairs={{0,8},{1,9},{2,10},{3,11},{4,12},{5,13},{6,14},{7,15},{8,0},{9,1},... | collective-permute-start | bytes 491528 | tf_op jit(solution)/shard_map/ppermute | solution.py:379
  12.2 0.1 collective-permute-start.6
  12.2 0.1 slice_bitcast_fusion.1.targets_ref
  12.3 1.1 %collective-permute-done.6 = s32[4,1,20]{2,0,1:T(4,128)S(1)} collective-permute-done((s32[4,1,20]{2,0,1:T(4,128)S(1)}, s32[4,1,20]{2,0,1:T(4,128)S(1)}, u32[]{:S(2)}, u32[]{:S(2)}) %collective-permute-start.6) | collective-permute-done | bytes 352 | tf_op jit(solution)/shard_map/ppermute | solution.py:379
  13.4 1.7 %collective-permute-start.7 = (s32[4,2,20]{2,0,1:T(4,128)S(1)}, s32[4,2,20]{2,0,1:T(4,128)S(1)}, u32[]{:S(2)}, u32[]{:S(2)}) collective-permute-start(s32[4,2,20]{2,0,1:T(4,128)S(1)} %pad_add_fusion.2), channel_id=1, source_target_pairs={{0,2},{1,3},{2,0},{3,1},{4,6},{5,7},{6,4},{7,5},{8,10},{9,11},{10,... | collective-permute-start | bytes 1928 | tf_op jit(solution)/shard_map/ppermute | solution.py:379
  15.1 0.1 pad_add_fusion.5.me_ref
  15.2 0.2 shard_map.55
  15.4 6.7 %shard_map.56.source_ref = bf16[128,3968]{1,0:T(8,128)(2,1)S(1)} custom-call(bf16[128,3968]{1,0:T(8,128)(2,1)S(1)} %copy-done, bf16[11,128,3968]{2,1,0:T(8,128)(2,1)} %bitcast.45), custom_call_target="tpu_custom_call" | custom-call | flops 1 | bytes 1 | tf_op jit(solution)/shard_map/pallas_call | solution.py:20
  22.2 3.3 %shard_map.57 = (bf16[128,640]{1,0:T(8,128)(2,1)S(1)}, bf16[128,640]{1,0:T(8,128)(2,1)S(1)}, f32[240,3968]{1,0:T(8,128)S(1)}) custom-call(s32[2]{0:T(128)S(1)} %pad_add_fusion.5.me_ref, s32[2,128]{1,0:T(2,128)S(1)} %get-tuple-element.60.groups_ref, s32[16,20]{1,0:T(8,128)S(1)} %get-tuple-element.120.starts_ref, s32[16,20]{1,0:T(8,128)S(1)} %get-tuple-element.119.turns_ref, ...), custom_call_target="tpu_custom_call" | custom-call | flops 1 | bytes 1 | tf_op jit(solution)/shard_map/pallas_call | solution.py:20
  25.6 0.1 pad_maximum_fusion.refs_1_.refs_3_
  25.8 0.7 collective-permute-start.8
  26.5 2.5 %collective-permute-start.11 = (bf16[128,640]{1,0:T(8,128)(2,1)S(1)}, bf16[128,640]{1,0:T(8,128)(2,1)S(1)}, u32[]{:S(2)}, u32[]{:S(2)}) collective-permute-start(bf16[128,640]{1,0:T(8,128)(2,1)S(1)} %get-tuple-element.75), channel_id=1, source_target_pairs={{0,8},{1,9},{2,10},{3,11},{4,12},{5,13},{6,14},{7,15},{8,0},{9,1},... | collective-permute-start | bytes 491528 | tf_op jit(solution)/shard_map/ppermute | solution.py:379
  29.0 1.4 %collective-permute-start.12 = (bf16[128,640]{1,0:T(8,128)(2,1)S(1)}, bf16[128,640]{1,0:T(8,128)(2,1)S(1)}, u32[]{:S(2)}, u32[]{:S(2)}) collective-permute-start(bf16[128,640]{1,0:T(8,128)(2,1)S(1)} %get-tuple-element.76), channel_id=1, source_target_pairs={{0,12},{1,13},{2,14},{3,15},{4,8},{5,9},{6,10},{7,11},{8,4},{9,5},... | collective-permute-start | bytes 491528 | tf_op jit(solution)/shard_map/ppermute | solution.py:379
  30.4 2.7 %shard_map.58 = (bf16[128,640]{1,0:T(8,128)(2,1)S(1)}, bf16[128,640]{1,0:T(8,128)(2,1)S(1)}) custom-call(s32[2]{0:T(128)S(1)} %pad_add_fusion.5.me_ref, s32[2,128]{1,0:T(2,128)S(1)} %get-tuple-element.60.groups_ref, s32[16,20]{1,0:T(8,128)S(1)} %get-tuple-element.120.starts_ref, s32[16,20]{1,0:T(8,128)S(1)} %get-tuple-element.119.turns_ref, ...), custom_call_target="tpu_custom_call" | custom-call | flops 1 | bytes 1 | tf_op jit(solution)/shard_map/pallas_call | solution.py:20
  33.1 0.1 collective-permute-start.10
  33.3 0.1 pad_add_fusion.6.bins_ref
  33.4 0.1 slice.12.names_ref
  33.4 1.2 %shard_map.59.refs_4_ = f32[128,640]{1,0:T(8,128)S(1)} custom-call(s32[8]{0:T(128)S(1)} %pad_add_fusion.6.bins_ref, s32[4,128]{1,0:T(4,128)S(1)} %slice.12.names_ref, bf16[128,640]{1,0:T(8,128)(2,1)S(1)} %get-tuple-element.77.refs_0_, bf16[4,640,128]{2,1,0:T(8,128)(2,1)S(1)} %pad_maximum_fusion.refs_1_.refs_3_, ...), custom_call_target="tpu_custom_call" | custom-call | flops 1 | bytes 1 | tf_op jit(solution)/shard_map/pallas_call | solution.py:20
  34.6 6.9 %collective-permute-done.11.refs_1_.refs_2_ = bf16[128,640]{1,0:T(8,128)(2,1)S(1)} collective-permute-done((bf16[128,640]{1,0:T(8,128)(2,1)S(1)}, bf16[128,640]{1,0:T(8,128)(2,1)S(1)}, u32[]{:S(2)}, u32[]{:S(2)}) %collective-permute-start.11) | collective-permute-done | bytes 163872 | tf_op jit(solution)/shard_map/ppermute | solution.py:379
  41.5 1.4 %collective-permute-done.8.refs_6_ = bf16[4,640,128]{2,1,0:T(8,128)(2,1)S(1)} collective-permute-done((bf16[4,640,128]{2,1,0:T(8,128)(2,1)S(1)}, bf16[4,640,128]{2,1,0:T(8,128)(2,1)S(1)}, u32[]{:S(2)}, u32[]{:S(2)}) %collective-permute-start.8) | collective-permute-done | bytes 655392 | tf_op jit(solution)/shard_map/ppermute | solution.py:379
  42.9 1.2 %collective-permute-done.10.refs_0_.refs_1_ = bf16[128,640]{1,0:T(8,128)(2,1)S(1)} collective-permute-done((bf16[128,640]{1,0:T(8,128)(2,1)S(1)}, bf16[128,640]{1,0:T(8,128)(2,1)S(1)}, u32[]{:S(2)}, u32[]{:S(2)}) %collective-permute-start.10) | collective-permute-done | bytes 163872 | tf_op jit(solution)/shard_map/ppermute | solution.py:379
  44.1 0.1 pad_add_fusion.4.bins_ref
  44.2 1.8 %shard_map.60.refs_5_ = f32[384,640]{1,0:T(8,128)S(1)} custom-call(s32[8]{0:T(128)S(1)} %pad_add_fusion.6.bins_ref, s32[4,128]{1,0:T(4,128)S(1)} %slice.12.names_ref, bf16[128,640]{1,0:T(8,128)(2,1)S(1)} %collective-permute-done.10.refs_0_.refs_1_, bf16[128,640]{1,0:T(8,128)(2,1)S(1)} %collective-permute-done.11.refs_1_.refs_2_, ...), custom_call_target="tpu_custom_call" | custom-call | flops 1 | bytes 1 | tf_op jit(solution)/shard_map/pallas_call | solution.py:20
  46.0 0.2 collective-permute-done.13.refs_7_
  46.2 2.4 %shard_map.61 = (f32[512,640]{1,0:T(8,128)S(1)}, bf16[512,640]{1,0:T(8,128)(2,1)S(1)}, bf16[512,384]{1,0:T(8,128)(2,1)S(1)}, bf16[512,256]{1,0:T(8,128)(2,1)S(1)}, f32[4,128]{1,0:T(4,128)S(1)}) custom-call(s32[1]{0:T(128)} %bitcast.1.outer_ref, s32[8]{0:T(128)S(1)} %pad_add_fusion.4.bins_ref, s32[4,128]{1,0:T(4,128)S(1)} %slice.12.names_ref, ...), custom_call_target="tpu_custom_call" | custom-call | flops 1 | bytes 1 | tf_op jit(solution)/shard_map/pallas_call | solution.py:20
  48.6 0.8 collective-permute-start.17
  49.5 3.2 %collective-permute-start.14 = (f32[4,128]{1,0:T(4,128)S(1)}, f32[4,128]{1,0:T(4,128)S(1)}, u32[]{:S(2)}, u32[]{:S(2)}) collective-permute-start(f32[4,128]{1,0:T(4,128)S(1)} %get-tuple-element.84), channel_id=1, source_target_pairs={{0,4},{1,5},{2,6},{3,7},{4,0},{5,1},{6,2},{7,3},{8,12},{9,13},{10,... | collective-permute-start | bytes 6152 | tf_op jit(solution)/shard_map/ppermute | solution.py:379
  52.7 0.7 collective-permute-start.15
  53.4 1.7 %collective-permute-start.16 = (f32[4,128]{1,0:T(4,128)S(1)}, f32[4,128]{1,0:T(4,128)S(1)}, u32[]{:S(2)}, u32[]{:S(2)}) collective-permute-start(f32[4,128]{1,0:T(4,128)S(1)} %get-tuple-element.84), channel_id=1, source_target_pairs={{0,12},{1,13},{2,14},{3,15},{4,8},{5,9},{6,10},{7,11},{8,4},{9,5},... | collective-permute-start | bytes 6152 | tf_op jit(solution)/shard_map/ppermute | solution.py:379
  55.0 1.1 %collective-permute-start.18 = (bf16[512,256]{1,0:T(8,128)(2,1)S(1)}, bf16[512,256]{1,0:T(8,128)(2,1)S(1)}, u32[]{:S(2)}, u32[]{:S(2)}) collective-permute-start(bf16[512,256]{1,0:T(8,128)(2,1)S(1)} %get-tuple-element.88), channel_id=1, source_target_pairs={{0,4},{1,5},{2,6},{3,7},{4,12},{5,13},{6,14},{7,15},{8,0},{9,1},{1... | collective-permute-start | bytes 786440 | tf_op jit(solution)/shard_map/ppermute | solution.py:386
  56.2 2.8 %collective-permute-done.14 = f32[4,128]{1,0:T(4,128)S(1)} collective-permute-done((f32[4,128]{1,0:T(4,128)S(1)}, f32[4,128]{1,0:T(4,128)S(1)}, u32[]{:S(2)}, u32[]{:S(2)}) %collective-permute-start.14) | collective-permute-done | bytes 2080 | tf_op jit(solution)/shard_map/ppermute | solution.py:379
  59.0 2.6 %collective-permute-done.15 = f32[4,128]{1,0:T(4,128)S(1)} collective-permute-done((f32[4,128]{1,0:T(4,128)S(1)}, f32[4,128]{1,0:T(4,128)S(1)}, u32[]{:S(2)}, u32[]{:S(2)}) %collective-permute-start.15) | collective-permute-done | bytes 2080 | tf_op jit(solution)/shard_map/ppermute | solution.py:379
  61.6 1.3 %collective-permute-done.16 = f32[4,128]{1,0:T(4,128)S(1)} collective-permute-done((f32[4,128]{1,0:T(4,128)S(1)}, f32[4,128]{1,0:T(4,128)S(1)}, u32[]{:S(2)}, u32[]{:S(2)}) %collective-permute-start.16) | collective-permute-done | bytes 2080 | tf_op jit(solution)/shard_map/ppermute | solution.py:379
  62.9 0.2 shard_map.62.refs_0_.refs_2_
  63.1 0.8 shard_map.63
  63.9 2.9 %collective-permute-done.18.refs_1_ = bf16[512,256]{1,0:T(8,128)(2,1)S(1)} collective-permute-done((bf16[512,256]{1,0:T(8,128)(2,1)S(1)}, bf16[512,256]{1,0:T(8,128)(2,1)S(1)}, u32[]{:S(2)}, u32[]{:S(2)}) %collective-permute-start.18) | collective-permute-done | bytes 262176 | tf_op jit(solution)/shard_map/ppermute | solution.py:386
  66.8 0.9 shard_map.64
  67.6 0.1 collective-permute-start.22
  67.7 0.6 collective-permute-start.19
  68.3 0.2 collective-permute-start.20
  68.5 0.9 collective-permute-done.22.got_ref
  69.4 0.1 shard_map.66
  69.5 0.8 shard_map.67
  70.3 0.2 collective-permute-start.23
  70.5 1.4 %collective-permute-start.25 = (bf16[1,160,640]{2,1,0:T(8,128)(2,1)S(1)}, bf16[1,160,640]{2,1,0:T(8,128)(2,1)S(1)}, u32[]{:S(2)}, u32[]{:S(2)}) collective-permute-start(bf16[1,160,640]{2,1,0:T(8,128)(2,1)S(1)} %get-tuple-element.103), channel_id=1, source_target_pairs={{0,2},{1,3},{2,0},{3,1},{4,6},{5,7},{6,4},{7,5},{8,10},{9,11},{10,... | collective-permute-start | bytes 614408 | tf_op jit(solution)/shard_map/ppermute | solution.py:379
  72.0 0.7 collective-permute-start.21
  72.8 1.5 %collective-permute-start.24 = (bf16[1,160,640]{2,1,0:T(8,128)(2,1)S(1)}, bf16[1,160,640]{2,1,0:T(8,128)(2,1)S(1)}, u32[]{:S(2)}, u32[]{:S(2)}) collective-permute-start(bf16[1,160,640]{2,1,0:T(8,128)(2,1)S(1)} %get-tuple-element.102), channel_id=1, source_target_pairs={{0,2},{1,3},{2,0},{3,1},{4,6},{5,7},{6,4},{7,5},{8,10},{9,11},{10,... | collective-permute-start | bytes 614408 | tf_op jit(solution)/shard_map/ppermute | solution.py:379
  74.3 4.2 %collective-permute-done.25 = bf16[1,160,640]{2,1,0:T(8,128)(2,1)S(1)} collective-permute-done((bf16[1,160,640]{2,1,0:T(8,128)(2,1)S(1)}, bf16[1,160,640]{2,1,0:T(8,128)(2,1)S(1)}, u32[]{:S(2)}, u32[]{:S(2)}) %collective-permute-start.25) | collective-permute-done | bytes 204832 | tf_op jit(solution)/shard_map/ppermute | solution.py:379
  78.5 4.4 %collective-permute-done.21 = bf16[1,160,640]{2,1,0:T(8,128)(2,1)S(1)} collective-permute-done((bf16[1,160,640]{2,1,0:T(8,128)(2,1)S(1)}, bf16[1,160,640]{2,1,0:T(8,128)(2,1)S(1)}, u32[]{:S(2)}, u32[]{:S(2)}) %collective-permute-start.21) | collective-permute-done | bytes 204832 | tf_op jit(solution)/shard_map/ppermute | solution.py:379
  82.8 2.9 %collective-permute-done.19.refs_1_ = bf16[512,640]{1,0:T(8,128)(2,1)S(1)} collective-permute-done((bf16[512,640]{1,0:T(8,128)(2,1)S(1)}, bf16[512,640]{1,0:T(8,128)(2,1)S(1)}, u32[]{:S(2)}, u32[]{:S(2)}) %collective-permute-start.19) | collective-permute-done | bytes 655392 | tf_op jit(solution)/shard_map/ppermute | solution.py:386
  85.7 0.9 collective-permute-done.24
  86.7 0.8 shard_map.69
  87.5 0.1 collective-permute-start.26
  87.6 1.7 %collective-permute-start.28 = (bf16[160,640]{1,0:T(8,128)(2,1)S(1)}, bf16[160,640]{1,0:T(8,128)(2,1)S(1)}, u32[]{:S(2)}, u32[]{:S(2)}) collective-permute-start(bf16[160,640]{1,0:T(8,128)(2,1)S(1)} %fusion), channel_id=1, source_target_pairs={{0,8},{1,9},{2,10},{3,11},{4,0},{5,1},{6,2},{7,3},{8,12},{9,13},{1... | collective-permute-start | bytes 614408 | tf_op jit(solution)/shard_map/ppermute | solution.py:386
  89.5 1.4 %collective-permute-start.27 = (bf16[1,160,640]{2,1,0:T(8,128)(2,1)S(1)}, bf16[1,160,640]{2,1,0:T(8,128)(2,1)S(1)}, u32[]{:S(2)}, u32[]{:S(2)}) collective-permute-start(bf16[1,160,640]{2,1,0:T(8,128)(2,1)S(1)} %get-tuple-element.108), channel_id=1, source_target_pairs={{0,2},{1,3},{2,0},{3,1},{4,6},{5,7},{6,4},{7,5},{8,10},{9,11},{10,... | collective-permute-start | bytes 614408 | tf_op jit(solution)/shard_map/ppermute | solution.py:379
  90.9 1.5 %shard_map.71.refs_4_ = f32[160,2560]{1,0:T(8,128)} custom-call(s32[4]{0:T(128)S(1)} %shift-right-arithmetic_xor_fusion.at_ref, f32[160,640]{1,0:T(8,128)S(1)} %bitcast.39, bf16[160,640]{1,0:T(8,128)(2,1)S(1)} %bitcast.42, f32[160,640]{1,0:T(8,128)S(1)} %bitcast.40, bf16[160,640]{1,0:T(8,128)(2,1)S(1)} %bitcast.43), custom_call_target="tpu_custom_call" | custom-call | flops 1 | bytes 1 | tf_op jit(solution)/shard_map/pallas_call | solution.py:353
  92.4 3.5 %collective-permute-done.28.refs_2_ = bf16[160,640]{1,0:T(8,128)(2,1)S(1)} collective-permute-done((bf16[160,640]{1,0:T(8,128)(2,1)S(1)}, bf16[160,640]{1,0:T(8,128)(2,1)S(1)}, u32[]{:S(2)}, u32[]{:S(2)}) %collective-permute-start.28) | collective-permute-done | bytes 204832 | tf_op jit(solution)/shard_map/ppermute | solution.py:386
  95.9 0.9 collective-permute-done.27
  96.7 1.5 %shard_map.72 = f32[160,2560]{1,0:T(8,128)} custom-call(s32[4]{0:T(128)S(1)} %shift-right-arithmetic_xor_fusion.at_ref, f32[160,640]{1,0:T(8,128)S(1)} %bitcast.41, bf16[160,640]{1,0:T(8,128)(2,1)S(1)} %bitcast.44, bf16[160,640]{1,0:T(8,128)(2,1)S(1)} %collective-permute-done.28.refs_2_, ...), custom_call_target="tpu_custom_call", output_to_operand_aliasing={{}: (5, {})} | custom-call | flops 1 | bytes 1 | tf_op jit(solution)/shard_map/pallas_call | solution.py:353
  (35 shorter events, 0.5 us)
Async XLA Ops:
  0.0 15.4 %copy-start = (bf16[128,3968]{1,0:T(8,128)(2,1)S(1)}, bf16[128,3968]{1,0:T(8,128)(2,1)}, u32[]{:S(2)}) copy-start(bf16[128,3968]{1,0:T(8,128)(2,1)} %flux_ref) | copy-start | bytes 3047428
  0.8 11.3 %collective-permute-start = (s32[148]{0:T(256)S(1)}, s32[148]{0:T(256)S(1)}, u32[]{:S(2)}, u32[]{:S(2)}) collective-permute-start(s32[148]{0:T(256)S(1)} %pad_add_fusion.3), channel_id=1, source_target_pairs={{0,4},{1,5},{2,6},{3,7},{4,0},{5,1},{6,2},{7,3},{8,12},{9,13},{10,... | collective-permute-start | bytes 1784 | tf_op jit(solution)/shard_map/ppermute | solution.py:379
  3.9 8.3 %collective-permute-start.1 = (s32[148]{0:T(256)S(1)}, s32[148]{0:T(256)S(1)}, u32[]{:S(2)}, u32[]{:S(2)}) collective-permute-start(s32[148]{0:T(256)S(1)} %pad_add_fusion.3), channel_id=1, source_target_pairs={{0,8},{1,9},{2,10},{3,11},{4,12},{5,13},{6,14},{7,15},{8,0},{9,1},... | collective-permute-start | bytes 1784 | tf_op jit(solution)/shard_map/ppermute | solution.py:379
  6.4 5.7 %collective-permute-start.2 = (s32[148]{0:T(256)S(1)}, s32[148]{0:T(256)S(1)}, u32[]{:S(2)}, u32[]{:S(2)}) collective-permute-start(s32[148]{0:T(256)S(1)} %pad_add_fusion.3), channel_id=1, source_target_pairs={{0,12},{1,13},{2,14},{3,15},{4,8},{5,9},{6,10},{7,11},{8,4},{9,5},... | collective-permute-start | bytes 1784 | tf_op jit(solution)/shard_map/ppermute | solution.py:379
  7.7 17.9 %collective-permute-start.3 = (bf16[640,128]{1,0:T(8,128)(2,1)S(1)}, bf16[640,128]{1,0:T(8,128)(2,1)S(1)}, u32[]{:S(2)}, u32[]{:S(2)}) collective-permute-start(bf16[640,128]{1,0:T(8,128)(2,1)S(1)} %get-tuple-element.117), channel_id=1, source_target_pairs={{0,4},{1,5},{2,6},{3,7},{4,0},{5,1},{6,2},{7,3},{8,12},{9,13},{10,... | collective-permute-start | bytes 491528 | tf_op jit(solution)/shard_map/ppermute | solution.py:379
  8.6 17.0 %collective-permute-start.4 = (bf16[640,128]{1,0:T(8,128)(2,1)S(1)}, bf16[640,128]{1,0:T(8,128)(2,1)S(1)}, u32[]{:S(2)}, u32[]{:S(2)}) collective-permute-start(bf16[640,128]{1,0:T(8,128)(2,1)S(1)} %get-tuple-element.116), channel_id=1, source_target_pairs={{0,8},{1,9},{2,10},{3,11},{4,12},{5,13},{6,14},{7,15},{8,0},{9,1},... | collective-permute-start | bytes 491528 | tf_op jit(solution)/shard_map/ppermute | solution.py:379
  12.1 13.5 %collective-permute-start.5 = (bf16[640,128]{1,0:T(8,128)(2,1)S(1)}, bf16[640,128]{1,0:T(8,128)(2,1)S(1)}, u32[]{:S(2)}, u32[]{:S(2)}) collective-permute-start(bf16[640,128]{1,0:T(8,128)(2,1)S(1)} %get-tuple-element.115), channel_id=1, source_target_pairs={{0,12},{1,13},{2,14},{3,15},{4,8},{5,9},{6,10},{7,11},{8,4},{9,5},... | collective-permute-start | bytes 491528 | tf_op jit(solution)/shard_map/ppermute | solution.py:379
  12.2 1.2 %collective-permute-start.6 = (s32[4,1,20]{2,0,1:T(4,128)S(1)}, s32[4,1,20]{2,0,1:T(4,128)S(1)}, u32[]{:S(2)}, u32[]{:S(2)}) collective-permute-start(s32[4,1,20]{2,0,1:T(4,128)S(1)} %slice_bitcast_fusion), channel_id=1, source_target_pairs={{0,1},{1,0},{2,3},{3,2},{4,5},{5,4},{6,7},{7,6},{8,9},{9,8},{10,11... | collective-permute-start | bytes 968 | tf_op jit(solution)/shard_map/ppermute | solution.py:379
  13.4 8.8 %collective-permute-start.7 = (s32[4,2,20]{2,0,1:T(4,128)S(1)}, s32[4,2,20]{2,0,1:T(4,128)S(1)}, u32[]{:S(2)}, u32[]{:S(2)}) collective-permute-start(s32[4,2,20]{2,0,1:T(4,128)S(1)} %pad_add_fusion.2), channel_id=1, source_target_pairs={{0,2},{1,3},{2,0},{3,1},{4,6},{5,7},{6,4},{7,5},{8,10},{9,11},{10,... | collective-permute-start | bytes 1928 | tf_op jit(solution)/shard_map/ppermute | solution.py:379
  25.7 4.7 %collective-permute-start.9 = (bf16[4,640,128]{2,1,0:T(8,128)(2,1)S(1)}, bf16[4,640,128]{2,1,0:T(8,128)(2,1)S(1)}, u32[]{:S(2)}, u32[]{:S(2)}) collective-permute-start(bf16[4,640,128]{2,1,0:T(8,128)(2,1)S(1)} %pad_maximum_fusion.refs_1_.refs_3_), channel_id=1, source_target_pairs={{0,1},{1,0},{2,3},{3,2},{4,5},{5,4},{6,7},{7,6},{8,9},{9,8},{10,11... | collective-permute-start | bytes 1966088 | tf_op jit(solution)/shard_map/ppermute | solution.py:379
  25.8 17.1 %collective-permute-start.8 = (bf16[4,640,128]{2,1,0:T(8,128)(2,1)S(1)}, bf16[4,640,128]{2,1,0:T(8,128)(2,1)S(1)}, u32[]{:S(2)}, u32[]{:S(2)}) collective-permute-start(bf16[4,640,128]{2,1,0:T(8,128)(2,1)S(1)} %pad_maximum_fusion.refs_1_.refs_3_), channel_id=1, source_target_pairs={{0,2},{1,3},{2,0},{3,1},{4,6},{5,7},{6,4},{7,5},{8,10},{9,11},{10,... | collective-permute-start | bytes 1966088 | tf_op jit(solution)/shard_map/ppermute | solution.py:379
  26.5 15.0 %collective-permute-start.11 = (bf16[128,640]{1,0:T(8,128)(2,1)S(1)}, bf16[128,640]{1,0:T(8,128)(2,1)S(1)}, u32[]{:S(2)}, u32[]{:S(2)}) collective-permute-start(bf16[128,640]{1,0:T(8,128)(2,1)S(1)} %get-tuple-element.75), channel_id=1, source_target_pairs={{0,8},{1,9},{2,10},{3,11},{4,12},{5,13},{6,14},{7,15},{8,0},{9,1},... | collective-permute-start | bytes 491528 | tf_op jit(solution)/shard_map/ppermute | solution.py:379
  29.0 12.5 %collective-permute-start.12 = (bf16[128,640]{1,0:T(8,128)(2,1)S(1)}, bf16[128,640]{1,0:T(8,128)(2,1)S(1)}, u32[]{:S(2)}, u32[]{:S(2)}) collective-permute-start(bf16[128,640]{1,0:T(8,128)(2,1)S(1)} %get-tuple-element.76), channel_id=1, source_target_pairs={{0,12},{1,13},{2,14},{3,15},{4,8},{5,9},{6,10},{7,11},{8,4},{9,5},... | collective-permute-start | bytes 491528 | tf_op jit(solution)/shard_map/ppermute | solution.py:379
  33.1 11.0 %collective-permute-start.10 = (bf16[128,640]{1,0:T(8,128)(2,1)S(1)}, bf16[128,640]{1,0:T(8,128)(2,1)S(1)}, u32[]{:S(2)}, u32[]{:S(2)}) collective-permute-start(bf16[128,640]{1,0:T(8,128)(2,1)S(1)} %get-tuple-element.74), channel_id=1, source_target_pairs={{0,4},{1,5},{2,6},{3,7},{4,0},{5,1},{6,2},{7,3},{8,12},{9,13},{10,... | collective-permute-start | bytes 491528 | tf_op jit(solution)/shard_map/ppermute | solution.py:379
  44.1 2.1 %collective-permute-start.13 = (bf16[4,640,128]{2,1,0:T(8,128)(2,1)S(1)}, bf16[4,640,128]{2,1,0:T(8,128)(2,1)S(1)}, u32[]{:S(2)}, u32[]{:S(2)}) collective-permute-start(bf16[4,640,128]{2,1,0:T(8,128)(2,1)S(1)} %collective-permute-done.8.refs_6_), channel_id=1, source_target_pairs={{0,1},{1,0},{2,3},{3,2},{4,5},{5,4},{6,7},{7,6},{8,9},{9,8},{10,11... | collective-permute-start | bytes 1966088 | tf_op jit(solution)/shard_map/ppermute | solution.py:379
  48.6 14.2 %collective-permute-start.17 = (bf16[512,384]{1,0:T(8,128)(2,1)S(1)}, bf16[512,384]{1,0:T(8,128)(2,1)S(1)}, u32[]{:S(2)}, u32[]{:S(2)}) collective-permute-start(bf16[512,384]{1,0:T(8,128)(2,1)S(1)} %get-tuple-element.85), channel_id=1, source_target_pairs={{0,4},{1,5},{2,6},{3,7},{4,12},{5,13},{6,14},{7,15},{8,0},{9,1},{1... | collective-permute-start | bytes 1179656 | tf_op jit(solution)/shard_map/ppermute | solution.py:386
  49.5 9.5 %collective-permute-start.14 = (f32[4,128]{1,0:T(4,128)S(1)}, f32[4,128]{1,0:T(4,128)S(1)}, u32[]{:S(2)}, u32[]{:S(2)}) collective-permute-start(f32[4,128]{1,0:T(4,128)S(1)} %get-tuple-element.84), channel_id=1, source_target_pairs={{0,4},{1,5},{2,6},{3,7},{4,0},{5,1},{6,2},{7,3},{8,12},{9,13},{10,... | collective-permute-start | bytes 6152 | tf_op jit(solution)/shard_map/ppermute | solution.py:379
  52.7 8.9 %collective-permute-start.15 = (f32[4,128]{1,0:T(4,128)S(1)}, f32[4,128]{1,0:T(4,128)S(1)}, u32[]{:S(2)}, u32[]{:S(2)}) collective-permute-start(f32[4,128]{1,0:T(4,128)S(1)} %get-tuple-element.84), channel_id=1, source_target_pairs={{0,8},{1,9},{2,10},{3,11},{4,12},{5,13},{6,14},{7,15},{8,0},{9,1},... | collective-permute-start | bytes 6152 | tf_op jit(solution)/shard_map/ppermute | solution.py:379
  53.4 9.5 %collective-permute-start.16 = (f32[4,128]{1,0:T(4,128)S(1)}, f32[4,128]{1,0:T(4,128)S(1)}, u32[]{:S(2)}, u32[]{:S(2)}) collective-permute-start(f32[4,128]{1,0:T(4,128)S(1)} %get-tuple-element.84), channel_id=1, source_target_pairs={{0,12},{1,13},{2,14},{3,15},{4,8},{5,9},{6,10},{7,11},{8,4},{9,5},... | collective-permute-start | bytes 6152 | tf_op jit(solution)/shard_map/ppermute | solution.py:379
  55.0 11.7 %collective-permute-start.18 = (bf16[512,256]{1,0:T(8,128)(2,1)S(1)}, bf16[512,256]{1,0:T(8,128)(2,1)S(1)}, u32[]{:S(2)}, u32[]{:S(2)}) collective-permute-start(bf16[512,256]{1,0:T(8,128)(2,1)S(1)} %get-tuple-element.88), channel_id=1, source_target_pairs={{0,4},{1,5},{2,6},{3,7},{4,12},{5,13},{6,14},{7,15},{8,0},{9,1},{1... | collective-permute-start | bytes 786440 | tf_op jit(solution)/shard_map/ppermute | solution.py:386
  67.6 1.8 %collective-permute-start.22 = (bf16[2,160,640]{2,1,0:T(8,128)(2,1)S(1)}, bf16[2,160,640]{2,1,0:T(8,128)(2,1)S(1)}, u32[]{:S(2)}, u32[]{:S(2)}) collective-permute-start(bf16[2,160,640]{2,1,0:T(8,128)(2,1)S(1)} %get-tuple-element.97), channel_id=1, source_target_pairs={{0,1},{1,0},{2,3},{3,2},{4,5},{5,4},{6,7},{7,6},{8,9},{9,8},{10,11... | collective-permute-start | bytes 1228808 | tf_op jit(solution)/shard_map/ppermute | solution.py:379
  67.7 18.0 %collective-permute-start.19 = (bf16[512,640]{1,0:T(8,128)(2,1)S(1)}, bf16[512,640]{1,0:T(8,128)(2,1)S(1)}, u32[]{:S(2)}, u32[]{:S(2)}) collective-permute-start(bf16[512,640]{1,0:T(8,128)(2,1)S(1)} %get-tuple-element.99.refs_1_), channel_id=1, source_target_pairs={{0,4},{1,5},{2,6},{3,7},{4,12},{5,13},{6,14},{7,15},{8,0},{9,1},{1... | collective-permute-start | bytes 1966088 | tf_op jit(solution)/shard_map/ppermute | solution.py:386
  68.3 3.6 %collective-permute-start.20 = (bf16[2,160,640]{2,1,0:T(8,128)(2,1)S(1)}, bf16[2,160,640]{2,1,0:T(8,128)(2,1)S(1)}, u32[]{:S(2)}, u32[]{:S(2)}) collective-permute-start(bf16[2,160,640]{2,1,0:T(8,128)(2,1)S(1)} %get-tuple-element.94), channel_id=1, source_target_pairs={{0,1},{1,0},{2,3},{3,2},{4,5},{5,4},{6,7},{7,6},{8,9},{9,8},{10,11... | collective-permute-start | bytes 1228808 | tf_op jit(solution)/shard_map/ppermute | solution.py:379
  70.3 2.4 %collective-permute-start.23 = (bf16[2,160,640]{2,1,0:T(8,128)(2,1)S(1)}, bf16[2,160,640]{2,1,0:T(8,128)(2,1)S(1)}, u32[]{:S(2)}, u32[]{:S(2)}) collective-permute-start(bf16[2,160,640]{2,1,0:T(8,128)(2,1)S(1)} %get-tuple-element.101), channel_id=1, source_target_pairs={{0,1},{1,0},{2,3},{3,2},{4,5},{5,4},{6,7},{7,6},{8,9},{9,8},{10,11... | collective-permute-start | bytes 1228808 | tf_op jit(solution)/shard_map/ppermute | solution.py:379
  70.5 7.9 %collective-permute-start.25 = (bf16[1,160,640]{2,1,0:T(8,128)(2,1)S(1)}, bf16[1,160,640]{2,1,0:T(8,128)(2,1)S(1)}, u32[]{:S(2)}, u32[]{:S(2)}) collective-permute-start(bf16[1,160,640]{2,1,0:T(8,128)(2,1)S(1)} %get-tuple-element.103), channel_id=1, source_target_pairs={{0,2},{1,3},{2,0},{3,1},{4,6},{5,7},{6,4},{7,5},{8,10},{9,11},{10,... | collective-permute-start | bytes 614408 | tf_op jit(solution)/shard_map/ppermute | solution.py:379
  72.0 10.8 %collective-permute-start.21 = (bf16[1,160,640]{2,1,0:T(8,128)(2,1)S(1)}, bf16[1,160,640]{2,1,0:T(8,128)(2,1)S(1)}, u32[]{:S(2)}, u32[]{:S(2)}) collective-permute-start(bf16[1,160,640]{2,1,0:T(8,128)(2,1)S(1)} %get-tuple-element.95), channel_id=1, source_target_pairs={{0,2},{1,3},{2,0},{3,1},{4,6},{5,7},{6,4},{7,5},{8,10},{9,11},{10,... | collective-permute-start | bytes 614408 | tf_op jit(solution)/shard_map/ppermute | solution.py:379
  72.8 13.9 %collective-permute-start.24 = (bf16[1,160,640]{2,1,0:T(8,128)(2,1)S(1)}, bf16[1,160,640]{2,1,0:T(8,128)(2,1)S(1)}, u32[]{:S(2)}, u32[]{:S(2)}) collective-permute-start(bf16[1,160,640]{2,1,0:T(8,128)(2,1)S(1)} %get-tuple-element.102), channel_id=1, source_target_pairs={{0,2},{1,3},{2,0},{3,1},{4,6},{5,7},{6,4},{7,5},{8,10},{9,11},{10,... | collective-permute-start | bytes 614408 | tf_op jit(solution)/shard_map/ppermute | solution.py:379
  87.5 1.9 %collective-permute-start.26 = (bf16[2,160,640]{2,1,0:T(8,128)(2,1)S(1)}, bf16[2,160,640]{2,1,0:T(8,128)(2,1)S(1)}, u32[]{:S(2)}, u32[]{:S(2)}) collective-permute-start(bf16[2,160,640]{2,1,0:T(8,128)(2,1)S(1)} %get-tuple-element.106), channel_id=1, source_target_pairs={{0,1},{1,0},{2,3},{3,2},{4,5},{5,4},{6,7},{7,6},{8,9},{9,8},{10,11... | collective-permute-start | bytes 1228808 | tf_op jit(solution)/shard_map/ppermute | solution.py:379
  87.6 8.2 %collective-permute-start.28 = (bf16[160,640]{1,0:T(8,128)(2,1)S(1)}, bf16[160,640]{1,0:T(8,128)(2,1)S(1)}, u32[]{:S(2)}, u32[]{:S(2)}) collective-permute-start(bf16[160,640]{1,0:T(8,128)(2,1)S(1)} %fusion), channel_id=1, source_target_pairs={{0,8},{1,9},{2,10},{3,11},{4,0},{5,1},{6,2},{7,3},{8,12},{9,13},{1... | collective-permute-start | bytes 614408 | tf_op jit(solution)/shard_map/ppermute | solution.py:386
  89.5 7.3 %collective-permute-start.27 = (bf16[1,160,640]{2,1,0:T(8,128)(2,1)S(1)}, bf16[1,160,640]{2,1,0:T(8,128)(2,1)S(1)}, u32[]{:S(2)}, u32[]{:S(2)}) collective-permute-start(bf16[1,160,640]{2,1,0:T(8,128)(2,1)S(1)} %get-tuple-element.108), channel_id=1, source_target_pairs={{0,2},{1,3},{2,0},{3,1},{4,6},{5,7},{6,4},{7,5},{8,10},{9,11},{10,... | collective-permute-start | bytes 614408 | tf_op jit(solution)/shard_map/ppermute | solution.py:379

commit v18 on v15

--- a/solution.py
+++ b/solution.py
@@ -182,11 +182,11 @@
     )
 
 
-def masked_rest(windows, names, bins_ref, weights, band, window, named_ref, value_ref, begun):
+def masked_rest(windows, names, bins_ref, weights, band, columns, window, named_ref, value_ref, begun):
     count = windows[0].shape[0]
     for i in range(len(windows)):
         own = slice(i * count, (i + 1) * count)
-        window[own, :] = windows[i][...]
+        window[own, :] = windows[i][:, columns[0] : columns[1]]
         named_ref[own, :] = jnp.broadcast_to(names[i], (band, count)).T
     named = named_ref[...]
     for p in range(len(weights)):
@@ -196,26 +196,27 @@
         ]
         for at in range(0, window.shape[1], band):
             lanes = slice(at, at + band)
+            rows = slice(columns[0] + at, columns[0] + at + band)
             masked = jnp.concatenate([window[:, lanes] * hit for hit in hits], axis=1)
-            columns = jnp.concatenate([weights[p][b, lanes, :] for b in range(OUTER)], axis=1)
-            value = lax.dot_general(masked, columns, (((1,), (1,)), ((), ())), preferred_element_type=F32)
+            weight = jnp.concatenate([weights[p][b, rows, :] for b in range(OUTER)], axis=1)
+            value = lax.dot_general(masked, weight, (((1,), (1,)), ((), ())), preferred_element_type=F32)
             if p or begun:
                 value = value + value_ref[:, lanes]
             value_ref[:, lanes] = value
 
 
-def begin_kernel(aways, npieces, band, bins_ref, names_ref, *refs):
+def begin_kernel(aways, npieces, band, columns, bins_ref, names_ref, *refs):
     windows, weights = refs[: len(aways)], refs[len(aways) : len(aways) + npieces]
     value_ref, window, named_ref = refs[len(aways) + npieces :]
     names = [names_ref[away : away + 1, :].astype(F32) for away in aways]
-    masked_rest(windows, names, bins_ref, weights, band, window, named_ref, value_ref, False)
-
-
-def begin_rest(bins, names, aways, windows, weights, band):
-    count, width = windows[0].shape
-    rows = len(aways) * count
-    return call(
-        functools.partial(begin_kernel, aways, len(weights), band),
+    masked_rest(windows, names, bins_ref, weights, band, columns, window, named_ref, value_ref, False)
+
+
+def begin_rest(bins, names, aways, windows, weights, columns, band):
+    count = windows[0].shape[0]
+    rows, width = len(aways) * count, columns[1] - columns[0]
+    return call(
+        functools.partial(begin_kernel, aways, len(weights), band, columns),
         jax.ShapeDtypeStruct((rows, width), F32),
         [SMEM] + [VMEM] * (1 + len(aways) + len(weights)),
         (bins, names, *windows, *weights),
@@ -223,17 +224,14 @@
     )
 
 
-def end_kernel(nbegun, npieces, band, outer_ref, bins_ref, names_ref, *refs):
-    windows, begun, weights = refs[:OUTER], refs[OUTER : OUTER + nbegun], refs[OUTER + nbegun : OUTER + nbegun + npieces]
-    rest_ref, sent_ref, *sents, squares_ref, window, named_ref, value_ref = refs[OUTER + nbegun + npieces :]
-    split = sents[0].shape[1]
-    count, width = windows[0].shape
-    row = 0
-    for part in begun:
-        value_ref[row : row + part.shape[0], :] = part[...]
-        row += part.shape[0]
+def end_kernel(npieces, band, columns, outer_ref, bins_ref, names_ref, *refs):
+    windows, (own_ref, others_ref), refs = refs[:OUTER], refs[OUTER : OUTER + 2], refs[OUTER + 2 :]
+    weights, (rest_ref, sent_ref, squares_ref, window, named_ref, value_ref) = refs[:npieces], refs[npieces:]
+    count, width = windows[0].shape[0], columns[1] - columns[0]
+    value_ref[:count, :] = own_ref[:, columns[0] : columns[1]]
+    value_ref[count:, :] = others_ref[...]
     names = [names_ref[away : away + 1, :].astype(F32) for away in range(OUTER)]
-    masked_rest(windows, names, bins_ref, weights, band, window, named_ref, value_ref, True)
+    masked_rest(windows, names, bins_ref, weights, band, columns, window, named_ref, value_ref, True)
     for away in range(OUTER):
         own = slice(away * count, (away + 1) * count)
         place = outer_ref[0] ^ away
@@ -243,50 +241,52 @@
             value = value_ref[own, at : at + band]
             rest_ref[rows, at : at + band] = value
             sent_ref[rows, at : at + band] = value.astype(BF16)
-            part = int(at >= split)
-            sents[part][rows, at - part * split : at - part * split + band] = value.astype(BF16)
             total = total + value * value
         squares_ref[pl.ds(place, 1), :] = jnp.sum(total.T, axis=0, keepdims=True)
 
 
-def end_rest(outer, bins, names, windows, begun, weights, band):
-    count, width = windows[0].shape
-    rows = OUTER * count
-    split = (width // band + 1) // 2 * band
-    return call(
-        functools.partial(end_kernel, len(begun), len(weights), band),
+def end_rest(outer, bins, names, windows, own, others, weights, columns, band):
+    count = windows[0].shape[0]
+    rows, width = OUTER * count, columns[1] - columns[0]
+    return call(
+        functools.partial(end_kernel, len(weights), band, columns),
         (
             jax.ShapeDtypeStruct((rows, width), F32),
             jax.ShapeDtypeStruct((rows, width), BF16),
-            jax.ShapeDtypeStruct((rows, split), BF16),
-            jax.ShapeDtypeStruct((rows, width - split), BF16),
             jax.ShapeDtypeStruct((OUTER, count), F32),
         ),
-        [SMEM, SMEM] + [VMEM] * (1 + OUTER + len(begun) + len(weights)),
-        (outer, bins, names, *windows, *begun, *weights),
+        [SMEM, SMEM] + [VMEM] * (1 + OUTER + 2 + len(weights)),
+        (outer, bins, names, *windows, own, others, *weights),
         [pltpu.VMEM((rows, width), BF16), pltpu.VMEM((rows, band), F32), pltpu.VMEM((rows, width), F32)],
     )
 
 
-def scale_kernel(rest_ref, factor_ref, out_ref):
+def scale_kernel(nparts, *refs):
+    parts, factor_ref, out_ref = refs[:nparts], refs[nparts], refs[nparts + 1]
     outers, count = factor_ref.shape
-    width = rest_ref.shape[1]
     for outer in range(outers):
         own = slice(outer * count, (outer + 1) * count)
         factor = jnp.broadcast_to(factor_ref[outer : outer + 1, :], (128, count)).T
-        for at in range(0, width, 128):
-            out_ref[own, at : at + 128] = (rest_ref[own, at : at + 128] * factor).astype(BF16)
-
-
-def product_kernel(ntall, q_ref, *refs):
-    talls, wide_ref, (send_ref, keep_ref, *joined_ref, value) = refs[:ntall], refs[ntall], refs[ntall + 1 :]
+        column = 0
+        for part in parts:
+            for at in range(0, part.shape[1], 128):
+                out_ref[own, column : column + 128] = (part[own, at : at + 128] * factor).astype(BF16)
+                column += 128
+
+
+def product_kernel(ntall, nwide, q_ref, *refs):
+    talls, wides, refs = refs[:ntall], refs[ntall : ntall + nwide], refs[ntall + nwide :]
+    send_ref, keep_ref, *joined_ref, value = refs
     pairs, share, _ = keep_ref.shape
     row = 0
     for tall in talls:
         rows = slice(row, row + tall.shape[1])
-        value[rows, :] = lax.dot_general(
-            tall[...], wide_ref[...], (((0,), (0,)), ((), ())), preferred_element_type=F32
-        )
+        column = 0
+        for wide in wides:
+            value[rows, column : column + wide.shape[1]] = lax.dot_general(
+                tall[...], wide[...], (((0,), (0,)), ((), ())), preferred_element_type=F32
+            )
+            column += wide.shape[1]
         if joined_ref:
             joined_ref[0][:, rows] = tall[...]
         row += tall.shape[1]
@@ -298,16 +298,16 @@
             keep_ref[e // 2] = own
 
 
-def product(q, talls, wide, inner, join=False):
+def product(q, talls, wides, inner, join=False):
     rows = sum(tall.shape[1] for tall in talls)
-    columns = wide.shape[1]
+    columns = sum(wide.shape[1] for wide in wides)
     shape = (inner // 2, rows // inner, columns)
-    joined = (jax.ShapeDtypeStruct((wide.shape[0], rows), BF16),) if join else ()
-    return call(
-        functools.partial(product_kernel, len(talls)),
+    joined = (jax.ShapeDtypeStruct((wides[0].shape[0], rows), BF16),) if join else ()
+    return call(
+        functools.partial(product_kernel, len(talls), len(wides)),
         (jax.ShapeDtypeStruct(shape, BF16), jax.ShapeDtypeStruct(shape, F32), *joined),
-        [SMEM] + [VMEM] * (len(talls) + 1),
-        (q, *talls, wide),
+        [SMEM] + [VMEM] * (len(talls) + len(wides)),
+        (q, *talls, *wides),
         [pltpu.VMEM((rows, columns), F32)],
     )
 
@@ -428,13 +428,19 @@
         near_bins = near_bins + [piece ^ bit for piece in near_bins]
     far_bins = jnp.concatenate([piece ^ (inner // 2) for piece in near_bins])
     near_bins = jnp.concatenate(near_bins)
-    begun = [begin_rest(near_bins, names, (0,), arrived[:1], near, band)]
-    across, begun[0], *arrived = lax.optimization_barrier((weights[1], begun[0], *arrived))
-    begun.append(begin_rest(near_bins, names, (1, 2, 3), arrived[1:], near, band))
+    splits = [(0, (per + 1) // 2 * band), ((per + 1) // 2 * band, width)]
+    own = begin_rest(near_bins, names, (0,), arrived[:1], near, (0, width), band)
+    across, own, *arrived = lax.optimization_barrier((weights[1], own, *arrived))
     far = [across]
     for bit in bits:
         far = far + [swap(piece, bit) for piece in far]
-    rest, sent, *sents, squares = end_rest(outer1, far_bins, names, arrived, begun, far, band)
+    rests, sents, squares = [], [], 0.0
+    for columns in splits:
+        others = begin_rest(near_bins, names, (1, 2, 3), arrived[1:], near, columns, band)
+        rest, sent, square = end_rest(outer1, far_bins, names, arrived, own, others, far, columns, band)
+        rests.append(rest)
+        sents.append(sent)
+        squares = squares + square
 
     firsts = [step(part, 1) for part in sents]
     total = squares
@@ -443,7 +449,12 @@
     total, firsts[0] = lax.optimization_barrier((total, firsts[0]))
     scale = lax.rsqrt(total / nrest + 1e-06)
     factor = scale * scale / (count * n)
-    scaled = call(scale_kernel, jax.ShapeDtypeStruct(rest.shape, BF16), [VMEM, VMEM], (rest, factor))
+    scaled = call(
+        functools.partial(scale_kernel, len(rests)),
+        jax.ShapeDtypeStruct((rows, width), BF16),
+        [VMEM] * (len(rests) + 1),
+        (*rests, factor),
+    )
 
     def reduce(send, held):
         bit = 1
@@ -456,20 +467,20 @@
         return swap(send, inner // 2)[0]
 
     q1 = q.reshape(1)
-    send0, held0 = product(q1, [scaled], sent, inner)
+    send0, held0 = product(q1, [scaled], sents, inner)
     firsts[1], send0 = lax.optimization_barrier((firsts[1], send0))
     send0, held0 = reduce(send0, held0)
     got0 = finish(send0)
-    sendm, heldm, first = product(q1, firsts, scaled, inner, join=True)
+    sendm, heldm, first = product(q1, firsts, [scaled], inner, join=True)
     second = step(first, 1)
     sendm, heldm = reduce(sendm, heldm)
     sendm, first = lax.optimization_barrier((sendm, first))
     gotm = finish(sendm)
-    send1, held1 = reduce(*product(q1, [scaled], first, inner))
+    send1, held1 = reduce(*product(q1, [scaled], [first], inner))
     got1 = finish(send1)
     second, got0, got1, gotm = lax.optimization_barrier((second, got0, got1, gotm))
     back = step((heldm + gotm.astype(F32)).astype(BF16), -1)
-    send2, held2 = reduce(*product(q1, [scaled], second, inner))
+    send2, held2 = reduce(*product(q1, [scaled], [second], inner))
     got2 = finish(send2)
     at = fold_at((fold_at(outer) - jnp.arange(OUTER, dtype=I32)) % OUTER)
     begun = place(at, [0, 1], [(held0, got0), (held1, got1)])

time: 98.4 us -> 97.6 us (level)
  waiting for transfers between devices: 39.1 us -> 36.8 us
  Pallas kernels: 23.8 us -> 25.2 us
    ppermute x25, waiting for transfers between devices: 29.6 us -> 27.5 us  [swap(): return lax.ppermute(array, 'spec', [(i, i ^ bit) for i in range(n)])]
    pallas_call x15 -> x17, Pallas kernels: 20.8 us -> 22.2 us  [call(): pl.pallas_call(kernel, out_shape=out_shape, in_specs=in_specs, out_specs=...]
  transfers between devices with their start and end apart: 29 -> 29, of which waited for: 15 -> 16; matrix products, arithmetic and copies ran while one was open for 2% -> 2% of each run, Pallas kernels for 19% -> 21%
where the time goes in v18:
time: 97.6 us; the launch traced here: 97.3 us
  waiting for transfers between devices  36.8 us (38%)
  starting transfers between devices  32.4 us (33%)
  Pallas kernels  25.2 us (26%)
  local copies, waits for them, and re-layouts  1.37 us (1%)
  other arithmetic  1.28 us (1%)
    ppermute x25, waiting for transfers between devices, swap(): return lax.ppermute(array, 'spec', [(i, i ^ bit) for i in range(n)])  27.5 us
    ppermute x25, starting transfers between devices, swap(): return lax.ppermute(array, 'spec', [(i, i ^ bit) for i in range(n)])  27.4 us
    pallas_call x17, Pallas kernels, call(): pl.pallas_call(kernel, out_shape=out_shape, in_specs=in_specs, out_specs=...  22.2 us
    ppermute x4, waiting for transfers between devices, step(): lax.ppermute(array, 'spec', [(o * inner + i, to[o] * inner + i) for o in...  9.34 us
    ppermute x4, starting transfers between devices, step(): lax.ppermute(array, 'spec', [(o * inner + i, to[o] * inner + i) for o in...  5.08 us
    pallas_call x2, Pallas kernels, place(): pl.pallas_call(functools.partial(place_kernel, slots, last), out_shape=ja...  2.98 us
  transfers between devices with their start and end apart: 29, of which 16 were waited for; matrix products, arithmetic and copies ran while one was open for 2% of the time, Pallas kernels for 21%

profile of v18, /device:TPU:0, one launch (start us, length us, event | category | flops | bytes accessed | tf_op | source)
XLA Modules:
  0.0 97.3 jit_solution(10138227004376626677)
XLA Ops:
  0.0 0.8 pad_add_fusion.3
  0.8 3.0 %collective-permute-start = (s32[148]{0:T(256)S(1)}, s32[148]{0:T(256)S(1)}, u32[]{:S(2)}, u32[]{:S(2)}) collective-permute-start(s32[148]{0:T(256)S(1)} %pad_add_fusion.3), channel_id=1, source_target_pairs={{0,4},{1,5},{2,6},{3,7},{4,0},{5,1},{6,2},{7,3},{8,12},{9,13},{10,... | collective-permute-start | bytes 1784 | tf_op jit(solution)/shard_map/ppermute | solution.py:375
  3.9 2.6 %collective-permute-start.1 = (s32[148]{0:T(256)S(1)}, s32[148]{0:T(256)S(1)}, u32[]{:S(2)}, u32[]{:S(2)}) collective-permute-start(s32[148]{0:T(256)S(1)} %pad_add_fusion.3), channel_id=1, source_target_pairs={{0,8},{1,9},{2,10},{3,11},{4,12},{5,13},{6,14},{7,15},{8,0},{9,1},... | collective-permute-start | bytes 1784 | tf_op jit(solution)/shard_map/ppermute | solution.py:375
  6.5 1.2 %dynamic-slice_bitcast_fusion = (bf16[640,128]{1,0:T(8,128)(2,1)S(1)}, bf16[640,128]{1,0:T(8,128)(2,1)S(1)}, bf16[640,128]{1,0:T(8,128)(2,1)S(1)}, bf16[640,128]{1,0:T(8,128)(2,1)S(1)}) fusion(bf16[4,640,128]{2,1,0:T(8,128)(2,1)} %bitcast.47, s32[]{:T(128)S(6)} %select_n.41, s32[]{:T(128)S(6)} %select_n.40, s32[]{:T(128)S(6)} %select_n.39, s32[]{:T(128)S(6)} %select_n.38), kind=kLoop, calls=%fused_computation.3 | loop fusion | bytes 1310736 | tf_op jit(solution)/shard_map/jit(dynamic_index_in_dim)/squeeze | solution.py:401
  7.7 1.0 collective-permute-start.3
  8.6 3.5 %collective-permute-start.4 = (bf16[640,128]{1,0:T(8,128)(2,1)S(1)}, bf16[640,128]{1,0:T(8,128)(2,1)S(1)}, u32[]{:S(2)}, u32[]{:S(2)}) collective-permute-start(bf16[640,128]{1,0:T(8,128)(2,1)S(1)} %get-tuple-element.120), channel_id=1, source_target_pairs={{0,8},{1,9},{2,10},{3,11},{4,12},{5,13},{6,14},{7,15},{8,0},{9,1},... | collective-permute-start | bytes 491528 | tf_op jit(solution)/shard_map/ppermute | solution.py:375
  12.2 0.1 collective-permute-start.6
  12.2 0.1 slice_bitcast_fusion.1.targets_ref
  12.3 1.1 %collective-permute-done.6 = s32[4,1,20]{2,0,1:T(4,128)S(1)} collective-permute-done((s32[4,1,20]{2,0,1:T(4,128)S(1)}, s32[4,1,20]{2,0,1:T(4,128)S(1)}, u32[]{:S(2)}, u32[]{:S(2)}) %collective-permute-start.6) | collective-permute-done | bytes 352 | tf_op jit(solution)/shard_map/ppermute | solution.py:375
  13.4 1.7 %collective-permute-start.7 = (s32[4,2,20]{2,0,1:T(4,128)S(1)}, s32[4,2,20]{2,0,1:T(4,128)S(1)}, u32[]{:S(2)}, u32[]{:S(2)}) collective-permute-start(s32[4,2,20]{2,0,1:T(4,128)S(1)} %pad_add_fusion.2), channel_id=1, source_target_pairs={{0,2},{1,3},{2,0},{3,1},{4,6},{5,7},{6,4},{7,5},{8,10},{9,11},{10,... | collective-permute-start | bytes 1928 | tf_op jit(solution)/shard_map/ppermute | solution.py:375
  15.1 0.1 pad_add_fusion.5.me_ref
  15.2 0.2 shard_map.55
  15.4 6.7 %shard_map.56.smoothed_ref = bf16[128,3968]{1,0:T(8,128)(2,1)S(1)} custom-call(bf16[128,3968]{1,0:T(8,128)(2,1)S(1)} %copy-done, bf16[11,128,3968]{2,1,0:T(8,128)(2,1)} %bitcast.45), custom_call_target="tpu_custom_call" | custom-call | flops 1 | bytes 1 | tf_op jit(solution)/shard_map/pallas_call | solution.py:20
  22.2 4.7 %shard_map.57 = (bf16[128,640]{1,0:T(8,128)(2,1)S(1)}, bf16[128,640]{1,0:T(8,128)(2,1)S(1)}, bf16[128,640]{1,0:T(8,128)(2,1)S(1)}, bf16[128,640]{1,0:T(8,128)(2,1)S(1)}) custom-call(s32[2]{0:T(128)S(1)} %pad_add_fusion.5.me_ref, s32[2,128]{1,0:T(2,128)S(1)} %get-tuple-element.62.groups_ref, s32[16,20]{1,0:T(8,128)S(1)} %get-tuple-element.124.starts_ref, ...), custom_call_target="tpu_custom_call" | custom-call | flops 1 | bytes 1 | tf_op jit(solution)/shard_map/pallas_call | solution.py:20
  27.0 0.1 pad_maximum_fusion.refs_1_.refs_3_
  27.1 0.1 collective-permute-start.9
  27.1 0.4 collective-permute-start.8
  27.5 1.5 %collective-permute-start.11 = (bf16[128,640]{1,0:T(8,128)(2,1)S(1)}, bf16[128,640]{1,0:T(8,128)(2,1)S(1)}, u32[]{:S(2)}, u32[]{:S(2)}) collective-permute-start(bf16[128,640]{1,0:T(8,128)(2,1)S(1)} %get-tuple-element.78), channel_id=1, source_target_pairs={{0,8},{1,9},{2,10},{3,11},{4,12},{5,13},{6,14},{7,15},{8,0},{9,1},... | collective-permute-start | bytes 491528 | tf_op jit(solution)/shard_map/ppermute | solution.py:375
  29.0 2.3 %collective-permute-start.12 = (bf16[128,640]{1,0:T(8,128)(2,1)S(1)}, bf16[128,640]{1,0:T(8,128)(2,1)S(1)}, u32[]{:S(2)}, u32[]{:S(2)}) collective-permute-start(bf16[128,640]{1,0:T(8,128)(2,1)S(1)} %get-tuple-element.79), channel_id=1, source_target_pairs={{0,12},{1,13},{2,14},{3,15},{4,8},{5,9},{6,10},{7,11},{8,4},{9,5},... | collective-permute-start | bytes 491528 | tf_op jit(solution)/shard_map/ppermute | solution.py:375
  31.3 0.6 collective-permute-start.10
  31.9 0.1 pad_add_fusion.6.bins_ref
  32.0 0.1 slice.12.names_ref
  32.0 1.1 %shard_map.58.refs_4_ = f32[128,640]{1,0:T(8,128)S(1)} custom-call(s32[8]{0:T(128)S(1)} %pad_add_fusion.6.bins_ref, s32[4,128]{1,0:T(4,128)S(1)} %slice.12.names_ref, bf16[128,640]{1,0:T(8,128)(2,1)S(1)} %get-tuple-element.80.refs_0_, bf16[4,640,128]{2,1,0:T(8,128)(2,1)S(1)} %pad_maximum_fusion.refs_1_.refs_3_, ...), custom_call_target="tpu_custom_call" | custom-call | flops 1 | bytes 1 | tf_op jit(solution)/shard_map/pallas_call | solution.py:20
  33.2 9.3 %collective-permute-done.11.refs_1_.refs_2_ = bf16[128,640]{1,0:T(8,128)(2,1)S(1)} collective-permute-done((bf16[128,640]{1,0:T(8,128)(2,1)S(1)}, bf16[128,640]{1,0:T(8,128)(2,1)S(1)}, u32[]{:S(2)}, u32[]{:S(2)}) %collective-permute-start.11) | collective-permute-done | bytes 163872 | tf_op jit(solution)/shard_map/ppermute | solution.py:375
  42.5 1.8 %collective-permute-done.8.refs_6_ = bf16[4,640,128]{2,1,0:T(8,128)(2,1)S(1)} collective-permute-done((bf16[4,640,128]{2,1,0:T(8,128)(2,1)S(1)}, bf16[4,640,128]{2,1,0:T(8,128)(2,1)S(1)}, u32[]{:S(2)}, u32[]{:S(2)}) %collective-permute-start.8) | collective-permute-done | bytes 655392 | tf_op jit(solution)/shard_map/ppermute | solution.py:375
  44.3 0.1 pad_add_fusion.4.bins_ref
  44.4 1.4 %shard_map.59.refs_5_ = f32[384,384]{1,0:T(8,128)S(1)} custom-call(s32[8]{0:T(128)S(1)} %pad_add_fusion.6.bins_ref, s32[4,128]{1,0:T(4,128)S(1)} %slice.12.names_ref, bf16[128,640]{1,0:T(8,128)(2,1)S(1)} %collective-permute-done.10.refs_0_.refs_1_, bf16[128,640]{1,0:T(8,128)(2,1)S(1)} %collective-permute-done.11.refs_1_.refs_2_, ...), custom_call_target="tpu_custom_call" | custom-call | flops 1 | bytes 1 | tf_op jit(solution)/shard_map/pallas_call | solution.py:20
  45.8 0.6 collective-permute-done.13.refs_7_
  46.4 1.7 %shard_map.60 = (f32[512,384]{1,0:T(8,128)S(1)}, bf16[512,384]{1,0:T(8,128)(2,1)S(1)}, f32[4,128]{1,0:T(4,128)S(1)}) custom-call(s32[1]{0:T(128)} %bitcast.1.outer_ref, s32[8]{0:T(128)S(1)} %pad_add_fusion.4.bins_ref, s32[4,128]{1,0:T(4,128)S(1)} %slice.12.names_ref, bf16[128,640]{1,0:T(8,128)(2,1)S(1)} %get-tuple-element.80.refs_0_, ...), custom_call_target="tpu_custom_call" | custom-call | flops 1 | bytes 1 | tf_op jit(solution)/shard_map/pallas_call | solution.py:20
  48.1 1.6 %collective-permute-start.17 = (bf16[512,384]{1,0:T(8,128)(2,1)S(1)}, bf16[512,384]{1,0:T(8,128)(2,1)S(1)}, u32[]{:S(2)}, u32[]{:S(2)}) collective-permute-start(bf16[512,384]{1,0:T(8,128)(2,1)S(1)} %get-tuple-element.90.refs_1_), channel_id=1, source_target_pairs={{0,4},{1,5},{2,6},{3,7},{4,12},{5,13},{6,14},{7,15},{8,0},{9,1},{1... | collective-permute-start | bytes 1179656 | tf_op jit(solution)/shard_map/ppermute | solution.py:382
  49.6 1.2 %shard_map.61.refs_5_ = f32[384,256]{1,0:T(8,128)S(1)} custom-call(s32[8]{0:T(128)S(1)} %pad_add_fusion.6.bins_ref, s32[4,128]{1,0:T(4,128)S(1)} %slice.12.names_ref, bf16[128,640]{1,0:T(8,128)(2,1)S(1)} %collective-permute-done.10.refs_0_.refs_1_, bf16[128,640]{1,0:T(8,128)(2,1)S(1)} %collective-permute-done.11.refs_1_.refs_2_, ...), custom_call_target="tpu_custom_call" | custom-call | flops 1 | bytes 1 | tf_op jit(solution)/shard_map/pallas_call | solution.py:20
  50.8 1.4 %shard_map.62 = (f32[512,256]{1,0:T(8,128)S(1)}, bf16[512,256]{1,0:T(8,128)(2,1)S(1)}, f32[4,128]{1,0:T(4,128)S(1)}) custom-call(s32[1]{0:T(128)} %bitcast.1.outer_ref, s32[8]{0:T(128)S(1)} %pad_add_fusion.4.bins_ref, s32[4,128]{1,0:T(4,128)S(1)} %slice.12.names_ref, bf16[128,640]{1,0:T(8,128)(2,1)S(1)} %get-tuple-element.80.refs_0_, ...), custom_call_target="tpu_custom_call" | custom-call | flops 1 | bytes 1 | tf_op jit(solution)/shard_map/pallas_call | solution.py:20
  52.2 2.7 %collective-permute-start.14 = (f32[4,128]{1,0:T(4,128)S(1)}, f32[4,128]{1,0:T(4,128)S(1)}, u32[]{:S(2)}, u32[]{:S(2)}) collective-permute-start(f32[4,128]{1,0:T(4,128)S(1)} %add.60), channel_id=1, source_target_pairs={{0,4},{1,5},{2,6},{3,7},{4,0},{5,1},{6,2},{7,3},{8,12},{9,13},{10,... | collective-permute-start | bytes 6152 | tf_op jit(solution)/shard_map/ppermute | solution.py:375
  54.9 0.4 collective-permute-start.15
  55.3 2.1 %collective-permute-start.16 = (f32[4,128]{1,0:T(4,128)S(1)}, f32[4,128]{1,0:T(4,128)S(1)}, u32[]{:S(2)}, u32[]{:S(2)}) collective-permute-start(f32[4,128]{1,0:T(4,128)S(1)} %add.60), channel_id=1, source_target_pairs={{0,12},{1,13},{2,14},{3,15},{4,8},{5,9},{6,10},{7,11},{8,4},{9,5},... | collective-permute-start | bytes 6152 | tf_op jit(solution)/shard_map/ppermute | solution.py:375
  57.3 1.0 %collective-permute-start.18 = (bf16[512,256]{1,0:T(8,128)(2,1)S(1)}, bf16[512,256]{1,0:T(8,128)(2,1)S(1)}, u32[]{:S(2)}, u32[]{:S(2)}) collective-permute-start(bf16[512,256]{1,0:T(8,128)(2,1)S(1)} %get-tuple-element.93.refs_2_), channel_id=1, source_target_pairs={{0,4},{1,5},{2,6},{3,7},{4,12},{5,13},{6,14},{7,15},{8,0},{9,1},{1... | collective-permute-start | bytes 786440 | tf_op jit(solution)/shard_map/ppermute | solution.py:382
  58.4 0.8 collective-permute-done.14
  59.2 1.2 %collective-permute-done.15 = f32[4,128]{1,0:T(4,128)S(1)} collective-permute-done((f32[4,128]{1,0:T(4,128)S(1)}, f32[4,128]{1,0:T(4,128)S(1)}, u32[]{:S(2)}, u32[]{:S(2)}) %collective-permute-start.15) | collective-permute-done | bytes 2080 | tf_op jit(solution)/shard_map/ppermute | solution.py:375
  60.3 1.8 %collective-permute-done.16 = f32[4,128]{1,0:T(4,128)S(1)} collective-permute-done((f32[4,128]{1,0:T(4,128)S(1)}, f32[4,128]{1,0:T(4,128)S(1)}, u32[]{:S(2)}, u32[]{:S(2)}) %collective-permute-start.16) | collective-permute-done | bytes 2080 | tf_op jit(solution)/shard_map/ppermute | solution.py:375
  62.2 0.2 shard_map.63.refs_0_.refs_2_
  62.4 0.8 shard_map.64
  63.2 2.8 %collective-permute-done.18.refs_1_ = bf16[512,256]{1,0:T(8,128)(2,1)S(1)} collective-permute-done((bf16[512,256]{1,0:T(8,128)(2,1)S(1)}, bf16[512,256]{1,0:T(8,128)(2,1)S(1)}, u32[]{:S(2)}, u32[]{:S(2)}) %collective-permute-start.18) | collective-permute-done | bytes 262176 | tf_op jit(solution)/shard_map/ppermute | solution.py:382
  66.0 0.9 shard_map.65
  66.8 0.1 collective-permute-start.22
  66.9 0.8 collective-permute-start.19
  67.8 0.2 collective-permute-start.20
  67.9 0.7 collective-permute-done.22.got_ref
  68.7 0.1 shard_map.67
  68.7 0.8 shard_map.68
  69.6 0.2 collective-permute-start.23
  69.8 1.4 %collective-permute-start.25 = (bf16[1,160,640]{2,1,0:T(8,128)(2,1)S(1)}, bf16[1,160,640]{2,1,0:T(8,128)(2,1)S(1)}, u32[]{:S(2)}, u32[]{:S(2)}) collective-permute-start(bf16[1,160,640]{2,1,0:T(8,128)(2,1)S(1)} %get-tuple-element.107), channel_id=1, source_target_pairs={{0,2},{1,3},{2,0},{3,1},{4,6},{5,7},{6,4},{7,5},{8,10},{9,11},{10,... | collective-permute-start | bytes 614408 | tf_op jit(solution)/shard_map/ppermute | solution.py:375
  71.2 0.7 collective-permute-start.21
  72.0 1.4 %collective-permute-start.24 = (bf16[1,160,640]{2,1,0:T(8,128)(2,1)S(1)}, bf16[1,160,640]{2,1,0:T(8,128)(2,1)S(1)}, u32[]{:S(2)}, u32[]{:S(2)}) collective-permute-start(bf16[1,160,640]{2,1,0:T(8,128)(2,1)S(1)} %get-tuple-element.106), channel_id=1, source_target_pairs={{0,2},{1,3},{2,0},{3,1},{4,6},{5,7},{6,4},{7,5},{8,10},{9,11},{10,... | collective-permute-start | bytes 614408 | tf_op jit(solution)/shard_map/ppermute | solution.py:375
  73.5 4.2 %collective-permute-done.25 = bf16[1,160,640]{2,1,0:T(8,128)(2,1)S(1)} collective-permute-done((bf16[1,160,640]{2,1,0:T(8,128)(2,1)S(1)}, bf16[1,160,640]{2,1,0:T(8,128)(2,1)S(1)}, u32[]{:S(2)}, u32[]{:S(2)}) %collective-permute-start.25) | collective-permute-done | bytes 204832 | tf_op jit(solution)/shard_map/ppermute | solution.py:375
  77.7 4.4 %collective-permute-done.21 = bf16[1,160,640]{2,1,0:T(8,128)(2,1)S(1)} collective-permute-done((bf16[1,160,640]{2,1,0:T(8,128)(2,1)S(1)}, bf16[1,160,640]{2,1,0:T(8,128)(2,1)S(1)}, u32[]{:S(2)}, u32[]{:S(2)}) %collective-permute-start.21) | collective-permute-done | bytes 204832 | tf_op jit(solution)/shard_map/ppermute | solution.py:375
  82.1 2.9 %collective-permute-done.19.refs_1_ = bf16[512,640]{1,0:T(8,128)(2,1)S(1)} collective-permute-done((bf16[512,640]{1,0:T(8,128)(2,1)S(1)}, bf16[512,640]{1,0:T(8,128)(2,1)S(1)}, u32[]{:S(2)}, u32[]{:S(2)}) %collective-permute-start.19) | collective-permute-done | bytes 655392 | tf_op jit(solution)/shard_map/ppermute | solution.py:382
  85.0 0.9 collective-permute-done.24
  85.9 0.8 shard_map.70
  86.8 1.6 %collective-permute-start.28 = (bf16[160,640]{1,0:T(8,128)(2,1)S(1)}, bf16[160,640]{1,0:T(8,128)(2,1)S(1)}, u32[]{:S(2)}, u32[]{:S(2)}) collective-permute-start(bf16[160,640]{1,0:T(8,128)(2,1)S(1)} %fusion), channel_id=1, source_target_pairs={{0,8},{1,9},{2,10},{3,11},{4,0},{5,1},{6,2},{7,3},{8,12},{9,13},{1... | collective-permute-start | bytes 614408 | tf_op jit(solution)/shard_map/ppermute | solution.py:382
  88.6 1.5 %collective-permute-start.27 = (bf16[1,160,640]{2,1,0:T(8,128)(2,1)S(1)}, bf16[1,160,640]{2,1,0:T(8,128)(2,1)S(1)}, u32[]{:S(2)}, u32[]{:S(2)}) collective-permute-start(bf16[1,160,640]{2,1,0:T(8,128)(2,1)S(1)} %get-tuple-element.112), channel_id=1, source_target_pairs={{0,2},{1,3},{2,0},{3,1},{4,6},{5,7},{6,4},{7,5},{8,10},{9,11},{10,... | collective-permute-start | bytes 614408 | tf_op jit(solution)/shard_map/ppermute | solution.py:375
  90.1 1.5 %shard_map.72.refs_4_ = f32[160,2560]{1,0:T(8,128)} custom-call(s32[4]{0:T(128)S(1)} %shift-right-arithmetic_xor_fusion.at_ref, f32[160,640]{1,0:T(8,128)S(1)} %bitcast.39, bf16[160,640]{1,0:T(8,128)(2,1)S(1)} %bitcast.42, f32[160,640]{1,0:T(8,128)S(1)} %bitcast.40, bf16[160,640]{1,0:T(8,128)(2,1)S(1)} %bitcast.43), custom_call_target="tpu_custom_call" | custom-call | flops 1 | bytes 1 | tf_op jit(solution)/shard_map/pallas_call | solution.py:349
  91.6 3.7 %collective-permute-done.28.refs_2_ = bf16[160,640]{1,0:T(8,128)(2,1)S(1)} collective-permute-done((bf16[160,640]{1,0:T(8,128)(2,1)S(1)}, bf16[160,640]{1,0:T(8,128)(2,1)S(1)}, u32[]{:S(2)}, u32[]{:S(2)}) %collective-permute-start.28) | collective-permute-done | bytes 204832 | tf_op jit(solution)/shard_map/ppermute | solution.py:382
  95.3 0.5 collective-permute-done.27
  95.8 1.5 %shard_map.73 = f32[160,2560]{1,0:T(8,128)} custom-call(s32[4]{0:T(128)S(1)} %shift-right-arithmetic_xor_fusion.at_ref, f32[160,640]{1,0:T(8,128)S(1)} %bitcast.41, bf16[160,640]{1,0:T(8,128)(2,1)S(1)} %bitcast.44, bf16[160,640]{1,0:T(8,128)(2,1)S(1)} %collective-permute-done.28.refs_2_, ...), custom_call_target="tpu_custom_call", output_to_operand_aliasing={{}: (5, {})} | custom-call | flops 1 | bytes 1 | tf_op jit(solution)/shard_map/pallas_call | solution.py:349
  (37 shorter events, 0.5 us)
Async XLA Ops:
  0.0 15.4 %copy-start = (bf16[128,3968]{1,0:T(8,128)(2,1)S(1)}, bf16[128,3968]{1,0:T(8,128)(2,1)}, u32[]{:S(2)}) copy-start(bf16[128,3968]{1,0:T(8,128)(2,1)} %flux_ref) | copy-start | bytes 3047428
  0.8 11.3 %collective-permute-start = (s32[148]{0:T(256)S(1)}, s32[148]{0:T(256)S(1)}, u32[]{:S(2)}, u32[]{:S(2)}) collective-permute-start(s32[148]{0:T(256)S(1)} %pad_add_fusion.3), channel_id=1, source_target_pairs={{0,4},{1,5},{2,6},{3,7},{4,0},{5,1},{6,2},{7,3},{8,12},{9,13},{10,... | collective-permute-start | bytes 1784 | tf_op jit(solution)/shard_map/ppermute | solution.py:375
  3.9 8.3 %collective-permute-start.1 = (s32[148]{0:T(256)S(1)}, s32[148]{0:T(256)S(1)}, u32[]{:S(2)}, u32[]{:S(2)}) collective-permute-start(s32[148]{0:T(256)S(1)} %pad_add_fusion.3), channel_id=1, source_target_pairs={{0,8},{1,9},{2,10},{3,11},{4,12},{5,13},{6,14},{7,15},{8,0},{9,1},... | collective-permute-start | bytes 1784 | tf_op jit(solution)/shard_map/ppermute | solution.py:375
  6.4 5.7 %collective-permute-start.2 = (s32[148]{0:T(256)S(1)}, s32[148]{0:T(256)S(1)}, u32[]{:S(2)}, u32[]{:S(2)}) collective-permute-start(s32[148]{0:T(256)S(1)} %pad_add_fusion.3), channel_id=1, source_target_pairs={{0,12},{1,13},{2,14},{3,15},{4,8},{5,9},{6,10},{7,11},{8,4},{9,5},... | collective-permute-start | bytes 1784 | tf_op jit(solution)/shard_map/ppermute | solution.py:375
  7.7 19.3 %collective-permute-start.3 = (bf16[640,128]{1,0:T(8,128)(2,1)S(1)}, bf16[640,128]{1,0:T(8,128)(2,1)S(1)}, u32[]{:S(2)}, u32[]{:S(2)}) collective-permute-start(bf16[640,128]{1,0:T(8,128)(2,1)S(1)} %get-tuple-element.121), channel_id=1, source_target_pairs={{0,4},{1,5},{2,6},{3,7},{4,0},{5,1},{6,2},{7,3},{8,12},{9,13},{10,... | collective-permute-start | bytes 491528 | tf_op jit(solution)/shard_map/ppermute | solution.py:375
  8.6 18.3 %collective-permute-start.4 = (bf16[640,128]{1,0:T(8,128)(2,1)S(1)}, bf16[640,128]{1,0:T(8,128)(2,1)S(1)}, u32[]{:S(2)}, u32[]{:S(2)}) collective-permute-start(bf16[640,128]{1,0:T(8,128)(2,1)S(1)} %get-tuple-element.120), channel_id=1, source_target_pairs={{0,8},{1,9},{2,10},{3,11},{4,12},{5,13},{6,14},{7,15},{8,0},{9,1},... | collective-permute-start | bytes 491528 | tf_op jit(solution)/shard_map/ppermute | solution.py:375
  12.1 14.9 %collective-permute-start.5 = (bf16[640,128]{1,0:T(8,128)(2,1)S(1)}, bf16[640,128]{1,0:T(8,128)(2,1)S(1)}, u32[]{:S(2)}, u32[]{:S(2)}) collective-permute-start(bf16[640,128]{1,0:T(8,128)(2,1)S(1)} %get-tuple-element.119), channel_id=1, source_target_pairs={{0,12},{1,13},{2,14},{3,15},{4,8},{5,9},{6,10},{7,11},{8,4},{9,5},... | collective-permute-start | bytes 491528 | tf_op jit(solution)/shard_map/ppermute | solution.py:375
  12.2 1.2 %collective-permute-start.6 = (s32[4,1,20]{2,0,1:T(4,128)S(1)}, s32[4,1,20]{2,0,1:T(4,128)S(1)}, u32[]{:S(2)}, u32[]{:S(2)}) collective-permute-start(s32[4,1,20]{2,0,1:T(4,128)S(1)} %slice_bitcast_fusion), channel_id=1, source_target_pairs={{0,1},{1,0},{2,3},{3,2},{4,5},{5,4},{6,7},{7,6},{8,9},{9,8},{10,11... | collective-permute-start | bytes 968 | tf_op jit(solution)/shard_map/ppermute | solution.py:375
  13.4 8.8 %collective-permute-start.7 = (s32[4,2,20]{2,0,1:T(4,128)S(1)}, s32[4,2,20]{2,0,1:T(4,128)S(1)}, u32[]{:S(2)}, u32[]{:S(2)}) collective-permute-start(s32[4,2,20]{2,0,1:T(4,128)S(1)} %pad_add_fusion.2), channel_id=1, source_target_pairs={{0,2},{1,3},{2,0},{3,1},{4,6},{5,7},{6,4},{7,5},{8,10},{9,11},{10,... | collective-permute-start | bytes 1928 | tf_op jit(solution)/shard_map/ppermute | solution.py:375
  27.1 4.3 %collective-permute-start.9 = (bf16[4,640,128]{2,1,0:T(8,128)(2,1)S(1)}, bf16[4,640,128]{2,1,0:T(8,128)(2,1)S(1)}, u32[]{:S(2)}, u32[]{:S(2)}) collective-permute-start(bf16[4,640,128]{2,1,0:T(8,128)(2,1)S(1)} %pad_maximum_fusion.refs_1_.refs_3_), channel_id=1, source_target_pairs={{0,1},{1,0},{2,3},{3,2},{4,5},{5,4},{6,7},{7,6},{8,9},{9,8},{10,11... | collective-permute-start | bytes 1966088 | tf_op jit(solution)/shard_map/ppermute | solution.py:375
  27.1 17.1 %collective-permute-start.8 = (bf16[4,640,128]{2,1,0:T(8,128)(2,1)S(1)}, bf16[4,640,128]{2,1,0:T(8,128)(2,1)S(1)}, u32[]{:S(2)}, u32[]{:S(2)}) collective-permute-start(bf16[4,640,128]{2,1,0:T(8,128)(2,1)S(1)} %pad_maximum_fusion.refs_1_.refs_3_), channel_id=1, source_target_pairs={{0,2},{1,3},{2,0},{3,1},{4,6},{5,7},{6,4},{7,5},{8,10},{9,11},{10,... | collective-permute-start | bytes 1966088 | tf_op jit(solution)/shard_map/ppermute | solution.py:375
  27.5 15.0 %collective-permute-start.11 = (bf16[128,640]{1,0:T(8,128)(2,1)S(1)}, bf16[128,640]{1,0:T(8,128)(2,1)S(1)}, u32[]{:S(2)}, u32[]{:S(2)}) collective-permute-start(bf16[128,640]{1,0:T(8,128)(2,1)S(1)} %get-tuple-element.78), channel_id=1, source_target_pairs={{0,8},{1,9},{2,10},{3,11},{4,12},{5,13},{6,14},{7,15},{8,0},{9,1},... | collective-permute-start | bytes 491528 | tf_op jit(solution)/shard_map/ppermute | solution.py:375
  29.0 13.5 %collective-permute-start.12 = (bf16[128,640]{1,0:T(8,128)(2,1)S(1)}, bf16[128,640]{1,0:T(8,128)(2,1)S(1)}, u32[]{:S(2)}, u32[]{:S(2)}) collective-permute-start(bf16[128,640]{1,0:T(8,128)(2,1)S(1)} %get-tuple-element.79), channel_id=1, source_target_pairs={{0,12},{1,13},{2,14},{3,15},{4,8},{5,9},{6,10},{7,11},{8,4},{9,5},... | collective-permute-start | bytes 491528 | tf_op jit(solution)/shard_map/ppermute | solution.py:375
  31.3 13.0 %collective-permute-start.10 = (bf16[128,640]{1,0:T(8,128)(2,1)S(1)}, bf16[128,640]{1,0:T(8,128)(2,1)S(1)}, u32[]{:S(2)}, u32[]{:S(2)}) collective-permute-start(bf16[128,640]{1,0:T(8,128)(2,1)S(1)} %get-tuple-element.77), channel_id=1, source_target_pairs={{0,4},{1,5},{2,6},{3,7},{4,0},{5,1},{6,2},{7,3},{8,12},{9,13},{10,... | collective-permute-start | bytes 491528 | tf_op jit(solution)/shard_map/ppermute | solution.py:375
  44.3 2.1 %collective-permute-start.13 = (bf16[4,640,128]{2,1,0:T(8,128)(2,1)S(1)}, bf16[4,640,128]{2,1,0:T(8,128)(2,1)S(1)}, u32[]{:S(2)}, u32[]{:S(2)}) collective-permute-start(bf16[4,640,128]{2,1,0:T(8,128)(2,1)S(1)} %collective-permute-done.8.refs_6_), channel_id=1, source_target_pairs={{0,1},{1,0},{2,3},{3,2},{4,5},{5,4},{6,7},{7,6},{8,9},{9,8},{10,11... | collective-permute-start | bytes 1966088 | tf_op jit(solution)/shard_map/ppermute | solution.py:375
  48.1 14.1 %collective-permute-start.17 = (bf16[512,384]{1,0:T(8,128)(2,1)S(1)}, bf16[512,384]{1,0:T(8,128)(2,1)S(1)}, u32[]{:S(2)}, u32[]{:S(2)}) collective-permute-start(bf16[512,384]{1,0:T(8,128)(2,1)S(1)} %get-tuple-element.90.refs_1_), channel_id=1, source_target_pairs={{0,4},{1,5},{2,6},{3,7},{4,12},{5,13},{6,14},{7,15},{8,0},{9,1},{1... | collective-permute-start | bytes 1179656 | tf_op jit(solution)/shard_map/ppermute | solution.py:382
  52.2 7.0 %collective-permute-start.14 = (f32[4,128]{1,0:T(4,128)S(1)}, f32[4,128]{1,0:T(4,128)S(1)}, u32[]{:S(2)}, u32[]{:S(2)}) collective-permute-start(f32[4,128]{1,0:T(4,128)S(1)} %add.60), channel_id=1, source_target_pairs={{0,4},{1,5},{2,6},{3,7},{4,0},{5,1},{6,2},{7,3},{8,12},{9,13},{10,... | collective-permute-start | bytes 6152 | tf_op jit(solution)/shard_map/ppermute | solution.py:375
  54.9 5.4 %collective-permute-start.15 = (f32[4,128]{1,0:T(4,128)S(1)}, f32[4,128]{1,0:T(4,128)S(1)}, u32[]{:S(2)}, u32[]{:S(2)}) collective-permute-start(f32[4,128]{1,0:T(4,128)S(1)} %add.60), channel_id=1, source_target_pairs={{0,8},{1,9},{2,10},{3,11},{4,12},{5,13},{6,14},{7,15},{8,0},{9,1},... | collective-permute-start | bytes 6152 | tf_op jit(solution)/shard_map/ppermute | solution.py:375
  55.3 6.9 %collective-permute-start.16 = (f32[4,128]{1,0:T(4,128)S(1)}, f32[4,128]{1,0:T(4,128)S(1)}, u32[]{:S(2)}, u32[]{:S(2)}) collective-permute-start(f32[4,128]{1,0:T(4,128)S(1)} %add.60), channel_id=1, source_target_pairs={{0,12},{1,13},{2,14},{3,15},{4,8},{5,9},{6,10},{7,11},{8,4},{9,5},... | collective-permute-start | bytes 6152 | tf_op jit(solution)/shard_map/ppermute | solution.py:375
  57.3 8.6 %collective-permute-start.18 = (bf16[512,256]{1,0:T(8,128)(2,1)S(1)}, bf16[512,256]{1,0:T(8,128)(2,1)S(1)}, u32[]{:S(2)}, u32[]{:S(2)}) collective-permute-start(bf16[512,256]{1,0:T(8,128)(2,1)S(1)} %get-tuple-element.93.refs_2_), channel_id=1, source_target_pairs={{0,4},{1,5},{2,6},{3,7},{4,12},{5,13},{6,14},{7,15},{8,0},{9,1},{1... | collective-permute-start | bytes 786440 | tf_op jit(solution)/shard_map/ppermute | solution.py:382
  66.8 1.8 %collective-permute-start.22 = (bf16[2,160,640]{2,1,0:T(8,128)(2,1)S(1)}, bf16[2,160,640]{2,1,0:T(8,128)(2,1)S(1)}, u32[]{:S(2)}, u32[]{:S(2)}) collective-permute-start(bf16[2,160,640]{2,1,0:T(8,128)(2,1)S(1)} %get-tuple-element.101), channel_id=1, source_target_pairs={{0,1},{1,0},{2,3},{3,2},{4,5},{5,4},{6,7},{7,6},{8,9},{9,8},{10,11... | collective-permute-start | bytes 1228808 | tf_op jit(solution)/shard_map/ppermute | solution.py:375
  66.9 18.0 %collective-permute-start.19 = (bf16[512,640]{1,0:T(8,128)(2,1)S(1)}, bf16[512,640]{1,0:T(8,128)(2,1)S(1)}, u32[]{:S(2)}, u32[]{:S(2)}) collective-permute-start(bf16[512,640]{1,0:T(8,128)(2,1)S(1)} %get-tuple-element.103.refs_1_), channel_id=1, source_target_pairs={{0,4},{1,5},{2,6},{3,7},{4,12},{5,13},{6,14},{7,15},{8,0},{9,1},{1... | collective-permute-start | bytes 1966088 | tf_op jit(solution)/shard_map/ppermute | solution.py:382
  67.8 3.4 %collective-permute-start.20 = (bf16[2,160,640]{2,1,0:T(8,128)(2,1)S(1)}, bf16[2,160,640]{2,1,0:T(8,128)(2,1)S(1)}, u32[]{:S(2)}, u32[]{:S(2)}) collective-permute-start(bf16[2,160,640]{2,1,0:T(8,128)(2,1)S(1)} %get-tuple-element.98), channel_id=1, source_target_pairs={{0,1},{1,0},{2,3},{3,2},{4,5},{5,4},{6,7},{7,6},{8,9},{9,8},{10,11... | collective-permute-start | bytes 1228808 | tf_op jit(solution)/shard_map/ppermute | solution.py:375
  69.6 2.4 %collective-permute-start.23 = (bf16[2,160,640]{2,1,0:T(8,128)(2,1)S(1)}, bf16[2,160,640]{2,1,0:T(8,128)(2,1)S(1)}, u32[]{:S(2)}, u32[]{:S(2)}) collective-permute-start(bf16[2,160,640]{2,1,0:T(8,128)(2,1)S(1)} %get-tuple-element.105), channel_id=1, source_target_pairs={{0,1},{1,0},{2,3},{3,2},{4,5},{5,4},{6,7},{7,6},{8,9},{9,8},{10,11... | collective-permute-start | bytes 1228808 | tf_op jit(solution)/shard_map/ppermute | solution.py:375
  69.8 7.9 %collective-permute-start.25 = (bf16[1,160,640]{2,1,0:T(8,128)(2,1)S(1)}, bf16[1,160,640]{2,1,0:T(8,128)(2,1)S(1)}, u32[]{:S(2)}, u32[]{:S(2)}) collective-permute-start(bf16[1,160,640]{2,1,0:T(8,128)(2,1)S(1)} %get-tuple-element.107), channel_id=1, source_target_pairs={{0,2},{1,3},{2,0},{3,1},{4,6},{5,7},{6,4},{7,5},{8,10},{9,11},{10,... | collective-permute-start | bytes 614408 | tf_op jit(solution)/shard_map/ppermute | solution.py:375
  71.2 10.8 %collective-permute-start.21 = (bf16[1,160,640]{2,1,0:T(8,128)(2,1)S(1)}, bf16[1,160,640]{2,1,0:T(8,128)(2,1)S(1)}, u32[]{:S(2)}, u32[]{:S(2)}) collective-permute-start(bf16[1,160,640]{2,1,0:T(8,128)(2,1)S(1)} %get-tuple-element.99), channel_id=1, source_target_pairs={{0,2},{1,3},{2,0},{3,1},{4,6},{5,7},{6,4},{7,5},{8,10},{9,11},{10,... | collective-permute-start | bytes 614408 | tf_op jit(solution)/shard_map/ppermute | solution.py:375
  72.0 13.9 %collective-permute-start.24 = (bf16[1,160,640]{2,1,0:T(8,128)(2,1)S(1)}, bf16[1,160,640]{2,1,0:T(8,128)(2,1)S(1)}, u32[]{:S(2)}, u32[]{:S(2)}) collective-permute-start(bf16[1,160,640]{2,1,0:T(8,128)(2,1)S(1)} %get-tuple-element.106), channel_id=1, source_target_pairs={{0,2},{1,3},{2,0},{3,1},{4,6},{5,7},{6,4},{7,5},{8,10},{9,11},{10,... | collective-permute-start | bytes 614408 | tf_op jit(solution)/shard_map/ppermute | solution.py:375
  86.7 1.8 %collective-permute-start.26 = (bf16[2,160,640]{2,1,0:T(8,128)(2,1)S(1)}, bf16[2,160,640]{2,1,0:T(8,128)(2,1)S(1)}, u32[]{:S(2)}, u32[]{:S(2)}) collective-permute-start(bf16[2,160,640]{2,1,0:T(8,128)(2,1)S(1)} %get-tuple-element.110), channel_id=1, source_target_pairs={{0,1},{1,0},{2,3},{3,2},{4,5},{5,4},{6,7},{7,6},{8,9},{9,8},{10,11... | collective-permute-start | bytes 1228808 | tf_op jit(solution)/shard_map/ppermute | solution.py:375
  86.8 8.4 %collective-permute-start.28 = (bf16[160,640]{1,0:T(8,128)(2,1)S(1)}, bf16[160,640]{1,0:T(8,128)(2,1)S(1)}, u32[]{:S(2)}, u32[]{:S(2)}) collective-permute-start(bf16[160,640]{1,0:T(8,128)(2,1)S(1)} %fusion), channel_id=1, source_target_pairs={{0,8},{1,9},{2,10},{3,11},{4,0},{5,1},{6,2},{7,3},{8,12},{9,13},{1... | collective-permute-start | bytes 614408 | tf_op jit(solution)/shard_map/ppermute | solution.py:382
  88.6 7.2 %collective-permute-start.27 = (bf16[1,160,640]{2,1,0:T(8,128)(2,1)S(1)}, bf16[1,160,640]{2,1,0:T(8,128)(2,1)S(1)}, u32[]{:S(2)}, u32[]{:S(2)}) collective-permute-start(bf16[1,160,640]{2,1,0:T(8,128)(2,1)S(1)} %get-tuple-element.112), channel_id=1, source_target_pairs={{0,2},{1,3},{2,0},{3,1},{4,6},{5,7},{6,4},{7,5},{8,10},{9,11},{10,... | collective-permute-start | bytes 614408 | tf_op jit(solution)/shard_map/ppermute | solution.py:375

commit v19 on v18

--- a/solution.py
+++ b/solution.py
@@ -33,7 +33,7 @@
     rows, nobs = flux.shape
     taps = resolution.shape[0]
     tiles = rows // tall
-    ahead = min(3, tiles)
+    ahead = min(4, tiles)
 
     def own_rows(tile):
         return pl.ds(pl.multiple_of(tile * tall, tall), tall)
@@ -187,17 +187,19 @@
     for i in range(len(windows)):
         own = slice(i * count, (i + 1) * count)
         window[own, :] = windows[i][:, columns[0] : columns[1]]
-        named_ref[own, :] = jnp.broadcast_to(names[i], (band, count)).T
+        named_ref[own, :] = jnp.broadcast_to(names[i], (band, count)).T.astype(BF16)
     named = named_ref[...]
     for p in range(len(weights)):
         hits = [
-            (named == bins_ref[p * OUTER + b].astype(F32)).astype(F32).astype(BF16)
+            named == jnp.full((1, band), bins_ref[p * OUTER + b].astype(F32), F32).astype(BF16)
             for b in range(OUTER)
         ]
         for at in range(0, window.shape[1], band):
             lanes = slice(at, at + band)
             rows = slice(columns[0] + at, columns[0] + at + band)
-            masked = jnp.concatenate([window[:, lanes] * hit for hit in hits], axis=1)
+            masked = jnp.concatenate(
+                [jnp.where(hit, window[:, lanes], jnp.zeros((), BF16)) for hit in hits], axis=1
+            )
             weight = jnp.concatenate([weights[p][b, rows, :] for b in range(OUTER)], axis=1)
             value = lax.dot_general(masked, weight, (((1,), (1,)), ((), ())), preferred_element_type=F32)
             if p or begun:
@@ -220,7 +222,7 @@
         jax.ShapeDtypeStruct((rows, width), F32),
         [SMEM] + [VMEM] * (1 + len(aways) + len(weights)),
         (bins, names, *windows, *weights),
-        [pltpu.VMEM((rows, width), BF16), pltpu.VMEM((rows, band), F32)],
+        [pltpu.VMEM((rows, width), BF16), pltpu.VMEM((rows, band), BF16)],
     )
 
 
@@ -257,7 +259,7 @@
         ),
         [SMEM, SMEM] + [VMEM] * (1 + OUTER + 2 + len(weights)),
         (outer, bins, names, *windows, own, others, *weights),
-        [pltpu.VMEM((rows, width), BF16), pltpu.VMEM((rows, band), F32), pltpu.VMEM((rows, width), F32)],
+        [pltpu.VMEM((rows, width), BF16), pltpu.VMEM((rows, band), BF16), pltpu.VMEM((rows, width), F32)],
     )
 
 

time: 97.6 us -> 97.5 us (level)
  transfers between devices with their start and end apart: 29 -> 29, of which waited for: 16 -> 15; matrix products, arithmetic and copies ran while one was open for 2% -> 2% of each run, Pallas kernels for 21% -> 21%
where the time goes in v19:
time: 97.5 us; the launch traced here: 97.3 us
  waiting for transfers between devices  37 us (38%)
  starting transfers between devices  32.4 us (33%)
  Pallas kernels  25 us (26%)
  local copies, waits for them, and re-layouts  1.37 us (1%)
  other arithmetic  1.28 us (1%)
    ppermute x25, waiting for transfers between devices, swap(): return lax.ppermute(array, 'spec', [(i, i ^ bit) for i in range(n)])  27.7 us
    ppermute x25, starting transfers between devices, swap(): return lax.ppermute(array, 'spec', [(i, i ^ bit) for i in range(n)])  27.2 us
    pallas_call x17, Pallas kernels, call(): pl.pallas_call(kernel, out_shape=out_shape, in_specs=in_specs, out_specs=...  22.1 us
    ppermute x4, waiting for transfers between devices, step(): lax.ppermute(array, 'spec', [(o * inner + i, to[o] * inner + i) for o in...  9.21 us
    ppermute x4, starting transfers between devices, step(): lax.ppermute(array, 'spec', [(o * inner + i, to[o] * inner + i) for o in...  5.17 us
    pallas_call x2, Pallas kernels, place(): pl.pallas_call(functools.partial(place_kernel, slots, last), out_shape=ja...  2.98 us
  transfers between devices with their start and end apart: 29, of which 15 were waited for; matrix products, arithmetic and copies ran while one was open for 2% of the time, Pallas kernels for 21%

profile of v19, /device:TPU:0, one launch (start us, length us, event | category | flops | bytes accessed | tf_op | source)
XLA Modules:
  0.0 97.3 jit_solution(12890468610058461172)
XLA Ops:
  0.0 0.8 pad_add_fusion.3
  0.8 3.0 %collective-permute-start = (s32[148]{0:T(256)S(1)}, s32[148]{0:T(256)S(1)}, u32[]{:S(2)}, u32[]{:S(2)}) collective-permute-start(s32[148]{0:T(256)S(1)} %pad_add_fusion.3), channel_id=1, source_target_pairs={{0,4},{1,5},{2,6},{3,7},{4,0},{5,1},{6,2},{7,3},{8,12},{9,13},{10,... | collective-permute-start | bytes 1784 | tf_op jit(solution)/shard_map/ppermute | solution.py:377
  3.9 2.6 %collective-permute-start.1 = (s32[148]{0:T(256)S(1)}, s32[148]{0:T(256)S(1)}, u32[]{:S(2)}, u32[]{:S(2)}) collective-permute-start(s32[148]{0:T(256)S(1)} %pad_add_fusion.3), channel_id=1, source_target_pairs={{0,8},{1,9},{2,10},{3,11},{4,12},{5,13},{6,14},{7,15},{8,0},{9,1},... | collective-permute-start | bytes 1784 | tf_op jit(solution)/shard_map/ppermute | solution.py:377
  6.5 1.2 %dynamic-slice_bitcast_fusion = (bf16[640,128]{1,0:T(8,128)(2,1)S(1)}, bf16[640,128]{1,0:T(8,128)(2,1)S(1)}, bf16[640,128]{1,0:T(8,128)(2,1)S(1)}, bf16[640,128]{1,0:T(8,128)(2,1)S(1)}) fusion(bf16[4,640,128]{2,1,0:T(8,128)(2,1)} %bitcast.47, s32[]{:T(128)S(6)} %select_n.41, s32[]{:T(128)S(6)} %select_n.40, s32[]{:T(128)S(6)} %select_n.39, s32[]{:T(128)S(6)} %select_n.38), kind=kLoop, calls=%fused_computation.3 | loop fusion | bytes 1310736 | tf_op jit(solution)/shard_map/jit(dynamic_index_in_dim)/squeeze | solution.py:403
  7.7 1.0 collective-permute-start.3
  8.6 3.5 %collective-permute-start.4 = (bf16[640,128]{1,0:T(8,128)(2,1)S(1)}, bf16[640,128]{1,0:T(8,128)(2,1)S(1)}, u32[]{:S(2)}, u32[]{:S(2)}) collective-permute-start(bf16[640,128]{1,0:T(8,128)(2,1)S(1)} %get-tuple-element.120), channel_id=1, source_target_pairs={{0,8},{1,9},{2,10},{3,11},{4,12},{5,13},{6,14},{7,15},{8,0},{9,1},... | collective-permute-start | bytes 491528 | tf_op jit(solution)/shard_map/ppermute | solution.py:377
  12.2 0.1 collective-permute-start.6
  12.2 0.1 slice_bitcast_fusion.1.targets_ref
  12.3 1.1 %collective-permute-done.6 = s32[4,1,20]{2,0,1:T(4,128)S(1)} collective-permute-done((s32[4,1,20]{2,0,1:T(4,128)S(1)}, s32[4,1,20]{2,0,1:T(4,128)S(1)}, u32[]{:S(2)}, u32[]{:S(2)}) %collective-permute-start.6) | collective-permute-done | bytes 352 | tf_op jit(solution)/shard_map/ppermute | solution.py:377
  13.4 1.7 %collective-permute-start.7 = (s32[4,2,20]{2,0,1:T(4,128)S(1)}, s32[4,2,20]{2,0,1:T(4,128)S(1)}, u32[]{:S(2)}, u32[]{:S(2)}) collective-permute-start(s32[4,2,20]{2,0,1:T(4,128)S(1)} %pad_add_fusion.2), channel_id=1, source_target_pairs={{0,2},{1,3},{2,0},{3,1},{4,6},{5,7},{6,4},{7,5},{8,10},{9,11},{10,... | collective-permute-start | bytes 1928 | tf_op jit(solution)/shard_map/ppermute | solution.py:377
  15.1 0.1 pad_add_fusion.5.me_ref
  15.2 0.2 shard_map.55
  15.4 6.6 %shard_map.56.smoothed_ref = bf16[128,3968]{1,0:T(8,128)(2,1)S(1)} custom-call(bf16[128,3968]{1,0:T(8,128)(2,1)S(1)} %copy-done, bf16[11,128,3968]{2,1,0:T(8,128)(2,1)} %bitcast.45), custom_call_target="tpu_custom_call" | custom-call | flops 1 | bytes 1 | tf_op jit(solution)/shard_map/pallas_call | solution.py:20
  22.1 4.7 %shard_map.57 = (bf16[128,640]{1,0:T(8,128)(2,1)S(1)}, bf16[128,640]{1,0:T(8,128)(2,1)S(1)}, bf16[128,640]{1,0:T(8,128)(2,1)S(1)}, bf16[128,640]{1,0:T(8,128)(2,1)S(1)}) custom-call(s32[2]{0:T(128)S(1)} %pad_add_fusion.5.me_ref, s32[2,128]{1,0:T(2,128)S(1)} %get-tuple-element.62.groups_ref, s32[16,20]{1,0:T(8,128)S(1)} %get-tuple-element.124.starts_ref, ...), custom_call_target="tpu_custom_call" | custom-call | flops 1 | bytes 1 | tf_op jit(solution)/shard_map/pallas_call | solution.py:20
  26.8 0.1 pad_maximum_fusion.refs_1_.refs_3_
  26.9 0.1 collective-permute-start.9
  27.0 0.4 collective-permute-start.8
  27.3 1.7 %collective-permute-start.11 = (bf16[128,640]{1,0:T(8,128)(2,1)S(1)}, bf16[128,640]{1,0:T(8,128)(2,1)S(1)}, u32[]{:S(2)}, u32[]{:S(2)}) collective-permute-start(bf16[128,640]{1,0:T(8,128)(2,1)S(1)} %get-tuple-element.78), channel_id=1, source_target_pairs={{0,8},{1,9},{2,10},{3,11},{4,12},{5,13},{6,14},{7,15},{8,0},{9,1},... | collective-permute-start | bytes 491528 | tf_op jit(solution)/shard_map/ppermute | solution.py:377
  29.0 2.1 %collective-permute-start.12 = (bf16[128,640]{1,0:T(8,128)(2,1)S(1)}, bf16[128,640]{1,0:T(8,128)(2,1)S(1)}, u32[]{:S(2)}, u32[]{:S(2)}) collective-permute-start(bf16[128,640]{1,0:T(8,128)(2,1)S(1)} %get-tuple-element.79), channel_id=1, source_target_pairs={{0,12},{1,13},{2,14},{3,15},{4,8},{5,9},{6,10},{7,11},{8,4},{9,5},... | collective-permute-start | bytes 491528 | tf_op jit(solution)/shard_map/ppermute | solution.py:377
  31.2 0.6 collective-permute-start.10
  31.7 0.1 pad_add_fusion.6.bins_ref
  31.8 0.1 slice.12.names_ref
  31.9 1.1 %shard_map.58.refs_4_ = f32[128,640]{1,0:T(8,128)S(1)} custom-call(s32[8]{0:T(128)S(1)} %pad_add_fusion.6.bins_ref, s32[4,128]{1,0:T(4,128)S(1)} %slice.12.names_ref, bf16[128,640]{1,0:T(8,128)(2,1)S(1)} %get-tuple-element.80.refs_0_, bf16[4,640,128]{2,1,0:T(8,128)(2,1)S(1)} %pad_maximum_fusion.refs_1_.refs_3_, ...), custom_call_target="tpu_custom_call" | custom-call | flops 1 | bytes 1 | tf_op jit(solution)/shard_map/pallas_call | solution.py:20
  33.0 9.3 %collective-permute-done.11.refs_1_.refs_2_ = bf16[128,640]{1,0:T(8,128)(2,1)S(1)} collective-permute-done((bf16[128,640]{1,0:T(8,128)(2,1)S(1)}, bf16[128,640]{1,0:T(8,128)(2,1)S(1)}, u32[]{:S(2)}, u32[]{:S(2)}) %collective-permute-start.11) | collective-permute-done | bytes 163872 | tf_op jit(solution)/shard_map/ppermute | solution.py:377
  42.4 1.8 %collective-permute-done.8.refs_6_ = bf16[4,640,128]{2,1,0:T(8,128)(2,1)S(1)} collective-permute-done((bf16[4,640,128]{2,1,0:T(8,128)(2,1)S(1)}, bf16[4,640,128]{2,1,0:T(8,128)(2,1)S(1)}, u32[]{:S(2)}, u32[]{:S(2)}) %collective-permute-start.8) | collective-permute-done | bytes 655392 | tf_op jit(solution)/shard_map/ppermute | solution.py:377
  44.1 0.1 pad_add_fusion.4.bins_ref
  44.2 1.4 %shard_map.59.refs_5_ = f32[384,384]{1,0:T(8,128)S(1)} custom-call(s32[8]{0:T(128)S(1)} %pad_add_fusion.6.bins_ref, s32[4,128]{1,0:T(4,128)S(1)} %slice.12.names_ref, bf16[128,640]{1,0:T(8,128)(2,1)S(1)} %collective-permute-done.10.refs_0_.refs_1_, bf16[128,640]{1,0:T(8,128)(2,1)S(1)} %collective-permute-done.11.refs_1_.refs_2_, ...), custom_call_target="tpu_custom_call" | custom-call | flops 1 | bytes 1 | tf_op jit(solution)/shard_map/pallas_call | solution.py:20
  45.6 0.6 collective-permute-done.13.refs_7_
  46.2 1.7 %shard_map.60 = (f32[512,384]{1,0:T(8,128)S(1)}, bf16[512,384]{1,0:T(8,128)(2,1)S(1)}, f32[4,128]{1,0:T(4,128)S(1)}) custom-call(s32[1]{0:T(128)} %bitcast.1.outer_ref, s32[8]{0:T(128)S(1)} %pad_add_fusion.4.bins_ref, s32[4,128]{1,0:T(4,128)S(1)} %slice.12.names_ref, bf16[128,640]{1,0:T(8,128)(2,1)S(1)} %get-tuple-element.80.refs_0_, ...), custom_call_target="tpu_custom_call" | custom-call | flops 1 | bytes 1 | tf_op jit(solution)/shard_map/pallas_call | solution.py:20
  47.9 1.6 %collective-permute-start.17 = (bf16[512,384]{1,0:T(8,128)(2,1)S(1)}, bf16[512,384]{1,0:T(8,128)(2,1)S(1)}, u32[]{:S(2)}, u32[]{:S(2)}) collective-permute-start(bf16[512,384]{1,0:T(8,128)(2,1)S(1)} %get-tuple-element.90.refs_1_), channel_id=1, source_target_pairs={{0,4},{1,5},{2,6},{3,7},{4,12},{5,13},{6,14},{7,15},{8,0},{9,1},{1... | collective-permute-start | bytes 1179656 | tf_op jit(solution)/shard_map/ppermute | solution.py:384
  49.5 1.2 %shard_map.61.refs_5_ = f32[384,256]{1,0:T(8,128)S(1)} custom-call(s32[8]{0:T(128)S(1)} %pad_add_fusion.6.bins_ref, s32[4,128]{1,0:T(4,128)S(1)} %slice.12.names_ref, bf16[128,640]{1,0:T(8,128)(2,1)S(1)} %collective-permute-done.10.refs_0_.refs_1_, bf16[128,640]{1,0:T(8,128)(2,1)S(1)} %collective-permute-done.11.refs_1_.refs_2_, ...), custom_call_target="tpu_custom_call" | custom-call | flops 1 | bytes 1 | tf_op jit(solution)/shard_map/pallas_call | solution.py:20
  50.7 1.4 %shard_map.62 = (f32[512,256]{1,0:T(8,128)S(1)}, bf16[512,256]{1,0:T(8,128)(2,1)S(1)}, f32[4,128]{1,0:T(4,128)S(1)}) custom-call(s32[1]{0:T(128)} %bitcast.1.outer_ref, s32[8]{0:T(128)S(1)} %pad_add_fusion.4.bins_ref, s32[4,128]{1,0:T(4,128)S(1)} %slice.12.names_ref, bf16[128,640]{1,0:T(8,128)(2,1)S(1)} %get-tuple-element.80.refs_0_, ...), custom_call_target="tpu_custom_call" | custom-call | flops 1 | bytes 1 | tf_op jit(solution)/shard_map/pallas_call | solution.py:20
  52.1 2.7 %collective-permute-start.14 = (f32[4,128]{1,0:T(4,128)S(1)}, f32[4,128]{1,0:T(4,128)S(1)}, u32[]{:S(2)}, u32[]{:S(2)}) collective-permute-start(f32[4,128]{1,0:T(4,128)S(1)} %add.60), channel_id=1, source_target_pairs={{0,4},{1,5},{2,6},{3,7},{4,0},{5,1},{6,2},{7,3},{8,12},{9,13},{10,... | collective-permute-start | bytes 6152 | tf_op jit(solution)/shard_map/ppermute | solution.py:377
  54.8 0.5 collective-permute-start.15
  55.3 1.9 %collective-permute-start.16 = (f32[4,128]{1,0:T(4,128)S(1)}, f32[4,128]{1,0:T(4,128)S(1)}, u32[]{:S(2)}, u32[]{:S(2)}) collective-permute-start(f32[4,128]{1,0:T(4,128)S(1)} %add.60), channel_id=1, source_target_pairs={{0,12},{1,13},{2,14},{3,15},{4,8},{5,9},{6,10},{7,11},{8,4},{9,5},... | collective-permute-start | bytes 6152 | tf_op jit(solution)/shard_map/ppermute | solution.py:377
  57.2 1.0 %collective-permute-start.18 = (bf16[512,256]{1,0:T(8,128)(2,1)S(1)}, bf16[512,256]{1,0:T(8,128)(2,1)S(1)}, u32[]{:S(2)}, u32[]{:S(2)}) collective-permute-start(bf16[512,256]{1,0:T(8,128)(2,1)S(1)} %get-tuple-element.93.refs_2_), channel_id=1, source_target_pairs={{0,4},{1,5},{2,6},{3,7},{4,12},{5,13},{6,14},{7,15},{8,0},{9,1},{1... | collective-permute-start | bytes 786440 | tf_op jit(solution)/shard_map/ppermute | solution.py:384
  58.3 0.7 collective-permute-done.14
  59.0 1.2 %collective-permute-done.15 = f32[4,128]{1,0:T(4,128)S(1)} collective-permute-done((f32[4,128]{1,0:T(4,128)S(1)}, f32[4,128]{1,0:T(4,128)S(1)}, u32[]{:S(2)}, u32[]{:S(2)}) %collective-permute-start.15) | collective-permute-done | bytes 2080 | tf_op jit(solution)/shard_map/ppermute | solution.py:377
  60.2 2.0 %collective-permute-done.16 = f32[4,128]{1,0:T(4,128)S(1)} collective-permute-done((f32[4,128]{1,0:T(4,128)S(1)}, f32[4,128]{1,0:T(4,128)S(1)}, u32[]{:S(2)}, u32[]{:S(2)}) %collective-permute-start.16) | collective-permute-done | bytes 2080 | tf_op jit(solution)/shard_map/ppermute | solution.py:377
  62.2 0.2 shard_map.63.refs_0_.refs_2_
  62.4 0.8 shard_map.64
  63.2 2.6 %collective-permute-done.18.refs_1_ = bf16[512,256]{1,0:T(8,128)(2,1)S(1)} collective-permute-done((bf16[512,256]{1,0:T(8,128)(2,1)S(1)}, bf16[512,256]{1,0:T(8,128)(2,1)S(1)}, u32[]{:S(2)}, u32[]{:S(2)}) %collective-permute-start.18) | collective-permute-done | bytes 262176 | tf_op jit(solution)/shard_map/ppermute | solution.py:384
  65.9 0.9 shard_map.65
  66.7 0.1 collective-permute-start.22
  66.8 0.8 collective-permute-start.19
  67.6 0.2 collective-permute-start.20
  67.8 0.8 collective-permute-done.22.got_ref
  68.5 0.1 shard_map.67
  68.6 0.8 shard_map.68
  69.4 0.2 collective-permute-start.23
  69.6 1.3 %collective-permute-start.25 = (bf16[1,160,640]{2,1,0:T(8,128)(2,1)S(1)}, bf16[1,160,640]{2,1,0:T(8,128)(2,1)S(1)}, u32[]{:S(2)}, u32[]{:S(2)}) collective-permute-start(bf16[1,160,640]{2,1,0:T(8,128)(2,1)S(1)} %get-tuple-element.107), channel_id=1, source_target_pairs={{0,2},{1,3},{2,0},{3,1},{4,6},{5,7},{6,4},{7,5},{8,10},{9,11},{10,... | collective-permute-start | bytes 614408 | tf_op jit(solution)/shard_map/ppermute | solution.py:377
  71.1 0.8 collective-permute-start.21
  71.9 1.4 %collective-permute-start.24 = (bf16[1,160,640]{2,1,0:T(8,128)(2,1)S(1)}, bf16[1,160,640]{2,1,0:T(8,128)(2,1)S(1)}, u32[]{:S(2)}, u32[]{:S(2)}) collective-permute-start(bf16[1,160,640]{2,1,0:T(8,128)(2,1)S(1)} %get-tuple-element.106), channel_id=1, source_target_pairs={{0,2},{1,3},{2,0},{3,1},{4,6},{5,7},{6,4},{7,5},{8,10},{9,11},{10,... | collective-permute-start | bytes 614408 | tf_op jit(solution)/shard_map/ppermute | solution.py:377
  73.3 4.2 %collective-permute-done.25 = bf16[1,160,640]{2,1,0:T(8,128)(2,1)S(1)} collective-permute-done((bf16[1,160,640]{2,1,0:T(8,128)(2,1)S(1)}, bf16[1,160,640]{2,1,0:T(8,128)(2,1)S(1)}, u32[]{:S(2)}, u32[]{:S(2)}) %collective-permute-start.25) | collective-permute-done | bytes 204832 | tf_op jit(solution)/shard_map/ppermute | solution.py:377
  77.6 4.4 %collective-permute-done.21 = bf16[1,160,640]{2,1,0:T(8,128)(2,1)S(1)} collective-permute-done((bf16[1,160,640]{2,1,0:T(8,128)(2,1)S(1)}, bf16[1,160,640]{2,1,0:T(8,128)(2,1)S(1)}, u32[]{:S(2)}, u32[]{:S(2)}) %collective-permute-start.21) | collective-permute-done | bytes 204832 | tf_op jit(solution)/shard_map/ppermute | solution.py:377
  81.9 2.9 %collective-permute-done.19.refs_1_ = bf16[512,640]{1,0:T(8,128)(2,1)S(1)} collective-permute-done((bf16[512,640]{1,0:T(8,128)(2,1)S(1)}, bf16[512,640]{1,0:T(8,128)(2,1)S(1)}, u32[]{:S(2)}, u32[]{:S(2)}) %collective-permute-start.19) | collective-permute-done | bytes 655392 | tf_op jit(solution)/shard_map/ppermute | solution.py:384
  84.8 0.9 collective-permute-done.24
  85.8 0.8 shard_map.70
  86.7 1.7 %collective-permute-start.28 = (bf16[160,640]{1,0:T(8,128)(2,1)S(1)}, bf16[160,640]{1,0:T(8,128)(2,1)S(1)}, u32[]{:S(2)}, u32[]{:S(2)}) collective-permute-start(bf16[160,640]{1,0:T(8,128)(2,1)S(1)} %fusion), channel_id=1, source_target_pairs={{0,8},{1,9},{2,10},{3,11},{4,0},{5,1},{6,2},{7,3},{8,12},{9,13},{1... | collective-permute-start | bytes 614408 | tf_op jit(solution)/shard_map/ppermute | solution.py:384
  88.5 1.4 %collective-permute-start.27 = (bf16[1,160,640]{2,1,0:T(8,128)(2,1)S(1)}, bf16[1,160,640]{2,1,0:T(8,128)(2,1)S(1)}, u32[]{:S(2)}, u32[]{:S(2)}) collective-permute-start(bf16[1,160,640]{2,1,0:T(8,128)(2,1)S(1)} %get-tuple-element.112), channel_id=1, source_target_pairs={{0,2},{1,3},{2,0},{3,1},{4,6},{5,7},{6,4},{7,5},{8,10},{9,11},{10,... | collective-permute-start | bytes 614408 | tf_op jit(solution)/shard_map/ppermute | solution.py:377
  90.0 1.5 %shard_map.72.refs_4_ = f32[160,2560]{1,0:T(8,128)} custom-call(s32[4]{0:T(128)S(1)} %shift-right-arithmetic_xor_fusion.at_ref, f32[160,640]{1,0:T(8,128)S(1)} %bitcast.39, bf16[160,640]{1,0:T(8,128)(2,1)S(1)} %bitcast.42, f32[160,640]{1,0:T(8,128)S(1)} %bitcast.40, bf16[160,640]{1,0:T(8,128)(2,1)S(1)} %bitcast.43), custom_call_target="tpu_custom_call" | custom-call | flops 1 | bytes 1 | tf_op jit(solution)/shard_map/pallas_call | solution.py:351
  91.4 3.7 %collective-permute-done.28.refs_2_ = bf16[160,640]{1,0:T(8,128)(2,1)S(1)} collective-permute-done((bf16[160,640]{1,0:T(8,128)(2,1)S(1)}, bf16[160,640]{1,0:T(8,128)(2,1)S(1)}, u32[]{:S(2)}, u32[]{:S(2)}) %collective-permute-start.28) | collective-permute-done | bytes 204832 | tf_op jit(solution)/shard_map/ppermute | solution.py:384
  95.1 0.7 collective-permute-done.27
  95.8 1.5 %shard_map.73 = f32[160,2560]{1,0:T(8,128)} custom-call(s32[4]{0:T(128)S(1)} %shift-right-arithmetic_xor_fusion.at_ref, f32[160,640]{1,0:T(8,128)S(1)} %bitcast.41, bf16[160,640]{1,0:T(8,128)(2,1)S(1)} %bitcast.44, bf16[160,640]{1,0:T(8,128)(2,1)S(1)} %collective-permute-done.28.refs_2_, ...), custom_call_target="tpu_custom_call", output_to_operand_aliasing={{}: (5, {})} | custom-call | flops 1 | bytes 1 | tf_op jit(solution)/shard_map/pallas_call | solution.py:351
  (37 shorter events, 0.5 us)
Async XLA Ops:
  0.0 15.4 %copy-start = (bf16[128,3968]{1,0:T(8,128)(2,1)S(1)}, bf16[128,3968]{1,0:T(8,128)(2,1)}, u32[]{:S(2)}) copy-start(bf16[128,3968]{1,0:T(8,128)(2,1)} %flux_ref) | copy-start | bytes 3047428
  0.8 11.3 %collective-permute-start = (s32[148]{0:T(256)S(1)}, s32[148]{0:T(256)S(1)}, u32[]{:S(2)}, u32[]{:S(2)}) collective-permute-start(s32[148]{0:T(256)S(1)} %pad_add_fusion.3), channel_id=1, source_target_pairs={{0,4},{1,5},{2,6},{3,7},{4,0},{5,1},{6,2},{7,3},{8,12},{9,13},{10,... | collective-permute-start | bytes 1784 | tf_op jit(solution)/shard_map/ppermute | solution.py:377
  3.9 8.3 %collective-permute-start.1 = (s32[148]{0:T(256)S(1)}, s32[148]{0:T(256)S(1)}, u32[]{:S(2)}, u32[]{:S(2)}) collective-permute-start(s32[148]{0:T(256)S(1)} %pad_add_fusion.3), channel_id=1, source_target_pairs={{0,8},{1,9},{2,10},{3,11},{4,12},{5,13},{6,14},{7,15},{8,0},{9,1},... | collective-permute-start | bytes 1784 | tf_op jit(solution)/shard_map/ppermute | solution.py:377
  6.4 5.7 %collective-permute-start.2 = (s32[148]{0:T(256)S(1)}, s32[148]{0:T(256)S(1)}, u32[]{:S(2)}, u32[]{:S(2)}) collective-permute-start(s32[148]{0:T(256)S(1)} %pad_add_fusion.3), channel_id=1, source_target_pairs={{0,12},{1,13},{2,14},{3,15},{4,8},{5,9},{6,10},{7,11},{8,4},{9,5},... | collective-permute-start | bytes 1784 | tf_op jit(solution)/shard_map/ppermute | solution.py:377
  7.7 19.1 %collective-permute-start.3 = (bf16[640,128]{1,0:T(8,128)(2,1)S(1)}, bf16[640,128]{1,0:T(8,128)(2,1)S(1)}, u32[]{:S(2)}, u32[]{:S(2)}) collective-permute-start(bf16[640,128]{1,0:T(8,128)(2,1)S(1)} %get-tuple-element.121), channel_id=1, source_target_pairs={{0,4},{1,5},{2,6},{3,7},{4,0},{5,1},{6,2},{7,3},{8,12},{9,13},{10,... | collective-permute-start | bytes 491528 | tf_op jit(solution)/shard_map/ppermute | solution.py:377
  8.6 18.2 %collective-permute-start.4 = (bf16[640,128]{1,0:T(8,128)(2,1)S(1)}, bf16[640,128]{1,0:T(8,128)(2,1)S(1)}, u32[]{:S(2)}, u32[]{:S(2)}) collective-permute-start(bf16[640,128]{1,0:T(8,128)(2,1)S(1)} %get-tuple-element.120), channel_id=1, source_target_pairs={{0,8},{1,9},{2,10},{3,11},{4,12},{5,13},{6,14},{7,15},{8,0},{9,1},... | collective-permute-start | bytes 491528 | tf_op jit(solution)/shard_map/ppermute | solution.py:377
  12.1 14.7 %collective-permute-start.5 = (bf16[640,128]{1,0:T(8,128)(2,1)S(1)}, bf16[640,128]{1,0:T(8,128)(2,1)S(1)}, u32[]{:S(2)}, u32[]{:S(2)}) collective-permute-start(bf16[640,128]{1,0:T(8,128)(2,1)S(1)} %get-tuple-element.119), channel_id=1, source_target_pairs={{0,12},{1,13},{2,14},{3,15},{4,8},{5,9},{6,10},{7,11},{8,4},{9,5},... | collective-permute-start | bytes 491528 | tf_op jit(solution)/shard_map/ppermute | solution.py:377
  12.2 1.2 %collective-permute-start.6 = (s32[4,1,20]{2,0,1:T(4,128)S(1)}, s32[4,1,20]{2,0,1:T(4,128)S(1)}, u32[]{:S(2)}, u32[]{:S(2)}) collective-permute-start(s32[4,1,20]{2,0,1:T(4,128)S(1)} %slice_bitcast_fusion), channel_id=1, source_target_pairs={{0,1},{1,0},{2,3},{3,2},{4,5},{5,4},{6,7},{7,6},{8,9},{9,8},{10,11... | collective-permute-start | bytes 968 | tf_op jit(solution)/shard_map/ppermute | solution.py:377
  13.4 8.6 %collective-permute-start.7 = (s32[4,2,20]{2,0,1:T(4,128)S(1)}, s32[4,2,20]{2,0,1:T(4,128)S(1)}, u32[]{:S(2)}, u32[]{:S(2)}) collective-permute-start(s32[4,2,20]{2,0,1:T(4,128)S(1)} %pad_add_fusion.2), channel_id=1, source_target_pairs={{0,2},{1,3},{2,0},{3,1},{4,6},{5,7},{6,4},{7,5},{8,10},{9,11},{10,... | collective-permute-start | bytes 1928 | tf_op jit(solution)/shard_map/ppermute | solution.py:377
  26.9 4.3 %collective-permute-start.9 = (bf16[4,640,128]{2,1,0:T(8,128)(2,1)S(1)}, bf16[4,640,128]{2,1,0:T(8,128)(2,1)S(1)}, u32[]{:S(2)}, u32[]{:S(2)}) collective-permute-start(bf16[4,640,128]{2,1,0:T(8,128)(2,1)S(1)} %pad_maximum_fusion.refs_1_.refs_3_), channel_id=1, source_target_pairs={{0,1},{1,0},{2,3},{3,2},{4,5},{5,4},{6,7},{7,6},{8,9},{9,8},{10,11... | collective-permute-start | bytes 1966088 | tf_op jit(solution)/shard_map/ppermute | solution.py:377
  27.0 17.1 %collective-permute-start.8 = (bf16[4,640,128]{2,1,0:T(8,128)(2,1)S(1)}, bf16[4,640,128]{2,1,0:T(8,128)(2,1)S(1)}, u32[]{:S(2)}, u32[]{:S(2)}) collective-permute-start(bf16[4,640,128]{2,1,0:T(8,128)(2,1)S(1)} %pad_maximum_fusion.refs_1_.refs_3_), channel_id=1, source_target_pairs={{0,2},{1,3},{2,0},{3,1},{4,6},{5,7},{6,4},{7,5},{8,10},{9,11},{10,... | collective-permute-start | bytes 1966088 | tf_op jit(solution)/shard_map/ppermute | solution.py:377
  27.3 15.0 %collective-permute-start.11 = (bf16[128,640]{1,0:T(8,128)(2,1)S(1)}, bf16[128,640]{1,0:T(8,128)(2,1)S(1)}, u32[]{:S(2)}, u32[]{:S(2)}) collective-permute-start(bf16[128,640]{1,0:T(8,128)(2,1)S(1)} %get-tuple-element.78), channel_id=1, source_target_pairs={{0,8},{1,9},{2,10},{3,11},{4,12},{5,13},{6,14},{7,15},{8,0},{9,1},... | collective-permute-start | bytes 491528 | tf_op jit(solution)/shard_map/ppermute | solution.py:377
  29.0 13.3 %collective-permute-start.12 = (bf16[128,640]{1,0:T(8,128)(2,1)S(1)}, bf16[128,640]{1,0:T(8,128)(2,1)S(1)}, u32[]{:S(2)}, u32[]{:S(2)}) collective-permute-start(bf16[128,640]{1,0:T(8,128)(2,1)S(1)} %get-tuple-element.79), channel_id=1, source_target_pairs={{0,12},{1,13},{2,14},{3,15},{4,8},{5,9},{6,10},{7,11},{8,4},{9,5},... | collective-permute-start | bytes 491528 | tf_op jit(solution)/shard_map/ppermute | solution.py:377
  31.2 13.0 %collective-permute-start.10 = (bf16[128,640]{1,0:T(8,128)(2,1)S(1)}, bf16[128,640]{1,0:T(8,128)(2,1)S(1)}, u32[]{:S(2)}, u32[]{:S(2)}) collective-permute-start(bf16[128,640]{1,0:T(8,128)(2,1)S(1)} %get-tuple-element.77), channel_id=1, source_target_pairs={{0,4},{1,5},{2,6},{3,7},{4,0},{5,1},{6,2},{7,3},{8,12},{9,13},{10,... | collective-permute-start | bytes 491528 | tf_op jit(solution)/shard_map/ppermute | solution.py:377
  44.1 2.1 %collective-permute-start.13 = (bf16[4,640,128]{2,1,0:T(8,128)(2,1)S(1)}, bf16[4,640,128]{2,1,0:T(8,128)(2,1)S(1)}, u32[]{:S(2)}, u32[]{:S(2)}) collective-permute-start(bf16[4,640,128]{2,1,0:T(8,128)(2,1)S(1)} %collective-permute-done.8.refs_6_), channel_id=1, source_target_pairs={{0,1},{1,0},{2,3},{3,2},{4,5},{5,4},{6,7},{7,6},{8,9},{9,8},{10,11... | collective-permute-start | bytes 1966088 | tf_op jit(solution)/shard_map/ppermute | solution.py:377
  47.9 14.3 %collective-permute-start.17 = (bf16[512,384]{1,0:T(8,128)(2,1)S(1)}, bf16[512,384]{1,0:T(8,128)(2,1)S(1)}, u32[]{:S(2)}, u32[]{:S(2)}) collective-permute-start(bf16[512,384]{1,0:T(8,128)(2,1)S(1)} %get-tuple-element.90.refs_1_), channel_id=1, source_target_pairs={{0,4},{1,5},{2,6},{3,7},{4,12},{5,13},{6,14},{7,15},{8,0},{9,1},{1... | collective-permute-start | bytes 1179656 | tf_op jit(solution)/shard_map/ppermute | solution.py:384
  52.1 6.9 %collective-permute-start.14 = (f32[4,128]{1,0:T(4,128)S(1)}, f32[4,128]{1,0:T(4,128)S(1)}, u32[]{:S(2)}, u32[]{:S(2)}) collective-permute-start(f32[4,128]{1,0:T(4,128)S(1)} %add.60), channel_id=1, source_target_pairs={{0,4},{1,5},{2,6},{3,7},{4,0},{5,1},{6,2},{7,3},{8,12},{9,13},{10,... | collective-permute-start | bytes 6152 | tf_op jit(solution)/shard_map/ppermute | solution.py:377
  54.8 5.4 %collective-permute-start.15 = (f32[4,128]{1,0:T(4,128)S(1)}, f32[4,128]{1,0:T(4,128)S(1)}, u32[]{:S(2)}, u32[]{:S(2)}) collective-permute-start(f32[4,128]{1,0:T(4,128)S(1)} %add.60), channel_id=1, source_target_pairs={{0,8},{1,9},{2,10},{3,11},{4,12},{5,13},{6,14},{7,15},{8,0},{9,1},... | collective-permute-start | bytes 6152 | tf_op jit(solution)/shard_map/ppermute | solution.py:377
  55.3 6.8 %collective-permute-start.16 = (f32[4,128]{1,0:T(4,128)S(1)}, f32[4,128]{1,0:T(4,128)S(1)}, u32[]{:S(2)}, u32[]{:S(2)}) collective-permute-start(f32[4,128]{1,0:T(4,128)S(1)} %add.60), channel_id=1, source_target_pairs={{0,12},{1,13},{2,14},{3,15},{4,8},{5,9},{6,10},{7,11},{8,4},{9,5},... | collective-permute-start | bytes 6152 | tf_op jit(solution)/shard_map/ppermute | solution.py:377
  57.2 8.6 %collective-permute-start.18 = (bf16[512,256]{1,0:T(8,128)(2,1)S(1)}, bf16[512,256]{1,0:T(8,128)(2,1)S(1)}, u32[]{:S(2)}, u32[]{:S(2)}) collective-permute-start(bf16[512,256]{1,0:T(8,128)(2,1)S(1)} %get-tuple-element.93.refs_2_), channel_id=1, source_target_pairs={{0,4},{1,5},{2,6},{3,7},{4,12},{5,13},{6,14},{7,15},{8,0},{9,1},{1... | collective-permute-start | bytes 786440 | tf_op jit(solution)/shard_map/ppermute | solution.py:384
  66.7 1.8 %collective-permute-start.22 = (bf16[2,160,640]{2,1,0:T(8,128)(2,1)S(1)}, bf16[2,160,640]{2,1,0:T(8,128)(2,1)S(1)}, u32[]{:S(2)}, u32[]{:S(2)}) collective-permute-start(bf16[2,160,640]{2,1,0:T(8,128)(2,1)S(1)} %get-tuple-element.101), channel_id=1, source_target_pairs={{0,1},{1,0},{2,3},{3,2},{4,5},{5,4},{6,7},{7,6},{8,9},{9,8},{10,11... | collective-permute-start | bytes 1228808 | tf_op jit(solution)/shard_map/ppermute | solution.py:377
  66.8 18.0 %collective-permute-start.19 = (bf16[512,640]{1,0:T(8,128)(2,1)S(1)}, bf16[512,640]{1,0:T(8,128)(2,1)S(1)}, u32[]{:S(2)}, u32[]{:S(2)}) collective-permute-start(bf16[512,640]{1,0:T(8,128)(2,1)S(1)} %get-tuple-element.103.refs_1_), channel_id=1, source_target_pairs={{0,4},{1,5},{2,6},{3,7},{4,12},{5,13},{6,14},{7,15},{8,0},{9,1},{1... | collective-permute-start | bytes 1966088 | tf_op jit(solution)/shard_map/ppermute | solution.py:384
  67.6 3.4 %collective-permute-start.20 = (bf16[2,160,640]{2,1,0:T(8,128)(2,1)S(1)}, bf16[2,160,640]{2,1,0:T(8,128)(2,1)S(1)}, u32[]{:S(2)}, u32[]{:S(2)}) collective-permute-start(bf16[2,160,640]{2,1,0:T(8,128)(2,1)S(1)} %get-tuple-element.98), channel_id=1, source_target_pairs={{0,1},{1,0},{2,3},{3,2},{4,5},{5,4},{6,7},{7,6},{8,9},{9,8},{10,11... | collective-permute-start | bytes 1228808 | tf_op jit(solution)/shard_map/ppermute | solution.py:377
  69.4 2.4 %collective-permute-start.23 = (bf16[2,160,640]{2,1,0:T(8,128)(2,1)S(1)}, bf16[2,160,640]{2,1,0:T(8,128)(2,1)S(1)}, u32[]{:S(2)}, u32[]{:S(2)}) collective-permute-start(bf16[2,160,640]{2,1,0:T(8,128)(2,1)S(1)} %get-tuple-element.105), channel_id=1, source_target_pairs={{0,1},{1,0},{2,3},{3,2},{4,5},{5,4},{6,7},{7,6},{8,9},{9,8},{10,11... | collective-permute-start | bytes 1228808 | tf_op jit(solution)/shard_map/ppermute | solution.py:377
  69.6 7.9 %collective-permute-start.25 = (bf16[1,160,640]{2,1,0:T(8,128)(2,1)S(1)}, bf16[1,160,640]{2,1,0:T(8,128)(2,1)S(1)}, u32[]{:S(2)}, u32[]{:S(2)}) collective-permute-start(bf16[1,160,640]{2,1,0:T(8,128)(2,1)S(1)} %get-tuple-element.107), channel_id=1, source_target_pairs={{0,2},{1,3},{2,0},{3,1},{4,6},{5,7},{6,4},{7,5},{8,10},{9,11},{10,... | collective-permute-start | bytes 614408 | tf_op jit(solution)/shard_map/ppermute | solution.py:377
  71.1 10.9 %collective-permute-start.21 = (bf16[1,160,640]{2,1,0:T(8,128)(2,1)S(1)}, bf16[1,160,640]{2,1,0:T(8,128)(2,1)S(1)}, u32[]{:S(2)}, u32[]{:S(2)}) collective-permute-start(bf16[1,160,640]{2,1,0:T(8,128)(2,1)S(1)} %get-tuple-element.99), channel_id=1, source_target_pairs={{0,2},{1,3},{2,0},{3,1},{4,6},{5,7},{6,4},{7,5},{8,10},{9,11},{10,... | collective-permute-start | bytes 614408 | tf_op jit(solution)/shard_map/ppermute | solution.py:377
  71.9 13.9 %collective-permute-start.24 = (bf16[1,160,640]{2,1,0:T(8,128)(2,1)S(1)}, bf16[1,160,640]{2,1,0:T(8,128)(2,1)S(1)}, u32[]{:S(2)}, u32[]{:S(2)}) collective-permute-start(bf16[1,160,640]{2,1,0:T(8,128)(2,1)S(1)} %get-tuple-element.106), channel_id=1, source_target_pairs={{0,2},{1,3},{2,0},{3,1},{4,6},{5,7},{6,4},{7,5},{8,10},{9,11},{10,... | collective-permute-start | bytes 614408 | tf_op jit(solution)/shard_map/ppermute | solution.py:377
  86.6 1.9 %collective-permute-start.26 = (bf16[2,160,640]{2,1,0:T(8,128)(2,1)S(1)}, bf16[2,160,640]{2,1,0:T(8,128)(2,1)S(1)}, u32[]{:S(2)}, u32[]{:S(2)}) collective-permute-start(bf16[2,160,640]{2,1,0:T(8,128)(2,1)S(1)} %get-tuple-element.110), channel_id=1, source_target_pairs={{0,1},{1,0},{2,3},{3,2},{4,5},{5,4},{6,7},{7,6},{8,9},{9,8},{10,11... | collective-permute-start | bytes 1228808 | tf_op jit(solution)/shard_map/ppermute | solution.py:377
  86.7 8.4 %collective-permute-start.28 = (bf16[160,640]{1,0:T(8,128)(2,1)S(1)}, bf16[160,640]{1,0:T(8,128)(2,1)S(1)}, u32[]{:S(2)}, u32[]{:S(2)}) collective-permute-start(bf16[160,640]{1,0:T(8,128)(2,1)S(1)} %fusion), channel_id=1, source_target_pairs={{0,8},{1,9},{2,10},{3,11},{4,0},{5,1},{6,2},{7,3},{8,12},{9,13},{1... | collective-permute-start | bytes 614408 | tf_op jit(solution)/shard_map/ppermute | solution.py:384
  88.5 7.3 %collective-permute-start.27 = (bf16[1,160,640]{2,1,0:T(8,128)(2,1)S(1)}, bf16[1,160,640]{2,1,0:T(8,128)(2,1)S(1)}, u32[]{:S(2)}, u32[]{:S(2)}) collective-permute-start(bf16[1,160,640]{2,1,0:T(8,128)(2,1)S(1)} %get-tuple-element.112), channel_id=1, source_target_pairs={{0,2},{1,3},{2,0},{3,1},{4,6},{5,7},{6,4},{7,5},{8,10},{9,11},{10,... | collective-permute-start | bytes 614408 | tf_op jit(solution)/shard_map/ppermute | solution.py:377

commit v20 on v19

--- a/solution.py
+++ b/solution.py
@@ -130,22 +130,24 @@
     )
 
 
-def cut_kernel(per, band, unroll, me_ref, groups_ref, starts_ref, turns_ref, smoothed_ref, placing_ref, *refs):
-    outs, (placed, cut) = refs[:OUTER], refs[OUTER:]
-    placed[...] = jnp.dot(placing_ref[...], smoothed_ref[...], preferred_element_type=F32)
+def cut_kernel(aways, per, band, unroll, placed_here, me_ref, groups_ref, starts_ref, turns_ref, placing_ref, source_ref, *refs):
+    outs, refs = refs[: len(aways)], refs[len(aways) :]
+    placed, cut = refs if placed_here else (source_ref, refs[0])
+    if placed_here:
+        placed[...] = jnp.dot(placing_ref[...], source_ref[...], preferred_element_type=F32)
 
     def some_groups(step, carry):
         for i in range(unroll):
             group = step * unroll + i
             rows = pl.ds(pl.multiple_of(group * GROUP, GROUP), GROUP)
             entry = groups_ref[0, group] ^ me_ref[0]
-            for away in range(OUTER):
+            for k, away in enumerate(aways):
                 first = (me_ref[1] ^ away) * per
                 for j in range(per):
                     start = pl.multiple_of(starts_ref[entry, first + j], band)
                     wide = placed[rows, pl.ds(start, 2 * band)]
                     turned = pltpu.roll(wide, turns_ref[entry, first + j], 1)
-                    at = (away * per + j) * band
+                    at = (k * per + j) * band
                     cut[rows, at : at + band] = turned[:, :band]
         return carry
 
@@ -154,7 +156,7 @@
         cut[rows, :] = jnp.zeros((unroll * GROUP, cut.shape[1]), F32)
         return carry
 
-    steps = placed.shape[0] // GROUP // unroll
+    steps = cut.shape[0] // GROUP // unroll
     done = jnp.minimum((groups_ref[1, 0] + unroll - 1) // unroll, steps)
     lax.fori_loop(0, done, some_groups, 0)
     lax.fori_loop(done, steps, clear_groups, 0)
@@ -162,22 +164,24 @@
     back = lax.dot_general(
         placing_ref[...], cut[...].astype(BF16), (((0,), (0,)), ((), ())), preferred_element_type=F32
     ).astype(BF16)
-    for away in range(OUTER):
-        outs[away][...] = back[:, away * width : (away + 1) * width]
-
-
-def cut_windows(me, groups, starts, turns, smoothed, placing, band):
+    for k in range(len(aways)):
+        outs[k][...] = back[:, k * width : (k + 1) * width]
+
+
+def cut_windows(aways, me, groups, starts, turns, placing, source, band):
     per = starts.shape[1] // OUTER
     places, rows = placing.shape
-    nobs = smoothed.shape[1]
+    nobs = source.shape[1]
     width = per * band
+    placed_here = source.dtype == BF16
     unroll = max(k for k in range(1, 7) if places // GROUP % k == 0)
-    return call(
-        functools.partial(cut_kernel, per, band, unroll),
-        (jax.ShapeDtypeStruct((rows, width), BF16),) * OUTER,
+    placed = (jax.ShapeDtypeStruct((places, nobs), F32),) if placed_here else ()
+    return call(
+        functools.partial(cut_kernel, aways, per, band, unroll, placed_here),
+        (jax.ShapeDtypeStruct((rows, width), BF16),) * len(aways) + placed,
         [SMEM] * 4 + [VMEM] * 2,
-        (me, groups, starts, turns, smoothed, placing),
-        [pltpu.VMEM((places, nobs), F32), pltpu.VMEM((places, OUTER * width), F32)],
+        (me, groups, starts, turns, placing, source),
+        [pltpu.VMEM((places, len(aways) * width), F32)],
         limit=max(12 * 1024 * 1024, places * (nobs + OUTER * width) * 6),
     )
 
@@ -411,9 +415,10 @@
     chunk = jnp.minimum(offsets // band, nobs // band - 2)
     turns = (2 * band + chunk * band - offsets) & (2 * band - 1)
     outer1 = outer.reshape(1)
-    windows = cut_windows(jnp.stack([me, outer]), group_bins, chunk * band, turns, smoothed, placing, band)
-
-    pieces, *windows = lax.optimization_barrier((pieces, *windows))
+    tables = (jnp.stack([me, outer]), group_bins, chunk * band, turns, placing)
+    *distant, placed = cut_windows((2, 3), *tables, smoothed, band)
+
+    pieces, *distant = lax.optimization_barrier((pieces, *distant))
     mixed = jnp.stack(pieces)
     bit = inner // 2
     weights = [mixed, swap(mixed, bit)]
@@ -423,7 +428,8 @@
         bit //= 2
         bits.append(bit)
         near = near + [swap(piece, bit) for piece in near]
-    windows[1], near[-1] = lax.optimization_barrier((windows[1], near[-1]))
+    placed, near[-1] = lax.optimization_barrier((placed, near[-1]))
+    windows = cut_windows((0, 1), *tables, placed, band) + tuple(distant)
     arrived = [windows[0]] + [swap(windows[away], away * inner) for away in range(1, OUTER)]
     near_bins = [mine]
     for bit in bits:

time: 97.5 us -> 98 us (level)
  Pallas kernels: 25 us -> 26.4 us
  waiting for transfers between devices: 37 us -> 35.7 us
  local copies, waits for them, and re-layouts: 1.37 us -> 2.57 us
    ppermute x4, starting transfers between devices: 5.17 us -> 3.25 us  [step(): lax.ppermute(array, 'spec', [(o * inner + i, to[o] * inner + i) for o in...]
    pallas_call x17 -> x18, Pallas kernels: 22.1 us -> 23.4 us  [call(): pl.pallas_call(kernel, out_shape=out_shape, in_specs=in_specs, out_specs=...]
    ppermute x25, starting transfers between devices: 27.2 us -> 28.5 us  [swap(): return lax.ppermute(array, 'spec', [(i, i ^ bit) for i in range(n)])]
    unnamed x2, local copies, waits for them, and re-layouts: 0.01 us -> 1.21 us
  transfers between devices with their start and end apart: 29 -> 29, of which waited for: 15 -> 17; matrix products, arithmetic and copies ran while one was open for 2% -> 2% of each run, Pallas kernels for 21% -> 22%
where the time goes in v20:
time: 98 us; the launch traced here: 97.8 us
  waiting for transfers between devices  35.7 us (36%)
  starting transfers between devices  31.7 us (32%)
  Pallas kernels  26.4 us (27%)
  local copies, waits for them, and re-layouts  2.57 us (3%)
  other arithmetic  1.19 us (1%)
    ppermute x25, starting transfers between devices, swap(): return lax.ppermute(array, 'spec', [(i, i ^ bit) for i in range(n)])  28.5 us
    ppermute x25, waiting for transfers between devices, swap(): return lax.ppermute(array, 'spec', [(i, i ^ bit) for i in range(n)])  26.9 us
    pallas_call x18, Pallas kernels, call(): pl.pallas_call(kernel, out_shape=out_shape, in_specs=in_specs, out_specs=...  23.4 us
    ppermute x4, waiting for transfers between devices, step(): lax.ppermute(array, 'spec', [(o * inner + i, to[o] * inner + i) for o in...  8.79 us
    ppermute x4, starting transfers between devices, step(): lax.ppermute(array, 'spec', [(o * inner + i, to[o] * inner + i) for o in...  3.25 us
    pallas_call x2, Pallas kernels, place(): pl.pallas_call(functools.partial(place_kernel, slots, last), out_shape=ja...  2.98 us
  transfers between devices with their start and end apart: 29, of which 17 were waited for; matrix products, arithmetic and copies ran while one was open for 2% of the time, Pallas kernels for 22%

profile of v20, /device:TPU:0, one launch (start us, length us, event | category | flops | bytes accessed | tf_op | source)
XLA Modules:
  0.0 97.8 jit_solution(15459867842870129498)
XLA Ops:
  0.0 0.7 pad_add_fusion.3
  0.7 3.0 %collective-permute-start = (s32[148]{0:T(256)S(1)}, s32[148]{0:T(256)S(1)}, u32[]{:S(2)}, u32[]{:S(2)}) collective-permute-start(s32[148]{0:T(256)S(1)} %pad_add_fusion.3), channel_id=1, source_target_pairs={{0,4},{1,5},{2,6},{3,7},{4,0},{5,1},{6,2},{7,3},{8,12},{9,13},{10,... | collective-permute-start | bytes 1784 | tf_op jit(solution)/shard_map/ppermute | solution.py:381
  3.8 2.6 %collective-permute-start.1 = (s32[148]{0:T(256)S(1)}, s32[148]{0:T(256)S(1)}, u32[]{:S(2)}, u32[]{:S(2)}) collective-permute-start(s32[148]{0:T(256)S(1)} %pad_add_fusion.3), channel_id=1, source_target_pairs={{0,8},{1,9},{2,10},{3,11},{4,12},{5,13},{6,14},{7,15},{8,0},{9,1},... | collective-permute-start | bytes 1784 | tf_op jit(solution)/shard_map/ppermute | solution.py:381
  6.4 1.2 %dynamic-slice_bitcast_fusion = (bf16[640,128]{1,0:T(8,128)(2,1)S(1)}, bf16[640,128]{1,0:T(8,128)(2,1)S(1)}, bf16[640,128]{1,0:T(8,128)(2,1)S(1)}, bf16[640,128]{1,0:T(8,128)(2,1)S(1)}) fusion(bf16[4,640,128]{2,1,0:T(8,128)(2,1)} %bitcast.47, s32[]{:T(128)S(6)} %select_n.41, s32[]{:T(128)S(6)} %select_n.40, s32[]{:T(128)S(6)} %select_n.39, s32[]{:T(128)S(6)} %select_n.38), kind=kLoop, calls=%fused_computation.3 | loop fusion | bytes 1310736 | tf_op jit(solution)/shard_map/jit(dynamic_index_in_dim)/squeeze | solution.py:407
  7.6 1.0 collective-permute-start.3
  8.5 3.5 %collective-permute-start.4 = (bf16[640,128]{1,0:T(8,128)(2,1)S(1)}, bf16[640,128]{1,0:T(8,128)(2,1)S(1)}, u32[]{:S(2)}, u32[]{:S(2)}) collective-permute-start(bf16[640,128]{1,0:T(8,128)(2,1)S(1)} %get-tuple-element.118), channel_id=1, source_target_pairs={{0,8},{1,9},{2,10},{3,11},{4,12},{5,13},{6,14},{7,15},{8,0},{9,1},... | collective-permute-start | bytes 491528 | tf_op jit(solution)/shard_map/ppermute | solution.py:381
  12.1 0.1 slice_bitcast_fusion.1.targets_ref
  12.2 1.1 %collective-permute-done.6 = s32[4,1,20]{2,0,1:T(4,128)S(1)} collective-permute-done((s32[4,1,20]{2,0,1:T(4,128)S(1)}, s32[4,1,20]{2,0,1:T(4,128)S(1)}, u32[]{:S(2)}, u32[]{:S(2)}) %collective-permute-start.6) | collective-permute-done | bytes 352 | tf_op jit(solution)/shard_map/ppermute | solution.py:381
  13.3 1.7 %collective-permute-start.7 = (s32[4,2,20]{2,0,1:T(4,128)S(1)}, s32[4,2,20]{2,0,1:T(4,128)S(1)}, u32[]{:S(2)}, u32[]{:S(2)}) collective-permute-start(s32[4,2,20]{2,0,1:T(4,128)S(1)} %pad_add_fusion.2), channel_id=1, source_target_pairs={{0,2},{1,3},{2,0},{3,1},{4,6},{5,7},{6,4},{7,5},{8,10},{9,11},{10,... | collective-permute-start | bytes 1928 | tf_op jit(solution)/shard_map/ppermute | solution.py:381
  15.0 0.1 pad_add_fusion.5.me_ref
  15.1 0.2 shard_map.55
  15.3 1.2 %copy-done = bf16[128,3968]{1,0:T(8,128)(2,1)S(1)} copy-done((bf16[128,3968]{1,0:T(8,128)(2,1)S(1)}, bf16[128,3968]{1,0:T(8,128)(2,1)}, u32[]{:S(2)}) %copy-start) | copy-done | bytes 1015832
  16.6 6.5 %shard_map.56.source_ref = bf16[128,3968]{1,0:T(8,128)(2,1)S(1)} custom-call(bf16[128,3968]{1,0:T(8,128)(2,1)S(1)} %copy-done, bf16[11,128,3968]{2,1,0:T(8,128)(2,1)} %bitcast.45), custom_call_target="tpu_custom_call" | custom-call | flops 1 | bytes 1 | tf_op jit(solution)/shard_map/pallas_call | solution.py:20
  23.1 3.3 %shard_map.57 = (bf16[128,640]{1,0:T(8,128)(2,1)S(1)}, bf16[128,640]{1,0:T(8,128)(2,1)S(1)}, f32[240,3968]{1,0:T(8,128)S(1)}) custom-call(s32[2]{0:T(128)S(1)} %pad_add_fusion.5.me_ref, s32[2,128]{1,0:T(2,128)S(1)} %get-tuple-element.61.groups_ref, s32[16,20]{1,0:T(8,128)S(1)} %get-tuple-element.122.starts_ref, s32[16,20]{1,0:T(8,128)S(1)} %get-tuple-element.121.turns_ref, ...), custom_call_target="tpu_custom_call" | custom-call | flops 1 | bytes 1 | tf_op jit(solution)/shard_map/pallas_call | solution.py:20
  26.5 0.1 pad_maximum_fusion.refs_1_.refs_3_
  26.7 0.4 collective-permute-start.8
  27.1 1.9 %collective-permute-start.11 = (bf16[128,640]{1,0:T(8,128)(2,1)S(1)}, bf16[128,640]{1,0:T(8,128)(2,1)S(1)}, u32[]{:S(2)}, u32[]{:S(2)}) collective-permute-start(bf16[128,640]{1,0:T(8,128)(2,1)S(1)} %get-tuple-element.76), channel_id=1, source_target_pairs={{0,8},{1,9},{2,10},{3,11},{4,12},{5,13},{6,14},{7,15},{8,0},{9,1},... | collective-permute-start | bytes 491528 | tf_op jit(solution)/shard_map/ppermute | solution.py:381
  29.0 1.9 %collective-permute-start.12 = (bf16[128,640]{1,0:T(8,128)(2,1)S(1)}, bf16[128,640]{1,0:T(8,128)(2,1)S(1)}, u32[]{:S(2)}, u32[]{:S(2)}) collective-permute-start(bf16[128,640]{1,0:T(8,128)(2,1)S(1)} %get-tuple-element.77), channel_id=1, source_target_pairs={{0,12},{1,13},{2,14},{3,15},{4,8},{5,9},{6,10},{7,11},{8,4},{9,5},... | collective-permute-start | bytes 491528 | tf_op jit(solution)/shard_map/ppermute | solution.py:381
  30.9 2.7 %shard_map.58 = (bf16[128,640]{1,0:T(8,128)(2,1)S(1)}, bf16[128,640]{1,0:T(8,128)(2,1)S(1)}) custom-call(s32[2]{0:T(128)S(1)} %pad_add_fusion.5.me_ref, s32[2,128]{1,0:T(2,128)S(1)} %get-tuple-element.61.groups_ref, s32[16,20]{1,0:T(8,128)S(1)} %get-tuple-element.122.starts_ref, s32[16,20]{1,0:T(8,128)S(1)} %get-tuple-element.121.turns_ref, ...), custom_call_target="tpu_custom_call" | custom-call | flops 1 | bytes 1 | tf_op jit(solution)/shard_map/pallas_call | solution.py:20
  33.6 0.6 collective-permute-start.10
  34.2 0.1 pad_add_fusion.6.bins_ref
  34.3 0.1 slice.12.names_ref
  34.3 1.2 %shard_map.59.refs_4_ = f32[128,640]{1,0:T(8,128)S(1)} custom-call(s32[8]{0:T(128)S(1)} %pad_add_fusion.6.bins_ref, s32[4,128]{1,0:T(4,128)S(1)} %slice.12.names_ref, bf16[128,640]{1,0:T(8,128)(2,1)S(1)} %get-tuple-element.78.refs_0_, bf16[4,640,128]{2,1,0:T(8,128)(2,1)S(1)} %pad_maximum_fusion.refs_1_.refs_3_, ...), custom_call_target="tpu_custom_call" | custom-call | flops 1 | bytes 1 | tf_op jit(solution)/shard_map/pallas_call | solution.py:20
  35.5 6.5 %collective-permute-done.11.refs_1_.refs_2_ = bf16[128,640]{1,0:T(8,128)(2,1)S(1)} collective-permute-done((bf16[128,640]{1,0:T(8,128)(2,1)S(1)}, bf16[128,640]{1,0:T(8,128)(2,1)S(1)}, u32[]{:S(2)}, u32[]{:S(2)}) %collective-permute-start.11) | collective-permute-done | bytes 163872 | tf_op jit(solution)/shard_map/ppermute | solution.py:381
  42.1 1.8 %collective-permute-done.8.refs_6_ = bf16[4,640,128]{2,1,0:T(8,128)(2,1)S(1)} collective-permute-done((bf16[4,640,128]{2,1,0:T(8,128)(2,1)S(1)}, bf16[4,640,128]{2,1,0:T(8,128)(2,1)S(1)}, u32[]{:S(2)}, u32[]{:S(2)}) %collective-permute-start.8) | collective-permute-done | bytes 655392 | tf_op jit(solution)/shard_map/ppermute | solution.py:381
  43.9 0.9 collective-permute-done.10.refs_0_.refs_1_
  44.8 0.1 pad_add_fusion.4.bins_ref
  44.9 1.4 %shard_map.60.refs_5_ = f32[384,384]{1,0:T(8,128)S(1)} custom-call(s32[8]{0:T(128)S(1)} %pad_add_fusion.6.bins_ref, s32[4,128]{1,0:T(4,128)S(1)} %slice.12.names_ref, bf16[128,640]{1,0:T(8,128)(2,1)S(1)} %collective-permute-done.10.refs_0_.refs_1_, bf16[128,640]{1,0:T(8,128)(2,1)S(1)} %collective-permute-done.11.refs_1_.refs_2_, ...), custom_call_target="tpu_custom_call" | custom-call | flops 1 | bytes 1 | tf_op jit(solution)/shard_map/pallas_call | solution.py:20
  46.3 0.6 collective-permute-done.13.refs_7_
  46.9 1.7 %shard_map.61 = (f32[512,384]{1,0:T(8,128)S(1)}, bf16[512,384]{1,0:T(8,128)(2,1)S(1)}, f32[4,128]{1,0:T(4,128)S(1)}) custom-call(s32[1]{0:T(128)} %bitcast.1.outer_ref, s32[8]{0:T(128)S(1)} %pad_add_fusion.4.bins_ref, s32[4,128]{1,0:T(4,128)S(1)} %slice.12.names_ref, bf16[128,640]{1,0:T(8,128)(2,1)S(1)} %get-tuple-element.78.refs_0_, ...), custom_call_target="tpu_custom_call" | custom-call | flops 1 | bytes 1 | tf_op jit(solution)/shard_map/pallas_call | solution.py:20
  48.6 0.7 collective-permute-start.17
  49.2 1.2 %shard_map.62.refs_5_ = f32[384,256]{1,0:T(8,128)S(1)} custom-call(s32[8]{0:T(128)S(1)} %pad_add_fusion.6.bins_ref, s32[4,128]{1,0:T(4,128)S(1)} %slice.12.names_ref, bf16[128,640]{1,0:T(8,128)(2,1)S(1)} %collective-permute-done.10.refs_0_.refs_1_, bf16[128,640]{1,0:T(8,128)(2,1)S(1)} %collective-permute-done.11.refs_1_.refs_2_, ...), custom_call_target="tpu_custom_call" | custom-call | flops 1 | bytes 1 | tf_op jit(solution)/shard_map/pallas_call | solution.py:20
  50.4 1.4 %shard_map.63 = (f32[512,256]{1,0:T(8,128)S(1)}, bf16[512,256]{1,0:T(8,128)(2,1)S(1)}, f32[4,128]{1,0:T(4,128)S(1)}) custom-call(s32[1]{0:T(128)} %bitcast.1.outer_ref, s32[8]{0:T(128)S(1)} %pad_add_fusion.4.bins_ref, s32[4,128]{1,0:T(4,128)S(1)} %slice.12.names_ref, bf16[128,640]{1,0:T(8,128)(2,1)S(1)} %get-tuple-element.78.refs_0_, ...), custom_call_target="tpu_custom_call" | custom-call | flops 1 | bytes 1 | tf_op jit(solution)/shard_map/pallas_call | solution.py:20
  51.8 2.8 %collective-permute-start.14 = (f32[4,128]{1,0:T(4,128)S(1)}, f32[4,128]{1,0:T(4,128)S(1)}, u32[]{:S(2)}, u32[]{:S(2)}) collective-permute-start(f32[4,128]{1,0:T(4,128)S(1)} %add.60), channel_id=1, source_target_pairs={{0,4},{1,5},{2,6},{3,7},{4,0},{5,1},{6,2},{7,3},{8,12},{9,13},{10,... | collective-permute-start | bytes 6152 | tf_op jit(solution)/shard_map/ppermute | solution.py:381
  54.6 0.6 collective-permute-start.15
  55.2 1.8 %collective-permute-start.16 = (f32[4,128]{1,0:T(4,128)S(1)}, f32[4,128]{1,0:T(4,128)S(1)}, u32[]{:S(2)}, u32[]{:S(2)}) collective-permute-start(f32[4,128]{1,0:T(4,128)S(1)} %add.60), channel_id=1, source_target_pairs={{0,12},{1,13},{2,14},{3,15},{4,8},{5,9},{6,10},{7,11},{8,4},{9,5},... | collective-permute-start | bytes 6152 | tf_op jit(solution)/shard_map/ppermute | solution.py:381
  57.1 1.0 %collective-permute-start.18 = (bf16[512,256]{1,0:T(8,128)(2,1)S(1)}, bf16[512,256]{1,0:T(8,128)(2,1)S(1)}, u32[]{:S(2)}, u32[]{:S(2)}) collective-permute-start(bf16[512,256]{1,0:T(8,128)(2,1)S(1)} %get-tuple-element.91.refs_2_), channel_id=1, source_target_pairs={{0,4},{1,5},{2,6},{3,7},{4,12},{5,13},{6,14},{7,15},{8,0},{9,1},{1... | collective-permute-start | bytes 786440 | tf_op jit(solution)/shard_map/ppermute | solution.py:388
  58.1 0.7 collective-permute-done.14
  58.8 2.8 %collective-permute-done.15 = f32[4,128]{1,0:T(4,128)S(1)} collective-permute-done((f32[4,128]{1,0:T(4,128)S(1)}, f32[4,128]{1,0:T(4,128)S(1)}, u32[]{:S(2)}, u32[]{:S(2)}) %collective-permute-start.15) | collective-permute-done | bytes 2080 | tf_op jit(solution)/shard_map/ppermute | solution.py:381
  61.6 0.5 collective-permute-done.16
  62.1 0.2 shard_map.64.refs_0_.refs_2_
  62.3 0.8 shard_map.65
  63.1 3.3 %collective-permute-done.18.refs_1_ = bf16[512,256]{1,0:T(8,128)(2,1)S(1)} collective-permute-done((bf16[512,256]{1,0:T(8,128)(2,1)S(1)}, bf16[512,256]{1,0:T(8,128)(2,1)S(1)}, u32[]{:S(2)}, u32[]{:S(2)}) %collective-permute-start.18) | collective-permute-done | bytes 262176 | tf_op jit(solution)/shard_map/ppermute | solution.py:388
  66.5 0.8 shard_map.66
  67.5 0.4 collective-permute-start.20
  67.9 1.2 %collective-permute-done.22.got_ref = bf16[2,160,640]{2,1,0:T(8,128)(2,1)S(1)} collective-permute-done((bf16[2,160,640]{2,1,0:T(8,128)(2,1)S(1)}, bf16[2,160,640]{2,1,0:T(8,128)(2,1)S(1)}, u32[]{:S(2)}, u32[]{:S(2)}) %collective-permute-start.22) | collective-permute-done | bytes 409632 | tf_op jit(solution)/shard_map/ppermute | solution.py:381
  69.1 0.1 shard_map.68
  69.2 0.8 shard_map.69
  70.0 0.2 collective-permute-start.23
  70.2 1.7 %collective-permute-start.25 = (bf16[1,160,640]{2,1,0:T(8,128)(2,1)S(1)}, bf16[1,160,640]{2,1,0:T(8,128)(2,1)S(1)}, u32[]{:S(2)}, u32[]{:S(2)}) collective-permute-start(bf16[1,160,640]{2,1,0:T(8,128)(2,1)S(1)} %get-tuple-element.105), channel_id=1, source_target_pairs={{0,2},{1,3},{2,0},{3,1},{4,6},{5,7},{6,4},{7,5},{8,10},{9,11},{10,... | collective-permute-start | bytes 614408 | tf_op jit(solution)/shard_map/ppermute | solution.py:381
  72.1 0.4 collective-permute-start.21
  72.5 1.8 %collective-permute-start.24 = (bf16[1,160,640]{2,1,0:T(8,128)(2,1)S(1)}, bf16[1,160,640]{2,1,0:T(8,128)(2,1)S(1)}, u32[]{:S(2)}, u32[]{:S(2)}) collective-permute-start(bf16[1,160,640]{2,1,0:T(8,128)(2,1)S(1)} %get-tuple-element.104), channel_id=1, source_target_pairs={{0,2},{1,3},{2,0},{3,1},{4,6},{5,7},{6,4},{7,5},{8,10},{9,11},{10,... | collective-permute-start | bytes 614408 | tf_op jit(solution)/shard_map/ppermute | solution.py:381
  74.3 3.8 %collective-permute-done.25 = bf16[1,160,640]{2,1,0:T(8,128)(2,1)S(1)} collective-permute-done((bf16[1,160,640]{2,1,0:T(8,128)(2,1)S(1)}, bf16[1,160,640]{2,1,0:T(8,128)(2,1)S(1)}, u32[]{:S(2)}, u32[]{:S(2)}) %collective-permute-start.25) | collective-permute-done | bytes 204832 | tf_op jit(solution)/shard_map/ppermute | solution.py:381
  78.2 4.4 %collective-permute-done.21 = bf16[1,160,640]{2,1,0:T(8,128)(2,1)S(1)} collective-permute-done((bf16[1,160,640]{2,1,0:T(8,128)(2,1)S(1)}, bf16[1,160,640]{2,1,0:T(8,128)(2,1)S(1)}, u32[]{:S(2)}, u32[]{:S(2)}) %collective-permute-start.21) | collective-permute-done | bytes 204832 | tf_op jit(solution)/shard_map/ppermute | solution.py:381
  82.5 2.9 %collective-permute-done.19.refs_1_ = bf16[512,640]{1,0:T(8,128)(2,1)S(1)} collective-permute-done((bf16[512,640]{1,0:T(8,128)(2,1)S(1)}, bf16[512,640]{1,0:T(8,128)(2,1)S(1)}, u32[]{:S(2)}, u32[]{:S(2)}) %collective-permute-start.19) | collective-permute-done | bytes 655392 | tf_op jit(solution)/shard_map/ppermute | solution.py:388
  85.4 0.9 collective-permute-done.24
  86.4 0.8 shard_map.71
  87.3 1.5 %collective-permute-start.28 = (bf16[160,640]{1,0:T(8,128)(2,1)S(1)}, bf16[160,640]{1,0:T(8,128)(2,1)S(1)}, u32[]{:S(2)}, u32[]{:S(2)}) collective-permute-start(bf16[160,640]{1,0:T(8,128)(2,1)S(1)} %fusion), channel_id=1, source_target_pairs={{0,8},{1,9},{2,10},{3,11},{4,0},{5,1},{6,2},{7,3},{8,12},{9,13},{1... | collective-permute-start | bytes 614408 | tf_op jit(solution)/shard_map/ppermute | solution.py:388
  88.8 0.2 collective-permute-done.26.got_ref
  89.1 1.8 %collective-permute-start.27 = (bf16[1,160,640]{2,1,0:T(8,128)(2,1)S(1)}, bf16[1,160,640]{2,1,0:T(8,128)(2,1)S(1)}, u32[]{:S(2)}, u32[]{:S(2)}) collective-permute-start(bf16[1,160,640]{2,1,0:T(8,128)(2,1)S(1)} %get-tuple-element.110), channel_id=1, source_target_pairs={{0,2},{1,3},{2,0},{3,1},{4,6},{5,7},{6,4},{7,5},{8,10},{9,11},{10,... | collective-permute-start | bytes 614408 | tf_op jit(solution)/shard_map/ppermute | solution.py:381
  90.9 1.5 %shard_map.73.refs_4_ = f32[160,2560]{1,0:T(8,128)} custom-call(s32[4]{0:T(128)S(1)} %shift-right-arithmetic_xor_fusion.at_ref, f32[160,640]{1,0:T(8,128)S(1)} %bitcast.39, bf16[160,640]{1,0:T(8,128)(2,1)S(1)} %bitcast.42, f32[160,640]{1,0:T(8,128)S(1)} %bitcast.40, bf16[160,640]{1,0:T(8,128)(2,1)S(1)} %bitcast.43), custom_call_target="tpu_custom_call" | custom-call | flops 1 | bytes 1 | tf_op jit(solution)/shard_map/pallas_call | solution.py:355
  92.4 2.6 %collective-permute-done.28.refs_2_ = bf16[160,640]{1,0:T(8,128)(2,1)S(1)} collective-permute-done((bf16[160,640]{1,0:T(8,128)(2,1)S(1)}, bf16[160,640]{1,0:T(8,128)(2,1)S(1)}, u32[]{:S(2)}, u32[]{:S(2)}) %collective-permute-start.28) | collective-permute-done | bytes 204832 | tf_op jit(solution)/shard_map/ppermute | solution.py:388
  94.9 1.3 %collective-permute-done.27 = bf16[1,160,640]{2,1,0:T(8,128)(2,1)S(1)} collective-permute-done((bf16[1,160,640]{2,1,0:T(8,128)(2,1)S(1)}, bf16[1,160,640]{2,1,0:T(8,128)(2,1)S(1)}, u32[]{:S(2)}, u32[]{:S(2)}) %collective-permute-start.27) | collective-permute-done | bytes 204832 | tf_op jit(solution)/shard_map/ppermute | solution.py:381
  96.3 1.5 %shard_map.74 = f32[160,2560]{1,0:T(8,128)} custom-call(s32[4]{0:T(128)S(1)} %shift-right-arithmetic_xor_fusion.at_ref, f32[160,640]{1,0:T(8,128)S(1)} %bitcast.41, bf16[160,640]{1,0:T(8,128)(2,1)S(1)} %bitcast.44, bf16[160,640]{1,0:T(8,128)(2,1)S(1)} %collective-permute-done.28.refs_2_, ...), custom_call_target="tpu_custom_call", output_to_operand_aliasing={{}: (5, {})} | custom-call | flops 1 | bytes 1 | tf_op jit(solution)/shard_map/pallas_call | solution.py:355
  (38 shorter events, 0.8 us)
Async XLA Ops:
  0.7 11.3 %collective-permute-start = (s32[148]{0:T(256)S(1)}, s32[148]{0:T(256)S(1)}, u32[]{:S(2)}, u32[]{:S(2)}) collective-permute-start(s32[148]{0:T(256)S(1)} %pad_add_fusion.3), channel_id=1, source_target_pairs={{0,4},{1,5},{2,6},{3,7},{4,0},{5,1},{6,2},{7,3},{8,12},{9,13},{10,... | collective-permute-start | bytes 1784 | tf_op jit(solution)/shard_map/ppermute | solution.py:381
  3.8 8.3 %collective-permute-start.1 = (s32[148]{0:T(256)S(1)}, s32[148]{0:T(256)S(1)}, u32[]{:S(2)}, u32[]{:S(2)}) collective-permute-start(s32[148]{0:T(256)S(1)} %pad_add_fusion.3), channel_id=1, source_target_pairs={{0,8},{1,9},{2,10},{3,11},{4,12},{5,13},{6,14},{7,15},{8,0},{9,1},... | collective-permute-start | bytes 1784 | tf_op jit(solution)/shard_map/ppermute | solution.py:381
  6.4 5.7 %collective-permute-start.2 = (s32[148]{0:T(256)S(1)}, s32[148]{0:T(256)S(1)}, u32[]{:S(2)}, u32[]{:S(2)}) collective-permute-start(s32[148]{0:T(256)S(1)} %pad_add_fusion.3), channel_id=1, source_target_pairs={{0,12},{1,13},{2,14},{3,15},{4,8},{5,9},{6,10},{7,11},{8,4},{9,5},... | collective-permute-start | bytes 1784 | tf_op jit(solution)/shard_map/ppermute | solution.py:381
  7.6 18.9 %collective-permute-start.3 = (bf16[640,128]{1,0:T(8,128)(2,1)S(1)}, bf16[640,128]{1,0:T(8,128)(2,1)S(1)}, u32[]{:S(2)}, u32[]{:S(2)}) collective-permute-start(bf16[640,128]{1,0:T(8,128)(2,1)S(1)} %get-tuple-element.119), channel_id=1, source_target_pairs={{0,4},{1,5},{2,6},{3,7},{4,0},{5,1},{6,2},{7,3},{8,12},{9,13},{10,... | collective-permute-start | bytes 491528 | tf_op jit(solution)/shard_map/ppermute | solution.py:381
  8.5 18.0 %collective-permute-start.4 = (bf16[640,128]{1,0:T(8,128)(2,1)S(1)}, bf16[640,128]{1,0:T(8,128)(2,1)S(1)}, u32[]{:S(2)}, u32[]{:S(2)}) collective-permute-start(bf16[640,128]{1,0:T(8,128)(2,1)S(1)} %get-tuple-element.118), channel_id=1, source_target_pairs={{0,8},{1,9},{2,10},{3,11},{4,12},{5,13},{6,14},{7,15},{8,0},{9,1},... | collective-permute-start | bytes 491528 | tf_op jit(solution)/shard_map/ppermute | solution.py:381
  12.0 14.5 %collective-permute-start.5 = (bf16[640,128]{1,0:T(8,128)(2,1)S(1)}, bf16[640,128]{1,0:T(8,128)(2,1)S(1)}, u32[]{:S(2)}, u32[]{:S(2)}) collective-permute-start(bf16[640,128]{1,0:T(8,128)(2,1)S(1)} %get-tuple-element.117), channel_id=1, source_target_pairs={{0,12},{1,13},{2,14},{3,15},{4,8},{5,9},{6,10},{7,11},{8,4},{9,5},... | collective-permute-start | bytes 491528 | tf_op jit(solution)/shard_map/ppermute | solution.py:381
  12.1 1.2 %collective-permute-start.6 = (s32[4,1,20]{2,0,1:T(4,128)S(1)}, s32[4,1,20]{2,0,1:T(4,128)S(1)}, u32[]{:S(2)}, u32[]{:S(2)}) collective-permute-start(s32[4,1,20]{2,0,1:T(4,128)S(1)} %slice_bitcast_fusion), channel_id=1, source_target_pairs={{0,1},{1,0},{2,3},{3,2},{4,5},{5,4},{6,7},{7,6},{8,9},{9,8},{10,11... | collective-permute-start | bytes 968 | tf_op jit(solution)/shard_map/ppermute | solution.py:381
  13.3 9.8 %collective-permute-start.7 = (s32[4,2,20]{2,0,1:T(4,128)S(1)}, s32[4,2,20]{2,0,1:T(4,128)S(1)}, u32[]{:S(2)}, u32[]{:S(2)}) collective-permute-start(s32[4,2,20]{2,0,1:T(4,128)S(1)} %pad_add_fusion.2), channel_id=1, source_target_pairs={{0,2},{1,3},{2,0},{3,1},{4,6},{5,7},{6,4},{7,5},{8,10},{9,11},{10,... | collective-permute-start | bytes 1928 | tf_op jit(solution)/shard_map/ppermute | solution.py:381
  15.3 1.2 %copy-start = (bf16[128,3968]{1,0:T(8,128)(2,1)S(1)}, bf16[128,3968]{1,0:T(8,128)(2,1)}, u32[]{:S(2)}) copy-start(bf16[128,3968]{1,0:T(8,128)(2,1)} %flux_ref) | copy-start | bytes 3047428
  26.6 4.3 %collective-permute-start.9 = (bf16[4,640,128]{2,1,0:T(8,128)(2,1)S(1)}, bf16[4,640,128]{2,1,0:T(8,128)(2,1)S(1)}, u32[]{:S(2)}, u32[]{:S(2)}) collective-permute-start(bf16[4,640,128]{2,1,0:T(8,128)(2,1)S(1)} %pad_maximum_fusion.refs_1_.refs_3_), channel_id=1, source_target_pairs={{0,1},{1,0},{2,3},{3,2},{4,5},{5,4},{6,7},{7,6},{8,9},{9,8},{10,11... | collective-permute-start | bytes 1966088 | tf_op jit(solution)/shard_map/ppermute | solution.py:381
  26.7 17.1 %collective-permute-start.8 = (bf16[4,640,128]{2,1,0:T(8,128)(2,1)S(1)}, bf16[4,640,128]{2,1,0:T(8,128)(2,1)S(1)}, u32[]{:S(2)}, u32[]{:S(2)}) collective-permute-start(bf16[4,640,128]{2,1,0:T(8,128)(2,1)S(1)} %pad_maximum_fusion.refs_1_.refs_3_), channel_id=1, source_target_pairs={{0,2},{1,3},{2,0},{3,1},{4,6},{5,7},{6,4},{7,5},{8,10},{9,11},{10,... | collective-permute-start | bytes 1966088 | tf_op jit(solution)/shard_map/ppermute | solution.py:381
  27.1 15.0 %collective-permute-start.11 = (bf16[128,640]{1,0:T(8,128)(2,1)S(1)}, bf16[128,640]{1,0:T(8,128)(2,1)S(1)}, u32[]{:S(2)}, u32[]{:S(2)}) collective-permute-start(bf16[128,640]{1,0:T(8,128)(2,1)S(1)} %get-tuple-element.76), channel_id=1, source_target_pairs={{0,8},{1,9},{2,10},{3,11},{4,12},{5,13},{6,14},{7,15},{8,0},{9,1},... | collective-permute-start | bytes 491528 | tf_op jit(solution)/shard_map/ppermute | solution.py:381
  29.0 13.1 %collective-permute-start.12 = (bf16[128,640]{1,0:T(8,128)(2,1)S(1)}, bf16[128,640]{1,0:T(8,128)(2,1)S(1)}, u32[]{:S(2)}, u32[]{:S(2)}) collective-permute-start(bf16[128,640]{1,0:T(8,128)(2,1)S(1)} %get-tuple-element.77), channel_id=1, source_target_pairs={{0,12},{1,13},{2,14},{3,15},{4,8},{5,9},{6,10},{7,11},{8,4},{9,5},... | collective-permute-start | bytes 491528 | tf_op jit(solution)/shard_map/ppermute | solution.py:381
  33.6 11.2 %collective-permute-start.10 = (bf16[128,640]{1,0:T(8,128)(2,1)S(1)}, bf16[128,640]{1,0:T(8,128)(2,1)S(1)}, u32[]{:S(2)}, u32[]{:S(2)}) collective-permute-start(bf16[128,640]{1,0:T(8,128)(2,1)S(1)} %get-tuple-element.75), channel_id=1, source_target_pairs={{0,4},{1,5},{2,6},{3,7},{4,0},{5,1},{6,2},{7,3},{8,12},{9,13},{10,... | collective-permute-start | bytes 491528 | tf_op jit(solution)/shard_map/ppermute | solution.py:381
  44.8 2.1 %collective-permute-start.13 = (bf16[4,640,128]{2,1,0:T(8,128)(2,1)S(1)}, bf16[4,640,128]{2,1,0:T(8,128)(2,1)S(1)}, u32[]{:S(2)}, u32[]{:S(2)}) collective-permute-start(bf16[4,640,128]{2,1,0:T(8,128)(2,1)S(1)} %collective-permute-done.8.refs_6_), channel_id=1, source_target_pairs={{0,1},{1,0},{2,3},{3,2},{4,5},{5,4},{6,7},{7,6},{8,9},{9,8},{10,11... | collective-permute-start | bytes 1966088 | tf_op jit(solution)/shard_map/ppermute | solution.py:381
  48.6 13.5 %collective-permute-start.17 = (bf16[512,384]{1,0:T(8,128)(2,1)S(1)}, bf16[512,384]{1,0:T(8,128)(2,1)S(1)}, u32[]{:S(2)}, u32[]{:S(2)}) collective-permute-start(bf16[512,384]{1,0:T(8,128)(2,1)S(1)} %get-tuple-element.88.refs_1_), channel_id=1, source_target_pairs={{0,4},{1,5},{2,6},{3,7},{4,12},{5,13},{6,14},{7,15},{8,0},{9,1},{1... | collective-permute-start | bytes 1179656 | tf_op jit(solution)/shard_map/ppermute | solution.py:388
  51.8 6.9 %collective-permute-start.14 = (f32[4,128]{1,0:T(4,128)S(1)}, f32[4,128]{1,0:T(4,128)S(1)}, u32[]{:S(2)}, u32[]{:S(2)}) collective-permute-start(f32[4,128]{1,0:T(4,128)S(1)} %add.60), channel_id=1, source_target_pairs={{0,4},{1,5},{2,6},{3,7},{4,0},{5,1},{6,2},{7,3},{8,12},{9,13},{10,... | collective-permute-start | bytes 6152 | tf_op jit(solution)/shard_map/ppermute | solution.py:381
  54.6 7.0 %collective-permute-start.15 = (f32[4,128]{1,0:T(4,128)S(1)}, f32[4,128]{1,0:T(4,128)S(1)}, u32[]{:S(2)}, u32[]{:S(2)}) collective-permute-start(f32[4,128]{1,0:T(4,128)S(1)} %add.60), channel_id=1, source_target_pairs={{0,8},{1,9},{2,10},{3,11},{4,12},{5,13},{6,14},{7,15},{8,0},{9,1},... | collective-permute-start | bytes 6152 | tf_op jit(solution)/shard_map/ppermute | solution.py:381
  55.2 6.8 %collective-permute-start.16 = (f32[4,128]{1,0:T(4,128)S(1)}, f32[4,128]{1,0:T(4,128)S(1)}, u32[]{:S(2)}, u32[]{:S(2)}) collective-permute-start(f32[4,128]{1,0:T(4,128)S(1)} %add.60), channel_id=1, source_target_pairs={{0,12},{1,13},{2,14},{3,15},{4,8},{5,9},{6,10},{7,11},{8,4},{9,5},... | collective-permute-start | bytes 6152 | tf_op jit(solution)/shard_map/ppermute | solution.py:381
  57.1 9.4 %collective-permute-start.18 = (bf16[512,256]{1,0:T(8,128)(2,1)S(1)}, bf16[512,256]{1,0:T(8,128)(2,1)S(1)}, u32[]{:S(2)}, u32[]{:S(2)}) collective-permute-start(bf16[512,256]{1,0:T(8,128)(2,1)S(1)} %get-tuple-element.91.refs_2_), channel_id=1, source_target_pairs={{0,4},{1,5},{2,6},{3,7},{4,12},{5,13},{6,14},{7,15},{8,0},{9,1},{1... | collective-permute-start | bytes 786440 | tf_op jit(solution)/shard_map/ppermute | solution.py:388
  67.3 1.8 %collective-permute-start.22 = (bf16[2,160,640]{2,1,0:T(8,128)(2,1)S(1)}, bf16[2,160,640]{2,1,0:T(8,128)(2,1)S(1)}, u32[]{:S(2)}, u32[]{:S(2)}) collective-permute-start(bf16[2,160,640]{2,1,0:T(8,128)(2,1)S(1)} %get-tuple-element.99), channel_id=1, source_target_pairs={{0,1},{1,0},{2,3},{3,2},{4,5},{5,4},{6,7},{7,6},{8,9},{9,8},{10,11... | collective-permute-start | bytes 1228808 | tf_op jit(solution)/shard_map/ppermute | solution.py:381
  67.4 18.0 %collective-permute-start.19 = (bf16[512,640]{1,0:T(8,128)(2,1)S(1)}, bf16[512,640]{1,0:T(8,128)(2,1)S(1)}, u32[]{:S(2)}, u32[]{:S(2)}) collective-permute-start(bf16[512,640]{1,0:T(8,128)(2,1)S(1)} %get-tuple-element.101.refs_1_), channel_id=1, source_target_pairs={{0,4},{1,5},{2,6},{3,7},{4,12},{5,13},{6,14},{7,15},{8,0},{9,1},{1... | collective-permute-start | bytes 1966088 | tf_op jit(solution)/shard_map/ppermute | solution.py:388
  67.5 4.5 %collective-permute-start.20 = (bf16[2,160,640]{2,1,0:T(8,128)(2,1)S(1)}, bf16[2,160,640]{2,1,0:T(8,128)(2,1)S(1)}, u32[]{:S(2)}, u32[]{:S(2)}) collective-permute-start(bf16[2,160,640]{2,1,0:T(8,128)(2,1)S(1)} %get-tuple-element.96), channel_id=1, source_target_pairs={{0,1},{1,0},{2,3},{3,2},{4,5},{5,4},{6,7},{7,6},{8,9},{9,8},{10,11... | collective-permute-start | bytes 1228808 | tf_op jit(solution)/shard_map/ppermute | solution.py:381
  70.0 2.4 %collective-permute-start.23 = (bf16[2,160,640]{2,1,0:T(8,128)(2,1)S(1)}, bf16[2,160,640]{2,1,0:T(8,128)(2,1)S(1)}, u32[]{:S(2)}, u32[]{:S(2)}) collective-permute-start(bf16[2,160,640]{2,1,0:T(8,128)(2,1)S(1)} %get-tuple-element.103), channel_id=1, source_target_pairs={{0,1},{1,0},{2,3},{3,2},{4,5},{5,4},{6,7},{7,6},{8,9},{9,8},{10,11... | collective-permute-start | bytes 1228808 | tf_op jit(solution)/shard_map/ppermute | solution.py:381
  70.2 7.9 %collective-permute-start.25 = (bf16[1,160,640]{2,1,0:T(8,128)(2,1)S(1)}, bf16[1,160,640]{2,1,0:T(8,128)(2,1)S(1)}, u32[]{:S(2)}, u32[]{:S(2)}) collective-permute-start(bf16[1,160,640]{2,1,0:T(8,128)(2,1)S(1)} %get-tuple-element.105), channel_id=1, source_target_pairs={{0,2},{1,3},{2,0},{3,1},{4,6},{5,7},{6,4},{7,5},{8,10},{9,11},{10,... | collective-permute-start | bytes 614408 | tf_op jit(solution)/shard_map/ppermute | solution.py:381
  72.1 10.5 %collective-permute-start.21 = (bf16[1,160,640]{2,1,0:T(8,128)(2,1)S(1)}, bf16[1,160,640]{2,1,0:T(8,128)(2,1)S(1)}, u32[]{:S(2)}, u32[]{:S(2)}) collective-permute-start(bf16[1,160,640]{2,1,0:T(8,128)(2,1)S(1)} %get-tuple-element.97), channel_id=1, source_target_pairs={{0,2},{1,3},{2,0},{3,1},{4,6},{5,7},{6,4},{7,5},{8,10},{9,11},{10,... | collective-permute-start | bytes 614408 | tf_op jit(solution)/shard_map/ppermute | solution.py:381
  72.5 13.9 %collective-permute-start.24 = (bf16[1,160,640]{2,1,0:T(8,128)(2,1)S(1)}, bf16[1,160,640]{2,1,0:T(8,128)(2,1)S(1)}, u32[]{:S(2)}, u32[]{:S(2)}) collective-permute-start(bf16[1,160,640]{2,1,0:T(8,128)(2,1)S(1)} %get-tuple-element.104), channel_id=1, source_target_pairs={{0,2},{1,3},{2,0},{3,1},{4,6},{5,7},{6,4},{7,5},{8,10},{9,11},{10,... | collective-permute-start | bytes 614408 | tf_op jit(solution)/shard_map/ppermute | solution.py:381
  87.2 1.8 %collective-permute-start.26 = (bf16[2,160,640]{2,1,0:T(8,128)(2,1)S(1)}, bf16[2,160,640]{2,1,0:T(8,128)(2,1)S(1)}, u32[]{:S(2)}, u32[]{:S(2)}) collective-permute-start(bf16[2,160,640]{2,1,0:T(8,128)(2,1)S(1)} %get-tuple-element.108), channel_id=1, source_target_pairs={{0,1},{1,0},{2,3},{3,2},{4,5},{5,4},{6,7},{7,6},{8,9},{9,8},{10,11... | collective-permute-start | bytes 1228808 | tf_op jit(solution)/shard_map/ppermute | solution.py:381
  87.3 7.6 %collective-permute-start.28 = (bf16[160,640]{1,0:T(8,128)(2,1)S(1)}, bf16[160,640]{1,0:T(8,128)(2,1)S(1)}, u32[]{:S(2)}, u32[]{:S(2)}) collective-permute-start(bf16[160,640]{1,0:T(8,128)(2,1)S(1)} %fusion), channel_id=1, source_target_pairs={{0,8},{1,9},{2,10},{3,11},{4,0},{5,1},{6,2},{7,3},{8,12},{9,13},{1... | collective-permute-start | bytes 614408 | tf_op jit(solution)/shard_map/ppermute | solution.py:388
  89.1 7.2 %collective-permute-start.27 = (bf16[1,160,640]{2,1,0:T(8,128)(2,1)S(1)}, bf16[1,160,640]{2,1,0:T(8,128)(2,1)S(1)}, u32[]{:S(2)}, u32[]{:S(2)}) collective-permute-start(bf16[1,160,640]{2,1,0:T(8,128)(2,1)S(1)} %get-tuple-element.110), channel_id=1, source_target_pairs={{0,2},{1,3},{2,0},{3,1},{4,6},{5,7},{6,4},{7,5},{8,10},{9,11},{10,... | collective-permute-start | bytes 614408 | tf_op jit(solution)/shard_map/ppermute | solution.py:381
